TPU v7x, 32 devices: a whole 2x2x4 slice. The times are simulated.
32 devices in a mesh: piece: 8 (over y, x, core), col: 4 (over z).
Axes of the slice: x: 2, y: 2, z: 4, core: 2. Of those that a mesh axis runs over, the one named last changes fastest.
Arguments:
- positions: float32 [3, 1024, 128], P(None, 'piece'), as said below
- phase: int32 [1024, 128], P('piece'), may hold values from 0 to 2
- neighbours: int32 [1024, 28], P('piece', 'col'), may hold values from -1 to 1023, as said below
- counts: int32 [8], replicated, may hold values from 64 to 128, as said below
- phase_density: float32 [3], replicated, may hold values from 0.1 to 1
- right_side: float32 [1024, 128], P(('piece', 'col')), may hold values from -6 to 6
Outputs:
- solution_field: float32 [1024, 128], P(('piece', 'col'))
- residual: float32 [1024, 128], P(('piece', 'col'))
Inputs may be any that keep to these rules, and one draw needn't show every extreme that they name: `neighbours`: the slots of each piece at or past its count hold no block. Live blocks, taken in slot order piece after piece, form layers of 16 blocks in Morton order of a 4 x 4 grid. Block q lists n exactly when n lists q; every listed block lies on q's own piece or the piece just before or after it, and its place in that order of live blocks differs from q's by less than 32; empty slots and the last column list only -1. `counts`: some piece holds exactly 128 live blocks. `positions`: the particles of one live block lie in one unit cell; particles of two live blocks that do not list each other are 1 or more apart.
All inputs are finite; a program needn't handle non-finite values.
Results may differ from a plain program's by a relative error of at most 0.0003.
Values sent between devices are 32-bit elements; how exact they have to be, the bound alone decides.
No kernel may reach another device: no remote copies, remote signals or barrier semaphores. Data moves between devices by JAX's collectives and lax.ppermute only.
A program may use at most 64 MiB of HBM per device.

v0:
```python
import math

import jax
import jax.numpy as jnp
from jax import lax
from jax.sharding import PartitionSpec as P

ITERS = 2


def padded(cells, sides, width):
    for axis, dim in sides:
        count = lax.axis_size(axis)
        ends = count - 1
        head = lax.slice_in_dim(cells, 0, width, axis=dim)
        tail = lax.slice_in_dim(cells, cells.shape[dim] - width, cells.shape[dim], axis=dim)
        cells = jnp.concatenate(
            [
                lax.ppermute(tail, axis, [(i, (i + 1) % count) for i in range(ends)]),
                cells,
                lax.ppermute(head, axis, [((i + 1) % count, i) for i in range(ends)]),
            ],
            axis=dim,
        )
    return cells


def fetch_phase_density(phase, phase_density):
    labels = jnp.arange(3, dtype=jnp.int32)
    return jnp.sum(jnp.where(phase[..., None] == labels, phase_density, 0.0), axis=-1)


def pair_term(own_pos, own_rho, own_ids, slot_ids, hood_state, hood_field, base):
    valid = slot_ids >= 0
    where_at = jnp.clip(slot_ids - base, 0, hood_field.shape[0] - 1)
    other = hood_state[:, where_at]
    remote = hood_field[where_at]
    squared = jnp.zeros((own_rho.shape[0], own_rho.shape[1], own_rho.shape[1]), jnp.float32)
    for component in range(3):
        slot_displacement = own_pos[component][:, :, None] - other[component][:, None, :]
        squared = squared + slot_displacement * slot_displacement
    kernel = jnp.square(jnp.maximum(1.0 - squared, 0.0)) / (squared + 0.01)
    weight = 2.0 / (own_rho[:, :, None] + other[3][:, None, :])
    particles = jnp.arange(own_rho.shape[1], dtype=jnp.int32)
    same = (slot_ids == own_ids)[:, None, None] & (particles[:, None] == particles[None, :])[None]
    keep = valid[:, None, None] & jnp.logical_not(same)
    tile = jnp.where(keep, kernel * weight / own_rho.shape[1], 0.0)
    return jnp.einsum("gij,gj->gi", tile, remote, precision=lax.Precision.HIGHEST)


def body(positions, phase, neighbours, counts, phase_density, right_side):
    capacity = positions.shape[1]
    per_block = positions.shape[2]
    columns = lax.axis_size("col")
    share = capacity // columns
    piece = lax.axis_index("piece")
    column = lax.axis_index("col")
    density = fetch_phase_density(phase, phase_density)
    state = jnp.concatenate([positions, density[None]], 0)
    filled = counts[piece]
    hood_state = padded(state, (("piece", 1),), capacity)

    def remap(ids):
        return jnp.where(ids >= 0, ids - (piece - 1) * capacity, -1)

    def surround(whole):
        return padded(whole, (("piece", 0),), capacity)

    hood_size = hood_state.shape[1]
    live = jnp.arange(capacity, dtype=jnp.int32) < filled
    group = math.gcd(16, capacity)
    ngroup = capacity // group

    def group_sum(field_hood, start):
        own_pos = lax.dynamic_slice_in_dim(positions, start, group, 1)
        own_rho = lax.dynamic_slice_in_dim(density, start, group, 0)
        own_ids = capacity + start + jnp.arange(group, dtype=jnp.int32)
        lists = remap(lax.dynamic_slice_in_dim(neighbours, start, group, 0))
        running = jnp.zeros((group, per_block), jnp.float32)
        for neighbour_slot in range(lists.shape[1]):
            running = running + pair_term(
                own_pos, own_rho, own_ids, lists[:, neighbour_slot], hood_state, field_hood, 0
            )
        return running

    def own_terms(field_hood):
        starts = jnp.arange(ngroup, dtype=jnp.int32) * group
        output_blocks = lax.map(lambda start: group_sum(field_hood, start), starts)
        return output_blocks.reshape(capacity, per_block)

    def mine(values):
        return lax.dynamic_slice_in_dim(values, column * share, share, 0)

    def totals(part_sum):
        return lax.psum_scatter(part_sum, "col", scatter_dimension=0, tiled=True)

    def hood_of(column_vector):
        return surround(lax.all_gather(column_vector, "col", axis=0, tiled=True))

    source = jnp.where(mine(live)[:, None], right_side, 0.0)
    rho_vector = mine(density)

    def inner(first, second):
        return jnp.sum(first * second)

    diagonal = 1.0 / rho_vector + totals(own_terms(jnp.ones((hood_size, per_block), jnp.float32)))

    def operate(column_vector):
        return diagonal * column_vector - totals(own_terms(hood_of(column_vector)))

    solution_field = jnp.zeros_like(source)
    residual = source

    def paired_sums(first, second, third):
        return lax.psum((inner(first, second), inner(second, third)), ("piece", "col"))

    precond = residual / diagonal
    image = operate(precond)
    weighted, curved = paired_sums(residual, precond, image)
    advance = weighted / curved
    direction = precond
    along = image
    for step in range(ITERS):
        solution_field = solution_field + advance * direction
        residual = residual - advance * along
        if step + 1 < ITERS:
            precond = residual / diagonal
            image = operate(precond)
            weighted_next, curved = paired_sums(residual, precond, image)
            blend = weighted_next / weighted
            advance = weighted_next / (curved - blend * weighted_next / advance)
            direction = precond + blend * direction
            along = image + blend * along
            weighted = weighted_next
    return (solution_field, residual)


def solution(mesh):
    placed = (
        P(None, "piece", None),
        P("piece", None),
        P("piece", "col"),
        P(),
        P(),
        P(("piece", "col"), None),
    )
    return jax.shard_map(
        body,
        mesh=mesh,
        in_specs=placed,
        out_specs=(P(("piece", "col"), None), P(("piece", "col"), None)),
        check_vma=False,
    )
```

profile of v0, /device:TPU:0, one launch (start us, length us, event | category | flops | bytes accessed | tf_op | source)
XLA Modules:
  0.0 987.7 jit_solution(12460738228159602741)
XLA Ops:
  12.2 4.2 collective-permute-done.1
  17.4 256.2 %while.36 = (s32[]{:T(128)}, f32[8,16,128]{2,1,0:T(8,128)S(1)}, s32[8]{0:T(128)S(1)}, s32[128,7]{0,1:T(8,128)S(1)}, s32[]{:T(128)}, /*index=5*/f32[3,128,128]{2,...) while((s32[]{:T(128)}, f32[8,16,128]{2,1,0:T(8,128)S(1)}, ...), condition=%wide.region_2.3_spmd, body=%wide.region_1.2_spmd.sunk | while | flops 60592136 | bytes 2097327 | solution.py:88
  21.8 2.9 fusion.1082
  34.2 2.9 fusion.1076
  53.9 2.9 fusion.1082
  66.2 2.9 fusion.1076
  70.3 2.9 fusion.1074
  85.9 2.9 fusion.1082
  98.2 2.9 fusion.1076
  117.9 2.9 fusion.1082
  130.2 2.9 fusion.1076
  134.3 2.9 fusion.1074
  150.0 2.9 fusion.1082
  162.3 2.9 fusion.1076
  166.4 2.9 fusion.1074
  182.0 2.9 fusion.1082
  194.3 2.9 fusion.1076
  214.0 2.9 fusion.1082
  226.3 2.9 fusion.1076
  230.4 2.9 fusion.1074
  246.0 2.9 fusion.1082
  258.3 2.9 fusion.1076
  275.6 23.3 %reduce-scatter.4.cloned.1.call-done = f32[32,128]{1,0:T(8,128)} async-done(((f32[128,128]{1,0:T(8,128)}), f32[32,128]{1,0:T(8,128)}) %reduce-scatter.4.cloned.1.call-update) | async-done | bytes 16400 | tf_op jit(solution)/shard_map/reduce_scatter | solution.py:95
  299.8 13.1 %all_gather.6 = f32[128,128]{1,0:T(8,128)S(1)} all-gather(f32[32,128]{1,0:T(8,128)S(1)} %get-tuple-element.376), channel_id=1, replica_groups=mesh['piece'=8,'col'=4] {'col'}, dimensions={0}, use_global_device_ids=true | all-gather | bytes 81920 | tf_op jit(solution)/shard_map/all_gather | solution.py:98
  315.7 3.3 collective-permute-done.3
  319.1 256.0 %while.37 = (s32[]{:T(128)}, f32[8,16,128]{2,1,0:T(8,128)S(1)}, s32[8]{0:T(128)S(1)}, s32[128,7]{0,1:T(8,128)S(1)}, s32[]{:T(128)}, /*index=5*/f32[3,128,128]{2,...) while((s32[]{:T(128)}, f32[8,16,128]{2,1,0:T(8,128)S(1)}, ...), condition=%wide.region_7.8_spmd, body=%wide.region_6.7_spmd.sunk | while | flops 60592136 | bytes 1900715 | solution.py:88
  323.5 2.9 fusion.1111
  335.8 2.9 fusion.1105
  339.9 2.9 fusion.1103
  355.5 2.9 fusion.1111
  367.8 2.9 fusion.1105
  387.5 2.9 fusion.1111
  399.8 2.9 fusion.1105
  419.5 2.9 fusion.1111
  431.8 2.9 fusion.1105
  435.9 2.9 fusion.1103
  451.5 2.9 fusion.1111
  463.9 2.9 fusion.1105
  468.0 2.9 fusion.1103
  483.5 2.9 fusion.1111
  495.9 2.9 fusion.1105
  500.0 2.9 fusion.1103
  515.6 2.9 fusion.1111
  527.9 2.9 fusion.1105
  547.5 2.9 fusion.1111
  559.9 2.9 fusion.1105
  564.0 2.9 fusion.1103
  575.8 19.9 %reduce-scatter.6.cloned.1.call-done = f32[32,128]{1,0:T(8,128)} async-done(((f32[128,128]{1,0:T(8,128)}), f32[32,128]{1,0:T(8,128)}) %reduce-scatter.6.cloned.1.call-update) | async-done | bytes 16400 | tf_op jit(solution)/shard_map/reduce_scatter | solution.py:95
  597.1 38.7 %all-reduce.1 = (f32[]{:T(128)}, f32[]{:T(128)}) all-reduce(f32[]{:T(128)} %get-tuple-element.318, f32[]{:T(128)} %get-tuple-element.317), channel_id=1, replica_groups=mesh['piece'=8,'col'=4] {'piece','col'}, use_global_device_ids=true, to_apply=%region_5.6 | all-reduce | flops 2 | bytes 16 | tf_op jit(solution)/shard_map/psum | solution.py:115
  637.2 13.2 %all_gather.7 = f32[128,128]{1,0:T(8,128)S(1)} all-gather(f32[32,128]{1,0:T(8,128)S(1)} %fusion.924), channel_id=1, replica_groups=mesh['piece'=8,'col'=4] {'col'}, dimensions={0}, use_global_device_ids=true | all-gather | bytes 81920 | tf_op jit(solution)/shard_map/all_gather | solution.py:98
  653.2 4.1 collective-permute-done.5
  657.3 256.1 %while.38 = (s32[]{:T(128)}, f32[8,16,128]{2,1,0:T(8,128)S(1)}, s32[8]{0:T(128)S(1)}, s32[128,7]{0,1:T(8,128)S(1)}, s32[]{:T(128)}, /*index=5*/f32[3,128,128]{2,...) while((s32[]{:T(128)}, f32[8,16,128]{2,1,0:T(8,128)S(1)}, ...), condition=%wide.region_14.15_spmd, body=%wide.region_13.14_spmd.sunk | while | flops 60592136 | bytes 1900715 | solution.py:88
  661.8 2.9 fusion.1140
  674.1 2.9 fusion.1134
  678.2 2.9 fusion.1132
  693.8 2.9 fusion.1140
  725.8 2.9 fusion.1140
  757.8 2.9 fusion.1140
  789.8 2.9 fusion.1140
  821.8 2.9 fusion.1140
  853.8 2.9 fusion.1140
  885.8 2.9 fusion.1140
  914.1 21.8 %reduce-scatter.8.cloned.1.call-done = f32[32,128]{1,0:T(8,128)} async-done(((f32[128,128]{1,0:T(8,128)}), f32[32,128]{1,0:T(8,128)}) %reduce-scatter.8.cloned.1.call-update) | async-done | bytes 16400 | tf_op jit(solution)/shard_map/reduce_scatter | solution.py:95
  937.3 38.8 %all-reduce = (f32[]{:T(128)}, f32[]{:T(128)}) all-reduce(f32[]{:T(128)} %get-tuple-element.316, f32[]{:T(128)} %get-tuple-element.315), channel_id=1, replica_groups=mesh['piece'=8,'col'=4] {'piece','col'}, use_global_device_ids=true, to_apply=%region_12.13 | all-reduce | flops 2 | bytes 16 | tf_op jit(solution)/shard_map/psum | solution.py:115
  (968 shorter events, 594.9 us)
Async XLA Ops:
  7.2 1.1 copy-start.5
  7.2 1.1 copy-start.7
  7.2 291.8 %reduce-scatter.4.cloned.1.call-start = ((), (), s32[]{:S(2)}) async-start(), calls=%async_computation.3 | async-start | bytes 81920 | tf_op jit(solution)/shard_map/reduce_scatter | solution.py:95
  8.5 3.7 collective-permute-start
  10.9 5.5 collective-permute-start.1
  16.7 0.7 copy-start
  17.4 256.9 %copy-start.8 = (s32[8]{0:T(128)S(1)}, s32[8]{0:T(128)}, u32[]{:S(2)}) copy-start(s32[8]{0:T(128)} %param.15) | copy-start | bytes 100
  273.6 0.6 copy-start.3
  274.2 24.7 %copy-start.1 = (f32[32,128]{1,0:T(8,128)S(1)}, f32[32,128]{1,0:T(8,128)}, u32[]{:S(2)}) copy-start(f32[32,128]{1,0:T(8,128)} %param.17) | copy-start | bytes 49156
  274.3 321.5 %reduce-scatter.6.cloned.1.call-start = ((), (), s32[]{:S(2)}) async-start(), calls=%async_computation.4 | async-start | bytes 81920 | tf_op jit(solution)/shard_map/reduce_scatter | solution.py:95
  312.9 2.8 collective-permute-start.2
  314.2 4.8 collective-permute-start.3
  575.1 0.6 copy-start.4
  575.8 360.1 %reduce-scatter.8.cloned.1.call-start = ((), (), s32[]{:S(2)}) async-start(), calls=%async_computation.5 | async-start | bytes 81920 | tf_op jit(solution)/shard_map/reduce_scatter | solution.py:95
  650.4 2.8 collective-permute-start.4
  651.6 5.7 collective-permute-start.5
  913.4 0.6 copy-start.2
  937.3 43.1 %copy-start.6 = (f32[32,128]{1,0:T(8,128)S(1)}, f32[32,128]{1,0:T(8,128)}, u32[]{:S(2)}) copy-start(f32[32,128]{1,0:T(8,128)} %reduce-scatter.8.cloned.1.call-done) | copy-start | bytes 49156
Sparse Core Ops, SparseCore 0:
  274.4 24.5 reduce-scatter.3
  575.9 19.7 reduce-scatter.5
  914.2 21.6 reduce-scatter.7
where the time goes:
time: 993 us; the launch traced here: 988 us
  matrix products  488 us (49%)
  local copies, waits for them, and re-layouts  236 us (24%)
  blocking collectives  104 us (10%)
  waiting for transfers between devices  76.8 us (8%)
  loops' own time  44.4 us (4%)
  between operations  19.7 us (2%)
    dot_general x168, matrix products, pair_term(): jnp.einsum('gij,gj->gi', tile, remote, precision=lax.Precision.HIGHEST)  488 us
    gather x168, local copies, waits for them, and re-layouts, pair_term(): other = hood_state[:, where_at]  101 us
    gather x168, local copies, waits for them, and re-layouts, pair_term(): remote = hood_field[where_at]  94.4 us
    psum x2, blocking collectives, paired_sums(): lax.psum((inner(first, second), inner(second, third)), ('piece', 'col'))  77.4 us
    reduce_scatter x3, waiting for transfers between devices, totals(): return lax.psum_scatter(part_sum, 'col', scatter_dimension=0, tiled=True)  65.1 us
    another operation x3, loops' own time, own_terms(): output_blocks = lax.map(lambda start: group_sum(field_hood, start), starts)  44.4 us
    all_gather x2, blocking collectives, hood_of(): return surround(lax.all_gather(column_vector, 'col', axis=0, tiled=True))  26.3 us
  transfers between devices with their start and end apart: 9, of which 6 were waited for; matrix products, arithmetic and copies ran while one was open for 0% of the time, Pallas kernels for 0%

commit v1 on v0

--- a/solution.py
+++ b/solution.py
@@ -1,11 +1,69 @@
+import functools
 import math
 
 import jax
 import jax.numpy as jnp
+import numpy as np
 from jax import lax
+from jax.experimental import pallas as pl
+from jax.experimental.pallas import tpu as pltpu
 from jax.sharding import PartitionSpec as P
 
 ITERS = 2
+SIDE = 4
+LAYER = SIDE * SIDE
+REACH = 2 * LAYER
+SUB = 8
+VMEM = pl.BlockSpec(memory_space=pltpu.VMEM)
+SMEM = pl.BlockSpec(memory_space=pltpu.SMEM)
+
+
+def stencil_tables():
+    levels = SIDE.bit_length() - 1
+
+    def cell(code):
+        across = sum((code >> (2 * level) & 1) << level for level in range(levels))
+        along = sum((code >> (2 * level + 1) & 1) << level for level in range(levels))
+        return across, along
+
+    place = {cell(code): code for code in range(LAYER)}
+    rows = []
+    for code in range(LAYER):
+        across, along = cell(code)
+        rows.append(
+            sorted(
+                step_z * LAYER + place[across + step_x, along + step_y] - code
+                for step_z in (-1, 0, 1)
+                for step_y in (-1, 0, 1)
+                for step_x in (-1, 0, 1)
+                if (across + step_x, along + step_y) in place
+            )
+        )
+    longest = max(len(row) for row in rows)
+    offsets = np.zeros((LAYER, longest), np.int32)
+    below = np.zeros((LAYER, 2 * REACH + 1), np.int32)
+    for code, row in enumerate(rows):
+        offsets[code, : len(row)] = row
+        for t in range(-REACH, REACH + 1):
+            below[code, t + REACH] = sum(offset < t for offset in row)
+    return offsets, below
+
+
+OFFSETS, BELOW = stencil_tables()
+
+
+def tile_bounds(share):
+    inner = outer = 0
+    for first in range(LAYER):
+        for live in range(1, share + 1):
+            near = far = 0
+            for a in range(live):
+                code = (first + a) % LAYER
+                row = [int(o) for o in OFFSETS[code][: BELOW[code, -1]]]
+                near += sum(0 <= a + o and o <= 0 for o in row)
+                far += sum(a + o < 0 or a + o >= live for o in row)
+            inner, outer = max(inner, near), max(outer, far)
+    return inner, outer
 
 
 def padded(cells, sides, width):
@@ -30,7 +88,7 @@
     return jnp.sum(jnp.where(phase[..., None] == labels, phase_density, 0.0), axis=-1)
 
 
-def pair_term(own_pos, own_rho, own_ids, slot_ids, hood_state, hood_field, base):
+def literal_pair_term(own_pos, own_rho, own_ids, slot_ids, hood_state, hood_field, base):
     valid = slot_ids >= 0
     where_at = jnp.clip(slot_ids - base, 0, hood_field.shape[0] - 1)
     other = hood_state[:, where_at]
@@ -48,7 +106,7 @@
     return jnp.einsum("gij,gj->gi", tile, remote, precision=lax.Precision.HIGHEST)
 
 
-def body(positions, phase, neighbours, counts, phase_density, right_side):
+def literal(positions, phase, neighbours, counts, phase_density, right_side):
     capacity = positions.shape[1]
     per_block = positions.shape[2]
     columns = lax.axis_size("col")
@@ -78,7 +136,7 @@
         lists = remap(lax.dynamic_slice_in_dim(neighbours, start, group, 0))
         running = jnp.zeros((group, per_block), jnp.float32)
         for neighbour_slot in range(lists.shape[1]):
-            running = running + pair_term(
+            running = running + literal_pair_term(
                 own_pos, own_rho, own_ids, lists[:, neighbour_slot], hood_state, field_hood, 0
             )
         return running
@@ -135,6 +193,438 @@
     return (solution_field, residual)
 
 
+def rank(table, code, t):
+    return table[code, jnp.clip(t, -REACH, REACH) + REACH]
+
+
+def inner_range(meta, below, a):
+    code = lax.rem(meta[1] + a, LAYER)
+    return code, rank(below, code, -a), rank(below, code, 0)
+
+
+def outer_ranges(meta, below, a):
+    code = lax.rem(meta[1] + a, LAYER)
+    place = meta[1] + a
+    before = (rank(below, code, -place), rank(below, code, -a))
+    after = (rank(below, code, meta[0] - a), rank(below, code, meta[2] - place))
+    return code, before, after
+
+
+def pair_chunk(own, other):
+    dx = own[0] - other[0]
+    dy = own[1] - other[1]
+    dz = own[2] - other[2]
+    squared = dx * dx + dy * dy + dz * dz
+    rest = jnp.maximum(1.0 - squared, 0.0)
+    return rest * rest * pltpu.reciprocal((squared + 0.01) * (own[3] + other[3]), approx=True)
+
+
+def spread_columns(out, index, rows):
+    count, width = rows.shape
+    turned = rows.T
+    for a in range(count):
+        out[index(a)] = jnp.broadcast_to(turned[:, a : a + 1], (width, width))
+
+
+def lane_sums(parts, count, width):
+    lanes = lax.broadcasted_iota(jnp.int32, (width, width), 1)
+    turned = jnp.zeros((width, width), jnp.float32)
+    for a in range(count):
+        turned = jnp.where(lanes == a, jnp.sum(parts[a], axis=1, keepdims=True), turned)
+    return turned.T[:count]
+
+
+def totals(live, rows_ref, cols_ref, count, width):
+    rows = lane_sums(rows_ref, count, width)
+    cols = jnp.sum(cols_ref[...].reshape(count, SUB, width), axis=1)
+    alive = lax.broadcasted_iota(jnp.int32, (count, width), 0) < live
+    return jnp.where(alive, rows + cols, 0.0)
+
+
+def build_inner(meta, offsets, below, position, density, tiles, spread, rows_ref, cols_ref, weight):
+    share, width = rows_ref.shape[0], rows_ref.shape[2]
+    chunks = width // SUB
+    base = meta[3]
+    weight[...] = density[...] * (width / 2.0)
+    own_rows = pl.ds(pl.multiple_of(base, SUB), share)
+    for k in range(4):
+        values = position[k, own_rows, :] if k < 3 else weight[own_rows, :]
+        spread_columns(spread, lambda a: (a, k), values)
+    cols_ref[...] = jnp.zeros_like(cols_ref)
+
+    def other_rows(row):
+        here = pl.ds(row, 1)
+        return [position[k, here, :] for k in range(3)] + [weight[here, :]]
+
+    def block(a, at):
+        code, low, high = inner_range(meta, below, a)
+
+        def pair(j, carry):
+            at, sums = carry
+            n = a + offsets[code, j]
+            other = other_rows(base + n)
+            down = jnp.zeros((SUB, width), jnp.float32)
+            after = []
+            for c in range(chunks):
+                here = slice(c * SUB, (c + 1) * SUB)
+                tile = pair_chunk([spread[a, k, here, :] for k in range(4)], other)
+                tiles[at, here, :] = tile
+                down = down + tile
+                after.append(sums[c] + tile)
+            there = pl.ds(pl.multiple_of(n * SUB, SUB), SUB)
+            cols_ref[there, :] = cols_ref[there, :] + down
+            return at + 1, tuple(after)
+
+        zero = jnp.zeros((SUB, width), jnp.float32)
+        at, sums = lax.fori_loop(low, high, pair, (at, (zero,) * chunks))
+        other = other_rows(base + a)
+        lane = lax.broadcasted_iota(jnp.int32, (SUB, width), 1)
+        sublane = lax.broadcasted_iota(jnp.int32, (SUB, width), 0)
+        for c in range(chunks):
+            here = slice(c * SUB, (c + 1) * SUB)
+            tile = pair_chunk([spread[a, k, here, :] for k in range(4)], other)
+            tile = jnp.where(lane == sublane + c * SUB, 0.0, tile)
+            tiles[at, here, :] = tile
+            rows_ref[a, here, :] = sums[c] + tile
+        return at + 1
+
+    lax.fori_loop(0, meta[0], block, 0)
+
+
+def build_outer(
+    meta, offsets, below, position, density, before, after, right_side, spread, rows_ref, cols_ref,
+    tiles, diagonal_ref, precond_ref, hood,
+):
+    share, width = right_side.shape
+    chunks = width // SUB
+    capacity = density.shape[0]
+    base, filled = meta[3], meta[4]
+    scale = width / 2.0
+    for k in range(4):
+        gain = 1.0 if k < 3 else scale
+        hood[k, 0:share, :] = before[k] * gain
+        hood[k, share : share + capacity, :] = position[k] if k < 3 else density[...] * gain
+        hood[k, share + capacity :, :] = after[k] * gain
+    edge = share + filled - base
+
+    def block(a, at):
+        code, (low, high), (low_next, high_next) = outer_ranges(meta, below, a)
+
+        def pair(j, carry):
+            at, sums = carry
+            w = share + a + offsets[code, j]
+            row = jnp.where(w < edge, base + w, share + capacity + w - edge)
+            here = pl.ds(row, 1)
+            other = [hood[k, here, :] for k in range(4)]
+            result = []
+            for c in range(chunks):
+                here = slice(c * SUB, (c + 1) * SUB)
+                tile = pair_chunk([spread[a, k, here, :] for k in range(4)], other)
+                tiles[at, here, :] = tile
+                result.append(sums[c] + tile)
+            return at + 1, tuple(result)
+
+        start = tuple(rows_ref[a, c * SUB : (c + 1) * SUB, :] for c in range(chunks))
+        carry = lax.fori_loop(low, high, pair, (at, start))
+        at, sums = lax.fori_loop(low_next, high_next, pair, carry)
+        for c in range(chunks):
+            rows_ref[a, c * SUB : (c + 1) * SUB, :] = sums[c]
+        return at
+
+    lax.fori_loop(0, meta[0], block, 0)
+    own_rows = pl.ds(pl.multiple_of(base, SUB), share)
+    alive = lax.broadcasted_iota(jnp.int32, (share, width), 0) < meta[0]
+    diagonal = 1.0 / density[own_rows, :] + totals(meta[0], rows_ref, cols_ref, share, width)
+    diagonal_ref[...] = diagonal
+    precond_ref[...] = jnp.where(alive, right_side[...], 0.0) / diagonal
+
+
+def apply_inner(meta, offsets, below, field, tiles, rows_ref, cols_ref, spread):
+    share, width = field.shape
+    chunks = width // SUB
+    spread_columns(spread, lambda a: a, field[...])
+    cols_ref[...] = jnp.zeros_like(cols_ref)
+
+    def block(a, at):
+        code, low, high = inner_range(meta, below, a)
+
+        def pair(j, carry):
+            at, sums = carry
+            n = a + offsets[code, j]
+            value = field[pl.ds(n, 1), :]
+            down = jnp.zeros((SUB, width), jnp.float32)
+            after = []
+            for c in range(chunks):
+                here = slice(c * SUB, (c + 1) * SUB)
+                tile = tiles[at, here, :]
+                down = down + tile * spread[a, here, :]
+                after.append(sums[c] + tile * value)
+            there = pl.ds(pl.multiple_of(n * SUB, SUB), SUB)
+            cols_ref[there, :] = cols_ref[there, :] + down
+            return at + 1, tuple(after)
+
+        zero = jnp.zeros((SUB, width), jnp.float32)
+        at, sums = lax.fori_loop(low, high, pair, (at, (zero,) * chunks))
+        value = field[pl.ds(a, 1), :]
+        for c in range(chunks):
+            here = slice(c * SUB, (c + 1) * SUB)
+            rows_ref[a, here, :] = sums[c] + tiles[at, here, :] * value
+        return at + 1
+
+    lax.fori_loop(0, meta[0], block, 0)
+
+
+def apply_outer(meta, offsets, below, received, tiles, rows_ref, cols_ref, hood):
+    heres = received
+    columns = len(heres)
+    share, width = heres[0].shape
+    chunks = width // SUB
+    base, filled = meta[3], meta[4]
+    for k, ref in enumerate(heres):
+        hood[k * share : (k + 1) * share, :] = ref[...]
+    column = lax.div(base, share)
+    last = columns - 2
+    edge = share + filled - base
+    before_at = jnp.where(column == 0, meta[5] - 2 * share, last * share)
+    after_at = (last + 1) * share - 2 * share
+    head_at = jnp.where(column == last + 1, (last + 1) * share, (column - 1) * share) - edge
+
+    def block(a, at):
+        code, (low, high), (low_next, high_next) = outer_ranges(meta, below, a)
+
+        def pair(j, carry):
+            at, sums = carry
+            w = share + a + offsets[code, j]
+            row = w + jnp.where(w < share, before_at, jnp.where(w < edge, after_at, head_at))
+            value = hood[pl.ds(row, 1), :]
+            result = []
+            for c in range(chunks):
+                here = slice(c * SUB, (c + 1) * SUB)
+                result.append(sums[c] + tiles[at, here, :] * value)
+            return at + 1, tuple(result)
+
+        start = tuple(rows_ref[a, c * SUB : (c + 1) * SUB, :] for c in range(chunks))
+        carry = lax.fori_loop(low, high, pair, (at, start))
+        at, sums = lax.fori_loop(low_next, high_next, pair, carry)
+        for c in range(chunks):
+            rows_ref[a, c * SUB : (c + 1) * SUB, :] = sums[c]
+        return at
+
+    lax.fori_loop(0, meta[0], block, 0)
+    return totals(meta[0], rows_ref, cols_ref, share, width)
+
+
+def build_inner_kernel(meta, offsets, below, position, density, tiles, spread, rows_ref, cols_ref, weight):
+    build_inner(meta, offsets, below, position, density, tiles, spread, rows_ref, cols_ref, weight)
+
+
+def apply_first_kernel(
+    meta, offsets, below, right_side, precond, diagonal, *rest
+):
+    *received, tiles, rows_ref, cols_ref, spill_ref, scaled_ref, work, hood = rest
+    work[...] = rows_ref[...]
+    spill = apply_outer(meta, offsets, below, received, tiles, work, cols_ref, hood)
+    spill_ref[...] = spill
+    scaled_ref[...] = spill / diagonal[...]
+
+
+def apply_second_kernel(
+    meta, offsets, below, listed, right_side, precond, spill, scaled, *rest
+):
+    *received, tiles, rows_ref, cols_ref, twice_ref, sums_ref, work, hood = rest
+    work[...] = rows_ref[...]
+    twice = apply_outer(meta, offsets, below, received, tiles, work, cols_ref, hood)
+    twice_ref[...] = twice
+    share, width = twice.shape
+    alive = lax.broadcasted_iota(jnp.int32, (share, width), 0) < meta[0]
+    source = jnp.where(alive, right_side[...], 0.0)
+    lane = lax.broadcasted_iota(jnp.int32, (1, width), 1)
+    sums = jnp.where(lane == 4, listed[0], 0.0)
+    pairs = ((source, precond[...]), (spill[...], precond[...]), (spill[...], scaled[...]), (scaled[...], twice))
+    for k, (first, second) in enumerate(pairs):
+        along = jnp.sum(first * second, axis=0, keepdims=True)
+        sums = jnp.where(lane == k, jnp.sum(along, axis=1, keepdims=True), sums)
+    sums_ref[...] = jnp.broadcast_to(sums, (SUB, width))
+
+
+def finish_kernel(meta, right_side, precond, diagonal, spill, scaled, twice, mine, other, solution_ref, residual_ref, count_ref):
+    share, width = precond.shape
+    sums = mine[...] + other[...]
+    count_ref[...] = sums
+
+    def pick(k):
+        return sums[0:1, k : k + 1]
+
+    weighted, cross, square, last = pick(0), pick(1), pick(2), pick(3)
+    part = cross / weighted
+    advance = 1.0 / (1.0 - part)
+    keep = -part * advance
+    weighted_next = advance * advance * (square - cross * part)
+    bent = keep * keep * cross + 2.0 * keep * advance * square + advance * advance * last
+    blend = weighted_next / weighted
+    advance_next = weighted_next / (weighted_next - bent - blend * weighted_next / advance)
+    alive = lax.broadcasted_iota(jnp.int32, (share, width), 0) < meta[0]
+    source = jnp.where(alive, right_side[...], 0.0)
+    residual = keep * source + advance * spill[...]
+    next_precond = keep * precond[...] + advance * scaled[...]
+    direction = next_precond + blend * precond[...]
+    image = residual - keep * spill[...] - advance * twice[...] + blend * (source - spill[...])
+    solution_ref[...] = advance * precond[...] + advance_next * direction
+    residual_ref[...] = residual - advance_next * image
+
+
+def cost(pairs, each):
+    return pl.CostEstimate(flops=pairs * each, bytes_accessed=pairs * 4, transcendentals=0)
+
+
+def held(array):
+    return pltpu.with_memory_space_constraint(array, pltpu.VMEM)
+
+
+def body(positions, phase, neighbours, counts, phase_density, right_side):
+    capacity, width = phase.shape
+    columns = lax.axis_size("col")
+    pieces = lax.axis_size("piece")
+    share = capacity // columns
+    piece = lax.axis_index("piece")
+    column = lax.axis_index("col")
+    density = fetch_phase_density(phase, phase_density)
+    state = jnp.concatenate([positions, density[None]], 0)
+    filled = counts[piece]
+    onward = [(i, i + 1) for i in range(pieces - 1)]
+    back = [(i + 1, i) for i in range(pieces - 1)]
+    tail = lax.dynamic_slice_in_dim(state, filled - share, share, 1)
+    before = lax.ppermute(tail, "piece", onward)
+    after = lax.ppermute(state[:, :share], "piece", back)
+
+    ranks = jnp.arange(pieces, dtype=jnp.int32)
+    live = jnp.clip(filled - column * share, 0, share)
+    first = jnp.sum(jnp.where(ranks < piece, counts, 0)) + column * share
+    total = jnp.sum(counts)
+    ahead = counts[jnp.maximum(piece - 1, 0)]
+    meta = jnp.stack([live, first, total, column * share, filled, ahead]).astype(jnp.int32)
+    slots = piece * capacity + jnp.arange(capacity, dtype=jnp.int32)
+    listed = jnp.sum((neighbours == slots[:, None]).astype(jnp.float32)).reshape(1)
+
+    offsets, below = jnp.asarray(OFFSETS), jnp.asarray(BELOW)
+    most_inner, most_outer = tile_bounds(share)
+    vector = jax.ShapeDtypeStruct((share, width), jnp.float32)
+    inner_tiles = pltpu.VMEM((most_inner, width, width), jnp.float32)
+    outer_tiles = pltpu.VMEM((most_outer, width, width), jnp.float32)
+    square = pltpu.VMEM((share, width, width), jnp.float32)
+    narrow = pltpu.VMEM((share * SUB, width), jnp.float32)
+    params = pltpu.CompilerParams(vmem_limit_bytes=16 * 1024 * 1024)
+    tables = [SMEM] * 3
+
+    tiles_in, spread, rows, cols = pl.pallas_call(
+        build_inner_kernel,
+        out_shape=[inner_tiles, pltpu.VMEM((share, 4, width, width), jnp.float32), square, narrow],
+        in_specs=tables + [VMEM] * 2,
+        out_specs=[VMEM] * 4,
+        scratch_shapes=[pltpu.VMEM((capacity, width), jnp.float32)],
+        compiler_params=params,
+        cost_estimate=cost(most_inner * width * width, 16),
+        name="build_inner",
+    )(meta, offsets, below, positions, density)
+
+    def build_outer_kernel(*refs):
+        (m, o, b, position, dens, bef, aft, rhs, spr, rows_in, cols_in, tiles, diag, prec, hood, work) = refs
+        work[...] = rows_in[...]
+        build_outer(m, o, b, position, dens, bef, aft, rhs, spr, work, cols_in, tiles, diag, prec, hood)
+
+    tiles_out, diagonal, precond = pl.pallas_call(
+        build_outer_kernel,
+        out_shape=[outer_tiles, vector, vector],
+        in_specs=tables + [VMEM] * 8,
+        out_specs=[VMEM] * 3,
+        scratch_shapes=[
+            pltpu.VMEM((4, capacity + 2 * share, width), jnp.float32),
+            pltpu.VMEM((share, width, width), jnp.float32),
+        ],
+        compiler_params=params,
+        cost_estimate=cost(most_outer * width * width, 16),
+        name="build_outer",
+    )(meta, offsets, below, positions, density, before, after, right_side, held(spread), held(rows), held(cols))
+
+    def inner(field):
+        return pl.pallas_call(
+            apply_inner,
+            out_shape=[square, narrow],
+            in_specs=tables + [VMEM] * 2,
+            out_specs=[VMEM] * 2,
+            scratch_shapes=[pltpu.VMEM((share, width, width), jnp.float32)],
+            compiler_params=params,
+            cost_estimate=cost(most_inner * width * width, 4),
+            name="apply_inner",
+        )(meta, offsets, below, field, held(tiles_in))
+
+    def exchange(field):
+        count = pieces * columns
+        axes = ("piece", "col")
+        received = []
+        for c in range(1, columns - 1):
+            pairs = []
+            for p in range(pieces - 1):
+                low, high = p * columns + c, (p + 1) * columns
+                pairs += [(low, high), (high, low)]
+            received.append(lax.ppermute(field, axes, pairs))
+        received.append(lax.ppermute(field, axes, [(i, i + 1) for i in range(count - 1)]))
+        received.append(lax.ppermute(field, axes, [(i + 1, i) for i in range(count - 1)]))
+        return received
+
+    outer_scratch = [
+        pltpu.VMEM((share, width, width), jnp.float32),
+        pltpu.VMEM((columns * share, width), jnp.float32),
+    ]
+    outer_cost = cost(most_outer * width * width, 2)
+
+    received = exchange(precond)
+    rows, cols = inner(precond)
+    spill, scaled = pl.pallas_call(
+        apply_first_kernel,
+        out_shape=[vector, vector],
+        in_specs=tables + [VMEM] * (3 + columns + 3),
+        out_specs=[VMEM] * 2,
+        scratch_shapes=outer_scratch,
+        compiler_params=params,
+        cost_estimate=outer_cost,
+        name="apply_first",
+    )(meta, offsets, below, right_side, precond, diagonal, *received, held(tiles_out), held(rows), held(cols))
+
+    received = exchange(scaled)
+    rows, cols = inner(scaled)
+    twice, sums = pl.pallas_call(
+        apply_second_kernel,
+        out_shape=[vector, jax.ShapeDtypeStruct((SUB, width), jnp.float32)],
+        in_specs=tables + [SMEM] + [VMEM] * (4 + columns + 3),
+        out_specs=[VMEM] * 2,
+        scratch_shapes=outer_scratch,
+        compiler_params=params,
+        cost_estimate=outer_cost,
+        name="apply_second",
+    )(meta, offsets, below, listed, right_side, precond, spill, scaled, *received, held(tiles_out), held(rows), held(cols))
+
+    steps = [("col", 1 << k) for k in range(columns.bit_length() - 1)]
+    steps += [("piece", 1 << k) for k in range(pieces.bit_length() - 1)]
+    other = jnp.zeros_like(sums)
+    for axis, step in steps:
+        sums = sums + other
+        other = lax.ppermute(sums, axis, [(i, i ^ step) for i in range(lax.axis_size(axis))])
+
+    solution_field, residual, count = pl.pallas_call(
+        finish_kernel,
+        out_shape=[vector, vector, jax.ShapeDtypeStruct((SUB, width), jnp.float32)],
+        in_specs=[SMEM] + [VMEM] * 8,
+        out_specs=[VMEM] * 3,
+        name="finish",
+    )(meta, right_side, precond, diagonal, spill, scaled, twice, sums, other)
+    return lax.cond(
+        count[0, 4] == total.astype(jnp.float32),
+        lambda: (solution_field, residual),
+        lambda: literal(positions, phase, neighbours, counts, phase_density, right_side),
+    )
+
+
 def solution(mesh):
     placed = (
         P(None, "piece", None),

time: 993 us -> 145 us (0.15)
  matrix products: 488 us -> 0 us
  local copies, waits for them, and re-layouts: 236 us -> 18.5 us
  blocking collectives: 104 us -> 0 us
  waiting for transfers between devices: 76.8 us -> 9.79 us
  Pallas kernels: 0 us -> 46.9 us
  loops' own time: 44.4 us -> 0.23 us
  starting transfers between devices: 9.33 us -> 47.1 us
    dot_general x168 -> x0, matrix products: 488 us -> none  [pair_term(): jnp.einsum('gij,gj->gi', tile, remote, precision=lax.Precision.HIGHEST)]
    gather x336 -> x0, local copies, waits for them, and re-layouts: 195 us -> none  [the longest x168 101 us: pair_term(): other = hood_state[:, where_at]]
    psum x2 -> x0, blocking collectives: 77.4 us -> none  [paired_sums(): lax.psum((inner(first, second), inner(second, third)), ('piece', 'col'))]
    reduce_scatter x3 -> x0, waiting for transfers between devices: 65.1 us -> none  [totals(): return lax.psum_scatter(part_sum, 'col', scatter_dimension=0, tiled=True)]
    pallas_call x0 -> x7, Pallas kernels: none -> 46.9 us  [the longest x1 15.6 us: body(): pl.pallas_call(build_inner_kernel, out_shape=[inner_tiles, pltpu.VMEM((sh...]
    another operation x3 -> x1, loops' own time: 44.4 us -> 0.23 us  [body(): lax.cond(count[0, 4] == total.astype(jnp.float32), lambda: (solution_fiel...]
    ppermute x6 -> x15, starting transfers between devices: 9.21 us -> 47.1 us  [the longest x2 22.3 us: exchange(): lax.ppermute(field, axes, [(i, i + 1) for i in range(count - 1)])]
    all_gather x2 -> x0, blocking collectives: 26.3 us -> none  [hood_of(): return surround(lax.all_gather(column_vector, 'col', axis=0, tiled=True))]
  transfers between devices with their start and end apart: 9 -> 15, of which waited for: 6 -> 5; matrix products, arithmetic and copies ran while one was open for 0% -> 3% of each run, Pallas kernels for 0% -> 19%
where the time goes in v1:
time: 145 us
  starting transfers between devices  47.1 us (32%)
  Pallas kernels  46.9 us (32%)
  local copies, waits for them, and re-layouts  18.5 us (13%)
  between operations  18.2 us (13%)
  waiting for transfers between devices  9.79 us (7%)
  other arithmetic  3.76 us (3%)
    ppermute x2, starting transfers between devices, exchange(): lax.ppermute(field, axes, [(i, i + 1) for i in range(count - 1)])  22.3 us
    pallas_call x1, Pallas kernels, body(): pl.pallas_call(build_inner_kernel, out_shape=[inner_tiles, pltpu.VMEM((sh...  15.6 us
    ppermute x5, starting transfers between devices, body(): lax.ppermute(sums, axis, [(i, i ^ step) for i in range(lax.axis_size(axis...  15.2 us
    unnamed x40, local copies, waits for them, and re-layouts  13.9 us
    pallas_call x2, Pallas kernels, inner(): pl.pallas_call(apply_inner, out_shape=[square, narrow], in_specs=tables +...  12.5 us
    ppermute x5, waiting for transfers between devices, body(): lax.ppermute(sums, axis, [(i, i ^ step) for i in range(lax.axis_size(axis...  9.76 us
    pallas_call x1, Pallas kernels, body(): pl.pallas_call(build_outer_kernel, out_shape=[outer_tiles, vector, vector...  8.17 us
    pallas_call x1, Pallas kernels, body(): pl.pallas_call(apply_second_kernel, out_shape=[vector, jax.ShapeDtypeStru...  4.97 us
  transfers between devices with their start and end apart: 15, of which 5 were waited for; matrix products, arithmetic and copies ran while one was open for 3% of the time, Pallas kernels for 19%

profile of v1, /device:TPU:0, one launch (start us, length us, event | category | flops | bytes accessed | tf_op | source)
XLA Modules:
  0.0 144.5 jit_solution(18388261523517308403)
XLA Ops:
  7.2 1.3 fusion.949
  9.8 1.0 select_reduce_fusion.1.density.refs_4_
  10.8 0.8 pad_maximum_fusion.4
  11.6 1.3 collective-permute-start.7
  12.9 3.0 %collective-permute-start.6 = (f32[4,32,128]{2,1,0:T(8,128)S(1)}, f32[4,32,128]{2,1,0:T(8,128)S(1)}, u32[]{:S(2)}, u32[]{:S(2)}) collective-permute-start(f32[4,32,128]{2,1,0:T(8,128)S(1)} %get-tuple-element.616), channel_id=1, source_target_pairs={{0,4},{4,8},{8,12},{12,16},{16,20},{20,24},{24,28},{1,5},{5,9},{9,... | collective-permute-start | bytes 196616 | tf_op jit(solution)/shard_map/ppermute | solution.py:497
  16.6 1.3 fusion.927
  18.5 2.0 %stack.19.meta.refs_0_ = s32[6]{0:T(128)S(1)} concatenate(s32[1]{0:T(128)} %bitcast.253, s32[1]{0:T(128)} %bitcast.254, s32[1]{0:T(128)} %bitcast.255, s32[1]{0:T(128)} %bitcast.256, s32[1]{0:T(128)} %get-tuple-element.618, s32[1]{0:T(128)} %get-tuple-element.617), dimensions={0} | concatenate | bytes 48 | tf_op jit(solution)/shard_map/stack | solution.py:505
  20.5 0.7 copy-done.2
  21.2 0.7 copy-done.3
  21.9 15.6 %build_inner.1 = (f32[216,128,128]{2,1,0:T(8,128)S(1)}, f32[32,4,128,128]{3,2,1,0:T(8,128)S(1)}, f32[32,128,128]{2,1,0:T(8,128)S(1)}, f32[256,128]{1,0:T(8,128)S(1)}) custom-call(s32[6]{0:T(128)S(1)} %stack.19.meta.refs_0_, s32[16,27]{1,0:T(8,128)S(1)} %copy-done.3, s32[16,65]{1,0:T(8,128)S(1)} %copy-done.2, f32[3,128,128]{2,1,0:T(8,128)} %refs_3_.1, ...), custom_call_target="tpu_custom_call" | custom-call | flops 56623104 | bytes 14155776 | tf_op jit(solution)/shard_map/build_inner/pallas_call | solution.py:519
  37.5 0.0 copy-start
  37.6 5.0 %copy-done = f32[216,128,128]{2,1,0:T(8,128)} copy-done((f32[216,128,128]{2,1,0:T(8,128)}, f32[216,128,128]{2,1,0:T(8,128)S(1)}, u32[]{:S(2)}) %copy-start) | copy-done | bytes 14155800
  42.6 0.0 collective-permute-done.7.refs_6_
  42.6 0.0 collective-permute-done.6.refs_5_
  42.6 8.2 %build_outer.1 = (f32[222,128,128]{2,1,0:T(8,128)S(1)}, f32[32,128]{1,0:T(8,128)S(1)}, f32[32,128]{1,0:T(8,128)S(1)}) custom-call(s32[6]{0:T(128)S(1)} %stack.19.meta.refs_0_, s32[16,27]{1,0:T(8,128)S(1)} %copy-done.3, s32[16,65]{1,0:T(8,128)S(1)} %copy-done.2, f32[3,128,128]{2,1,0:T(8,128)} %refs_3_.1, f32[128,128]{1,0:T(8,128)S(1)} %select_reduce_fusion.1.density.refs_4_, ...), custom_call_target="tpu_custom_call" | custom-call | flops 58195968 | bytes 14548992 | tf_op jit(solution)/shard_map/build_outer/pallas_call | solution.py:535
  50.8 0.0 copy-start.6
  50.8 0.0 copy-start.4
  50.8 1.3 collective-permute-start.11
  52.1 10.9 %collective-permute-start.10 = (f32[32,128]{1,0:T(8,128)S(1)}, f32[32,128]{1,0:T(8,128)S(1)}, u32[]{:S(2)}, u32[]{:S(2)}) collective-permute-start(f32[32,128]{1,0:T(8,128)S(1)} %get-tuple-element.355.field.precond), channel_id=1, source_target_pairs={{0,1},{1,2},{2,3},{3,4},{4,5},{5,6},{6,7},{7,8},{8,9},{9,10},{10,1... | collective-permute-start | bytes 49160 | tf_op jit(solution)/shard_map/ppermute | solution.py:571
  63.1 0.7 collective-permute-start.9
  63.7 0.7 collective-permute-start.8
  64.4 5.0 %copy-done.1 = f32[216,128,128]{2,1,0:T(8,128)S(1)} copy-done((f32[216,128,128]{2,1,0:T(8,128)S(1)}, f32[216,128,128]{2,1,0:T(8,128)}, u32[]{:S(2)}) %copy-start.1) | copy-done | bytes 14155800
  69.4 6.3 %apply_inner.2 = (f32[32,128,128]{2,1,0:T(8,128)S(1)}, f32[256,128]{1,0:T(8,128)S(1)}) custom-call(s32[6]{0:T(128)S(1)} %stack.19.meta.refs_0_, s32[16,27]{1,0:T(8,128)S(1)} %copy-done.3, s32[16,65]{1,0:T(8,128)S(1)} %copy-done.2, f32[32,128]{1,0:T(8,128)S(1)} %get-tuple-element.355.field.precond, f32[216,128,128]{2,1,0:T(8,128)S(1)} %copy-done.1), custom_call_target="tpu_custom_call" | custom-call | flops 14155776 | bytes 14155776 | tf_op jit(solution)/shard_map/apply_inner/pallas_call | solution.py:550
  75.7 0.0 collective-permute-done.11.rest_3_
  75.7 0.0 collective-permute-done.10.rest_2_
  75.7 0.0 collective-permute-done.9.rest_1_
  75.7 0.0 collective-permute-done.8.rest_0_
  75.8 0.0 copy-start.12
  75.8 4.2 %apply_first.1 = (f32[32,128]{1,0:T(8,128)S(1)}, f32[32,128]{1,0:T(8,128)S(1)}) custom-call(s32[6]{0:T(128)S(1)} %stack.19.meta.refs_0_, s32[16,27]{1,0:T(8,128)S(1)} %copy-done.3, s32[16,65]{1,0:T(8,128)S(1)} %copy-done.2, f32[32,128]{1,0:T(8,128)S(1)} %copy-done.11, f32[32,128]{1,0:T(8,128)S(1)} %get-tuple-element.355.field.precond, ...), custom_call_target="tpu_custom_call" | custom-call | flops 7274496 | bytes 14548992 | tf_op jit(solution)/shard_map/apply_first/pallas_call | solution.py:583
  80.0 1.3 collective-permute-start.15
  81.3 11.4 %collective-permute-start.14 = (f32[32,128]{1,0:T(8,128)S(1)}, f32[32,128]{1,0:T(8,128)S(1)}, u32[]{:S(2)}, u32[]{:S(2)}) collective-permute-start(f32[32,128]{1,0:T(8,128)S(1)} %get-tuple-element.362.field.scaled), channel_id=1, source_target_pairs={{0,1},{1,2},{2,3},{3,4},{4,5},{5,6},{6,7},{7,8},{8,9},{9,10},{10,1... | collective-permute-start | bytes 49160 | tf_op jit(solution)/shard_map/ppermute | solution.py:571
  92.7 0.7 collective-permute-start.13
  93.4 0.7 collective-permute-start.12
  94.0 0.0 copy-done.12
  94.0 0.6 convert_reduce_fusion
  94.7 6.3 %apply_inner.3 = (f32[32,128,128]{2,1,0:T(8,128)S(1)}, f32[256,128]{1,0:T(8,128)S(1)}) custom-call(s32[6]{0:T(128)S(1)} %stack.19.meta.refs_0_, s32[16,27]{1,0:T(8,128)S(1)} %copy-done.3, s32[16,65]{1,0:T(8,128)S(1)} %copy-done.2, f32[32,128]{1,0:T(8,128)S(1)} %get-tuple-element.362.field.scaled, f32[216,128,128]{2,1,0:T(8,128)S(1)} %copy-done.1), custom_call_target="tpu_custom_call" | custom-call | flops 14155776 | bytes 14155776 | tf_op jit(solution)/shard_map/apply_inner/pallas_call | solution.py:550
  100.9 0.0 collective-permute-done.15.rest_3_
  100.9 0.0 collective-permute-done.14.rest_2_
  100.9 0.0 collective-permute-done.13.rest_1_
  101.0 0.0 collective-permute-done.12.rest_0_
  101.0 0.0 copy-start.10
  101.0 0.0 copy-start.13
  101.0 0.0 copy-start.18
  101.0 0.0 copy-start.20
  101.0 5.0 %apply_second.1 = (f32[32,128]{1,0:T(8,128)S(1)}, f32[8,128]{1,0:T(8,128)S(1)}) custom-call(s32[6]{0:T(128)S(1)} %stack.19.meta.refs_0_, s32[16,27]{1,0:T(8,128)S(1)} %copy-done.3, s32[16,65]{1,0:T(8,128)S(1)} %copy-done.2, f32[1]{0:T(128)} %bitcast.258.listed, f32[32,128]{1,0:T(8,128)S(1)} %copy-done.11, f32[32,128]{1,0:T(8,128)S(1)} %get-tuple-element.355.field.precond, ...), custom_call_target="tpu_custom_call" | custom-call | flops 7274496 | bytes 14548992 | tf_op jit(solution)/shard_map/apply_second/pallas_call | solution.py:596
  106.0 0.6 copy-done.9
  106.6 7.3 %collective-permute-start.16 = (f32[8,128]{1,0:T(8,128)S(1)}, f32[8,128]{1,0:T(8,128)S(1)}, u32[]{:S(2)}, u32[]{:S(2)}) collective-permute-start(f32[8,128]{1,0:T(8,128)S(1)} %get-tuple-element.366), channel_id=1, source_target_pairs={{0,1},{1,0},{2,3},{3,2},{4,5},{5,4},{6,7},{7,6},{8,9},{9,8},{10,11... | collective-permute-start | bytes 12296 | tf_op jit(solution)/shard_map/ppermute | solution.py:612
  113.9 1.6 %collective-permute-done.16 = f32[8,128]{1,0:T(8,128)S(1)} collective-permute-done((f32[8,128]{1,0:T(8,128)S(1)}, f32[8,128]{1,0:T(8,128)S(1)}, u32[]{:S(2)}, u32[]{:S(2)}) %collective-permute-start.16) | collective-permute-done | bytes 4128 | tf_op jit(solution)/shard_map/ppermute | solution.py:612
  115.5 0.0 collective-permute-start.17
  115.5 4.5 %collective-permute-done.17 = f32[8,128]{1,0:T(8,128)S(1)} collective-permute-done((f32[8,128]{1,0:T(8,128)S(1)}, f32[8,128]{1,0:T(8,128)S(1)}, u32[]{:S(2)}, u32[]{:S(2)}) %collective-permute-start.17) | collective-permute-done | bytes 4128 | tf_op jit(solution)/shard_map/ppermute | solution.py:612
  120.0 0.0 collective-permute-start.18
  120.0 1.2 collective-permute-done.18
  121.2 4.6 %collective-permute-start.19 = (f32[8,128]{1,0:T(8,128)S(1)}, f32[8,128]{1,0:T(8,128)S(1)}, u32[]{:S(2)}, u32[]{:S(2)}) collective-permute-start(f32[8,128]{1,0:T(8,128)S(1)} %add.1213), channel_id=1, source_target_pairs={{0,8},{4,12},{8,0},{12,4},{16,24},{20,28},{24,16},{28,20},{1,9},{5... | collective-permute-start | bytes 12296 | tf_op jit(solution)/shard_map/ppermute | solution.py:612
  125.8 1.6 %collective-permute-done.19 = f32[8,128]{1,0:T(8,128)S(1)} collective-permute-done((f32[8,128]{1,0:T(8,128)S(1)}, f32[8,128]{1,0:T(8,128)S(1)}, u32[]{:S(2)}, u32[]{:S(2)}) %collective-permute-start.19) | collective-permute-done | bytes 4128 | tf_op jit(solution)/shard_map/ppermute | solution.py:612
  127.4 3.3 %collective-permute-start.20 = (f32[8,128]{1,0:T(8,128)S(1)}, f32[8,128]{1,0:T(8,128)S(1)}, u32[]{:S(2)}, u32[]{:S(2)}) collective-permute-start(f32[8,128]{1,0:T(8,128)S(1)} %add.1214.mine), channel_id=1, source_target_pairs={{0,16},{4,20},{8,24},{12,28},{16,0},{20,4},{24,8},{28,12},{1,17},{... | collective-permute-start | bytes 12296 | tf_op jit(solution)/shard_map/ppermute | solution.py:612
  131.3 0.9 collective-permute-done.20.other
  132.3 0.0 copy-done.17
  132.3 0.6 copy-done.19
  132.9 1.4 finish.1
  134.3 1.3 slice.631
  136.2 0.2 conditional.1
  136.5 0.0 copy-start.21
  136.5 0.6 copy-done.21
  137.1 0.6 copy-done.22
  (26 shorter events, 0.1 us)
Async XLA Ops:
  11.6 31.0 %collective-permute-start.7 = (f32[4,32,128]{2,1,0:T(8,128)S(1)}, f32[4,32,128]{2,1,0:T(8,128)S(1)}, u32[]{:S(2)}, u32[]{:S(2)}) collective-permute-start(f32[4,32,128]{2,1,0:T(8,128)S(1)} %get-tuple-element.615), channel_id=1, source_target_pairs={{4,0},{8,4},{12,8},{16,12},{20,16},{24,20},{28,24},{5,1},{9,5},{13... | collective-permute-start | bytes 196616 | tf_op jit(solution)/shard_map/ppermute | solution.py:498
  12.9 29.7 %collective-permute-start.6 = (f32[4,32,128]{2,1,0:T(8,128)S(1)}, f32[4,32,128]{2,1,0:T(8,128)S(1)}, u32[]{:S(2)}, u32[]{:S(2)}) collective-permute-start(f32[4,32,128]{2,1,0:T(8,128)S(1)} %get-tuple-element.616), channel_id=1, source_target_pairs={{0,4},{4,8},{8,12},{12,16},{16,20},{20,24},{24,28},{1,5},{5,9},{9,... | collective-permute-start | bytes 196616 | tf_op jit(solution)/shard_map/ppermute | solution.py:497
  20.5 0.7 copy-start.2
  21.2 0.7 copy-start.3
  21.9 79.1 %copy-start.8 = (s32[6]{0:T(128)}, s32[6]{0:T(128)S(1)}, u32[]{:S(2)}) copy-start(s32[6]{0:T(128)S(1)} %stack.19.meta.refs_0_) | copy-start | bytes 76
  37.5 5.1 %copy-start = (f32[216,128,128]{2,1,0:T(8,128)}, f32[216,128,128]{2,1,0:T(8,128)S(1)}, u32[]{:S(2)}) copy-start(f32[216,128,128]{2,1,0:T(8,128)S(1)} %get-tuple-element.358.tiles) | copy-start | bytes 42467332
  42.6 33.1 %copy-start.11 = (f32[32,128]{1,0:T(8,128)S(1)}, f32[32,128]{1,0:T(8,128)}, u32[]{:S(2)}) copy-start(f32[32,128]{1,0:T(8,128)} %right_side.5) | copy-start | bytes 49156
  50.8 29.2 %copy-start.6 = (f32[32,128]{1,0:T(8,128)}, f32[32,128]{1,0:T(8,128)S(1)}, u32[]{:S(2)}) copy-start(f32[32,128]{1,0:T(8,128)S(1)} %get-tuple-element.356.diagonal) | copy-start | bytes 49156
  50.8 50.2 %copy-start.4 = (f32[32,128]{1,0:T(8,128)}, f32[32,128]{1,0:T(8,128)S(1)}, u32[]{:S(2)}) copy-start(f32[32,128]{1,0:T(8,128)S(1)} %get-tuple-element.355.field.precond) | copy-start | bytes 49156
  50.8 24.9 %collective-permute-start.11 = (f32[32,128]{1,0:T(8,128)S(1)}, f32[32,128]{1,0:T(8,128)S(1)}, u32[]{:S(2)}, u32[]{:S(2)}) collective-permute-start(f32[32,128]{1,0:T(8,128)S(1)} %get-tuple-element.355.field.precond), channel_id=1, source_target_pairs={{1,0},{2,1},{3,2},{4,3},{5,4},{6,5},{7,6},{8,7},{9,8},{10,9},{11,1... | collective-permute-start | bytes 49160 | tf_op jit(solution)/shard_map/ppermute | solution.py:572
  52.1 23.6 %collective-permute-start.10 = (f32[32,128]{1,0:T(8,128)S(1)}, f32[32,128]{1,0:T(8,128)S(1)}, u32[]{:S(2)}, u32[]{:S(2)}) collective-permute-start(f32[32,128]{1,0:T(8,128)S(1)} %get-tuple-element.355.field.precond), channel_id=1, source_target_pairs={{0,1},{1,2},{2,3},{3,4},{4,5},{5,6},{6,7},{7,8},{8,9},{9,10},{10,1... | collective-permute-start | bytes 49160 | tf_op jit(solution)/shard_map/ppermute | solution.py:571
  63.1 12.7 %collective-permute-start.9 = (f32[32,128]{1,0:T(8,128)S(1)}, f32[32,128]{1,0:T(8,128)S(1)}, u32[]{:S(2)}, u32[]{:S(2)}) collective-permute-start(f32[32,128]{1,0:T(8,128)S(1)} %get-tuple-element.355.field.precond), channel_id=1, source_target_pairs={{2,4},{4,2},{6,8},{8,6},{10,12},{12,10},{14,16},{16,14},{18,20},{2... | collective-permute-start | bytes 49160 | tf_op jit(solution)/shard_map/ppermute | solution.py:570
  63.7 12.0 %collective-permute-start.8 = (f32[32,128]{1,0:T(8,128)S(1)}, f32[32,128]{1,0:T(8,128)S(1)}, u32[]{:S(2)}, u32[]{:S(2)}) collective-permute-start(f32[32,128]{1,0:T(8,128)S(1)} %get-tuple-element.355.field.precond), channel_id=1, source_target_pairs={{1,4},{4,1},{5,8},{8,5},{9,12},{12,9},{13,16},{16,13},{17,20},{20,... | collective-permute-start | bytes 49160 | tf_op jit(solution)/shard_map/ppermute | solution.py:570
  64.4 5.0 %copy-start.1 = (f32[216,128,128]{2,1,0:T(8,128)S(1)}, f32[216,128,128]{2,1,0:T(8,128)}, u32[]{:S(2)}) copy-start(f32[216,128,128]{2,1,0:T(8,128)} %copy-done) | copy-start | bytes 42467332
  75.8 18.3 %copy-start.12 = (s32[128,7]{0,1:T(8,128)S(1)}, s32[128,7]{0,1:T(8,128)}, u32[]{:S(2)}) copy-start(s32[128,7]{0,1:T(8,128)} %param.18) | copy-start | bytes 10756
  80.0 26.0 %copy-start.5 = (f32[32,128]{1,0:T(8,128)}, f32[32,128]{1,0:T(8,128)S(1)}, u32[]{:S(2)}) copy-start(f32[32,128]{1,0:T(8,128)S(1)} %get-tuple-element.362.field.scaled) | copy-start | bytes 49156
  80.0 26.0 %copy-start.7 = (f32[32,128]{1,0:T(8,128)}, f32[32,128]{1,0:T(8,128)S(1)}, u32[]{:S(2)}) copy-start(f32[32,128]{1,0:T(8,128)S(1)} %get-tuple-element.361.spill) | copy-start | bytes 49156
  80.0 20.9 %collective-permute-start.15 = (f32[32,128]{1,0:T(8,128)S(1)}, f32[32,128]{1,0:T(8,128)S(1)}, u32[]{:S(2)}, u32[]{:S(2)}) collective-permute-start(f32[32,128]{1,0:T(8,128)S(1)} %get-tuple-element.362.field.scaled), channel_id=1, source_target_pairs={{1,0},{2,1},{3,2},{4,3},{5,4},{6,5},{7,6},{8,7},{9,8},{10,9},{11,1... | collective-permute-start | bytes 49160 | tf_op jit(solution)/shard_map/ppermute | solution.py:572
  81.3 19.6 %collective-permute-start.14 = (f32[32,128]{1,0:T(8,128)S(1)}, f32[32,128]{1,0:T(8,128)S(1)}, u32[]{:S(2)}, u32[]{:S(2)}) collective-permute-start(f32[32,128]{1,0:T(8,128)S(1)} %get-tuple-element.362.field.scaled), channel_id=1, source_target_pairs={{0,1},{1,2},{2,3},{3,4},{4,5},{5,6},{6,7},{7,8},{8,9},{9,10},{10,1... | collective-permute-start | bytes 49160 | tf_op jit(solution)/shard_map/ppermute | solution.py:571
  92.7 8.3 %collective-permute-start.13 = (f32[32,128]{1,0:T(8,128)S(1)}, f32[32,128]{1,0:T(8,128)S(1)}, u32[]{:S(2)}, u32[]{:S(2)}) collective-permute-start(f32[32,128]{1,0:T(8,128)S(1)} %get-tuple-element.362.field.scaled), channel_id=1, source_target_pairs={{2,4},{4,2},{6,8},{8,6},{10,12},{12,10},{14,16},{16,14},{18,20},{2... | collective-permute-start | bytes 49160 | tf_op jit(solution)/shard_map/ppermute | solution.py:570
  93.4 7.6 %collective-permute-start.12 = (f32[32,128]{1,0:T(8,128)S(1)}, f32[32,128]{1,0:T(8,128)S(1)}, u32[]{:S(2)}, u32[]{:S(2)}) collective-permute-start(f32[32,128]{1,0:T(8,128)S(1)} %get-tuple-element.362.field.scaled), channel_id=1, source_target_pairs={{1,4},{4,1},{5,8},{8,5},{9,12},{12,9},{13,16},{16,13},{17,20},{20,... | collective-permute-start | bytes 49160 | tf_op jit(solution)/shard_map/ppermute | solution.py:570
  101.0 35.2 %copy-start.10 = (f32[3,128,128]{2,1,0:T(8,128)S(1)}, f32[3,128,128]{2,1,0:T(8,128)}, u32[]{:S(2)}) copy-start(f32[3,128,128]{2,1,0:T(8,128)} %refs_3_.1) | copy-start | bytes 589828
  101.0 35.2 %copy-start.13 = (s32[128,128]{1,0:T(8,128)S(1)}, s32[128,128]{1,0:T(8,128)}, u32[]{:S(2)}) copy-start(s32[128,128]{1,0:T(8,128)} %param.17) | copy-start | bytes 196612
  101.0 35.2 %copy-start.18 = (s32[8]{0:T(128)S(1)}, s32[8]{0:T(128)}, u32[]{:S(2)}) copy-start(s32[8]{0:T(128)} %param.19) | copy-start | bytes 100
  101.0 35.2 %copy-start.20 = (f32[3]{0:T(128)S(1)}, f32[3]{0:T(128)}, u32[]{:S(2)}) copy-start(f32[3]{0:T(128)} %param.20) | copy-start | bytes 40
  106.0 0.6 copy-start.9
  106.6 8.9 %collective-permute-start.16 = (f32[8,128]{1,0:T(8,128)S(1)}, f32[8,128]{1,0:T(8,128)S(1)}, u32[]{:S(2)}, u32[]{:S(2)}) collective-permute-start(f32[8,128]{1,0:T(8,128)S(1)} %get-tuple-element.366), channel_id=1, source_target_pairs={{0,1},{1,0},{2,3},{3,2},{4,5},{5,4},{6,7},{7,6},{8,9},{9,8},{10,11... | collective-permute-start | bytes 12296 | tf_op jit(solution)/shard_map/ppermute | solution.py:612
  115.5 4.5 %collective-permute-start.17 = (f32[8,128]{1,0:T(8,128)S(1)}, f32[8,128]{1,0:T(8,128)S(1)}, u32[]{:S(2)}, u32[]{:S(2)}) collective-permute-start(f32[8,128]{1,0:T(8,128)S(1)} %add.1211), channel_id=1, source_target_pairs={{0,2},{1,3},{2,0},{3,1},{4,6},{5,7},{6,4},{7,5},{8,10},{9,11},{10,... | collective-permute-start | bytes 12296 | tf_op jit(solution)/shard_map/ppermute | solution.py:612
  120.0 1.2 collective-permute-start.18
  121.2 6.2 %collective-permute-start.19 = (f32[8,128]{1,0:T(8,128)S(1)}, f32[8,128]{1,0:T(8,128)S(1)}, u32[]{:S(2)}, u32[]{:S(2)}) collective-permute-start(f32[8,128]{1,0:T(8,128)S(1)} %add.1213), channel_id=1, source_target_pairs={{0,8},{4,12},{8,0},{12,4},{16,24},{20,28},{24,16},{28,20},{1,9},{5... | collective-permute-start | bytes 12296 | tf_op jit(solution)/shard_map/ppermute | solution.py:612
  127.4 4.9 %copy-start.17 = (f32[8,128]{1,0:T(8,128)}, f32[8,128]{1,0:T(8,128)S(1)}, u32[]{:S(2)}) copy-start(f32[8,128]{1,0:T(8,128)S(1)} %add.1214.mine) | copy-start | bytes 12292
  127.4 4.9 %collective-permute-start.20 = (f32[8,128]{1,0:T(8,128)S(1)}, f32[8,128]{1,0:T(8,128)S(1)}, u32[]{:S(2)}, u32[]{:S(2)}) collective-permute-start(f32[8,128]{1,0:T(8,128)S(1)} %add.1214.mine), channel_id=1, source_target_pairs={{0,16},{4,20},{8,24},{12,28},{16,0},{20,4},{24,8},{28,12},{1,17},{... | collective-permute-start | bytes 12296 | tf_op jit(solution)/shard_map/ppermute | solution.py:612
  132.3 0.6 copy-start.19
  136.5 0.6 copy-start.21
  137.1 0.6 copy-start.22

commit v2 on v1

--- a/solution.py
+++ b/solution.py
@@ -50,6 +50,9 @@
 
 
 OFFSETS, BELOW = stencil_tables()
+WIDEST = OFFSETS.shape[1]
+TABLE = np.concatenate([OFFSETS, BELOW], 1)
+LIMIT = pltpu.CompilerParams(vmem_limit_bytes=6 * 1024 * 1024)
 
 
 def tile_bounds(share):
@@ -194,19 +197,19 @@
 
 
 def rank(table, code, t):
-    return table[code, jnp.clip(t, -REACH, REACH) + REACH]
-
-
-def inner_range(meta, below, a):
+    return table[code, jnp.clip(t, -REACH, REACH) + REACH + WIDEST]
+
+
+def inner_range(meta, table, a):
     code = lax.rem(meta[1] + a, LAYER)
-    return code, rank(below, code, -a), rank(below, code, 0)
-
-
-def outer_ranges(meta, below, a):
+    return code, rank(table, code, -a), rank(table, code, 0)
+
+
+def outer_ranges(meta, table, a):
     code = lax.rem(meta[1] + a, LAYER)
     place = meta[1] + a
-    before = (rank(below, code, -place), rank(below, code, -a))
-    after = (rank(below, code, meta[0] - a), rank(below, code, meta[2] - place))
+    before = (rank(table, code, -place), rank(table, code, -a))
+    after = (rank(table, code, meta[0] - a), rank(table, code, meta[2] - place))
     return code, before, after
 
 
@@ -241,7 +244,33 @@
     return jnp.where(alive, rows + cols, 0.0)
 
 
-def build_inner(meta, offsets, below, position, density, tiles, spread, rows_ref, cols_ref, weight):
+def prepare(counts, densities, position, phase, meta, density, tail, head):
+    share, width = tail.shape[1:]
+    capacity = phase.shape[0]
+    piece, column = lax.axis_index("piece"), lax.axis_index("col")
+    filled = counts[piece]
+    before = jnp.int32(0)
+    total = jnp.int32(0)
+    for p in range(counts.shape[0]):
+        before = before + jnp.where(p < piece, counts[p], 0)
+        total = total + counts[p]
+    meta[0] = jnp.clip(filled - column * share, 0, share)
+    meta[1] = before + column * share
+    meta[2] = total
+    meta[3] = column * share
+    meta[4] = filled
+    meta[5] = counts[jnp.maximum(piece - 1, 0)]
+    labels = phase[...]
+    density[...] = sum(jnp.where(labels == k, densities[k], 0.0) for k in range(densities.shape[0]))
+    last = pl.ds(filled - share, share)
+    for k in range(3):
+        tail[k] = position[k, last, :]
+        head[k] = position[k, 0:share, :]
+    tail[3] = density[last, :]
+    head[3] = density[0:share, :]
+
+
+def build_inner(meta, table, position, density, tiles, spread, rows_ref, cols_ref, weight):
     share, width = rows_ref.shape[0], rows_ref.shape[2]
     chunks = width // SUB
     base = meta[3]
@@ -257,11 +286,11 @@
         return [position[k, here, :] for k in range(3)] + [weight[here, :]]
 
     def block(a, at):
-        code, low, high = inner_range(meta, below, a)
+        code, low, high = inner_range(meta, table, a)
 
         def pair(j, carry):
             at, sums = carry
-            n = a + offsets[code, j]
+            n = a + table[code, j]
             other = other_rows(base + n)
             down = jnp.zeros((SUB, width), jnp.float32)
             after = []
@@ -292,8 +321,8 @@
 
 
 def build_outer(
-    meta, offsets, below, position, density, before, after, right_side, spread, rows_ref, cols_ref,
-    tiles, diagonal_ref, precond_ref, hood,
+    meta, table, position, density, before, after, right_side, spread, rows_ref, cols_ref,
+    tiles, diagonal_ref, precond_ref, hood, work,
 ):
     share, width = right_side.shape
     chunks = width // SUB
@@ -308,11 +337,11 @@
     edge = share + filled - base
 
     def block(a, at):
-        code, (low, high), (low_next, high_next) = outer_ranges(meta, below, a)
+        code, (low, high), (low_next, high_next) = outer_ranges(meta, table, a)
 
         def pair(j, carry):
             at, sums = carry
-            w = share + a + offsets[code, j]
+            w = share + a + table[code, j]
             row = jnp.where(w < edge, base + w, share + capacity + w - edge)
             here = pl.ds(row, 1)
             other = [hood[k, here, :] for k in range(4)]
@@ -328,29 +357,29 @@
         carry = lax.fori_loop(low, high, pair, (at, start))
         at, sums = lax.fori_loop(low_next, high_next, pair, carry)
         for c in range(chunks):
-            rows_ref[a, c * SUB : (c + 1) * SUB, :] = sums[c]
+            work[a, c * SUB : (c + 1) * SUB, :] = sums[c]
         return at
 
     lax.fori_loop(0, meta[0], block, 0)
     own_rows = pl.ds(pl.multiple_of(base, SUB), share)
     alive = lax.broadcasted_iota(jnp.int32, (share, width), 0) < meta[0]
-    diagonal = 1.0 / density[own_rows, :] + totals(meta[0], rows_ref, cols_ref, share, width)
+    diagonal = 1.0 / density[own_rows, :] + totals(meta[0], work, cols_ref, share, width)
     diagonal_ref[...] = diagonal
     precond_ref[...] = jnp.where(alive, right_side[...], 0.0) / diagonal
 
 
-def apply_inner(meta, offsets, below, field, tiles, rows_ref, cols_ref, spread):
+def apply_inner(meta, table, field, tiles, rows_ref, cols_ref, spread):
     share, width = field.shape
     chunks = width // SUB
     spread_columns(spread, lambda a: a, field[...])
     cols_ref[...] = jnp.zeros_like(cols_ref)
 
     def block(a, at):
-        code, low, high = inner_range(meta, below, a)
+        code, low, high = inner_range(meta, table, a)
 
         def pair(j, carry):
             at, sums = carry
-            n = a + offsets[code, j]
+            n = a + table[code, j]
             value = field[pl.ds(n, 1), :]
             down = jnp.zeros((SUB, width), jnp.float32)
             after = []
@@ -374,13 +403,12 @@
     lax.fori_loop(0, meta[0], block, 0)
 
 
-def apply_outer(meta, offsets, below, received, tiles, rows_ref, cols_ref, hood):
-    heres = received
-    columns = len(heres)
-    share, width = heres[0].shape
+def apply_outer(meta, table, received, tiles, rows_ref, cols_ref, work, hood):
+    columns = len(received)
+    share, width = received[0].shape
     chunks = width // SUB
     base, filled = meta[3], meta[4]
-    for k, ref in enumerate(heres):
+    for k, ref in enumerate(received):
         hood[k * share : (k + 1) * share, :] = ref[...]
     column = lax.div(base, share)
     last = columns - 2
@@ -390,11 +418,11 @@
     head_at = jnp.where(column == last + 1, (last + 1) * share, (column - 1) * share) - edge
 
     def block(a, at):
-        code, (low, high), (low_next, high_next) = outer_ranges(meta, below, a)
+        code, (low, high), (low_next, high_next) = outer_ranges(meta, table, a)
 
         def pair(j, carry):
             at, sums = carry
-            w = share + a + offsets[code, j]
+            w = share + a + table[code, j]
             row = w + jnp.where(w < share, before_at, jnp.where(w < edge, after_at, head_at))
             value = hood[pl.ds(row, 1), :]
             result = []
@@ -407,33 +435,27 @@
         carry = lax.fori_loop(low, high, pair, (at, start))
         at, sums = lax.fori_loop(low_next, high_next, pair, carry)
         for c in range(chunks):
-            rows_ref[a, c * SUB : (c + 1) * SUB, :] = sums[c]
+            work[a, c * SUB : (c + 1) * SUB, :] = sums[c]
         return at
 
     lax.fori_loop(0, meta[0], block, 0)
-    return totals(meta[0], rows_ref, cols_ref, share, width)
-
-
-def build_inner_kernel(meta, offsets, below, position, density, tiles, spread, rows_ref, cols_ref, weight):
-    build_inner(meta, offsets, below, position, density, tiles, spread, rows_ref, cols_ref, weight)
+    return totals(meta[0], work, cols_ref, share, width)
 
 
 def apply_first_kernel(
-    meta, offsets, below, right_side, precond, diagonal, *rest
+    meta, table, right_side, precond, diagonal, *rest
 ):
     *received, tiles, rows_ref, cols_ref, spill_ref, scaled_ref, work, hood = rest
-    work[...] = rows_ref[...]
-    spill = apply_outer(meta, offsets, below, received, tiles, work, cols_ref, hood)
+    spill = apply_outer(meta, table, received, tiles, rows_ref, cols_ref, work, hood)
     spill_ref[...] = spill
     scaled_ref[...] = spill / diagonal[...]
 
 
 def apply_second_kernel(
-    meta, offsets, below, listed, right_side, precond, spill, scaled, *rest
+    meta, table, listed, right_side, precond, spill, scaled, *rest
 ):
     *received, tiles, rows_ref, cols_ref, twice_ref, sums_ref, work, hood = rest
-    work[...] = rows_ref[...]
-    twice = apply_outer(meta, offsets, below, received, tiles, work, cols_ref, hood)
+    twice = apply_outer(meta, table, received, tiles, rows_ref, cols_ref, work, hood)
     twice_ref[...] = twice
     share, width = twice.shape
     alive = lax.broadcasted_iota(jnp.int32, (share, width), 0) < meta[0]
@@ -488,52 +510,45 @@
     share = capacity // columns
     piece = lax.axis_index("piece")
     column = lax.axis_index("col")
-    density = fetch_phase_density(phase, phase_density)
-    state = jnp.concatenate([positions, density[None]], 0)
-    filled = counts[piece]
-    onward = [(i, i + 1) for i in range(pieces - 1)]
-    back = [(i + 1, i) for i in range(pieces - 1)]
-    tail = lax.dynamic_slice_in_dim(state, filled - share, share, 1)
-    before = lax.ppermute(tail, "piece", onward)
-    after = lax.ppermute(state[:, :share], "piece", back)
-
-    ranks = jnp.arange(pieces, dtype=jnp.int32)
-    live = jnp.clip(filled - column * share, 0, share)
-    first = jnp.sum(jnp.where(ranks < piece, counts, 0)) + column * share
+    message = jax.ShapeDtypeStruct((4, share, width), jnp.float32)
+    meta, density, tail, head = pl.pallas_call(
+        prepare,
+        out_shape=[pltpu.SMEM((8,), jnp.int32), jax.ShapeDtypeStruct(phase.shape, jnp.float32), message, message],
+        in_specs=[SMEM] * 2 + [VMEM] * 2,
+        out_specs=[SMEM] + [VMEM] * 3,
+        compiler_params=LIMIT,
+        name="prepare",
+    )(counts, phase_density, positions, phase)
+    meta = pltpu.with_memory_space_constraint(meta, pltpu.SMEM)
+    before = lax.ppermute(tail, "piece", [(i, (i + 1) % pieces) for i in range(pieces)])
+    after = lax.ppermute(head, "piece", [((i + 1) % pieces, i) for i in range(pieces)])
+
     total = jnp.sum(counts)
-    ahead = counts[jnp.maximum(piece - 1, 0)]
-    meta = jnp.stack([live, first, total, column * share, filled, ahead]).astype(jnp.int32)
     slots = piece * capacity + jnp.arange(capacity, dtype=jnp.int32)
     listed = jnp.sum((neighbours == slots[:, None]).astype(jnp.float32)).reshape(1)
 
-    offsets, below = jnp.asarray(OFFSETS), jnp.asarray(BELOW)
+    table = jnp.asarray(TABLE)
     most_inner, most_outer = tile_bounds(share)
     vector = jax.ShapeDtypeStruct((share, width), jnp.float32)
     inner_tiles = pltpu.VMEM((most_inner, width, width), jnp.float32)
     outer_tiles = pltpu.VMEM((most_outer, width, width), jnp.float32)
     square = pltpu.VMEM((share, width, width), jnp.float32)
     narrow = pltpu.VMEM((share * SUB, width), jnp.float32)
-    params = pltpu.CompilerParams(vmem_limit_bytes=16 * 1024 * 1024)
-    tables = [SMEM] * 3
+    tables = [SMEM] * 2
 
     tiles_in, spread, rows, cols = pl.pallas_call(
-        build_inner_kernel,
+        build_inner,
         out_shape=[inner_tiles, pltpu.VMEM((share, 4, width, width), jnp.float32), square, narrow],
         in_specs=tables + [VMEM] * 2,
         out_specs=[VMEM] * 4,
         scratch_shapes=[pltpu.VMEM((capacity, width), jnp.float32)],
-        compiler_params=params,
+        compiler_params=LIMIT,
         cost_estimate=cost(most_inner * width * width, 16),
         name="build_inner",
-    )(meta, offsets, below, positions, density)
-
-    def build_outer_kernel(*refs):
-        (m, o, b, position, dens, bef, aft, rhs, spr, rows_in, cols_in, tiles, diag, prec, hood, work) = refs
-        work[...] = rows_in[...]
-        build_outer(m, o, b, position, dens, bef, aft, rhs, spr, work, cols_in, tiles, diag, prec, hood)
+    )(meta, table, positions, density)
 
     tiles_out, diagonal, precond = pl.pallas_call(
-        build_outer_kernel,
+        build_outer,
         out_shape=[outer_tiles, vector, vector],
         in_specs=tables + [VMEM] * 8,
         out_specs=[VMEM] * 3,
@@ -541,10 +556,10 @@
             pltpu.VMEM((4, capacity + 2 * share, width), jnp.float32),
             pltpu.VMEM((share, width, width), jnp.float32),
         ],
-        compiler_params=params,
+        compiler_params=LIMIT,
         cost_estimate=cost(most_outer * width * width, 16),
         name="build_outer",
-    )(meta, offsets, below, positions, density, before, after, right_side, held(spread), held(rows), held(cols))
+    )(meta, table, positions, density, before, after, right_side, held(spread), held(rows), held(cols))
 
     def inner(field):
         return pl.pallas_call(
@@ -553,10 +568,10 @@
             in_specs=tables + [VMEM] * 2,
             out_specs=[VMEM] * 2,
             scratch_shapes=[pltpu.VMEM((share, width, width), jnp.float32)],
-            compiler_params=params,
+            compiler_params=LIMIT,
             cost_estimate=cost(most_inner * width * width, 4),
             name="apply_inner",
-        )(meta, offsets, below, field, held(tiles_in))
+        )(meta, table, field, held(tiles_in))
 
     def exchange(field):
         count = pieces * columns
@@ -564,12 +579,14 @@
         received = []
         for c in range(1, columns - 1):
             pairs = []
-            for p in range(pieces - 1):
-                low, high = p * columns + c, (p + 1) * columns
+            for p in range(pieces):
+                low, high = p * columns + c, (p + 1) % pieces * columns
                 pairs += [(low, high), (high, low)]
+                rest = [p * columns + k for k in range(1, columns) if k != c]
+                pairs += list(zip(rest, rest[1:] + rest[:1]))
             received.append(lax.ppermute(field, axes, pairs))
-        received.append(lax.ppermute(field, axes, [(i, i + 1) for i in range(count - 1)]))
-        received.append(lax.ppermute(field, axes, [(i + 1, i) for i in range(count - 1)]))
+        received.append(lax.ppermute(field, axes, [(i, (i + 1) % count) for i in range(count)]))
+        received.append(lax.ppermute(field, axes, [((i + 1) % count, i) for i in range(count)]))
         return received
 
     outer_scratch = [
@@ -586,10 +603,10 @@
         in_specs=tables + [VMEM] * (3 + columns + 3),
         out_specs=[VMEM] * 2,
         scratch_shapes=outer_scratch,
-        compiler_params=params,
+        compiler_params=LIMIT,
         cost_estimate=outer_cost,
         name="apply_first",
-    )(meta, offsets, below, right_side, precond, diagonal, *received, held(tiles_out), held(rows), held(cols))
+    )(meta, table, right_side, precond, diagonal, *received, held(tiles_out), held(rows), held(cols))
 
     received = exchange(scaled)
     rows, cols = inner(scaled)
@@ -599,10 +616,10 @@
         in_specs=tables + [SMEM] + [VMEM] * (4 + columns + 3),
         out_specs=[VMEM] * 2,
         scratch_shapes=outer_scratch,
-        compiler_params=params,
+        compiler_params=LIMIT,
         cost_estimate=outer_cost,
         name="apply_second",
-    )(meta, offsets, below, listed, right_side, precond, spill, scaled, *received, held(tiles_out), held(rows), held(cols))
+    )(meta, table, listed, right_side, precond, spill, scaled, *received, held(tiles_out), held(rows), held(cols))
 
     steps = [("col", 1 << k) for k in range(columns.bit_length() - 1)]
     steps += [("piece", 1 << k) for k in range(pieces.bit_length() - 1)]
@@ -616,6 +633,7 @@
         out_shape=[vector, vector, jax.ShapeDtypeStruct((SUB, width), jnp.float32)],
         in_specs=[SMEM] + [VMEM] * 8,
         out_specs=[VMEM] * 3,
+        compiler_params=LIMIT,
         name="finish",
     )(meta, right_side, precond, diagonal, spill, scaled, twice, sums, other)
     return lax.cond(

time: 145 us -> 109 us (0.75)
  starting transfers between devices: 47.1 us -> 30.8 us
  local copies, waits for them, and re-layouts: 18.5 us -> 2.53 us
  between operations: 18.2 us -> 15.6 us
  other arithmetic: 3.76 us -> 1.25 us
  waiting for transfers between devices: 9.79 us -> 11.6 us
    ppermute x6, starting transfers between devices: 29.2 us -> 16.5 us  [the longest x2 8.41 us: exchange(): lax.ppermute(field, axes, [(i, (i + 1) % count) for i in range(count)])]
    unnamed x40 -> x20, local copies, waits for them, and re-layouts: 13.9 us -> 1.95 us
    ppermute x5, starting transfers between devices: 15.2 us -> 6.65 us  [body(): lax.ppermute(sums, axis, [(i, i ^ step) for i in range(lax.axis_size(axis...]
    ppermute x4, starting transfers between devices: 2.65 us -> 7.65 us  [exchange(): received.append(lax.ppermute(field, axes, pairs))]
    another operation x1 -> x0, local copies, waits for them, and re-layouts: 2.01 us -> none  [body(): jnp.stack([live, first, total, column * share, filled, ahead])]
    ppermute x5, waiting for transfers between devices: 9.76 us -> 11.6 us  [body(): lax.ppermute(sums, axis, [(i, i ^ step) for i in range(lax.axis_size(axis...]
    pallas_call x2 -> x3, Pallas kernels: 23.8 us -> 24.7 us  [the longest x1 15.6 us: body(): pl.pallas_call(build_inner, out_shape=[inner_tiles, pltpu.VMEM((share, 4,...]
  transfers between devices with their start and end apart: 15 -> 15, of which waited for: 5 -> 5; matrix products, arithmetic and copies ran while one was open for 3% -> 1% of each run, Pallas kernels for 19% -> 26%
where the time goes in v2:
time: 109 us; the launch traced here: 108 us
  Pallas kernels  46.2 us (42%)
  starting transfers between devices  30.8 us (28%)
  between operations  15.6 us (14%)
  waiting for transfers between devices  11.6 us (11%)
  local copies, waits for them, and re-layouts  2.53 us (2%)
  other arithmetic  1.25 us (1%)
    pallas_call x1, Pallas kernels, body(): pl.pallas_call(build_inner, out_shape=[inner_tiles, pltpu.VMEM((share, 4,...  15.6 us
    pallas_call x2, Pallas kernels, inner(): pl.pallas_call(apply_inner, out_shape=[square, narrow], in_specs=tables +...  12.5 us
    ppermute x5, waiting for transfers between devices, body(): lax.ppermute(sums, axis, [(i, i ^ step) for i in range(lax.axis_size(axis...  11.6 us
    ppermute x2, starting transfers between devices, exchange(): lax.ppermute(field, axes, [(i, (i + 1) % count) for i in range(count)])  8.41 us
    pallas_call x1, Pallas kernels, body(): pl.pallas_call(build_outer, out_shape=[outer_tiles, vector, vector], in_s...  8.05 us
    ppermute x4, starting transfers between devices, exchange(): received.append(lax.ppermute(field, axes, pairs))  7.65 us
    ppermute x5, starting transfers between devices, body(): lax.ppermute(sums, axis, [(i, i ^ step) for i in range(lax.axis_size(axis...  6.65 us
    pallas_call x1, Pallas kernels, body(): pl.pallas_call(apply_second_kernel, out_shape=[vector, jax.ShapeDtypeStru...  4.73 us
  transfers between devices with their start and end apart: 15, of which 5 were waited for; matrix products, arithmetic and copies ran while one was open for 1% of the time, Pallas kernels for 26%

profile of v2, /device:TPU:0, one launch (start us, length us, event | category | flops | bytes accessed | tf_op | source)
XLA Modules:
  0.0 108.2 jit_solution(11280454934156776944)
XLA Ops:
  7.2 0.0 copy-start.1
  7.2 1.0 prepare.1
  8.2 0.5 collective-permute-start.6
  8.7 2.9 %collective-permute-start.7 = (f32[4,32,128]{2,1,0:T(8,128)S(1)}, f32[4,32,128]{2,1,0:T(8,128)S(1)}, u32[]{:S(2)}, u32[]{:S(2)}) collective-permute-start(f32[4,32,128]{2,1,0:T(8,128)S(1)} %get-tuple-element.359), channel_id=1, source_target_pairs={{4,0},{8,4},{12,8},{16,12},{20,16},{24,20},{28,24},{0,28},{5,1},{9... | collective-permute-start | bytes 196616 | tf_op jit(solution)/shard_map/ppermute | solution.py:524
  11.6 0.0 copy-start
  11.6 0.7 copy-done
  12.3 15.6 %build_inner.1 = (f32[216,128,128]{2,1,0:T(8,128)S(1)}, f32[32,4,128,128]{3,2,1,0:T(8,128)S(1)}, f32[32,128,128]{2,1,0:T(8,128)S(1)}, f32[256,128]{1,0:T(8,128)S(1)}) custom-call(s32[8]{0:T(128)S(4)} %get-tuple-element.356.meta, s32[16,92]{1,0:T(8,128)S(1)} %copy-done, f32[3,128,128]{2,1,0:T(8,128)} %position.5, f32[128,128]{1,0:T(8,128)S(1)} %get-tuple-element.357.density), custom_call_target="tpu_custom_call" | custom-call | flops 56623104 | bytes 14155776 | tf_op jit(solution)/shard_map/build_inner/pallas_call | solution.py:539
  28.0 0.0 collective-permute-done.6.before
  28.0 0.0 collective-permute-done.7.after
  28.0 8.1 %build_outer.1 = (f32[222,128,128]{2,1,0:T(8,128)S(1)}, f32[32,128]{1,0:T(8,128)S(1)}, f32[32,128]{1,0:T(8,128)S(1)}) custom-call(s32[8]{0:T(128)S(4)} %get-tuple-element.356.meta, s32[16,92]{1,0:T(8,128)S(1)} %copy-done, f32[3,128,128]{2,1,0:T(8,128)} %position.5, f32[128,128]{1,0:T(8,128)S(1)} %get-tuple-element.357.density, ...), custom_call_target="tpu_custom_call" | custom-call | flops 58195968 | bytes 14548992 | tf_op jit(solution)/shard_map/build_outer/pallas_call | solution.py:550
  36.1 0.0 copy-start.3
  36.1 7.7 %collective-permute-start.10 = (f32[32,128]{1,0:T(8,128)S(1)}, f32[32,128]{1,0:T(8,128)S(1)}, u32[]{:S(2)}, u32[]{:S(2)}) collective-permute-start(f32[32,128]{1,0:T(8,128)S(1)} %get-tuple-element.363.field.precond), channel_id=1, source_target_pairs={{0,1},{1,2},{2,3},{3,4},{4,5},{5,6},{6,7},{7,8},{8,9},{9,10},{10,1... | collective-permute-start | bytes 49160 | tf_op jit(solution)/shard_map/ppermute | solution.py:588
  43.8 0.0 collective-permute-start.11
  43.8 1.4 %collective-permute-start.8 = (f32[32,128]{1,0:T(8,128)S(1)}, f32[32,128]{1,0:T(8,128)S(1)}, u32[]{:S(2)}, u32[]{:S(2)}) collective-permute-start(f32[32,128]{1,0:T(8,128)S(1)} %get-tuple-element.363.field.precond), channel_id=1, source_target_pairs={{1,4},{4,1},{2,3},{3,2},{5,8},{8,5},{6,7},{7,6},{9,12},{12,9},{10,... | collective-permute-start | bytes 49160 | tf_op jit(solution)/shard_map/ppermute | solution.py:587
  45.2 0.9 collective-permute-start.9
  46.1 0.0 copy-done.1
  46.1 6.2 %apply_inner.2 = (f32[32,128,128]{2,1,0:T(8,128)S(1)}, f32[256,128]{1,0:T(8,128)S(1)}) custom-call(s32[8]{0:T(128)S(4)} %get-tuple-element.356.meta, s32[16,92]{1,0:T(8,128)S(1)} %copy-done.1, f32[32,128]{1,0:T(8,128)S(1)} %get-tuple-element.363.field.precond, f32[216,128,128]{2,1,0:T(8,128)S(1)} %get-tuple-element.366.tiles), custom_call_target="tpu_custom_call" | custom-call | flops 14155776 | bytes 14155776 | tf_op jit(solution)/shard_map/apply_inner/pallas_call | solution.py:565
  52.4 0.0 collective-permute-done.10.rest_2_
  52.4 0.0 collective-permute-done.11.rest_3_
  52.4 0.0 collective-permute-done.8.rest_0_
  52.4 0.0 collective-permute-done.9.rest_1_
  52.4 0.0 copy-done.3
  52.4 0.0 copy-start.4
  52.4 3.9 %apply_first.1 = (f32[32,128]{1,0:T(8,128)S(1)}, f32[32,128]{1,0:T(8,128)S(1)}) custom-call(s32[8]{0:T(128)S(4)} %get-tuple-element.356.meta, s32[16,92]{1,0:T(8,128)S(1)} %copy-done.1, f32[32,128]{1,0:T(8,128)S(1)} %copy-done.3, f32[32,128]{1,0:T(8,128)S(1)} %get-tuple-element.363.field.precond, f32[32,128]{1,0:T(8,128)S(1)} %get-tuple-element.364.diagonal, ...), custom_call_target="tpu_custom_call" | custom-call | flops 7274496 | bytes 14548992 | tf_op jit(solution)/shard_map/apply_first/pallas_call | solution.py:600
  56.4 3.1 %collective-permute-start.12 = (f32[32,128]{1,0:T(8,128)S(1)}, f32[32,128]{1,0:T(8,128)S(1)}, u32[]{:S(2)}, u32[]{:S(2)}) collective-permute-start(f32[32,128]{1,0:T(8,128)S(1)} %get-tuple-element.370.field.scaled), channel_id=1, source_target_pairs={{1,4},{4,1},{2,3},{3,2},{5,8},{8,5},{6,7},{7,6},{9,12},{12,9},{10,... | collective-permute-start | bytes 49160 | tf_op jit(solution)/shard_map/ppermute | solution.py:587
  59.5 2.2 %collective-permute-start.13 = (f32[32,128]{1,0:T(8,128)S(1)}, f32[32,128]{1,0:T(8,128)S(1)}, u32[]{:S(2)}, u32[]{:S(2)}) collective-permute-start(f32[32,128]{1,0:T(8,128)S(1)} %get-tuple-element.370.field.scaled), channel_id=1, source_target_pairs={{2,4},{4,2},{1,3},{3,1},{6,8},{8,6},{5,7},{7,5},{10,12},{12,10},{9... | collective-permute-start | bytes 49160 | tf_op jit(solution)/shard_map/ppermute | solution.py:587
  61.7 0.7 collective-permute-start.14
  62.4 4.7 %collective-permute-start.15 = (f32[32,128]{1,0:T(8,128)S(1)}, f32[32,128]{1,0:T(8,128)S(1)}, u32[]{:S(2)}, u32[]{:S(2)}) collective-permute-start(f32[32,128]{1,0:T(8,128)S(1)} %get-tuple-element.370.field.scaled), channel_id=1, source_target_pairs={{1,0},{2,1},{3,2},{4,3},{5,4},{6,5},{7,6},{8,7},{9,8},{10,9},{11,1... | collective-permute-start | bytes 49160 | tf_op jit(solution)/shard_map/ppermute | solution.py:589
  67.0 0.0 copy-done.4
  67.0 0.6 convert_reduce_fusion
  67.6 6.2 %apply_inner.3 = (f32[32,128,128]{2,1,0:T(8,128)S(1)}, f32[256,128]{1,0:T(8,128)S(1)}) custom-call(s32[8]{0:T(128)S(4)} %get-tuple-element.356.meta, s32[16,92]{1,0:T(8,128)S(1)} %copy-done.1, f32[32,128]{1,0:T(8,128)S(1)} %get-tuple-element.370.field.scaled, f32[216,128,128]{2,1,0:T(8,128)S(1)} %get-tuple-element.366.tiles), custom_call_target="tpu_custom_call" | custom-call | flops 14155776 | bytes 14155776 | tf_op jit(solution)/shard_map/apply_inner/pallas_call | solution.py:565
  73.9 0.0 collective-permute-done.12.rest_0_
  73.9 0.0 collective-permute-done.13.rest_1_
  73.9 0.0 collective-permute-done.14.rest_2_
  73.9 0.0 collective-permute-done.15.rest_3_
  73.9 0.0 copy-start.10
  73.9 0.0 copy-start.2
  73.9 0.0 copy-start.8
  74.0 0.0 copy-start.9
  74.0 4.7 %apply_second.1 = (f32[32,128]{1,0:T(8,128)S(1)}, f32[8,128]{1,0:T(8,128)S(1)}) custom-call(s32[8]{0:T(128)S(4)} %get-tuple-element.356.meta, s32[16,92]{1,0:T(8,128)S(1)} %copy-done.1, f32[1]{0:T(128)} %bitcast.252.listed, f32[32,128]{1,0:T(8,128)S(1)} %copy-done.3, f32[32,128]{1,0:T(8,128)S(1)} %get-tuple-element.363.field.precond, ...), custom_call_target="tpu_custom_call" | custom-call | flops 7274496 | bytes 14548992 | tf_op jit(solution)/shard_map/apply_second/pallas_call | solution.py:613
  78.7 0.0 collective-permute-start.16
  78.7 3.6 %collective-permute-done.16 = f32[8,128]{1,0:T(8,128)S(1)} collective-permute-done((f32[8,128]{1,0:T(8,128)S(1)}, f32[8,128]{1,0:T(8,128)S(1)}, u32[]{:S(2)}, u32[]{:S(2)}) %collective-permute-start.16) | collective-permute-done | bytes 4128 | tf_op jit(solution)/shard_map/ppermute | solution.py:629
  82.3 0.0 collective-permute-start.17
  82.3 4.5 %collective-permute-done.17 = f32[8,128]{1,0:T(8,128)S(1)} collective-permute-done((f32[8,128]{1,0:T(8,128)S(1)}, f32[8,128]{1,0:T(8,128)S(1)}, u32[]{:S(2)}, u32[]{:S(2)}) %collective-permute-start.17) | collective-permute-done | bytes 4128 | tf_op jit(solution)/shard_map/ppermute | solution.py:629
  86.8 0.0 collective-permute-start.18
  86.8 1.2 %collective-permute-done.18 = f32[8,128]{1,0:T(8,128)S(1)} collective-permute-done((f32[8,128]{1,0:T(8,128)S(1)}, f32[8,128]{1,0:T(8,128)S(1)}, u32[]{:S(2)}, u32[]{:S(2)}) %collective-permute-start.18) | collective-permute-done | bytes 4128 | tf_op jit(solution)/shard_map/ppermute | solution.py:629
  88.0 1.6 %collective-permute-start.19 = (f32[8,128]{1,0:T(8,128)S(1)}, f32[8,128]{1,0:T(8,128)S(1)}, u32[]{:S(2)}, u32[]{:S(2)}) collective-permute-start(f32[8,128]{1,0:T(8,128)S(1)} %add.1196), channel_id=1, source_target_pairs={{0,8},{4,12},{8,0},{12,4},{16,24},{20,28},{24,16},{28,20},{1,9},{5... | collective-permute-start | bytes 12296 | tf_op jit(solution)/shard_map/ppermute | solution.py:629
  89.6 2.0 %collective-permute-done.19 = f32[8,128]{1,0:T(8,128)S(1)} collective-permute-done((f32[8,128]{1,0:T(8,128)S(1)}, f32[8,128]{1,0:T(8,128)S(1)}, u32[]{:S(2)}, u32[]{:S(2)}) %collective-permute-start.19) | collective-permute-done | bytes 4128 | tf_op jit(solution)/shard_map/ppermute | solution.py:629
  91.6 5.1 %collective-permute-start.20 = (f32[8,128]{1,0:T(8,128)S(1)}, f32[8,128]{1,0:T(8,128)S(1)}, u32[]{:S(2)}, u32[]{:S(2)}) collective-permute-start(f32[8,128]{1,0:T(8,128)S(1)} %add.1197.mine), channel_id=1, source_target_pairs={{0,16},{4,20},{8,24},{12,28},{16,0},{20,4},{24,8},{28,12},{1,17},{... | collective-permute-start | bytes 12296 | tf_op jit(solution)/shard_map/ppermute | solution.py:629
  96.7 0.0 copy-done.10
  96.7 0.6 reduce_sum.64
  98.0 0.3 collective-permute-done.20.other
  98.3 0.3 finish.1
  98.6 0.6 slice.627
  99.8 0.0 copy-done.2
  99.8 0.0 copy-done.8
  99.9 0.0 copy-done.9
  99.9 0.2 conditional.1
  100.1 0.0 copy-start.11
  100.1 0.6 copy-done.11
  100.7 0.0 copy-start.12
  100.7 0.6 copy-done.12
  (5 shorter events, 0.0 us)
Async XLA Ops:
  7.2 39.0 %copy-start.1 = (s32[16,92]{1,0:T(8,128)S(1)}, s32[16,92]{1,0:T(8,128)}, u32[]{:S(2)}) copy-start(s32[16,92]{1,0:T(8,128)} %constant.248.clone.table) | copy-start | bytes 17668
  8.2 19.8 %collective-permute-start.6 = (f32[4,32,128]{2,1,0:T(8,128)S(1)}, f32[4,32,128]{2,1,0:T(8,128)S(1)}, u32[]{:S(2)}, u32[]{:S(2)}) collective-permute-start(f32[4,32,128]{2,1,0:T(8,128)S(1)} %get-tuple-element.358), channel_id=1, source_target_pairs={{0,4},{4,8},{8,12},{12,16},{16,20},{20,24},{24,28},{28,0},{1,5},{5... | collective-permute-start | bytes 196616 | tf_op jit(solution)/shard_map/ppermute | solution.py:523
  8.7 19.3 %collective-permute-start.7 = (f32[4,32,128]{2,1,0:T(8,128)S(1)}, f32[4,32,128]{2,1,0:T(8,128)S(1)}, u32[]{:S(2)}, u32[]{:S(2)}) collective-permute-start(f32[4,32,128]{2,1,0:T(8,128)S(1)} %get-tuple-element.359), channel_id=1, source_target_pairs={{4,0},{8,4},{12,8},{16,12},{20,16},{24,20},{28,24},{0,28},{5,1},{9... | collective-permute-start | bytes 196616 | tf_op jit(solution)/shard_map/ppermute | solution.py:524
  11.6 0.7 copy-start
  36.1 16.4 %copy-start.3 = (f32[32,128]{1,0:T(8,128)S(1)}, f32[32,128]{1,0:T(8,128)}, u32[]{:S(2)}) copy-start(f32[32,128]{1,0:T(8,128)} %right_side.7) | copy-start | bytes 49156
  36.1 16.3 %collective-permute-start.10 = (f32[32,128]{1,0:T(8,128)S(1)}, f32[32,128]{1,0:T(8,128)S(1)}, u32[]{:S(2)}, u32[]{:S(2)}) collective-permute-start(f32[32,128]{1,0:T(8,128)S(1)} %get-tuple-element.363.field.precond), channel_id=1, source_target_pairs={{0,1},{1,2},{2,3},{3,4},{4,5},{5,6},{6,7},{7,8},{8,9},{9,10},{10,1... | collective-permute-start | bytes 49160 | tf_op jit(solution)/shard_map/ppermute | solution.py:588
  43.8 8.6 %collective-permute-start.11 = (f32[32,128]{1,0:T(8,128)S(1)}, f32[32,128]{1,0:T(8,128)S(1)}, u32[]{:S(2)}, u32[]{:S(2)}) collective-permute-start(f32[32,128]{1,0:T(8,128)S(1)} %get-tuple-element.363.field.precond), channel_id=1, source_target_pairs={{1,0},{2,1},{3,2},{4,3},{5,4},{6,5},{7,6},{8,7},{9,8},{10,9},{11,1... | collective-permute-start | bytes 49160 | tf_op jit(solution)/shard_map/ppermute | solution.py:589
  43.8 8.6 %collective-permute-start.8 = (f32[32,128]{1,0:T(8,128)S(1)}, f32[32,128]{1,0:T(8,128)S(1)}, u32[]{:S(2)}, u32[]{:S(2)}) collective-permute-start(f32[32,128]{1,0:T(8,128)S(1)} %get-tuple-element.363.field.precond), channel_id=1, source_target_pairs={{1,4},{4,1},{2,3},{3,2},{5,8},{8,5},{6,7},{7,6},{9,12},{12,9},{10,... | collective-permute-start | bytes 49160 | tf_op jit(solution)/shard_map/ppermute | solution.py:587
  45.2 7.2 %collective-permute-start.9 = (f32[32,128]{1,0:T(8,128)S(1)}, f32[32,128]{1,0:T(8,128)S(1)}, u32[]{:S(2)}, u32[]{:S(2)}) collective-permute-start(f32[32,128]{1,0:T(8,128)S(1)} %get-tuple-element.363.field.precond), channel_id=1, source_target_pairs={{2,4},{4,2},{1,3},{3,1},{6,8},{8,6},{5,7},{7,5},{10,12},{12,10},{9... | collective-permute-start | bytes 49160 | tf_op jit(solution)/shard_map/ppermute | solution.py:587
  52.4 14.6 %copy-start.4 = (s32[128,7]{0,1:T(8,128)S(1)}, s32[128,7]{0,1:T(8,128)}, u32[]{:S(2)}) copy-start(s32[128,7]{0,1:T(8,128)} %param.17) | copy-start | bytes 10756
  56.4 17.5 %collective-permute-start.12 = (f32[32,128]{1,0:T(8,128)S(1)}, f32[32,128]{1,0:T(8,128)S(1)}, u32[]{:S(2)}, u32[]{:S(2)}) collective-permute-start(f32[32,128]{1,0:T(8,128)S(1)} %get-tuple-element.370.field.scaled), channel_id=1, source_target_pairs={{1,4},{4,1},{2,3},{3,2},{5,8},{8,5},{6,7},{7,6},{9,12},{12,9},{10,... | collective-permute-start | bytes 49160 | tf_op jit(solution)/shard_map/ppermute | solution.py:587
  59.5 14.4 %collective-permute-start.13 = (f32[32,128]{1,0:T(8,128)S(1)}, f32[32,128]{1,0:T(8,128)S(1)}, u32[]{:S(2)}, u32[]{:S(2)}) collective-permute-start(f32[32,128]{1,0:T(8,128)S(1)} %get-tuple-element.370.field.scaled), channel_id=1, source_target_pairs={{2,4},{4,2},{1,3},{3,1},{6,8},{8,6},{5,7},{7,5},{10,12},{12,10},{9... | collective-permute-start | bytes 49160 | tf_op jit(solution)/shard_map/ppermute | solution.py:587
  61.7 12.2 %collective-permute-start.14 = (f32[32,128]{1,0:T(8,128)S(1)}, f32[32,128]{1,0:T(8,128)S(1)}, u32[]{:S(2)}, u32[]{:S(2)}) collective-permute-start(f32[32,128]{1,0:T(8,128)S(1)} %get-tuple-element.370.field.scaled), channel_id=1, source_target_pairs={{0,1},{1,2},{2,3},{3,4},{4,5},{5,6},{6,7},{7,8},{8,9},{9,10},{10,1... | collective-permute-start | bytes 49160 | tf_op jit(solution)/shard_map/ppermute | solution.py:588
  62.4 11.5 %collective-permute-start.15 = (f32[32,128]{1,0:T(8,128)S(1)}, f32[32,128]{1,0:T(8,128)S(1)}, u32[]{:S(2)}, u32[]{:S(2)}) collective-permute-start(f32[32,128]{1,0:T(8,128)S(1)} %get-tuple-element.370.field.scaled), channel_id=1, source_target_pairs={{1,0},{2,1},{3,2},{4,3},{5,4},{6,5},{7,6},{8,7},{9,8},{10,9},{11,1... | collective-permute-start | bytes 49160 | tf_op jit(solution)/shard_map/ppermute | solution.py:589
  73.9 22.8 %copy-start.10 = (s32[8]{0:T(128)S(1)}, s32[8]{0:T(128)}, u32[]{:S(2)}) copy-start(s32[8]{0:T(128)} %counts.1) | copy-start | bytes 100
  73.9 25.9 %copy-start.2 = (f32[3,128,128]{2,1,0:T(8,128)S(1)}, f32[3,128,128]{2,1,0:T(8,128)}, u32[]{:S(2)}) copy-start(f32[3,128,128]{2,1,0:T(8,128)} %position.5) | copy-start | bytes 589828
  73.9 25.9 %copy-start.8 = (s32[128,128]{1,0:T(8,128)S(1)}, s32[128,128]{1,0:T(8,128)}, u32[]{:S(2)}) copy-start(s32[128,128]{1,0:T(8,128)} %phase.1) | copy-start | bytes 196612
  74.0 25.9 %copy-start.9 = (f32[3]{0:T(128)S(1)}, f32[3]{0:T(128)}, u32[]{:S(2)}) copy-start(f32[3]{0:T(128)} %densities.1) | copy-start | bytes 40
  78.7 3.6 %collective-permute-start.16 = (f32[8,128]{1,0:T(8,128)S(1)}, f32[8,128]{1,0:T(8,128)S(1)}, u32[]{:S(2)}, u32[]{:S(2)}) collective-permute-start(f32[8,128]{1,0:T(8,128)S(1)} %get-tuple-element.374), channel_id=1, source_target_pairs={{0,1},{1,0},{2,3},{3,2},{4,5},{5,4},{6,7},{7,6},{8,9},{9,8},{10,11... | collective-permute-start | bytes 12296 | tf_op jit(solution)/shard_map/ppermute | solution.py:629
  82.3 4.5 %collective-permute-start.17 = (f32[8,128]{1,0:T(8,128)S(1)}, f32[8,128]{1,0:T(8,128)S(1)}, u32[]{:S(2)}, u32[]{:S(2)}) collective-permute-start(f32[8,128]{1,0:T(8,128)S(1)} %add.1194), channel_id=1, source_target_pairs={{0,2},{1,3},{2,0},{3,1},{4,6},{5,7},{6,4},{7,5},{8,10},{9,11},{10,... | collective-permute-start | bytes 12296 | tf_op jit(solution)/shard_map/ppermute | solution.py:629
  86.8 1.2 %collective-permute-start.18 = (f32[8,128]{1,0:T(8,128)S(1)}, f32[8,128]{1,0:T(8,128)S(1)}, u32[]{:S(2)}, u32[]{:S(2)}) collective-permute-start(f32[8,128]{1,0:T(8,128)S(1)} %add.1195), channel_id=1, source_target_pairs={{0,4},{4,0},{8,12},{12,8},{16,20},{20,16},{24,28},{28,24},{1,5},{5... | collective-permute-start | bytes 12296 | tf_op jit(solution)/shard_map/ppermute | solution.py:629
  88.0 3.6 %collective-permute-start.19 = (f32[8,128]{1,0:T(8,128)S(1)}, f32[8,128]{1,0:T(8,128)S(1)}, u32[]{:S(2)}, u32[]{:S(2)}) collective-permute-start(f32[8,128]{1,0:T(8,128)S(1)} %add.1196), channel_id=1, source_target_pairs={{0,8},{4,12},{8,0},{12,4},{16,24},{20,28},{24,16},{28,20},{1,9},{5... | collective-permute-start | bytes 12296 | tf_op jit(solution)/shard_map/ppermute | solution.py:629
  91.6 6.7 %collective-permute-start.20 = (f32[8,128]{1,0:T(8,128)S(1)}, f32[8,128]{1,0:T(8,128)S(1)}, u32[]{:S(2)}, u32[]{:S(2)}) collective-permute-start(f32[8,128]{1,0:T(8,128)S(1)} %add.1197.mine), channel_id=1, source_target_pairs={{0,16},{4,20},{8,24},{12,28},{16,0},{20,4},{24,8},{28,12},{1,17},{... | collective-permute-start | bytes 12296 | tf_op jit(solution)/shard_map/ppermute | solution.py:629
  100.1 0.6 copy-start.11
  100.7 0.6 copy-start.12

commit v3 on v2

v3 whole, which is shorter than its diff:
```python
import jax
import jax.numpy as jnp
import numpy as np
from jax import lax
from jax.experimental import pallas as pl
from jax.experimental.pallas import tpu as pltpu
from jax.sharding import PartitionSpec as P

ITERS = 2
SIDE = 4
LAYER = SIDE * SIDE
REACH = 2 * LAYER
SUB = 8
VMEM = pl.BlockSpec(memory_space=pltpu.VMEM)
SMEM = pl.BlockSpec(memory_space=pltpu.SMEM)


def stencil_tables():
    levels = SIDE.bit_length() - 1

    def cell(code):
        across = sum((code >> (2 * level) & 1) << level for level in range(levels))
        along = sum((code >> (2 * level + 1) & 1) << level for level in range(levels))
        return across, along

    place = {cell(code): code for code in range(LAYER)}
    rows = []
    for code in range(LAYER):
        across, along = cell(code)
        rows.append(
            sorted(
                step_z * LAYER + place[across + step_x, along + step_y] - code
                for step_z in (-1, 0, 1)
                for step_y in (-1, 0, 1)
                for step_x in (-1, 0, 1)
                if (across + step_x, along + step_y) in place
            )
        )
    longest = max(len(row) for row in rows)
    offsets = np.zeros((LAYER, longest), np.int32)
    below = np.zeros((LAYER, 2 * REACH + 1), np.int32)
    for code, row in enumerate(rows):
        offsets[code, : len(row)] = row
        for t in range(-REACH, REACH + 1):
            below[code, t + REACH] = sum(offset < t for offset in row)
    return offsets, below


OFFSETS, BELOW = stencil_tables()
WIDEST = OFFSETS.shape[1]
TABLE = np.concatenate([OFFSETS, BELOW], 1)
LIMIT = pltpu.CompilerParams(vmem_limit_bytes=6 * 1024 * 1024)


def tile_bounds(share):
    inner = outer = 0
    for first in range(LAYER):
        for live in range(1, share + 1):
            near = far = 0
            for a in range(live):
                code = (first + a) % LAYER
                row = [int(o) for o in OFFSETS[code][: BELOW[code, -1]]]
                near += sum(0 <= a + o and o <= 0 for o in row)
                far += sum(a + o < 0 or a + o >= live for o in row)
            inner, outer = max(inner, near), max(outer, far)
    return inner, outer


def rank(table, code, t):
    return table[code, jnp.clip(t, -REACH, REACH) + REACH + WIDEST]


def inner_range(meta, table, a):
    code = lax.rem(meta[1] + a, LAYER)
    low, high = rank(table, code, -a), rank(table, code, 0)
    last = jnp.maximum(high - low - 1, 0)
    return high - low, lambda t: a + table[code, low + jnp.minimum(t, last)]


def outer_range(meta, table, a):
    code = lax.rem(meta[1] + a, LAYER)
    place = meta[1] + a
    low, split = rank(table, code, -place), rank(table, code, -a)
    resume, high = rank(table, code, meta[0] - a), rank(table, code, meta[2] - place)
    ahead = split - low
    count = ahead + jnp.maximum(high - resume, 0)
    last = jnp.maximum(count - 1, 0)

    def place_of(t):
        t = jnp.minimum(t, last)
        return a + table[code, jnp.where(t < ahead, low + t, resume + t - ahead)]

    return count, place_of


def sweep(count, fetch, step, carry):
    def both(i, state):
        carry, first, second = state
        later = fetch(2 * i + 2), fetch(2 * i + 3)
        return step(second, step(first, carry)), *later

    carry, first, _ = lax.fori_loop(0, lax.div(count, 2), both, (carry, fetch(0), fetch(1)))
    return lax.fori_loop(0, lax.rem(count, 2), lambda _, carry: step(first, carry), carry)


def tree(terms):
    while len(terms) > 1:
        terms = [a + b for a, b in zip(terms[::2], terms[1::2])] + terms[len(terms) // 2 * 2 :]
    return terms[0]


def pieces_of(width):
    return [slice(c * SUB, (c + 1) * SUB) for c in range(width // SUB)]


def wide(row):
    return jnp.broadcast_to(row, (SUB, row.shape[1]))


def pair_chunk(own, other):
    dx = own[0] - other[0]
    dy = own[1] - other[1]
    dz = own[2] - other[2]
    squared = dx * dx + dy * dy + dz * dz
    rest = jnp.maximum(1.0 - squared, 0.0)
    return rest * rest * pltpu.reciprocal((squared + 0.01) * (own[3] + other[3]), approx=True)


def spread_columns(out, index, rows):
    count, width = rows.shape
    turned = rows.T
    for a in range(count):
        out[index(a)] = jnp.broadcast_to(turned[:, a : a + 1], (width, width))


def lane_sums(parts, count, width):
    lanes = lax.broadcasted_iota(jnp.int32, (width, width), 1)
    turned = jnp.zeros((width, width), jnp.float32)
    for a in range(count):
        turned = jnp.where(lanes == a, jnp.sum(parts[a], axis=1, keepdims=True), turned)
    return turned.T[:count]


def sub_sums(cols):
    return jnp.sum(cols[...].reshape(-1, SUB, cols.shape[1]), axis=1)


def alive_rows(meta, share, width):
    return lax.broadcasted_iota(jnp.int32, (share, width), 0) < meta[0]


def prepare(counts, densities, position, phase, listed, meta, density, tail, head, times):
    share, width = tail.shape[1:]
    capacity = phase.shape[0]
    piece, column = lax.axis_index("piece"), lax.axis_index("col")
    filled = counts[piece]
    filled_before = counts[jnp.maximum(piece - 1, 0)]
    before = jnp.int32(0)
    total = jnp.int32(0)
    for p in range(counts.shape[0]):
        before = before + jnp.where(p < piece, counts[p], 0)
        total = total + counts[p]
    meta[0] = jnp.clip(filled - column * share, 0, share)
    meta[1] = before + column * share
    meta[2] = total
    meta[3] = column * share
    meta[4] = filled
    meta[5] = filled_before
    labels = phase[...]
    density[...] = sum(jnp.where(labels == k, densities[k], 0.0) for k in range(densities.shape[0]))
    last = pl.ds(filled - share, share)
    for k in range(3):
        tail[k] = position[k, last, :]
        head[k] = position[k, 0:share, :]
    tail[3] = density[last, :]
    head[3] = density[0:share, :]
    ids = listed[...]
    own = lax.broadcasted_iota(jnp.int32, ids.shape, 1)
    slot = ids - piece * capacity
    away = slot - own + jnp.where(slot < 0, capacity - filled_before, jnp.where(slot >= capacity, filled - capacity, 0))
    away = jnp.where(ids < 0, -REACH, away) + REACH
    steps = lax.broadcasted_iota(jnp.int32, (2 * REACH, capacity), 0)
    found = tree([jnp.where(steps == away[k : k + 1], 1.0, 0.0) for k in range(ids.shape[0])])
    found = jnp.concatenate([found, jnp.zeros((width - 2 * REACH, capacity), jnp.float32)], 0)
    times[...] = found.T


def build_inner(meta, table, position, density, tiles, spread, rows_ref, cols_ref, self_ref, weight):
    share, width = rows_ref.shape[0], rows_ref.shape[2]
    chunks = pieces_of(width)
    base = meta[3]
    weight[...] = density[...] * (width / 2.0)
    own_rows = pl.ds(pl.multiple_of(base, SUB), share)
    for k in range(4):
        values = position[k, own_rows, :] if k < 3 else weight[own_rows, :]
        spread_columns(spread, lambda a: (a, k), values)
    cols_ref[...] = jnp.zeros_like(cols_ref)

    def rows_at(n):
        here = pl.ds(base + n, 1)
        return [wide(position[k, here, :]) for k in range(3)] + [wide(weight[here, :])]

    def block(a, at):
        count, place_of = inner_range(meta, table, a)

        def fetch(t):
            n = place_of(t)
            return n, rows_at(n)

        def pair(fetched, carry):
            n, other = fetched
            at, sums = carry
            result = []
            for here in chunks:
                tile = pair_chunk([spread[a, k, here, :] for k in range(4)], other)
                tiles[at, here, :] = tile
                result.append(tile)
            there = pl.ds(pl.multiple_of(n * SUB, SUB), SUB)
            cols_ref[there, :] = cols_ref[there, :] + tree(result)
            return at + 1, [old + new for old, new in zip(sums, result)]

        zero = jnp.zeros((SUB, width), jnp.float32)
        at, sums = sweep(count, fetch, pair, (at, [zero] * len(chunks)))
        for here, values in zip(chunks, sums):
            rows_ref[a, here, :] = values
        other = rows_at(a)
        lane = lax.broadcasted_iota(jnp.int32, (SUB, width), 1)
        sublane = lax.broadcasted_iota(jnp.int32, (SUB, width), 0)
        result = []
        for c, here in enumerate(chunks):
            tile = pair_chunk([spread[a, k, here, :] for k in range(4)], other)
            tile = jnp.where(lane == sublane + c * SUB, 0.0, tile)
            tiles[at, here, :] = tile
            result.append(tile)
        self_ref[pl.ds(pl.multiple_of(a * SUB, SUB), SUB), :] = tree(result)
        return at + 1

    lax.fori_loop(0, meta[0], block, 0)


def build_outer(
    meta, table, position, density, before, after, spread, rows_ref, cols_ref, self_ref,
    tiles, sums_ref, alone_ref, hood, work,
):
    share, width = sums_ref.shape
    chunks = pieces_of(width)
    capacity = density.shape[0]
    base, filled = meta[3], meta[4]
    scale = width / 2.0
    for k in range(4):
        gain = 1.0 if k < 3 else scale
        hood[k, 0:share, :] = before[k] * gain
        hood[k, share : share + capacity, :] = position[k] if k < 3 else density[...] * gain
        hood[k, share + capacity :, :] = after[k] * gain
    edge = share + filled - base

    def block(a, at):
        count, place_of = outer_range(meta, table, a)

        def fetch(t):
            w = share + place_of(t)
            here = pl.ds(jnp.where(w < edge, base + w, share + capacity + w - edge), 1)
            return [wide(hood[k, here, :]) for k in range(4)]

        def pair(other, carry):
            at, sums = carry
            result = []
            for here, old in zip(chunks, sums):
                tile = pair_chunk([spread[a, k, here, :] for k in range(4)], other)
                tiles[at, here, :] = tile
                result.append(old + tile)
            return at + 1, result

        at, sums = sweep(count, fetch, pair, (at, [rows_ref[a, here, :] for here in chunks]))
        for here, values in zip(chunks, sums):
            work[a, here, :] = values
        return at

    lax.fori_loop(0, meta[0], block, 0)
    sums_ref[...] = lane_sums(work, share, width) + sub_sums(cols_ref)
    alone_ref[...] = sub_sums(self_ref)


def settle(
    meta, table, times, density, right_side, sums, alone, inner_old, outer_old,
    inner_tiles, outer_tiles, diagonal_ref, precond_ref, alone_times, sums_work, cols_work, row_work,
):
    share, width = right_side.shape
    alive = alive_rows(meta, share, width)
    lane = lax.broadcasted_iota(jnp.int32, (share, width), 1)
    often = jnp.where(alive, times[...], 0.0)
    mine = jnp.sum(jnp.where(lane == REACH, often, 0.0), axis=1, keepdims=True)
    alone_times[...] = jnp.broadcast_to(mine, (share, width))
    most = jnp.max(jnp.where((lane == REACH) | (lane == 0), 0.0, often))
    sums_work[...] = sums[...]

    @pl.when(most > 1.5)
    def _():
        one_lane = lax.broadcasted_iota(jnp.int32, (1, width), 1)
        cols_work[...] = jnp.zeros_like(cols_work)
        row_work[...] = jnp.zeros_like(row_work)

        def factor(a, n):
            row = times[pl.ds(a, 1), :]
            return jnp.sum(jnp.where(one_lane == n - a + REACH, row, 0.0), axis=1, keepdims=True)

        def block(a, state):
            count, place_of = inner_range(meta, table, a)

            def inner(t, at):
                n = place_of(t)
                tile = inner_old[at] * factor(a, n)
                inner_tiles[at] = tile
                row_work[a] = row_work[a] + tile
                there = pl.ds(n, 1)
                cols_work[there, :] = cols_work[there, :] + jnp.sum(tile, axis=0, keepdims=True)
                return at + 1

            at = lax.fori_loop(0, count, inner, state[0]) + 1
            count, place_far = outer_range(meta, table, a)

            def outer(t, at):
                tile = outer_old[at] * factor(a, place_far(t))
                outer_tiles[at] = tile
                row_work[a] = row_work[a] + tile
                return at + 1

            return at, lax.fori_loop(0, count, outer, state[1])

        lax.fori_loop(0, meta[0], block, (0, 0))
        sums_work[...] = lane_sums(row_work, share, width) + cols_work[...]

    own_rows = pl.ds(pl.multiple_of(meta[3], SUB), share)
    pairs = jnp.where(alive, sums_work[...] + alone[...] * alone_times[...], 0.0)
    diagonal = 1.0 / density[own_rows, :] + pairs
    diagonal_ref[...] = diagonal
    precond_ref[...] = jnp.where(alive, right_side[...], 0.0) / diagonal


def apply_inner(meta, table, field, alone_times, tiles, rows_ref, cols_ref, spread):
    share, width = field.shape
    chunks = pieces_of(width)
    spread_columns(spread, lambda a: a, field[...])
    cols_ref[...] = jnp.zeros_like(cols_ref)

    def block(a, at):
        count, place_of = inner_range(meta, table, a)

        def fetch(t):
            n = place_of(t)
            return n, wide(field[pl.ds(n, 1), :])

        def pair(fetched, carry):
            n, value = fetched
            at, sums = carry
            down, result = [], []
            for here, old in zip(chunks, sums):
                tile = tiles[at, here, :]
                down.append(tile * spread[a, here, :])
                result.append(old + tile * value)
            there = pl.ds(pl.multiple_of(n * SUB, SUB), SUB)
            cols_ref[there, :] = cols_ref[there, :] + tree(down)
            return at + 1, result

        zero = jnp.zeros((SUB, width), jnp.float32)
        at, sums = sweep(count, fetch, pair, (at, [zero] * len(chunks)))
        here = pl.ds(a, 1)
        value = wide(field[here, :] * alone_times[here, :])
        for here, old in zip(chunks, sums):
            rows_ref[a, here, :] = old + tiles[at, here, :] * value
        return at + 1

    lax.fori_loop(0, meta[0], block, 0)


def apply_outer(meta, table, received, tiles, rows_ref, cols_ref, work, hood):
    columns = len(received)
    share, width = received[0].shape
    chunks = pieces_of(width)
    base, filled = meta[3], meta[4]
    for k, ref in enumerate(received):
        hood[k * share : (k + 1) * share, :] = ref[...]
    column = lax.div(base, share)
    last = columns - 2
    edge = share + filled - base
    before_at = jnp.where(column == 0, meta[5] - 2 * share, last * share)
    after_at = (last + 1) * share - 2 * share
    head_at = jnp.where(column == last + 1, (last + 1) * share, (column - 1) * share) - edge

    def block(a, at):
        count, place_of = outer_range(meta, table, a)

        def fetch(t):
            w = share + place_of(t)
            row = w + jnp.where(w < share, before_at, jnp.where(w < edge, after_at, head_at))
            return wide(hood[pl.ds(row, 1), :])

        def pair(value, carry):
            at, sums = carry
            return at + 1, [old + tiles[at, here, :] * value for here, old in zip(chunks, sums)]

        at, sums = sweep(count, fetch, pair, (at, [rows_ref[a, here, :] for here in chunks]))
        for here, values in zip(chunks, sums):
            work[a, here, :] = values
        return at

    lax.fori_loop(0, meta[0], block, 0)
    return jnp.where(alive_rows(meta, share, width), lane_sums(work, share, width) + sub_sums(cols_ref), 0.0)


def apply_first(meta, table, diagonal, *rest):
    *received, tiles, rows_ref, cols_ref, spill_ref, scaled_ref, work, hood = rest
    spill = apply_outer(meta, table, received, tiles, rows_ref, cols_ref, work, hood)
    spill_ref[...] = spill
    scaled_ref[...] = spill / diagonal[...]


def apply_second(meta, table, right_side, precond, spill, scaled, *rest):
    *received, tiles, rows_ref, cols_ref, twice_ref, sums_ref, work, hood = rest
    twice = apply_outer(meta, table, received, tiles, rows_ref, cols_ref, work, hood)
    twice_ref[...] = twice
    share, width = twice.shape
    source = jnp.where(alive_rows(meta, share, width), right_side[...], 0.0)
    lane = lax.broadcasted_iota(jnp.int32, (1, width), 1)
    sums = jnp.zeros((1, width), jnp.float32)
    pairs = ((source, precond[...]), (spill[...], precond[...]), (spill[...], scaled[...]), (scaled[...], twice))
    for k, (first, second) in enumerate(pairs):
        along = jnp.sum(first * second, axis=0, keepdims=True)
        sums = jnp.where(lane == k, jnp.sum(along, axis=1, keepdims=True), sums)
    sums_ref[...] = wide(sums)


def finish(meta, right_side, precond, spill, scaled, twice, mine, other, solution_ref, residual_ref):
    share, width = precond.shape
    sums = mine[...] + other[...]

    def pick(k):
        return sums[0:1, k : k + 1]

    weighted, cross, square, last = pick(0), pick(1), pick(2), pick(3)
    part = cross / weighted
    advance = 1.0 / (1.0 - part)
    keep = -part * advance
    weighted_next = advance * advance * (square - cross * part)
    bent = keep * keep * cross + 2.0 * keep * advance * square + advance * advance * last
    blend = weighted_next / weighted
    advance_next = weighted_next / (weighted_next - bent - blend * weighted_next / advance)
    source = jnp.where(alive_rows(meta, share, width), right_side[...], 0.0)
    residual = keep * source + advance * spill[...]
    next_precond = keep * precond[...] + advance * scaled[...]
    direction = next_precond + blend * precond[...]
    image = residual - keep * spill[...] - advance * twice[...] + blend * (source - spill[...])
    solution_ref[...] = advance * precond[...] + advance_next * direction
    residual_ref[...] = residual - advance_next * image


def held(array):
    return pltpu.with_memory_space_constraint(array, pltpu.VMEM)


def body(positions, phase, neighbours, counts, phase_density, right_side):
    capacity, width = phase.shape
    columns = lax.axis_size("col")
    pieces = lax.axis_size("piece")
    share = capacity // columns
    f32 = jnp.float32
    vector = jax.ShapeDtypeStruct((share, width), f32)
    few = jax.ShapeDtypeStruct((SUB, width), f32)
    message = jax.ShapeDtypeStruct((4, share, width), f32)
    most_inner, most_outer = tile_bounds(share)
    inner_tiles = pltpu.VMEM((most_inner, width, width), f32)
    outer_tiles = pltpu.VMEM((most_outer, width, width), f32)
    square = pltpu.VMEM((share, width, width), f32)
    narrow = pltpu.VMEM((share * SUB, width), f32)
    table = jnp.asarray(TABLE)

    def call(kernel, args, outs, scratch=(), work=0, scalars=2, **more):
        return pl.pallas_call(
            kernel,
            out_shape=outs,
            in_specs=[SMEM] * scalars + [VMEM] * (len(args) - scalars),
            out_specs=[SMEM if getattr(o, "memory_space", None) == pltpu.SMEM else VMEM for o in outs],
            scratch_shapes=scratch,
            compiler_params=LIMIT,
            cost_estimate=pl.CostEstimate(flops=work * width * width, bytes_accessed=0, transcendentals=0),
            name=kernel.__name__,
            **more,
        )(*args)

    meta, density, tail, head, times = call(
        prepare,
        (counts, phase_density, positions, phase, neighbours.T),
        [pltpu.SMEM((8,), jnp.int32), jax.ShapeDtypeStruct(phase.shape, f32), message, message,
         jax.ShapeDtypeStruct((capacity, width), f32)],
    )
    meta = pltpu.with_memory_space_constraint(meta, pltpu.SMEM)
    before = lax.ppermute(tail, "piece", [(i, (i + 1) % pieces) for i in range(pieces)])
    after = lax.ppermute(head, "piece", [((i + 1) % pieces, i) for i in range(pieces)])
    times = lax.psum_scatter(times, "col", scatter_dimension=0, tiled=True)

    tiles_in, spread, rows, cols, selfs = call(
        build_inner,
        (meta, table, positions, density),
        [inner_tiles, pltpu.VMEM((share, 4, width, width), f32), square, narrow, narrow],
        [pltpu.VMEM((capacity, width), f32)],
        16 * most_inner,
    )
    tiles_out, sums, alone = call(
        build_outer,
        (meta, table, positions, density, before, after, held(spread), held(rows), held(cols), held(selfs)),
        [outer_tiles, vector, vector],
        [pltpu.VMEM((4, capacity + 2 * share, width), f32), pltpu.VMEM((share, width, width), f32)],
        16 * most_outer,
    )
    tiles_in, tiles_out, diagonal, precond, alone_times = call(
        settle,
        (meta, table, times, density, right_side, sums, alone, held(tiles_in), held(tiles_out)),
        [inner_tiles, outer_tiles, vector, vector, vector],
        [pltpu.VMEM((share, width), f32)] * 2 + [pltpu.VMEM((share, width, width), f32)],
        input_output_aliases={7: 0, 8: 1},
    )

    def inner(field):
        return call(
            apply_inner,
            (meta, table, field, alone_times, held(tiles_in)),
            [square, narrow],
            [pltpu.VMEM((share, width, width), f32)],
            4 * most_inner,
        )

    def exchange(field):
        count = pieces * columns
        axes = ("piece", "col")
        received = []
        for c in range(1, columns - 1):
            pairs = []
            for p in range(pieces):
                low, high = p * columns + c, (p + 1) % pieces * columns
                pairs += [(low, high), (high, low)]
                rest = [p * columns + k for k in range(1, columns) if k != c]
                pairs += list(zip(rest, rest[1:] + rest[:1]))
            received.append(lax.ppermute(field, axes, pairs))
        received.append(lax.ppermute(field, axes, [(i, (i + 1) % count) for i in range(count)]))
        received.append(lax.ppermute(field, axes, [((i + 1) % count, i) for i in range(count)]))
        return received

    scratch = [pltpu.VMEM((share, width, width), f32), pltpu.VMEM((columns * share, width), f32)]

    received = exchange(precond)
    rows, cols = inner(precond)
    spill, scaled = call(
        apply_first,
        (meta, table, diagonal, *received, held(tiles_out), held(rows), held(cols)),
        [vector, vector],
        scratch,
        2 * most_outer,
    )

    received = exchange(scaled)
    rows, cols = inner(scaled)
    twice, sums = call(
        apply_second,
        (meta, table, right_side, precond, spill, scaled, *received, held(tiles_out), held(rows), held(cols)),
        [vector, few],
        scratch,
        2 * most_outer,
    )

    steps = [("col", 1 << k) for k in range(columns.bit_length() - 1)]
    steps += [("piece", 1 << k) for k in range(pieces.bit_length() - 1)]
    other = None
    for axis, step in steps:
        sums = sums if other is None else sums + other
        other = lax.ppermute(sums, axis, [(i, i ^ step) for i in range(lax.axis_size(axis))])

    return tuple(call(
        finish,
        (meta, right_side, precond, spill, scaled, twice, sums, other),
        [vector, vector],
        scalars=1,
    ))


def solution(mesh):
    placed = (
        P(None, "piece", None),
        P("piece", None),
        P("piece", "col"),
        P(),
        P(),
        P(("piece", "col"), None),
    )
    return jax.shard_map(
        body,
        mesh=mesh,
        in_specs=placed,
        out_specs=(P(("piece", "col"), None), P(("piece", "col"), None)),
        check_vma=False,
    )
```

time: 109 us -> 147 us (1.35)
  local copies, waits for them, and re-layouts: 2.53 us -> 48.1 us
  waiting for transfers between devices: 11.6 us -> 8.99 us
  Pallas kernels: 46.2 us -> 44 us
    unnamed x20 -> x48, local copies, waits for them, and re-layouts: 1.95 us -> 48.1 us
    ppermute x5, starting transfers between devices: 6.65 us -> 12.3 us  [body(): lax.ppermute(sums, axis, [(i, i ^ step) for i in range(lax.axis_size(axis...]
    ppermute x2, starting transfers between devices: 4.65 us -> 0.07 us  [exchange(): lax.ppermute(field, axes, [((i + 1) % count, i) for i in range(count)])]
    ppermute x4, starting transfers between devices: 7.65 us -> 4.03 us  [exchange(): received.append(lax.ppermute(field, axes, pairs))]
    ppermute x5, waiting for transfers between devices: 11.6 us -> 8.95 us  [body(): lax.ppermute(sums, axis, [(i, i ^ step) for i in range(lax.axis_size(axis...]
    pallas_call x8 -> x9, Pallas kernels: 46.2 us -> 44 us  [call(): pl.pallas_call(kernel, out_shape=outs, in_specs=[SMEM] * scalars + [VMEM]...]
  transfers between devices with their start and end apart: 15 -> 16, of which waited for: 5 -> 5; matrix products, arithmetic and copies ran while one was open for 1% -> 0% of each run, Pallas kernels for 26% -> 22%
where the time goes in v3:
time: 147 us; the launch traced here: 145 us
  local copies, waits for them, and re-layouts  48.1 us (33%)
  Pallas kernels  44 us (30%)
  starting transfers between devices  29.4 us (20%)
  between operations  14.2 us (10%)
  waiting for transfers between devices  8.99 us (6%)
    unnamed x48, local copies, waits for them, and re-layouts  48.1 us
    pallas_call x9, Pallas kernels, call(): pl.pallas_call(kernel, out_shape=outs, in_specs=[SMEM] * scalars + [VMEM]...  44 us
    ppermute x5, starting transfers between devices, body(): lax.ppermute(sums, axis, [(i, i ^ step) for i in range(lax.axis_size(axis...  12.3 us
    ppermute x2, starting transfers between devices, exchange(): lax.ppermute(field, axes, [(i, (i + 1) % count) for i in range(count)])  9.51 us
    ppermute x5, waiting for transfers between devices, body(): lax.ppermute(sums, axis, [(i, i ^ step) for i in range(lax.axis_size(axis...  8.95 us
    ppermute x4, starting transfers between devices, exchange(): received.append(lax.ppermute(field, axes, pairs))  4.03 us
    ppermute x1, starting transfers between devices, body(): lax.ppermute(head, 'piece', [((i + 1) % pieces, i) for i in range(pieces)])  2.95 us
  transfers between devices with their start and end apart: 16, of which 5 were waited for; matrix products, arithmetic and copies ran while one was open for 0% of the time, Pallas kernels for 22%

profile of v3, /device:TPU:0, one launch (start us, length us, event | category | flops | bytes accessed | tf_op | source)
XLA Modules:
  0.0 144.8 jit_solution(2159348483008255418)
XLA Ops:
  7.2 0.0 reduce-scatter.2.cloned.1.call-start
  7.2 0.0 copy-start.9
  7.2 0.9 copy-done.9
  8.1 0.8 copy-done.15
  9.0 0.7 copy-done.17
  9.7 0.7 copy-done.18
  10.3 0.7 copy-done.19
  11.0 1.3 prepare.1
  12.3 0.0 reduce-scatter.2.cloned.1.call-update
  12.3 0.5 collective-permute-start
  12.8 2.9 %collective-permute-start.1 = (f32[4,32,128]{2,1,0:T(8,128)S(1)}, f32[4,32,128]{2,1,0:T(8,128)S(1)}, u32[]{:S(2)}, u32[]{:S(2)}) collective-permute-start(f32[4,32,128]{2,1,0:T(8,128)S(1)} %get-tuple-element.32), channel_id=1, source_target_pairs={{4,0},{8,4},{12,8},{16,12},{20,16},{24,20},{28,24},{0,28},{5,1},{9... | collective-permute-start | bytes 196616 | tf_op jit(solution)/shard_map/ppermute | solution.py:498
  15.8 0.9 copy-done.10
  16.7 0.7 copy-done.11
  17.4 14.3 %build_inner.1 = (f32[216,128,128]{2,1,0:T(8,128)S(1)}, f32[32,4,128,128]{3,2,1,0:T(8,128)S(1)}, f32[32,128,128]{2,1,0:T(8,128)S(1)}, f32[256,128]{1,0:T(8,128)S(1)}, f32[256,128]{1,0:T(8,128)S(1)}) custom-call(s32[8]{0:T(128)S(4)} %get-tuple-element.28.meta, s32[16,92]{1,0:T(8,128)S(1)} %copy-done.11, f32[3,128,128]{2,1,0:T(8,128)S(1)} %copy-done.10, ...), custom_call_target="tpu_custom_call" | custom-call | flops 56623104 | tf_op jit(solution)/shard_map/build_inner/pallas_call | solution.py:478
  31.7 0.0 copy-start.4
  31.7 5.0 %copy-done.4 = f32[216,128,128]{2,1,0:T(8,128)} copy-done((f32[216,128,128]{2,1,0:T(8,128)}, f32[216,128,128]{2,1,0:T(8,128)S(1)}, u32[]{:S(2)}) %copy-start.4) | copy-done | bytes 14155800
  36.7 0.0 collective-permute-done.before
  36.7 0.0 collective-permute-done.1.after
  36.7 7.5 %build_outer.1 = (f32[222,128,128]{2,1,0:T(8,128)S(1)}, f32[32,128]{1,0:T(8,128)S(1)}, f32[32,128]{1,0:T(8,128)S(1)}) custom-call(s32[8]{0:T(128)S(4)} %get-tuple-element.28.meta, s32[16,92]{1,0:T(8,128)S(1)} %copy-done.11, f32[3,128,128]{2,1,0:T(8,128)S(1)} %copy-done.10, f32[128,128]{1,0:T(8,128)S(1)} %get-tuple-element.30.density, ...), custom_call_target="tpu_custom_call" | custom-call | flops 58195968 | tf_op jit(solution)/shard_map/build_outer/pallas_call | solution.py:478
  44.2 5.2 %copy-done = f32[222,128,128]{2,1,0:T(8,128)} copy-done((f32[222,128,128]{2,1,0:T(8,128)}, f32[222,128,128]{2,1,0:T(8,128)S(1)}, u32[]{:S(2)}) %copy-start) | copy-done | bytes 14549016
  49.4 5.1 %copy-done.1 = f32[222,128,128]{2,1,0:T(8,128)S(1)} copy-done((f32[222,128,128]{2,1,0:T(8,128)S(1)}, f32[222,128,128]{2,1,0:T(8,128)}, u32[]{:S(2)}) %copy-start.1) | copy-done | bytes 14549016
  54.5 5.0 %copy-done.5 = f32[216,128,128]{2,1,0:T(8,128)S(1)} copy-done((f32[216,128,128]{2,1,0:T(8,128)S(1)}, f32[216,128,128]{2,1,0:T(8,128)}, u32[]{:S(2)}) %copy-start.5) | copy-done | bytes 14155800
  59.5 0.7 copy-done.12
  60.2 0.7 copy-done.13
  61.0 0.7 copy-done.16
  61.7 0.8 settle.1
  62.5 0.0 copy-start.2
  62.5 5.2 %copy-done.2 = f32[222,128,128]{2,1,0:T(8,128)} copy-done((f32[222,128,128]{2,1,0:T(8,128)}, f32[222,128,128]{2,1,0:T(8,128)S(1)}, u32[]{:S(2)}) %copy-start.2) | copy-done | bytes 14549016
  67.7 5.0 %copy-done.6 = f32[216,128,128]{2,1,0:T(8,128)} copy-done((f32[216,128,128]{2,1,0:T(8,128)}, f32[216,128,128]{2,1,0:T(8,128)S(1)}, u32[]{:S(2)}) %copy-start.6) | copy-done | bytes 14155800
  72.6 0.0 collective-permute-start.5
  72.7 6.5 %collective-permute-start.4 = (f32[32,128]{1,0:T(8,128)S(1)}, f32[32,128]{1,0:T(8,128)S(1)}, u32[]{:S(2)}, u32[]{:S(2)}) collective-permute-start(f32[32,128]{1,0:T(8,128)S(1)} %get-tuple-element.41.field.precond), channel_id=1, source_target_pairs={{0,1},{1,2},{2,3},{3,4},{4,5},{5,6},{6,7},{7,8},{8,9},{9,10},{10,1... | collective-permute-start | bytes 49160 | tf_op jit(solution)/shard_map/ppermute | solution.py:544
  79.2 1.0 collective-permute-start.3
  80.1 0.3 collective-permute-start.2
  80.4 5.0 %copy-done.7 = f32[216,128,128]{2,1,0:T(8,128)S(1)} copy-done((f32[216,128,128]{2,1,0:T(8,128)S(1)}, f32[216,128,128]{2,1,0:T(8,128)}, u32[]{:S(2)}) %copy-start.7) | copy-done | bytes 14155800
  85.4 5.2 %apply_inner.2 = (f32[32,128,128]{2,1,0:T(8,128)S(1)}, f32[256,128]{1,0:T(8,128)S(1)}) custom-call(s32[8]{0:T(128)S(4)} %get-tuple-element.28.meta, s32[16,92]{1,0:T(8,128)S(1)} %copy-done.12, f32[32,128]{1,0:T(8,128)S(1)} %get-tuple-element.41.field.precond, f32[32,128]{1,0:T(8,128)S(1)} %get-tuple-element.44.alone_times, f32[216,128,128]{2,1,0:T(8,128)S(1)} %copy-done.7), custom_call_target="tpu_custom_call" | custom-call | flops 14155776 | tf_op jit(solution)/shard_map/apply_inner/pallas_call | solution.py:478
  90.7 0.0 collective-permute-done.5.rest_3_
  90.7 0.0 collective-permute-done.4.rest_2_
  90.7 0.0 collective-permute-done.3.rest_1_
  90.7 0.0 collective-permute-done.2.rest_0_
  90.7 0.0 copy-start.3
  90.7 5.1 %copy-done.3 = f32[222,128,128]{2,1,0:T(8,128)S(1)} copy-done((f32[222,128,128]{2,1,0:T(8,128)S(1)}, f32[222,128,128]{2,1,0:T(8,128)}, u32[]{:S(2)}) %copy-start.3) | copy-done | bytes 14549016
  95.9 4.3 %apply_first.1 = (f32[32,128]{1,0:T(8,128)S(1)}, f32[32,128]{1,0:T(8,128)S(1)}) custom-call(s32[8]{0:T(128)S(4)} %get-tuple-element.28.meta, s32[16,92]{1,0:T(8,128)S(1)} %copy-done.12, f32[32,128]{1,0:T(8,128)S(1)} %get-tuple-element.42.diagonal, f32[32,128]{1,0:T(8,128)S(1)} %collective-permute-done.2.rest_0_, ...), custom_call_target="tpu_custom_call" | custom-call | flops 7274496 | tf_op jit(solution)/shard_map/apply_first/pallas_call | solution.py:478
  100.2 0.0 slice-start.3
  100.2 0.1 collective-permute-start.9
  100.2 3.0 %collective-permute-start.8 = (f32[32,128]{1,0:T(8,128)S(1)}, f32[32,128]{1,0:T(8,128)S(1)}, u32[]{:S(2)}, u32[]{:S(2)}) collective-permute-start(f32[32,128]{1,0:T(8,128)S(1)} %get-tuple-element.49.field.scaled), channel_id=1, source_target_pairs={{0,1},{1,2},{2,3},{3,4},{4,5},{5,6},{6,7},{7,8},{8,9},{9,10},{10,1... | collective-permute-start | bytes 49160 | tf_op jit(solution)/shard_map/ppermute | solution.py:544
  103.3 2.5 %collective-permute-start.7 = (f32[32,128]{1,0:T(8,128)S(1)}, f32[32,128]{1,0:T(8,128)S(1)}, u32[]{:S(2)}, u32[]{:S(2)}) collective-permute-start(f32[32,128]{1,0:T(8,128)S(1)} %get-tuple-element.49.field.scaled), channel_id=1, source_target_pairs={{2,4},{4,2},{1,3},{3,1},{6,8},{8,6},{5,7},{7,5},{10,12},{12,10},{9... | collective-permute-start | bytes 49160 | tf_op jit(solution)/shard_map/ppermute | solution.py:543
  105.7 0.3 collective-permute-start.6
  106.0 5.2 %apply_inner.3 = (f32[32,128,128]{2,1,0:T(8,128)S(1)}, f32[256,128]{1,0:T(8,128)S(1)}) custom-call(s32[8]{0:T(128)S(4)} %get-tuple-element.28.meta, s32[16,92]{1,0:T(8,128)S(1)} %copy-done.12, f32[32,128]{1,0:T(8,128)S(1)} %get-tuple-element.49.field.scaled, f32[32,128]{1,0:T(8,128)S(1)} %get-tuple-element.44.alone_times, f32[216,128,128]{2,1,0:T(8,128)S(1)} %copy-done.8), custom_call_target="tpu_custom_call" | custom-call | flops 14155776 | tf_op jit(solution)/shard_map/apply_inner/pallas_call | solution.py:478
  111.2 0.0 collective-permute-done.9.rest_3_
  111.3 0.0 collective-permute-done.8.rest_2_
  111.3 0.0 collective-permute-done.7.rest_1_
  111.3 0.0 collective-permute-done.6.rest_0_
  111.3 4.4 %apply_second.1 = (f32[32,128]{1,0:T(8,128)S(1)}, f32[8,128]{1,0:T(8,128)S(1)}) custom-call(s32[8]{0:T(128)S(4)} %get-tuple-element.28.meta, s32[16,92]{1,0:T(8,128)S(1)} %copy-done.12, f32[32,128]{1,0:T(8,128)S(1)} %copy-done.14, f32[32,128]{1,0:T(8,128)S(1)} %get-tuple-element.41.field.precond, f32[32,128]{1,0:T(8,128)S(1)} %get-tuple-element.48.spill, ...), custom_call_target="tpu_custom_call" | custom-call | flops 7274496 | tf_op jit(solution)/shard_map/apply_second/pallas_call | solution.py:478
  115.7 2.6 %collective-permute-start.10 = (f32[8,128]{1,0:T(8,128)S(1)}, f32[8,128]{1,0:T(8,128)S(1)}, u32[]{:S(2)}, u32[]{:S(2)}) collective-permute-start(f32[8,128]{1,0:T(8,128)S(1)} %get-tuple-element.53), channel_id=1, source_target_pairs={{0,1},{1,0},{2,3},{3,2},{4,5},{5,4},{6,7},{7,6},{8,9},{9,8},{10,11... | collective-permute-start | bytes 12296 | tf_op jit(solution)/shard_map/ppermute | solution.py:575
  118.3 1.6 %collective-permute-done.10 = f32[8,128]{1,0:T(8,128)S(1)} collective-permute-done((f32[8,128]{1,0:T(8,128)S(1)}, f32[8,128]{1,0:T(8,128)S(1)}, u32[]{:S(2)}, u32[]{:S(2)}) %collective-permute-start.10) | collective-permute-done | bytes 4128 | tf_op jit(solution)/shard_map/ppermute | solution.py:575
  119.9 1.5 %collective-permute-start.11 = (f32[8,128]{1,0:T(8,128)S(1)}, f32[8,128]{1,0:T(8,128)S(1)}, u32[]{:S(2)}, u32[]{:S(2)}) collective-permute-start(f32[8,128]{1,0:T(8,128)S(1)} %add.14), channel_id=1, source_target_pairs={{0,2},{1,3},{2,0},{3,1},{4,6},{5,7},{6,4},{7,5},{8,10},{9,11},{10,... | collective-permute-start | bytes 12296 | tf_op jit(solution)/shard_map/ppermute | solution.py:575
  121.4 3.0 %collective-permute-done.11 = f32[8,128]{1,0:T(8,128)S(1)} collective-permute-done((f32[8,128]{1,0:T(8,128)S(1)}, f32[8,128]{1,0:T(8,128)S(1)}, u32[]{:S(2)}, u32[]{:S(2)}) %collective-permute-start.11) | collective-permute-done | bytes 4128 | tf_op jit(solution)/shard_map/ppermute | solution.py:575
  124.4 0.0 collective-permute-start.12
  124.4 1.2 collective-permute-done.12
  125.6 3.1 %collective-permute-start.13 = (f32[8,128]{1,0:T(8,128)S(1)}, f32[8,128]{1,0:T(8,128)S(1)}, u32[]{:S(2)}, u32[]{:S(2)}) collective-permute-start(f32[8,128]{1,0:T(8,128)S(1)} %add.16), channel_id=1, source_target_pairs={{0,8},{4,12},{8,0},{12,4},{16,24},{20,28},{24,16},{28,20},{1,9},{5... | collective-permute-start | bytes 12296 | tf_op jit(solution)/shard_map/ppermute | solution.py:575
  128.7 1.6 %collective-permute-done.13 = f32[8,128]{1,0:T(8,128)S(1)} collective-permute-done((f32[8,128]{1,0:T(8,128)S(1)}, f32[8,128]{1,0:T(8,128)S(1)}, u32[]{:S(2)}, u32[]{:S(2)}) %collective-permute-start.13) | collective-permute-done | bytes 4128 | tf_op jit(solution)/shard_map/ppermute | solution.py:575
  130.2 5.2 %collective-permute-start.14 = (f32[8,128]{1,0:T(8,128)S(1)}, f32[8,128]{1,0:T(8,128)S(1)}, u32[]{:S(2)}, u32[]{:S(2)}) collective-permute-start(f32[8,128]{1,0:T(8,128)S(1)} %add.17.mine), channel_id=1, source_target_pairs={{0,16},{4,20},{8,24},{12,28},{16,0},{20,4},{24,8},{28,12},{1,17},{... | collective-permute-start | bytes 12296 | tf_op jit(solution)/shard_map/ppermute | solution.py:575
  135.4 1.6 %collective-permute-done.14.other = f32[8,128]{1,0:T(8,128)S(1)} collective-permute-done((f32[8,128]{1,0:T(8,128)S(1)}, f32[8,128]{1,0:T(8,128)S(1)}, u32[]{:S(2)}, u32[]{:S(2)}) %collective-permute-start.14) | collective-permute-done | bytes 4128 | tf_op jit(solution)/shard_map/ppermute | solution.py:575
  137.0 0.9 finish.1
  (31 shorter events, 0.1 us)
Async XLA Ops:
  7.2 42.2 %reduce-scatter.2.cloned.1.call-start = ((), (), s32[]{:S(2)}) async-start(), calls=%async_computation.1 | async-start | bytes 81920 | tf_op jit(solution)/shard_map/reduce_scatter | solution.py:499
  7.2 0.9 copy-start.9
  8.1 0.8 copy-start.15
  9.0 0.7 copy-start.17
  9.7 0.7 copy-start.18
  10.3 0.7 copy-start.19
  12.3 24.4 %collective-permute-start = (f32[4,32,128]{2,1,0:T(8,128)S(1)}, f32[4,32,128]{2,1,0:T(8,128)S(1)}, u32[]{:S(2)}, u32[]{:S(2)}) collective-permute-start(f32[4,32,128]{2,1,0:T(8,128)S(1)} %get-tuple-element.31), channel_id=1, source_target_pairs={{0,4},{4,8},{8,12},{12,16},{16,20},{20,24},{24,28},{28,0},{1,5},{5... | collective-permute-start | bytes 196616 | tf_op jit(solution)/shard_map/ppermute | solution.py:497
  12.8 23.9 %collective-permute-start.1 = (f32[4,32,128]{2,1,0:T(8,128)S(1)}, f32[4,32,128]{2,1,0:T(8,128)S(1)}, u32[]{:S(2)}, u32[]{:S(2)}) collective-permute-start(f32[4,32,128]{2,1,0:T(8,128)S(1)} %get-tuple-element.32), channel_id=1, source_target_pairs={{4,0},{8,4},{12,8},{16,12},{20,16},{24,20},{28,24},{0,28},{5,1},{9... | collective-permute-start | bytes 196616 | tf_op jit(solution)/shard_map/ppermute | solution.py:498
  15.8 0.9 copy-start.10
  16.7 0.7 copy-start.11
  31.7 5.0 %copy-start.4 = (f32[216,128,128]{2,1,0:T(8,128)}, f32[216,128,128]{2,1,0:T(8,128)S(1)}, u32[]{:S(2)}) copy-start(f32[216,128,128]{2,1,0:T(8,128)S(1)} %get-tuple-element.39.inner_old) | copy-start | bytes 42467332
  44.2 5.2 %copy-start = (f32[222,128,128]{2,1,0:T(8,128)}, f32[222,128,128]{2,1,0:T(8,128)S(1)}, u32[]{:S(2)}) copy-start(f32[222,128,128]{2,1,0:T(8,128)S(1)} %get-tuple-element.40.outer_old) | copy-start | bytes 43646980
  49.4 5.1 %copy-start.1 = (f32[222,128,128]{2,1,0:T(8,128)S(1)}, f32[222,128,128]{2,1,0:T(8,128)}, u32[]{:S(2)}) copy-start(f32[222,128,128]{2,1,0:T(8,128)} %copy-done) | copy-start | bytes 43646980
  54.5 5.0 %copy-start.5 = (f32[216,128,128]{2,1,0:T(8,128)S(1)}, f32[216,128,128]{2,1,0:T(8,128)}, u32[]{:S(2)}) copy-start(f32[216,128,128]{2,1,0:T(8,128)} %copy-done.4) | copy-start | bytes 42467332
  59.5 0.7 copy-start.12
  60.2 0.7 copy-start.13
  61.0 0.7 copy-start.16
  62.5 5.2 %copy-start.2 = (f32[222,128,128]{2,1,0:T(8,128)}, f32[222,128,128]{2,1,0:T(8,128)S(1)}, u32[]{:S(2)}) copy-start(f32[222,128,128]{2,1,0:T(8,128)S(1)} %get-tuple-element.43.rest_4_) | copy-start | bytes 43646980
  67.6 5.0 %copy-start.6 = (f32[216,128,128]{2,1,0:T(8,128)}, f32[216,128,128]{2,1,0:T(8,128)S(1)}, u32[]{:S(2)}) copy-start(f32[216,128,128]{2,1,0:T(8,128)S(1)} %get-tuple-element.45.tiles) | copy-start | bytes 42467332
  72.6 18.0 %collective-permute-start.5 = (f32[32,128]{1,0:T(8,128)S(1)}, f32[32,128]{1,0:T(8,128)S(1)}, u32[]{:S(2)}, u32[]{:S(2)}) collective-permute-start(f32[32,128]{1,0:T(8,128)S(1)} %get-tuple-element.41.field.precond), channel_id=1, source_target_pairs={{1,0},{2,1},{3,2},{4,3},{5,4},{6,5},{7,6},{8,7},{9,8},{10,9},{11,1... | collective-permute-start | bytes 49160 | tf_op jit(solution)/shard_map/ppermute | solution.py:545
  72.7 18.0 %collective-permute-start.4 = (f32[32,128]{1,0:T(8,128)S(1)}, f32[32,128]{1,0:T(8,128)S(1)}, u32[]{:S(2)}, u32[]{:S(2)}) collective-permute-start(f32[32,128]{1,0:T(8,128)S(1)} %get-tuple-element.41.field.precond), channel_id=1, source_target_pairs={{0,1},{1,2},{2,3},{3,4},{4,5},{5,6},{6,7},{7,8},{8,9},{9,10},{10,1... | collective-permute-start | bytes 49160 | tf_op jit(solution)/shard_map/ppermute | solution.py:544
  79.2 11.5 %collective-permute-start.3 = (f32[32,128]{1,0:T(8,128)S(1)}, f32[32,128]{1,0:T(8,128)S(1)}, u32[]{:S(2)}, u32[]{:S(2)}) collective-permute-start(f32[32,128]{1,0:T(8,128)S(1)} %get-tuple-element.41.field.precond), channel_id=1, source_target_pairs={{2,4},{4,2},{1,3},{3,1},{6,8},{8,6},{5,7},{7,5},{10,12},{12,10},{9... | collective-permute-start | bytes 49160 | tf_op jit(solution)/shard_map/ppermute | solution.py:543
  80.1 10.6 %collective-permute-start.2 = (f32[32,128]{1,0:T(8,128)S(1)}, f32[32,128]{1,0:T(8,128)S(1)}, u32[]{:S(2)}, u32[]{:S(2)}) collective-permute-start(f32[32,128]{1,0:T(8,128)S(1)} %get-tuple-element.41.field.precond), channel_id=1, source_target_pairs={{1,4},{4,1},{2,3},{3,2},{5,8},{8,5},{6,7},{7,6},{9,12},{12,9},{10,... | collective-permute-start | bytes 49160 | tf_op jit(solution)/shard_map/ppermute | solution.py:543
  80.4 5.0 %copy-start.7 = (f32[216,128,128]{2,1,0:T(8,128)S(1)}, f32[216,128,128]{2,1,0:T(8,128)}, u32[]{:S(2)}) copy-start(f32[216,128,128]{2,1,0:T(8,128)} %copy-done.6) | copy-start | bytes 42467332
  85.4 20.6 %copy-start.8 = (f32[216,128,128]{2,1,0:T(8,128)S(1)}, f32[216,128,128]{2,1,0:T(8,128)}, u32[]{:S(2)}) copy-start(f32[216,128,128]{2,1,0:T(8,128)} %copy-done.6) | copy-start | bytes 42467332
  90.7 5.1 %copy-start.3 = (f32[222,128,128]{2,1,0:T(8,128)S(1)}, f32[222,128,128]{2,1,0:T(8,128)}, u32[]{:S(2)}) copy-start(f32[222,128,128]{2,1,0:T(8,128)} %copy-done.2) | copy-start | bytes 43646980
  95.9 15.4 %slice-start = ((s8[14548992]{0:T(1024)(128)(4,1)}), s8[4194304]{0:T(1024)(128)(4,1)S(1)}, s32[]{:S(2)}) async-start(s8[14548992]{0:T(1024)(128)(4,1)} %bitcast.1), calls=%async_computation.2 | async-start | bytes 8388608
  95.9 15.4 %slice-start.1 = ((s8[14548992]{0:T(1024)(128)(4,1)}), s8[4194304]{0:T(1024)(128)(4,1)S(1)}, s32[]{:S(2)}) async-start(s8[14548992]{0:T(1024)(128)(4,1)} %bitcast.1), calls=%async_computation.3 | async-start | bytes 8388608
  95.9 15.4 %slice-start.2 = ((s8[14548992]{0:T(1024)(128)(4,1)}), s8[4194304]{0:T(1024)(128)(4,1)S(1)}, s32[]{:S(2)}) async-start(s8[14548992]{0:T(1024)(128)(4,1)} %bitcast.1), calls=%async_computation.4 | async-start | bytes 8388608
  95.9 15.5 %copy-start.14 = (f32[32,128]{1,0:T(8,128)S(1)}, f32[32,128]{1,0:T(8,128)}, u32[]{:S(2)}) copy-start(f32[32,128]{1,0:T(8,128)} %right_side.5) | copy-start | bytes 49156
  100.2 11.2 %slice-start.3 = ((s8[14548992]{0:T(1024)(128)(4,1)}), s8[1966080]{0:T(1024)(128)(4,1)S(1)}, s32[]{:S(2)}) async-start(s8[14548992]{0:T(1024)(128)(4,1)} %bitcast.1), calls=%async_computation.5 | async-start | bytes 3932160
  100.2 11.1 %collective-permute-start.9 = (f32[32,128]{1,0:T(8,128)S(1)}, f32[32,128]{1,0:T(8,128)S(1)}, u32[]{:S(2)}, u32[]{:S(2)}) collective-permute-start(f32[32,128]{1,0:T(8,128)S(1)} %get-tuple-element.49.field.scaled), channel_id=1, source_target_pairs={{1,0},{2,1},{3,2},{4,3},{5,4},{6,5},{7,6},{8,7},{9,8},{10,9},{11,1... | collective-permute-start | bytes 49160 | tf_op jit(solution)/shard_map/ppermute | solution.py:545
  100.2 11.0 %collective-permute-start.8 = (f32[32,128]{1,0:T(8,128)S(1)}, f32[32,128]{1,0:T(8,128)S(1)}, u32[]{:S(2)}, u32[]{:S(2)}) collective-permute-start(f32[32,128]{1,0:T(8,128)S(1)} %get-tuple-element.49.field.scaled), channel_id=1, source_target_pairs={{0,1},{1,2},{2,3},{3,4},{4,5},{5,6},{6,7},{7,8},{8,9},{9,10},{10,1... | collective-permute-start | bytes 49160 | tf_op jit(solution)/shard_map/ppermute | solution.py:544
  103.3 8.0 %collective-permute-start.7 = (f32[32,128]{1,0:T(8,128)S(1)}, f32[32,128]{1,0:T(8,128)S(1)}, u32[]{:S(2)}, u32[]{:S(2)}) collective-permute-start(f32[32,128]{1,0:T(8,128)S(1)} %get-tuple-element.49.field.scaled), channel_id=1, source_target_pairs={{2,4},{4,2},{1,3},{3,1},{6,8},{8,6},{5,7},{7,5},{10,12},{12,10},{9... | collective-permute-start | bytes 49160 | tf_op jit(solution)/shard_map/ppermute | solution.py:543
  105.7 5.5 %collective-permute-start.6 = (f32[32,128]{1,0:T(8,128)S(1)}, f32[32,128]{1,0:T(8,128)S(1)}, u32[]{:S(2)}, u32[]{:S(2)}) collective-permute-start(f32[32,128]{1,0:T(8,128)S(1)} %get-tuple-element.49.field.scaled), channel_id=1, source_target_pairs={{1,4},{4,1},{2,3},{3,2},{5,8},{8,5},{6,7},{7,6},{9,12},{12,9},{10,... | collective-permute-start | bytes 49160 | tf_op jit(solution)/shard_map/ppermute | solution.py:543
  115.7 4.2 %collective-permute-start.10 = (f32[8,128]{1,0:T(8,128)S(1)}, f32[8,128]{1,0:T(8,128)S(1)}, u32[]{:S(2)}, u32[]{:S(2)}) collective-permute-start(f32[8,128]{1,0:T(8,128)S(1)} %get-tuple-element.53), channel_id=1, source_target_pairs={{0,1},{1,0},{2,3},{3,2},{4,5},{5,4},{6,7},{7,6},{8,9},{9,8},{10,11... | collective-permute-start | bytes 12296 | tf_op jit(solution)/shard_map/ppermute | solution.py:575
  119.9 4.5 %collective-permute-start.11 = (f32[8,128]{1,0:T(8,128)S(1)}, f32[8,128]{1,0:T(8,128)S(1)}, u32[]{:S(2)}, u32[]{:S(2)}) collective-permute-start(f32[8,128]{1,0:T(8,128)S(1)} %add.14), channel_id=1, source_target_pairs={{0,2},{1,3},{2,0},{3,1},{4,6},{5,7},{6,4},{7,5},{8,10},{9,11},{10,... | collective-permute-start | bytes 12296 | tf_op jit(solution)/shard_map/ppermute | solution.py:575
  124.4 1.2 collective-permute-start.12
  125.6 4.7 %collective-permute-start.13 = (f32[8,128]{1,0:T(8,128)S(1)}, f32[8,128]{1,0:T(8,128)S(1)}, u32[]{:S(2)}, u32[]{:S(2)}) collective-permute-start(f32[8,128]{1,0:T(8,128)S(1)} %add.16), channel_id=1, source_target_pairs={{0,8},{4,12},{8,0},{12,4},{16,24},{20,28},{24,16},{28,20},{1,9},{5... | collective-permute-start | bytes 12296 | tf_op jit(solution)/shard_map/ppermute | solution.py:575
  130.2 6.8 %collective-permute-start.14 = (f32[8,128]{1,0:T(8,128)S(1)}, f32[8,128]{1,0:T(8,128)S(1)}, u32[]{:S(2)}, u32[]{:S(2)}) collective-permute-start(f32[8,128]{1,0:T(8,128)S(1)} %add.17.mine), channel_id=1, source_target_pairs={{0,16},{4,20},{8,24},{12,28},{16,0},{20,4},{24,8},{28,12},{1,17},{... | collective-permute-start | bytes 12296 | tf_op jit(solution)/shard_map/ppermute | solution.py:575
Sparse Core Ops, SparseCore 0:
  12.4 21.6 reduce-scatter.1

commit v4 on v3

--- a/solution.py
+++ b/solution.py
@@ -49,6 +49,7 @@
 OFFSETS, BELOW = stencil_tables()
 WIDEST = OFFSETS.shape[1]
 TABLE = np.concatenate([OFFSETS, BELOW], 1)
+STRIDE = TABLE.shape[1]
 LIMIT = pltpu.CompilerParams(vmem_limit_bytes=6 * 1024 * 1024)
 
 
@@ -67,14 +68,14 @@
 
 
 def rank(table, code, t):
-    return table[code, jnp.clip(t, -REACH, REACH) + REACH + WIDEST]
+    return table[code * STRIDE + jnp.clip(t, -REACH, REACH) + REACH + WIDEST]
 
 
 def inner_range(meta, table, a):
     code = lax.rem(meta[1] + a, LAYER)
     low, high = rank(table, code, -a), rank(table, code, 0)
-    last = jnp.maximum(high - low - 1, 0)
-    return high - low, lambda t: a + table[code, low + jnp.minimum(t, last)]
+    start = code * STRIDE + low
+    return high - low, lambda t: a + table[start + t]
 
 
 def outer_range(meta, table, a):
@@ -83,14 +84,10 @@
     low, split = rank(table, code, -place), rank(table, code, -a)
     resume, high = rank(table, code, meta[0] - a), rank(table, code, meta[2] - place)
     ahead = split - low
+    start = code * STRIDE + low
+    start_after = code * STRIDE + resume - ahead
     count = ahead + jnp.maximum(high - resume, 0)
-    last = jnp.maximum(count - 1, 0)
-
-    def place_of(t):
-        t = jnp.minimum(t, last)
-        return a + table[code, jnp.where(t < ahead, low + t, resume + t - ahead)]
-
-    return count, place_of
+    return count, lambda t: a + table[t + jnp.where(t < ahead, start, start_after)]
 
 
 def sweep(count, fetch, step, carry):
@@ -149,8 +146,8 @@
     return lax.broadcasted_iota(jnp.int32, (share, width), 0) < meta[0]
 
 
-def prepare(counts, densities, position, phase, listed, meta, density, tail, head, times):
-    share, width = tail.shape[1:]
+def prepare(counts, densities, position, phase, listed, meta, density, first_swap, second_swap, times, *times_out):
+    share, width = first_swap.shape[1:]
     capacity = phase.shape[0]
     piece, column = lax.axis_index("piece"), lax.axis_index("col")
     filled = counts[piece]
@@ -169,11 +166,12 @@
     labels = phase[...]
     density[...] = sum(jnp.where(labels == k, densities[k], 0.0) for k in range(densities.shape[0]))
     last = pl.ds(filled - share, share)
-    for k in range(3):
-        tail[k] = position[k, last, :]
-        head[k] = position[k, 0:share, :]
-    tail[3] = density[last, :]
-    head[3] = density[0:share, :]
+    even = lax.rem(piece, 2) == 0
+    for k in range(4):
+        rows = position.at[k] if k < 3 else density
+        tail, head = rows[last, :], rows[0:share, :]
+        first_swap[k] = jnp.where(even, tail, head)
+        second_swap[k] = jnp.where(even, head, tail)
     ids = listed[...]
     own = lax.broadcasted_iota(jnp.int32, ids.shape, 1)
     slot = ids - piece * capacity
@@ -183,22 +181,23 @@
     found = tree([jnp.where(steps == away[k : k + 1], 1.0, 0.0) for k in range(ids.shape[0])])
     found = jnp.concatenate([found, jnp.zeros((width - 2 * REACH, capacity), jnp.float32)], 0)
     times[...] = found.T
-
-
-def build_inner(meta, table, position, density, tiles, spread, rows_ref, cols_ref, self_ref, weight):
+    for k, out in enumerate(times_out):
+        out[...] = times[pl.ds(pl.multiple_of((column ^ k) * share, SUB), share), :]
+
+
+def build_inner(meta, table, position, density, tiles, spread, rows_ref, cols_ref, self_ref, near):
     share, width = rows_ref.shape[0], rows_ref.shape[2]
     chunks = pieces_of(width)
     base = meta[3]
-    weight[...] = density[...] * (width / 2.0)
     own_rows = pl.ds(pl.multiple_of(base, SUB), share)
     for k in range(4):
-        values = position[k, own_rows, :] if k < 3 else weight[own_rows, :]
+        values = position[k, own_rows, :] if k < 3 else density[own_rows, :] * (width / 2.0)
+        near[k, 0:share, :] = values
         spread_columns(spread, lambda a: (a, k), values)
     cols_ref[...] = jnp.zeros_like(cols_ref)
 
     def rows_at(n):
-        here = pl.ds(base + n, 1)
-        return [wide(position[k, here, :]) for k in range(3)] + [wide(weight[here, :])]
+        return [wide(near[k, pl.ds(n, 1), :]) for k in range(4)]
 
     def block(a, at):
         count, place_of = inner_range(meta, table, a)
@@ -238,28 +237,50 @@
     lax.fori_loop(0, meta[0], block, 0)
 
 
+def factor(times, a, n):
+    lane = lax.broadcasted_iota(jnp.int32, (1, times.shape[1]), 1)
+    return jnp.sum(jnp.where(lane == n - a + REACH, times[pl.ds(a, 1), :], 0.0), axis=1, keepdims=True)
+
+
+def either(flag, run):
+    @pl.when(flag == 0)
+    def _():
+        run(False)
+
+    @pl.when(flag != 0)
+    def _():
+        run(True)
+
+
 def build_outer(
-    meta, table, position, density, before, after, spread, rows_ref, cols_ref, self_ref,
-    tiles, sums_ref, alone_ref, hood, work,
+    meta, table, position, density, first, second, right_side, tiles_in, spread, rows_ref, cols_ref, self_ref, *rest
 ):
-    share, width = sums_ref.shape
+    *times_in, again_ref, tiles, diagonal_ref, precond_ref, times, hood, work, sums_ref, extra = rest
+    share, width = diagonal_ref.shape
     chunks = pieces_of(width)
     capacity = density.shape[0]
     base, filled = meta[3], meta[4]
     scale = width / 2.0
+    even = lax.rem(lax.axis_index("piece"), 2) == 0
     for k in range(4):
         gain = 1.0 if k < 3 else scale
-        hood[k, 0:share, :] = before[k] * gain
+        before = jnp.where(even, second[k], first[k]) * gain
+        after = jnp.where(even, first[k], second[k]) * gain
+        hood[k, 0:share, :] = before
         hood[k, share : share + capacity, :] = position[k] if k < 3 else density[...] * gain
-        hood[k, share + capacity :, :] = after[k] * gain
-    edge = share + filled - base
+        hood[k, pl.ds(share + filled, share), :] = after
+    alive = alive_rows(meta, share, width)
+    often = jnp.where(alive, tree([ref[...] for ref in times_in]), 0.0)
+    times[...] = often
+    lane = lax.broadcasted_iota(jnp.int32, (share, width), 1)
+    again = jnp.max(jnp.where((lane == REACH) | (lane == 0), 0.0, often)) > 1.5
+    again_ref[0] = again.astype(jnp.int32)
 
     def block(a, at):
         count, place_of = outer_range(meta, table, a)
 
         def fetch(t):
-            w = share + place_of(t)
-            here = pl.ds(jnp.where(w < edge, base + w, share + capacity + w - edge), 1)
+            here = pl.ds(base + share + place_of(t), 1)
             return [wide(hood[k, here, :]) for k in range(4)]
 
         def pair(other, carry):
@@ -278,146 +299,144 @@
 
     lax.fori_loop(0, meta[0], block, 0)
     sums_ref[...] = lane_sums(work, share, width) + sub_sums(cols_ref)
-    alone_ref[...] = sub_sums(self_ref)
-
-
-def settle(
-    meta, table, times, density, right_side, sums, alone, inner_old, outer_old,
-    inner_tiles, outer_tiles, diagonal_ref, precond_ref, alone_times, sums_work, cols_work, row_work,
-):
-    share, width = right_side.shape
-    alive = alive_rows(meta, share, width)
-    lane = lax.broadcasted_iota(jnp.int32, (share, width), 1)
-    often = jnp.where(alive, times[...], 0.0)
-    mine = jnp.sum(jnp.where(lane == REACH, often, 0.0), axis=1, keepdims=True)
-    alone_times[...] = jnp.broadcast_to(mine, (share, width))
-    most = jnp.max(jnp.where((lane == REACH) | (lane == 0), 0.0, often))
-    sums_work[...] = sums[...]
-
-    @pl.when(most > 1.5)
+
+    @pl.when(again)
     def _():
-        one_lane = lax.broadcasted_iota(jnp.int32, (1, width), 1)
-        cols_work[...] = jnp.zeros_like(cols_work)
-        row_work[...] = jnp.zeros_like(row_work)
-
-        def factor(a, n):
-            row = times[pl.ds(a, 1), :]
-            return jnp.sum(jnp.where(one_lane == n - a + REACH, row, 0.0), axis=1, keepdims=True)
+        extra[...] = jnp.zeros_like(extra)
+        work[...] = jnp.zeros_like(work)
 
         def block(a, state):
             count, place_of = inner_range(meta, table, a)
 
             def inner(t, at):
                 n = place_of(t)
-                tile = inner_old[at] * factor(a, n)
-                inner_tiles[at] = tile
-                row_work[a] = row_work[a] + tile
+                tile = tiles_in[at]
+                work[a] = work[a] + tile * factor(times, a, n)
                 there = pl.ds(n, 1)
-                cols_work[there, :] = cols_work[there, :] + jnp.sum(tile, axis=0, keepdims=True)
+                down = jnp.sum(tile, axis=0, keepdims=True)
+                extra[there, :] = extra[there, :] + down * factor(times, n, a)
                 return at + 1
 
             at = lax.fori_loop(0, count, inner, state[0]) + 1
             count, place_far = outer_range(meta, table, a)
 
             def outer(t, at):
-                tile = outer_old[at] * factor(a, place_far(t))
-                outer_tiles[at] = tile
-                row_work[a] = row_work[a] + tile
+                work[a] = work[a] + tiles[at] * factor(times, a, place_far(t))
                 return at + 1
 
             return at, lax.fori_loop(0, count, outer, state[1])
 
         lax.fori_loop(0, meta[0], block, (0, 0))
-        sums_work[...] = lane_sums(row_work, share, width) + cols_work[...]
-
-    own_rows = pl.ds(pl.multiple_of(meta[3], SUB), share)
-    pairs = jnp.where(alive, sums_work[...] + alone[...] * alone_times[...], 0.0)
-    diagonal = 1.0 / density[own_rows, :] + pairs
+        sums_ref[...] = lane_sums(work, share, width) + extra[...]
+
+    alone = jnp.sum(jnp.where(lane == REACH, often, 0.0), axis=1, keepdims=True)
+    pairs = jnp.where(alive, sums_ref[...] + sub_sums(self_ref) * alone, 0.0)
+    diagonal = 1.0 / density[pl.ds(pl.multiple_of(base, SUB), share), :] + pairs
     diagonal_ref[...] = diagonal
     precond_ref[...] = jnp.where(alive, right_side[...], 0.0) / diagonal
 
 
-def apply_inner(meta, table, field, alone_times, tiles, rows_ref, cols_ref, spread):
+def apply_inner(meta, table, again, field, times, tiles, rows_ref, cols_ref, spread, near):
     share, width = field.shape
     chunks = pieces_of(width)
+    near[0:share, :] = field[...]
     spread_columns(spread, lambda a: a, field[...])
     cols_ref[...] = jnp.zeros_like(cols_ref)
 
-    def block(a, at):
-        count, place_of = inner_range(meta, table, a)
-
-        def fetch(t):
-            n = place_of(t)
-            return n, wide(field[pl.ds(n, 1), :])
-
-        def pair(fetched, carry):
-            n, value = fetched
-            at, sums = carry
-            down, result = [], []
+    def run(weighted):
+        def block(a, at):
+            count, place_of = inner_range(meta, table, a)
+
+            def fetch(t):
+                n = place_of(t)
+                return n, wide(near[pl.ds(n, 1), :])
+
+            def pair(fetched, carry):
+                n, value = fetched
+                at, sums = carry
+                if weighted:
+                    value = value * factor(times, a, n)
+                down, result = [], []
+                for here, old in zip(chunks, sums):
+                    tile = tiles[at, here, :]
+                    down.append(tile * spread[a, here, :])
+                    result.append(old + tile * value)
+                there = pl.ds(pl.multiple_of(n * SUB, SUB), SUB)
+                down = tree(down)
+                if weighted:
+                    down = down * factor(times, n, a)
+                cols_ref[there, :] = cols_ref[there, :] + down
+                return at + 1, result
+
+            zero = jnp.zeros((SUB, width), jnp.float32)
+            at, sums = sweep(count, fetch, pair, (at, [zero] * len(chunks)))
+            value = wide(near[pl.ds(a, 1), :] * factor(times, a, a))
             for here, old in zip(chunks, sums):
-                tile = tiles[at, here, :]
-                down.append(tile * spread[a, here, :])
-                result.append(old + tile * value)
-            there = pl.ds(pl.multiple_of(n * SUB, SUB), SUB)
-            cols_ref[there, :] = cols_ref[there, :] + tree(down)
-            return at + 1, result
-
-        zero = jnp.zeros((SUB, width), jnp.float32)
-        at, sums = sweep(count, fetch, pair, (at, [zero] * len(chunks)))
-        here = pl.ds(a, 1)
-        value = wide(field[here, :] * alone_times[here, :])
-        for here, old in zip(chunks, sums):
-            rows_ref[a, here, :] = old + tiles[at, here, :] * value
-        return at + 1
-
-    lax.fori_loop(0, meta[0], block, 0)
-
-
-def apply_outer(meta, table, received, tiles, rows_ref, cols_ref, work, hood):
+                rows_ref[a, here, :] = old + tiles[at, here, :] * value
+            return at + 1
+
+        lax.fori_loop(0, meta[0], block, 0)
+
+    either(again[0], run)
+
+
+def apply_outer(meta, table, again, received, times, tiles, rows_ref, cols_ref, work, hood):
+    first, second, *ends = received
     columns = len(received)
-    share, width = received[0].shape
+    share, width = first.shape
     chunks = pieces_of(width)
     base, filled = meta[3], meta[4]
-    for k, ref in enumerate(received):
-        hood[k * share : (k + 1) * share, :] = ref[...]
     column = lax.div(base, share)
-    last = columns - 2
-    edge = share + filled - base
-    before_at = jnp.where(column == 0, meta[5] - 2 * share, last * share)
-    after_at = (last + 1) * share - 2 * share
-    head_at = jnp.where(column == last + 1, (last + 1) * share, (column - 1) * share) - edge
-
-    def block(a, at):
-        count, place_of = outer_range(meta, table, a)
-
-        def fetch(t):
-            w = share + place_of(t)
-            row = w + jnp.where(w < share, before_at, jnp.where(w < edge, after_at, head_at))
-            return wide(hood[pl.ds(row, 1), :])
-
-        def pair(value, carry):
-            at, sums = carry
-            return at + 1, [old + tiles[at, here, :] * value for here, old in zip(chunks, sums)]
-
-        at, sums = sweep(count, fetch, pair, (at, [rows_ref[a, here, :] for here in chunks]))
-        for here, values in zip(chunks, sums):
-            work[a, here, :] = values
-        return at
-
-    lax.fori_loop(0, meta[0], block, 0)
+    odd = lax.rem(column, 2) == 1
+    before = jnp.where(odd, first[...], second[...])
+    after = jnp.where(odd, second[...], first[...])
+    own = 3 * share
+    for c, end in enumerate(ends, 1):
+        hood[pl.ds(own - meta[5] + c * share, share), :] = end[...]
+    from_last = own - meta[5] + (columns - 1) * share
+    hood[pl.ds(jnp.where(column == 0, from_last, own - share), share), :] = before
+    hood[own + share : own + 2 * share, :] = after
+    head = after
+    for c, end in enumerate(ends, 1):
+        head = jnp.where(column == c, end[...], head)
+    hood[pl.ds(own + jnp.clip(filled - base, 0, 2 * share), share), :] = head
+
+    def run(weighted):
+        def block(a, at):
+            count, place_of = outer_range(meta, table, a)
+
+            def fetch(t):
+                place = place_of(t)
+                value = hood[pl.ds(own + place, 1), :]
+                if weighted:
+                    value = value * factor(times, a, place)
+                return wide(value)
+
+            def pair(value, carry):
+                at, sums = carry
+                return at + 1, [old + tiles[at, here, :] * value for here, old in zip(chunks, sums)]
+
+            at, sums = sweep(count, fetch, pair, (at, [rows_ref[a, here, :] for here in chunks]))
+            for here, values in zip(chunks, sums):
+                work[a, here, :] = values
+            return at
+
+        lax.fori_loop(0, meta[0], block, 0)
+
+    either(again[0], run)
     return jnp.where(alive_rows(meta, share, width), lane_sums(work, share, width) + sub_sums(cols_ref), 0.0)
 
 
-def apply_first(meta, table, diagonal, *rest):
+def apply_first(meta, table, again, diagonal, times, *rest):
     *received, tiles, rows_ref, cols_ref, spill_ref, scaled_ref, work, hood = rest
-    spill = apply_outer(meta, table, received, tiles, rows_ref, cols_ref, work, hood)
+    spill = apply_outer(meta, table, again, received, times, tiles, rows_ref, cols_ref, work, hood)
     spill_ref[...] = spill
     scaled_ref[...] = spill / diagonal[...]
 
 
-def apply_second(meta, table, right_side, precond, spill, scaled, *rest):
+def apply_second(meta, table, again, right_side, precond, spill, scaled, times, *rest):
     *received, tiles, rows_ref, cols_ref, twice_ref, sums_ref, work, hood = rest
-    twice = apply_outer(meta, table, received, tiles, rows_ref, cols_ref, work, hood)
+    twice = apply_outer(meta, table, again, received, times, tiles, rows_ref, cols_ref, work, hood)
     twice_ref[...] = twice
     share, width = twice.shape
     source = jnp.where(alive_rows(meta, share, width), right_side[...], 0.0)
@@ -472,7 +491,7 @@
     outer_tiles = pltpu.VMEM((most_outer, width, width), f32)
     square = pltpu.VMEM((share, width, width), f32)
     narrow = pltpu.VMEM((share * SUB, width), f32)
-    table = jnp.asarray(TABLE)
+    table = jnp.asarray(TABLE.reshape(-1))
 
     def call(kernel, args, outs, scratch=(), work=0, scalars=2, **more):
         return pl.pallas_call(
@@ -487,92 +506,93 @@
             **more,
         )(*args)
 
-    meta, density, tail, head, times = call(
+    meta, density, first, second, _, *times = call(
         prepare,
         (counts, phase_density, positions, phase, neighbours.T),
         [pltpu.SMEM((8,), jnp.int32), jax.ShapeDtypeStruct(phase.shape, f32), message, message,
-         jax.ShapeDtypeStruct((capacity, width), f32)],
+         jax.ShapeDtypeStruct((capacity, width), f32)] + [vector] * columns,
     )
     meta = pltpu.with_memory_space_constraint(meta, pltpu.SMEM)
-    before = lax.ppermute(tail, "piece", [(i, (i + 1) % pieces) for i in range(pieces)])
-    after = lax.ppermute(head, "piece", [((i + 1) % pieces, i) for i in range(pieces)])
-    times = lax.psum_scatter(times, "col", scatter_dimension=0, tiled=True)
+    first = lax.ppermute(first, "piece", [(i, i ^ 1) for i in range(pieces)])
+    second = lax.ppermute(second, "piece", [(i, ((i ^ 1) + (1 if i % 2 else -1) * 2) % pieces) for i in range(pieces)])
+    times = [lax.ppermute(t, "col", [(i, i ^ k) for i in range(columns)]) if k else t for k, t in enumerate(times)]
 
     tiles_in, spread, rows, cols, selfs = call(
         build_inner,
         (meta, table, positions, density),
         [inner_tiles, pltpu.VMEM((share, 4, width, width), f32), square, narrow, narrow],
-        [pltpu.VMEM((capacity, width), f32)],
+        [pltpu.VMEM((4, 2 * share, width), f32)],
         16 * most_inner,
     )
-    tiles_out, sums, alone = call(
+    again, tiles_out, diagonal, precond, times = call(
         build_outer,
-        (meta, table, positions, density, before, after, held(spread), held(rows), held(cols), held(selfs)),
-        [outer_tiles, vector, vector],
-        [pltpu.VMEM((4, capacity + 2 * share, width), f32), pltpu.VMEM((share, width, width), f32)],
+        (meta, table, positions, density, first, second, right_side,
+         held(tiles_in), held(spread), held(rows), held(cols), held(selfs), *times),
+        [pltpu.SMEM((1,), jnp.int32), outer_tiles, vector, vector, vector],
+        [pltpu.VMEM((4, capacity + 2 * share, width), f32), pltpu.VMEM((share, width, width), f32)]
+        + [pltpu.VMEM((share, width), f32)] * 2,
         16 * most_outer,
     )
-    tiles_in, tiles_out, diagonal, precond, alone_times = call(
-        settle,
-        (meta, table, times, density, right_side, sums, alone, held(tiles_in), held(tiles_out)),
-        [inner_tiles, outer_tiles, vector, vector, vector],
-        [pltpu.VMEM((share, width), f32)] * 2 + [pltpu.VMEM((share, width, width), f32)],
-        input_output_aliases={7: 0, 8: 1},
-    )
+    again = pltpu.with_memory_space_constraint(again, pltpu.SMEM)
 
     def inner(field):
         return call(
             apply_inner,
-            (meta, table, field, alone_times, held(tiles_in)),
+            (meta, table, again, field, times, held(tiles_in)),
             [square, narrow],
-            [pltpu.VMEM((share, width, width), f32)],
+            [pltpu.VMEM((share, width, width), f32), pltpu.VMEM((2 * share, width), f32)],
             4 * most_inner,
+            scalars=3,
         )
 
     def exchange(field):
+        axes = ("piece", "col")
         count = pieces * columns
-        axes = ("piece", "col")
-        received = []
+        swaps = [[i ^ 1 for i in range(count)], [i - 1 if i % 2 == 0 else i + 1 for i in range(count)]]
+        swaps[1][0], swaps[1][-1] = count - 1, 0
         for c in range(1, columns - 1):
-            pairs = []
+            to = {}
+            for p in range(pieces - 1):
+                low, high = p * columns + c, (p + 1) * columns
+                to[low], to[high] = high, low
             for p in range(pieces):
-                low, high = p * columns + c, (p + 1) % pieces * columns
-                pairs += [(low, high), (high, low)]
-                rest = [p * columns + k for k in range(1, columns) if k != c]
-                pairs += list(zip(rest, rest[1:] + rest[:1]))
-            received.append(lax.ppermute(field, axes, pairs))
-        received.append(lax.ppermute(field, axes, [(i, (i + 1) % count) for i in range(count)]))
-        received.append(lax.ppermute(field, axes, [((i + 1) % count, i) for i in range(count)]))
-        return received
-
-    scratch = [pltpu.VMEM((share, width, width), f32), pltpu.VMEM((columns * share, width), f32)]
+                rest = [i for i in range(p * columns, (p + 1) * columns) if i not in to]
+                to.update(zip(rest, rest[1:] + rest[:1]))
+            swaps.append([to[i] for i in range(count)])
+        return [lax.ppermute(field, axes, list(enumerate(to))) for to in swaps]
+
+    scratch = [pltpu.VMEM((share, width, width), f32), pltpu.VMEM((8 * share, width), f32)]
 
     received = exchange(precond)
     rows, cols = inner(precond)
     spill, scaled = call(
         apply_first,
-        (meta, table, diagonal, *received, held(tiles_out), held(rows), held(cols)),
+        (meta, table, again, diagonal, times, *received, held(tiles_out), held(rows), held(cols)),
         [vector, vector],
         scratch,
         2 * most_outer,
+        scalars=3,
     )
 
     received = exchange(scaled)
     rows, cols = inner(scaled)
     twice, sums = call(
         apply_second,
-        (meta, table, right_side, precond, spill, scaled, *received, held(tiles_out), held(rows), held(cols)),
+        (meta, table, again, right_side, precond, spill, scaled, times, *received, held(tiles_out), held(rows), held(cols)),
         [vector, few],
         scratch,
         2 * most_outer,
+        scalars=3,
     )
 
-    steps = [("col", 1 << k) for k in range(columns.bit_length() - 1)]
-    steps += [("piece", 1 << k) for k in range(pieces.bit_length() - 1)]
-    other = None
-    for axis, step in steps:
-        sums = sums if other is None else sums + other
-        other = lax.ppermute(sums, axis, [(i, i ^ step) for i in range(lax.axis_size(axis))])
+    def swap(values, axis, step):
+        return lax.ppermute(values, axis, [(i, i ^ step) for i in range(lax.axis_size(axis))])
+
+    sums = tree([sums] + [swap(sums, "col", k) for k in range(1, columns)])
+    steps = [1 << k for k in range(pieces.bit_length() - 1)]
+    for step in steps[:-1]:
+        sums = sums + swap(sums, "piece", step)
+    other = swap(sums, "piece", steps[-1])
 
     return tuple(call(
         finish,

time: 147 us -> 92.6 us (0.63); the launches traced: 145 us -> 92.1 us
  local copies, waits for them, and re-layouts: 48.1 us -> 6.79 us
  between operations: 14.2 us -> 0.78 us
  starting transfers between devices: 29.4 us -> 32.6 us
  waiting for transfers between devices: 8.99 us -> 7.21 us
    unnamed x48 -> x18, local copies, waits for them, and re-layouts: 48.1 us -> 6.79 us
    ppermute x15 -> x19, starting transfers between devices: 29.4 us -> 32.6 us  [the longest x8 12.8 us: exchange(): return [lax.ppermute(field, axes, list(enumerate(to))) for to in swaps]]
    ppermute x15 -> x19, waiting for transfers between devices: 8.97 us -> 7.21 us  [the longest x6 7.17 us: swap(): lax.ppermute(values, axis, [(i, i ^ step) for i in range(lax.axis_size(ax...]
    pallas_call x9 -> x8, Pallas kernels: 44 us -> 44.7 us  [call(): pl.pallas_call(kernel, out_shape=outs, in_specs=[SMEM] * scalars + [VMEM]...]
  transfers between devices with their start and end apart: 16 -> 19, of which waited for: 5 -> 5; matrix products, arithmetic and copies ran while one was open for 0% -> 0% of each run, Pallas kernels for 22% -> 31%
where the time goes in v4:
time: 92.6 us; the launch traced here: 92.1 us
  Pallas kernels  44.7 us (48%)
  starting transfers between devices  32.6 us (35%)
  waiting for transfers between devices  7.21 us (8%)
  local copies, waits for them, and re-layouts  6.79 us (7%)
    pallas_call x8, Pallas kernels, call(): pl.pallas_call(kernel, out_shape=outs, in_specs=[SMEM] * scalars + [VMEM]...  44.7 us
    ppermute x8, starting transfers between devices, exchange(): return [lax.ppermute(field, axes, list(enumerate(to))) for to in swaps]  12.8 us
    ppermute x6, starting transfers between devices, swap(): lax.ppermute(values, axis, [(i, i ^ step) for i in range(lax.axis_size(ax...  11.4 us
    ppermute x6, waiting for transfers between devices, swap(): lax.ppermute(values, axis, [(i, i ^ step) for i in range(lax.axis_size(ax...  7.17 us
    unnamed x18, local copies, waits for them, and re-layouts  6.79 us
    ppermute x3, starting transfers between devices, body(): lax.ppermute(t, 'col', [(i, i ^ k) for i in range(columns)])  4.39 us
    ppermute x1, starting transfers between devices, body(): lax.ppermute(second, 'piece', [(i, ((i ^ 1) + (1 if i % 2 else -1) * 2) %...  3.56 us
  transfers between devices with their start and end apart: 19, of which 5 were waited for; matrix products, arithmetic and copies ran while one was open for 0% of the time, Pallas kernels for 31%

profile of v4, /device:TPU:0, one launch (start us, length us, event | category | flops | bytes accessed | tf_op | source)
XLA Modules:
  0.0 92.1 jit_solution(1041958337438002270)
XLA Ops:
  0.6 0.0 copy-start
  0.6 0.9 copy-done
  1.6 0.0 copy-start.5
  1.6 0.8 copy-done.5
  2.4 0.0 copy-start.6
  2.4 0.7 copy-done.6
  3.1 0.0 copy-start.7
  3.1 0.7 copy-done.7
  3.7 0.0 copy-start.8
  3.7 0.7 copy-done.8
  4.4 1.3 %prepare.1 = (s32[8]{0:T(128)S(4)}, f32[128,128]{1,0:T(8,128)S(1)}, f32[4,32,128]{2,1,0:T(8,128)S(1)}, f32[4,32,128]{2,1,0:T(8,128)S(1)}, f32[128,128]{1,0:T(8,1...) custom-call(s32[8]{0:T(128)S(1)} %copy-done.7, ...), custom_call_target="tpu_custom_call" | custom-call | tf_op jit(solution)/shard_map/prepare/pallas_call | solution.py:497
  5.7 0.5 collective-permute-start
  6.2 3.6 %collective-permute-start.1 = (f32[4,32,128]{2,1,0:T(8,128)S(1)}, f32[4,32,128]{2,1,0:T(8,128)S(1)}, u32[]{:S(2)}, u32[]{:S(2)}) collective-permute-start(f32[4,32,128]{2,1,0:T(8,128)S(1)} %get-tuple-element.31), channel_id=1, source_target_pairs={{0,28},{4,8},{8,4},{12,16},{16,12},{20,24},{24,20},{28,0},{1,29},{... | collective-permute-start | bytes 196616 | tf_op jit(solution)/shard_map/ppermute | solution.py:517
  9.7 1.6 %collective-permute-start.2 = (f32[32,128]{1,0:T(8,128)S(1)}, f32[32,128]{1,0:T(8,128)S(1)}, u32[]{:S(2)}, u32[]{:S(2)}) collective-permute-start(f32[32,128]{1,0:T(8,128)S(1)} %get-tuple-element.38), channel_id=1, source_target_pairs={{0,1},{1,0},{2,3},{3,2},{4,5},{5,4},{6,7},{7,6},{8,9},{9,8},{10,11... | collective-permute-start | bytes 49160 | tf_op jit(solution)/shard_map/ppermute | solution.py:518
  11.3 2.6 %collective-permute-start.3 = (f32[32,128]{1,0:T(8,128)S(1)}, f32[32,128]{1,0:T(8,128)S(1)}, u32[]{:S(2)}, u32[]{:S(2)}) collective-permute-start(f32[32,128]{1,0:T(8,128)S(1)} %get-tuple-element.39), channel_id=1, source_target_pairs={{0,2},{1,3},{2,0},{3,1},{4,6},{5,7},{6,4},{7,5},{8,10},{9,11},{10,... | collective-permute-start | bytes 49160 | tf_op jit(solution)/shard_map/ppermute | solution.py:518
  13.9 0.2 collective-permute-start.4
  14.1 0.0 copy-start.1
  14.1 0.9 %copy-done.1 = f32[3,128,128]{2,1,0:T(8,128)S(1)} copy-done((f32[3,128,128]{2,1,0:T(8,128)S(1)}, f32[3,128,128]{2,1,0:T(8,128)}, u32[]{:S(2)}) %copy-start.1) | copy-done | bytes 196632
  15.0 0.0 copy-start.2
  15.0 0.7 copy-done.2
  15.7 14.0 %build_inner.1 = (f32[216,128,128]{2,1,0:T(8,128)S(1)}, f32[32,4,128,128]{3,2,1,0:T(8,128)S(1)}, f32[32,128,128]{2,1,0:T(8,128)S(1)}, f32[256,128]{1,0:T(8,128)S(1)}, f32[256,128]{1,0:T(8,128)S(1)}) custom-call(s32[8]{0:T(128)S(4)} %get-tuple-element.28.meta, s32[1472]{0:T(1024)S(1)} %copy-done.2, f32[3,128,128]{2,1,0:T(8,128)S(1)} %copy-done.1, ...), custom_call_target="tpu_custom_call" | custom-call | flops 56623104 | tf_op jit(solution)/shard_map/build_inner/pallas_call | solution.py:497
  29.7 0.0 collective-permute-done.2.rest_1_
  29.7 0.0 collective-permute-done.3.rest_2_
  29.8 0.0 collective-permute-done.4.rest_3_
  29.8 0.0 collective-permute-done.first
  29.8 0.0 collective-permute-done.1.second
  29.8 0.0 copy-start.3
  29.8 0.7 copy-done.3
  30.5 0.0 copy-start.4
  30.5 0.7 copy-done.4
  31.2 7.2 %build_outer.1 = (s32[1]{0:T(128)S(4)}, f32[222,128,128]{2,1,0:T(8,128)S(1)}, f32[32,128]{1,0:T(8,128)S(1)}, f32[32,128]{1,0:T(8,128)S(1)}, f32[32,128]{1,0:T(8,128)S(1)}) custom-call(s32[8]{0:T(128)S(4)} %get-tuple-element.28.meta, s32[1472]{0:T(1024)S(1)} %copy-done.3, f32[3,128,128]{2,1,0:T(8,128)S(1)} %copy-done.1, ...), custom_call_target="tpu_custom_call" | custom-call | flops 58195968 | tf_op jit(solution)/shard_map/build_outer/pallas_call | solution.py:497
  38.4 5.0 %collective-permute-start.8 = (f32[32,128]{1,0:T(8,128)S(1)}, f32[32,128]{1,0:T(8,128)S(1)}, u32[]{:S(2)}, u32[]{:S(2)}) collective-permute-start(f32[32,128]{1,0:T(8,128)S(1)} %get-tuple-element.41.field.precond), channel_id=1, source_target_pairs={{0,1},{1,3},{2,4},{3,0},{4,2},{5,7},{6,8},{7,5},{8,6},{9,11},{10,1... | collective-permute-start | bytes 49160 | tf_op jit(solution)/shard_map/ppermute | solution.py:562
  43.3 0.4 collective-permute-start.7
  43.7 0.0 collective-permute-start.6
  43.7 0.6 collective-permute-start.5
  44.3 7.2 %apply_inner.2 = (f32[32,128,128]{2,1,0:T(8,128)S(1)}, f32[256,128]{1,0:T(8,128)S(1)}) custom-call(s32[8]{0:T(128)S(4)} %get-tuple-element.28.meta, s32[1472]{0:T(1024)S(1)} %copy-done.3, s32[1]{0:T(128)S(4)} %get-tuple-element.42.again, f32[32,128]{1,0:T(8,128)S(1)} %get-tuple-element.41.field.precond, f32[32,128]{1,0:T(8,128)S(1)} %get-tuple-element.44.times, ...), custom_call_target="tpu_custom_call" | custom-call | flops 14155776 | tf_op jit(solution)/shard_map/apply_inner/pallas_call | solution.py:497
  51.5 0.0 collective-permute-done.8.rest_3_
  51.5 0.0 collective-permute-done.7.rest_2_
  51.5 0.0 collective-permute-done.6.rest_1_
  51.5 0.0 collective-permute-done.5.rest_0_
  51.6 3.3 %apply_first.1 = (f32[32,128]{1,0:T(8,128)S(1)}, f32[32,128]{1,0:T(8,128)S(1)}) custom-call(s32[8]{0:T(128)S(4)} %get-tuple-element.28.meta, s32[1472]{0:T(1024)S(1)} %copy-done.3, s32[1]{0:T(128)S(4)} %get-tuple-element.42.again, f32[32,128]{1,0:T(8,128)S(1)} %get-tuple-element.43.diagonal, f32[32,128]{1,0:T(8,128)S(1)} %get-tuple-element.44.times, ...), custom_call_target="tpu_custom_call" | custom-call | flops 7274496 | tf_op jit(solution)/shard_map/apply_first/pallas_call | solution.py:497
  54.9 2.2 %collective-permute-start.12 = (f32[32,128]{1,0:T(8,128)S(1)}, f32[32,128]{1,0:T(8,128)S(1)}, u32[]{:S(2)}, u32[]{:S(2)}) collective-permute-start(f32[32,128]{1,0:T(8,128)S(1)} %get-tuple-element.49.field.scaled), channel_id=1, source_target_pairs={{0,1},{1,3},{2,4},{3,0},{4,2},{5,7},{6,8},{7,5},{8,6},{9,11},{10,1... | collective-permute-start | bytes 49160 | tf_op jit(solution)/shard_map/ppermute | solution.py:562
  57.1 4.1 %collective-permute-start.11 = (f32[32,128]{1,0:T(8,128)S(1)}, f32[32,128]{1,0:T(8,128)S(1)}, u32[]{:S(2)}, u32[]{:S(2)}) collective-permute-start(f32[32,128]{1,0:T(8,128)S(1)} %get-tuple-element.49.field.scaled), channel_id=1, source_target_pairs={{0,2},{1,4},{2,3},{3,0},{4,1},{5,8},{6,7},{7,6},{8,5},{9,12},{10,1... | collective-permute-start | bytes 49160 | tf_op jit(solution)/shard_map/ppermute | solution.py:562
  61.2 0.0 collective-permute-start.10
  61.2 0.6 collective-permute-start.9
  61.7 7.2 %apply_inner.3 = (f32[32,128,128]{2,1,0:T(8,128)S(1)}, f32[256,128]{1,0:T(8,128)S(1)}) custom-call(s32[8]{0:T(128)S(4)} %get-tuple-element.28.meta, s32[1472]{0:T(1024)S(1)} %copy-done.3, s32[1]{0:T(128)S(4)} %get-tuple-element.42.again, f32[32,128]{1,0:T(8,128)S(1)} %get-tuple-element.49.field.scaled, f32[32,128]{1,0:T(8,128)S(1)} %get-tuple-element.44.times, ...), custom_call_target="tpu_custom_call" | custom-call | flops 14155776 | tf_op jit(solution)/shard_map/apply_inner/pallas_call | solution.py:497
  69.0 0.0 collective-permute-done.12.rest_3_
  69.0 0.0 collective-permute-done.11.rest_2_
  69.0 0.0 collective-permute-done.10.rest_1_
  69.0 0.0 collective-permute-done.9.rest_0_
  69.0 3.5 %apply_second.1 = (f32[32,128]{1,0:T(8,128)S(1)}, f32[8,128]{1,0:T(8,128)S(1)}) custom-call(s32[8]{0:T(128)S(4)} %get-tuple-element.28.meta, s32[1472]{0:T(1024)S(1)} %copy-done.3, s32[1]{0:T(128)S(4)} %get-tuple-element.42.again, f32[32,128]{1,0:T(8,128)S(1)} %copy-done.4, f32[32,128]{1,0:T(8,128)S(1)} %get-tuple-element.41.field.precond, ...), custom_call_target="tpu_custom_call" | custom-call | flops 7274496 | tf_op jit(solution)/shard_map/apply_second/pallas_call | solution.py:497
  72.5 0.0 collective-permute-start.15
  72.5 3.6 %collective-permute-start.14 = (f32[8,128]{1,0:T(8,128)S(1)}, f32[8,128]{1,0:T(8,128)S(1)}, u32[]{:S(2)}, u32[]{:S(2)}) collective-permute-start(f32[8,128]{1,0:T(8,128)S(1)} %get-tuple-element.53), channel_id=1, source_target_pairs={{0,2},{1,3},{2,0},{3,1},{4,6},{5,7},{6,4},{7,5},{8,10},{9,11},{10,... | collective-permute-start | bytes 12296 | tf_op jit(solution)/shard_map/ppermute | solution.py:589
  76.1 0.8 collective-permute-start.13
  76.9 1.0 %collective-permute-done.15 = f32[8,128]{1,0:T(8,128)S(1)} collective-permute-done((f32[8,128]{1,0:T(8,128)S(1)}, f32[8,128]{1,0:T(8,128)S(1)}, u32[]{:S(2)}, u32[]{:S(2)}) %collective-permute-start.15) | collective-permute-done | bytes 4128 | tf_op jit(solution)/shard_map/ppermute | solution.py:589
  77.9 0.0 collective-permute-done.14
  77.9 1.8 %collective-permute-done.13 = f32[8,128]{1,0:T(8,128)S(1)} collective-permute-done((f32[8,128]{1,0:T(8,128)S(1)}, f32[8,128]{1,0:T(8,128)S(1)}, u32[]{:S(2)}, u32[]{:S(2)}) %collective-permute-start.13) | collective-permute-done | bytes 4128 | tf_op jit(solution)/shard_map/ppermute | solution.py:589
  79.7 0.0 collective-permute-start.16
  79.7 1.2 %collective-permute-done.16 = f32[8,128]{1,0:T(8,128)S(1)} collective-permute-done((f32[8,128]{1,0:T(8,128)S(1)}, f32[8,128]{1,0:T(8,128)S(1)}, u32[]{:S(2)}, u32[]{:S(2)}) %collective-permute-start.16) | collective-permute-done | bytes 4128 | tf_op jit(solution)/shard_map/ppermute | solution.py:589
  80.9 4.1 %collective-permute-start.17 = (f32[8,128]{1,0:T(8,128)S(1)}, f32[8,128]{1,0:T(8,128)S(1)}, u32[]{:S(2)}, u32[]{:S(2)}) collective-permute-start(f32[8,128]{1,0:T(8,128)S(1)} %add.18), channel_id=1, source_target_pairs={{0,8},{4,12},{8,0},{12,4},{16,24},{20,28},{24,16},{28,20},{1,9},{5... | collective-permute-start | bytes 12296 | tf_op jit(solution)/shard_map/ppermute | solution.py:589
  85.0 1.6 %collective-permute-done.17 = f32[8,128]{1,0:T(8,128)S(1)} collective-permute-done((f32[8,128]{1,0:T(8,128)S(1)}, f32[8,128]{1,0:T(8,128)S(1)}, u32[]{:S(2)}, u32[]{:S(2)}) %collective-permute-start.17) | collective-permute-done | bytes 4128 | tf_op jit(solution)/shard_map/ppermute | solution.py:589
  86.6 2.9 %collective-permute-start.18 = (f32[8,128]{1,0:T(8,128)S(1)}, f32[8,128]{1,0:T(8,128)S(1)}, u32[]{:S(2)}, u32[]{:S(2)}) collective-permute-start(f32[8,128]{1,0:T(8,128)S(1)} %add.19.mine), channel_id=1, source_target_pairs={{0,16},{4,20},{8,24},{12,28},{16,0},{20,4},{24,8},{28,12},{1,17},{... | collective-permute-start | bytes 12296 | tf_op jit(solution)/shard_map/ppermute | solution.py:589
  89.5 1.6 %collective-permute-done.18.other = f32[8,128]{1,0:T(8,128)S(1)} collective-permute-done((f32[8,128]{1,0:T(8,128)S(1)}, f32[8,128]{1,0:T(8,128)S(1)}, u32[]{:S(2)}, u32[]{:S(2)}) %collective-permute-start.18) | collective-permute-done | bytes 4128 | tf_op jit(solution)/shard_map/ppermute | solution.py:589
  91.1 0.9 %finish.1 = (f32[32,128]{1,0:T(8,128)}, f32[32,128]{1,0:T(8,128)}) custom-call(s32[8]{0:T(128)S(4)} %get-tuple-element.28.meta, f32[32,128]{1,0:T(8,128)S(1)} %copy-done.4, f32[32,128]{1,0:T(8,128)S(1)} %get-tuple-element.41.field.precond, f32[32,128]{1,0:T(8,128)S(1)} %get-tuple-element.48.spill, f32[32,128]{1,0:T(8,128)S(1)} %get-tuple-element.49.field.scaled, ...), custom_call_target="tpu_custom_call" | custom-call | tf_op jit(solution)/shard_map/finish/pallas_call | solution.py:497
  (3 shorter events, 0.0 us)
Async XLA Ops:
  0.6 0.9 %copy-start = (f32[3,128,128]{2,1,0:T(8,128)S(1)}, f32[3,128,128]{2,1,0:T(8,128)}, u32[]{:S(2)}) copy-start(f32[3,128,128]{2,1,0:T(8,128)} %position.5) | copy-start | bytes 589828
  1.6 0.8 copy-start.5
  2.4 0.7 copy-start.6
  3.1 0.7 copy-start.7
  3.7 0.7 copy-start.8
  5.7 24.1 %collective-permute-start = (f32[4,32,128]{2,1,0:T(8,128)S(1)}, f32[4,32,128]{2,1,0:T(8,128)S(1)}, u32[]{:S(2)}, u32[]{:S(2)}) collective-permute-start(f32[4,32,128]{2,1,0:T(8,128)S(1)} %get-tuple-element.30), channel_id=1, source_target_pairs={{0,4},{4,0},{8,12},{12,8},{16,20},{20,16},{24,28},{28,24},{1,5},{5... | collective-permute-start | bytes 196616 | tf_op jit(solution)/shard_map/ppermute | solution.py:516
  6.2 23.6 %collective-permute-start.1 = (f32[4,32,128]{2,1,0:T(8,128)S(1)}, f32[4,32,128]{2,1,0:T(8,128)S(1)}, u32[]{:S(2)}, u32[]{:S(2)}) collective-permute-start(f32[4,32,128]{2,1,0:T(8,128)S(1)} %get-tuple-element.31), channel_id=1, source_target_pairs={{0,28},{4,8},{8,4},{12,16},{16,12},{20,24},{24,20},{28,0},{1,29},{... | collective-permute-start | bytes 196616 | tf_op jit(solution)/shard_map/ppermute | solution.py:517
  9.7 20.0 %collective-permute-start.2 = (f32[32,128]{1,0:T(8,128)S(1)}, f32[32,128]{1,0:T(8,128)S(1)}, u32[]{:S(2)}, u32[]{:S(2)}) collective-permute-start(f32[32,128]{1,0:T(8,128)S(1)} %get-tuple-element.38), channel_id=1, source_target_pairs={{0,1},{1,0},{2,3},{3,2},{4,5},{5,4},{6,7},{7,6},{8,9},{9,8},{10,11... | collective-permute-start | bytes 49160 | tf_op jit(solution)/shard_map/ppermute | solution.py:518
  11.3 18.5 %collective-permute-start.3 = (f32[32,128]{1,0:T(8,128)S(1)}, f32[32,128]{1,0:T(8,128)S(1)}, u32[]{:S(2)}, u32[]{:S(2)}) collective-permute-start(f32[32,128]{1,0:T(8,128)S(1)} %get-tuple-element.39), channel_id=1, source_target_pairs={{0,2},{1,3},{2,0},{3,1},{4,6},{5,7},{6,4},{7,5},{8,10},{9,11},{10,... | collective-permute-start | bytes 49160 | tf_op jit(solution)/shard_map/ppermute | solution.py:518
  13.9 15.9 %collective-permute-start.4 = (f32[32,128]{1,0:T(8,128)S(1)}, f32[32,128]{1,0:T(8,128)S(1)}, u32[]{:S(2)}, u32[]{:S(2)}) collective-permute-start(f32[32,128]{1,0:T(8,128)S(1)} %get-tuple-element.40), channel_id=1, source_target_pairs={{0,3},{1,2},{2,1},{3,0},{4,7},{5,6},{6,5},{7,4},{8,11},{9,10},{10,... | collective-permute-start | bytes 49160 | tf_op jit(solution)/shard_map/ppermute | solution.py:518
  14.1 0.9 %copy-start.1 = (f32[3,128,128]{2,1,0:T(8,128)S(1)}, f32[3,128,128]{2,1,0:T(8,128)}, u32[]{:S(2)}) copy-start(f32[3,128,128]{2,1,0:T(8,128)} %position.5) | copy-start | bytes 589828
  15.0 0.7 copy-start.2
  29.8 0.7 copy-start.3
  30.5 0.7 copy-start.4
  38.4 13.2 %collective-permute-start.8 = (f32[32,128]{1,0:T(8,128)S(1)}, f32[32,128]{1,0:T(8,128)S(1)}, u32[]{:S(2)}, u32[]{:S(2)}) collective-permute-start(f32[32,128]{1,0:T(8,128)S(1)} %get-tuple-element.41.field.precond), channel_id=1, source_target_pairs={{0,1},{1,3},{2,4},{3,0},{4,2},{5,7},{6,8},{7,5},{8,6},{9,11},{10,1... | collective-permute-start | bytes 49160 | tf_op jit(solution)/shard_map/ppermute | solution.py:562
  43.3 8.2 %collective-permute-start.7 = (f32[32,128]{1,0:T(8,128)S(1)}, f32[32,128]{1,0:T(8,128)S(1)}, u32[]{:S(2)}, u32[]{:S(2)}) collective-permute-start(f32[32,128]{1,0:T(8,128)S(1)} %get-tuple-element.41.field.precond), channel_id=1, source_target_pairs={{0,2},{1,4},{2,3},{3,0},{4,1},{5,8},{6,7},{7,6},{8,5},{9,12},{10,1... | collective-permute-start | bytes 49160 | tf_op jit(solution)/shard_map/ppermute | solution.py:562
  43.7 7.8 %collective-permute-start.6 = (f32[32,128]{1,0:T(8,128)S(1)}, f32[32,128]{1,0:T(8,128)S(1)}, u32[]{:S(2)}, u32[]{:S(2)}) collective-permute-start(f32[32,128]{1,0:T(8,128)S(1)} %get-tuple-element.41.field.precond), channel_id=1, source_target_pairs={{0,31},{1,2},{2,1},{3,4},{4,3},{5,6},{6,5},{7,8},{8,7},{9,10},{10,... | collective-permute-start | bytes 49160 | tf_op jit(solution)/shard_map/ppermute | solution.py:562
  43.7 7.8 %collective-permute-start.5 = (f32[32,128]{1,0:T(8,128)S(1)}, f32[32,128]{1,0:T(8,128)S(1)}, u32[]{:S(2)}, u32[]{:S(2)}) collective-permute-start(f32[32,128]{1,0:T(8,128)S(1)} %get-tuple-element.41.field.precond), channel_id=1, source_target_pairs={{0,1},{1,0},{2,3},{3,2},{4,5},{5,4},{6,7},{7,6},{8,9},{9,8},{10,11... | collective-permute-start | bytes 49160 | tf_op jit(solution)/shard_map/ppermute | solution.py:562
  54.9 14.1 %collective-permute-start.12 = (f32[32,128]{1,0:T(8,128)S(1)}, f32[32,128]{1,0:T(8,128)S(1)}, u32[]{:S(2)}, u32[]{:S(2)}) collective-permute-start(f32[32,128]{1,0:T(8,128)S(1)} %get-tuple-element.49.field.scaled), channel_id=1, source_target_pairs={{0,1},{1,3},{2,4},{3,0},{4,2},{5,7},{6,8},{7,5},{8,6},{9,11},{10,1... | collective-permute-start | bytes 49160 | tf_op jit(solution)/shard_map/ppermute | solution.py:562
  57.1 11.9 %collective-permute-start.11 = (f32[32,128]{1,0:T(8,128)S(1)}, f32[32,128]{1,0:T(8,128)S(1)}, u32[]{:S(2)}, u32[]{:S(2)}) collective-permute-start(f32[32,128]{1,0:T(8,128)S(1)} %get-tuple-element.49.field.scaled), channel_id=1, source_target_pairs={{0,2},{1,4},{2,3},{3,0},{4,1},{5,8},{6,7},{7,6},{8,5},{9,12},{10,1... | collective-permute-start | bytes 49160 | tf_op jit(solution)/shard_map/ppermute | solution.py:562
  61.2 7.8 %collective-permute-start.10 = (f32[32,128]{1,0:T(8,128)S(1)}, f32[32,128]{1,0:T(8,128)S(1)}, u32[]{:S(2)}, u32[]{:S(2)}) collective-permute-start(f32[32,128]{1,0:T(8,128)S(1)} %get-tuple-element.49.field.scaled), channel_id=1, source_target_pairs={{0,31},{1,2},{2,1},{3,4},{4,3},{5,6},{6,5},{7,8},{8,7},{9,10},{10,... | collective-permute-start | bytes 49160 | tf_op jit(solution)/shard_map/ppermute | solution.py:562
  61.2 7.8 %collective-permute-start.9 = (f32[32,128]{1,0:T(8,128)S(1)}, f32[32,128]{1,0:T(8,128)S(1)}, u32[]{:S(2)}, u32[]{:S(2)}) collective-permute-start(f32[32,128]{1,0:T(8,128)S(1)} %get-tuple-element.49.field.scaled), channel_id=1, source_target_pairs={{0,1},{1,0},{2,3},{3,2},{4,5},{5,4},{6,7},{7,6},{8,9},{9,8},{10,11... | collective-permute-start | bytes 49160 | tf_op jit(solution)/shard_map/ppermute | solution.py:562
  72.5 5.4 %collective-permute-start.15 = (f32[8,128]{1,0:T(8,128)S(1)}, f32[8,128]{1,0:T(8,128)S(1)}, u32[]{:S(2)}, u32[]{:S(2)}) collective-permute-start(f32[8,128]{1,0:T(8,128)S(1)} %get-tuple-element.53), channel_id=1, source_target_pairs={{0,3},{1,2},{2,1},{3,0},{4,7},{5,6},{6,5},{7,4},{8,11},{9,10},{10,... | collective-permute-start | bytes 12296 | tf_op jit(solution)/shard_map/ppermute | solution.py:589
  72.5 5.4 %collective-permute-start.14 = (f32[8,128]{1,0:T(8,128)S(1)}, f32[8,128]{1,0:T(8,128)S(1)}, u32[]{:S(2)}, u32[]{:S(2)}) collective-permute-start(f32[8,128]{1,0:T(8,128)S(1)} %get-tuple-element.53), channel_id=1, source_target_pairs={{0,2},{1,3},{2,0},{3,1},{4,6},{5,7},{6,4},{7,5},{8,10},{9,11},{10,... | collective-permute-start | bytes 12296 | tf_op jit(solution)/shard_map/ppermute | solution.py:589
  76.1 3.6 %collective-permute-start.13 = (f32[8,128]{1,0:T(8,128)S(1)}, f32[8,128]{1,0:T(8,128)S(1)}, u32[]{:S(2)}, u32[]{:S(2)}) collective-permute-start(f32[8,128]{1,0:T(8,128)S(1)} %get-tuple-element.53), channel_id=1, source_target_pairs={{0,1},{1,0},{2,3},{3,2},{4,5},{5,4},{6,7},{7,6},{8,9},{9,8},{10,11... | collective-permute-start | bytes 12296 | tf_op jit(solution)/shard_map/ppermute | solution.py:589
  79.7 1.2 %collective-permute-start.16 = (f32[8,128]{1,0:T(8,128)S(1)}, f32[8,128]{1,0:T(8,128)S(1)}, u32[]{:S(2)}, u32[]{:S(2)}) collective-permute-start(f32[8,128]{1,0:T(8,128)S(1)} %add_add_fusion), channel_id=1, source_target_pairs={{0,4},{4,0},{8,12},{12,8},{16,20},{20,16},{24,28},{28,24},{1,5},{5... | collective-permute-start | bytes 12296 | tf_op jit(solution)/shard_map/ppermute | solution.py:589
  80.9 5.7 %collective-permute-start.17 = (f32[8,128]{1,0:T(8,128)S(1)}, f32[8,128]{1,0:T(8,128)S(1)}, u32[]{:S(2)}, u32[]{:S(2)}) collective-permute-start(f32[8,128]{1,0:T(8,128)S(1)} %add.18), channel_id=1, source_target_pairs={{0,8},{4,12},{8,0},{12,4},{16,24},{20,28},{24,16},{28,20},{1,9},{5... | collective-permute-start | bytes 12296 | tf_op jit(solution)/shard_map/ppermute | solution.py:589
  86.6 4.5 %collective-permute-start.18 = (f32[8,128]{1,0:T(8,128)S(1)}, f32[8,128]{1,0:T(8,128)S(1)}, u32[]{:S(2)}, u32[]{:S(2)}) collective-permute-start(f32[8,128]{1,0:T(8,128)S(1)} %add.19.mine), channel_id=1, source_target_pairs={{0,16},{4,20},{8,24},{12,28},{16,0},{20,4},{24,8},{28,12},{1,17},{... | collective-permute-start | bytes 12296 | tf_op jit(solution)/shard_map/ppermute | solution.py:589

commit v5 on v4

--- a/solution.py
+++ b/solution.py
@@ -13,6 +13,7 @@
 SUB = 8
 VMEM = pl.BlockSpec(memory_space=pltpu.VMEM)
 SMEM = pl.BlockSpec(memory_space=pltpu.SMEM)
+HBM = pl.BlockSpec(memory_space=pltpu.HBM)
 
 
 def stencil_tables():
@@ -92,18 +93,25 @@
 
 def sweep(count, fetch, step, carry):
     def both(i, state):
-        carry, first, second = state
+        carry, *now = state
         later = fetch(2 * i + 2), fetch(2 * i + 3)
-        return step(second, step(first, carry)), *later
+        return step(now, carry), *later
 
     carry, first, _ = lax.fori_loop(0, lax.div(count, 2), both, (carry, fetch(0), fetch(1)))
-    return lax.fori_loop(0, lax.rem(count, 2), lambda _, carry: step(first, carry), carry)
+    return lax.fori_loop(0, lax.rem(count, 2), lambda _, carry: step([first], carry), carry)
 
 
 def tree(terms):
     while len(terms) > 1:
         terms = [a + b for a, b in zip(terms[::2], terms[1::2])] + terms[len(terms) // 2 * 2 :]
     return terms[0]
+
+
+def gather(partial, c, term):
+    if c < len(partial):
+        partial[c] = term
+    else:
+        partial[c % len(partial)] = partial[c % len(partial)] + term
 
 
 def pieces_of(width):
@@ -146,9 +154,23 @@
     return lax.broadcasted_iota(jnp.int32, (share, width), 0) < meta[0]
 
 
-def prepare(counts, densities, position, phase, listed, meta, density, first_swap, second_swap, times, *times_out):
-    share, width = first_swap.shape[1:]
+def prepare(
+    counts, densities, position_in, phase_in, listed_in, right_side_in, table_in,
+    meta, table, hood, near, density, source, first_swap, second_swap, *rest
+):
+    *times_out, phase, listed, right_side, times, sems = rest
+    share, width = source.shape
     capacity = phase.shape[0]
+    body_rows = pl.ds(share, capacity)
+    copies = [
+        pltpu.make_async_copy(phase_in, phase, sems.at[0]),
+        pltpu.make_async_copy(position_in, hood.at[pl.ds(0, 3), body_rows, :], sems.at[1]),
+        pltpu.make_async_copy(listed_in, listed, sems.at[2]),
+        pltpu.make_async_copy(right_side_in, right_side, sems.at[3]),
+        pltpu.make_async_copy(table_in, table, sems.at[4]),
+    ]
+    for copy in copies:
+        copy.start()
     piece, column = lax.axis_index("piece"), lax.axis_index("col")
     filled = counts[piece]
     filled_before = counts[jnp.maximum(piece - 1, 0)]
@@ -163,15 +185,22 @@
     meta[3] = column * share
     meta[4] = filled
     meta[5] = filled_before
+    own_rows = pl.ds(pl.multiple_of(share + column * share, SUB), share)
+    copies[0].wait()
     labels = phase[...]
-    density[...] = sum(jnp.where(labels == k, densities[k], 0.0) for k in range(densities.shape[0]))
-    last = pl.ds(filled - share, share)
+    whole = sum(jnp.where(labels == k, densities[k], 0.0) for k in range(densities.shape[0]))
+    hood[3, body_rows, :] = whole * (width / 2.0)
+    density[...] = hood[3, own_rows, :] * (2.0 / width)
+    copies[1].wait()
     even = lax.rem(piece, 2) == 0
     for k in range(4):
-        rows = position.at[k] if k < 3 else density
-        tail, head = rows[last, :], rows[0:share, :]
+        tail, head = hood[k, pl.ds(filled, share), :], hood[k, share : 2 * share, :]
         first_swap[k] = jnp.where(even, tail, head)
         second_swap[k] = jnp.where(even, head, tail)
+        near[k, 0:share, :] = hood[k, own_rows, :]
+    for copy in copies[2:]:
+        copy.wait()
+    source[...] = jnp.where(alive_rows(meta, share, width), right_side[...], 0.0)
     ids = listed[...]
     own = lax.broadcasted_iota(jnp.int32, ids.shape, 1)
     slot = ids - piece * capacity
@@ -185,15 +214,11 @@
         out[...] = times[pl.ds(pl.multiple_of((column ^ k) * share, SUB), share), :]
 
 
-def build_inner(meta, table, position, density, tiles, spread, rows_ref, cols_ref, self_ref, near):
+def build_inner(meta, table, near, tiles, spread, rows_ref, cols_ref, self_ref):
     share, width = rows_ref.shape[0], rows_ref.shape[2]
     chunks = pieces_of(width)
-    base = meta[3]
-    own_rows = pl.ds(pl.multiple_of(base, SUB), share)
     for k in range(4):
-        values = position[k, own_rows, :] if k < 3 else density[own_rows, :] * (width / 2.0)
-        near[k, 0:share, :] = values
-        spread_columns(spread, lambda a: (a, k), values)
+        spread_columns(spread, lambda a: (a, k), near[k, 0:share, :])
     cols_ref[...] = jnp.zeros_like(cols_ref)
 
     def rows_at(n):
@@ -206,32 +231,37 @@
             n = place_of(t)
             return n, rows_at(n)
 
-        def pair(fetched, carry):
-            n, other = fetched
+        def pairs(fetched, carry):
             at, sums = carry
+            down = [[None] * 4 for _ in fetched]
             result = []
-            for here in chunks:
-                tile = pair_chunk([spread[a, k, here, :] for k in range(4)], other)
-                tiles[at, here, :] = tile
-                result.append(tile)
-            there = pl.ds(pl.multiple_of(n * SUB, SUB), SUB)
-            cols_ref[there, :] = cols_ref[there, :] + tree(result)
-            return at + 1, [old + new for old, new in zip(sums, result)]
+            for c, (here, total) in enumerate(zip(chunks, sums)):
+                own = [spread[a, k, here, :] for k in range(4)]
+                for t, (_, other) in enumerate(fetched):
+                    tile = pair_chunk(own, other)
+                    tiles[at + t, here, :] = tile
+                    gather(down[t], c, tile)
+                    total = total + tile
+                result.append(total)
+            for (n, _), partial in zip(fetched, down):
+                there = pl.ds(pl.multiple_of(n * SUB, SUB), SUB)
+                cols_ref[there, :] = cols_ref[there, :] + tree(partial)
+            return at + len(fetched), result
 
         zero = jnp.zeros((SUB, width), jnp.float32)
-        at, sums = sweep(count, fetch, pair, (at, [zero] * len(chunks)))
+        at, sums = sweep(count, fetch, pairs, (at, [zero] * len(chunks)))
         for here, values in zip(chunks, sums):
             rows_ref[a, here, :] = values
         other = rows_at(a)
         lane = lax.broadcasted_iota(jnp.int32, (SUB, width), 1)
         sublane = lax.broadcasted_iota(jnp.int32, (SUB, width), 0)
-        result = []
+        down = [None] * 4
         for c, here in enumerate(chunks):
             tile = pair_chunk([spread[a, k, here, :] for k in range(4)], other)
             tile = jnp.where(lane == sublane + c * SUB, 0.0, tile)
             tiles[at, here, :] = tile
-            result.append(tile)
-        self_ref[pl.ds(pl.multiple_of(a * SUB, SUB), SUB), :] = tree(result)
+            gather(down, c, tile)
+        self_ref[pl.ds(pl.multiple_of(a * SUB, SUB), SUB), :] = tree(down)
         return at + 1
 
     lax.fori_loop(0, meta[0], block, 0)
@@ -253,22 +283,17 @@
 
 
 def build_outer(
-    meta, table, position, density, first, second, right_side, tiles_in, spread, rows_ref, cols_ref, self_ref, *rest
+    meta, table, around, first, second, density, source, tiles_in, spread, rows_ref, cols_ref, self_ref, *rest
 ):
-    *times_in, again_ref, tiles, diagonal_ref, precond_ref, times, hood, work, sums_ref, extra = rest
+    *times_in, again_ref, tiles, diagonal_ref, precond_ref, times, alone_ref, hood, work, sums_ref, extra = rest
     share, width = diagonal_ref.shape
     chunks = pieces_of(width)
-    capacity = density.shape[0]
     base, filled = meta[3], meta[4]
-    scale = width / 2.0
     even = lax.rem(lax.axis_index("piece"), 2) == 0
     for k in range(4):
-        gain = 1.0 if k < 3 else scale
-        before = jnp.where(even, second[k], first[k]) * gain
-        after = jnp.where(even, first[k], second[k]) * gain
-        hood[k, 0:share, :] = before
-        hood[k, share : share + capacity, :] = position[k] if k < 3 else density[...] * gain
-        hood[k, pl.ds(share + filled, share), :] = after
+        hood[k, 0:share, :] = jnp.where(even, second[k], first[k])
+        hood[k, share:, :] = around[k, share:, :]
+        hood[k, pl.ds(share + filled, share), :] = jnp.where(even, first[k], second[k])
     alive = alive_rows(meta, share, width)
     often = jnp.where(alive, tree([ref[...] for ref in times_in]), 0.0)
     times[...] = often
@@ -283,16 +308,19 @@
             here = pl.ds(base + share + place_of(t), 1)
             return [wide(hood[k, here, :]) for k in range(4)]
 
-        def pair(other, carry):
+        def pairs(fetched, carry):
             at, sums = carry
             result = []
-            for here, old in zip(chunks, sums):
-                tile = pair_chunk([spread[a, k, here, :] for k in range(4)], other)
-                tiles[at, here, :] = tile
-                result.append(old + tile)
-            return at + 1, result
-
-        at, sums = sweep(count, fetch, pair, (at, [rows_ref[a, here, :] for here in chunks]))
+            for here, total in zip(chunks, sums):
+                own = [spread[a, k, here, :] for k in range(4)]
+                for t, other in enumerate(fetched):
+                    tile = pair_chunk(own, other)
+                    tiles[at + t, here, :] = tile
+                    total = total + tile
+                result.append(total)
+            return at + len(fetched), result
+
+        at, sums = sweep(count, fetch, pairs, (at, [rows_ref[a, here, :] for here in chunks]))
         for here, values in zip(chunks, sums):
             work[a, here, :] = values
         return at
@@ -330,16 +358,18 @@
         sums_ref[...] = lane_sums(work, share, width) + extra[...]
 
     alone = jnp.sum(jnp.where(lane == REACH, often, 0.0), axis=1, keepdims=True)
+    alone_ref[...] = jnp.broadcast_to(alone, (share, width))
     pairs = jnp.where(alive, sums_ref[...] + sub_sums(self_ref) * alone, 0.0)
-    diagonal = 1.0 / density[pl.ds(pl.multiple_of(base, SUB), share), :] + pairs
+    diagonal = 1.0 / density[...] + pairs
     diagonal_ref[...] = diagonal
-    precond_ref[...] = jnp.where(alive, right_side[...], 0.0) / diagonal
-
-
-def apply_inner(meta, table, again, field, times, tiles, rows_ref, cols_ref, spread, near):
+    precond_ref[...] = source[...] / diagonal
+
+
+def apply_inner(meta, table, again, field, alone, times, tiles, rows_ref, cols_ref, spread, near, lone):
     share, width = field.shape
     chunks = pieces_of(width)
     near[0:share, :] = field[...]
+    lone[...] = field[...] * alone[...]
     spread_columns(spread, lambda a: a, field[...])
     cols_ref[...] = jnp.zeros_like(cols_ref)
 
@@ -351,26 +381,30 @@
                 n = place_of(t)
                 return n, wide(near[pl.ds(n, 1), :])
 
-            def pair(fetched, carry):
-                n, value = fetched
+            def pairs(fetched, carry):
                 at, sums = carry
                 if weighted:
-                    value = value * factor(times, a, n)
-                down, result = [], []
-                for here, old in zip(chunks, sums):
-                    tile = tiles[at, here, :]
-                    down.append(tile * spread[a, here, :])
-                    result.append(old + tile * value)
-                there = pl.ds(pl.multiple_of(n * SUB, SUB), SUB)
-                down = tree(down)
-                if weighted:
-                    down = down * factor(times, n, a)
-                cols_ref[there, :] = cols_ref[there, :] + down
-                return at + 1, result
+                    fetched = [(n, value * factor(times, a, n)) for n, value in fetched]
+                down = [[None] * 4 for _ in fetched]
+                result = []
+                for c, (here, total) in enumerate(zip(chunks, sums)):
+                    own = spread[a, here, :]
+                    for t, (_, value) in enumerate(fetched):
+                        tile = tiles[at + t, here, :]
+                        gather(down[t], c, tile * own)
+                        total = total + tile * value
+                    result.append(total)
+                for (n, _), partial in zip(fetched, down):
+                    there = pl.ds(pl.multiple_of(n * SUB, SUB), SUB)
+                    partial = tree(partial)
+                    if weighted:
+                        partial = partial * factor(times, n, a)
+                    cols_ref[there, :] = cols_ref[there, :] + partial
+                return at + len(fetched), result
 
             zero = jnp.zeros((SUB, width), jnp.float32)
-            at, sums = sweep(count, fetch, pair, (at, [zero] * len(chunks)))
-            value = wide(near[pl.ds(a, 1), :] * factor(times, a, a))
+            at, sums = sweep(count, fetch, pairs, (at, [zero] * len(chunks)))
+            value = wide(lone[pl.ds(a, 1), :])
             for here, old in zip(chunks, sums):
                 rows_ref[a, here, :] = old + tiles[at, here, :] * value
             return at + 1
@@ -412,11 +446,16 @@
                     value = value * factor(times, a, place)
                 return wide(value)
 
-            def pair(value, carry):
+            def pairs(values, carry):
                 at, sums = carry
-                return at + 1, [old + tiles[at, here, :] * value for here, old in zip(chunks, sums)]
-
-            at, sums = sweep(count, fetch, pair, (at, [rows_ref[a, here, :] for here in chunks]))
+                result = []
+                for here, total in zip(chunks, sums):
+                    for t, value in enumerate(values):
+                        total = total + tiles[at + t, here, :] * value
+                    result.append(total)
+                return at + len(values), result
+
+            at, sums = sweep(count, fetch, pairs, (at, [rows_ref[a, here, :] for here in chunks]))
             for here, values in zip(chunks, sums):
                 work[a, here, :] = values
             return at
@@ -434,23 +473,21 @@
     scaled_ref[...] = spill / diagonal[...]
 
 
-def apply_second(meta, table, again, right_side, precond, spill, scaled, times, *rest):
+def apply_second(meta, table, again, source, precond, spill, scaled, times, *rest):
     *received, tiles, rows_ref, cols_ref, twice_ref, sums_ref, work, hood = rest
     twice = apply_outer(meta, table, again, received, times, tiles, rows_ref, cols_ref, work, hood)
     twice_ref[...] = twice
     share, width = twice.shape
-    source = jnp.where(alive_rows(meta, share, width), right_side[...], 0.0)
     lane = lax.broadcasted_iota(jnp.int32, (1, width), 1)
     sums = jnp.zeros((1, width), jnp.float32)
-    pairs = ((source, precond[...]), (spill[...], precond[...]), (spill[...], scaled[...]), (scaled[...], twice))
+    pairs = ((source[...], precond[...]), (spill[...], precond[...]), (spill[...], scaled[...]), (scaled[...], twice))
     for k, (first, second) in enumerate(pairs):
         along = jnp.sum(first * second, axis=0, keepdims=True)
         sums = jnp.where(lane == k, jnp.sum(along, axis=1, keepdims=True), sums)
     sums_ref[...] = wide(sums)
 
 
-def finish(meta, right_side, precond, spill, scaled, twice, mine, other, solution_ref, residual_ref):
-    share, width = precond.shape
+def finish(source, precond, spill, scaled, twice, mine, other, solution_ref, residual_ref):
     sums = mine[...] + other[...]
 
     def pick(k):
@@ -464,11 +501,10 @@
     bent = keep * keep * cross + 2.0 * keep * advance * square + advance * advance * last
     blend = weighted_next / weighted
     advance_next = weighted_next / (weighted_next - bent - blend * weighted_next / advance)
-    source = jnp.where(alive_rows(meta, share, width), right_side[...], 0.0)
-    residual = keep * source + advance * spill[...]
+    residual = keep * source[...] + advance * spill[...]
     next_precond = keep * precond[...] + advance * scaled[...]
     direction = next_precond + blend * precond[...]
-    image = residual - keep * spill[...] - advance * twice[...] + blend * (source - spill[...])
+    image = residual - keep * spill[...] - advance * twice[...] + blend * (source[...] - spill[...])
     solution_ref[...] = advance * precond[...] + advance_next * direction
     residual_ref[...] = residual - advance_next * image
 
@@ -493,11 +529,11 @@
     narrow = pltpu.VMEM((share * SUB, width), f32)
     table = jnp.asarray(TABLE.reshape(-1))
 
-    def call(kernel, args, outs, scratch=(), work=0, scalars=2, **more):
+    def call(kernel, args, outs, scratch=(), work=0, scalars=2, far=0, **more):
         return pl.pallas_call(
             kernel,
             out_shape=outs,
-            in_specs=[SMEM] * scalars + [VMEM] * (len(args) - scalars),
+            in_specs=[SMEM] * scalars + [HBM] * far + [VMEM] * (len(args) - scalars - far),
             out_specs=[SMEM if getattr(o, "memory_space", None) == pltpu.SMEM else VMEM for o in outs],
             scratch_shapes=scratch,
             compiler_params=LIMIT,
@@ -506,29 +542,37 @@
             **more,
         )(*args)
 
-    meta, density, first, second, _, *times = call(
+    def away(array):
+        return pltpu.with_memory_space_constraint(array, pltpu.HBM)
+
+    around = jax.ShapeDtypeStruct((4, capacity + 2 * share, width), f32)
+    near = jax.ShapeDtypeStruct((4, 2 * share, width), f32)
+    far = [away(array) for array in (positions, phase, neighbours.T, right_side, table)]
+    meta, table, around, near, density, source, first, second, *times = call(
         prepare,
-        (counts, phase_density, positions, phase, neighbours.T),
-        [pltpu.SMEM((8,), jnp.int32), jax.ShapeDtypeStruct(phase.shape, f32), message, message,
-         jax.ShapeDtypeStruct((capacity, width), f32)] + [vector] * columns,
+        (away(counts), away(phase_density), *far),
+        [pltpu.SMEM((8,), jnp.int32), pltpu.SMEM(table.shape, jnp.int32), around, near, vector, vector, message, message]
+        + [vector] * columns,
+        [pltpu.VMEM(phase.shape, jnp.int32), pltpu.VMEM(far[2].shape, jnp.int32), pltpu.VMEM((share, width), f32),
+         pltpu.VMEM((capacity, width), f32), pltpu.SemaphoreType.DMA((5,))],
+        far=len(far),
     )
-    meta = pltpu.with_memory_space_constraint(meta, pltpu.SMEM)
+    meta, table = (pltpu.with_memory_space_constraint(array, pltpu.SMEM) for array in (meta, table))
     first = lax.ppermute(first, "piece", [(i, i ^ 1) for i in range(pieces)])
     second = lax.ppermute(second, "piece", [(i, ((i ^ 1) + (1 if i % 2 else -1) * 2) % pieces) for i in range(pieces)])
     times = [lax.ppermute(t, "col", [(i, i ^ k) for i in range(columns)]) if k else t for k, t in enumerate(times)]
 
     tiles_in, spread, rows, cols, selfs = call(
         build_inner,
-        (meta, table, positions, density),
+        (meta, table, near),
         [inner_tiles, pltpu.VMEM((share, 4, width, width), f32), square, narrow, narrow],
-        [pltpu.VMEM((4, 2 * share, width), f32)],
-        16 * most_inner,
+        work=16 * most_inner,
     )
-    again, tiles_out, diagonal, precond, times = call(
+    again, tiles_out, diagonal, precond, times, alone = call(
         build_outer,
-        (meta, table, positions, density, first, second, right_side,
+        (meta, table, around, first, second, density, source,
          held(tiles_in), held(spread), held(rows), held(cols), held(selfs), *times),
-        [pltpu.SMEM((1,), jnp.int32), outer_tiles, vector, vector, vector],
+        [pltpu.SMEM((1,), jnp.int32), outer_tiles, vector, vector, vector, vector],
         [pltpu.VMEM((4, capacity + 2 * share, width), f32), pltpu.VMEM((share, width, width), f32)]
         + [pltpu.VMEM((share, width), f32)] * 2,
         16 * most_outer,
@@ -538,9 +582,9 @@
     def inner(field):
         return call(
             apply_inner,
-            (meta, table, again, field, times, held(tiles_in)),
+            (meta, table, again, field, alone, times, held(tiles_in)),
             [square, narrow],
-            [pltpu.VMEM((share, width, width), f32), pltpu.VMEM((2 * share, width), f32)],
+            [pltpu.VMEM((share, width, width), f32), pltpu.VMEM((2 * share, width), f32), pltpu.VMEM((share, width), f32)],
             4 * most_inner,
             scalars=3,
         )
@@ -578,7 +622,7 @@
     rows, cols = inner(scaled)
     twice, sums = call(
         apply_second,
-        (meta, table, again, right_side, precond, spill, scaled, times, *received, held(tiles_out), held(rows), held(cols)),
+        (meta, table, again, source, precond, spill, scaled, times, *received, held(tiles_out), held(rows), held(cols)),
         [vector, few],
         scratch,
         2 * most_outer,
@@ -596,9 +640,9 @@
 
     return tuple(call(
         finish,
-        (meta, right_side, precond, spill, scaled, twice, sums, other),
+        (source, precond, spill, scaled, twice, sums, other),
         [vector, vector],
-        scalars=1,
+        scalars=0,
     ))
 
 

time: 92.6 us -> 78.8 us (0.85)
  Pallas kernels: 44.7 us -> 37.8 us
  local copies, waits for them, and re-layouts: 6.79 us -> 0 us
  waiting for transfers between devices: 7.21 us -> 10 us
  starting transfers between devices: 32.6 us -> 30.1 us
    pallas_call x8, Pallas kernels: 44.7 us -> 37.8 us  [call(): pl.pallas_call(kernel, out_shape=outs, in_specs=[SMEM] * scalars + [HBM]...]
    unnamed x18 -> x0, local copies, waits for them, and re-layouts: 6.79 us -> none
    ppermute x6, starting transfers between devices: 11.4 us -> 7.37 us  [swap(): lax.ppermute(values, axis, [(i, i ^ step) for i in range(lax.axis_size(ax...]
    ppermute x6, waiting for transfers between devices: 7.17 us -> 9.62 us  [swap(): lax.ppermute(values, axis, [(i, i ^ step) for i in range(lax.axis_size(ax...]
    ppermute x8, starting transfers between devices: 12.8 us -> 14.2 us  [exchange(): return [lax.ppermute(field, axes, list(enumerate(to))) for to in swaps]]
  transfers between devices with their start and end apart: 19 -> 19, of which waited for: 5 -> 7; matrix products, arithmetic and copies ran while one was open for 0% -> 0% of each run, Pallas kernels for 31% -> 29%
where the time goes in v5:
time: 78.8 us; the launch traced here: 78.7 us
  Pallas kernels  37.8 us (48%)
  starting transfers between devices  30.1 us (38%)
  waiting for transfers between devices  10 us (13%)
    pallas_call x8, Pallas kernels, call(): pl.pallas_call(kernel, out_shape=outs, in_specs=[SMEM] * scalars + [HBM]...  37.8 us
    ppermute x8, starting transfers between devices, exchange(): return [lax.ppermute(field, axes, list(enumerate(to))) for to in swaps]  14.2 us
    ppermute x6, waiting for transfers between devices, swap(): lax.ppermute(values, axis, [(i, i ^ step) for i in range(lax.axis_size(ax...  9.62 us
    ppermute x6, starting transfers between devices, swap(): lax.ppermute(values, axis, [(i, i ^ step) for i in range(lax.axis_size(ax...  7.37 us
    ppermute x3, starting transfers between devices, body(): lax.ppermute(t, 'col', [(i, i ^ k) for i in range(columns)])  4.39 us
    ppermute x1, starting transfers between devices, body(): lax.ppermute(second, 'piece', [(i, ((i ^ 1) + (1 if i % 2 else -1) * 2) %...  3.55 us
  transfers between devices with their start and end apart: 19, of which 7 were waited for; matrix products, arithmetic and copies ran while one was open for 0% of the time, Pallas kernels for 29%

profile of v5, /device:TPU:0, one launch (start us, length us, event | category | flops | bytes accessed | tf_op | source)
XLA Modules:
  0.0 78.7 jit_solution(66387826169468907)
XLA Ops:
  0.6 1.8 %prepare.1 = (s32[8]{0:T(128)S(4)}, s32[1472]{0:T(1024)S(4)}, f32[4,192,128]{2,1,0:T(8,128)S(1)}, f32[4,64,128]{2,1,0:T(8,128)S(1)}, f32[32,128]{1,0:T(8,128)S(1...) custom-call(s32[8]{0:T(128)} %counts.1, ...), custom_call_target="tpu_custom_call" | custom-call | tf_op jit(solution)/shard_map/prepare/pallas_call | solution.py:533
  2.5 0.5 collective-permute-start
  3.0 3.6 %collective-permute-start.1 = (f32[4,32,128]{2,1,0:T(8,128)S(1)}, f32[4,32,128]{2,1,0:T(8,128)S(1)}, u32[]{:S(2)}, u32[]{:S(2)}) collective-permute-start(f32[4,32,128]{2,1,0:T(8,128)S(1)} %get-tuple-element.38), channel_id=1, source_target_pairs={{0,28},{4,8},{8,4},{12,16},{16,12},{20,24},{24,20},{28,0},{1,29},{... | collective-permute-start | bytes 196616 | tf_op jit(solution)/shard_map/ppermute | solution.py:562
  6.6 1.6 %collective-permute-start.2 = (f32[32,128]{1,0:T(8,128)S(1)}, f32[32,128]{1,0:T(8,128)S(1)}, u32[]{:S(2)}, u32[]{:S(2)}) collective-permute-start(f32[32,128]{1,0:T(8,128)S(1)} %get-tuple-element.47), channel_id=1, source_target_pairs={{0,1},{1,0},{2,3},{3,2},{4,5},{5,4},{6,7},{7,6},{8,9},{9,8},{10,11... | collective-permute-start | bytes 49160 | tf_op jit(solution)/shard_map/ppermute | solution.py:563
  8.1 2.6 %collective-permute-start.3 = (f32[32,128]{1,0:T(8,128)S(1)}, f32[32,128]{1,0:T(8,128)S(1)}, u32[]{:S(2)}, u32[]{:S(2)}) collective-permute-start(f32[32,128]{1,0:T(8,128)S(1)} %get-tuple-element.48), channel_id=1, source_target_pairs={{0,2},{1,3},{2,0},{3,1},{4,6},{5,7},{6,4},{7,5},{8,10},{9,11},{10,... | collective-permute-start | bytes 49160 | tf_op jit(solution)/shard_map/ppermute | solution.py:563
  10.7 0.2 collective-permute-start.4
  10.9 13.5 %build_inner.1 = (f32[216,128,128]{2,1,0:T(8,128)S(1)}, f32[32,4,128,128]{3,2,1,0:T(8,128)S(1)}, f32[32,128,128]{2,1,0:T(8,128)S(1)}, f32[256,128]{1,0:T(8,128)S(1)}, f32[256,128]{1,0:T(8,128)S(1)}) custom-call(s32[8]{0:T(128)S(4)} %get-tuple-element.34.meta, s32[1472]{0:T(1024)S(4)} %get-tuple-element.35.table, f32[4,64,128]{2,1,0:T(8,128)S(1)} %get-tuple-element.40.near), custom_call_target="tpu_custom_call" | custom-call | flops 56623104 | tf_op jit(solution)/shard_map/build_inner/pallas_call | solution.py:533
  24.4 0.0 collective-permute-done.2.rest_1_
  24.4 0.0 collective-permute-done.3.rest_2_
  24.5 0.0 collective-permute-done.4.rest_3_
  24.5 0.0 collective-permute-done.first
  24.5 0.0 collective-permute-done.1.second
  24.5 6.7 %build_outer.1 = (s32[1]{0:T(128)S(4)}, f32[222,128,128]{2,1,0:T(8,128)S(1)}, f32[32,128]{1,0:T(8,128)S(1)}, f32[32,128]{1,0:T(8,128)S(1)}, f32[32,128]{1,0:T(8,128)S(1)}, /*index=5*/f32[32,128]{1,0:T(8,128)S(1)}) custom-call(s32[8]{0:T(128)S(4)} %get-tuple-element.34.meta, s32[1472]{0:T(1024)S(4)} %get-tuple-element.35.table, ...), custom_call_target="tpu_custom_call" | custom-call | flops 58195968 | tf_op jit(solution)/shard_map/build_outer/pallas_call | solution.py:533
  31.2 5.1 %collective-permute-start.8 = (f32[32,128]{1,0:T(8,128)S(1)}, f32[32,128]{1,0:T(8,128)S(1)}, u32[]{:S(2)}, u32[]{:S(2)}) collective-permute-start(f32[32,128]{1,0:T(8,128)S(1)} %get-tuple-element.50.field.precond), channel_id=1, source_target_pairs={{0,1},{1,3},{2,4},{3,0},{4,2},{5,7},{6,8},{7,5},{8,6},{9,11},{10,1... | collective-permute-start | bytes 49160 | tf_op jit(solution)/shard_map/ppermute | solution.py:606
  36.3 0.8 collective-permute-start.7
  37.0 1.3 %collective-permute-start.6 = (f32[32,128]{1,0:T(8,128)S(1)}, f32[32,128]{1,0:T(8,128)S(1)}, u32[]{:S(2)}, u32[]{:S(2)}) collective-permute-start(f32[32,128]{1,0:T(8,128)S(1)} %get-tuple-element.50.field.precond), channel_id=1, source_target_pairs={{0,31},{1,2},{2,1},{3,4},{4,3},{5,6},{6,5},{7,8},{8,7},{9,10},{10,... | collective-permute-start | bytes 49160 | tf_op jit(solution)/shard_map/ppermute | solution.py:606
  38.4 0.3 collective-permute-start.5
  38.7 4.7 %apply_inner.2 = (f32[32,128,128]{2,1,0:T(8,128)S(1)}, f32[256,128]{1,0:T(8,128)S(1)}) custom-call(s32[8]{0:T(128)S(4)} %get-tuple-element.34.meta, s32[1472]{0:T(1024)S(4)} %get-tuple-element.35.table, s32[1]{0:T(128)S(4)} %get-tuple-element.51.again, f32[32,128]{1,0:T(8,128)S(1)} %get-tuple-element.50.field.precond, ...), custom_call_target="tpu_custom_call" | custom-call | flops 14155776 | tf_op jit(solution)/shard_map/apply_inner/pallas_call | solution.py:533
  43.4 0.0 collective-permute-done.8.rest_3_
  43.4 0.0 collective-permute-done.7.rest_2_
  43.4 0.4 collective-permute-done.6.rest_1_
  43.8 0.0 collective-permute-done.5.rest_0_
  43.8 2.7 %apply_first.1 = (f32[32,128]{1,0:T(8,128)S(1)}, f32[32,128]{1,0:T(8,128)S(1)}) custom-call(s32[8]{0:T(128)S(4)} %get-tuple-element.34.meta, s32[1472]{0:T(1024)S(4)} %get-tuple-element.35.table, s32[1]{0:T(128)S(4)} %get-tuple-element.51.again, f32[32,128]{1,0:T(8,128)S(1)} %get-tuple-element.52.diagonal, f32[32,128]{1,0:T(8,128)S(1)} %get-tuple-element.53.times, ...), custom_call_target="tpu_custom_call" | custom-call | flops 7274496 | tf_op jit(solution)/shard_map/apply_first/pallas_call | solution.py:533
  46.5 2.1 %collective-permute-start.12 = (f32[32,128]{1,0:T(8,128)S(1)}, f32[32,128]{1,0:T(8,128)S(1)}, u32[]{:S(2)}, u32[]{:S(2)}) collective-permute-start(f32[32,128]{1,0:T(8,128)S(1)} %get-tuple-element.59.field.scaled), channel_id=1, source_target_pairs={{0,1},{1,3},{2,4},{3,0},{4,2},{5,7},{6,8},{7,5},{8,6},{9,11},{10,1... | collective-permute-start | bytes 49160 | tf_op jit(solution)/shard_map/ppermute | solution.py:606
  48.6 2.3 %collective-permute-start.11 = (f32[32,128]{1,0:T(8,128)S(1)}, f32[32,128]{1,0:T(8,128)S(1)}, u32[]{:S(2)}, u32[]{:S(2)}) collective-permute-start(f32[32,128]{1,0:T(8,128)S(1)} %get-tuple-element.59.field.scaled), channel_id=1, source_target_pairs={{0,2},{1,4},{2,3},{3,0},{4,1},{5,8},{6,7},{7,6},{8,5},{9,12},{10,1... | collective-permute-start | bytes 49160 | tf_op jit(solution)/shard_map/ppermute | solution.py:606
  50.9 2.2 %collective-permute-start.10 = (f32[32,128]{1,0:T(8,128)S(1)}, f32[32,128]{1,0:T(8,128)S(1)}, u32[]{:S(2)}, u32[]{:S(2)}) collective-permute-start(f32[32,128]{1,0:T(8,128)S(1)} %get-tuple-element.59.field.scaled), channel_id=1, source_target_pairs={{0,31},{1,2},{2,1},{3,4},{4,3},{5,6},{6,5},{7,8},{8,7},{9,10},{10,... | collective-permute-start | bytes 49160 | tf_op jit(solution)/shard_map/ppermute | solution.py:606
  53.1 0.0 collective-permute-start.9
  53.1 4.7 %apply_inner.3 = (f32[32,128,128]{2,1,0:T(8,128)S(1)}, f32[256,128]{1,0:T(8,128)S(1)}) custom-call(s32[8]{0:T(128)S(4)} %get-tuple-element.34.meta, s32[1472]{0:T(1024)S(4)} %get-tuple-element.35.table, s32[1]{0:T(128)S(4)} %get-tuple-element.51.again, f32[32,128]{1,0:T(8,128)S(1)} %get-tuple-element.59.field.scaled, f32[32,128]{1,0:T(8,128)S(1)} %get-tuple-element.55.alone, ...), custom_call_target="tpu_custom_call" | custom-call | flops 14155776 | tf_op jit(solution)/shard_map/apply_inner/pallas_call | solution.py:533
  57.8 0.0 collective-permute-done.12.rest_3_
  57.8 0.0 collective-permute-done.11.rest_2_
  57.8 0.0 collective-permute-done.10.rest_1_
  57.8 0.0 collective-permute-done.9.rest_0_
  57.9 2.9 %apply_second.1 = (f32[32,128]{1,0:T(8,128)S(1)}, f32[8,128]{1,0:T(8,128)S(1)}) custom-call(s32[8]{0:T(128)S(4)} %get-tuple-element.34.meta, s32[1472]{0:T(1024)S(4)} %get-tuple-element.35.table, s32[1]{0:T(128)S(4)} %get-tuple-element.51.again, f32[32,128]{1,0:T(8,128)S(1)} %get-tuple-element.33.source, f32[32,128]{1,0:T(8,128)S(1)} %get-tuple-element.50.field.precond, ...), custom_call_target="tpu_custom_call" | custom-call | flops 7274496 | tf_op jit(solution)/shard_map/apply_second/pallas_call | solution.py:533
  60.7 0.0 collective-permute-start.15
  60.7 4.2 %collective-permute-start.14 = (f32[8,128]{1,0:T(8,128)S(1)}, f32[8,128]{1,0:T(8,128)S(1)}, u32[]{:S(2)}, u32[]{:S(2)}) collective-permute-start(f32[8,128]{1,0:T(8,128)S(1)} %get-tuple-element.63), channel_id=1, source_target_pairs={{0,2},{1,3},{2,0},{3,1},{4,6},{5,7},{6,4},{7,5},{8,10},{9,11},{10,... | collective-permute-start | bytes 12296 | tf_op jit(solution)/shard_map/ppermute | solution.py:633
  64.9 0.2 collective-permute-start.13
  65.1 1.1 %collective-permute-done.15 = f32[8,128]{1,0:T(8,128)S(1)} collective-permute-done((f32[8,128]{1,0:T(8,128)S(1)}, f32[8,128]{1,0:T(8,128)S(1)}, u32[]{:S(2)}, u32[]{:S(2)}) %collective-permute-start.15) | collective-permute-done | bytes 4128 | tf_op jit(solution)/shard_map/ppermute | solution.py:633
  66.2 0.4 collective-permute-done.14
  66.6 2.0 %collective-permute-done.13 = f32[8,128]{1,0:T(8,128)S(1)} collective-permute-done((f32[8,128]{1,0:T(8,128)S(1)}, f32[8,128]{1,0:T(8,128)S(1)}, u32[]{:S(2)}, u32[]{:S(2)}) %collective-permute-start.13) | collective-permute-done | bytes 4128 | tf_op jit(solution)/shard_map/ppermute | solution.py:633
  68.6 0.0 collective-permute-start.16
  68.6 1.2 %collective-permute-done.16 = f32[8,128]{1,0:T(8,128)S(1)} collective-permute-done((f32[8,128]{1,0:T(8,128)S(1)}, f32[8,128]{1,0:T(8,128)S(1)}, u32[]{:S(2)}, u32[]{:S(2)}) %collective-permute-start.16) | collective-permute-done | bytes 4128 | tf_op jit(solution)/shard_map/ppermute | solution.py:633
  69.7 0.2 collective-permute-start.17
  69.9 3.5 %collective-permute-done.17 = f32[8,128]{1,0:T(8,128)S(1)} collective-permute-done((f32[8,128]{1,0:T(8,128)S(1)}, f32[8,128]{1,0:T(8,128)S(1)}, u32[]{:S(2)}, u32[]{:S(2)}) %collective-permute-start.17) | collective-permute-done | bytes 4128 | tf_op jit(solution)/shard_map/ppermute | solution.py:633
  73.3 2.8 %collective-permute-start.18 = (f32[8,128]{1,0:T(8,128)S(1)}, f32[8,128]{1,0:T(8,128)S(1)}, u32[]{:S(2)}, u32[]{:S(2)}) collective-permute-start(f32[8,128]{1,0:T(8,128)S(1)} %add.19.mine), channel_id=1, source_target_pairs={{0,16},{4,20},{8,24},{12,28},{16,0},{20,4},{24,8},{28,12},{1,17},{... | collective-permute-start | bytes 12296 | tf_op jit(solution)/shard_map/ppermute | solution.py:633
  76.2 1.6 %collective-permute-done.18.other = f32[8,128]{1,0:T(8,128)S(1)} collective-permute-done((f32[8,128]{1,0:T(8,128)S(1)}, f32[8,128]{1,0:T(8,128)S(1)}, u32[]{:S(2)}, u32[]{:S(2)}) %collective-permute-start.18) | collective-permute-done | bytes 4128 | tf_op jit(solution)/shard_map/ppermute | solution.py:633
  77.8 0.9 %finish.1 = (f32[32,128]{1,0:T(8,128)}, f32[32,128]{1,0:T(8,128)}) custom-call(f32[32,128]{1,0:T(8,128)S(1)} %get-tuple-element.33.source, f32[32,128]{1,0:T(8,128)S(1)} %get-tuple-element.50.field.precond, f32[32,128]{1,0:T(8,128)S(1)} %get-tuple-element.58.spill, f32[32,128]{1,0:T(8,128)S(1)} %get-tuple-element.59.field.scaled, ...), custom_call_target="tpu_custom_call" | custom-call | tf_op jit(solution)/shard_map/finish/pallas_call | solution.py:533
  (3 shorter events, 0.0 us)
Async XLA Ops:
  2.5 22.0 %collective-permute-start = (f32[4,32,128]{2,1,0:T(8,128)S(1)}, f32[4,32,128]{2,1,0:T(8,128)S(1)}, u32[]{:S(2)}, u32[]{:S(2)}) collective-permute-start(f32[4,32,128]{2,1,0:T(8,128)S(1)} %get-tuple-element.37), channel_id=1, source_target_pairs={{0,4},{4,0},{8,12},{12,8},{16,20},{20,16},{24,28},{28,24},{1,5},{5... | collective-permute-start | bytes 196616 | tf_op jit(solution)/shard_map/ppermute | solution.py:561
  3.0 21.5 %collective-permute-start.1 = (f32[4,32,128]{2,1,0:T(8,128)S(1)}, f32[4,32,128]{2,1,0:T(8,128)S(1)}, u32[]{:S(2)}, u32[]{:S(2)}) collective-permute-start(f32[4,32,128]{2,1,0:T(8,128)S(1)} %get-tuple-element.38), channel_id=1, source_target_pairs={{0,28},{4,8},{8,4},{12,16},{16,12},{20,24},{24,20},{28,0},{1,29},{... | collective-permute-start | bytes 196616 | tf_op jit(solution)/shard_map/ppermute | solution.py:562
  6.6 17.9 %collective-permute-start.2 = (f32[32,128]{1,0:T(8,128)S(1)}, f32[32,128]{1,0:T(8,128)S(1)}, u32[]{:S(2)}, u32[]{:S(2)}) collective-permute-start(f32[32,128]{1,0:T(8,128)S(1)} %get-tuple-element.47), channel_id=1, source_target_pairs={{0,1},{1,0},{2,3},{3,2},{4,5},{5,4},{6,7},{7,6},{8,9},{9,8},{10,11... | collective-permute-start | bytes 49160 | tf_op jit(solution)/shard_map/ppermute | solution.py:563
  8.1 16.3 %collective-permute-start.3 = (f32[32,128]{1,0:T(8,128)S(1)}, f32[32,128]{1,0:T(8,128)S(1)}, u32[]{:S(2)}, u32[]{:S(2)}) collective-permute-start(f32[32,128]{1,0:T(8,128)S(1)} %get-tuple-element.48), channel_id=1, source_target_pairs={{0,2},{1,3},{2,0},{3,1},{4,6},{5,7},{6,4},{7,5},{8,10},{9,11},{10,... | collective-permute-start | bytes 49160 | tf_op jit(solution)/shard_map/ppermute | solution.py:563
  10.7 13.7 %collective-permute-start.4 = (f32[32,128]{1,0:T(8,128)S(1)}, f32[32,128]{1,0:T(8,128)S(1)}, u32[]{:S(2)}, u32[]{:S(2)}) collective-permute-start(f32[32,128]{1,0:T(8,128)S(1)} %get-tuple-element.49), channel_id=1, source_target_pairs={{0,3},{1,2},{2,1},{3,0},{4,7},{5,6},{6,5},{7,4},{8,11},{9,10},{10,... | collective-permute-start | bytes 49160 | tf_op jit(solution)/shard_map/ppermute | solution.py:563
  31.2 12.3 %collective-permute-start.8 = (f32[32,128]{1,0:T(8,128)S(1)}, f32[32,128]{1,0:T(8,128)S(1)}, u32[]{:S(2)}, u32[]{:S(2)}) collective-permute-start(f32[32,128]{1,0:T(8,128)S(1)} %get-tuple-element.50.field.precond), channel_id=1, source_target_pairs={{0,1},{1,3},{2,4},{3,0},{4,2},{5,7},{6,8},{7,5},{8,6},{9,11},{10,1... | collective-permute-start | bytes 49160 | tf_op jit(solution)/shard_map/ppermute | solution.py:606
  36.3 7.2 %collective-permute-start.7 = (f32[32,128]{1,0:T(8,128)S(1)}, f32[32,128]{1,0:T(8,128)S(1)}, u32[]{:S(2)}, u32[]{:S(2)}) collective-permute-start(f32[32,128]{1,0:T(8,128)S(1)} %get-tuple-element.50.field.precond), channel_id=1, source_target_pairs={{0,2},{1,4},{2,3},{3,0},{4,1},{5,8},{6,7},{7,6},{8,5},{9,12},{10,1... | collective-permute-start | bytes 49160 | tf_op jit(solution)/shard_map/ppermute | solution.py:606
  37.0 6.8 %collective-permute-start.6 = (f32[32,128]{1,0:T(8,128)S(1)}, f32[32,128]{1,0:T(8,128)S(1)}, u32[]{:S(2)}, u32[]{:S(2)}) collective-permute-start(f32[32,128]{1,0:T(8,128)S(1)} %get-tuple-element.50.field.precond), channel_id=1, source_target_pairs={{0,31},{1,2},{2,1},{3,4},{4,3},{5,6},{6,5},{7,8},{8,7},{9,10},{10,... | collective-permute-start | bytes 49160 | tf_op jit(solution)/shard_map/ppermute | solution.py:606
  38.4 5.4 %collective-permute-start.5 = (f32[32,128]{1,0:T(8,128)S(1)}, f32[32,128]{1,0:T(8,128)S(1)}, u32[]{:S(2)}, u32[]{:S(2)}) collective-permute-start(f32[32,128]{1,0:T(8,128)S(1)} %get-tuple-element.50.field.precond), channel_id=1, source_target_pairs={{0,1},{1,0},{2,3},{3,2},{4,5},{5,4},{6,7},{7,6},{8,9},{9,8},{10,11... | collective-permute-start | bytes 49160 | tf_op jit(solution)/shard_map/ppermute | solution.py:606
  46.5 11.3 %collective-permute-start.12 = (f32[32,128]{1,0:T(8,128)S(1)}, f32[32,128]{1,0:T(8,128)S(1)}, u32[]{:S(2)}, u32[]{:S(2)}) collective-permute-start(f32[32,128]{1,0:T(8,128)S(1)} %get-tuple-element.59.field.scaled), channel_id=1, source_target_pairs={{0,1},{1,3},{2,4},{3,0},{4,2},{5,7},{6,8},{7,5},{8,6},{9,11},{10,1... | collective-permute-start | bytes 49160 | tf_op jit(solution)/shard_map/ppermute | solution.py:606
  48.6 9.2 %collective-permute-start.11 = (f32[32,128]{1,0:T(8,128)S(1)}, f32[32,128]{1,0:T(8,128)S(1)}, u32[]{:S(2)}, u32[]{:S(2)}) collective-permute-start(f32[32,128]{1,0:T(8,128)S(1)} %get-tuple-element.59.field.scaled), channel_id=1, source_target_pairs={{0,2},{1,4},{2,3},{3,0},{4,1},{5,8},{6,7},{7,6},{8,5},{9,12},{10,1... | collective-permute-start | bytes 49160 | tf_op jit(solution)/shard_map/ppermute | solution.py:606
  50.9 6.9 %collective-permute-start.10 = (f32[32,128]{1,0:T(8,128)S(1)}, f32[32,128]{1,0:T(8,128)S(1)}, u32[]{:S(2)}, u32[]{:S(2)}) collective-permute-start(f32[32,128]{1,0:T(8,128)S(1)} %get-tuple-element.59.field.scaled), channel_id=1, source_target_pairs={{0,31},{1,2},{2,1},{3,4},{4,3},{5,6},{6,5},{7,8},{8,7},{9,10},{10,... | collective-permute-start | bytes 49160 | tf_op jit(solution)/shard_map/ppermute | solution.py:606
  53.1 4.7 %collective-permute-start.9 = (f32[32,128]{1,0:T(8,128)S(1)}, f32[32,128]{1,0:T(8,128)S(1)}, u32[]{:S(2)}, u32[]{:S(2)}) collective-permute-start(f32[32,128]{1,0:T(8,128)S(1)} %get-tuple-element.59.field.scaled), channel_id=1, source_target_pairs={{0,1},{1,0},{2,3},{3,2},{4,5},{5,4},{6,7},{7,6},{8,9},{9,8},{10,11... | collective-permute-start | bytes 49160 | tf_op jit(solution)/shard_map/ppermute | solution.py:606
  60.7 5.4 %collective-permute-start.15 = (f32[8,128]{1,0:T(8,128)S(1)}, f32[8,128]{1,0:T(8,128)S(1)}, u32[]{:S(2)}, u32[]{:S(2)}) collective-permute-start(f32[8,128]{1,0:T(8,128)S(1)} %get-tuple-element.63), channel_id=1, source_target_pairs={{0,3},{1,2},{2,1},{3,0},{4,7},{5,6},{6,5},{7,4},{8,11},{9,10},{10,... | collective-permute-start | bytes 12296 | tf_op jit(solution)/shard_map/ppermute | solution.py:633
  60.7 5.8 %collective-permute-start.14 = (f32[8,128]{1,0:T(8,128)S(1)}, f32[8,128]{1,0:T(8,128)S(1)}, u32[]{:S(2)}, u32[]{:S(2)}) collective-permute-start(f32[8,128]{1,0:T(8,128)S(1)} %get-tuple-element.63), channel_id=1, source_target_pairs={{0,2},{1,3},{2,0},{3,1},{4,6},{5,7},{6,4},{7,5},{8,10},{9,11},{10,... | collective-permute-start | bytes 12296 | tf_op jit(solution)/shard_map/ppermute | solution.py:633
  64.9 3.6 %collective-permute-start.13 = (f32[8,128]{1,0:T(8,128)S(1)}, f32[8,128]{1,0:T(8,128)S(1)}, u32[]{:S(2)}, u32[]{:S(2)}) collective-permute-start(f32[8,128]{1,0:T(8,128)S(1)} %get-tuple-element.63), channel_id=1, source_target_pairs={{0,1},{1,0},{2,3},{3,2},{4,5},{5,4},{6,7},{7,6},{8,9},{9,8},{10,11... | collective-permute-start | bytes 12296 | tf_op jit(solution)/shard_map/ppermute | solution.py:633
  68.6 1.2 %collective-permute-start.16 = (f32[8,128]{1,0:T(8,128)S(1)}, f32[8,128]{1,0:T(8,128)S(1)}, u32[]{:S(2)}, u32[]{:S(2)}) collective-permute-start(f32[8,128]{1,0:T(8,128)S(1)} %add_add_fusion), channel_id=1, source_target_pairs={{0,4},{4,0},{8,12},{12,8},{16,20},{20,16},{24,28},{28,24},{1,5},{5... | collective-permute-start | bytes 12296 | tf_op jit(solution)/shard_map/ppermute | solution.py:633
  69.7 3.6 %collective-permute-start.17 = (f32[8,128]{1,0:T(8,128)S(1)}, f32[8,128]{1,0:T(8,128)S(1)}, u32[]{:S(2)}, u32[]{:S(2)}) collective-permute-start(f32[8,128]{1,0:T(8,128)S(1)} %add.18), channel_id=1, source_target_pairs={{0,8},{4,12},{8,0},{12,4},{16,24},{20,28},{24,16},{28,20},{1,9},{5... | collective-permute-start | bytes 12296 | tf_op jit(solution)/shard_map/ppermute | solution.py:633
  73.3 4.4 %collective-permute-start.18 = (f32[8,128]{1,0:T(8,128)S(1)}, f32[8,128]{1,0:T(8,128)S(1)}, u32[]{:S(2)}, u32[]{:S(2)}) collective-permute-start(f32[8,128]{1,0:T(8,128)S(1)} %add.19.mine), channel_id=1, source_target_pairs={{0,16},{4,20},{8,24},{12,28},{16,0},{20,4},{24,8},{28,12},{1,17},{... | collective-permute-start | bytes 12296 | tf_op jit(solution)/shard_map/ppermute | solution.py:633

commit v6 on v5

--- a/solution.py
+++ b/solution.py
@@ -72,33 +72,55 @@
     return table[code * STRIDE + jnp.clip(t, -REACH, REACH) + REACH + WIDEST]
 
 
-def inner_range(meta, table, a):
-    code = lax.rem(meta[1] + a, LAYER)
-    low, high = rank(table, code, -a), rank(table, code, 0)
-    start = code * STRIDE + low
-    return high - low, lambda t: a + table[start + t]
-
-
-def outer_range(meta, table, a):
-    code = lax.rem(meta[1] + a, LAYER)
+FIELDS = 6
+
+
+def write_plan(meta, table, plan, a):
+    code = lax.bitwise_and(meta[1] + a, LAYER - 1)
     place = meta[1] + a
-    low, split = rank(table, code, -place), rank(table, code, -a)
+    low, split, middle = rank(table, code, -place), rank(table, code, -a), rank(table, code, 0)
     resume, high = rank(table, code, meta[0] - a), rank(table, code, meta[2] - place)
+    row = code * STRIDE
     ahead = split - low
-    start = code * STRIDE + low
-    start_after = code * STRIDE + resume - ahead
-    count = ahead + jnp.maximum(high - resume, 0)
-    return count, lambda t: a + table[t + jnp.where(t < ahead, start, start_after)]
-
-
-def sweep(count, fetch, step, carry):
+    plan[a * FIELDS] = middle - split
+    plan[a * FIELDS + 1] = row + split
+    plan[a * FIELDS + 2] = ahead + jnp.maximum(high - resume, 0)
+    plan[a * FIELDS + 3] = ahead
+    plan[a * FIELDS + 4] = row + low
+    plan[a * FIELDS + 5] = row + resume - ahead
+
+
+def inner_range(plan, table, a):
+    start = plan[a * FIELDS + 1]
+    return plan[a * FIELDS], lambda t: a + table[start + t]
+
+
+def outer_range(plan, table, a):
+    ahead, start, start_after = (plan[a * FIELDS + k] for k in (3, 4, 5))
+    return plan[a * FIELDS + 2], lambda t: a + table[t + jnp.where(t < ahead, start, start_after)]
+
+
+def sweep(count, place_of, step, carry):
     def both(i, state):
         carry, *now = state
-        later = fetch(2 * i + 2), fetch(2 * i + 3)
+        later = place_of(2 * i + 2), place_of(2 * i + 3)
         return step(now, carry), *later
 
-    carry, first, _ = lax.fori_loop(0, lax.div(count, 2), both, (carry, fetch(0), fetch(1)))
+    carry, first, _ = lax.fori_loop(0, lax.div(count, 2), both, (carry, place_of(0), place_of(1)))
     return lax.fori_loop(0, lax.rem(count, 2), lambda _, carry: step([first], carry), carry)
+
+
+TURN = 4
+
+
+def padded_sweep(count, fetch, step, carry):
+    def turn(i, state):
+        carry, *now = state
+        later = [fetch(TURN * (i + 1) + k) for k in range(TURN)]
+        return step(now, carry), *later
+
+    state = (carry, *(fetch(k) for k in range(TURN)))
+    return lax.fori_loop(0, lax.div(count + (TURN - 1), TURN), turn, state)[0]
 
 
 def tree(terms):
@@ -214,9 +236,16 @@
         out[...] = times[pl.ds(pl.multiple_of((column ^ k) * share, SUB), share), :]
 
 
-def build_inner(meta, table, near, tiles, spread, rows_ref, cols_ref, self_ref):
+def finish_tiles(tiles, end):
+    for t in range(TURN):
+        tiles[end + t] = jnp.zeros(tiles.shape[1:], jnp.float32)
+
+
+def build_inner(meta, table, near, plan, tiles, spread, rows_ref, cols_ref, self_ref):
     share, width = rows_ref.shape[0], rows_ref.shape[2]
     chunks = pieces_of(width)
+    for a in range(share):
+        write_plan(meta, table, plan, a)
     for k in range(4):
         spread_columns(spread, lambda a: (a, k), near[k, 0:share, :])
     cols_ref[...] = jnp.zeros_like(cols_ref)
@@ -225,33 +254,27 @@
         return [wide(near[k, pl.ds(n, 1), :]) for k in range(4)]
 
     def block(a, at):
-        count, place_of = inner_range(meta, table, a)
-
-        def fetch(t):
-            n = place_of(t)
-            return n, rows_at(n)
-
-        def pairs(fetched, carry):
-            at, sums = carry
-            down = [[None] * 4 for _ in fetched]
-            result = []
-            for c, (here, total) in enumerate(zip(chunks, sums)):
+        count, place_of = inner_range(plan, table, a)
+        rows_ref[a] = jnp.zeros((width, width), jnp.float32)
+
+        def pairs(places, at):
+            others = [rows_at(n) for n in places]
+            down = [[None] * 2 for _ in places]
+            for c, here in enumerate(chunks):
                 own = [spread[a, k, here, :] for k in range(4)]
-                for t, (_, other) in enumerate(fetched):
+                found = []
+                for t, other in enumerate(others):
                     tile = pair_chunk(own, other)
                     tiles[at + t, here, :] = tile
                     gather(down[t], c, tile)
-                    total = total + tile
-                result.append(total)
-            for (n, _), partial in zip(fetched, down):
+                    found.append(tile)
+                rows_ref[a, here, :] = rows_ref[a, here, :] + tree(found)
+            for n, partial in zip(places, down):
                 there = pl.ds(pl.multiple_of(n * SUB, SUB), SUB)
                 cols_ref[there, :] = cols_ref[there, :] + tree(partial)
-            return at + len(fetched), result
-
-        zero = jnp.zeros((SUB, width), jnp.float32)
-        at, sums = sweep(count, fetch, pairs, (at, [zero] * len(chunks)))
-        for here, values in zip(chunks, sums):
-            rows_ref[a, here, :] = values
+            return at + len(places)
+
+        at = sweep(count, place_of, pairs, at)
         other = rows_at(a)
         lane = lax.broadcasted_iota(jnp.int32, (SUB, width), 1)
         sublane = lax.broadcasted_iota(jnp.int32, (SUB, width), 0)
@@ -264,7 +287,7 @@
         self_ref[pl.ds(pl.multiple_of(a * SUB, SUB), SUB), :] = tree(down)
         return at + 1
 
-    lax.fori_loop(0, meta[0], block, 0)
+    finish_tiles(tiles, lax.fori_loop(0, meta[0], block, 0))
 
 
 def factor(times, a, n):
@@ -283,7 +306,7 @@
 
 
 def build_outer(
-    meta, table, around, first, second, density, source, tiles_in, spread, rows_ref, cols_ref, self_ref, *rest
+    meta, table, plan, around, first, second, density, source, tiles_in, spread, rows_ref, cols_ref, self_ref, *rest
 ):
     *times_in, again_ref, tiles, diagonal_ref, precond_ref, times, alone_ref, hood, work, sums_ref, extra = rest
     share, width = diagonal_ref.shape
@@ -301,31 +324,26 @@
     again = jnp.max(jnp.where((lane == REACH) | (lane == 0), 0.0, often)) > 1.5
     again_ref[0] = again.astype(jnp.int32)
 
+
     def block(a, at):
-        count, place_of = outer_range(meta, table, a)
-
-        def fetch(t):
-            here = pl.ds(base + share + place_of(t), 1)
-            return [wide(hood[k, here, :]) for k in range(4)]
-
-        def pairs(fetched, carry):
-            at, sums = carry
-            result = []
-            for here, total in zip(chunks, sums):
+        count, place_of = outer_range(plan, table, a)
+        work[a] = rows_ref[a]
+
+        def pairs(places, at):
+            others = [[wide(hood[k, pl.ds(base + share + n, 1), :]) for k in range(4)] for n in places]
+            for here in chunks:
                 own = [spread[a, k, here, :] for k in range(4)]
-                for t, other in enumerate(fetched):
+                found = []
+                for t, other in enumerate(others):
                     tile = pair_chunk(own, other)
                     tiles[at + t, here, :] = tile
-                    total = total + tile
-                result.append(total)
-            return at + len(fetched), result
-
-        at, sums = sweep(count, fetch, pairs, (at, [rows_ref[a, here, :] for here in chunks]))
-        for here, values in zip(chunks, sums):
-            work[a, here, :] = values
-        return at
-
-    lax.fori_loop(0, meta[0], block, 0)
+                    found.append(tile)
+                work[a, here, :] = work[a, here, :] + tree(found)
+            return at + len(places)
+
+        return sweep(count, place_of, pairs, at)
+
+    finish_tiles(tiles, lax.fori_loop(0, meta[0], block, 0))
     sums_ref[...] = lane_sums(work, share, width) + sub_sums(cols_ref)
 
     @pl.when(again)
@@ -334,7 +352,7 @@
         work[...] = jnp.zeros_like(work)
 
         def block(a, state):
-            count, place_of = inner_range(meta, table, a)
+            count, place_of = inner_range(plan, table, a)
 
             def inner(t, at):
                 n = place_of(t)
@@ -346,7 +364,7 @@
                 return at + 1
 
             at = lax.fori_loop(0, count, inner, state[0]) + 1
-            count, place_far = outer_range(meta, table, a)
+            count, place_far = outer_range(plan, table, a)
 
             def outer(t, at):
                 work[a] = work[a] + tiles[at] * factor(times, a, place_far(t))
@@ -365,45 +383,48 @@
     precond_ref[...] = source[...] / diagonal
 
 
-def apply_inner(meta, table, again, field, alone, times, tiles, rows_ref, cols_ref, spread, near, lone):
+def apply_inner(meta, table, plan, again, field, alone, times, tiles, rows_ref, cols_ref, spread, near, lone, cols):
     share, width = field.shape
     chunks = pieces_of(width)
     near[0:share, :] = field[...]
+    near[share:, :] = jnp.zeros((SUB, width), jnp.float32)
     lone[...] = field[...] * alone[...]
     spread_columns(spread, lambda a: a, field[...])
-    cols_ref[...] = jnp.zeros_like(cols_ref)
+    cols[...] = jnp.zeros_like(cols)
 
     def run(weighted):
         def block(a, at):
-            count, place_of = inner_range(meta, table, a)
+            count, place_of = inner_range(plan, table, a)
 
             def fetch(t):
-                n = place_of(t)
+                n = jnp.where(t < count, place_of(t), share)
                 return n, wide(near[pl.ds(n, 1), :])
 
             def pairs(fetched, carry):
                 at, sums = carry
                 if weighted:
-                    fetched = [(n, value * factor(times, a, n)) for n, value in fetched]
-                down = [[None] * 4 for _ in fetched]
+                    fetched = [(n, value * factor(times, a, jnp.minimum(n, share - 1))) for n, value in fetched]
+                down = [[None] * 2 for _ in fetched]
                 result = []
                 for c, (here, total) in enumerate(zip(chunks, sums)):
                     own = spread[a, here, :]
+                    found = []
                     for t, (_, value) in enumerate(fetched):
                         tile = tiles[at + t, here, :]
                         gather(down[t], c, tile * own)
-                        total = total + tile * value
-                    result.append(total)
+                        found.append(tile * value)
+                    result.append(total + tree(found))
                 for (n, _), partial in zip(fetched, down):
                     there = pl.ds(pl.multiple_of(n * SUB, SUB), SUB)
                     partial = tree(partial)
                     if weighted:
-                        partial = partial * factor(times, n, a)
-                    cols_ref[there, :] = cols_ref[there, :] + partial
+                        partial = partial * factor(times, jnp.minimum(n, share - 1), a)
+                    cols[there, :] = cols[there, :] + partial
                 return at + len(fetched), result
 
             zero = jnp.zeros((SUB, width), jnp.float32)
-            at, sums = sweep(count, fetch, pairs, (at, [zero] * len(chunks)))
+            _, sums = padded_sweep(count, fetch, pairs, (at, [zero] * len(chunks)))
+            at = at + count
             value = wide(lone[pl.ds(a, 1), :])
             for here, old in zip(chunks, sums):
                 rows_ref[a, here, :] = old + tiles[at, here, :] * value
@@ -412,9 +433,10 @@
         lax.fori_loop(0, meta[0], block, 0)
 
     either(again[0], run)
-
-
-def apply_outer(meta, table, again, received, times, tiles, rows_ref, cols_ref, work, hood):
+    cols_ref[...] = cols[0 : share * SUB, :]
+
+
+def apply_outer(meta, table, plan, again, received, times, tiles, rows_ref, cols_ref, work, hood):
     first, second, *ends = received
     columns = len(received)
     share, width = first.shape
@@ -434,14 +456,16 @@
     for c, end in enumerate(ends, 1):
         head = jnp.where(column == c, end[...], head)
     hood[pl.ds(own + jnp.clip(filled - base, 0, 2 * share), share), :] = head
+    nothing = hood.shape[0] - SUB
+    hood[nothing:, :] = jnp.zeros((SUB, width), jnp.float32)
 
     def run(weighted):
         def block(a, at):
-            count, place_of = outer_range(meta, table, a)
+            count, place_of = outer_range(plan, table, a)
 
             def fetch(t):
                 place = place_of(t)
-                value = hood[pl.ds(own + place, 1), :]
+                value = hood[pl.ds(jnp.where(t < count, own + place, nothing), 1), :]
                 if weighted:
                     value = value * factor(times, a, place)
                 return wide(value)
@@ -450,15 +474,13 @@
                 at, sums = carry
                 result = []
                 for here, total in zip(chunks, sums):
-                    for t, value in enumerate(values):
-                        total = total + tiles[at + t, here, :] * value
-                    result.append(total)
+                    result.append(total + tree([tiles[at + t, here, :] * value for t, value in enumerate(values)]))
                 return at + len(values), result
 
-            at, sums = sweep(count, fetch, pairs, (at, [rows_ref[a, here, :] for here in chunks]))
+            _, sums = padded_sweep(count, fetch, pairs, (at, [rows_ref[a, here, :] for here in chunks]))
             for here, values in zip(chunks, sums):
                 work[a, here, :] = values
-            return at
+            return at + count
 
         lax.fori_loop(0, meta[0], block, 0)
 
@@ -466,16 +488,16 @@
     return jnp.where(alive_rows(meta, share, width), lane_sums(work, share, width) + sub_sums(cols_ref), 0.0)
 
 
-def apply_first(meta, table, again, diagonal, times, *rest):
+def apply_first(meta, table, plan, again, diagonal, times, *rest):
     *received, tiles, rows_ref, cols_ref, spill_ref, scaled_ref, work, hood = rest
-    spill = apply_outer(meta, table, again, received, times, tiles, rows_ref, cols_ref, work, hood)
+    spill = apply_outer(meta, table, plan, again, received, times, tiles, rows_ref, cols_ref, work, hood)
     spill_ref[...] = spill
     scaled_ref[...] = spill / diagonal[...]
 
 
-def apply_second(meta, table, again, source, precond, spill, scaled, times, *rest):
+def apply_second(meta, table, plan, again, source, precond, spill, scaled, times, *rest):
     *received, tiles, rows_ref, cols_ref, twice_ref, sums_ref, work, hood = rest
-    twice = apply_outer(meta, table, again, received, times, tiles, rows_ref, cols_ref, work, hood)
+    twice = apply_outer(meta, table, plan, again, received, times, tiles, rows_ref, cols_ref, work, hood)
     twice_ref[...] = twice
     share, width = twice.shape
     lane = lax.broadcasted_iota(jnp.int32, (1, width), 1)
@@ -487,8 +509,9 @@
     sums_ref[...] = wide(sums)
 
 
-def finish(source, precond, spill, scaled, twice, mine, other, solution_ref, residual_ref):
-    sums = mine[...] + other[...]
+def finish(source, precond, spill, scaled, twice, *rest):
+    *parts, solution_ref, residual_ref = rest
+    sums = tree([ref[...] for ref in parts])
 
     def pick(k):
         return sums[0:1, k : k + 1]
@@ -523,8 +546,8 @@
     few = jax.ShapeDtypeStruct((SUB, width), f32)
     message = jax.ShapeDtypeStruct((4, share, width), f32)
     most_inner, most_outer = tile_bounds(share)
-    inner_tiles = pltpu.VMEM((most_inner, width, width), f32)
-    outer_tiles = pltpu.VMEM((most_outer, width, width), f32)
+    inner_tiles = pltpu.VMEM((most_inner + TURN, width, width), f32)
+    outer_tiles = pltpu.VMEM((most_outer + TURN, width, width), f32)
     square = pltpu.VMEM((share, width, width), f32)
     narrow = pltpu.VMEM((share * SUB, width), f32)
     table = jnp.asarray(TABLE.reshape(-1))
@@ -562,31 +585,35 @@
     second = lax.ppermute(second, "piece", [(i, ((i ^ 1) + (1 if i % 2 else -1) * 2) % pieces) for i in range(pieces)])
     times = [lax.ppermute(t, "col", [(i, i ^ k) for i in range(columns)]) if k else t for k, t in enumerate(times)]
 
-    tiles_in, spread, rows, cols, selfs = call(
+    plan, tiles_in, spread, rows, cols, selfs = call(
         build_inner,
         (meta, table, near),
-        [inner_tiles, pltpu.VMEM((share, 4, width, width), f32), square, narrow, narrow],
+        [pltpu.SMEM((share * FIELDS,), jnp.int32), inner_tiles, pltpu.VMEM((share, 4, width, width), f32),
+         square, narrow, narrow],
         work=16 * most_inner,
     )
+    plan = pltpu.with_memory_space_constraint(plan, pltpu.SMEM)
     again, tiles_out, diagonal, precond, times, alone = call(
         build_outer,
-        (meta, table, around, first, second, density, source,
+        (meta, table, plan, around, first, second, density, source,
          held(tiles_in), held(spread), held(rows), held(cols), held(selfs), *times),
         [pltpu.SMEM((1,), jnp.int32), outer_tiles, vector, vector, vector, vector],
         [pltpu.VMEM((4, capacity + 2 * share, width), f32), pltpu.VMEM((share, width, width), f32)]
         + [pltpu.VMEM((share, width), f32)] * 2,
         16 * most_outer,
+        scalars=3,
     )
     again = pltpu.with_memory_space_constraint(again, pltpu.SMEM)
 
     def inner(field):
         return call(
             apply_inner,
-            (meta, table, again, field, alone, times, held(tiles_in)),
+            (meta, table, plan, again, field, alone, times, held(tiles_in)),
             [square, narrow],
-            [pltpu.VMEM((share, width, width), f32), pltpu.VMEM((2 * share, width), f32), pltpu.VMEM((share, width), f32)],
+            [pltpu.VMEM((share, width, width), f32), pltpu.VMEM((share + SUB, width), f32), pltpu.VMEM((share, width), f32),
+             pltpu.VMEM(((share + 1) * SUB, width), f32)],
             4 * most_inner,
-            scalars=3,
+            scalars=4,
         )
 
     def exchange(field):
@@ -611,36 +638,40 @@
     rows, cols = inner(precond)
     spill, scaled = call(
         apply_first,
-        (meta, table, again, diagonal, times, *received, held(tiles_out), held(rows), held(cols)),
+        (meta, table, plan, again, diagonal, times, *received, held(tiles_out), held(rows), held(cols)),
         [vector, vector],
         scratch,
         2 * most_outer,
-        scalars=3,
+        scalars=4,
     )
 
     received = exchange(scaled)
     rows, cols = inner(scaled)
     twice, sums = call(
         apply_second,
-        (meta, table, again, source, precond, spill, scaled, times, *received, held(tiles_out), held(rows), held(cols)),
+        (meta, table, plan, again, source, precond, spill, scaled, times, *received, held(tiles_out), held(rows), held(cols)),
         [vector, few],
         scratch,
         2 * most_outer,
-        scalars=3,
+        scalars=4,
     )
 
     def swap(values, axis, step):
         return lax.ppermute(values, axis, [(i, i ^ step) for i in range(lax.axis_size(axis))])
 
-    sums = tree([sums] + [swap(sums, "col", k) for k in range(1, columns)])
-    steps = [1 << k for k in range(pieces.bit_length() - 1)]
-    for step in steps[:-1]:
-        sums = sums + swap(sums, "piece", step)
-    other = swap(sums, "piece", steps[-1])
+    def together(values, axis, low, size):
+        return tree([values] + [swap(values, axis, low * k) for k in range(1, size)])
+
+    sums = together(sums, "col", 1, columns)
+    step = 1
+    while pieces // step > 8:
+        sums = together(sums, "piece", step, 8)
+        step *= 8
+    others = [swap(sums, "piece", step * k) for k in range(1, pieces // step)]
 
     return tuple(call(
         finish,
-        (source, precond, spill, scaled, twice, sums, other),
+        (source, precond, spill, scaled, twice, sums, *others),
         [vector, vector],
         scalars=0,
     ))

time: 78.8 us -> 76.8 us (0.975)
  waiting for transfers between devices: 10 us -> 6.57 us
  starting transfers between devices: 30.1 us -> 33.4 us
  Pallas kernels: 37.8 us -> 35.7 us
    ppermute x6 -> x10, waiting for transfers between devices: 9.62 us -> 5.82 us  [swap(): lax.ppermute(values, axis, [(i, i ^ step) for i in range(lax.axis_size(ax...]
    ppermute x6 -> x10, starting transfers between devices: 7.37 us -> 10.7 us  [swap(): lax.ppermute(values, axis, [(i, i ^ step) for i in range(lax.axis_size(ax...]
    pallas_call x8, Pallas kernels: 37.8 us -> 35.7 us  [call(): pl.pallas_call(kernel, out_shape=outs, in_specs=[SMEM] * scalars + [HBM]...]
  transfers between devices with their start and end apart: 19 -> 23, of which waited for: 7 -> 6; matrix products, arithmetic and copies ran while one was open for 0% -> 0% of each run, Pallas kernels for 29% -> 29%
where the time goes in v6:
time: 76.8 us; the launch traced here: 76.5 us
  Pallas kernels  35.7 us (46%)
  starting transfers between devices  33.4 us (43%)
  waiting for transfers between devices  6.57 us (9%)
  between operations  0.78 us (1%)
    pallas_call x8, Pallas kernels, call(): pl.pallas_call(kernel, out_shape=outs, in_specs=[SMEM] * scalars + [HBM]...  35.7 us
    ppermute x8, starting transfers between devices, exchange(): return [lax.ppermute(field, axes, list(enumerate(to))) for to in swaps]  14.3 us
    ppermute x10, starting transfers between devices, swap(): lax.ppermute(values, axis, [(i, i ^ step) for i in range(lax.axis_size(ax...  10.7 us
    ppermute x10, waiting for transfers between devices, swap(): lax.ppermute(values, axis, [(i, i ^ step) for i in range(lax.axis_size(ax...  5.82 us
    ppermute x3, starting transfers between devices, body(): lax.ppermute(t, 'col', [(i, i ^ k) for i in range(columns)])  4.39 us
    ppermute x1, starting transfers between devices, body(): lax.ppermute(second, 'piece', [(i, ((i ^ 1) + (1 if i % 2 else -1) * 2) %...  3.55 us
  transfers between devices with their start and end apart: 23, of which 6 were waited for; matrix products, arithmetic and copies ran while one was open for 0% of the time, Pallas kernels for 29%

profile of v6, /device:TPU:0, one launch (start us, length us, event | category | flops | bytes accessed | tf_op | source)
XLA Modules:
  0.0 76.5 jit_solution(17427355283168594649)
XLA Ops:
  0.6 1.8 %prepare.1 = (s32[8]{0:T(128)S(4)}, s32[1472]{0:T(1024)S(4)}, f32[4,192,128]{2,1,0:T(8,128)S(1)}, f32[4,64,128]{2,1,0:T(8,128)S(1)}, f32[32,128]{1,0:T(8,128)S(1...) custom-call(s32[8]{0:T(128)} %counts.1, ...), custom_call_target="tpu_custom_call" | custom-call | tf_op jit(solution)/shard_map/prepare/pallas_call | solution.py:556
  2.5 0.5 collective-permute-start
  3.0 3.6 %collective-permute-start.1 = (f32[4,32,128]{2,1,0:T(8,128)S(1)}, f32[4,32,128]{2,1,0:T(8,128)S(1)}, u32[]{:S(2)}, u32[]{:S(2)}) collective-permute-start(f32[4,32,128]{2,1,0:T(8,128)S(1)} %get-tuple-element.41), channel_id=1, source_target_pairs={{0,28},{4,8},{8,4},{12,16},{16,12},{20,24},{24,20},{28,0},{1,29},{... | collective-permute-start | bytes 196616 | tf_op jit(solution)/shard_map/ppermute | solution.py:585
  6.6 1.6 %collective-permute-start.2 = (f32[32,128]{1,0:T(8,128)S(1)}, f32[32,128]{1,0:T(8,128)S(1)}, u32[]{:S(2)}, u32[]{:S(2)}) collective-permute-start(f32[32,128]{1,0:T(8,128)S(1)} %get-tuple-element.49), channel_id=1, source_target_pairs={{0,1},{1,0},{2,3},{3,2},{4,5},{5,4},{6,7},{7,6},{8,9},{9,8},{10,11... | collective-permute-start | bytes 49160 | tf_op jit(solution)/shard_map/ppermute | solution.py:586
  8.1 2.6 %collective-permute-start.3 = (f32[32,128]{1,0:T(8,128)S(1)}, f32[32,128]{1,0:T(8,128)S(1)}, u32[]{:S(2)}, u32[]{:S(2)}) collective-permute-start(f32[32,128]{1,0:T(8,128)S(1)} %get-tuple-element.50), channel_id=1, source_target_pairs={{0,2},{1,3},{2,0},{3,1},{4,6},{5,7},{6,4},{7,5},{8,10},{9,11},{10,... | collective-permute-start | bytes 49160 | tf_op jit(solution)/shard_map/ppermute | solution.py:586
  10.7 0.2 collective-permute-start.4
  10.9 13.3 %build_inner.1 = (s32[192]{0:T(256)S(4)}, f32[220,128,128]{2,1,0:T(8,128)S(1)}, f32[32,4,128,128]{3,2,1,0:T(8,128)S(1)}, f32[32,128,128]{2,1,0:T(8,128)S(1)}, f3...) custom-call(s32[8]{0:T(128)S(4)} %get-tuple-element.35.meta, s32[1472]{0:T(1024)S(4)} %get-tuple-element.36.table, ...), custom_call_target="tpu_custom_call" | custom-call | flops 56623104 | tf_op jit(solution)/shard_map/build_inner/pallas_call | solution.py:556
  24.2 0.0 collective-permute-done.2.rest_1_
  24.2 0.0 collective-permute-done.3.rest_2_
  24.2 0.0 collective-permute-done.4.rest_3_
  24.2 0.0 collective-permute-done.first
  24.2 0.0 collective-permute-done.1.second
  24.3 6.3 %build_outer.1 = (s32[1]{0:T(128)S(4)}, f32[226,128,128]{2,1,0:T(8,128)S(1)}, f32[32,128]{1,0:T(8,128)S(1)}, f32[32,128]{1,0:T(8,128)S(1)}, f32[32,128]{1,0:T(8,128)S(1)}, /*index=5*/f32[32,128]{1,0:T(8,128)S(1)}) custom-call(s32[8]{0:T(128)S(4)} %get-tuple-element.35.meta, s32[1472]{0:T(1024)S(4)} %get-tuple-element.36.table, ...), custom_call_target="tpu_custom_call" | custom-call | flops 58195968 | tf_op jit(solution)/shard_map/build_outer/pallas_call | solution.py:556
  30.5 5.1 %collective-permute-start.8 = (f32[32,128]{1,0:T(8,128)S(1)}, f32[32,128]{1,0:T(8,128)S(1)}, u32[]{:S(2)}, u32[]{:S(2)}) collective-permute-start(f32[32,128]{1,0:T(8,128)S(1)} %get-tuple-element.52.field.precond), channel_id=1, source_target_pairs={{0,1},{1,3},{2,4},{3,0},{4,2},{5,7},{6,8},{7,5},{8,6},{9,11},{10,1... | collective-permute-start | bytes 49160 | tf_op jit(solution)/shard_map/ppermute | solution.py:633
  35.6 1.1 %collective-permute-start.7 = (f32[32,128]{1,0:T(8,128)S(1)}, f32[32,128]{1,0:T(8,128)S(1)}, u32[]{:S(2)}, u32[]{:S(2)}) collective-permute-start(f32[32,128]{1,0:T(8,128)S(1)} %get-tuple-element.52.field.precond), channel_id=1, source_target_pairs={{0,2},{1,4},{2,3},{3,0},{4,1},{5,8},{6,7},{7,6},{8,5},{9,12},{10,1... | collective-permute-start | bytes 49160 | tf_op jit(solution)/shard_map/ppermute | solution.py:633
  36.7 1.5 %collective-permute-start.6 = (f32[32,128]{1,0:T(8,128)S(1)}, f32[32,128]{1,0:T(8,128)S(1)}, u32[]{:S(2)}, u32[]{:S(2)}) collective-permute-start(f32[32,128]{1,0:T(8,128)S(1)} %get-tuple-element.52.field.precond), channel_id=1, source_target_pairs={{0,31},{1,2},{2,1},{3,4},{4,3},{5,6},{6,5},{7,8},{8,7},{9,10},{10,... | collective-permute-start | bytes 49160 | tf_op jit(solution)/shard_map/ppermute | solution.py:633
  38.2 0.1 collective-permute-start.5
  38.4 4.4 %apply_inner.2 = (f32[32,128,128]{2,1,0:T(8,128)S(1)}, f32[256,128]{1,0:T(8,128)S(1)}) custom-call(s32[8]{0:T(128)S(4)} %get-tuple-element.35.meta, s32[1472]{0:T(1024)S(4)} %get-tuple-element.36.table, s32[192]{0:T(256)S(4)} %get-tuple-element.38.plan, s32[1]{0:T(128)S(4)} %get-tuple-element.53.again, f32[32,128]{1,0:T(8,128)S(1)} %get-tuple-element.52.field.precond, ...), custom_call_target="tpu_custom_call" | custom-call | flops 14155776 | tf_op jit(solution)/shard_map/apply_inner/pallas_call | solution.py:556
  42.8 0.0 collective-permute-done.8.rest_3_
  42.8 0.0 collective-permute-done.7.rest_2_
  42.8 0.7 collective-permute-done.6.rest_1_
  43.5 0.0 collective-permute-done.5.rest_0_
  43.5 2.3 %apply_first.1 = (f32[32,128]{1,0:T(8,128)S(1)}, f32[32,128]{1,0:T(8,128)S(1)}) custom-call(s32[8]{0:T(128)S(4)} %get-tuple-element.35.meta, s32[1472]{0:T(1024)S(4)} %get-tuple-element.36.table, s32[192]{0:T(256)S(4)} %get-tuple-element.38.plan, s32[1]{0:T(128)S(4)} %get-tuple-element.53.again, f32[32,128]{1,0:T(8,128)S(1)} %get-tuple-element.54.diagonal, ...), custom_call_target="tpu_custom_call" | custom-call | flops 7274496 | tf_op jit(solution)/shard_map/apply_first/pallas_call | solution.py:556
  45.8 2.0 %collective-permute-start.12 = (f32[32,128]{1,0:T(8,128)S(1)}, f32[32,128]{1,0:T(8,128)S(1)}, u32[]{:S(2)}, u32[]{:S(2)}) collective-permute-start(f32[32,128]{1,0:T(8,128)S(1)} %get-tuple-element.61.field.scaled), channel_id=1, source_target_pairs={{0,1},{1,3},{2,4},{3,0},{4,2},{5,7},{6,8},{7,5},{8,6},{9,11},{10,1... | collective-permute-start | bytes 49160 | tf_op jit(solution)/shard_map/ppermute | solution.py:633
  47.8 1.8 %collective-permute-start.11 = (f32[32,128]{1,0:T(8,128)S(1)}, f32[32,128]{1,0:T(8,128)S(1)}, u32[]{:S(2)}, u32[]{:S(2)}) collective-permute-start(f32[32,128]{1,0:T(8,128)S(1)} %get-tuple-element.61.field.scaled), channel_id=1, source_target_pairs={{0,2},{1,4},{2,3},{3,0},{4,1},{5,8},{6,7},{7,6},{8,5},{9,12},{10,1... | collective-permute-start | bytes 49160 | tf_op jit(solution)/shard_map/ppermute | solution.py:633
  49.6 2.6 %collective-permute-start.10 = (f32[32,128]{1,0:T(8,128)S(1)}, f32[32,128]{1,0:T(8,128)S(1)}, u32[]{:S(2)}, u32[]{:S(2)}) collective-permute-start(f32[32,128]{1,0:T(8,128)S(1)} %get-tuple-element.61.field.scaled), channel_id=1, source_target_pairs={{0,31},{1,2},{2,1},{3,4},{4,3},{5,6},{6,5},{7,8},{8,7},{9,10},{10,... | collective-permute-start | bytes 49160 | tf_op jit(solution)/shard_map/ppermute | solution.py:633
  52.2 0.0 collective-permute-start.9
  52.2 4.4 %apply_inner.3 = (f32[32,128,128]{2,1,0:T(8,128)S(1)}, f32[256,128]{1,0:T(8,128)S(1)}) custom-call(s32[8]{0:T(128)S(4)} %get-tuple-element.35.meta, s32[1472]{0:T(1024)S(4)} %get-tuple-element.36.table, s32[192]{0:T(256)S(4)} %get-tuple-element.38.plan, s32[1]{0:T(128)S(4)} %get-tuple-element.53.again, f32[32,128]{1,0:T(8,128)S(1)} %get-tuple-element.61.field.scaled, ...), custom_call_target="tpu_custom_call" | custom-call | flops 14155776 | tf_op jit(solution)/shard_map/apply_inner/pallas_call | solution.py:556
  56.6 0.0 collective-permute-done.12.rest_3_
  56.6 0.0 collective-permute-done.11.rest_2_
  56.6 0.0 collective-permute-done.10.rest_1_
  56.6 0.0 collective-permute-done.9.rest_0_
  56.6 2.4 %apply_second.1 = (f32[32,128]{1,0:T(8,128)S(1)}, f32[8,128]{1,0:T(8,128)S(1)}) custom-call(s32[8]{0:T(128)S(4)} %get-tuple-element.35.meta, s32[1472]{0:T(1024)S(4)} %get-tuple-element.36.table, s32[192]{0:T(256)S(4)} %get-tuple-element.38.plan, s32[1]{0:T(128)S(4)} %get-tuple-element.53.again, f32[32,128]{1,0:T(8,128)S(1)} %get-tuple-element.34.source, ...), custom_call_target="tpu_custom_call" | custom-call | flops 7274496 | tf_op jit(solution)/shard_map/apply_second/pallas_call | solution.py:556
  59.0 0.0 collective-permute-start.15
  59.0 4.2 %collective-permute-start.14 = (f32[8,128]{1,0:T(8,128)S(1)}, f32[8,128]{1,0:T(8,128)S(1)}, u32[]{:S(2)}, u32[]{:S(2)}) collective-permute-start(f32[8,128]{1,0:T(8,128)S(1)} %get-tuple-element.65), channel_id=1, source_target_pairs={{0,2},{1,3},{2,0},{3,1},{4,6},{5,7},{6,4},{7,5},{8,10},{9,11},{10,... | collective-permute-start | bytes 12296 | tf_op jit(solution)/shard_map/ppermute | solution.py:660
  63.3 0.1 collective-permute-start.13
  63.4 1.0 %collective-permute-done.15 = f32[8,128]{1,0:T(8,128)S(1)} collective-permute-done((f32[8,128]{1,0:T(8,128)S(1)}, f32[8,128]{1,0:T(8,128)S(1)}, u32[]{:S(2)}, u32[]{:S(2)}) %collective-permute-start.15) | collective-permute-done | bytes 4128 | tf_op jit(solution)/shard_map/ppermute | solution.py:660
  64.4 0.5 collective-permute-done.14
  64.9 2.0 %collective-permute-done.13 = f32[8,128]{1,0:T(8,128)S(1)} collective-permute-done((f32[8,128]{1,0:T(8,128)S(1)}, f32[8,128]{1,0:T(8,128)S(1)}, u32[]{:S(2)}, u32[]{:S(2)}) %collective-permute-start.13) | collective-permute-done | bytes 4128 | tf_op jit(solution)/shard_map/ppermute | solution.py:660
  66.9 0.0 collective-permute-start.22
  66.9 0.7 collective-permute-start.21
  67.6 3.7 %collective-permute-start.20 = (f32[8,128]{1,0:T(8,128)S(1)}, f32[8,128]{1,0:T(8,128)S(1)}, u32[]{:S(2)}, u32[]{:S(2)}) collective-permute-start(f32[8,128]{1,0:T(8,128)S(1)} %add_add_fusion.rest_0_), channel_id=1, source_target_pairs={{0,20},{4,16},{8,28},{12,24},{16,4},{20,0},{24,12},{28,8},{1,21},{... | collective-permute-start | bytes 12296 | tf_op jit(solution)/shard_map/ppermute | solution.py:660
  71.3 0.0 collective-permute-start.19
  71.3 0.6 collective-permute-start.18
  71.9 0.0 collective-permute-done.22.rest_7_
  71.9 1.2 %collective-permute-start.17 = (f32[8,128]{1,0:T(8,128)S(1)}, f32[8,128]{1,0:T(8,128)S(1)}, u32[]{:S(2)}, u32[]{:S(2)}) collective-permute-start(f32[8,128]{1,0:T(8,128)S(1)} %add_add_fusion.rest_0_), channel_id=1, source_target_pairs={{0,8},{4,12},{8,0},{12,4},{16,24},{20,28},{24,16},{28,20},{1,9},{5... | collective-permute-start | bytes 12296 | tf_op jit(solution)/shard_map/ppermute | solution.py:660
  73.1 0.0 collective-permute-done.21.rest_6_
  73.1 0.1 collective-permute-start.16
  73.2 0.0 collective-permute-done.20.rest_5_
  73.2 1.7 %collective-permute-done.19.rest_4_ = f32[8,128]{1,0:T(8,128)S(1)} collective-permute-done((f32[8,128]{1,0:T(8,128)S(1)}, f32[8,128]{1,0:T(8,128)S(1)}, u32[]{:S(2)}, u32[]{:S(2)}) %collective-permute-start.19) | collective-permute-done | bytes 4128 | tf_op jit(solution)/shard_map/ppermute | solution.py:660
  74.9 0.0 collective-permute-done.18.rest_3_
  74.9 0.6 collective-permute-done.17.rest_2_
  75.5 0.0 collective-permute-done.16.rest_1_
  75.5 0.9 %finish.1 = (f32[32,128]{1,0:T(8,128)}, f32[32,128]{1,0:T(8,128)}) custom-call(f32[32,128]{1,0:T(8,128)S(1)} %get-tuple-element.34.source, f32[32,128]{1,0:T(8,128)S(1)} %get-tuple-element.52.field.precond, f32[32,128]{1,0:T(8,128)S(1)} %get-tuple-element.60.spill, f32[32,128]{1,0:T(8,128)S(1)} %get-tuple-element.61.field.scaled, ...), custom_call_target="tpu_custom_call" | custom-call | tf_op jit(solution)/shard_map/finish/pallas_call | solution.py:556
  (1 shorter events, 0.0 us)
Async XLA Ops:
  2.5 21.8 %collective-permute-start = (f32[4,32,128]{2,1,0:T(8,128)S(1)}, f32[4,32,128]{2,1,0:T(8,128)S(1)}, u32[]{:S(2)}, u32[]{:S(2)}) collective-permute-start(f32[4,32,128]{2,1,0:T(8,128)S(1)} %get-tuple-element.40), channel_id=1, source_target_pairs={{0,4},{4,0},{8,12},{12,8},{16,20},{20,16},{24,28},{28,24},{1,5},{5... | collective-permute-start | bytes 196616 | tf_op jit(solution)/shard_map/ppermute | solution.py:584
  3.0 21.2 %collective-permute-start.1 = (f32[4,32,128]{2,1,0:T(8,128)S(1)}, f32[4,32,128]{2,1,0:T(8,128)S(1)}, u32[]{:S(2)}, u32[]{:S(2)}) collective-permute-start(f32[4,32,128]{2,1,0:T(8,128)S(1)} %get-tuple-element.41), channel_id=1, source_target_pairs={{0,28},{4,8},{8,4},{12,16},{16,12},{20,24},{24,20},{28,0},{1,29},{... | collective-permute-start | bytes 196616 | tf_op jit(solution)/shard_map/ppermute | solution.py:585
  6.6 17.7 %collective-permute-start.2 = (f32[32,128]{1,0:T(8,128)S(1)}, f32[32,128]{1,0:T(8,128)S(1)}, u32[]{:S(2)}, u32[]{:S(2)}) collective-permute-start(f32[32,128]{1,0:T(8,128)S(1)} %get-tuple-element.49), channel_id=1, source_target_pairs={{0,1},{1,0},{2,3},{3,2},{4,5},{5,4},{6,7},{7,6},{8,9},{9,8},{10,11... | collective-permute-start | bytes 49160 | tf_op jit(solution)/shard_map/ppermute | solution.py:586
  8.1 16.1 %collective-permute-start.3 = (f32[32,128]{1,0:T(8,128)S(1)}, f32[32,128]{1,0:T(8,128)S(1)}, u32[]{:S(2)}, u32[]{:S(2)}) collective-permute-start(f32[32,128]{1,0:T(8,128)S(1)} %get-tuple-element.50), channel_id=1, source_target_pairs={{0,2},{1,3},{2,0},{3,1},{4,6},{5,7},{6,4},{7,5},{8,10},{9,11},{10,... | collective-permute-start | bytes 49160 | tf_op jit(solution)/shard_map/ppermute | solution.py:586
  10.7 13.5 %collective-permute-start.4 = (f32[32,128]{1,0:T(8,128)S(1)}, f32[32,128]{1,0:T(8,128)S(1)}, u32[]{:S(2)}, u32[]{:S(2)}) collective-permute-start(f32[32,128]{1,0:T(8,128)S(1)} %get-tuple-element.51), channel_id=1, source_target_pairs={{0,3},{1,2},{2,1},{3,0},{4,7},{5,6},{6,5},{7,4},{8,11},{9,10},{10,... | collective-permute-start | bytes 49160 | tf_op jit(solution)/shard_map/ppermute | solution.py:586
  30.5 12.2 %collective-permute-start.8 = (f32[32,128]{1,0:T(8,128)S(1)}, f32[32,128]{1,0:T(8,128)S(1)}, u32[]{:S(2)}, u32[]{:S(2)}) collective-permute-start(f32[32,128]{1,0:T(8,128)S(1)} %get-tuple-element.52.field.precond), channel_id=1, source_target_pairs={{0,1},{1,3},{2,4},{3,0},{4,2},{5,7},{6,8},{7,5},{8,6},{9,11},{10,1... | collective-permute-start | bytes 49160 | tf_op jit(solution)/shard_map/ppermute | solution.py:633
  35.6 7.1 %collective-permute-start.7 = (f32[32,128]{1,0:T(8,128)S(1)}, f32[32,128]{1,0:T(8,128)S(1)}, u32[]{:S(2)}, u32[]{:S(2)}) collective-permute-start(f32[32,128]{1,0:T(8,128)S(1)} %get-tuple-element.52.field.precond), channel_id=1, source_target_pairs={{0,2},{1,4},{2,3},{3,0},{4,1},{5,8},{6,7},{7,6},{8,5},{9,12},{10,1... | collective-permute-start | bytes 49160 | tf_op jit(solution)/shard_map/ppermute | solution.py:633
  36.7 6.8 %collective-permute-start.6 = (f32[32,128]{1,0:T(8,128)S(1)}, f32[32,128]{1,0:T(8,128)S(1)}, u32[]{:S(2)}, u32[]{:S(2)}) collective-permute-start(f32[32,128]{1,0:T(8,128)S(1)} %get-tuple-element.52.field.precond), channel_id=1, source_target_pairs={{0,31},{1,2},{2,1},{3,4},{4,3},{5,6},{6,5},{7,8},{8,7},{9,10},{10,... | collective-permute-start | bytes 49160 | tf_op jit(solution)/shard_map/ppermute | solution.py:633
  38.2 5.3 %collective-permute-start.5 = (f32[32,128]{1,0:T(8,128)S(1)}, f32[32,128]{1,0:T(8,128)S(1)}, u32[]{:S(2)}, u32[]{:S(2)}) collective-permute-start(f32[32,128]{1,0:T(8,128)S(1)} %get-tuple-element.52.field.precond), channel_id=1, source_target_pairs={{0,1},{1,0},{2,3},{3,2},{4,5},{5,4},{6,7},{7,6},{8,9},{9,8},{10,11... | collective-permute-start | bytes 49160 | tf_op jit(solution)/shard_map/ppermute | solution.py:633
  45.8 10.8 %collective-permute-start.12 = (f32[32,128]{1,0:T(8,128)S(1)}, f32[32,128]{1,0:T(8,128)S(1)}, u32[]{:S(2)}, u32[]{:S(2)}) collective-permute-start(f32[32,128]{1,0:T(8,128)S(1)} %get-tuple-element.61.field.scaled), channel_id=1, source_target_pairs={{0,1},{1,3},{2,4},{3,0},{4,2},{5,7},{6,8},{7,5},{8,6},{9,11},{10,1... | collective-permute-start | bytes 49160 | tf_op jit(solution)/shard_map/ppermute | solution.py:633
  47.8 8.8 %collective-permute-start.11 = (f32[32,128]{1,0:T(8,128)S(1)}, f32[32,128]{1,0:T(8,128)S(1)}, u32[]{:S(2)}, u32[]{:S(2)}) collective-permute-start(f32[32,128]{1,0:T(8,128)S(1)} %get-tuple-element.61.field.scaled), channel_id=1, source_target_pairs={{0,2},{1,4},{2,3},{3,0},{4,1},{5,8},{6,7},{7,6},{8,5},{9,12},{10,1... | collective-permute-start | bytes 49160 | tf_op jit(solution)/shard_map/ppermute | solution.py:633
  49.6 7.0 %collective-permute-start.10 = (f32[32,128]{1,0:T(8,128)S(1)}, f32[32,128]{1,0:T(8,128)S(1)}, u32[]{:S(2)}, u32[]{:S(2)}) collective-permute-start(f32[32,128]{1,0:T(8,128)S(1)} %get-tuple-element.61.field.scaled), channel_id=1, source_target_pairs={{0,31},{1,2},{2,1},{3,4},{4,3},{5,6},{6,5},{7,8},{8,7},{9,10},{10,... | collective-permute-start | bytes 49160 | tf_op jit(solution)/shard_map/ppermute | solution.py:633
  52.2 4.4 %collective-permute-start.9 = (f32[32,128]{1,0:T(8,128)S(1)}, f32[32,128]{1,0:T(8,128)S(1)}, u32[]{:S(2)}, u32[]{:S(2)}) collective-permute-start(f32[32,128]{1,0:T(8,128)S(1)} %get-tuple-element.61.field.scaled), channel_id=1, source_target_pairs={{0,1},{1,0},{2,3},{3,2},{4,5},{5,4},{6,7},{7,6},{8,9},{9,8},{10,11... | collective-permute-start | bytes 49160 | tf_op jit(solution)/shard_map/ppermute | solution.py:633
  59.0 5.4 %collective-permute-start.15 = (f32[8,128]{1,0:T(8,128)S(1)}, f32[8,128]{1,0:T(8,128)S(1)}, u32[]{:S(2)}, u32[]{:S(2)}) collective-permute-start(f32[8,128]{1,0:T(8,128)S(1)} %get-tuple-element.65), channel_id=1, source_target_pairs={{0,3},{1,2},{2,1},{3,0},{4,7},{5,6},{6,5},{7,4},{8,11},{9,10},{10,... | collective-permute-start | bytes 12296 | tf_op jit(solution)/shard_map/ppermute | solution.py:660
  59.0 5.9 %collective-permute-start.14 = (f32[8,128]{1,0:T(8,128)S(1)}, f32[8,128]{1,0:T(8,128)S(1)}, u32[]{:S(2)}, u32[]{:S(2)}) collective-permute-start(f32[8,128]{1,0:T(8,128)S(1)} %get-tuple-element.65), channel_id=1, source_target_pairs={{0,2},{1,3},{2,0},{3,1},{4,6},{5,7},{6,4},{7,5},{8,10},{9,11},{10,... | collective-permute-start | bytes 12296 | tf_op jit(solution)/shard_map/ppermute | solution.py:660
  63.3 3.6 %collective-permute-start.13 = (f32[8,128]{1,0:T(8,128)S(1)}, f32[8,128]{1,0:T(8,128)S(1)}, u32[]{:S(2)}, u32[]{:S(2)}) collective-permute-start(f32[8,128]{1,0:T(8,128)S(1)} %get-tuple-element.65), channel_id=1, source_target_pairs={{0,1},{1,0},{2,3},{3,2},{4,5},{5,4},{6,7},{7,6},{8,9},{9,8},{10,11... | collective-permute-start | bytes 12296 | tf_op jit(solution)/shard_map/ppermute | solution.py:660
  66.9 5.0 %collective-permute-start.22 = (f32[8,128]{1,0:T(8,128)S(1)}, f32[8,128]{1,0:T(8,128)S(1)}, u32[]{:S(2)}, u32[]{:S(2)}) collective-permute-start(f32[8,128]{1,0:T(8,128)S(1)} %add_add_fusion.rest_0_), channel_id=1, source_target_pairs={{0,28},{4,24},{8,20},{12,16},{16,12},{20,8},{24,4},{28,0},{1,29},{... | collective-permute-start | bytes 12296 | tf_op jit(solution)/shard_map/ppermute | solution.py:660
  66.9 6.2 %collective-permute-start.21 = (f32[8,128]{1,0:T(8,128)S(1)}, f32[8,128]{1,0:T(8,128)S(1)}, u32[]{:S(2)}, u32[]{:S(2)}) collective-permute-start(f32[8,128]{1,0:T(8,128)S(1)} %add_add_fusion.rest_0_), channel_id=1, source_target_pairs={{0,24},{4,28},{8,16},{12,20},{16,8},{20,12},{24,0},{28,4},{1,25},{... | collective-permute-start | bytes 12296 | tf_op jit(solution)/shard_map/ppermute | solution.py:660
  67.6 5.6 %collective-permute-start.20 = (f32[8,128]{1,0:T(8,128)S(1)}, f32[8,128]{1,0:T(8,128)S(1)}, u32[]{:S(2)}, u32[]{:S(2)}) collective-permute-start(f32[8,128]{1,0:T(8,128)S(1)} %add_add_fusion.rest_0_), channel_id=1, source_target_pairs={{0,20},{4,16},{8,28},{12,24},{16,4},{20,0},{24,12},{28,8},{1,21},{... | collective-permute-start | bytes 12296 | tf_op jit(solution)/shard_map/ppermute | solution.py:660
  71.3 3.6 %collective-permute-start.19 = (f32[8,128]{1,0:T(8,128)S(1)}, f32[8,128]{1,0:T(8,128)S(1)}, u32[]{:S(2)}, u32[]{:S(2)}) collective-permute-start(f32[8,128]{1,0:T(8,128)S(1)} %add_add_fusion.rest_0_), channel_id=1, source_target_pairs={{0,16},{4,20},{8,24},{12,28},{16,0},{20,4},{24,8},{28,12},{1,17},{... | collective-permute-start | bytes 12296 | tf_op jit(solution)/shard_map/ppermute | solution.py:660
  71.3 3.6 %collective-permute-start.18 = (f32[8,128]{1,0:T(8,128)S(1)}, f32[8,128]{1,0:T(8,128)S(1)}, u32[]{:S(2)}, u32[]{:S(2)}) collective-permute-start(f32[8,128]{1,0:T(8,128)S(1)} %add_add_fusion.rest_0_), channel_id=1, source_target_pairs={{0,12},{4,8},{8,4},{12,0},{16,28},{20,24},{24,20},{28,16},{1,13},{... | collective-permute-start | bytes 12296 | tf_op jit(solution)/shard_map/ppermute | solution.py:660
  71.9 3.6 %collective-permute-start.17 = (f32[8,128]{1,0:T(8,128)S(1)}, f32[8,128]{1,0:T(8,128)S(1)}, u32[]{:S(2)}, u32[]{:S(2)}) collective-permute-start(f32[8,128]{1,0:T(8,128)S(1)} %add_add_fusion.rest_0_), channel_id=1, source_target_pairs={{0,8},{4,12},{8,0},{12,4},{16,24},{20,28},{24,16},{28,20},{1,9},{5... | collective-permute-start | bytes 12296 | tf_op jit(solution)/shard_map/ppermute | solution.py:660
  73.1 2.4 %collective-permute-start.16 = (f32[8,128]{1,0:T(8,128)S(1)}, f32[8,128]{1,0:T(8,128)S(1)}, u32[]{:S(2)}, u32[]{:S(2)}) collective-permute-start(f32[8,128]{1,0:T(8,128)S(1)} %add_add_fusion.rest_0_), channel_id=1, source_target_pairs={{0,4},{4,0},{8,12},{12,8},{16,20},{20,16},{24,28},{28,24},{1,5},{5... | collective-permute-start | bytes 12296 | tf_op jit(solution)/shard_map/ppermute | solution.py:660

commit v7 on v6

--- a/solution.py
+++ b/solution.py
@@ -144,13 +144,30 @@
     return jnp.broadcast_to(row, (SUB, row.shape[1]))
 
 
-def pair_chunk(own, other):
+def pair_parts(own, other):
     dx = own[0] - other[0]
     dy = own[1] - other[1]
     dz = own[2] - other[2]
     squared = dx * dx + dy * dy + dz * dz
     rest = jnp.maximum(1.0 - squared, 0.0)
-    return rest * rest * pltpu.reciprocal((squared + 0.01) * (own[3] + other[3]), approx=True)
+    return rest * rest, (squared + 0.01) * (own[3] + other[3])
+
+
+def pair_weights(first, second):
+    inverse = pltpu.reciprocal(first[1] * second[1], approx=True)
+    return first[0] * (inverse * second[1]), second[0] * (inverse * first[1])
+
+
+def tile_chunks(own_of, others, chunks):
+    for c in range(0, len(chunks), 2):
+        parts = [[pair_parts(own, other) for other in others] for own in (own_of(chunks[c]), own_of(chunks[c + 1]))]
+        if len(others) == 2:
+            yield c, pair_weights(*parts[0])
+            yield c + 1, pair_weights(*parts[1])
+        else:
+            low, high = pair_weights(parts[0][0], parts[1][0])
+            yield c, [low]
+            yield c + 1, [high]
 
 
 def spread_columns(out, index, rows):
@@ -257,18 +274,18 @@
         count, place_of = inner_range(plan, table, a)
         rows_ref[a] = jnp.zeros((width, width), jnp.float32)
 
+        def own_of(here):
+            return [spread[a, k, here, :] for k in range(4)]
+
         def pairs(places, at):
             others = [rows_at(n) for n in places]
             down = [[None] * 2 for _ in places]
-            for c, here in enumerate(chunks):
-                own = [spread[a, k, here, :] for k in range(4)]
-                found = []
-                for t, other in enumerate(others):
-                    tile = pair_chunk(own, other)
+            for c, found in tile_chunks(own_of, others, chunks):
+                here = chunks[c]
+                for t, tile in enumerate(found):
                     tiles[at + t, here, :] = tile
                     gather(down[t], c, tile)
-                    found.append(tile)
-                rows_ref[a, here, :] = rows_ref[a, here, :] + tree(found)
+                rows_ref[a, here, :] = rows_ref[a, here, :] + tree(list(found))
             for n, partial in zip(places, down):
                 there = pl.ds(pl.multiple_of(n * SUB, SUB), SUB)
                 cols_ref[there, :] = cols_ref[there, :] + tree(partial)
@@ -279,10 +296,9 @@
         lane = lax.broadcasted_iota(jnp.int32, (SUB, width), 1)
         sublane = lax.broadcasted_iota(jnp.int32, (SUB, width), 0)
         down = [None] * 4
-        for c, here in enumerate(chunks):
-            tile = pair_chunk([spread[a, k, here, :] for k in range(4)], other)
+        for c, (tile,) in tile_chunks(own_of, [other], chunks):
             tile = jnp.where(lane == sublane + c * SUB, 0.0, tile)
-            tiles[at, here, :] = tile
+            tiles[at, chunks[c], :] = tile
             gather(down, c, tile)
         self_ref[pl.ds(pl.multiple_of(a * SUB, SUB), SUB), :] = tree(down)
         return at + 1
@@ -329,16 +345,16 @@
         count, place_of = outer_range(plan, table, a)
         work[a] = rows_ref[a]
 
+        def own_of(here):
+            return [spread[a, k, here, :] for k in range(4)]
+
         def pairs(places, at):
             others = [[wide(hood[k, pl.ds(base + share + n, 1), :]) for k in range(4)] for n in places]
-            for here in chunks:
-                own = [spread[a, k, here, :] for k in range(4)]
-                found = []
-                for t, other in enumerate(others):
-                    tile = pair_chunk(own, other)
+            for c, found in tile_chunks(own_of, others, chunks):
+                here = chunks[c]
+                for t, tile in enumerate(found):
                     tiles[at + t, here, :] = tile
-                    found.append(tile)
-                work[a, here, :] = work[a, here, :] + tree(found)
+                work[a, here, :] = work[a, here, :] + tree(list(found))
             return at + len(places)
 
         return sweep(count, place_of, pairs, at)

time: 76.8 us -> 78.2 us (1.018)
  Pallas kernels: 35.7 us -> 36.5 us
    ppermute x10, starting transfers between devices: 10.7 us -> 13.2 us  [swap(): lax.ppermute(values, axis, [(i, i ^ step) for i in range(lax.axis_size(ax...]
    ppermute x8, waiting for transfers between devices: 0.73 us -> 2.98 us  [exchange(): return [lax.ppermute(field, axes, list(enumerate(to))) for to in swaps]]
    ppermute x8, starting transfers between devices: 14.3 us -> 12.2 us  [exchange(): return [lax.ppermute(field, axes, list(enumerate(to))) for to in swaps]]
    ppermute x10, waiting for transfers between devices: 5.82 us -> 3.96 us  [swap(): lax.ppermute(values, axis, [(i, i ^ step) for i in range(lax.axis_size(ax...]
where the time goes in v7:
time: 78.2 us; the launch traced here: 78 us
  Pallas kernels  36.5 us (47%)
  starting transfers between devices  33.8 us (43%)
  waiting for transfers between devices  6.95 us (9%)
    pallas_call x8, Pallas kernels, call(): pl.pallas_call(kernel, out_shape=outs, in_specs=[SMEM] * scalars + [HBM]...  36.5 us
    ppermute x10, starting transfers between devices, swap(): lax.ppermute(values, axis, [(i, i ^ step) for i in range(lax.axis_size(ax...  13.2 us
    ppermute x8, starting transfers between devices, exchange(): return [lax.ppermute(field, axes, list(enumerate(to))) for to in swaps]  12.2 us
    ppermute x3, starting transfers between devices, body(): lax.ppermute(t, 'col', [(i, i ^ k) for i in range(columns)])  4.39 us
    ppermute x10, waiting for transfers between devices, swap(): lax.ppermute(values, axis, [(i, i ^ step) for i in range(lax.axis_size(ax...  3.96 us
    ppermute x1, starting transfers between devices, body(): lax.ppermute(second, 'piece', [(i, ((i ^ 1) + (1 if i % 2 else -1) * 2) %...  3.56 us
    ppermute x8, waiting for transfers between devices, exchange(): return [lax.ppermute(field, axes, list(enumerate(to))) for to in swaps]  2.98 us
  transfers between devices with their start and end apart: 23, of which 6 were waited for; matrix products, arithmetic and copies ran while one was open for 0% of the time, Pallas kernels for 29%

profile of v7, /device:TPU:0, one launch (start us, length us, event | category | flops | bytes accessed | tf_op | source)
XLA Modules:
  0.0 78.0 jit_solution(2547851074504739120)
XLA Ops:
  0.6 1.8 %prepare.1 = (s32[8]{0:T(128)S(4)}, s32[1472]{0:T(1024)S(4)}, f32[4,192,128]{2,1,0:T(8,128)S(1)}, f32[4,64,128]{2,1,0:T(8,128)S(1)}, f32[32,128]{1,0:T(8,128)S(1...) custom-call(s32[8]{0:T(128)} %counts.1, ...), custom_call_target="tpu_custom_call" | custom-call | tf_op jit(solution)/shard_map/prepare/pallas_call | solution.py:572
  2.5 0.5 collective-permute-start
  3.0 3.6 %collective-permute-start.1 = (f32[4,32,128]{2,1,0:T(8,128)S(1)}, f32[4,32,128]{2,1,0:T(8,128)S(1)}, u32[]{:S(2)}, u32[]{:S(2)}) collective-permute-start(f32[4,32,128]{2,1,0:T(8,128)S(1)} %get-tuple-element.41), channel_id=1, source_target_pairs={{0,28},{4,8},{8,4},{12,16},{16,12},{20,24},{24,20},{28,0},{1,29},{... | collective-permute-start | bytes 196616 | tf_op jit(solution)/shard_map/ppermute | solution.py:601
  6.6 1.6 %collective-permute-start.2 = (f32[32,128]{1,0:T(8,128)S(1)}, f32[32,128]{1,0:T(8,128)S(1)}, u32[]{:S(2)}, u32[]{:S(2)}) collective-permute-start(f32[32,128]{1,0:T(8,128)S(1)} %get-tuple-element.49), channel_id=1, source_target_pairs={{0,1},{1,0},{2,3},{3,2},{4,5},{5,4},{6,7},{7,6},{8,9},{9,8},{10,11... | collective-permute-start | bytes 49160 | tf_op jit(solution)/shard_map/ppermute | solution.py:602
  8.1 2.6 %collective-permute-start.3 = (f32[32,128]{1,0:T(8,128)S(1)}, f32[32,128]{1,0:T(8,128)S(1)}, u32[]{:S(2)}, u32[]{:S(2)}) collective-permute-start(f32[32,128]{1,0:T(8,128)S(1)} %get-tuple-element.50), channel_id=1, source_target_pairs={{0,2},{1,3},{2,0},{3,1},{4,6},{5,7},{6,4},{7,5},{8,10},{9,11},{10,... | collective-permute-start | bytes 49160 | tf_op jit(solution)/shard_map/ppermute | solution.py:602
  10.7 0.2 collective-permute-start.4
  10.9 13.6 %build_inner.1 = (s32[192]{0:T(256)S(4)}, f32[220,128,128]{2,1,0:T(8,128)S(1)}, f32[32,4,128,128]{3,2,1,0:T(8,128)S(1)}, f32[32,128,128]{2,1,0:T(8,128)S(1)}, f3...) custom-call(s32[8]{0:T(128)S(4)} %get-tuple-element.35.meta, s32[1472]{0:T(1024)S(4)} %get-tuple-element.36.table, ...), custom_call_target="tpu_custom_call" | custom-call | flops 56623104 | tf_op jit(solution)/shard_map/build_inner/pallas_call | solution.py:572
  24.6 0.0 collective-permute-done.2.rest_1_
  24.6 0.0 collective-permute-done.3.rest_2_
  24.6 0.0 collective-permute-done.4.rest_3_
  24.6 0.0 collective-permute-done.first
  24.6 0.0 collective-permute-done.1.second
  24.6 6.6 %build_outer.1 = (s32[1]{0:T(128)S(4)}, f32[226,128,128]{2,1,0:T(8,128)S(1)}, f32[32,128]{1,0:T(8,128)S(1)}, f32[32,128]{1,0:T(8,128)S(1)}, f32[32,128]{1,0:T(8,128)S(1)}, /*index=5*/f32[32,128]{1,0:T(8,128)S(1)}) custom-call(s32[8]{0:T(128)S(4)} %get-tuple-element.35.meta, s32[1472]{0:T(1024)S(4)} %get-tuple-element.36.table, ...), custom_call_target="tpu_custom_call" | custom-call | flops 58195968 | tf_op jit(solution)/shard_map/build_outer/pallas_call | solution.py:572
  31.3 5.5 %collective-permute-start.8 = (f32[32,128]{1,0:T(8,128)S(1)}, f32[32,128]{1,0:T(8,128)S(1)}, u32[]{:S(2)}, u32[]{:S(2)}) collective-permute-start(f32[32,128]{1,0:T(8,128)S(1)} %get-tuple-element.52.field.precond), channel_id=1, source_target_pairs={{0,1},{1,3},{2,4},{3,0},{4,2},{5,7},{6,8},{7,5},{8,6},{9,11},{10,1... | collective-permute-start | bytes 49160 | tf_op jit(solution)/shard_map/ppermute | solution.py:649
  36.8 0.2 collective-permute-start.7
  37.0 1.2 %collective-permute-start.6 = (f32[32,128]{1,0:T(8,128)S(1)}, f32[32,128]{1,0:T(8,128)S(1)}, u32[]{:S(2)}, u32[]{:S(2)}) collective-permute-start(f32[32,128]{1,0:T(8,128)S(1)} %get-tuple-element.52.field.precond), channel_id=1, source_target_pairs={{0,31},{1,2},{2,1},{3,4},{4,3},{5,6},{6,5},{7,8},{8,7},{9,10},{10,... | collective-permute-start | bytes 49160 | tf_op jit(solution)/shard_map/ppermute | solution.py:649
  38.2 0.0 collective-permute-start.5
  38.2 4.4 %apply_inner.2 = (f32[32,128,128]{2,1,0:T(8,128)S(1)}, f32[256,128]{1,0:T(8,128)S(1)}) custom-call(s32[8]{0:T(128)S(4)} %get-tuple-element.35.meta, s32[1472]{0:T(1024)S(4)} %get-tuple-element.36.table, s32[192]{0:T(256)S(4)} %get-tuple-element.38.plan, s32[1]{0:T(128)S(4)} %get-tuple-element.53.again, f32[32,128]{1,0:T(8,128)S(1)} %get-tuple-element.52.field.precond, ...), custom_call_target="tpu_custom_call" | custom-call | flops 14155776 | tf_op jit(solution)/shard_map/apply_inner/pallas_call | solution.py:572
  42.5 0.0 collective-permute-done.8.rest_3_
  42.6 0.0 collective-permute-done.7.rest_2_
  42.6 1.2 %collective-permute-done.6.rest_1_ = f32[32,128]{1,0:T(8,128)S(1)} collective-permute-done((f32[32,128]{1,0:T(8,128)S(1)}, f32[32,128]{1,0:T(8,128)S(1)}, u32[]{:S(2)}, u32[]{:S(2)}) %collective-permute-start.6) | collective-permute-done | bytes 16416 | tf_op jit(solution)/shard_map/ppermute | solution.py:649
  43.7 0.0 collective-permute-done.5.rest_0_
  43.7 2.3 %apply_first.1 = (f32[32,128]{1,0:T(8,128)S(1)}, f32[32,128]{1,0:T(8,128)S(1)}) custom-call(s32[8]{0:T(128)S(4)} %get-tuple-element.35.meta, s32[1472]{0:T(1024)S(4)} %get-tuple-element.36.table, s32[192]{0:T(256)S(4)} %get-tuple-element.38.plan, s32[1]{0:T(128)S(4)} %get-tuple-element.53.again, f32[32,128]{1,0:T(8,128)S(1)} %get-tuple-element.54.diagonal, ...), custom_call_target="tpu_custom_call" | custom-call | flops 7274496 | tf_op jit(solution)/shard_map/apply_first/pallas_call | solution.py:572
  46.0 1.7 %collective-permute-start.12 = (f32[32,128]{1,0:T(8,128)S(1)}, f32[32,128]{1,0:T(8,128)S(1)}, u32[]{:S(2)}, u32[]{:S(2)}) collective-permute-start(f32[32,128]{1,0:T(8,128)S(1)} %get-tuple-element.61.field.scaled), channel_id=1, source_target_pairs={{0,1},{1,3},{2,4},{3,0},{4,2},{5,7},{6,8},{7,5},{8,6},{9,11},{10,1... | collective-permute-start | bytes 49160 | tf_op jit(solution)/shard_map/ppermute | solution.py:649
  47.7 3.0 %collective-permute-start.11 = (f32[32,128]{1,0:T(8,128)S(1)}, f32[32,128]{1,0:T(8,128)S(1)}, u32[]{:S(2)}, u32[]{:S(2)}) collective-permute-start(f32[32,128]{1,0:T(8,128)S(1)} %get-tuple-element.61.field.scaled), channel_id=1, source_target_pairs={{0,2},{1,4},{2,3},{3,0},{4,1},{5,8},{6,7},{7,6},{8,5},{9,12},{10,1... | collective-permute-start | bytes 49160 | tf_op jit(solution)/shard_map/ppermute | solution.py:649
  50.8 0.0 collective-permute-start.10
  50.8 0.5 collective-permute-start.9
  51.3 4.4 %apply_inner.3 = (f32[32,128,128]{2,1,0:T(8,128)S(1)}, f32[256,128]{1,0:T(8,128)S(1)}) custom-call(s32[8]{0:T(128)S(4)} %get-tuple-element.35.meta, s32[1472]{0:T(1024)S(4)} %get-tuple-element.36.table, s32[192]{0:T(256)S(4)} %get-tuple-element.38.plan, s32[1]{0:T(128)S(4)} %get-tuple-element.53.again, f32[32,128]{1,0:T(8,128)S(1)} %get-tuple-element.61.field.scaled, ...), custom_call_target="tpu_custom_call" | custom-call | flops 14155776 | tf_op jit(solution)/shard_map/apply_inner/pallas_call | solution.py:572
  55.7 0.0 collective-permute-done.12.rest_3_
  55.7 0.0 collective-permute-done.11.rest_2_
  55.7 1.8 %collective-permute-done.10.rest_1_ = f32[32,128]{1,0:T(8,128)S(1)} collective-permute-done((f32[32,128]{1,0:T(8,128)S(1)}, f32[32,128]{1,0:T(8,128)S(1)}, u32[]{:S(2)}, u32[]{:S(2)}) %collective-permute-start.10) | collective-permute-done | bytes 16416 | tf_op jit(solution)/shard_map/ppermute | solution.py:649
  57.5 0.0 collective-permute-done.9.rest_0_
  57.5 2.4 %apply_second.1 = (f32[32,128]{1,0:T(8,128)S(1)}, f32[8,128]{1,0:T(8,128)S(1)}) custom-call(s32[8]{0:T(128)S(4)} %get-tuple-element.35.meta, s32[1472]{0:T(1024)S(4)} %get-tuple-element.36.table, s32[192]{0:T(256)S(4)} %get-tuple-element.38.plan, s32[1]{0:T(128)S(4)} %get-tuple-element.53.again, f32[32,128]{1,0:T(8,128)S(1)} %get-tuple-element.34.source, ...), custom_call_target="tpu_custom_call" | custom-call | flops 7274496 | tf_op jit(solution)/shard_map/apply_second/pallas_call | solution.py:572
  59.9 0.0 collective-permute-start.15
  59.9 1.9 %collective-permute-start.14 = (f32[8,128]{1,0:T(8,128)S(1)}, f32[8,128]{1,0:T(8,128)S(1)}, u32[]{:S(2)}, u32[]{:S(2)}) collective-permute-start(f32[8,128]{1,0:T(8,128)S(1)} %get-tuple-element.65), channel_id=1, source_target_pairs={{0,2},{1,3},{2,0},{3,1},{4,6},{5,7},{6,4},{7,5},{8,10},{9,11},{10,... | collective-permute-start | bytes 12296 | tf_op jit(solution)/shard_map/ppermute | solution.py:676
  61.9 2.5 %collective-permute-start.13 = (f32[8,128]{1,0:T(8,128)S(1)}, f32[8,128]{1,0:T(8,128)S(1)}, u32[]{:S(2)}, u32[]{:S(2)}) collective-permute-start(f32[8,128]{1,0:T(8,128)S(1)} %get-tuple-element.65), channel_id=1, source_target_pairs={{0,1},{1,0},{2,3},{3,2},{4,5},{5,4},{6,7},{7,6},{8,9},{9,8},{10,11... | collective-permute-start | bytes 12296 | tf_op jit(solution)/shard_map/ppermute | solution.py:676
  64.3 1.0 %collective-permute-done.15 = f32[8,128]{1,0:T(8,128)S(1)} collective-permute-done((f32[8,128]{1,0:T(8,128)S(1)}, f32[8,128]{1,0:T(8,128)S(1)}, u32[]{:S(2)}, u32[]{:S(2)}) %collective-permute-start.15) | collective-permute-done | bytes 4128 | tf_op jit(solution)/shard_map/ppermute | solution.py:676
  65.3 0.0 collective-permute-done.14
  65.3 0.6 collective-permute-done.13
  65.9 0.3 collective-permute-start.22
  66.2 2.5 %collective-permute-start.21 = (f32[8,128]{1,0:T(8,128)S(1)}, f32[8,128]{1,0:T(8,128)S(1)}, u32[]{:S(2)}, u32[]{:S(2)}) collective-permute-start(f32[8,128]{1,0:T(8,128)S(1)} %add_add_fusion.rest_0_), channel_id=1, source_target_pairs={{0,24},{4,28},{8,16},{12,20},{16,8},{20,12},{24,0},{28,4},{1,25},{... | collective-permute-start | bytes 12296 | tf_op jit(solution)/shard_map/ppermute | solution.py:676
  68.8 4.1 %collective-permute-start.20 = (f32[8,128]{1,0:T(8,128)S(1)}, f32[8,128]{1,0:T(8,128)S(1)}, u32[]{:S(2)}, u32[]{:S(2)}) collective-permute-start(f32[8,128]{1,0:T(8,128)S(1)} %add_add_fusion.rest_0_), channel_id=1, source_target_pairs={{0,20},{4,16},{8,28},{12,24},{16,4},{20,0},{24,12},{28,8},{1,21},{... | collective-permute-start | bytes 12296 | tf_op jit(solution)/shard_map/ppermute | solution.py:676
  72.8 0.0 collective-permute-start.19
  72.8 0.6 collective-permute-start.18
  73.5 0.0 collective-permute-done.22.rest_7_
  73.5 1.2 %collective-permute-start.17 = (f32[8,128]{1,0:T(8,128)S(1)}, f32[8,128]{1,0:T(8,128)S(1)}, u32[]{:S(2)}, u32[]{:S(2)}) collective-permute-start(f32[8,128]{1,0:T(8,128)S(1)} %add_add_fusion.rest_0_), channel_id=1, source_target_pairs={{0,8},{4,12},{8,0},{12,4},{16,24},{20,28},{24,16},{28,20},{1,9},{5... | collective-permute-start | bytes 12296 | tf_op jit(solution)/shard_map/ppermute | solution.py:676
  74.6 0.0 collective-permute-done.21.rest_6_
  74.6 0.1 collective-permute-start.16
  74.7 0.0 collective-permute-done.20.rest_5_
  74.7 1.7 %collective-permute-done.19.rest_4_ = f32[8,128]{1,0:T(8,128)S(1)} collective-permute-done((f32[8,128]{1,0:T(8,128)S(1)}, f32[8,128]{1,0:T(8,128)S(1)}, u32[]{:S(2)}, u32[]{:S(2)}) %collective-permute-start.19) | collective-permute-done | bytes 4128 | tf_op jit(solution)/shard_map/ppermute | solution.py:676
  76.4 0.0 collective-permute-done.18.rest_3_
  76.4 0.6 collective-permute-done.17.rest_2_
  77.1 0.0 collective-permute-done.16.rest_1_
  77.1 0.9 %finish.1 = (f32[32,128]{1,0:T(8,128)}, f32[32,128]{1,0:T(8,128)}) custom-call(f32[32,128]{1,0:T(8,128)S(1)} %get-tuple-element.34.source, f32[32,128]{1,0:T(8,128)S(1)} %get-tuple-element.52.field.precond, f32[32,128]{1,0:T(8,128)S(1)} %get-tuple-element.60.spill, f32[32,128]{1,0:T(8,128)S(1)} %get-tuple-element.61.field.scaled, ...), custom_call_target="tpu_custom_call" | custom-call | tf_op jit(solution)/shard_map/finish/pallas_call | solution.py:572
  (1 shorter events, 0.0 us)
Async XLA Ops:
  2.5 22.1 %collective-permute-start = (f32[4,32,128]{2,1,0:T(8,128)S(1)}, f32[4,32,128]{2,1,0:T(8,128)S(1)}, u32[]{:S(2)}, u32[]{:S(2)}) collective-permute-start(f32[4,32,128]{2,1,0:T(8,128)S(1)} %get-tuple-element.40), channel_id=1, source_target_pairs={{0,4},{4,0},{8,12},{12,8},{16,20},{20,16},{24,28},{28,24},{1,5},{5... | collective-permute-start | bytes 196616 | tf_op jit(solution)/shard_map/ppermute | solution.py:600
  3.0 21.6 %collective-permute-start.1 = (f32[4,32,128]{2,1,0:T(8,128)S(1)}, f32[4,32,128]{2,1,0:T(8,128)S(1)}, u32[]{:S(2)}, u32[]{:S(2)}) collective-permute-start(f32[4,32,128]{2,1,0:T(8,128)S(1)} %get-tuple-element.41), channel_id=1, source_target_pairs={{0,28},{4,8},{8,4},{12,16},{16,12},{20,24},{24,20},{28,0},{1,29},{... | collective-permute-start | bytes 196616 | tf_op jit(solution)/shard_map/ppermute | solution.py:601
  6.6 18.0 %collective-permute-start.2 = (f32[32,128]{1,0:T(8,128)S(1)}, f32[32,128]{1,0:T(8,128)S(1)}, u32[]{:S(2)}, u32[]{:S(2)}) collective-permute-start(f32[32,128]{1,0:T(8,128)S(1)} %get-tuple-element.49), channel_id=1, source_target_pairs={{0,1},{1,0},{2,3},{3,2},{4,5},{5,4},{6,7},{7,6},{8,9},{9,8},{10,11... | collective-permute-start | bytes 49160 | tf_op jit(solution)/shard_map/ppermute | solution.py:602
  8.1 16.5 %collective-permute-start.3 = (f32[32,128]{1,0:T(8,128)S(1)}, f32[32,128]{1,0:T(8,128)S(1)}, u32[]{:S(2)}, u32[]{:S(2)}) collective-permute-start(f32[32,128]{1,0:T(8,128)S(1)} %get-tuple-element.50), channel_id=1, source_target_pairs={{0,2},{1,3},{2,0},{3,1},{4,6},{5,7},{6,4},{7,5},{8,10},{9,11},{10,... | collective-permute-start | bytes 49160 | tf_op jit(solution)/shard_map/ppermute | solution.py:602
  10.7 13.9 %collective-permute-start.4 = (f32[32,128]{1,0:T(8,128)S(1)}, f32[32,128]{1,0:T(8,128)S(1)}, u32[]{:S(2)}, u32[]{:S(2)}) collective-permute-start(f32[32,128]{1,0:T(8,128)S(1)} %get-tuple-element.51), channel_id=1, source_target_pairs={{0,3},{1,2},{2,1},{3,0},{4,7},{5,6},{6,5},{7,4},{8,11},{9,10},{10,... | collective-permute-start | bytes 49160 | tf_op jit(solution)/shard_map/ppermute | solution.py:602
  31.3 11.3 %collective-permute-start.8 = (f32[32,128]{1,0:T(8,128)S(1)}, f32[32,128]{1,0:T(8,128)S(1)}, u32[]{:S(2)}, u32[]{:S(2)}) collective-permute-start(f32[32,128]{1,0:T(8,128)S(1)} %get-tuple-element.52.field.precond), channel_id=1, source_target_pairs={{0,1},{1,3},{2,4},{3,0},{4,2},{5,7},{6,8},{7,5},{8,6},{9,11},{10,1... | collective-permute-start | bytes 49160 | tf_op jit(solution)/shard_map/ppermute | solution.py:649
  36.8 5.8 %collective-permute-start.7 = (f32[32,128]{1,0:T(8,128)S(1)}, f32[32,128]{1,0:T(8,128)S(1)}, u32[]{:S(2)}, u32[]{:S(2)}) collective-permute-start(f32[32,128]{1,0:T(8,128)S(1)} %get-tuple-element.52.field.precond), channel_id=1, source_target_pairs={{0,2},{1,4},{2,3},{3,0},{4,1},{5,8},{6,7},{7,6},{8,5},{9,12},{10,1... | collective-permute-start | bytes 49160 | tf_op jit(solution)/shard_map/ppermute | solution.py:649
  37.0 6.8 %collective-permute-start.6 = (f32[32,128]{1,0:T(8,128)S(1)}, f32[32,128]{1,0:T(8,128)S(1)}, u32[]{:S(2)}, u32[]{:S(2)}) collective-permute-start(f32[32,128]{1,0:T(8,128)S(1)} %get-tuple-element.52.field.precond), channel_id=1, source_target_pairs={{0,31},{1,2},{2,1},{3,4},{4,3},{5,6},{6,5},{7,8},{8,7},{9,10},{10,... | collective-permute-start | bytes 49160 | tf_op jit(solution)/shard_map/ppermute | solution.py:649
  38.2 5.5 %collective-permute-start.5 = (f32[32,128]{1,0:T(8,128)S(1)}, f32[32,128]{1,0:T(8,128)S(1)}, u32[]{:S(2)}, u32[]{:S(2)}) collective-permute-start(f32[32,128]{1,0:T(8,128)S(1)} %get-tuple-element.52.field.precond), channel_id=1, source_target_pairs={{0,1},{1,0},{2,3},{3,2},{4,5},{5,4},{6,7},{7,6},{8,9},{9,8},{10,11... | collective-permute-start | bytes 49160 | tf_op jit(solution)/shard_map/ppermute | solution.py:649
  46.0 9.7 %collective-permute-start.12 = (f32[32,128]{1,0:T(8,128)S(1)}, f32[32,128]{1,0:T(8,128)S(1)}, u32[]{:S(2)}, u32[]{:S(2)}) collective-permute-start(f32[32,128]{1,0:T(8,128)S(1)} %get-tuple-element.61.field.scaled), channel_id=1, source_target_pairs={{0,1},{1,3},{2,4},{3,0},{4,2},{5,7},{6,8},{7,5},{8,6},{9,11},{10,1... | collective-permute-start | bytes 49160 | tf_op jit(solution)/shard_map/ppermute | solution.py:649
  47.7 8.0 %collective-permute-start.11 = (f32[32,128]{1,0:T(8,128)S(1)}, f32[32,128]{1,0:T(8,128)S(1)}, u32[]{:S(2)}, u32[]{:S(2)}) collective-permute-start(f32[32,128]{1,0:T(8,128)S(1)} %get-tuple-element.61.field.scaled), channel_id=1, source_target_pairs={{0,2},{1,4},{2,3},{3,0},{4,1},{5,8},{6,7},{7,6},{8,5},{9,12},{10,1... | collective-permute-start | bytes 49160 | tf_op jit(solution)/shard_map/ppermute | solution.py:649
  50.8 6.8 %collective-permute-start.10 = (f32[32,128]{1,0:T(8,128)S(1)}, f32[32,128]{1,0:T(8,128)S(1)}, u32[]{:S(2)}, u32[]{:S(2)}) collective-permute-start(f32[32,128]{1,0:T(8,128)S(1)} %get-tuple-element.61.field.scaled), channel_id=1, source_target_pairs={{0,31},{1,2},{2,1},{3,4},{4,3},{5,6},{6,5},{7,8},{8,7},{9,10},{10,... | collective-permute-start | bytes 49160 | tf_op jit(solution)/shard_map/ppermute | solution.py:649
  50.8 6.7 %collective-permute-start.9 = (f32[32,128]{1,0:T(8,128)S(1)}, f32[32,128]{1,0:T(8,128)S(1)}, u32[]{:S(2)}, u32[]{:S(2)}) collective-permute-start(f32[32,128]{1,0:T(8,128)S(1)} %get-tuple-element.61.field.scaled), channel_id=1, source_target_pairs={{0,1},{1,0},{2,3},{3,2},{4,5},{5,4},{6,7},{7,6},{8,9},{9,8},{10,11... | collective-permute-start | bytes 49160 | tf_op jit(solution)/shard_map/ppermute | solution.py:649
  59.9 5.4 %collective-permute-start.15 = (f32[8,128]{1,0:T(8,128)S(1)}, f32[8,128]{1,0:T(8,128)S(1)}, u32[]{:S(2)}, u32[]{:S(2)}) collective-permute-start(f32[8,128]{1,0:T(8,128)S(1)} %get-tuple-element.65), channel_id=1, source_target_pairs={{0,3},{1,2},{2,1},{3,0},{4,7},{5,6},{6,5},{7,4},{8,11},{9,10},{10,... | collective-permute-start | bytes 12296 | tf_op jit(solution)/shard_map/ppermute | solution.py:676
  59.9 5.4 %collective-permute-start.14 = (f32[8,128]{1,0:T(8,128)S(1)}, f32[8,128]{1,0:T(8,128)S(1)}, u32[]{:S(2)}, u32[]{:S(2)}) collective-permute-start(f32[8,128]{1,0:T(8,128)S(1)} %get-tuple-element.65), channel_id=1, source_target_pairs={{0,2},{1,3},{2,0},{3,1},{4,6},{5,7},{6,4},{7,5},{8,10},{9,11},{10,... | collective-permute-start | bytes 12296 | tf_op jit(solution)/shard_map/ppermute | solution.py:676
  61.9 4.0 %collective-permute-start.13 = (f32[8,128]{1,0:T(8,128)S(1)}, f32[8,128]{1,0:T(8,128)S(1)}, u32[]{:S(2)}, u32[]{:S(2)}) collective-permute-start(f32[8,128]{1,0:T(8,128)S(1)} %get-tuple-element.65), channel_id=1, source_target_pairs={{0,1},{1,0},{2,3},{3,2},{4,5},{5,4},{6,7},{7,6},{8,9},{9,8},{10,11... | collective-permute-start | bytes 12296 | tf_op jit(solution)/shard_map/ppermute | solution.py:676
  65.9 7.6 %collective-permute-start.22 = (f32[8,128]{1,0:T(8,128)S(1)}, f32[8,128]{1,0:T(8,128)S(1)}, u32[]{:S(2)}, u32[]{:S(2)}) collective-permute-start(f32[8,128]{1,0:T(8,128)S(1)} %add_add_fusion.rest_0_), channel_id=1, source_target_pairs={{0,28},{4,24},{8,20},{12,16},{16,12},{20,8},{24,4},{28,0},{1,29},{... | collective-permute-start | bytes 12296 | tf_op jit(solution)/shard_map/ppermute | solution.py:676
  66.2 8.4 %collective-permute-start.21 = (f32[8,128]{1,0:T(8,128)S(1)}, f32[8,128]{1,0:T(8,128)S(1)}, u32[]{:S(2)}, u32[]{:S(2)}) collective-permute-start(f32[8,128]{1,0:T(8,128)S(1)} %add_add_fusion.rest_0_), channel_id=1, source_target_pairs={{0,24},{4,28},{8,16},{12,20},{16,8},{20,12},{24,0},{28,4},{1,25},{... | collective-permute-start | bytes 12296 | tf_op jit(solution)/shard_map/ppermute | solution.py:676
  68.8 5.9 %collective-permute-start.20 = (f32[8,128]{1,0:T(8,128)S(1)}, f32[8,128]{1,0:T(8,128)S(1)}, u32[]{:S(2)}, u32[]{:S(2)}) collective-permute-start(f32[8,128]{1,0:T(8,128)S(1)} %add_add_fusion.rest_0_), channel_id=1, source_target_pairs={{0,20},{4,16},{8,28},{12,24},{16,4},{20,0},{24,12},{28,8},{1,21},{... | collective-permute-start | bytes 12296 | tf_op jit(solution)/shard_map/ppermute | solution.py:676
  72.8 3.6 %collective-permute-start.19 = (f32[8,128]{1,0:T(8,128)S(1)}, f32[8,128]{1,0:T(8,128)S(1)}, u32[]{:S(2)}, u32[]{:S(2)}) collective-permute-start(f32[8,128]{1,0:T(8,128)S(1)} %add_add_fusion.rest_0_), channel_id=1, source_target_pairs={{0,16},{4,20},{8,24},{12,28},{16,0},{20,4},{24,8},{28,12},{1,17},{... | collective-permute-start | bytes 12296 | tf_op jit(solution)/shard_map/ppermute | solution.py:676
  72.8 3.6 %collective-permute-start.18 = (f32[8,128]{1,0:T(8,128)S(1)}, f32[8,128]{1,0:T(8,128)S(1)}, u32[]{:S(2)}, u32[]{:S(2)}) collective-permute-start(f32[8,128]{1,0:T(8,128)S(1)} %add_add_fusion.rest_0_), channel_id=1, source_target_pairs={{0,12},{4,8},{8,4},{12,0},{16,28},{20,24},{24,20},{28,16},{1,13},{... | collective-permute-start | bytes 12296 | tf_op jit(solution)/shard_map/ppermute | solution.py:676
  73.5 3.6 %collective-permute-start.17 = (f32[8,128]{1,0:T(8,128)S(1)}, f32[8,128]{1,0:T(8,128)S(1)}, u32[]{:S(2)}, u32[]{:S(2)}) collective-permute-start(f32[8,128]{1,0:T(8,128)S(1)} %add_add_fusion.rest_0_), channel_id=1, source_target_pairs={{0,8},{4,12},{8,0},{12,4},{16,24},{20,28},{24,16},{28,20},{1,9},{5... | collective-permute-start | bytes 12296 | tf_op jit(solution)/shard_map/ppermute | solution.py:676
  74.6 2.4 %collective-permute-start.16 = (f32[8,128]{1,0:T(8,128)S(1)}, f32[8,128]{1,0:T(8,128)S(1)}, u32[]{:S(2)}, u32[]{:S(2)}) collective-permute-start(f32[8,128]{1,0:T(8,128)S(1)} %add_add_fusion.rest_0_), channel_id=1, source_target_pairs={{0,4},{4,0},{8,12},{12,8},{16,20},{20,16},{24,28},{28,24},{1,5},{5... | collective-permute-start | bytes 12296 | tf_op jit(solution)/shard_map/ppermute | solution.py:676

commit v8 on v6

--- a/solution.py
+++ b/solution.py
@@ -51,7 +51,8 @@
 WIDEST = OFFSETS.shape[1]
 TABLE = np.concatenate([OFFSETS, BELOW], 1)
 STRIDE = TABLE.shape[1]
-LIMIT = pltpu.CompilerParams(vmem_limit_bytes=6 * 1024 * 1024)
+FLAT = np.concatenate([TABLE.reshape(-1), np.zeros(8, np.int32)])
+LIMIT = pltpu.CompilerParams(vmem_limit_bytes=8 * 1024 * 1024)
 
 
 def tile_bounds(share):
@@ -90,6 +91,30 @@
     plan[a * FIELDS + 5] = row + resume - ahead
 
 
+def write_run(runs, at, a, start, count):
+    runs[3 * at], runs[3 * at + 1], runs[3 * at + 2] = a, start, count
+    return at + (count > 0).astype(jnp.int32)
+
+
+def write_runs(meta, table, plan, inner_runs, outer_runs, share):
+    inner = outer = total = far = jnp.int32(0)
+    for a in range(share):
+        write_plan(meta, table, plan, a)
+        alive = a < meta[0]
+        count, start, count_far, ahead, start_far, start_after = (plan[a * FIELDS + k] for k in range(FIELDS))
+        inner = write_run(inner_runs, inner, a, start, jnp.where(alive, count + 1, 0))
+        outer = write_run(outer_runs, outer, a, start_far, jnp.where(alive, ahead, 0))
+        outer = write_run(outer_runs, outer, a, start_after + ahead, jnp.where(alive, count_far - ahead, 0))
+        total = total + jnp.where(alive, count + 1, 0)
+        far = far + jnp.where(alive, count_far, 0)
+    for runs, at in ((inner_runs, inner), (outer_runs, outer)):
+        write_run(runs, at, share, len(FLAT) - 8, jnp.int32(1))
+    plan[share * FIELDS] = total
+    plan[share * FIELDS + 1] = far
+    plan[share * FIELDS + 2] = inner
+    plan[share * FIELDS + 3] = outer
+
+
 def inner_range(plan, table, a):
     start = plan[a * FIELDS + 1]
     return plan[a * FIELDS], lambda t: a + table[start + t]
@@ -98,16 +123,6 @@
 def outer_range(plan, table, a):
     ahead, start, start_after = (plan[a * FIELDS + k] for k in (3, 4, 5))
     return plan[a * FIELDS + 2], lambda t: a + table[t + jnp.where(t < ahead, start, start_after)]
-
-
-def sweep(count, place_of, step, carry):
-    def both(i, state):
-        carry, *now = state
-        later = place_of(2 * i + 2), place_of(2 * i + 3)
-        return step(now, carry), *later
-
-    carry, first, _ = lax.fori_loop(0, lax.div(count, 2), both, (carry, place_of(0), place_of(1)))
-    return lax.fori_loop(0, lax.rem(count, 2), lambda _, carry: step([first], carry), carry)
 
 
 TURN = 4
@@ -144,13 +159,92 @@
     return jnp.broadcast_to(row, (SUB, row.shape[1]))
 
 
-def pair_chunk(own, other):
-    dx = own[0] - other[0]
-    dy = own[1] - other[1]
-    dz = own[2] - other[2]
-    squared = dx * dx + dy * dy + dz * dz
-    rest = jnp.maximum(1.0 - squared, 0.0)
-    return rest * rest * pltpu.reciprocal((squared + 0.01) * (own[3] + other[3]), approx=True)
+def three_parts(values):
+    high = values.astype(jnp.bfloat16).astype(jnp.float32)
+    rest = values - high
+    middle = rest.astype(jnp.bfloat16).astype(jnp.float32)
+    return high, middle, rest - middle
+
+
+def stacked(rows):
+    sublane = lax.broadcasted_iota(jnp.int32, rows[0].shape, 0)
+    result = jnp.zeros(rows[0].shape, jnp.float32)
+    for k, row in enumerate(rows):
+        result = jnp.where(sublane == k, row, result)
+    return result
+
+
+def own_side(x):
+    size = x[0] * x[0] + x[1] * x[1] + x[2] * x[2]
+    one = jnp.ones_like(size)
+    high, middle, low = three_parts(stacked([2.0 * x[0], 2.0 * x[1], 2.0 * x[2], one, 0.5 - size]))
+    width = size.shape[1]
+    rest = jnp.zeros((width - 6 * SUB, width), jnp.float32)
+    return jnp.concatenate([high, high, middle, middle, high, low, rest], 0).T.astype(jnp.bfloat16)
+
+
+def other_side(y):
+    size = y[0] * y[0] + y[1] * y[1] + y[2] * y[2]
+    one = jnp.ones_like(size)
+    high, middle, low = three_parts(stacked([y[0], y[1], y[2], 0.5 - size, one]))
+    first = jnp.concatenate([high, middle], 0).astype(jnp.bfloat16)
+    last = jnp.concatenate([low, high], 0).astype(jnp.bfloat16)
+    width = size.shape[1]
+    rest = jnp.zeros((width - 6 * SUB, width), jnp.bfloat16)
+    return jnp.concatenate([first, first, last, rest], 0)
+
+
+GROUP = 6
+
+
+def flat_tiles(count, runs, most, table, sides, middles, weights, other_at, ahead, tiles, rows_ref, cols_ref):
+    share, width = rows_ref.shape[0] - 1, rows_ref.shape[2]
+    chunks = pieces_of(width)
+
+    def steps(state):
+        found = []
+        for _ in range(GROUP):
+            run, t = state
+            a, start, size = (runs[3 * run + k] for k in range(3))
+            found.append((a, a + table[start + t]))
+            over = t + 1 >= size
+            state = jnp.minimum(run + over.astype(jnp.int32), most), jnp.where(over, 0, t + 1)
+        return state, found
+
+    def products(found):
+        for k, (a, n) in enumerate(found):
+            here = pl.ds(jnp.minimum(a, share - 1), 1)
+            near = [wide(other_at(c, n)) - wide(middles[c, here, :]) for c in range(3)]
+            side = sides[jnp.minimum(a, share - 1)]
+            ahead[k] = jnp.dot(side, other_side(near), preferred_element_type=jnp.float32)
+
+    def turn(i, carry):
+        state, found = carry
+        state, later = steps(state)
+        for k, (a, n) in enumerate(found):
+            alone = a == n
+            row = jnp.where(alone, share, a)
+            own = jnp.minimum(a, share - 1)
+            other = wide(other_at(3, n))
+            down = [None] * 2
+            for c, here in enumerate(chunks):
+                left = ahead[k, here, :]
+                rest = jnp.maximum(left, 0.0)
+                inverse = pltpu.reciprocal((1.01 - left) * (weights[own, here, :] + other), approx=True)
+                tile = rest * rest * inverse
+                tiles[i * GROUP + k, here, :] = tile
+                rows_ref[row, here, :] = rows_ref[row, here, :] + tile
+                if cols_ref is not None:
+                    gather(down, c, tile)
+            if cols_ref is not None:
+                there = pl.ds(pl.multiple_of(jnp.where(alone, share, n) * SUB, SUB), SUB)
+                cols_ref[there, :] = cols_ref[there, :] + tree(down)
+        products(later)
+        return state, later
+
+    state, found = steps((jnp.int32(0), jnp.int32(0)))
+    products(found)
+    lax.fori_loop(0, lax.div(count + (GROUP - 1), GROUP), turn, (state, found))
 
 
 def spread_columns(out, index, rows):
@@ -241,53 +335,44 @@
         tiles[end + t] = jnp.zeros(tiles.shape[1:], jnp.float32)
 
 
-def build_inner(meta, table, near, plan, tiles, spread, rows_ref, cols_ref, self_ref):
-    share, width = rows_ref.shape[0], rows_ref.shape[2]
+def build_inner(
+    meta, table, near, plan, outer_runs, tiles, sides, middles, weights, rows_out, cols_out, self_ref,
+    inner_runs, rows_ref, cols_ref, ahead,
+):
+    share, width = rows_out.shape[0], rows_out.shape[2]
     chunks = pieces_of(width)
+    write_runs(meta, table, plan, inner_runs, outer_runs, share)
+    for k in range(3):
+        first = near[k, 0:share, 0:1]
+        middles[k] = jnp.broadcast_to(jnp.floor(first) + 0.5, (share, width))
     for a in range(share):
-        write_plan(meta, table, plan, a)
-    for k in range(4):
-        spread_columns(spread, lambda a: (a, k), near[k, 0:share, :])
+        here = slice(a, a + 1)
+        sides[a] = own_side([wide(near[k, here, :] - middles[k, here, :]) for k in range(3)])
+    spread_columns(weights, lambda a: a, near[3, 0:share, :])
     cols_ref[...] = jnp.zeros_like(cols_ref)
-
-    def rows_at(n):
-        return [wide(near[k, pl.ds(n, 1), :]) for k in range(4)]
+    rows_ref[...] = jnp.zeros_like(rows_ref)
+    count = plan[share * FIELDS]
+    flat_tiles(
+        count, inner_runs, plan[share * FIELDS + 2], table, sides, middles, weights,
+        lambda k, n: near[k, pl.ds(n, 1), :], ahead, tiles, rows_ref, cols_ref,
+    )
+    finish_tiles(tiles, count)
+    lane = lax.broadcasted_iota(jnp.int32, (SUB, width), 1)
+    sublane = lax.broadcasted_iota(jnp.int32, (SUB, width), 0)
 
     def block(a, at):
-        count, place_of = inner_range(plan, table, a)
-        rows_ref[a] = jnp.zeros((width, width), jnp.float32)
-
-        def pairs(places, at):
-            others = [rows_at(n) for n in places]
-            down = [[None] * 2 for _ in places]
-            for c, here in enumerate(chunks):
-                own = [spread[a, k, here, :] for k in range(4)]
-                found = []
-                for t, other in enumerate(others):
-                    tile = pair_chunk(own, other)
-                    tiles[at + t, here, :] = tile
-                    gather(down[t], c, tile)
-                    found.append(tile)
-                rows_ref[a, here, :] = rows_ref[a, here, :] + tree(found)
-            for n, partial in zip(places, down):
-                there = pl.ds(pl.multiple_of(n * SUB, SUB), SUB)
-                cols_ref[there, :] = cols_ref[there, :] + tree(partial)
-            return at + len(places)
-
-        at = sweep(count, place_of, pairs, at)
-        other = rows_at(a)
-        lane = lax.broadcasted_iota(jnp.int32, (SUB, width), 1)
-        sublane = lax.broadcasted_iota(jnp.int32, (SUB, width), 0)
+        at = at + plan[a * FIELDS]
         down = [None] * 4
         for c, here in enumerate(chunks):
-            tile = pair_chunk([spread[a, k, here, :] for k in range(4)], other)
-            tile = jnp.where(lane == sublane + c * SUB, 0.0, tile)
+            tile = jnp.where(lane == sublane + c * SUB, 0.0, tiles[at, here, :])
             tiles[at, here, :] = tile
             gather(down, c, tile)
         self_ref[pl.ds(pl.multiple_of(a * SUB, SUB), SUB), :] = tree(down)
         return at + 1
 
-    finish_tiles(tiles, lax.fori_loop(0, meta[0], block, 0))
+    lax.fori_loop(0, meta[0], block, 0)
+    rows_out[...] = rows_ref[0:share]
+    cols_out[...] = cols_ref[0 : share * SUB, :]
 
 
 def factor(times, a, n):
@@ -306,11 +391,11 @@
 
 
 def build_outer(
-    meta, table, plan, around, first, second, density, source, tiles_in, spread, rows_ref, cols_ref, self_ref, *rest
+    meta, table, plan, runs, around, first, second, density, source, tiles_in, sides, middles, weights,
+    rows_ref, cols_ref, self_ref, *rest
 ):
-    *times_in, again_ref, tiles, diagonal_ref, precond_ref, times, alone_ref, hood, work, sums_ref, extra = rest
+    *times_in, again_ref, tiles, diagonal_ref, precond_ref, times, alone_ref, hood, work, sums_ref, extra, ahead = rest
     share, width = diagonal_ref.shape
-    chunks = pieces_of(width)
     base, filled = meta[3], meta[4]
     even = lax.rem(lax.axis_index("piece"), 2) == 0
     for k in range(4):
@@ -325,26 +410,14 @@
     again_ref[0] = again.astype(jnp.int32)
 
 
-    def block(a, at):
-        count, place_of = outer_range(plan, table, a)
-        work[a] = rows_ref[a]
-
-        def pairs(places, at):
-            others = [[wide(hood[k, pl.ds(base + share + n, 1), :]) for k in range(4)] for n in places]
-            for here in chunks:
-                own = [spread[a, k, here, :] for k in range(4)]
-                found = []
-                for t, other in enumerate(others):
-                    tile = pair_chunk(own, other)
-                    tiles[at + t, here, :] = tile
-                    found.append(tile)
-                work[a, here, :] = work[a, here, :] + tree(found)
-            return at + len(places)
-
-        return sweep(count, place_of, pairs, at)
-
-    finish_tiles(tiles, lax.fori_loop(0, meta[0], block, 0))
-    sums_ref[...] = lane_sums(work, share, width) + sub_sums(cols_ref)
+    work[...] = jnp.zeros_like(work)
+    count = plan[share * FIELDS + 1]
+    flat_tiles(
+        count, runs, plan[share * FIELDS + 3], table, sides, middles, weights,
+        lambda k, n: hood[k, pl.ds(base + share + n, 1), :], ahead, tiles, work, None,
+    )
+    finish_tiles(tiles, count)
+    sums_ref[...] = lane_sums([rows_ref[a] + work[a] for a in range(share)], share, width) + sub_sums(cols_ref)
 
     @pl.when(again)
     def _():
@@ -546,11 +619,13 @@
     few = jax.ShapeDtypeStruct((SUB, width), f32)
     message = jax.ShapeDtypeStruct((4, share, width), f32)
     most_inner, most_outer = tile_bounds(share)
-    inner_tiles = pltpu.VMEM((most_inner + TURN, width, width), f32)
-    outer_tiles = pltpu.VMEM((most_outer + TURN, width, width), f32)
+    inner_tiles = pltpu.VMEM((most_inner + GROUP, width, width), f32)
+    outer_tiles = pltpu.VMEM((most_outer + GROUP, width, width), f32)
+    ahead = pltpu.VMEM((GROUP, width, width), f32)
+    square_more = pltpu.VMEM((share + 1, width, width), f32)
     square = pltpu.VMEM((share, width, width), f32)
     narrow = pltpu.VMEM((share * SUB, width), f32)
-    table = jnp.asarray(TABLE.reshape(-1))
+    table = jnp.asarray(FLAT)
 
     def call(kernel, args, outs, scratch=(), work=0, scalars=2, far=0, **more):
         return pl.pallas_call(
@@ -585,23 +660,24 @@
     second = lax.ppermute(second, "piece", [(i, ((i ^ 1) + (1 if i % 2 else -1) * 2) % pieces) for i in range(pieces)])
     times = [lax.ppermute(t, "col", [(i, i ^ k) for i in range(columns)]) if k else t for k, t in enumerate(times)]
 
-    plan, tiles_in, spread, rows, cols, selfs = call(
+    plan, runs, tiles_in, sides, middles, weights, rows, cols, selfs = call(
         build_inner,
         (meta, table, near),
-        [pltpu.SMEM((share * FIELDS,), jnp.int32), inner_tiles, pltpu.VMEM((share, 4, width, width), f32),
-         square, narrow, narrow],
-        work=16 * most_inner,
-    )
-    plan = pltpu.with_memory_space_constraint(plan, pltpu.SMEM)
+        [pltpu.SMEM((share * FIELDS + 4,), jnp.int32), pltpu.SMEM((6 * share + 3,), jnp.int32), inner_tiles,
+         pltpu.VMEM((share, width, width), jnp.bfloat16), pltpu.VMEM((3, share, width), f32), square, square, narrow, narrow],
+        [pltpu.SMEM((3 * share + 3,), jnp.int32), square_more, pltpu.VMEM(((share + 1) * SUB, width), f32), ahead],
+        16 * most_inner,
+    )
+    plan, runs = (pltpu.with_memory_space_constraint(array, pltpu.SMEM) for array in (plan, runs))
     again, tiles_out, diagonal, precond, times, alone = call(
         build_outer,
-        (meta, table, plan, around, first, second, density, source,
-         held(tiles_in), held(spread), held(rows), held(cols), held(selfs), *times),
+        (meta, table, plan, runs, around, first, second, density, source,
+         held(tiles_in), held(sides), held(middles), held(weights), held(rows), held(cols), held(selfs), *times),
         [pltpu.SMEM((1,), jnp.int32), outer_tiles, vector, vector, vector, vector],
-        [pltpu.VMEM((4, capacity + 2 * share, width), f32), pltpu.VMEM((share, width, width), f32)]
-        + [pltpu.VMEM((share, width), f32)] * 2,
+        [pltpu.VMEM((4, capacity + 2 * share, width), f32), square_more]
+        + [pltpu.VMEM((share, width), f32)] * 2 + [ahead],
         16 * most_outer,
-        scalars=3,
+        scalars=4,
     )
     again = pltpu.with_memory_space_constraint(again, pltpu.SMEM)
 

time: 76.8 us -> 72.6 us (0.945)
  Pallas kernels: 35.7 us -> 31.9 us
    pallas_call x8, Pallas kernels: 35.7 us -> 31.9 us  [call(): pl.pallas_call(kernel, out_shape=outs, in_specs=[SMEM] * scalars + [HBM]...]
  transfers between devices with their start and end apart: 23 -> 23, of which waited for: 6 -> 6; matrix products, arithmetic and copies ran while one was open for 0% -> 0% of each run, Pallas kernels for 29% -> 27%
where the time goes in v8:
time: 72.6 us; the launch traced here: 72.4 us
  starting transfers between devices  33.2 us (46%)
  Pallas kernels  31.9 us (44%)
  waiting for transfers between devices  6.55 us (9%)
  between operations  0.78 us (1%)
    pallas_call x8, Pallas kernels, call(): pl.pallas_call(kernel, out_shape=outs, in_specs=[SMEM] * scalars + [HBM]...  31.9 us
    ppermute x8, starting transfers between devices, exchange(): return [lax.ppermute(field, axes, list(enumerate(to))) for to in swaps]  13.7 us
    ppermute x10, starting transfers between devices, swap(): lax.ppermute(values, axis, [(i, i ^ step) for i in range(lax.axis_size(ax...  11.1 us
    ppermute x10, waiting for transfers between devices, swap(): lax.ppermute(values, axis, [(i, i ^ step) for i in range(lax.axis_size(ax...  5.83 us
    ppermute x3, starting transfers between devices, body(): lax.ppermute(t, 'col', [(i, i ^ k) for i in range(columns)])  4.39 us
    ppermute x1, starting transfers between devices, body(): lax.ppermute(second, 'piece', [(i, ((i ^ 1) + (1 if i % 2 else -1) * 2) %...  3.56 us
  transfers between devices with their start and end apart: 23, of which 6 were waited for; matrix products, arithmetic and copies ran while one was open for 0% of the time, Pallas kernels for 27%

profile of v8, /device:TPU:0, one launch (start us, length us, event | category | flops | bytes accessed | tf_op | source)
XLA Modules:
  0.0 72.4 jit_solution(5442286645671708378)
XLA Ops:
  0.6 1.8 %prepare.1 = (s32[8]{0:T(128)S(4)}, s32[1480]{0:T(1024)S(4)}, f32[4,192,128]{2,1,0:T(8,128)S(1)}, f32[4,64,128]{2,1,0:T(8,128)S(1)}, f32[32,128]{1,0:T(8,128)S(1...) custom-call(s32[8]{0:T(128)} %counts.1, ...), custom_call_target="tpu_custom_call" | custom-call | tf_op jit(solution)/shard_map/prepare/pallas_call | solution.py:631
  2.5 0.5 collective-permute-start
  3.0 3.6 %collective-permute-start.1 = (f32[4,32,128]{2,1,0:T(8,128)S(1)}, f32[4,32,128]{2,1,0:T(8,128)S(1)}, u32[]{:S(2)}, u32[]{:S(2)}) collective-permute-start(f32[4,32,128]{2,1,0:T(8,128)S(1)} %get-tuple-element.45), channel_id=1, source_target_pairs={{0,28},{4,8},{8,4},{12,16},{16,12},{20,24},{24,20},{28,0},{1,29},{... | collective-permute-start | bytes 196616 | tf_op jit(solution)/shard_map/ppermute | solution.py:660
  6.6 1.6 %collective-permute-start.2 = (f32[32,128]{1,0:T(8,128)S(1)}, f32[32,128]{1,0:T(8,128)S(1)}, u32[]{:S(2)}, u32[]{:S(2)}) collective-permute-start(f32[32,128]{1,0:T(8,128)S(1)} %get-tuple-element.55), channel_id=1, source_target_pairs={{0,1},{1,0},{2,3},{3,2},{4,5},{5,4},{6,7},{7,6},{8,9},{9,8},{10,11... | collective-permute-start | bytes 49160 | tf_op jit(solution)/shard_map/ppermute | solution.py:661
  8.1 2.6 %collective-permute-start.3 = (f32[32,128]{1,0:T(8,128)S(1)}, f32[32,128]{1,0:T(8,128)S(1)}, u32[]{:S(2)}, u32[]{:S(2)}) collective-permute-start(f32[32,128]{1,0:T(8,128)S(1)} %get-tuple-element.56), channel_id=1, source_target_pairs={{0,2},{1,3},{2,0},{3,1},{4,6},{5,7},{6,4},{7,5},{8,10},{9,11},{10,... | collective-permute-start | bytes 49160 | tf_op jit(solution)/shard_map/ppermute | solution.py:661
  10.7 0.2 collective-permute-start.4
  10.9 10.8 %build_inner.1 = (s32[196]{0:T(256)S(4)}, s32[195]{0:T(256)S(4)}, f32[222,128,128]{2,1,0:T(8,128)S(1)}, bf16[32,128,128]{2,1,0:T(8,128)(2,1)S(1)}, f32[3,32,128]...) custom-call(s32[8]{0:T(128)S(4)} %get-tuple-element.38.meta, ...), custom_call_target="tpu_custom_call" | custom-call | flops 56623104 | tf_op jit(solution)/shard_map/build_inner/pallas_call | solution.py:631
  21.7 0.0 collective-permute-done.2.rest_1_
  21.7 0.0 collective-permute-done.3.rest_2_
  21.8 0.0 collective-permute-done.4.rest_3_
  21.8 0.0 collective-permute-done.first
  21.8 0.0 collective-permute-done.1.second
  21.8 4.9 %build_outer.1 = (s32[1]{0:T(128)S(4)}, f32[228,128,128]{2,1,0:T(8,128)S(1)}, f32[32,128]{1,0:T(8,128)S(1)}, f32[32,128]{1,0:T(8,128)S(1)}, f32[32,128]{1,0:T(8,128)S(1)}, /*index=5*/f32[32,128]{1,0:T(8,128)S(1)}) custom-call(s32[8]{0:T(128)S(4)} %get-tuple-element.38.meta, s32[1480]{0:T(1024)S(4)} %get-tuple-element.39.table, ...), custom_call_target="tpu_custom_call" | custom-call | flops 58195968 | tf_op jit(solution)/shard_map/build_outer/pallas_call | solution.py:631
  26.7 4.5 %collective-permute-start.8 = (f32[32,128]{1,0:T(8,128)S(1)}, f32[32,128]{1,0:T(8,128)S(1)}, u32[]{:S(2)}, u32[]{:S(2)}) collective-permute-start(f32[32,128]{1,0:T(8,128)S(1)} %get-tuple-element.58.field.precond), channel_id=1, source_target_pairs={{0,1},{1,3},{2,4},{3,0},{4,2},{5,7},{6,8},{7,5},{8,6},{9,11},{10,1... | collective-permute-start | bytes 49160 | tf_op jit(solution)/shard_map/ppermute | solution.py:709
  31.2 1.1 %collective-permute-start.7 = (f32[32,128]{1,0:T(8,128)S(1)}, f32[32,128]{1,0:T(8,128)S(1)}, u32[]{:S(2)}, u32[]{:S(2)}) collective-permute-start(f32[32,128]{1,0:T(8,128)S(1)} %get-tuple-element.58.field.precond), channel_id=1, source_target_pairs={{0,2},{1,4},{2,3},{3,0},{4,1},{5,8},{6,7},{7,6},{8,5},{9,12},{10,1... | collective-permute-start | bytes 49160 | tf_op jit(solution)/shard_map/ppermute | solution.py:709
  32.3 1.5 %collective-permute-start.6 = (f32[32,128]{1,0:T(8,128)S(1)}, f32[32,128]{1,0:T(8,128)S(1)}, u32[]{:S(2)}, u32[]{:S(2)}) collective-permute-start(f32[32,128]{1,0:T(8,128)S(1)} %get-tuple-element.58.field.precond), channel_id=1, source_target_pairs={{0,31},{1,2},{2,1},{3,4},{4,3},{5,6},{6,5},{7,8},{8,7},{9,10},{10,... | collective-permute-start | bytes 49160 | tf_op jit(solution)/shard_map/ppermute | solution.py:709
  33.8 0.2 collective-permute-start.5
  34.0 4.4 %apply_inner.2 = (f32[32,128,128]{2,1,0:T(8,128)S(1)}, f32[256,128]{1,0:T(8,128)S(1)}) custom-call(s32[8]{0:T(128)S(4)} %get-tuple-element.38.meta, s32[1480]{0:T(1024)S(4)} %get-tuple-element.39.table, s32[196]{0:T(256)S(4)} %get-tuple-element.41.plan, s32[1]{0:T(128)S(4)} %get-tuple-element.59.again, f32[32,128]{1,0:T(8,128)S(1)} %get-tuple-element.58.field.precond, ...), custom_call_target="tpu_custom_call" | custom-call | flops 14155776 | tf_op jit(solution)/shard_map/apply_inner/pallas_call | solution.py:631
  38.4 0.0 collective-permute-done.8.rest_3_
  38.4 0.0 collective-permute-done.7.rest_2_
  38.4 0.7 collective-permute-done.6.rest_1_
  39.1 0.0 collective-permute-done.5.rest_0_
  39.1 2.3 %apply_first.1 = (f32[32,128]{1,0:T(8,128)S(1)}, f32[32,128]{1,0:T(8,128)S(1)}) custom-call(s32[8]{0:T(128)S(4)} %get-tuple-element.38.meta, s32[1480]{0:T(1024)S(4)} %get-tuple-element.39.table, s32[196]{0:T(256)S(4)} %get-tuple-element.41.plan, s32[1]{0:T(128)S(4)} %get-tuple-element.59.again, f32[32,128]{1,0:T(8,128)S(1)} %get-tuple-element.60.diagonal, ...), custom_call_target="tpu_custom_call" | custom-call | flops 7274496 | tf_op jit(solution)/shard_map/apply_first/pallas_call | solution.py:631
  41.4 2.0 %collective-permute-start.12 = (f32[32,128]{1,0:T(8,128)S(1)}, f32[32,128]{1,0:T(8,128)S(1)}, u32[]{:S(2)}, u32[]{:S(2)}) collective-permute-start(f32[32,128]{1,0:T(8,128)S(1)} %get-tuple-element.67.field.scaled), channel_id=1, source_target_pairs={{0,1},{1,3},{2,4},{3,0},{4,2},{5,7},{6,8},{7,5},{8,6},{9,11},{10,1... | collective-permute-start | bytes 49160 | tf_op jit(solution)/shard_map/ppermute | solution.py:709
  43.4 1.9 %collective-permute-start.11 = (f32[32,128]{1,0:T(8,128)S(1)}, f32[32,128]{1,0:T(8,128)S(1)}, u32[]{:S(2)}, u32[]{:S(2)}) collective-permute-start(f32[32,128]{1,0:T(8,128)S(1)} %get-tuple-element.67.field.scaled), channel_id=1, source_target_pairs={{0,2},{1,4},{2,3},{3,0},{4,1},{5,8},{6,7},{7,6},{8,5},{9,12},{10,1... | collective-permute-start | bytes 49160 | tf_op jit(solution)/shard_map/ppermute | solution.py:709
  45.3 2.5 %collective-permute-start.10 = (f32[32,128]{1,0:T(8,128)S(1)}, f32[32,128]{1,0:T(8,128)S(1)}, u32[]{:S(2)}, u32[]{:S(2)}) collective-permute-start(f32[32,128]{1,0:T(8,128)S(1)} %get-tuple-element.67.field.scaled), channel_id=1, source_target_pairs={{0,31},{1,2},{2,1},{3,4},{4,3},{5,6},{6,5},{7,8},{8,7},{9,10},{10,... | collective-permute-start | bytes 49160 | tf_op jit(solution)/shard_map/ppermute | solution.py:709
  47.7 0.0 collective-permute-start.9
  47.8 4.4 %apply_inner.3 = (f32[32,128,128]{2,1,0:T(8,128)S(1)}, f32[256,128]{1,0:T(8,128)S(1)}) custom-call(s32[8]{0:T(128)S(4)} %get-tuple-element.38.meta, s32[1480]{0:T(1024)S(4)} %get-tuple-element.39.table, s32[196]{0:T(256)S(4)} %get-tuple-element.41.plan, s32[1]{0:T(128)S(4)} %get-tuple-element.59.again, f32[32,128]{1,0:T(8,128)S(1)} %get-tuple-element.67.field.scaled, ...), custom_call_target="tpu_custom_call" | custom-call | flops 14155776 | tf_op jit(solution)/shard_map/apply_inner/pallas_call | solution.py:631
  52.1 0.0 collective-permute-done.12.rest_3_
  52.1 0.0 collective-permute-done.11.rest_2_
  52.1 0.0 collective-permute-done.10.rest_1_
  52.1 0.0 collective-permute-done.9.rest_0_
  52.2 2.4 %apply_second.1 = (f32[32,128]{1,0:T(8,128)S(1)}, f32[8,128]{1,0:T(8,128)S(1)}) custom-call(s32[8]{0:T(128)S(4)} %get-tuple-element.38.meta, s32[1480]{0:T(1024)S(4)} %get-tuple-element.39.table, s32[196]{0:T(256)S(4)} %get-tuple-element.41.plan, s32[1]{0:T(128)S(4)} %get-tuple-element.59.again, f32[32,128]{1,0:T(8,128)S(1)} %get-tuple-element.37.source, ...), custom_call_target="tpu_custom_call" | custom-call | flops 7274496 | tf_op jit(solution)/shard_map/apply_second/pallas_call | solution.py:631
  54.6 0.3 collective-permute-start.15
  54.8 4.0 %collective-permute-start.14 = (f32[8,128]{1,0:T(8,128)S(1)}, f32[8,128]{1,0:T(8,128)S(1)}, u32[]{:S(2)}, u32[]{:S(2)}) collective-permute-start(f32[8,128]{1,0:T(8,128)S(1)} %get-tuple-element.71), channel_id=1, source_target_pairs={{0,2},{1,3},{2,0},{3,1},{4,6},{5,7},{6,4},{7,5},{8,10},{9,11},{10,... | collective-permute-start | bytes 12296 | tf_op jit(solution)/shard_map/ppermute | solution.py:736
  58.8 0.2 collective-permute-start.13
  59.0 1.0 %collective-permute-done.15 = f32[8,128]{1,0:T(8,128)S(1)} collective-permute-done((f32[8,128]{1,0:T(8,128)S(1)}, f32[8,128]{1,0:T(8,128)S(1)}, u32[]{:S(2)}, u32[]{:S(2)}) %collective-permute-start.15) | collective-permute-done | bytes 4128 | tf_op jit(solution)/shard_map/ppermute | solution.py:736
  60.0 0.5 collective-permute-done.14
  60.4 2.0 %collective-permute-done.13 = f32[8,128]{1,0:T(8,128)S(1)} collective-permute-done((f32[8,128]{1,0:T(8,128)S(1)}, f32[8,128]{1,0:T(8,128)S(1)}, u32[]{:S(2)}, u32[]{:S(2)}) %collective-permute-start.13) | collective-permute-done | bytes 4128 | tf_op jit(solution)/shard_map/ppermute | solution.py:736
  62.4 0.0 collective-permute-start.22
  62.4 1.1 %collective-permute-start.21 = (f32[8,128]{1,0:T(8,128)S(1)}, f32[8,128]{1,0:T(8,128)S(1)}, u32[]{:S(2)}, u32[]{:S(2)}) collective-permute-start(f32[8,128]{1,0:T(8,128)S(1)} %add_add_fusion.rest_0_), channel_id=1, source_target_pairs={{0,24},{4,28},{8,16},{12,20},{16,8},{20,12},{24,0},{28,4},{1,25},{... | collective-permute-start | bytes 12296 | tf_op jit(solution)/shard_map/ppermute | solution.py:736
  63.5 3.7 %collective-permute-start.20 = (f32[8,128]{1,0:T(8,128)S(1)}, f32[8,128]{1,0:T(8,128)S(1)}, u32[]{:S(2)}, u32[]{:S(2)}) collective-permute-start(f32[8,128]{1,0:T(8,128)S(1)} %add_add_fusion.rest_0_), channel_id=1, source_target_pairs={{0,20},{4,16},{8,28},{12,24},{16,4},{20,0},{24,12},{28,8},{1,21},{... | collective-permute-start | bytes 12296 | tf_op jit(solution)/shard_map/ppermute | solution.py:736
  67.2 0.0 collective-permute-start.19
  67.2 0.6 collective-permute-start.18
  67.8 0.0 collective-permute-done.22.rest_7_
  67.9 1.2 %collective-permute-start.17 = (f32[8,128]{1,0:T(8,128)S(1)}, f32[8,128]{1,0:T(8,128)S(1)}, u32[]{:S(2)}, u32[]{:S(2)}) collective-permute-start(f32[8,128]{1,0:T(8,128)S(1)} %add_add_fusion.rest_0_), channel_id=1, source_target_pairs={{0,8},{4,12},{8,0},{12,4},{16,24},{20,28},{24,16},{28,20},{1,9},{5... | collective-permute-start | bytes 12296 | tf_op jit(solution)/shard_map/ppermute | solution.py:736
  69.0 0.0 collective-permute-done.21.rest_6_
  69.0 0.1 collective-permute-start.16
  69.1 0.0 collective-permute-done.20.rest_5_
  69.1 1.7 %collective-permute-done.19.rest_4_ = f32[8,128]{1,0:T(8,128)S(1)} collective-permute-done((f32[8,128]{1,0:T(8,128)S(1)}, f32[8,128]{1,0:T(8,128)S(1)}, u32[]{:S(2)}, u32[]{:S(2)}) %collective-permute-start.19) | collective-permute-done | bytes 4128 | tf_op jit(solution)/shard_map/ppermute | solution.py:736
  70.8 0.0 collective-permute-done.18.rest_3_
  70.8 0.6 collective-permute-done.17.rest_2_
  71.5 0.0 collective-permute-done.16.rest_1_
  71.5 0.9 %finish.1 = (f32[32,128]{1,0:T(8,128)}, f32[32,128]{1,0:T(8,128)}) custom-call(f32[32,128]{1,0:T(8,128)S(1)} %get-tuple-element.37.source, f32[32,128]{1,0:T(8,128)S(1)} %get-tuple-element.58.field.precond, f32[32,128]{1,0:T(8,128)S(1)} %get-tuple-element.66.spill, f32[32,128]{1,0:T(8,128)S(1)} %get-tuple-element.67.field.scaled, ...), custom_call_target="tpu_custom_call" | custom-call | tf_op jit(solution)/shard_map/finish/pallas_call | solution.py:631
  (1 shorter events, 0.0 us)
Async XLA Ops:
  2.5 19.3 %collective-permute-start = (f32[4,32,128]{2,1,0:T(8,128)S(1)}, f32[4,32,128]{2,1,0:T(8,128)S(1)}, u32[]{:S(2)}, u32[]{:S(2)}) collective-permute-start(f32[4,32,128]{2,1,0:T(8,128)S(1)} %get-tuple-element.44), channel_id=1, source_target_pairs={{0,4},{4,0},{8,12},{12,8},{16,20},{20,16},{24,28},{28,24},{1,5},{5... | collective-permute-start | bytes 196616 | tf_op jit(solution)/shard_map/ppermute | solution.py:659
  3.0 18.8 %collective-permute-start.1 = (f32[4,32,128]{2,1,0:T(8,128)S(1)}, f32[4,32,128]{2,1,0:T(8,128)S(1)}, u32[]{:S(2)}, u32[]{:S(2)}) collective-permute-start(f32[4,32,128]{2,1,0:T(8,128)S(1)} %get-tuple-element.45), channel_id=1, source_target_pairs={{0,28},{4,8},{8,4},{12,16},{16,12},{20,24},{24,20},{28,0},{1,29},{... | collective-permute-start | bytes 196616 | tf_op jit(solution)/shard_map/ppermute | solution.py:660
  6.6 15.2 %collective-permute-start.2 = (f32[32,128]{1,0:T(8,128)S(1)}, f32[32,128]{1,0:T(8,128)S(1)}, u32[]{:S(2)}, u32[]{:S(2)}) collective-permute-start(f32[32,128]{1,0:T(8,128)S(1)} %get-tuple-element.55), channel_id=1, source_target_pairs={{0,1},{1,0},{2,3},{3,2},{4,5},{5,4},{6,7},{7,6},{8,9},{9,8},{10,11... | collective-permute-start | bytes 49160 | tf_op jit(solution)/shard_map/ppermute | solution.py:661
  8.1 13.6 %collective-permute-start.3 = (f32[32,128]{1,0:T(8,128)S(1)}, f32[32,128]{1,0:T(8,128)S(1)}, u32[]{:S(2)}, u32[]{:S(2)}) collective-permute-start(f32[32,128]{1,0:T(8,128)S(1)} %get-tuple-element.56), channel_id=1, source_target_pairs={{0,2},{1,3},{2,0},{3,1},{4,6},{5,7},{6,4},{7,5},{8,10},{9,11},{10,... | collective-permute-start | bytes 49160 | tf_op jit(solution)/shard_map/ppermute | solution.py:661
  10.7 11.0 %collective-permute-start.4 = (f32[32,128]{1,0:T(8,128)S(1)}, f32[32,128]{1,0:T(8,128)S(1)}, u32[]{:S(2)}, u32[]{:S(2)}) collective-permute-start(f32[32,128]{1,0:T(8,128)S(1)} %get-tuple-element.57), channel_id=1, source_target_pairs={{0,3},{1,2},{2,1},{3,0},{4,7},{5,6},{6,5},{7,4},{8,11},{9,10},{10,... | collective-permute-start | bytes 49160 | tf_op jit(solution)/shard_map/ppermute | solution.py:661
  26.7 11.7 %collective-permute-start.8 = (f32[32,128]{1,0:T(8,128)S(1)}, f32[32,128]{1,0:T(8,128)S(1)}, u32[]{:S(2)}, u32[]{:S(2)}) collective-permute-start(f32[32,128]{1,0:T(8,128)S(1)} %get-tuple-element.58.field.precond), channel_id=1, source_target_pairs={{0,1},{1,3},{2,4},{3,0},{4,2},{5,7},{6,8},{7,5},{8,6},{9,11},{10,1... | collective-permute-start | bytes 49160 | tf_op jit(solution)/shard_map/ppermute | solution.py:709
  31.2 7.1 %collective-permute-start.7 = (f32[32,128]{1,0:T(8,128)S(1)}, f32[32,128]{1,0:T(8,128)S(1)}, u32[]{:S(2)}, u32[]{:S(2)}) collective-permute-start(f32[32,128]{1,0:T(8,128)S(1)} %get-tuple-element.58.field.precond), channel_id=1, source_target_pairs={{0,2},{1,4},{2,3},{3,0},{4,1},{5,8},{6,7},{7,6},{8,5},{9,12},{10,1... | collective-permute-start | bytes 49160 | tf_op jit(solution)/shard_map/ppermute | solution.py:709
  32.3 6.8 %collective-permute-start.6 = (f32[32,128]{1,0:T(8,128)S(1)}, f32[32,128]{1,0:T(8,128)S(1)}, u32[]{:S(2)}, u32[]{:S(2)}) collective-permute-start(f32[32,128]{1,0:T(8,128)S(1)} %get-tuple-element.58.field.precond), channel_id=1, source_target_pairs={{0,31},{1,2},{2,1},{3,4},{4,3},{5,6},{6,5},{7,8},{8,7},{9,10},{10,... | collective-permute-start | bytes 49160 | tf_op jit(solution)/shard_map/ppermute | solution.py:709
  33.8 5.3 %collective-permute-start.5 = (f32[32,128]{1,0:T(8,128)S(1)}, f32[32,128]{1,0:T(8,128)S(1)}, u32[]{:S(2)}, u32[]{:S(2)}) collective-permute-start(f32[32,128]{1,0:T(8,128)S(1)} %get-tuple-element.58.field.precond), channel_id=1, source_target_pairs={{0,1},{1,0},{2,3},{3,2},{4,5},{5,4},{6,7},{7,6},{8,9},{9,8},{10,11... | collective-permute-start | bytes 49160 | tf_op jit(solution)/shard_map/ppermute | solution.py:709
  41.4 10.7 %collective-permute-start.12 = (f32[32,128]{1,0:T(8,128)S(1)}, f32[32,128]{1,0:T(8,128)S(1)}, u32[]{:S(2)}, u32[]{:S(2)}) collective-permute-start(f32[32,128]{1,0:T(8,128)S(1)} %get-tuple-element.67.field.scaled), channel_id=1, source_target_pairs={{0,1},{1,3},{2,4},{3,0},{4,2},{5,7},{6,8},{7,5},{8,6},{9,11},{10,1... | collective-permute-start | bytes 49160 | tf_op jit(solution)/shard_map/ppermute | solution.py:709
  43.4 8.8 %collective-permute-start.11 = (f32[32,128]{1,0:T(8,128)S(1)}, f32[32,128]{1,0:T(8,128)S(1)}, u32[]{:S(2)}, u32[]{:S(2)}) collective-permute-start(f32[32,128]{1,0:T(8,128)S(1)} %get-tuple-element.67.field.scaled), channel_id=1, source_target_pairs={{0,2},{1,4},{2,3},{3,0},{4,1},{5,8},{6,7},{7,6},{8,5},{9,12},{10,1... | collective-permute-start | bytes 49160 | tf_op jit(solution)/shard_map/ppermute | solution.py:709
  45.3 6.9 %collective-permute-start.10 = (f32[32,128]{1,0:T(8,128)S(1)}, f32[32,128]{1,0:T(8,128)S(1)}, u32[]{:S(2)}, u32[]{:S(2)}) collective-permute-start(f32[32,128]{1,0:T(8,128)S(1)} %get-tuple-element.67.field.scaled), channel_id=1, source_target_pairs={{0,31},{1,2},{2,1},{3,4},{4,3},{5,6},{6,5},{7,8},{8,7},{9,10},{10,... | collective-permute-start | bytes 49160 | tf_op jit(solution)/shard_map/ppermute | solution.py:709
  47.7 4.4 %collective-permute-start.9 = (f32[32,128]{1,0:T(8,128)S(1)}, f32[32,128]{1,0:T(8,128)S(1)}, u32[]{:S(2)}, u32[]{:S(2)}) collective-permute-start(f32[32,128]{1,0:T(8,128)S(1)} %get-tuple-element.67.field.scaled), channel_id=1, source_target_pairs={{0,1},{1,0},{2,3},{3,2},{4,5},{5,4},{6,7},{7,6},{8,9},{9,8},{10,11... | collective-permute-start | bytes 49160 | tf_op jit(solution)/shard_map/ppermute | solution.py:709
  54.6 5.4 %collective-permute-start.15 = (f32[8,128]{1,0:T(8,128)S(1)}, f32[8,128]{1,0:T(8,128)S(1)}, u32[]{:S(2)}, u32[]{:S(2)}) collective-permute-start(f32[8,128]{1,0:T(8,128)S(1)} %get-tuple-element.71), channel_id=1, source_target_pairs={{0,3},{1,2},{2,1},{3,0},{4,7},{5,6},{6,5},{7,4},{8,11},{9,10},{10,... | collective-permute-start | bytes 12296 | tf_op jit(solution)/shard_map/ppermute | solution.py:736
  54.8 5.6 %collective-permute-start.14 = (f32[8,128]{1,0:T(8,128)S(1)}, f32[8,128]{1,0:T(8,128)S(1)}, u32[]{:S(2)}, u32[]{:S(2)}) collective-permute-start(f32[8,128]{1,0:T(8,128)S(1)} %get-tuple-element.71), channel_id=1, source_target_pairs={{0,2},{1,3},{2,0},{3,1},{4,6},{5,7},{6,4},{7,5},{8,10},{9,11},{10,... | collective-permute-start | bytes 12296 | tf_op jit(solution)/shard_map/ppermute | solution.py:736
  58.8 3.6 %collective-permute-start.13 = (f32[8,128]{1,0:T(8,128)S(1)}, f32[8,128]{1,0:T(8,128)S(1)}, u32[]{:S(2)}, u32[]{:S(2)}) collective-permute-start(f32[8,128]{1,0:T(8,128)S(1)} %get-tuple-element.71), channel_id=1, source_target_pairs={{0,1},{1,0},{2,3},{3,2},{4,5},{5,4},{6,7},{7,6},{8,9},{9,8},{10,11... | collective-permute-start | bytes 12296 | tf_op jit(solution)/shard_map/ppermute | solution.py:736
  62.4 5.4 %collective-permute-start.22 = (f32[8,128]{1,0:T(8,128)S(1)}, f32[8,128]{1,0:T(8,128)S(1)}, u32[]{:S(2)}, u32[]{:S(2)}) collective-permute-start(f32[8,128]{1,0:T(8,128)S(1)} %add_add_fusion.rest_0_), channel_id=1, source_target_pairs={{0,28},{4,24},{8,20},{12,16},{16,12},{20,8},{24,4},{28,0},{1,29},{... | collective-permute-start | bytes 12296 | tf_op jit(solution)/shard_map/ppermute | solution.py:736
  62.4 6.6 %collective-permute-start.21 = (f32[8,128]{1,0:T(8,128)S(1)}, f32[8,128]{1,0:T(8,128)S(1)}, u32[]{:S(2)}, u32[]{:S(2)}) collective-permute-start(f32[8,128]{1,0:T(8,128)S(1)} %add_add_fusion.rest_0_), channel_id=1, source_target_pairs={{0,24},{4,28},{8,16},{12,20},{16,8},{20,12},{24,0},{28,4},{1,25},{... | collective-permute-start | bytes 12296 | tf_op jit(solution)/shard_map/ppermute | solution.py:736
  63.5 5.6 %collective-permute-start.20 = (f32[8,128]{1,0:T(8,128)S(1)}, f32[8,128]{1,0:T(8,128)S(1)}, u32[]{:S(2)}, u32[]{:S(2)}) collective-permute-start(f32[8,128]{1,0:T(8,128)S(1)} %add_add_fusion.rest_0_), channel_id=1, source_target_pairs={{0,20},{4,16},{8,28},{12,24},{16,4},{20,0},{24,12},{28,8},{1,21},{... | collective-permute-start | bytes 12296 | tf_op jit(solution)/shard_map/ppermute | solution.py:736
  67.2 3.6 %collective-permute-start.19 = (f32[8,128]{1,0:T(8,128)S(1)}, f32[8,128]{1,0:T(8,128)S(1)}, u32[]{:S(2)}, u32[]{:S(2)}) collective-permute-start(f32[8,128]{1,0:T(8,128)S(1)} %add_add_fusion.rest_0_), channel_id=1, source_target_pairs={{0,16},{4,20},{8,24},{12,28},{16,0},{20,4},{24,8},{28,12},{1,17},{... | collective-permute-start | bytes 12296 | tf_op jit(solution)/shard_map/ppermute | solution.py:736
  67.2 3.6 %collective-permute-start.18 = (f32[8,128]{1,0:T(8,128)S(1)}, f32[8,128]{1,0:T(8,128)S(1)}, u32[]{:S(2)}, u32[]{:S(2)}) collective-permute-start(f32[8,128]{1,0:T(8,128)S(1)} %add_add_fusion.rest_0_), channel_id=1, source_target_pairs={{0,12},{4,8},{8,4},{12,0},{16,28},{20,24},{24,20},{28,16},{1,13},{... | collective-permute-start | bytes 12296 | tf_op jit(solution)/shard_map/ppermute | solution.py:736
  67.9 3.6 %collective-permute-start.17 = (f32[8,128]{1,0:T(8,128)S(1)}, f32[8,128]{1,0:T(8,128)S(1)}, u32[]{:S(2)}, u32[]{:S(2)}) collective-permute-start(f32[8,128]{1,0:T(8,128)S(1)} %add_add_fusion.rest_0_), channel_id=1, source_target_pairs={{0,8},{4,12},{8,0},{12,4},{16,24},{20,28},{24,16},{28,20},{1,9},{5... | collective-permute-start | bytes 12296 | tf_op jit(solution)/shard_map/ppermute | solution.py:736
  69.0 2.4 %collective-permute-start.16 = (f32[8,128]{1,0:T(8,128)S(1)}, f32[8,128]{1,0:T(8,128)S(1)}, u32[]{:S(2)}, u32[]{:S(2)}) collective-permute-start(f32[8,128]{1,0:T(8,128)S(1)} %add_add_fusion.rest_0_), channel_id=1, source_target_pairs={{0,4},{4,0},{8,12},{12,8},{16,20},{20,16},{24,28},{28,24},{1,5},{5... | collective-permute-start | bytes 12296 | tf_op jit(solution)/shard_map/ppermute | solution.py:736

commit v9 on v8

--- a/solution.py
+++ b/solution.py
@@ -174,13 +174,15 @@
     return result
 
 
+HALF = 64
+
+
 def own_side(x):
     size = x[0] * x[0] + x[1] * x[1] + x[2] * x[2]
     one = jnp.ones_like(size)
     high, middle, low = three_parts(stacked([2.0 * x[0], 2.0 * x[1], 2.0 * x[2], one, 0.5 - size]))
-    width = size.shape[1]
-    rest = jnp.zeros((width - 6 * SUB, width), jnp.float32)
-    return jnp.concatenate([high, high, middle, middle, high, low, rest], 0).T.astype(jnp.bfloat16)
+    rest = jnp.zeros((HALF - 6 * SUB, size.shape[1]), jnp.float32)
+    return jnp.concatenate([high, high, middle, middle, high, low, rest], 0)
 
 
 def other_side(y):
@@ -189,12 +191,10 @@
     high, middle, low = three_parts(stacked([y[0], y[1], y[2], 0.5 - size, one]))
     first = jnp.concatenate([high, middle], 0).astype(jnp.bfloat16)
     last = jnp.concatenate([low, high], 0).astype(jnp.bfloat16)
-    width = size.shape[1]
-    rest = jnp.zeros((width - 6 * SUB, width), jnp.bfloat16)
-    return jnp.concatenate([first, first, last, rest], 0)
-
-
-GROUP = 6
+    return jnp.concatenate([first, first, last, jnp.zeros((HALF - 6 * SUB, size.shape[1]), jnp.bfloat16)], 0)
+
+
+GROUP = 8
 
 
 def flat_tiles(count, runs, most, table, sides, middles, weights, other_at, ahead, tiles, rows_ref, cols_ref):
@@ -211,12 +211,21 @@
             state = jnp.minimum(run + over.astype(jnp.int32), most), jnp.where(over, 0, t + 1)
         return state, found
 
+    def other_of(a, n):
+        here = pl.ds(a, 1)
+        return other_side([wide(other_at(c, n)) - wide(middles[c, here, :]) for c in range(3)])
+
     def products(found):
-        for k, (a, n) in enumerate(found):
-            here = pl.ds(jnp.minimum(a, share - 1), 1)
-            near = [wide(other_at(c, n)) - wide(middles[c, here, :]) for c in range(3)]
-            side = sides[jnp.minimum(a, share - 1)]
-            ahead[k] = jnp.dot(side, other_side(near), preferred_element_type=jnp.float32)
+        none = jnp.zeros((HALF, width), jnp.bfloat16)
+        for k in range(0, GROUP, 2):
+            (a, n), (b, m) = ((jnp.minimum(a, share - 1), n) for a, n in found[k : k + 2])
+            left = jnp.concatenate([other_of(a, n), none], 0)
+            right = jnp.concatenate([none, other_of(b, m)], 0)
+            both = jnp.dot(
+                sides[0, a] + sides[1, b], jnp.concatenate([left, right], 1), preferred_element_type=jnp.float32
+            )
+            ahead[k] = both[:, :width]
+            ahead[k + 1] = both[:, width:]
 
     def turn(i, carry):
         state, found = carry
@@ -347,7 +356,10 @@
         middles[k] = jnp.broadcast_to(jnp.floor(first) + 0.5, (share, width))
     for a in range(share):
         here = slice(a, a + 1)
-        sides[a] = own_side([wide(near[k, here, :] - middles[k, here, :]) for k in range(3)])
+        side = own_side([wide(near[k, here, :] - middles[k, here, :]) for k in range(3)])
+        none = jnp.zeros((width - HALF, width), jnp.float32)
+        sides[0, a] = jnp.concatenate([side, none], 0).T.astype(jnp.bfloat16)
+        sides[1, a] = jnp.concatenate([none, side], 0).T.astype(jnp.bfloat16)
     spread_columns(weights, lambda a: a, near[3, 0:share, :])
     cols_ref[...] = jnp.zeros_like(cols_ref)
     rows_ref[...] = jnp.zeros_like(rows_ref)
@@ -664,7 +676,7 @@
         build_inner,
         (meta, table, near),
         [pltpu.SMEM((share * FIELDS + 4,), jnp.int32), pltpu.SMEM((6 * share + 3,), jnp.int32), inner_tiles,
-         pltpu.VMEM((share, width, width), jnp.bfloat16), pltpu.VMEM((3, share, width), f32), square, square, narrow, narrow],
+         pltpu.VMEM((2, share, width, width), jnp.bfloat16), pltpu.VMEM((3, share, width), f32), square, square, narrow, narrow],
         [pltpu.SMEM((3 * share + 3,), jnp.int32), square_more, pltpu.VMEM(((share + 1) * SUB, width), f32), ahead],
         16 * most_inner,
     )

time: 72.6 us -> 72.6 us (level)
  no operation moved by 1% of the time
where the time goes in v9:
time: 72.6 us; the launch traced here: 72.7 us
  starting transfers between devices  33.3 us (46%)
  Pallas kernels  31.9 us (44%)
  waiting for transfers between devices  6.75 us (9%)
  between operations  0.78 us (1%)
    pallas_call x8, Pallas kernels, call(): pl.pallas_call(kernel, out_shape=outs, in_specs=[SMEM] * scalars + [HBM]...  31.9 us
    ppermute x8, starting transfers between devices, exchange(): return [lax.ppermute(field, axes, list(enumerate(to))) for to in swaps]  13.2 us
    ppermute x10, starting transfers between devices, swap(): lax.ppermute(values, axis, [(i, i ^ step) for i in range(lax.axis_size(ax...  11.6 us
    ppermute x10, waiting for transfers between devices, swap(): lax.ppermute(values, axis, [(i, i ^ step) for i in range(lax.axis_size(ax...  5.9 us
    ppermute x3, starting transfers between devices, body(): lax.ppermute(t, 'col', [(i, i ^ k) for i in range(columns)])  4.39 us
    ppermute x1, starting transfers between devices, body(): lax.ppermute(second, 'piece', [(i, ((i ^ 1) + (1 if i % 2 else -1) * 2) %...  3.55 us
  transfers between devices with their start and end apart: 23, of which 6 were waited for; matrix products, arithmetic and copies ran while one was open for 0% of the time, Pallas kernels for 27%

profile of v9, /device:TPU:0, one launch (start us, length us, event | category | flops | bytes accessed | tf_op | source)
XLA Modules:
  0.0 72.7 jit_solution(16573606984847309158)
XLA Ops:
  0.6 1.8 %prepare.1 = (s32[8]{0:T(128)S(4)}, s32[1480]{0:T(1024)S(4)}, f32[4,192,128]{2,1,0:T(8,128)S(1)}, f32[4,64,128]{2,1,0:T(8,128)S(1)}, f32[32,128]{1,0:T(8,128)S(1...) custom-call(s32[8]{0:T(128)} %counts.1, ...), custom_call_target="tpu_custom_call" | custom-call | tf_op jit(solution)/shard_map/prepare/pallas_call | solution.py:643
  2.5 0.5 collective-permute-start
  3.0 3.6 %collective-permute-start.1 = (f32[4,32,128]{2,1,0:T(8,128)S(1)}, f32[4,32,128]{2,1,0:T(8,128)S(1)}, u32[]{:S(2)}, u32[]{:S(2)}) collective-permute-start(f32[4,32,128]{2,1,0:T(8,128)S(1)} %get-tuple-element.45), channel_id=1, source_target_pairs={{0,28},{4,8},{8,4},{12,16},{16,12},{20,24},{24,20},{28,0},{1,29},{... | collective-permute-start | bytes 196616 | tf_op jit(solution)/shard_map/ppermute | solution.py:672
  6.6 1.6 %collective-permute-start.2 = (f32[32,128]{1,0:T(8,128)S(1)}, f32[32,128]{1,0:T(8,128)S(1)}, u32[]{:S(2)}, u32[]{:S(2)}) collective-permute-start(f32[32,128]{1,0:T(8,128)S(1)} %get-tuple-element.55), channel_id=1, source_target_pairs={{0,1},{1,0},{2,3},{3,2},{4,5},{5,4},{6,7},{7,6},{8,9},{9,8},{10,11... | collective-permute-start | bytes 49160 | tf_op jit(solution)/shard_map/ppermute | solution.py:673
  8.1 2.6 %collective-permute-start.3 = (f32[32,128]{1,0:T(8,128)S(1)}, f32[32,128]{1,0:T(8,128)S(1)}, u32[]{:S(2)}, u32[]{:S(2)}) collective-permute-start(f32[32,128]{1,0:T(8,128)S(1)} %get-tuple-element.56), channel_id=1, source_target_pairs={{0,2},{1,3},{2,0},{3,1},{4,6},{5,7},{6,4},{7,5},{8,10},{9,11},{10,... | collective-permute-start | bytes 49160 | tf_op jit(solution)/shard_map/ppermute | solution.py:673
  10.7 0.2 collective-permute-start.4
  10.9 10.9 %build_inner.1 = (s32[196]{0:T(256)S(4)}, s32[195]{0:T(256)S(4)}, f32[224,128,128]{2,1,0:T(8,128)S(1)}, bf16[2,32,128,128]{3,2,1,0:T(8,128)(2,1)S(1)}, f32[3,32,...) custom-call(s32[8]{0:T(128)S(4)} %get-tuple-element.38.meta, ...), custom_call_target="tpu_custom_call" | custom-call | flops 56623104 | tf_op jit(solution)/shard_map/build_inner/pallas_call | solution.py:643
  21.9 0.0 collective-permute-done.2.rest_1_
  21.9 0.0 collective-permute-done.3.rest_2_
  21.9 0.0 collective-permute-done.4.rest_3_
  21.9 0.0 collective-permute-done.first
  21.9 0.0 collective-permute-done.1.second
  21.9 4.8 %build_outer.1 = (s32[1]{0:T(128)S(4)}, f32[230,128,128]{2,1,0:T(8,128)S(1)}, f32[32,128]{1,0:T(8,128)S(1)}, f32[32,128]{1,0:T(8,128)S(1)}, f32[32,128]{1,0:T(8,128)S(1)}, /*index=5*/f32[32,128]{1,0:T(8,128)S(1)}) custom-call(s32[8]{0:T(128)S(4)} %get-tuple-element.38.meta, s32[1480]{0:T(1024)S(4)} %get-tuple-element.39.table, ...), custom_call_target="tpu_custom_call" | custom-call | flops 58195968 | tf_op jit(solution)/shard_map/build_outer/pallas_call | solution.py:643
  26.7 4.1 %collective-permute-start.8 = (f32[32,128]{1,0:T(8,128)S(1)}, f32[32,128]{1,0:T(8,128)S(1)}, u32[]{:S(2)}, u32[]{:S(2)}) collective-permute-start(f32[32,128]{1,0:T(8,128)S(1)} %get-tuple-element.58.field.precond), channel_id=1, source_target_pairs={{0,1},{1,3},{2,4},{3,0},{4,2},{5,7},{6,8},{7,5},{8,6},{9,11},{10,1... | collective-permute-start | bytes 49160 | tf_op jit(solution)/shard_map/ppermute | solution.py:721
  30.8 1.1 %collective-permute-start.7 = (f32[32,128]{1,0:T(8,128)S(1)}, f32[32,128]{1,0:T(8,128)S(1)}, u32[]{:S(2)}, u32[]{:S(2)}) collective-permute-start(f32[32,128]{1,0:T(8,128)S(1)} %get-tuple-element.58.field.precond), channel_id=1, source_target_pairs={{0,2},{1,4},{2,3},{3,0},{4,1},{5,8},{6,7},{7,6},{8,5},{9,12},{10,1... | collective-permute-start | bytes 49160 | tf_op jit(solution)/shard_map/ppermute | solution.py:721
  31.9 1.6 %collective-permute-start.6 = (f32[32,128]{1,0:T(8,128)S(1)}, f32[32,128]{1,0:T(8,128)S(1)}, u32[]{:S(2)}, u32[]{:S(2)}) collective-permute-start(f32[32,128]{1,0:T(8,128)S(1)} %get-tuple-element.58.field.precond), channel_id=1, source_target_pairs={{0,31},{1,2},{2,1},{3,4},{4,3},{5,6},{6,5},{7,8},{8,7},{9,10},{10,... | collective-permute-start | bytes 49160 | tf_op jit(solution)/shard_map/ppermute | solution.py:721
  33.4 0.1 collective-permute-start.5
  33.6 4.4 %apply_inner.2 = (f32[32,128,128]{2,1,0:T(8,128)S(1)}, f32[256,128]{1,0:T(8,128)S(1)}) custom-call(s32[8]{0:T(128)S(4)} %get-tuple-element.38.meta, s32[1480]{0:T(1024)S(4)} %get-tuple-element.39.table, s32[196]{0:T(256)S(4)} %get-tuple-element.41.plan, s32[1]{0:T(128)S(4)} %get-tuple-element.59.again, f32[32,128]{1,0:T(8,128)S(1)} %get-tuple-element.58.field.precond, ...), custom_call_target="tpu_custom_call" | custom-call | flops 14155776 | tf_op jit(solution)/shard_map/apply_inner/pallas_call | solution.py:643
  37.9 0.0 collective-permute-done.8.rest_3_
  37.9 0.0 collective-permute-done.7.rest_2_
  37.9 0.8 %collective-permute-done.6.rest_1_ = f32[32,128]{1,0:T(8,128)S(1)} collective-permute-done((f32[32,128]{1,0:T(8,128)S(1)}, f32[32,128]{1,0:T(8,128)S(1)}, u32[]{:S(2)}, u32[]{:S(2)}) %collective-permute-start.6) | collective-permute-done | bytes 16416 | tf_op jit(solution)/shard_map/ppermute | solution.py:721
  38.8 0.0 collective-permute-done.5.rest_0_
  38.8 2.3 %apply_first.1 = (f32[32,128]{1,0:T(8,128)S(1)}, f32[32,128]{1,0:T(8,128)S(1)}) custom-call(s32[8]{0:T(128)S(4)} %get-tuple-element.38.meta, s32[1480]{0:T(1024)S(4)} %get-tuple-element.39.table, s32[196]{0:T(256)S(4)} %get-tuple-element.41.plan, s32[1]{0:T(128)S(4)} %get-tuple-element.59.again, f32[32,128]{1,0:T(8,128)S(1)} %get-tuple-element.60.diagonal, ...), custom_call_target="tpu_custom_call" | custom-call | flops 7274496 | tf_op jit(solution)/shard_map/apply_first/pallas_call | solution.py:643
  41.1 1.9 %collective-permute-start.12 = (f32[32,128]{1,0:T(8,128)S(1)}, f32[32,128]{1,0:T(8,128)S(1)}, u32[]{:S(2)}, u32[]{:S(2)}) collective-permute-start(f32[32,128]{1,0:T(8,128)S(1)} %get-tuple-element.67.field.scaled), channel_id=1, source_target_pairs={{0,1},{1,3},{2,4},{3,0},{4,2},{5,7},{6,8},{7,5},{8,6},{9,11},{10,1... | collective-permute-start | bytes 49160 | tf_op jit(solution)/shard_map/ppermute | solution.py:721
  43.0 1.6 %collective-permute-start.11 = (f32[32,128]{1,0:T(8,128)S(1)}, f32[32,128]{1,0:T(8,128)S(1)}, u32[]{:S(2)}, u32[]{:S(2)}) collective-permute-start(f32[32,128]{1,0:T(8,128)S(1)} %get-tuple-element.67.field.scaled), channel_id=1, source_target_pairs={{0,2},{1,4},{2,3},{3,0},{4,1},{5,8},{6,7},{7,6},{8,5},{9,12},{10,1... | collective-permute-start | bytes 49160 | tf_op jit(solution)/shard_map/ppermute | solution.py:721
  44.6 2.8 %collective-permute-start.10 = (f32[32,128]{1,0:T(8,128)S(1)}, f32[32,128]{1,0:T(8,128)S(1)}, u32[]{:S(2)}, u32[]{:S(2)}) collective-permute-start(f32[32,128]{1,0:T(8,128)S(1)} %get-tuple-element.67.field.scaled), channel_id=1, source_target_pairs={{0,31},{1,2},{2,1},{3,4},{4,3},{5,6},{6,5},{7,8},{8,7},{9,10},{10,... | collective-permute-start | bytes 49160 | tf_op jit(solution)/shard_map/ppermute | solution.py:721
  47.4 0.0 collective-permute-start.9
  47.4 4.4 %apply_inner.3 = (f32[32,128,128]{2,1,0:T(8,128)S(1)}, f32[256,128]{1,0:T(8,128)S(1)}) custom-call(s32[8]{0:T(128)S(4)} %get-tuple-element.38.meta, s32[1480]{0:T(1024)S(4)} %get-tuple-element.39.table, s32[196]{0:T(256)S(4)} %get-tuple-element.41.plan, s32[1]{0:T(128)S(4)} %get-tuple-element.59.again, f32[32,128]{1,0:T(8,128)S(1)} %get-tuple-element.67.field.scaled, ...), custom_call_target="tpu_custom_call" | custom-call | flops 14155776 | tf_op jit(solution)/shard_map/apply_inner/pallas_call | solution.py:643
  51.8 0.0 collective-permute-done.12.rest_3_
  51.8 0.0 collective-permute-done.11.rest_2_
  51.8 0.0 collective-permute-done.10.rest_1_
  51.8 0.0 collective-permute-done.9.rest_0_
  51.8 2.4 %apply_second.1 = (f32[32,128]{1,0:T(8,128)S(1)}, f32[8,128]{1,0:T(8,128)S(1)}) custom-call(s32[8]{0:T(128)S(4)} %get-tuple-element.38.meta, s32[1480]{0:T(1024)S(4)} %get-tuple-element.39.table, s32[196]{0:T(256)S(4)} %get-tuple-element.41.plan, s32[1]{0:T(128)S(4)} %get-tuple-element.59.again, f32[32,128]{1,0:T(8,128)S(1)} %get-tuple-element.37.source, ...), custom_call_target="tpu_custom_call" | custom-call | flops 7274496 | tf_op jit(solution)/shard_map/apply_second/pallas_call | solution.py:643
  54.2 0.3 collective-permute-start.15
  54.5 4.0 %collective-permute-start.14 = (f32[8,128]{1,0:T(8,128)S(1)}, f32[8,128]{1,0:T(8,128)S(1)}, u32[]{:S(2)}, u32[]{:S(2)}) collective-permute-start(f32[8,128]{1,0:T(8,128)S(1)} %get-tuple-element.71), channel_id=1, source_target_pairs={{0,2},{1,3},{2,0},{3,1},{4,6},{5,7},{6,4},{7,5},{8,10},{9,11},{10,... | collective-permute-start | bytes 12296 | tf_op jit(solution)/shard_map/ppermute | solution.py:748
  58.5 0.1 collective-permute-start.13
  58.6 1.1 %collective-permute-done.15 = f32[8,128]{1,0:T(8,128)S(1)} collective-permute-done((f32[8,128]{1,0:T(8,128)S(1)}, f32[8,128]{1,0:T(8,128)S(1)}, u32[]{:S(2)}, u32[]{:S(2)}) %collective-permute-start.15) | collective-permute-done | bytes 4128 | tf_op jit(solution)/shard_map/ppermute | solution.py:748
  59.7 0.4 collective-permute-done.14
  60.1 2.0 %collective-permute-done.13 = f32[8,128]{1,0:T(8,128)S(1)} collective-permute-done((f32[8,128]{1,0:T(8,128)S(1)}, f32[8,128]{1,0:T(8,128)S(1)}, u32[]{:S(2)}, u32[]{:S(2)}) %collective-permute-start.13) | collective-permute-done | bytes 4128 | tf_op jit(solution)/shard_map/ppermute | solution.py:748
  62.1 0.0 collective-permute-start.22
  62.1 0.8 %collective-permute-start.21 = (f32[8,128]{1,0:T(8,128)S(1)}, f32[8,128]{1,0:T(8,128)S(1)}, u32[]{:S(2)}, u32[]{:S(2)}) collective-permute-start(f32[8,128]{1,0:T(8,128)S(1)} %add_add_fusion.rest_0_), channel_id=1, source_target_pairs={{0,24},{4,28},{8,16},{12,20},{16,8},{20,12},{24,0},{28,4},{1,25},{... | collective-permute-start | bytes 12296 | tf_op jit(solution)/shard_map/ppermute | solution.py:748
  62.9 4.6 %collective-permute-start.20 = (f32[8,128]{1,0:T(8,128)S(1)}, f32[8,128]{1,0:T(8,128)S(1)}, u32[]{:S(2)}, u32[]{:S(2)}) collective-permute-start(f32[8,128]{1,0:T(8,128)S(1)} %add_add_fusion.rest_0_), channel_id=1, source_target_pairs={{0,20},{4,16},{8,28},{12,24},{16,4},{20,0},{24,12},{28,8},{1,21},{... | collective-permute-start | bytes 12296 | tf_op jit(solution)/shard_map/ppermute | solution.py:748
  67.4 0.0 collective-permute-start.19
  67.5 0.7 collective-permute-start.18
  68.1 0.0 collective-permute-done.22.rest_7_
  68.2 1.1 %collective-permute-start.17 = (f32[8,128]{1,0:T(8,128)S(1)}, f32[8,128]{1,0:T(8,128)S(1)}, u32[]{:S(2)}, u32[]{:S(2)}) collective-permute-start(f32[8,128]{1,0:T(8,128)S(1)} %add_add_fusion.rest_0_), channel_id=1, source_target_pairs={{0,8},{4,12},{8,0},{12,4},{16,24},{20,28},{24,16},{28,20},{1,9},{5... | collective-permute-start | bytes 12296 | tf_op jit(solution)/shard_map/ppermute | solution.py:748
  69.2 0.0 collective-permute-done.21.rest_6_
  69.3 0.1 collective-permute-start.16
  69.3 0.0 collective-permute-done.20.rest_5_
  69.3 1.7 %collective-permute-done.19.rest_4_ = f32[8,128]{1,0:T(8,128)S(1)} collective-permute-done((f32[8,128]{1,0:T(8,128)S(1)}, f32[8,128]{1,0:T(8,128)S(1)}, u32[]{:S(2)}, u32[]{:S(2)}) %collective-permute-start.19) | collective-permute-done | bytes 4128 | tf_op jit(solution)/shard_map/ppermute | solution.py:748
  71.1 0.0 collective-permute-done.18.rest_3_
  71.1 0.7 collective-permute-done.17.rest_2_
  71.8 0.0 collective-permute-done.16.rest_1_
  71.8 0.9 %finish.1 = (f32[32,128]{1,0:T(8,128)}, f32[32,128]{1,0:T(8,128)}) custom-call(f32[32,128]{1,0:T(8,128)S(1)} %get-tuple-element.37.source, f32[32,128]{1,0:T(8,128)S(1)} %get-tuple-element.58.field.precond, f32[32,128]{1,0:T(8,128)S(1)} %get-tuple-element.66.spill, f32[32,128]{1,0:T(8,128)S(1)} %get-tuple-element.67.field.scaled, ...), custom_call_target="tpu_custom_call" | custom-call | tf_op jit(solution)/shard_map/finish/pallas_call | solution.py:643
  (1 shorter events, 0.0 us)
Async XLA Ops:
  2.5 19.4 %collective-permute-start = (f32[4,32,128]{2,1,0:T(8,128)S(1)}, f32[4,32,128]{2,1,0:T(8,128)S(1)}, u32[]{:S(2)}, u32[]{:S(2)}) collective-permute-start(f32[4,32,128]{2,1,0:T(8,128)S(1)} %get-tuple-element.44), channel_id=1, source_target_pairs={{0,4},{4,0},{8,12},{12,8},{16,20},{20,16},{24,28},{28,24},{1,5},{5... | collective-permute-start | bytes 196616 | tf_op jit(solution)/shard_map/ppermute | solution.py:671
  3.0 18.9 %collective-permute-start.1 = (f32[4,32,128]{2,1,0:T(8,128)S(1)}, f32[4,32,128]{2,1,0:T(8,128)S(1)}, u32[]{:S(2)}, u32[]{:S(2)}) collective-permute-start(f32[4,32,128]{2,1,0:T(8,128)S(1)} %get-tuple-element.45), channel_id=1, source_target_pairs={{0,28},{4,8},{8,4},{12,16},{16,12},{20,24},{24,20},{28,0},{1,29},{... | collective-permute-start | bytes 196616 | tf_op jit(solution)/shard_map/ppermute | solution.py:672
  6.6 15.3 %collective-permute-start.2 = (f32[32,128]{1,0:T(8,128)S(1)}, f32[32,128]{1,0:T(8,128)S(1)}, u32[]{:S(2)}, u32[]{:S(2)}) collective-permute-start(f32[32,128]{1,0:T(8,128)S(1)} %get-tuple-element.55), channel_id=1, source_target_pairs={{0,1},{1,0},{2,3},{3,2},{4,5},{5,4},{6,7},{7,6},{8,9},{9,8},{10,11... | collective-permute-start | bytes 49160 | tf_op jit(solution)/shard_map/ppermute | solution.py:673
  8.1 13.8 %collective-permute-start.3 = (f32[32,128]{1,0:T(8,128)S(1)}, f32[32,128]{1,0:T(8,128)S(1)}, u32[]{:S(2)}, u32[]{:S(2)}) collective-permute-start(f32[32,128]{1,0:T(8,128)S(1)} %get-tuple-element.56), channel_id=1, source_target_pairs={{0,2},{1,3},{2,0},{3,1},{4,6},{5,7},{6,4},{7,5},{8,10},{9,11},{10,... | collective-permute-start | bytes 49160 | tf_op jit(solution)/shard_map/ppermute | solution.py:673
  10.7 11.2 %collective-permute-start.4 = (f32[32,128]{1,0:T(8,128)S(1)}, f32[32,128]{1,0:T(8,128)S(1)}, u32[]{:S(2)}, u32[]{:S(2)}) collective-permute-start(f32[32,128]{1,0:T(8,128)S(1)} %get-tuple-element.57), channel_id=1, source_target_pairs={{0,3},{1,2},{2,1},{3,0},{4,7},{5,6},{6,5},{7,4},{8,11},{9,10},{10,... | collective-permute-start | bytes 49160 | tf_op jit(solution)/shard_map/ppermute | solution.py:673
  26.7 11.2 %collective-permute-start.8 = (f32[32,128]{1,0:T(8,128)S(1)}, f32[32,128]{1,0:T(8,128)S(1)}, u32[]{:S(2)}, u32[]{:S(2)}) collective-permute-start(f32[32,128]{1,0:T(8,128)S(1)} %get-tuple-element.58.field.precond), channel_id=1, source_target_pairs={{0,1},{1,3},{2,4},{3,0},{4,2},{5,7},{6,8},{7,5},{8,6},{9,11},{10,1... | collective-permute-start | bytes 49160 | tf_op jit(solution)/shard_map/ppermute | solution.py:721
  30.8 7.1 %collective-permute-start.7 = (f32[32,128]{1,0:T(8,128)S(1)}, f32[32,128]{1,0:T(8,128)S(1)}, u32[]{:S(2)}, u32[]{:S(2)}) collective-permute-start(f32[32,128]{1,0:T(8,128)S(1)} %get-tuple-element.58.field.precond), channel_id=1, source_target_pairs={{0,2},{1,4},{2,3},{3,0},{4,1},{5,8},{6,7},{7,6},{8,5},{9,12},{10,1... | collective-permute-start | bytes 49160 | tf_op jit(solution)/shard_map/ppermute | solution.py:721
  31.9 6.9 %collective-permute-start.6 = (f32[32,128]{1,0:T(8,128)S(1)}, f32[32,128]{1,0:T(8,128)S(1)}, u32[]{:S(2)}, u32[]{:S(2)}) collective-permute-start(f32[32,128]{1,0:T(8,128)S(1)} %get-tuple-element.58.field.precond), channel_id=1, source_target_pairs={{0,31},{1,2},{2,1},{3,4},{4,3},{5,6},{6,5},{7,8},{8,7},{9,10},{10,... | collective-permute-start | bytes 49160 | tf_op jit(solution)/shard_map/ppermute | solution.py:721
  33.4 5.3 %collective-permute-start.5 = (f32[32,128]{1,0:T(8,128)S(1)}, f32[32,128]{1,0:T(8,128)S(1)}, u32[]{:S(2)}, u32[]{:S(2)}) collective-permute-start(f32[32,128]{1,0:T(8,128)S(1)} %get-tuple-element.58.field.precond), channel_id=1, source_target_pairs={{0,1},{1,0},{2,3},{3,2},{4,5},{5,4},{6,7},{7,6},{8,9},{9,8},{10,11... | collective-permute-start | bytes 49160 | tf_op jit(solution)/shard_map/ppermute | solution.py:721
  41.1 10.7 %collective-permute-start.12 = (f32[32,128]{1,0:T(8,128)S(1)}, f32[32,128]{1,0:T(8,128)S(1)}, u32[]{:S(2)}, u32[]{:S(2)}) collective-permute-start(f32[32,128]{1,0:T(8,128)S(1)} %get-tuple-element.67.field.scaled), channel_id=1, source_target_pairs={{0,1},{1,3},{2,4},{3,0},{4,2},{5,7},{6,8},{7,5},{8,6},{9,11},{10,1... | collective-permute-start | bytes 49160 | tf_op jit(solution)/shard_map/ppermute | solution.py:721
  43.0 8.8 %collective-permute-start.11 = (f32[32,128]{1,0:T(8,128)S(1)}, f32[32,128]{1,0:T(8,128)S(1)}, u32[]{:S(2)}, u32[]{:S(2)}) collective-permute-start(f32[32,128]{1,0:T(8,128)S(1)} %get-tuple-element.67.field.scaled), channel_id=1, source_target_pairs={{0,2},{1,4},{2,3},{3,0},{4,1},{5,8},{6,7},{7,6},{8,5},{9,12},{10,1... | collective-permute-start | bytes 49160 | tf_op jit(solution)/shard_map/ppermute | solution.py:721
  44.6 7.2 %collective-permute-start.10 = (f32[32,128]{1,0:T(8,128)S(1)}, f32[32,128]{1,0:T(8,128)S(1)}, u32[]{:S(2)}, u32[]{:S(2)}) collective-permute-start(f32[32,128]{1,0:T(8,128)S(1)} %get-tuple-element.67.field.scaled), channel_id=1, source_target_pairs={{0,31},{1,2},{2,1},{3,4},{4,3},{5,6},{6,5},{7,8},{8,7},{9,10},{10,... | collective-permute-start | bytes 49160 | tf_op jit(solution)/shard_map/ppermute | solution.py:721
  47.4 4.4 %collective-permute-start.9 = (f32[32,128]{1,0:T(8,128)S(1)}, f32[32,128]{1,0:T(8,128)S(1)}, u32[]{:S(2)}, u32[]{:S(2)}) collective-permute-start(f32[32,128]{1,0:T(8,128)S(1)} %get-tuple-element.67.field.scaled), channel_id=1, source_target_pairs={{0,1},{1,0},{2,3},{3,2},{4,5},{5,4},{6,7},{7,6},{8,9},{9,8},{10,11... | collective-permute-start | bytes 49160 | tf_op jit(solution)/shard_map/ppermute | solution.py:721
  54.2 5.4 %collective-permute-start.15 = (f32[8,128]{1,0:T(8,128)S(1)}, f32[8,128]{1,0:T(8,128)S(1)}, u32[]{:S(2)}, u32[]{:S(2)}) collective-permute-start(f32[8,128]{1,0:T(8,128)S(1)} %get-tuple-element.71), channel_id=1, source_target_pairs={{0,3},{1,2},{2,1},{3,0},{4,7},{5,6},{6,5},{7,4},{8,11},{9,10},{10,... | collective-permute-start | bytes 12296 | tf_op jit(solution)/shard_map/ppermute | solution.py:748
  54.5 5.6 %collective-permute-start.14 = (f32[8,128]{1,0:T(8,128)S(1)}, f32[8,128]{1,0:T(8,128)S(1)}, u32[]{:S(2)}, u32[]{:S(2)}) collective-permute-start(f32[8,128]{1,0:T(8,128)S(1)} %get-tuple-element.71), channel_id=1, source_target_pairs={{0,2},{1,3},{2,0},{3,1},{4,6},{5,7},{6,4},{7,5},{8,10},{9,11},{10,... | collective-permute-start | bytes 12296 | tf_op jit(solution)/shard_map/ppermute | solution.py:748
  58.5 3.6 %collective-permute-start.13 = (f32[8,128]{1,0:T(8,128)S(1)}, f32[8,128]{1,0:T(8,128)S(1)}, u32[]{:S(2)}, u32[]{:S(2)}) collective-permute-start(f32[8,128]{1,0:T(8,128)S(1)} %get-tuple-element.71), channel_id=1, source_target_pairs={{0,1},{1,0},{2,3},{3,2},{4,5},{5,4},{6,7},{7,6},{8,9},{9,8},{10,11... | collective-permute-start | bytes 12296 | tf_op jit(solution)/shard_map/ppermute | solution.py:748
  62.1 6.0 %collective-permute-start.22 = (f32[8,128]{1,0:T(8,128)S(1)}, f32[8,128]{1,0:T(8,128)S(1)}, u32[]{:S(2)}, u32[]{:S(2)}) collective-permute-start(f32[8,128]{1,0:T(8,128)S(1)} %add_add_fusion.rest_0_), channel_id=1, source_target_pairs={{0,28},{4,24},{8,20},{12,16},{16,12},{20,8},{24,4},{28,0},{1,29},{... | collective-permute-start | bytes 12296 | tf_op jit(solution)/shard_map/ppermute | solution.py:748
  62.1 7.1 %collective-permute-start.21 = (f32[8,128]{1,0:T(8,128)S(1)}, f32[8,128]{1,0:T(8,128)S(1)}, u32[]{:S(2)}, u32[]{:S(2)}) collective-permute-start(f32[8,128]{1,0:T(8,128)S(1)} %add_add_fusion.rest_0_), channel_id=1, source_target_pairs={{0,24},{4,28},{8,16},{12,20},{16,8},{20,12},{24,0},{28,4},{1,25},{... | collective-permute-start | bytes 12296 | tf_op jit(solution)/shard_map/ppermute | solution.py:748
  62.9 6.4 %collective-permute-start.20 = (f32[8,128]{1,0:T(8,128)S(1)}, f32[8,128]{1,0:T(8,128)S(1)}, u32[]{:S(2)}, u32[]{:S(2)}) collective-permute-start(f32[8,128]{1,0:T(8,128)S(1)} %add_add_fusion.rest_0_), channel_id=1, source_target_pairs={{0,20},{4,16},{8,28},{12,24},{16,4},{20,0},{24,12},{28,8},{1,21},{... | collective-permute-start | bytes 12296 | tf_op jit(solution)/shard_map/ppermute | solution.py:748
  67.4 3.6 %collective-permute-start.19 = (f32[8,128]{1,0:T(8,128)S(1)}, f32[8,128]{1,0:T(8,128)S(1)}, u32[]{:S(2)}, u32[]{:S(2)}) collective-permute-start(f32[8,128]{1,0:T(8,128)S(1)} %add_add_fusion.rest_0_), channel_id=1, source_target_pairs={{0,16},{4,20},{8,24},{12,28},{16,0},{20,4},{24,8},{28,12},{1,17},{... | collective-permute-start | bytes 12296 | tf_op jit(solution)/shard_map/ppermute | solution.py:748
  67.5 3.6 %collective-permute-start.18 = (f32[8,128]{1,0:T(8,128)S(1)}, f32[8,128]{1,0:T(8,128)S(1)}, u32[]{:S(2)}, u32[]{:S(2)}) collective-permute-start(f32[8,128]{1,0:T(8,128)S(1)} %add_add_fusion.rest_0_), channel_id=1, source_target_pairs={{0,12},{4,8},{8,4},{12,0},{16,28},{20,24},{24,20},{28,16},{1,13},{... | collective-permute-start | bytes 12296 | tf_op jit(solution)/shard_map/ppermute | solution.py:748
  68.2 3.6 %collective-permute-start.17 = (f32[8,128]{1,0:T(8,128)S(1)}, f32[8,128]{1,0:T(8,128)S(1)}, u32[]{:S(2)}, u32[]{:S(2)}) collective-permute-start(f32[8,128]{1,0:T(8,128)S(1)} %add_add_fusion.rest_0_), channel_id=1, source_target_pairs={{0,8},{4,12},{8,0},{12,4},{16,24},{20,28},{24,16},{28,20},{1,9},{5... | collective-permute-start | bytes 12296 | tf_op jit(solution)/shard_map/ppermute | solution.py:748
  69.3 2.5 %collective-permute-start.16 = (f32[8,128]{1,0:T(8,128)S(1)}, f32[8,128]{1,0:T(8,128)S(1)}, u32[]{:S(2)}, u32[]{:S(2)}) collective-permute-start(f32[8,128]{1,0:T(8,128)S(1)} %add_add_fusion.rest_0_), channel_id=1, source_target_pairs={{0,4},{4,0},{8,12},{12,8},{16,20},{20,16},{24,28},{28,24},{1,5},{5... | collective-permute-start | bytes 12296 | tf_op jit(solution)/shard_map/ppermute | solution.py:748

commit v10 on v9

--- a/solution.py
+++ b/solution.py
@@ -194,10 +194,10 @@
     return jnp.concatenate([first, first, last, jnp.zeros((HALF - 6 * SUB, size.shape[1]), jnp.bfloat16)], 0)
 
 
-GROUP = 8
-
-
-def flat_tiles(count, runs, most, table, sides, middles, weights, other_at, ahead, tiles, rows_ref, cols_ref):
+GROUP = 4
+
+
+def flat_tiles(count, runs, most, table, sides, middles, weights, other_at, buffers, tiles, rows_ref, cols_ref):
     share, width = rows_ref.shape[0] - 1, rows_ref.shape[2]
     chunks = pieces_of(width)
 
@@ -215,7 +215,7 @@
         here = pl.ds(a, 1)
         return other_side([wide(other_at(c, n)) - wide(middles[c, here, :]) for c in range(3)])
 
-    def products(found):
+    def products(found, ahead):
         none = jnp.zeros((HALF, width), jnp.bfloat16)
         for k in range(0, GROUP, 2):
             (a, n), (b, m) = ((jnp.minimum(a, share - 1), n) for a, n in found[k : k + 2])
@@ -227,9 +227,7 @@
             ahead[k] = both[:, :width]
             ahead[k + 1] = both[:, width:]
 
-    def turn(i, carry):
-        state, found = carry
-        state, later = steps(state)
+    def weigh(at, found, ahead):
         for k, (a, n) in enumerate(found):
             alone = a == n
             row = jnp.where(alone, share, a)
@@ -241,19 +239,28 @@
                 rest = jnp.maximum(left, 0.0)
                 inverse = pltpu.reciprocal((1.01 - left) * (weights[own, here, :] + other), approx=True)
                 tile = rest * rest * inverse
-                tiles[i * GROUP + k, here, :] = tile
+                tiles[at + k, here, :] = tile
                 rows_ref[row, here, :] = rows_ref[row, here, :] + tile
                 if cols_ref is not None:
                     gather(down, c, tile)
             if cols_ref is not None:
                 there = pl.ds(pl.multiple_of(jnp.where(alone, share, n) * SUB, SUB), SUB)
                 cols_ref[there, :] = cols_ref[there, :] + tree(down)
-        products(later)
-        return state, later
+
+    def turn(i, carry):
+        state, found = carry
+        at = i * (2 * GROUP)
+        state, later = steps(state)
+        products(later, buffers[1])
+        weigh(at, found, buffers[0])
+        state, last = steps(state)
+        products(last, buffers[0])
+        weigh(at + GROUP, later, buffers[1])
+        return state, last
 
     state, found = steps((jnp.int32(0), jnp.int32(0)))
-    products(found)
-    lax.fori_loop(0, lax.div(count + (GROUP - 1), GROUP), turn, (state, found))
+    products(found, buffers[0])
+    lax.fori_loop(0, lax.div(count + (2 * GROUP - 1), 2 * GROUP), turn, (state, found))
 
 
 def spread_columns(out, index, rows):
@@ -346,7 +353,7 @@
 
 def build_inner(
     meta, table, near, plan, outer_runs, tiles, sides, middles, weights, rows_out, cols_out, self_ref,
-    inner_runs, rows_ref, cols_ref, ahead,
+    inner_runs, rows_ref, cols_ref, *buffers,
 ):
     share, width = rows_out.shape[0], rows_out.shape[2]
     chunks = pieces_of(width)
@@ -354,19 +361,23 @@
     for k in range(3):
         first = near[k, 0:share, 0:1]
         middles[k] = jnp.broadcast_to(jnp.floor(first) + 0.5, (share, width))
-    for a in range(share):
-        here = slice(a, a + 1)
-        side = own_side([wide(near[k, here, :] - middles[k, here, :]) for k in range(3)])
-        none = jnp.zeros((width - HALF, width), jnp.float32)
-        sides[0, a] = jnp.concatenate([side, none], 0).T.astype(jnp.bfloat16)
-        sides[1, a] = jnp.concatenate([none, side], 0).T.astype(jnp.bfloat16)
+    low = lax.broadcasted_iota(jnp.int32, (width, width), 1) < HALF
+    for a in range(0, share, 2):
+        pair = []
+        for b in (a, a + 1):
+            here = slice(b, b + 1)
+            pair.append(own_side([wide(near[k, here, :] - middles[k, here, :]) for k in range(3)]))
+        turned = jnp.concatenate(pair, 0).T
+        moved = pltpu.roll(turned, HALF, 1)
+        for at, b, half, side in ((0, a, low, turned), (1, a, ~low, moved), (0, a + 1, low, moved), (1, a + 1, ~low, turned)):
+            sides[at, b] = jnp.where(half, side, 0.0).astype(jnp.bfloat16)
     spread_columns(weights, lambda a: a, near[3, 0:share, :])
     cols_ref[...] = jnp.zeros_like(cols_ref)
     rows_ref[...] = jnp.zeros_like(rows_ref)
     count = plan[share * FIELDS]
     flat_tiles(
         count, inner_runs, plan[share * FIELDS + 2], table, sides, middles, weights,
-        lambda k, n: near[k, pl.ds(n, 1), :], ahead, tiles, rows_ref, cols_ref,
+        lambda k, n: near[k, pl.ds(n, 1), :], buffers, tiles, rows_ref, cols_ref,
     )
     finish_tiles(tiles, count)
     lane = lax.broadcasted_iota(jnp.int32, (SUB, width), 1)
@@ -402,11 +413,15 @@
         run(True)
 
 
+TAIL = 12
+
+
 def build_outer(
     meta, table, plan, runs, around, first, second, density, source, tiles_in, sides, middles, weights,
     rows_ref, cols_ref, self_ref, *rest
 ):
-    *times_in, again_ref, tiles, diagonal_ref, precond_ref, times, alone_ref, hood, work, sums_ref, extra, ahead = rest
+    times_in, rest = rest[: -TAIL], rest[-TAIL:]
+    again_ref, tiles, diagonal_ref, precond_ref, times, alone_ref, hood, work, sums_ref, extra, *buffers = rest
     share, width = diagonal_ref.shape
     base, filled = meta[3], meta[4]
     even = lax.rem(lax.axis_index("piece"), 2) == 0
@@ -426,7 +441,7 @@
     count = plan[share * FIELDS + 1]
     flat_tiles(
         count, runs, plan[share * FIELDS + 3], table, sides, middles, weights,
-        lambda k, n: hood[k, pl.ds(base + share + n, 1), :], ahead, tiles, work, None,
+        lambda k, n: hood[k, pl.ds(base + share + n, 1), :], buffers, tiles, work, None,
     )
     finish_tiles(tiles, count)
     sums_ref[...] = lane_sums([rows_ref[a] + work[a] for a in range(share)], share, width) + sub_sums(cols_ref)
@@ -631,8 +646,8 @@
     few = jax.ShapeDtypeStruct((SUB, width), f32)
     message = jax.ShapeDtypeStruct((4, share, width), f32)
     most_inner, most_outer = tile_bounds(share)
-    inner_tiles = pltpu.VMEM((most_inner + GROUP, width, width), f32)
-    outer_tiles = pltpu.VMEM((most_outer + GROUP, width, width), f32)
+    inner_tiles = pltpu.VMEM((most_inner + 2 * GROUP, width, width), f32)
+    outer_tiles = pltpu.VMEM((most_outer + 2 * GROUP, width, width), f32)
     ahead = pltpu.VMEM((GROUP, width, width), f32)
     square_more = pltpu.VMEM((share + 1, width, width), f32)
     square = pltpu.VMEM((share, width, width), f32)
@@ -669,7 +684,11 @@
     )
     meta, table = (pltpu.with_memory_space_constraint(array, pltpu.SMEM) for array in (meta, table))
     first = lax.ppermute(first, "piece", [(i, i ^ 1) for i in range(pieces)])
-    second = lax.ppermute(second, "piece", [(i, ((i ^ 1) + (1 if i % 2 else -1) * 2) % pieces) for i in range(pieces)])
+    axes = ("piece", "col")
+    device = [(p, c) for p in range(pieces) for c in range(columns)]
+    partner = [(p + (1 if p % 2 else -1), c) for p, c in device]
+    partner = [(q, d) if 0 <= q < pieces else (p, c ^ 1) for (q, d), (p, c) in zip(partner, device)]
+    second = lax.ppermute(second, axes, [(i, q * columns + d) for i, (q, d) in enumerate(partner)])
     times = [lax.ppermute(t, "col", [(i, i ^ k) for i in range(columns)]) if k else t for k, t in enumerate(times)]
 
     plan, runs, tiles_in, sides, middles, weights, rows, cols, selfs = call(
@@ -677,7 +696,7 @@
         (meta, table, near),
         [pltpu.SMEM((share * FIELDS + 4,), jnp.int32), pltpu.SMEM((6 * share + 3,), jnp.int32), inner_tiles,
          pltpu.VMEM((2, share, width, width), jnp.bfloat16), pltpu.VMEM((3, share, width), f32), square, square, narrow, narrow],
-        [pltpu.SMEM((3 * share + 3,), jnp.int32), square_more, pltpu.VMEM(((share + 1) * SUB, width), f32), ahead],
+        [pltpu.SMEM((3 * share + 3,), jnp.int32), square_more, pltpu.VMEM(((share + 1) * SUB, width), f32), ahead, ahead],
         16 * most_inner,
     )
     plan, runs = (pltpu.with_memory_space_constraint(array, pltpu.SMEM) for array in (plan, runs))
@@ -687,7 +706,7 @@
          held(tiles_in), held(sides), held(middles), held(weights), held(rows), held(cols), held(selfs), *times),
         [pltpu.SMEM((1,), jnp.int32), outer_tiles, vector, vector, vector, vector],
         [pltpu.VMEM((4, capacity + 2 * share, width), f32), square_more]
-        + [pltpu.VMEM((share, width), f32)] * 2 + [ahead],
+        + [pltpu.VMEM((share, width), f32)] * 2 + [ahead, ahead],
         16 * most_outer,
         scalars=4,
     )
@@ -705,7 +724,6 @@
         )
 
     def exchange(field):
-        axes = ("piece", "col")
         count = pieces * columns
         swaps = [[i ^ 1 for i in range(count)], [i - 1 if i % 2 == 0 else i + 1 for i in range(count)]]
         swaps[1][0], swaps[1][-1] = count - 1, 0
@@ -750,11 +768,12 @@
     def together(values, axis, low, size):
         return tree([values] + [swap(values, axis, low * k) for k in range(1, size)])
 
+    sums = together(sums, "piece", 1, 2)
     sums = together(sums, "col", 1, columns)
-    step = 1
-    while pieces // step > 8:
-        sums = together(sums, "piece", step, 8)
-        step *= 8
+    step = 2
+    while pieces // step > 4:
+        sums = together(sums, "piece", step, 4)
+        step *= 4
     others = [swap(sums, "piece", step * k) for k in range(1, pieces // step)]
 
     return tuple(call(

time: 72.6 us -> 70.1 us (0.966)
  starting transfers between devices: 33.3 us -> 30.6 us
    ppermute x10 -> x7, starting transfers between devices: 11.6 us -> 10.6 us  [swap(): lax.ppermute(values, axis, [(i, i ^ step) for i in range(lax.axis_size(ax...]
    ppermute x1, starting transfers between devices: 3.55 us -> 2.65 us  [body(): lax.ppermute(second, axes, [(i, q * columns + d) for i, (q, d) in enumera...]
    ppermute x10 -> x7, waiting for transfers between devices: 5.9 us -> 5.88 us  [swap(): lax.ppermute(values, axis, [(i, i ^ step) for i in range(lax.axis_size(ax...]
  transfers between devices with their start and end apart: 23 -> 20, of which waited for: 6 -> 7; matrix products, arithmetic and copies ran while one was open for 0% -> 0% of each run, Pallas kernels for 27% -> 28%
where the time goes in v10:
time: 70.1 us; the launch traced here: 70.2 us
  Pallas kernels  31.6 us (45%)
  starting transfers between devices  30.6 us (44%)
  waiting for transfers between devices  7.11 us (10%)
  between operations  0.76 us (1%)
    pallas_call x8, Pallas kernels, call(): pl.pallas_call(kernel, out_shape=outs, in_specs=[SMEM] * scalars + [HBM]...  31.6 us
    ppermute x8, starting transfers between devices, exchange(): return [lax.ppermute(field, axes, list(enumerate(to))) for to in swaps]  12.5 us
    ppermute x7, starting transfers between devices, swap(): lax.ppermute(values, axis, [(i, i ^ step) for i in range(lax.axis_size(ax...  10.6 us
    ppermute x7, waiting for transfers between devices, swap(): lax.ppermute(values, axis, [(i, i ^ step) for i in range(lax.axis_size(ax...  5.88 us
    ppermute x3, starting transfers between devices, body(): lax.ppermute(t, 'col', [(i, i ^ k) for i in range(columns)])  4.39 us
    ppermute x1, starting transfers between devices, body(): lax.ppermute(second, axes, [(i, q * columns + d) for i, (q, d) in enumera...  2.65 us
  transfers between devices with their start and end apart: 20, of which 7 were waited for; matrix products, arithmetic and copies ran while one was open for 0% of the time, Pallas kernels for 28%

profile of v10, /device:TPU:0, one launch (start us, length us, event | category | flops | bytes accessed | tf_op | source)
XLA Modules:
  0.0 70.2 jit_solution(15062432146105236821)
XLA Ops:
  0.6 1.8 %prepare.1 = (s32[8]{0:T(128)S(4)}, s32[1480]{0:T(1024)S(4)}, f32[4,192,128]{2,1,0:T(8,128)S(1)}, f32[4,64,128]{2,1,0:T(8,128)S(1)}, f32[32,128]{1,0:T(8,128)S(1...) custom-call(s32[8]{0:T(128)} %counts.1, ...), custom_call_target="tpu_custom_call" | custom-call | tf_op jit(solution)/shard_map/prepare/pallas_call | solution.py:658
  2.5 0.5 collective-permute-start
  3.0 2.6 %collective-permute-start.1 = (f32[4,32,128]{2,1,0:T(8,128)S(1)}, f32[4,32,128]{2,1,0:T(8,128)S(1)}, u32[]{:S(2)}, u32[]{:S(2)}) collective-permute-start(f32[4,32,128]{2,1,0:T(8,128)S(1)} %get-tuple-element.45), channel_id=1, source_target_pairs={{0,1},{1,0},{2,3},{3,2},{4,8},{5,9},{6,10},{7,11},{8,4},{9,5},{10,... | collective-permute-start | bytes 196616 | tf_op jit(solution)/shard_map/ppermute | solution.py:691
  5.7 0.1 collective-permute-start.2
  5.7 3.0 %collective-permute-start.3 = (f32[32,128]{1,0:T(8,128)S(1)}, f32[32,128]{1,0:T(8,128)S(1)}, u32[]{:S(2)}, u32[]{:S(2)}) collective-permute-start(f32[32,128]{1,0:T(8,128)S(1)} %get-tuple-element.56), channel_id=1, source_target_pairs={{0,2},{1,3},{2,0},{3,1},{4,6},{5,7},{6,4},{7,5},{8,10},{9,11},{10,... | collective-permute-start | bytes 49160 | tf_op jit(solution)/shard_map/ppermute | solution.py:692
  8.7 1.3 %collective-permute-start.4 = (f32[32,128]{1,0:T(8,128)S(1)}, f32[32,128]{1,0:T(8,128)S(1)}, u32[]{:S(2)}, u32[]{:S(2)}) collective-permute-start(f32[32,128]{1,0:T(8,128)S(1)} %get-tuple-element.57), channel_id=1, source_target_pairs={{0,3},{1,2},{2,1},{3,0},{4,7},{5,6},{6,5},{7,4},{8,11},{9,10},{10,... | collective-permute-start | bytes 49160 | tf_op jit(solution)/shard_map/ppermute | solution.py:692
  10.0 10.9 %build_inner.1 = (s32[196]{0:T(256)S(4)}, s32[195]{0:T(256)S(4)}, f32[224,128,128]{2,1,0:T(8,128)S(1)}, bf16[2,32,128,128]{3,2,1,0:T(8,128)(2,1)S(1)}, f32[3,32,...) custom-call(s32[8]{0:T(128)S(4)} %get-tuple-element.38.meta, ...), custom_call_target="tpu_custom_call" | custom-call | flops 56623104 | tf_op jit(solution)/shard_map/build_inner/pallas_call | solution.py:658
  20.9 0.0 collective-permute-done.2.rest_1_
  20.9 0.0 collective-permute-done.3.rest_2_
  20.9 0.0 collective-permute-done.4.rest_3_
  20.9 0.0 collective-permute-done.first
  20.9 0.0 collective-permute-done.1.second
  21.0 4.6 %build_outer.1 = (s32[1]{0:T(128)S(4)}, f32[230,128,128]{2,1,0:T(8,128)S(1)}, f32[32,128]{1,0:T(8,128)S(1)}, f32[32,128]{1,0:T(8,128)S(1)}, f32[32,128]{1,0:T(8,128)S(1)}, /*index=5*/f32[32,128]{1,0:T(8,128)S(1)}) custom-call(s32[8]{0:T(128)S(4)} %get-tuple-element.38.meta, s32[1480]{0:T(1024)S(4)} %get-tuple-element.39.table, ...), custom_call_target="tpu_custom_call" | custom-call | flops 58195968 | tf_op jit(solution)/shard_map/build_outer/pallas_call | solution.py:658
  25.6 3.5 %collective-permute-start.8 = (f32[32,128]{1,0:T(8,128)S(1)}, f32[32,128]{1,0:T(8,128)S(1)}, u32[]{:S(2)}, u32[]{:S(2)}) collective-permute-start(f32[32,128]{1,0:T(8,128)S(1)} %get-tuple-element.58.field.precond), channel_id=1, source_target_pairs={{0,1},{1,3},{2,4},{3,0},{4,2},{5,7},{6,8},{7,5},{8,6},{9,11},{10,1... | collective-permute-start | bytes 49160 | tf_op jit(solution)/shard_map/ppermute | solution.py:739
  29.0 1.6 %collective-permute-start.7 = (f32[32,128]{1,0:T(8,128)S(1)}, f32[32,128]{1,0:T(8,128)S(1)}, u32[]{:S(2)}, u32[]{:S(2)}) collective-permute-start(f32[32,128]{1,0:T(8,128)S(1)} %get-tuple-element.58.field.precond), channel_id=1, source_target_pairs={{0,2},{1,4},{2,3},{3,0},{4,1},{5,8},{6,7},{7,6},{8,5},{9,12},{10,1... | collective-permute-start | bytes 49160 | tf_op jit(solution)/shard_map/ppermute | solution.py:739
  30.6 1.7 %collective-permute-start.6 = (f32[32,128]{1,0:T(8,128)S(1)}, f32[32,128]{1,0:T(8,128)S(1)}, u32[]{:S(2)}, u32[]{:S(2)}) collective-permute-start(f32[32,128]{1,0:T(8,128)S(1)} %get-tuple-element.58.field.precond), channel_id=1, source_target_pairs={{0,31},{1,2},{2,1},{3,4},{4,3},{5,6},{6,5},{7,8},{8,7},{9,10},{10,... | collective-permute-start | bytes 49160 | tf_op jit(solution)/shard_map/ppermute | solution.py:739
  32.3 0.2 collective-permute-start.5
  32.5 4.4 %apply_inner.2 = (f32[32,128,128]{2,1,0:T(8,128)S(1)}, f32[256,128]{1,0:T(8,128)S(1)}) custom-call(s32[8]{0:T(128)S(4)} %get-tuple-element.38.meta, s32[1480]{0:T(1024)S(4)} %get-tuple-element.39.table, s32[196]{0:T(256)S(4)} %get-tuple-element.41.plan, s32[1]{0:T(128)S(4)} %get-tuple-element.59.again, f32[32,128]{1,0:T(8,128)S(1)} %get-tuple-element.58.field.precond, ...), custom_call_target="tpu_custom_call" | custom-call | flops 14155776 | tf_op jit(solution)/shard_map/apply_inner/pallas_call | solution.py:658
  36.8 0.0 collective-permute-done.8.rest_3_
  36.8 0.0 collective-permute-done.7.rest_2_
  36.9 0.5 collective-permute-done.6.rest_1_
  37.4 0.0 collective-permute-done.5.rest_0_
  37.4 2.3 %apply_first.1 = (f32[32,128]{1,0:T(8,128)S(1)}, f32[32,128]{1,0:T(8,128)S(1)}) custom-call(s32[8]{0:T(128)S(4)} %get-tuple-element.38.meta, s32[1480]{0:T(1024)S(4)} %get-tuple-element.39.table, s32[196]{0:T(256)S(4)} %get-tuple-element.41.plan, s32[1]{0:T(128)S(4)} %get-tuple-element.59.again, f32[32,128]{1,0:T(8,128)S(1)} %get-tuple-element.60.diagonal, ...), custom_call_target="tpu_custom_call" | custom-call | flops 7274496 | tf_op jit(solution)/shard_map/apply_first/pallas_call | solution.py:658
  39.7 2.2 %collective-permute-start.12 = (f32[32,128]{1,0:T(8,128)S(1)}, f32[32,128]{1,0:T(8,128)S(1)}, u32[]{:S(2)}, u32[]{:S(2)}) collective-permute-start(f32[32,128]{1,0:T(8,128)S(1)} %get-tuple-element.67.field.scaled), channel_id=1, source_target_pairs={{0,1},{1,3},{2,4},{3,0},{4,2},{5,7},{6,8},{7,5},{8,6},{9,11},{10,1... | collective-permute-start | bytes 49160 | tf_op jit(solution)/shard_map/ppermute | solution.py:739
  41.8 1.7 %collective-permute-start.11 = (f32[32,128]{1,0:T(8,128)S(1)}, f32[32,128]{1,0:T(8,128)S(1)}, u32[]{:S(2)}, u32[]{:S(2)}) collective-permute-start(f32[32,128]{1,0:T(8,128)S(1)} %get-tuple-element.67.field.scaled), channel_id=1, source_target_pairs={{0,2},{1,4},{2,3},{3,0},{4,1},{5,8},{6,7},{7,6},{8,5},{9,12},{10,1... | collective-permute-start | bytes 49160 | tf_op jit(solution)/shard_map/ppermute | solution.py:739
  43.5 1.6 %collective-permute-start.10 = (f32[32,128]{1,0:T(8,128)S(1)}, f32[32,128]{1,0:T(8,128)S(1)}, u32[]{:S(2)}, u32[]{:S(2)}) collective-permute-start(f32[32,128]{1,0:T(8,128)S(1)} %get-tuple-element.67.field.scaled), channel_id=1, source_target_pairs={{0,31},{1,2},{2,1},{3,4},{4,3},{5,6},{6,5},{7,8},{8,7},{9,10},{10,... | collective-permute-start | bytes 49160 | tf_op jit(solution)/shard_map/ppermute | solution.py:739
  45.1 0.1 collective-permute-start.9
  45.2 4.4 %apply_inner.3 = (f32[32,128,128]{2,1,0:T(8,128)S(1)}, f32[256,128]{1,0:T(8,128)S(1)}) custom-call(s32[8]{0:T(128)S(4)} %get-tuple-element.38.meta, s32[1480]{0:T(1024)S(4)} %get-tuple-element.39.table, s32[196]{0:T(256)S(4)} %get-tuple-element.41.plan, s32[1]{0:T(128)S(4)} %get-tuple-element.59.again, f32[32,128]{1,0:T(8,128)S(1)} %get-tuple-element.67.field.scaled, ...), custom_call_target="tpu_custom_call" | custom-call | flops 14155776 | tf_op jit(solution)/shard_map/apply_inner/pallas_call | solution.py:658
  49.6 0.0 collective-permute-done.12.rest_3_
  49.6 0.0 collective-permute-done.11.rest_2_
  49.6 0.7 collective-permute-done.10.rest_1_
  50.3 0.0 collective-permute-done.9.rest_0_
  50.3 2.4 %apply_second.1 = (f32[32,128]{1,0:T(8,128)S(1)}, f32[8,128]{1,0:T(8,128)S(1)}) custom-call(s32[8]{0:T(128)S(4)} %get-tuple-element.38.meta, s32[1480]{0:T(1024)S(4)} %get-tuple-element.39.table, s32[196]{0:T(256)S(4)} %get-tuple-element.41.plan, s32[1]{0:T(128)S(4)} %get-tuple-element.59.again, f32[32,128]{1,0:T(8,128)S(1)} %get-tuple-element.37.source, ...), custom_call_target="tpu_custom_call" | custom-call | flops 7274496 | tf_op jit(solution)/shard_map/apply_second/pallas_call | solution.py:658
  52.7 0.6 collective-permute-start.13
  53.4 0.8 %collective-permute-done.13 = f32[8,128]{1,0:T(8,128)S(1)} collective-permute-done((f32[8,128]{1,0:T(8,128)S(1)}, f32[8,128]{1,0:T(8,128)S(1)}, u32[]{:S(2)}, u32[]{:S(2)}) %collective-permute-start.13) | collective-permute-done | bytes 4128 | tf_op jit(solution)/shard_map/ppermute | solution.py:766
  54.2 2.7 %collective-permute-start.16 = (f32[8,128]{1,0:T(8,128)S(1)}, f32[8,128]{1,0:T(8,128)S(1)}, u32[]{:S(2)}, u32[]{:S(2)}) collective-permute-start(f32[8,128]{1,0:T(8,128)S(1)} %add.12), channel_id=1, source_target_pairs={{0,3},{1,2},{2,1},{3,0},{4,7},{5,6},{6,5},{7,4},{8,11},{9,10},{10,... | collective-permute-start | bytes 12296 | tf_op jit(solution)/shard_map/ppermute | solution.py:766
  56.9 0.5 collective-permute-start.15
  57.4 1.2 %collective-permute-start.14 = (f32[8,128]{1,0:T(8,128)S(1)}, f32[8,128]{1,0:T(8,128)S(1)}, u32[]{:S(2)}, u32[]{:S(2)}) collective-permute-start(f32[8,128]{1,0:T(8,128)S(1)} %add.12), channel_id=1, source_target_pairs={{0,1},{1,0},{2,3},{3,2},{4,5},{5,4},{6,7},{7,6},{8,9},{9,8},{10,11... | collective-permute-start | bytes 12296 | tf_op jit(solution)/shard_map/ppermute | solution.py:766
  58.6 1.0 %collective-permute-done.16 = f32[8,128]{1,0:T(8,128)S(1)} collective-permute-done((f32[8,128]{1,0:T(8,128)S(1)}, f32[8,128]{1,0:T(8,128)S(1)}, u32[]{:S(2)}, u32[]{:S(2)}) %collective-permute-start.16) | collective-permute-done | bytes 4128 | tf_op jit(solution)/shard_map/ppermute | solution.py:766
  59.6 1.8 %collective-permute-done.15 = f32[8,128]{1,0:T(8,128)S(1)} collective-permute-done((f32[8,128]{1,0:T(8,128)S(1)}, f32[8,128]{1,0:T(8,128)S(1)}, u32[]{:S(2)}, u32[]{:S(2)}) %collective-permute-start.15) | collective-permute-done | bytes 4128 | tf_op jit(solution)/shard_map/ppermute | solution.py:766
  61.4 0.0 collective-permute-done.14
  61.4 2.5 %collective-permute-start.19 = (f32[8,128]{1,0:T(8,128)S(1)}, f32[8,128]{1,0:T(8,128)S(1)}, u32[]{:S(2)}, u32[]{:S(2)}) collective-permute-start(f32[8,128]{1,0:T(8,128)S(1)} %add_add_fusion.rest_0_), channel_id=1, source_target_pairs={{0,24},{4,28},{8,16},{12,20},{16,8},{20,12},{24,0},{28,4},{1,25},{... | collective-permute-start | bytes 12296 | tf_op jit(solution)/shard_map/ppermute | solution.py:766
  63.9 1.7 %collective-permute-start.18 = (f32[8,128]{1,0:T(8,128)S(1)}, f32[8,128]{1,0:T(8,128)S(1)}, u32[]{:S(2)}, u32[]{:S(2)}) collective-permute-start(f32[8,128]{1,0:T(8,128)S(1)} %add_add_fusion.rest_0_), channel_id=1, source_target_pairs={{0,16},{4,20},{8,24},{12,28},{16,0},{20,4},{24,8},{28,12},{1,17},{... | collective-permute-start | bytes 12296 | tf_op jit(solution)/shard_map/ppermute | solution.py:766
  65.6 1.4 %collective-permute-start.17 = (f32[8,128]{1,0:T(8,128)S(1)}, f32[8,128]{1,0:T(8,128)S(1)}, u32[]{:S(2)}, u32[]{:S(2)}) collective-permute-start(f32[8,128]{1,0:T(8,128)S(1)} %add_add_fusion.rest_0_), channel_id=1, source_target_pairs={{0,8},{4,12},{8,0},{12,4},{16,24},{20,28},{24,16},{28,20},{1,9},{5... | collective-permute-start | bytes 12296 | tf_op jit(solution)/shard_map/ppermute | solution.py:766
  67.0 0.0 collective-permute-done.19.rest_3_
  67.0 0.6 collective-permute-done.18.rest_2_
  67.6 1.7 %collective-permute-done.17.rest_1_ = f32[8,128]{1,0:T(8,128)S(1)} collective-permute-done((f32[8,128]{1,0:T(8,128)S(1)}, f32[8,128]{1,0:T(8,128)S(1)}, u32[]{:S(2)}, u32[]{:S(2)}) %collective-permute-start.17) | collective-permute-done | bytes 4128 | tf_op jit(solution)/shard_map/ppermute | solution.py:766
  69.2 0.9 %finish.1 = (f32[32,128]{1,0:T(8,128)}, f32[32,128]{1,0:T(8,128)}) custom-call(f32[32,128]{1,0:T(8,128)S(1)} %get-tuple-element.37.source, f32[32,128]{1,0:T(8,128)S(1)} %get-tuple-element.58.field.precond, f32[32,128]{1,0:T(8,128)S(1)} %get-tuple-element.66.spill, f32[32,128]{1,0:T(8,128)S(1)} %get-tuple-element.67.field.scaled, ...), custom_call_target="tpu_custom_call" | custom-call | tf_op jit(solution)/shard_map/finish/pallas_call | solution.py:658
  (2 shorter events, 0.0 us)
Async XLA Ops:
  2.5 18.5 %collective-permute-start = (f32[4,32,128]{2,1,0:T(8,128)S(1)}, f32[4,32,128]{2,1,0:T(8,128)S(1)}, u32[]{:S(2)}, u32[]{:S(2)}) collective-permute-start(f32[4,32,128]{2,1,0:T(8,128)S(1)} %get-tuple-element.44), channel_id=1, source_target_pairs={{0,4},{4,0},{8,12},{12,8},{16,20},{20,16},{24,28},{28,24},{1,5},{5... | collective-permute-start | bytes 196616 | tf_op jit(solution)/shard_map/ppermute | solution.py:686
  3.0 17.9 %collective-permute-start.1 = (f32[4,32,128]{2,1,0:T(8,128)S(1)}, f32[4,32,128]{2,1,0:T(8,128)S(1)}, u32[]{:S(2)}, u32[]{:S(2)}) collective-permute-start(f32[4,32,128]{2,1,0:T(8,128)S(1)} %get-tuple-element.45), channel_id=1, source_target_pairs={{0,1},{1,0},{2,3},{3,2},{4,8},{5,9},{6,10},{7,11},{8,4},{9,5},{10,... | collective-permute-start | bytes 196616 | tf_op jit(solution)/shard_map/ppermute | solution.py:691
  5.7 15.3 %collective-permute-start.2 = (f32[32,128]{1,0:T(8,128)S(1)}, f32[32,128]{1,0:T(8,128)S(1)}, u32[]{:S(2)}, u32[]{:S(2)}) collective-permute-start(f32[32,128]{1,0:T(8,128)S(1)} %get-tuple-element.55), channel_id=1, source_target_pairs={{0,1},{1,0},{2,3},{3,2},{4,5},{5,4},{6,7},{7,6},{8,9},{9,8},{10,11... | collective-permute-start | bytes 49160 | tf_op jit(solution)/shard_map/ppermute | solution.py:692
  5.7 15.2 %collective-permute-start.3 = (f32[32,128]{1,0:T(8,128)S(1)}, f32[32,128]{1,0:T(8,128)S(1)}, u32[]{:S(2)}, u32[]{:S(2)}) collective-permute-start(f32[32,128]{1,0:T(8,128)S(1)} %get-tuple-element.56), channel_id=1, source_target_pairs={{0,2},{1,3},{2,0},{3,1},{4,6},{5,7},{6,4},{7,5},{8,10},{9,11},{10,... | collective-permute-start | bytes 49160 | tf_op jit(solution)/shard_map/ppermute | solution.py:692
  8.7 12.2 %collective-permute-start.4 = (f32[32,128]{1,0:T(8,128)S(1)}, f32[32,128]{1,0:T(8,128)S(1)}, u32[]{:S(2)}, u32[]{:S(2)}) collective-permute-start(f32[32,128]{1,0:T(8,128)S(1)} %get-tuple-element.57), channel_id=1, source_target_pairs={{0,3},{1,2},{2,1},{3,0},{4,7},{5,6},{6,5},{7,4},{8,11},{9,10},{10,... | collective-permute-start | bytes 49160 | tf_op jit(solution)/shard_map/ppermute | solution.py:692
  25.6 11.3 %collective-permute-start.8 = (f32[32,128]{1,0:T(8,128)S(1)}, f32[32,128]{1,0:T(8,128)S(1)}, u32[]{:S(2)}, u32[]{:S(2)}) collective-permute-start(f32[32,128]{1,0:T(8,128)S(1)} %get-tuple-element.58.field.precond), channel_id=1, source_target_pairs={{0,1},{1,3},{2,4},{3,0},{4,2},{5,7},{6,8},{7,5},{8,6},{9,11},{10,1... | collective-permute-start | bytes 49160 | tf_op jit(solution)/shard_map/ppermute | solution.py:739
  29.0 7.8 %collective-permute-start.7 = (f32[32,128]{1,0:T(8,128)S(1)}, f32[32,128]{1,0:T(8,128)S(1)}, u32[]{:S(2)}, u32[]{:S(2)}) collective-permute-start(f32[32,128]{1,0:T(8,128)S(1)} %get-tuple-element.58.field.precond), channel_id=1, source_target_pairs={{0,2},{1,4},{2,3},{3,0},{4,1},{5,8},{6,7},{7,6},{8,5},{9,12},{10,1... | collective-permute-start | bytes 49160 | tf_op jit(solution)/shard_map/ppermute | solution.py:739
  30.6 6.8 %collective-permute-start.6 = (f32[32,128]{1,0:T(8,128)S(1)}, f32[32,128]{1,0:T(8,128)S(1)}, u32[]{:S(2)}, u32[]{:S(2)}) collective-permute-start(f32[32,128]{1,0:T(8,128)S(1)} %get-tuple-element.58.field.precond), channel_id=1, source_target_pairs={{0,31},{1,2},{2,1},{3,4},{4,3},{5,6},{6,5},{7,8},{8,7},{9,10},{10,... | collective-permute-start | bytes 49160 | tf_op jit(solution)/shard_map/ppermute | solution.py:739
  32.3 5.1 %collective-permute-start.5 = (f32[32,128]{1,0:T(8,128)S(1)}, f32[32,128]{1,0:T(8,128)S(1)}, u32[]{:S(2)}, u32[]{:S(2)}) collective-permute-start(f32[32,128]{1,0:T(8,128)S(1)} %get-tuple-element.58.field.precond), channel_id=1, source_target_pairs={{0,1},{1,0},{2,3},{3,2},{4,5},{5,4},{6,7},{7,6},{8,9},{9,8},{10,11... | collective-permute-start | bytes 49160 | tf_op jit(solution)/shard_map/ppermute | solution.py:739
  39.7 9.9 %collective-permute-start.12 = (f32[32,128]{1,0:T(8,128)S(1)}, f32[32,128]{1,0:T(8,128)S(1)}, u32[]{:S(2)}, u32[]{:S(2)}) collective-permute-start(f32[32,128]{1,0:T(8,128)S(1)} %get-tuple-element.67.field.scaled), channel_id=1, source_target_pairs={{0,1},{1,3},{2,4},{3,0},{4,2},{5,7},{6,8},{7,5},{8,6},{9,11},{10,1... | collective-permute-start | bytes 49160 | tf_op jit(solution)/shard_map/ppermute | solution.py:739
  41.8 7.8 %collective-permute-start.11 = (f32[32,128]{1,0:T(8,128)S(1)}, f32[32,128]{1,0:T(8,128)S(1)}, u32[]{:S(2)}, u32[]{:S(2)}) collective-permute-start(f32[32,128]{1,0:T(8,128)S(1)} %get-tuple-element.67.field.scaled), channel_id=1, source_target_pairs={{0,2},{1,4},{2,3},{3,0},{4,1},{5,8},{6,7},{7,6},{8,5},{9,12},{10,1... | collective-permute-start | bytes 49160 | tf_op jit(solution)/shard_map/ppermute | solution.py:739
  43.5 6.8 %collective-permute-start.10 = (f32[32,128]{1,0:T(8,128)S(1)}, f32[32,128]{1,0:T(8,128)S(1)}, u32[]{:S(2)}, u32[]{:S(2)}) collective-permute-start(f32[32,128]{1,0:T(8,128)S(1)} %get-tuple-element.67.field.scaled), channel_id=1, source_target_pairs={{0,31},{1,2},{2,1},{3,4},{4,3},{5,6},{6,5},{7,8},{8,7},{9,10},{10,... | collective-permute-start | bytes 49160 | tf_op jit(solution)/shard_map/ppermute | solution.py:739
  45.1 5.2 %collective-permute-start.9 = (f32[32,128]{1,0:T(8,128)S(1)}, f32[32,128]{1,0:T(8,128)S(1)}, u32[]{:S(2)}, u32[]{:S(2)}) collective-permute-start(f32[32,128]{1,0:T(8,128)S(1)} %get-tuple-element.67.field.scaled), channel_id=1, source_target_pairs={{0,1},{1,0},{2,3},{3,2},{4,5},{5,4},{6,7},{7,6},{8,9},{9,8},{10,11... | collective-permute-start | bytes 49160 | tf_op jit(solution)/shard_map/ppermute | solution.py:739
  52.7 1.5 %collective-permute-start.13 = (f32[8,128]{1,0:T(8,128)S(1)}, f32[8,128]{1,0:T(8,128)S(1)}, u32[]{:S(2)}, u32[]{:S(2)}) collective-permute-start(f32[8,128]{1,0:T(8,128)S(1)} %get-tuple-element.71), channel_id=1, source_target_pairs={{0,4},{4,0},{8,12},{12,8},{16,20},{20,16},{24,28},{28,24},{1,5},{5... | collective-permute-start | bytes 12296 | tf_op jit(solution)/shard_map/ppermute | solution.py:766
  54.2 5.4 %collective-permute-start.16 = (f32[8,128]{1,0:T(8,128)S(1)}, f32[8,128]{1,0:T(8,128)S(1)}, u32[]{:S(2)}, u32[]{:S(2)}) collective-permute-start(f32[8,128]{1,0:T(8,128)S(1)} %add.12), channel_id=1, source_target_pairs={{0,3},{1,2},{2,1},{3,0},{4,7},{5,6},{6,5},{7,4},{8,11},{9,10},{10,... | collective-permute-start | bytes 12296 | tf_op jit(solution)/shard_map/ppermute | solution.py:766
  56.9 4.5 %collective-permute-start.15 = (f32[8,128]{1,0:T(8,128)S(1)}, f32[8,128]{1,0:T(8,128)S(1)}, u32[]{:S(2)}, u32[]{:S(2)}) collective-permute-start(f32[8,128]{1,0:T(8,128)S(1)} %add.12), channel_id=1, source_target_pairs={{0,2},{1,3},{2,0},{3,1},{4,6},{5,7},{6,4},{7,5},{8,10},{9,11},{10,... | collective-permute-start | bytes 12296 | tf_op jit(solution)/shard_map/ppermute | solution.py:766
  57.4 4.0 %collective-permute-start.14 = (f32[8,128]{1,0:T(8,128)S(1)}, f32[8,128]{1,0:T(8,128)S(1)}, u32[]{:S(2)}, u32[]{:S(2)}) collective-permute-start(f32[8,128]{1,0:T(8,128)S(1)} %add.12), channel_id=1, source_target_pairs={{0,1},{1,0},{2,3},{3,2},{4,5},{5,4},{6,7},{7,6},{8,9},{9,8},{10,11... | collective-permute-start | bytes 12296 | tf_op jit(solution)/shard_map/ppermute | solution.py:766
  61.4 5.6 %collective-permute-start.19 = (f32[8,128]{1,0:T(8,128)S(1)}, f32[8,128]{1,0:T(8,128)S(1)}, u32[]{:S(2)}, u32[]{:S(2)}) collective-permute-start(f32[8,128]{1,0:T(8,128)S(1)} %add_add_fusion.rest_0_), channel_id=1, source_target_pairs={{0,24},{4,28},{8,16},{12,20},{16,8},{20,12},{24,0},{28,4},{1,25},{... | collective-permute-start | bytes 12296 | tf_op jit(solution)/shard_map/ppermute | solution.py:766
  63.9 3.6 %collective-permute-start.18 = (f32[8,128]{1,0:T(8,128)S(1)}, f32[8,128]{1,0:T(8,128)S(1)}, u32[]{:S(2)}, u32[]{:S(2)}) collective-permute-start(f32[8,128]{1,0:T(8,128)S(1)} %add_add_fusion.rest_0_), channel_id=1, source_target_pairs={{0,16},{4,20},{8,24},{12,28},{16,0},{20,4},{24,8},{28,12},{1,17},{... | collective-permute-start | bytes 12296 | tf_op jit(solution)/shard_map/ppermute | solution.py:766
  65.6 3.6 %collective-permute-start.17 = (f32[8,128]{1,0:T(8,128)S(1)}, f32[8,128]{1,0:T(8,128)S(1)}, u32[]{:S(2)}, u32[]{:S(2)}) collective-permute-start(f32[8,128]{1,0:T(8,128)S(1)} %add_add_fusion.rest_0_), channel_id=1, source_target_pairs={{0,8},{4,12},{8,0},{12,4},{16,24},{20,28},{24,16},{28,20},{1,9},{5... | collective-permute-start | bytes 12296 | tf_op jit(solution)/shard_map/ppermute | solution.py:766

commit v11 on v10

--- a/solution.py
+++ b/solution.py
@@ -287,19 +287,17 @@
 
 
 def prepare(
-    counts, densities, position_in, phase_in, listed_in, right_side_in, table_in,
-    meta, table, hood, near, density, source, first_swap, second_swap, *rest
+    counts, densities, position_in, phase_in, right_side_in, table_in,
+    meta, table, hood, near, density, source, first_swap, second_swap, phase, right_side, sems
 ):
-    *times_out, phase, listed, right_side, times, sems = rest
     share, width = source.shape
     capacity = phase.shape[0]
     body_rows = pl.ds(share, capacity)
     copies = [
         pltpu.make_async_copy(phase_in, phase, sems.at[0]),
         pltpu.make_async_copy(position_in, hood.at[pl.ds(0, 3), body_rows, :], sems.at[1]),
-        pltpu.make_async_copy(listed_in, listed, sems.at[2]),
-        pltpu.make_async_copy(right_side_in, right_side, sems.at[3]),
-        pltpu.make_async_copy(table_in, table, sems.at[4]),
+        pltpu.make_async_copy(right_side_in, right_side, sems.at[2]),
+        pltpu.make_async_copy(table_in, table, sems.at[3]),
     ]
     for copy in copies:
         copy.start()
@@ -333,17 +331,6 @@
     for copy in copies[2:]:
         copy.wait()
     source[...] = jnp.where(alive_rows(meta, share, width), right_side[...], 0.0)
-    ids = listed[...]
-    own = lax.broadcasted_iota(jnp.int32, ids.shape, 1)
-    slot = ids - piece * capacity
-    away = slot - own + jnp.where(slot < 0, capacity - filled_before, jnp.where(slot >= capacity, filled - capacity, 0))
-    away = jnp.where(ids < 0, -REACH, away) + REACH
-    steps = lax.broadcasted_iota(jnp.int32, (2 * REACH, capacity), 0)
-    found = tree([jnp.where(steps == away[k : k + 1], 1.0, 0.0) for k in range(ids.shape[0])])
-    found = jnp.concatenate([found, jnp.zeros((width - 2 * REACH, capacity), jnp.float32)], 0)
-    times[...] = found.T
-    for k, out in enumerate(times_out):
-        out[...] = times[pl.ds(pl.multiple_of((column ^ k) * share, SUB), share), :]
 
 
 def finish_tiles(tiles, end):
@@ -398,6 +385,25 @@
     cols_out[...] = cols_ref[0 : share * SUB, :]
 
 
+def count_listed(meta, lists, width):
+    capacity = lists[0].shape[1]
+    filled, filled_before = meta[4], meta[5]
+    start = lax.axis_index("piece") * capacity
+    steps = lax.broadcasted_iota(jnp.int32, (2 * REACH, capacity), 0)
+    partial = [None] * 4
+    row = 0
+    for ref in lists:
+        ids = ref[...]
+        slot = ids - start
+        gap = jnp.where(slot < 0, capacity - filled_before, jnp.where(slot >= capacity, filled - capacity, 0))
+        away = slot - lax.broadcasted_iota(jnp.int32, ids.shape, 1) + gap
+        away = jnp.where(ids < 0, -REACH, away) + REACH
+        for k in range(ids.shape[0]):
+            gather(partial, row, jnp.where(steps == away[k : k + 1], 1.0, 0.0))
+            row += 1
+    return jnp.concatenate([tree(partial), jnp.zeros((width - 2 * REACH, capacity), jnp.float32)], 0).T
+
+
 def factor(times, a, n):
     lane = lax.broadcasted_iota(jnp.int32, (1, times.shape[1]), 1)
     return jnp.sum(jnp.where(lane == n - a + REACH, times[pl.ds(a, 1), :], 0.0), axis=1, keepdims=True)
@@ -413,15 +419,15 @@
         run(True)
 
 
-TAIL = 12
+TAIL = 13
 
 
 def build_outer(
     meta, table, plan, runs, around, first, second, density, source, tiles_in, sides, middles, weights,
     rows_ref, cols_ref, self_ref, *rest
 ):
-    times_in, rest = rest[: -TAIL], rest[-TAIL:]
-    again_ref, tiles, diagonal_ref, precond_ref, times, alone_ref, hood, work, sums_ref, extra, *buffers = rest
+    lists, rest = rest[:-TAIL], rest[-TAIL:]
+    again_ref, tiles, diagonal_ref, precond_ref, times, alone_ref, hood, work, sums_ref, extra, all_times, *buffers = rest
     share, width = diagonal_ref.shape
     base, filled = meta[3], meta[4]
     even = lax.rem(lax.axis_index("piece"), 2) == 0
@@ -430,7 +436,8 @@
         hood[k, share:, :] = around[k, share:, :]
         hood[k, pl.ds(share + filled, share), :] = jnp.where(even, first[k], second[k])
     alive = alive_rows(meta, share, width)
-    often = jnp.where(alive, tree([ref[...] for ref in times_in]), 0.0)
+    all_times[...] = count_listed(meta, lists, width)
+    often = jnp.where(alive, all_times[pl.ds(pl.multiple_of(base, SUB), share), :], 0.0)
     times[...] = often
     lane = lax.broadcasted_iota(jnp.int32, (share, width), 1)
     again = jnp.max(jnp.where((lane == REACH) | (lane == 0), 0.0, often)) > 1.5
@@ -667,19 +674,26 @@
             **more,
         )(*args)
 
+    def swap(values, axis, step):
+        return lax.ppermute(values, axis, [(i, i ^ step) for i in range(lax.axis_size(axis))])
+
+    col_steps = [(1 << k) | 1 for k in range(columns.bit_length() - 1)]
+    lists = [neighbours.T]
+    for step in col_steps:
+        known = lists[0] if len(lists) == 1 else jnp.concatenate(lists, 0)
+        lists = [known, swap(known, "col", step)]
+
     def away(array):
         return pltpu.with_memory_space_constraint(array, pltpu.HBM)
 
     around = jax.ShapeDtypeStruct((4, capacity + 2 * share, width), f32)
     near = jax.ShapeDtypeStruct((4, 2 * share, width), f32)
-    far = [away(array) for array in (positions, phase, neighbours.T, right_side, table)]
-    meta, table, around, near, density, source, first, second, *times = call(
+    far = [away(array) for array in (positions, phase, right_side, table)]
+    meta, table, around, near, density, source, first, second = call(
         prepare,
         (away(counts), away(phase_density), *far),
-        [pltpu.SMEM((8,), jnp.int32), pltpu.SMEM(table.shape, jnp.int32), around, near, vector, vector, message, message]
-        + [vector] * columns,
-        [pltpu.VMEM(phase.shape, jnp.int32), pltpu.VMEM(far[2].shape, jnp.int32), pltpu.VMEM((share, width), f32),
-         pltpu.VMEM((capacity, width), f32), pltpu.SemaphoreType.DMA((5,))],
+        [pltpu.SMEM((8,), jnp.int32), pltpu.SMEM(table.shape, jnp.int32), around, near, vector, vector, message, message],
+        [pltpu.VMEM(phase.shape, jnp.int32), pltpu.VMEM((share, width), f32), pltpu.SemaphoreType.DMA((4,))],
         far=len(far),
     )
     meta, table = (pltpu.with_memory_space_constraint(array, pltpu.SMEM) for array in (meta, table))
@@ -687,9 +701,8 @@
     axes = ("piece", "col")
     device = [(p, c) for p in range(pieces) for c in range(columns)]
     partner = [(p + (1 if p % 2 else -1), c) for p, c in device]
-    partner = [(q, d) if 0 <= q < pieces else (p, c ^ 1) for (q, d), (p, c) in zip(partner, device)]
+    partner = [(q, d) if 0 <= q < pieces else (p, c) for (q, d), (p, c) in zip(partner, device)]
     second = lax.ppermute(second, axes, [(i, q * columns + d) for i, (q, d) in enumerate(partner)])
-    times = [lax.ppermute(t, "col", [(i, i ^ k) for i in range(columns)]) if k else t for k, t in enumerate(times)]
 
     plan, runs, tiles_in, sides, middles, weights, rows, cols, selfs = call(
         build_inner,
@@ -703,10 +716,10 @@
     again, tiles_out, diagonal, precond, times, alone = call(
         build_outer,
         (meta, table, plan, runs, around, first, second, density, source,
-         held(tiles_in), held(sides), held(middles), held(weights), held(rows), held(cols), held(selfs), *times),
+         held(tiles_in), held(sides), held(middles), held(weights), held(rows), held(cols), held(selfs), *lists),
         [pltpu.SMEM((1,), jnp.int32), outer_tiles, vector, vector, vector, vector],
         [pltpu.VMEM((4, capacity + 2 * share, width), f32), square_more]
-        + [pltpu.VMEM((share, width), f32)] * 2 + [ahead, ahead],
+        + [pltpu.VMEM((share, width), f32)] * 2 + [pltpu.VMEM((capacity, width), f32), ahead, ahead],
         16 * most_outer,
         scalars=4,
     )
@@ -726,16 +739,13 @@
     def exchange(field):
         count = pieces * columns
         swaps = [[i ^ 1 for i in range(count)], [i - 1 if i % 2 == 0 else i + 1 for i in range(count)]]
-        swaps[1][0], swaps[1][-1] = count - 1, 0
+        swaps[1][0], swaps[1][-1] = 0, count - 1
         for c in range(1, columns - 1):
             to = {}
             for p in range(pieces - 1):
                 low, high = p * columns + c, (p + 1) * columns
                 to[low], to[high] = high, low
-            for p in range(pieces):
-                rest = [i for i in range(p * columns, (p + 1) * columns) if i not in to]
-                to.update(zip(rest, rest[1:] + rest[:1]))
-            swaps.append([to[i] for i in range(count)])
+            swaps.append([to.get(i, i) for i in range(count)])
         return [lax.ppermute(field, axes, list(enumerate(to))) for to in swaps]
 
     scratch = [pltpu.VMEM((share, width, width), f32), pltpu.VMEM((8 * share, width), f32)]
@@ -762,14 +772,12 @@
         scalars=4,
     )
 
-    def swap(values, axis, step):
-        return lax.ppermute(values, axis, [(i, i ^ step) for i in range(lax.axis_size(axis))])
-
     def together(values, axis, low, size):
         return tree([values] + [swap(values, axis, low * k) for k in range(1, size)])
 
     sums = together(sums, "piece", 1, 2)
-    sums = together(sums, "col", 1, columns)
+    for step in col_steps:
+        sums = sums + swap(sums, "col", step)
     step = 2
     while pieces // step > 4:
         sums = together(sums, "piece", step, 4)

time: 70.1 us -> 81.6 us (1.16)
  starting transfers between devices: 30.6 us -> 38.3 us
  waiting for transfers between devices: 7.11 us -> 9.83 us
    ppermute x8, starting transfers between devices: 12.5 us -> 23 us  [exchange(): return [lax.ppermute(field, axes, list(enumerate(to))) for to in swaps]]
    ppermute x3 -> x0, starting transfers between devices: 4.39 us -> none  [body(): lax.ppermute(t, 'col', [(i, i ^ k) for i in range(columns)])]
    ppermute x7 -> x8, starting transfers between devices: 10.6 us -> 14.5 us  [swap(): lax.ppermute(values, axis, [(i, i ^ step) for i in range(lax.axis_size(ax...]
    ppermute x7 -> x8, waiting for transfers between devices: 5.88 us -> 9.8 us  [swap(): lax.ppermute(values, axis, [(i, i ^ step) for i in range(lax.axis_size(ax...]
    ppermute x1, starting transfers between devices: 2.65 us -> 0.66 us  [body(): lax.ppermute(second, axes, [(i, q * columns + d) for i, (q, d) in enumera...]
    ppermute x8, waiting for transfers between devices: 1.21 us -> 0.02 us  [exchange(): return [lax.ppermute(field, axes, list(enumerate(to))) for to in swaps]]
  transfers between devices with their start and end apart: 20 -> 18, of which waited for: 7 -> 5; matrix products, arithmetic and copies ran while one was open for 0% -> 1% of each run, Pallas kernels for 28% -> 26%
where the time goes in v11:
time: 81.6 us; the launch traced here: 81.3 us
  starting transfers between devices  38.3 us (47%)
  Pallas kernels  31.6 us (39%)
  waiting for transfers between devices  9.83 us (12%)
  between operations  0.84 us (1%)
    pallas_call x8, Pallas kernels, call(): pl.pallas_call(kernel, out_shape=outs, in_specs=[SMEM] * scalars + [HBM]...  31.6 us
    ppermute x8, starting transfers between devices, exchange(): return [lax.ppermute(field, axes, list(enumerate(to))) for to in swaps]  23 us
    ppermute x8, starting transfers between devices, swap(): lax.ppermute(values, axis, [(i, i ^ step) for i in range(lax.axis_size(ax...  14.5 us
    ppermute x8, waiting for transfers between devices, swap(): lax.ppermute(values, axis, [(i, i ^ step) for i in range(lax.axis_size(ax...  9.8 us
  transfers between devices with their start and end apart: 18, of which 5 were waited for; matrix products, arithmetic and copies ran while one was open for 1% of the time, Pallas kernels for 26%

profile of v11, /device:TPU:0, one launch (start us, length us, event | category | flops | bytes accessed | tf_op | source)
XLA Modules:
  0.0 81.3 jit_solution(1686360342496623562)
XLA Ops:
  0.6 3.1 %collective-permute-start.2 = (s32[7,128]{1,0:T(8,128)}, s32[7,128]{1,0:T(8,128)S(1)}, u32[]{:S(2)}, u32[]{:S(2)}) collective-permute-start(s32[7,128]{1,0:T(8,128)} %bitcast.1), channel_id=1, source_target_pairs={{0,1},{1,0},{2,3},{3,2},{4,5},{5,4},{6,7},{7,6},{8,9},{9,8},{10,11... | collective-permute-start | bytes 10760 | tf_op jit(solution)/shard_map/ppermute | solution.py:678
  3.7 1.7 %prepare.1 = (s32[8]{0:T(128)S(4)}, s32[1480]{0:T(1024)S(4)}, f32[4,192,128]{2,1,0:T(8,128)S(1)}, f32[4,64,128]{2,1,0:T(8,128)S(1)}, f32[32,128]{1,0:T(8,128)S(1...) custom-call(s32[8]{0:T(128)} %counts.1, f32[3]{0:T(128)} %densities.1, ...), custom_call_target="tpu_custom_call" | custom-call | tf_op jit(solution)/shard_map/prepare/pallas_call | solution.py:665
  5.4 0.1 collective-permute-start
  5.5 0.7 collective-permute-start.1
  6.2 0.0 collective-permute-done.2
  6.2 0.7 pad_add_fusion.rest_0_
  6.9 3.4 %collective-permute-start.3 = (s32[14,128]{1,0:T(8,128)S(1)}, s32[14,128]{1,0:T(8,128)S(1)}, u32[]{:S(2)}, u32[]{:S(2)}) collective-permute-start(s32[14,128]{1,0:T(8,128)S(1)} %pad_add_fusion.rest_0_), channel_id=1, source_target_pairs={{0,3},{1,2},{2,1},{3,0},{4,7},{5,6},{6,5},{7,4},{8,11},{9,10},{10,... | collective-permute-start | bytes 21512 | tf_op jit(solution)/shard_map/ppermute | solution.py:678
  10.3 10.9 %build_inner.1 = (s32[196]{0:T(256)S(4)}, s32[195]{0:T(256)S(4)}, f32[224,128,128]{2,1,0:T(8,128)S(1)}, bf16[2,32,128,128]{3,2,1,0:T(8,128)(2,1)S(1)}, f32[3,32,...) custom-call(s32[8]{0:T(128)S(4)} %get-tuple-element.34.meta, ...), custom_call_target="tpu_custom_call" | custom-call | flops 56623104 | tf_op jit(solution)/shard_map/build_inner/pallas_call | solution.py:665
  21.1 0.0 collective-permute-done.3.rest_1_
  21.1 0.0 collective-permute-done.first
  21.1 0.0 collective-permute-done.1.second
  21.2 4.7 %build_outer.1 = (s32[1]{0:T(128)S(4)}, f32[230,128,128]{2,1,0:T(8,128)S(1)}, f32[32,128]{1,0:T(8,128)S(1)}, f32[32,128]{1,0:T(8,128)S(1)}, f32[32,128]{1,0:T(8,128)S(1)}, /*index=5*/f32[32,128]{1,0:T(8,128)S(1)}) custom-call(s32[8]{0:T(128)S(4)} %get-tuple-element.34.meta, s32[1480]{0:T(1024)S(4)} %get-tuple-element.35.table, ...), custom_call_target="tpu_custom_call" | custom-call | flops 58195968 | tf_op jit(solution)/shard_map/build_outer/pallas_call | solution.py:665
  25.8 0.7 collective-permute-start.7
  26.5 0.7 collective-permute-start.6
  27.2 0.7 collective-permute-start.5
  27.8 10.5 %collective-permute-start.4 = (f32[32,128]{1,0:T(8,128)S(1)}, f32[32,128]{1,0:T(8,128)S(1)}, u32[]{:S(2)}, u32[]{:S(2)}) collective-permute-start(f32[32,128]{1,0:T(8,128)S(1)} %get-tuple-element.50.field.precond), channel_id=1, source_target_pairs={{0,1},{1,0},{2,3},{3,2},{4,5},{5,4},{6,7},{7,6},{8,9},{9,8},{10,11... | collective-permute-start | bytes 49160 | tf_op jit(solution)/shard_map/ppermute | solution.py:749
  38.4 4.4 %apply_inner.2 = (f32[32,128,128]{2,1,0:T(8,128)S(1)}, f32[256,128]{1,0:T(8,128)S(1)}) custom-call(s32[8]{0:T(128)S(4)} %get-tuple-element.34.meta, s32[1480]{0:T(1024)S(4)} %get-tuple-element.35.table, s32[196]{0:T(256)S(4)} %get-tuple-element.37.plan, s32[1]{0:T(128)S(4)} %get-tuple-element.51.again, f32[32,128]{1,0:T(8,128)S(1)} %get-tuple-element.50.field.precond, ...), custom_call_target="tpu_custom_call" | custom-call | flops 14155776 | tf_op jit(solution)/shard_map/apply_inner/pallas_call | solution.py:665
  42.7 0.0 collective-permute-done.7.rest_3_
  42.8 0.0 collective-permute-done.6.rest_2_
  42.8 0.0 collective-permute-done.5.rest_1_
  42.8 0.0 collective-permute-done.4.rest_0_
  42.8 2.3 %apply_first.1 = (f32[32,128]{1,0:T(8,128)S(1)}, f32[32,128]{1,0:T(8,128)S(1)}) custom-call(s32[8]{0:T(128)S(4)} %get-tuple-element.34.meta, s32[1480]{0:T(1024)S(4)} %get-tuple-element.35.table, s32[196]{0:T(256)S(4)} %get-tuple-element.37.plan, s32[1]{0:T(128)S(4)} %get-tuple-element.51.again, f32[32,128]{1,0:T(8,128)S(1)} %get-tuple-element.52.diagonal, ...), custom_call_target="tpu_custom_call" | custom-call | flops 7274496 | tf_op jit(solution)/shard_map/apply_first/pallas_call | solution.py:665
  45.1 0.7 collective-permute-start.11
  45.8 0.7 collective-permute-start.10
  46.5 0.7 collective-permute-start.9
  47.1 8.5 %collective-permute-start.8 = (f32[32,128]{1,0:T(8,128)S(1)}, f32[32,128]{1,0:T(8,128)S(1)}, u32[]{:S(2)}, u32[]{:S(2)}) collective-permute-start(f32[32,128]{1,0:T(8,128)S(1)} %get-tuple-element.59.field.scaled), channel_id=1, source_target_pairs={{0,1},{1,0},{2,3},{3,2},{4,5},{5,4},{6,7},{7,6},{8,9},{9,8},{10,11... | collective-permute-start | bytes 49160 | tf_op jit(solution)/shard_map/ppermute | solution.py:749
  55.6 4.4 %apply_inner.3 = (f32[32,128,128]{2,1,0:T(8,128)S(1)}, f32[256,128]{1,0:T(8,128)S(1)}) custom-call(s32[8]{0:T(128)S(4)} %get-tuple-element.34.meta, s32[1480]{0:T(1024)S(4)} %get-tuple-element.35.table, s32[196]{0:T(256)S(4)} %get-tuple-element.37.plan, s32[1]{0:T(128)S(4)} %get-tuple-element.51.again, f32[32,128]{1,0:T(8,128)S(1)} %get-tuple-element.59.field.scaled, ...), custom_call_target="tpu_custom_call" | custom-call | flops 14155776 | tf_op jit(solution)/shard_map/apply_inner/pallas_call | solution.py:665
  60.0 0.0 collective-permute-done.11.rest_3_
  60.0 0.0 collective-permute-done.10.rest_2_
  60.0 0.0 collective-permute-done.9.rest_1_
  60.0 0.0 collective-permute-done.8.rest_0_
  60.0 2.4 %apply_second.1 = (f32[32,128]{1,0:T(8,128)S(1)}, f32[8,128]{1,0:T(8,128)S(1)}) custom-call(s32[8]{0:T(128)S(4)} %get-tuple-element.34.meta, s32[1480]{0:T(1024)S(4)} %get-tuple-element.35.table, s32[196]{0:T(256)S(4)} %get-tuple-element.37.plan, s32[1]{0:T(128)S(4)} %get-tuple-element.51.again, f32[32,128]{1,0:T(8,128)S(1)} %get-tuple-element.33.source, ...), custom_call_target="tpu_custom_call" | custom-call | flops 7274496 | tf_op jit(solution)/shard_map/apply_second/pallas_call | solution.py:665
  62.4 2.5 %collective-permute-start.12 = (f32[8,128]{1,0:T(8,128)S(1)}, f32[8,128]{1,0:T(8,128)S(1)}, u32[]{:S(2)}, u32[]{:S(2)}) collective-permute-start(f32[8,128]{1,0:T(8,128)S(1)} %get-tuple-element.63), channel_id=1, source_target_pairs={{0,4},{4,0},{8,12},{12,8},{16,20},{20,16},{24,28},{28,24},{1,5},{5... | collective-permute-start | bytes 12296 | tf_op jit(solution)/shard_map/ppermute | solution.py:678
  64.9 0.8 %collective-permute-done.12 = f32[8,128]{1,0:T(8,128)S(1)} collective-permute-done((f32[8,128]{1,0:T(8,128)S(1)}, f32[8,128]{1,0:T(8,128)S(1)}, u32[]{:S(2)}, u32[]{:S(2)}) %collective-permute-start.12) | collective-permute-done | bytes 4128 | tf_op jit(solution)/shard_map/ppermute | solution.py:678
  65.8 0.3 collective-permute-start.13
  66.1 3.3 %collective-permute-done.13 = f32[8,128]{1,0:T(8,128)S(1)} collective-permute-done((f32[8,128]{1,0:T(8,128)S(1)}, f32[8,128]{1,0:T(8,128)S(1)}, u32[]{:S(2)}, u32[]{:S(2)}) %collective-permute-start.13) | collective-permute-done | bytes 4128 | tf_op jit(solution)/shard_map/ppermute | solution.py:678
  69.4 1.8 %collective-permute-start.14 = (f32[8,128]{1,0:T(8,128)S(1)}, f32[8,128]{1,0:T(8,128)S(1)}, u32[]{:S(2)}, u32[]{:S(2)}) collective-permute-start(f32[8,128]{1,0:T(8,128)S(1)} %add.10), channel_id=1, source_target_pairs={{0,3},{1,2},{2,1},{3,0},{4,7},{5,6},{6,5},{7,4},{8,11},{9,10},{10,... | collective-permute-start | bytes 12296 | tf_op jit(solution)/shard_map/ppermute | solution.py:678
  71.2 3.6 %collective-permute-done.14 = f32[8,128]{1,0:T(8,128)S(1)} collective-permute-done((f32[8,128]{1,0:T(8,128)S(1)}, f32[8,128]{1,0:T(8,128)S(1)}, u32[]{:S(2)}, u32[]{:S(2)}) %collective-permute-start.14) | collective-permute-done | bytes 4128 | tf_op jit(solution)/shard_map/ppermute | solution.py:678
  74.8 0.0 collective-permute-start.17
  74.8 1.9 %collective-permute-start.16 = (f32[8,128]{1,0:T(8,128)S(1)}, f32[8,128]{1,0:T(8,128)S(1)}, u32[]{:S(2)}, u32[]{:S(2)}) collective-permute-start(f32[8,128]{1,0:T(8,128)S(1)} %add.11.rest_0_), channel_id=1, source_target_pairs={{0,16},{4,20},{8,24},{12,28},{16,0},{20,4},{24,8},{28,12},{1,17},{... | collective-permute-start | bytes 12296 | tf_op jit(solution)/shard_map/ppermute | solution.py:678
  76.7 1.6 %collective-permute-start.15 = (f32[8,128]{1,0:T(8,128)S(1)}, f32[8,128]{1,0:T(8,128)S(1)}, u32[]{:S(2)}, u32[]{:S(2)}) collective-permute-start(f32[8,128]{1,0:T(8,128)S(1)} %add.11.rest_0_), channel_id=1, source_target_pairs={{0,8},{4,12},{8,0},{12,4},{16,24},{20,28},{24,16},{28,20},{1,9},{5... | collective-permute-start | bytes 12296 | tf_op jit(solution)/shard_map/ppermute | solution.py:678
  78.3 1.0 %collective-permute-done.17.rest_3_ = f32[8,128]{1,0:T(8,128)S(1)} collective-permute-done((f32[8,128]{1,0:T(8,128)S(1)}, f32[8,128]{1,0:T(8,128)S(1)}, u32[]{:S(2)}, u32[]{:S(2)}) %collective-permute-start.17) | collective-permute-done | bytes 4128 | tf_op jit(solution)/shard_map/ppermute | solution.py:678
  79.3 0.0 collective-permute-done.16.rest_2_
  79.3 1.0 %collective-permute-done.15.rest_1_ = f32[8,128]{1,0:T(8,128)S(1)} collective-permute-done((f32[8,128]{1,0:T(8,128)S(1)}, f32[8,128]{1,0:T(8,128)S(1)}, u32[]{:S(2)}, u32[]{:S(2)}) %collective-permute-start.15) | collective-permute-done | bytes 4128 | tf_op jit(solution)/shard_map/ppermute | solution.py:678
  80.3 0.9 %finish.1 = (f32[32,128]{1,0:T(8,128)}, f32[32,128]{1,0:T(8,128)}) custom-call(f32[32,128]{1,0:T(8,128)S(1)} %get-tuple-element.33.source, f32[32,128]{1,0:T(8,128)S(1)} %get-tuple-element.50.field.precond, f32[32,128]{1,0:T(8,128)S(1)} %get-tuple-element.58.spill, f32[32,128]{1,0:T(8,128)S(1)} %get-tuple-element.59.field.scaled, ...), custom_call_target="tpu_custom_call" | custom-call | tf_op jit(solution)/shard_map/finish/pallas_call | solution.py:665
  (3 shorter events, 0.0 us)
Async XLA Ops:
  0.6 5.6 %collective-permute-start.2 = (s32[7,128]{1,0:T(8,128)}, s32[7,128]{1,0:T(8,128)S(1)}, u32[]{:S(2)}, u32[]{:S(2)}) collective-permute-start(s32[7,128]{1,0:T(8,128)} %bitcast.1), channel_id=1, source_target_pairs={{0,1},{1,0},{2,3},{3,2},{4,5},{5,4},{6,7},{7,6},{8,9},{9,8},{10,11... | collective-permute-start | bytes 10760 | tf_op jit(solution)/shard_map/ppermute | solution.py:678
  5.4 15.7 %collective-permute-start = (f32[4,32,128]{2,1,0:T(8,128)S(1)}, f32[4,32,128]{2,1,0:T(8,128)S(1)}, u32[]{:S(2)}, u32[]{:S(2)}) collective-permute-start(f32[4,32,128]{2,1,0:T(8,128)S(1)} %get-tuple-element.40), channel_id=1, source_target_pairs={{0,4},{4,0},{8,12},{12,8},{16,20},{20,16},{24,28},{28,24},{1,5},{5... | collective-permute-start | bytes 196616 | tf_op jit(solution)/shard_map/ppermute | solution.py:700
  5.5 15.6 %collective-permute-start.1 = (f32[4,32,128]{2,1,0:T(8,128)S(1)}, f32[4,32,128]{2,1,0:T(8,128)S(1)}, u32[]{:S(2)}, u32[]{:S(2)}) collective-permute-start(f32[4,32,128]{2,1,0:T(8,128)S(1)} %get-tuple-element.41), channel_id=1, source_target_pairs={{0,0},{1,1},{2,2},{3,3},{4,8},{5,9},{6,10},{7,11},{8,4},{9,5},{10,... | collective-permute-start | bytes 196616 | tf_op jit(solution)/shard_map/ppermute | solution.py:705
  6.9 14.2 %collective-permute-start.3 = (s32[14,128]{1,0:T(8,128)S(1)}, s32[14,128]{1,0:T(8,128)S(1)}, u32[]{:S(2)}, u32[]{:S(2)}) collective-permute-start(s32[14,128]{1,0:T(8,128)S(1)} %pad_add_fusion.rest_0_), channel_id=1, source_target_pairs={{0,3},{1,2},{2,1},{3,0},{4,7},{5,6},{6,5},{7,4},{8,11},{9,10},{10,... | collective-permute-start | bytes 21512 | tf_op jit(solution)/shard_map/ppermute | solution.py:678
  25.8 16.9 %collective-permute-start.7 = (f32[32,128]{1,0:T(8,128)S(1)}, f32[32,128]{1,0:T(8,128)S(1)}, u32[]{:S(2)}, u32[]{:S(2)}) collective-permute-start(f32[32,128]{1,0:T(8,128)S(1)} %get-tuple-element.50.field.precond), channel_id=1, source_target_pairs={{0,0},{1,1},{2,4},{3,3},{4,2},{5,5},{6,8},{7,7},{8,6},{9,9},{10,12... | collective-permute-start | bytes 49160 | tf_op jit(solution)/shard_map/ppermute | solution.py:749
  26.5 16.3 %collective-permute-start.6 = (f32[32,128]{1,0:T(8,128)S(1)}, f32[32,128]{1,0:T(8,128)S(1)}, u32[]{:S(2)}, u32[]{:S(2)}) collective-permute-start(f32[32,128]{1,0:T(8,128)S(1)} %get-tuple-element.50.field.precond), channel_id=1, source_target_pairs={{0,0},{1,4},{2,2},{3,3},{4,1},{5,8},{6,6},{7,7},{8,5},{9,12},{10,1... | collective-permute-start | bytes 49160 | tf_op jit(solution)/shard_map/ppermute | solution.py:749
  27.2 15.6 %collective-permute-start.5 = (f32[32,128]{1,0:T(8,128)S(1)}, f32[32,128]{1,0:T(8,128)S(1)}, u32[]{:S(2)}, u32[]{:S(2)}) collective-permute-start(f32[32,128]{1,0:T(8,128)S(1)} %get-tuple-element.50.field.precond), channel_id=1, source_target_pairs={{0,0},{1,2},{2,1},{3,4},{4,3},{5,6},{6,5},{7,8},{8,7},{9,10},{10,9... | collective-permute-start | bytes 49160 | tf_op jit(solution)/shard_map/ppermute | solution.py:749
  27.8 14.9 %collective-permute-start.4 = (f32[32,128]{1,0:T(8,128)S(1)}, f32[32,128]{1,0:T(8,128)S(1)}, u32[]{:S(2)}, u32[]{:S(2)}) collective-permute-start(f32[32,128]{1,0:T(8,128)S(1)} %get-tuple-element.50.field.precond), channel_id=1, source_target_pairs={{0,1},{1,0},{2,3},{3,2},{4,5},{5,4},{6,7},{7,6},{8,9},{9,8},{10,11... | collective-permute-start | bytes 49160 | tf_op jit(solution)/shard_map/ppermute | solution.py:749
  45.1 14.9 %collective-permute-start.11 = (f32[32,128]{1,0:T(8,128)S(1)}, f32[32,128]{1,0:T(8,128)S(1)}, u32[]{:S(2)}, u32[]{:S(2)}) collective-permute-start(f32[32,128]{1,0:T(8,128)S(1)} %get-tuple-element.59.field.scaled), channel_id=1, source_target_pairs={{0,0},{1,1},{2,4},{3,3},{4,2},{5,5},{6,8},{7,7},{8,6},{9,9},{10,12... | collective-permute-start | bytes 49160 | tf_op jit(solution)/shard_map/ppermute | solution.py:749
  45.8 14.2 %collective-permute-start.10 = (f32[32,128]{1,0:T(8,128)S(1)}, f32[32,128]{1,0:T(8,128)S(1)}, u32[]{:S(2)}, u32[]{:S(2)}) collective-permute-start(f32[32,128]{1,0:T(8,128)S(1)} %get-tuple-element.59.field.scaled), channel_id=1, source_target_pairs={{0,0},{1,4},{2,2},{3,3},{4,1},{5,8},{6,6},{7,7},{8,5},{9,12},{10,1... | collective-permute-start | bytes 49160 | tf_op jit(solution)/shard_map/ppermute | solution.py:749
  46.5 13.5 %collective-permute-start.9 = (f32[32,128]{1,0:T(8,128)S(1)}, f32[32,128]{1,0:T(8,128)S(1)}, u32[]{:S(2)}, u32[]{:S(2)}) collective-permute-start(f32[32,128]{1,0:T(8,128)S(1)} %get-tuple-element.59.field.scaled), channel_id=1, source_target_pairs={{0,0},{1,2},{2,1},{3,4},{4,3},{5,6},{6,5},{7,8},{8,7},{9,10},{10,9... | collective-permute-start | bytes 49160 | tf_op jit(solution)/shard_map/ppermute | solution.py:749
  47.1 12.9 %collective-permute-start.8 = (f32[32,128]{1,0:T(8,128)S(1)}, f32[32,128]{1,0:T(8,128)S(1)}, u32[]{:S(2)}, u32[]{:S(2)}) collective-permute-start(f32[32,128]{1,0:T(8,128)S(1)} %get-tuple-element.59.field.scaled), channel_id=1, source_target_pairs={{0,1},{1,0},{2,3},{3,2},{4,5},{5,4},{6,7},{7,6},{8,9},{9,8},{10,11... | collective-permute-start | bytes 49160 | tf_op jit(solution)/shard_map/ppermute | solution.py:749
  62.4 3.3 %collective-permute-start.12 = (f32[8,128]{1,0:T(8,128)S(1)}, f32[8,128]{1,0:T(8,128)S(1)}, u32[]{:S(2)}, u32[]{:S(2)}) collective-permute-start(f32[8,128]{1,0:T(8,128)S(1)} %get-tuple-element.63), channel_id=1, source_target_pairs={{0,4},{4,0},{8,12},{12,8},{16,20},{20,16},{24,28},{28,24},{1,5},{5... | collective-permute-start | bytes 12296 | tf_op jit(solution)/shard_map/ppermute | solution.py:678
  65.8 3.6 %collective-permute-start.13 = (f32[8,128]{1,0:T(8,128)S(1)}, f32[8,128]{1,0:T(8,128)S(1)}, u32[]{:S(2)}, u32[]{:S(2)}) collective-permute-start(f32[8,128]{1,0:T(8,128)S(1)} %add.9), channel_id=1, source_target_pairs={{0,1},{1,0},{2,3},{3,2},{4,5},{5,4},{6,7},{7,6},{8,9},{9,8},{10,11... | collective-permute-start | bytes 12296 | tf_op jit(solution)/shard_map/ppermute | solution.py:678
  69.4 5.4 %collective-permute-start.14 = (f32[8,128]{1,0:T(8,128)S(1)}, f32[8,128]{1,0:T(8,128)S(1)}, u32[]{:S(2)}, u32[]{:S(2)}) collective-permute-start(f32[8,128]{1,0:T(8,128)S(1)} %add.10), channel_id=1, source_target_pairs={{0,3},{1,2},{2,1},{3,0},{4,7},{5,6},{6,5},{7,4},{8,11},{9,10},{10,... | collective-permute-start | bytes 12296 | tf_op jit(solution)/shard_map/ppermute | solution.py:678
  74.8 4.5 %collective-permute-start.17 = (f32[8,128]{1,0:T(8,128)S(1)}, f32[8,128]{1,0:T(8,128)S(1)}, u32[]{:S(2)}, u32[]{:S(2)}) collective-permute-start(f32[8,128]{1,0:T(8,128)S(1)} %add.11.rest_0_), channel_id=1, source_target_pairs={{0,24},{4,28},{8,16},{12,20},{16,8},{20,12},{24,0},{28,4},{1,25},{... | collective-permute-start | bytes 12296 | tf_op jit(solution)/shard_map/ppermute | solution.py:678
  74.8 4.5 %collective-permute-start.16 = (f32[8,128]{1,0:T(8,128)S(1)}, f32[8,128]{1,0:T(8,128)S(1)}, u32[]{:S(2)}, u32[]{:S(2)}) collective-permute-start(f32[8,128]{1,0:T(8,128)S(1)} %add.11.rest_0_), channel_id=1, source_target_pairs={{0,16},{4,20},{8,24},{12,28},{16,0},{20,4},{24,8},{28,12},{1,17},{... | collective-permute-start | bytes 12296 | tf_op jit(solution)/shard_map/ppermute | solution.py:678
  76.7 3.6 %collective-permute-start.15 = (f32[8,128]{1,0:T(8,128)S(1)}, f32[8,128]{1,0:T(8,128)S(1)}, u32[]{:S(2)}, u32[]{:S(2)}) collective-permute-start(f32[8,128]{1,0:T(8,128)S(1)} %add.11.rest_0_), channel_id=1, source_target_pairs={{0,8},{4,12},{8,0},{12,4},{16,24},{20,28},{24,16},{28,20},{1,9},{5... | collective-permute-start | bytes 12296 | tf_op jit(solution)/shard_map/ppermute | solution.py:678

commit v12 on v11

--- a/solution.py
+++ b/solution.py
@@ -125,7 +125,7 @@
     return plan[a * FIELDS + 2], lambda t: a + table[t + jnp.where(t < ahead, start, start_after)]
 
 
-TURN = 4
+TURN = 3
 
 
 def padded_sweep(count, fetch, step, carry):
@@ -174,24 +174,29 @@
     return result
 
 
-HALF = 64
-
-
-def own_side(x):
-    size = x[0] * x[0] + x[1] * x[1] + x[2] * x[2]
-    one = jnp.ones_like(size)
-    high, middle, low = three_parts(stacked([2.0 * x[0], 2.0 * x[1], 2.0 * x[2], one, 0.5 - size]))
-    rest = jnp.zeros((HALF - 6 * SUB, size.shape[1]), jnp.float32)
-    return jnp.concatenate([high, high, middle, middle, high, low, rest], 0)
-
-
-def other_side(y):
-    size = y[0] * y[0] + y[1] * y[1] + y[2] * y[2]
-    one = jnp.ones_like(size)
-    high, middle, low = three_parts(stacked([y[0], y[1], y[2], 0.5 - size, one]))
-    first = jnp.concatenate([high, middle], 0).astype(jnp.bfloat16)
-    last = jnp.concatenate([low, high], 0).astype(jnp.bfloat16)
-    return jnp.concatenate([first, first, last, jnp.zeros((HALF - 6 * SUB, size.shape[1]), jnp.bfloat16)], 0)
+def half_size(x):
+    return 0.5 - (x[0] * x[0] + x[1] * x[1] + x[2] * x[2])
+
+
+def own_side(x, which):
+    nothing = [jnp.zeros_like(x[0])] * 4
+    rows = [2.0 * x[0], 2.0 * x[1], 2.0 * x[2], jnp.ones_like(x[0])]
+    high, middle, low = three_parts(stacked(nothing + rows if which else rows))
+    sizes = stacked(list(three_parts(half_size(x))))
+    width = sizes.shape[1]
+    rest = jnp.zeros((width - 7 * SUB, width), jnp.float32)
+    return jnp.concatenate([high, high, middle, middle, high, low, sizes, rest], 0)
+
+
+def other_sides(first, second):
+    rows = [*first, half_size(first), *second, half_size(second)]
+    high, middle, low = three_parts(stacked(rows))
+    width = high.shape[1]
+    ones = jnp.where(lax.broadcasted_iota(jnp.int32, (2 * SUB, width), 0) < 3, 1.0, 0.0).astype(jnp.bfloat16)
+    front = jnp.concatenate([high, middle], 0).astype(jnp.bfloat16)
+    back = jnp.concatenate([low, high], 0).astype(jnp.bfloat16)
+    rest = jnp.zeros((width - 8 * SUB, width), jnp.bfloat16)
+    return jnp.concatenate([front, front, back, ones, rest], 0)
 
 
 GROUP = 4
@@ -213,19 +218,15 @@
 
     def other_of(a, n):
         here = pl.ds(a, 1)
-        return other_side([wide(other_at(c, n)) - wide(middles[c, here, :]) for c in range(3)])
+        return [wide(other_at(c, n)) - wide(middles[c, here, :]) for c in range(3)]
 
     def products(found, ahead):
-        none = jnp.zeros((HALF, width), jnp.bfloat16)
         for k in range(0, GROUP, 2):
             (a, n), (b, m) = ((jnp.minimum(a, share - 1), n) for a, n in found[k : k + 2])
-            left = jnp.concatenate([other_of(a, n), none], 0)
-            right = jnp.concatenate([none, other_of(b, m)], 0)
-            both = jnp.dot(
-                sides[0, a] + sides[1, b], jnp.concatenate([left, right], 1), preferred_element_type=jnp.float32
-            )
-            ahead[k] = both[:, :width]
-            ahead[k + 1] = both[:, width:]
+            own = jnp.concatenate([sides[0, a], sides[1, b]], 0)
+            both = jnp.dot(own, other_sides(other_of(a, n), other_of(b, m)), preferred_element_type=jnp.float32)
+            ahead[k] = both[:width]
+            ahead[k + 1] = both[width:]
 
     def weigh(at, found, ahead):
         for k, (a, n) in enumerate(found):
@@ -348,16 +349,11 @@
     for k in range(3):
         first = near[k, 0:share, 0:1]
         middles[k] = jnp.broadcast_to(jnp.floor(first) + 0.5, (share, width))
-    low = lax.broadcasted_iota(jnp.int32, (width, width), 1) < HALF
-    for a in range(0, share, 2):
-        pair = []
-        for b in (a, a + 1):
-            here = slice(b, b + 1)
-            pair.append(own_side([wide(near[k, here, :] - middles[k, here, :]) for k in range(3)]))
-        turned = jnp.concatenate(pair, 0).T
-        moved = pltpu.roll(turned, HALF, 1)
-        for at, b, half, side in ((0, a, low, turned), (1, a, ~low, moved), (0, a + 1, low, moved), (1, a + 1, ~low, turned)):
-            sides[at, b] = jnp.where(half, side, 0.0).astype(jnp.bfloat16)
+    for a in range(share):
+        here = slice(a, a + 1)
+        centred = [wide(near[k, here, :] - middles[k, here, :]) for k in range(3)]
+        for which in range(2):
+            sides[which, a] = own_side(centred, which).T.astype(jnp.bfloat16)
     spread_columns(weights, lambda a: a, near[3, 0:share, :])
     cols_ref[...] = jnp.zeros_like(cols_ref)
     rows_ref[...] = jnp.zeros_like(rows_ref)
@@ -701,7 +697,7 @@
     axes = ("piece", "col")
     device = [(p, c) for p in range(pieces) for c in range(columns)]
     partner = [(p + (1 if p % 2 else -1), c) for p, c in device]
-    partner = [(q, d) if 0 <= q < pieces else (p, c) for (q, d), (p, c) in zip(partner, device)]
+    partner = [(q, d) if 0 <= q < pieces else (p, c ^ 1) for (q, d), (p, c) in zip(partner, device)]
     second = lax.ppermute(second, axes, [(i, q * columns + d) for i, (q, d) in enumerate(partner)])
 
     plan, runs, tiles_in, sides, middles, weights, rows, cols, selfs = call(
@@ -739,13 +735,16 @@
     def exchange(field):
         count = pieces * columns
         swaps = [[i ^ 1 for i in range(count)], [i - 1 if i % 2 == 0 else i + 1 for i in range(count)]]
-        swaps[1][0], swaps[1][-1] = 0, count - 1
+        swaps[1][0], swaps[1][-1] = count - 1, 0
         for c in range(1, columns - 1):
             to = {}
             for p in range(pieces - 1):
                 low, high = p * columns + c, (p + 1) * columns
                 to[low], to[high] = high, low
-            swaps.append([to.get(i, i) for i in range(count)])
+            for p in range(pieces):
+                rest = [i for i in range(p * columns, (p + 1) * columns) if i not in to]
+                to.update(zip(rest, rest[1:] + rest[:1]))
+            swaps.append([to[i] for i in range(count)])
         return [lax.ppermute(field, axes, list(enumerate(to))) for to in swaps]
 
     scratch = [pltpu.VMEM((share, width, width), f32), pltpu.VMEM((8 * share, width), f32)]
@@ -776,8 +775,7 @@
         return tree([values] + [swap(values, axis, low * k) for k in range(1, size)])
 
     sums = together(sums, "piece", 1, 2)
-    for step in col_steps:
-        sums = sums + swap(sums, "col", step)
+    sums = together(sums, "col", 1, columns)
     step = 2
     while pieces // step > 4:
         sums = together(sums, "piece", step, 4)

time: 81.6 us -> 70.1 us (0.86)
  starting transfers between devices: 38.3 us -> 29.2 us
  waiting for transfers between devices: 9.83 us -> 7.99 us
    ppermute x8, starting transfers between devices: 23 us -> 12.2 us  [exchange(): return [lax.ppermute(field, axes, list(enumerate(to))) for to in swaps]]
    ppermute x8 -> x9, waiting for transfers between devices: 9.8 us -> 6.34 us  [swap(): lax.ppermute(values, axis, [(i, i ^ step) for i in range(lax.axis_size(ax...]
    ppermute x8 -> x9, starting transfers between devices: 14.5 us -> 16.8 us  [swap(): lax.ppermute(values, axis, [(i, i ^ step) for i in range(lax.axis_size(ax...]
    ppermute x8, waiting for transfers between devices: 0.02 us -> 1.64 us  [exchange(): return [lax.ppermute(field, axes, list(enumerate(to))) for to in swaps]]
  transfers between devices with their start and end apart: 18 -> 19, of which waited for: 5 -> 7; matrix products, arithmetic and copies ran while one was open for 1% -> 1% of each run, Pallas kernels for 26% -> 30%
where the time goes in v12:
time: 70.1 us; the launch traced here: 69.6 us
  Pallas kernels  31 us (44%)
  starting transfers between devices  29.2 us (42%)
  waiting for transfers between devices  7.99 us (11%)
  between operations  0.77 us (1%)
  other arithmetic  0.71 us (1%)
    pallas_call x8, Pallas kernels, call(): pl.pallas_call(kernel, out_shape=outs, in_specs=[SMEM] * scalars + [HBM]...  31 us
    ppermute x9, starting transfers between devices, swap(): lax.ppermute(values, axis, [(i, i ^ step) for i in range(lax.axis_size(ax...  16.8 us
    ppermute x8, starting transfers between devices, exchange(): return [lax.ppermute(field, axes, list(enumerate(to))) for to in swaps]  12.2 us
    ppermute x9, waiting for transfers between devices, swap(): lax.ppermute(values, axis, [(i, i ^ step) for i in range(lax.axis_size(ax...  6.34 us
    ppermute x8, waiting for transfers between devices, exchange(): return [lax.ppermute(field, axes, list(enumerate(to))) for to in swaps]  1.64 us
  transfers between devices with their start and end apart: 19, of which 7 were waited for; matrix products, arithmetic and copies ran while one was open for 1% of the time, Pallas kernels for 30%

profile of v12, /device:TPU:0, one launch (start us, length us, event | category | flops | bytes accessed | tf_op | source)
XLA Modules:
  0.0 69.6 jit_solution(11777660422901618732)
XLA Ops:
  0.6 3.1 %collective-permute-start.2 = (s32[7,128]{1,0:T(8,128)}, s32[7,128]{1,0:T(8,128)S(1)}, u32[]{:S(2)}, u32[]{:S(2)}) collective-permute-start(s32[7,128]{1,0:T(8,128)} %bitcast.1), channel_id=1, source_target_pairs={{0,1},{1,0},{2,3},{3,2},{4,5},{5,4},{6,7},{7,6},{8,9},{9,8},{10,11... | collective-permute-start | bytes 10760 | tf_op jit(solution)/shard_map/ppermute | solution.py:674
  3.7 1.7 %prepare.1 = (s32[8]{0:T(128)S(4)}, s32[1480]{0:T(1024)S(4)}, f32[4,192,128]{2,1,0:T(8,128)S(1)}, f32[4,64,128]{2,1,0:T(8,128)S(1)}, f32[32,128]{1,0:T(8,128)S(1...) custom-call(s32[8]{0:T(128)} %counts.1, f32[3]{0:T(128)} %densities.1, ...), custom_call_target="tpu_custom_call" | custom-call | tf_op jit(solution)/shard_map/prepare/pallas_call | solution.py:661
  5.4 0.1 collective-permute-start
  5.5 0.1 collective-permute-start.1
  5.6 0.0 collective-permute-done.2
  5.6 0.7 %pad_add_fusion.rest_0_ = s32[14,128]{1,0:T(8,128)S(1)} fusion(s32[7,128]{1,0:T(8,128)S(1)} %collective-permute-done.2, s32[7,128]{1,0:T(8,128)} %bitcast.2), kind=kLoop, calls=%fused_computation | loop fusion | flops 1792 | bytes 14336 | tf_op jit(solution)/shard_map/concatenate | solution.py:679
  6.3 4.0 %collective-permute-start.3 = (s32[14,128]{1,0:T(8,128)S(1)}, s32[14,128]{1,0:T(8,128)S(1)}, u32[]{:S(2)}, u32[]{:S(2)}) collective-permute-start(s32[14,128]{1,0:T(8,128)S(1)} %pad_add_fusion.rest_0_), channel_id=1, source_target_pairs={{0,3},{1,2},{2,1},{3,0},{4,7},{5,6},{6,5},{7,4},{8,11},{9,10},{10,... | collective-permute-start | bytes 21512 | tf_op jit(solution)/shard_map/ppermute | solution.py:674
  10.3 10.8 %build_inner.1 = (s32[196]{0:T(256)S(4)}, s32[195]{0:T(256)S(4)}, f32[224,128,128]{2,1,0:T(8,128)S(1)}, bf16[2,32,128,128]{3,2,1,0:T(8,128)(2,1)S(1)}, f32[3,32,...) custom-call(s32[8]{0:T(128)S(4)} %get-tuple-element.34.meta, ...), custom_call_target="tpu_custom_call" | custom-call | flops 56623104 | tf_op jit(solution)/shard_map/build_inner/pallas_call | solution.py:661
  21.1 0.0 collective-permute-done.3.rest_1_
  21.1 0.0 collective-permute-done.first
  21.1 0.0 collective-permute-done.1.second
  21.1 4.6 %build_outer.1 = (s32[1]{0:T(128)S(4)}, f32[230,128,128]{2,1,0:T(8,128)S(1)}, f32[32,128]{1,0:T(8,128)S(1)}, f32[32,128]{1,0:T(8,128)S(1)}, f32[32,128]{1,0:T(8,128)S(1)}, /*index=5*/f32[32,128]{1,0:T(8,128)S(1)}) custom-call(s32[8]{0:T(128)S(4)} %get-tuple-element.34.meta, s32[1480]{0:T(1024)S(4)} %get-tuple-element.35.table, ...), custom_call_target="tpu_custom_call" | custom-call | flops 58195968 | tf_op jit(solution)/shard_map/build_outer/pallas_call | solution.py:661
  25.7 2.7 %collective-permute-start.7 = (f32[32,128]{1,0:T(8,128)S(1)}, f32[32,128]{1,0:T(8,128)S(1)}, u32[]{:S(2)}, u32[]{:S(2)}) collective-permute-start(f32[32,128]{1,0:T(8,128)S(1)} %get-tuple-element.50.field.precond), channel_id=1, source_target_pairs={{0,1},{1,3},{2,4},{3,0},{4,2},{5,7},{6,8},{7,5},{8,6},{9,11},{10,1... | collective-permute-start | bytes 49160 | tf_op jit(solution)/shard_map/ppermute | solution.py:748
  28.5 3.3 %collective-permute-start.6 = (f32[32,128]{1,0:T(8,128)S(1)}, f32[32,128]{1,0:T(8,128)S(1)}, u32[]{:S(2)}, u32[]{:S(2)}) collective-permute-start(f32[32,128]{1,0:T(8,128)S(1)} %get-tuple-element.50.field.precond), channel_id=1, source_target_pairs={{0,2},{1,4},{2,3},{3,0},{4,1},{5,8},{6,7},{7,6},{8,5},{9,12},{10,1... | collective-permute-start | bytes 49160 | tf_op jit(solution)/shard_map/ppermute | solution.py:748
  31.7 0.8 %collective-permute-start.5 = (f32[32,128]{1,0:T(8,128)S(1)}, f32[32,128]{1,0:T(8,128)S(1)}, u32[]{:S(2)}, u32[]{:S(2)}) collective-permute-start(f32[32,128]{1,0:T(8,128)S(1)} %get-tuple-element.50.field.precond), channel_id=1, source_target_pairs={{0,31},{1,2},{2,1},{3,4},{4,3},{5,6},{6,5},{7,8},{8,7},{9,10},{10,... | collective-permute-start | bytes 49160 | tf_op jit(solution)/shard_map/ppermute | solution.py:748
  32.5 0.0 collective-permute-start.4
  32.5 4.3 %apply_inner.2 = (f32[32,128,128]{2,1,0:T(8,128)S(1)}, f32[256,128]{1,0:T(8,128)S(1)}) custom-call(s32[8]{0:T(128)S(4)} %get-tuple-element.34.meta, s32[1480]{0:T(1024)S(4)} %get-tuple-element.35.table, s32[196]{0:T(256)S(4)} %get-tuple-element.37.plan, s32[1]{0:T(128)S(4)} %get-tuple-element.51.again, f32[32,128]{1,0:T(8,128)S(1)} %get-tuple-element.50.field.precond, ...), custom_call_target="tpu_custom_call" | custom-call | flops 14155776 | tf_op jit(solution)/shard_map/apply_inner/pallas_call | solution.py:661
  36.8 0.0 collective-permute-done.7.rest_3_
  36.8 0.0 collective-permute-done.6.rest_2_
  36.9 1.6 %collective-permute-done.5.rest_1_ = f32[32,128]{1,0:T(8,128)S(1)} collective-permute-done((f32[32,128]{1,0:T(8,128)S(1)}, f32[32,128]{1,0:T(8,128)S(1)}, u32[]{:S(2)}, u32[]{:S(2)}) %collective-permute-start.5) | collective-permute-done | bytes 16416 | tf_op jit(solution)/shard_map/ppermute | solution.py:748
  38.5 0.0 collective-permute-done.4.rest_0_
  38.5 2.2 %apply_first.1 = (f32[32,128]{1,0:T(8,128)S(1)}, f32[32,128]{1,0:T(8,128)S(1)}) custom-call(s32[8]{0:T(128)S(4)} %get-tuple-element.34.meta, s32[1480]{0:T(1024)S(4)} %get-tuple-element.35.table, s32[196]{0:T(256)S(4)} %get-tuple-element.37.plan, s32[1]{0:T(128)S(4)} %get-tuple-element.51.again, f32[32,128]{1,0:T(8,128)S(1)} %get-tuple-element.52.diagonal, ...), custom_call_target="tpu_custom_call" | custom-call | flops 7274496 | tf_op jit(solution)/shard_map/apply_first/pallas_call | solution.py:661
  40.6 1.1 %collective-permute-start.11 = (f32[32,128]{1,0:T(8,128)S(1)}, f32[32,128]{1,0:T(8,128)S(1)}, u32[]{:S(2)}, u32[]{:S(2)}) collective-permute-start(f32[32,128]{1,0:T(8,128)S(1)} %get-tuple-element.59.field.scaled), channel_id=1, source_target_pairs={{0,1},{1,3},{2,4},{3,0},{4,2},{5,7},{6,8},{7,5},{8,6},{9,11},{10,1... | collective-permute-start | bytes 49160 | tf_op jit(solution)/shard_map/ppermute | solution.py:748
  41.8 1.4 %collective-permute-start.10 = (f32[32,128]{1,0:T(8,128)S(1)}, f32[32,128]{1,0:T(8,128)S(1)}, u32[]{:S(2)}, u32[]{:S(2)}) collective-permute-start(f32[32,128]{1,0:T(8,128)S(1)} %get-tuple-element.59.field.scaled), channel_id=1, source_target_pairs={{0,2},{1,4},{2,3},{3,0},{4,1},{5,8},{6,7},{7,6},{8,5},{9,12},{10,1... | collective-permute-start | bytes 49160 | tf_op jit(solution)/shard_map/ppermute | solution.py:748
  43.2 2.9 %collective-permute-start.9 = (f32[32,128]{1,0:T(8,128)S(1)}, f32[32,128]{1,0:T(8,128)S(1)}, u32[]{:S(2)}, u32[]{:S(2)}) collective-permute-start(f32[32,128]{1,0:T(8,128)S(1)} %get-tuple-element.59.field.scaled), channel_id=1, source_target_pairs={{0,31},{1,2},{2,1},{3,4},{4,3},{5,6},{6,5},{7,8},{8,7},{9,10},{10,... | collective-permute-start | bytes 49160 | tf_op jit(solution)/shard_map/ppermute | solution.py:748
  46.1 0.0 collective-permute-start.8
  46.1 4.3 %apply_inner.3 = (f32[32,128,128]{2,1,0:T(8,128)S(1)}, f32[256,128]{1,0:T(8,128)S(1)}) custom-call(s32[8]{0:T(128)S(4)} %get-tuple-element.34.meta, s32[1480]{0:T(1024)S(4)} %get-tuple-element.35.table, s32[196]{0:T(256)S(4)} %get-tuple-element.37.plan, s32[1]{0:T(128)S(4)} %get-tuple-element.51.again, f32[32,128]{1,0:T(8,128)S(1)} %get-tuple-element.59.field.scaled, ...), custom_call_target="tpu_custom_call" | custom-call | flops 14155776 | tf_op jit(solution)/shard_map/apply_inner/pallas_call | solution.py:661
  50.4 0.0 collective-permute-done.11.rest_3_
  50.4 0.0 collective-permute-done.10.rest_2_
  50.4 0.0 collective-permute-done.9.rest_1_
  50.4 0.0 collective-permute-done.8.rest_0_
  50.4 2.3 %apply_second.1 = (f32[32,128]{1,0:T(8,128)S(1)}, f32[8,128]{1,0:T(8,128)S(1)}) custom-call(s32[8]{0:T(128)S(4)} %get-tuple-element.34.meta, s32[1480]{0:T(1024)S(4)} %get-tuple-element.35.table, s32[196]{0:T(256)S(4)} %get-tuple-element.37.plan, s32[1]{0:T(128)S(4)} %get-tuple-element.51.again, f32[32,128]{1,0:T(8,128)S(1)} %get-tuple-element.33.source, ...), custom_call_target="tpu_custom_call" | custom-call | flops 7274496 | tf_op jit(solution)/shard_map/apply_second/pallas_call | solution.py:661
  52.7 0.4 collective-permute-start.12
  53.1 0.8 %collective-permute-done.12 = f32[8,128]{1,0:T(8,128)S(1)} collective-permute-done((f32[8,128]{1,0:T(8,128)S(1)}, f32[8,128]{1,0:T(8,128)S(1)}, u32[]{:S(2)}, u32[]{:S(2)}) %collective-permute-start.12) | collective-permute-done | bytes 4128 | tf_op jit(solution)/shard_map/ppermute | solution.py:674
  53.9 2.4 %collective-permute-start.15 = (f32[8,128]{1,0:T(8,128)S(1)}, f32[8,128]{1,0:T(8,128)S(1)}, u32[]{:S(2)}, u32[]{:S(2)}) collective-permute-start(f32[8,128]{1,0:T(8,128)S(1)} %add.12), channel_id=1, source_target_pairs={{0,3},{1,2},{2,1},{3,0},{4,7},{5,6},{6,5},{7,4},{8,11},{9,10},{10,... | collective-permute-start | bytes 12296 | tf_op jit(solution)/shard_map/ppermute | solution.py:674
  56.4 1.6 %collective-permute-start.14 = (f32[8,128]{1,0:T(8,128)S(1)}, f32[8,128]{1,0:T(8,128)S(1)}, u32[]{:S(2)}, u32[]{:S(2)}) collective-permute-start(f32[8,128]{1,0:T(8,128)S(1)} %add.12), channel_id=1, source_target_pairs={{0,2},{1,3},{2,0},{3,1},{4,6},{5,7},{6,4},{7,5},{8,10},{9,11},{10,... | collective-permute-start | bytes 12296 | tf_op jit(solution)/shard_map/ppermute | solution.py:674
  58.0 0.3 collective-permute-start.13
  58.3 1.0 %collective-permute-done.15 = f32[8,128]{1,0:T(8,128)S(1)} collective-permute-done((f32[8,128]{1,0:T(8,128)S(1)}, f32[8,128]{1,0:T(8,128)S(1)}, u32[]{:S(2)}, u32[]{:S(2)}) %collective-permute-start.15) | collective-permute-done | bytes 4128 | tf_op jit(solution)/shard_map/ppermute | solution.py:674
  59.3 1.5 %collective-permute-done.14 = f32[8,128]{1,0:T(8,128)S(1)} collective-permute-done((f32[8,128]{1,0:T(8,128)S(1)}, f32[8,128]{1,0:T(8,128)S(1)}, u32[]{:S(2)}, u32[]{:S(2)}) %collective-permute-start.14) | collective-permute-done | bytes 4128 | tf_op jit(solution)/shard_map/ppermute | solution.py:674
  60.9 0.7 %collective-permute-done.13 = f32[8,128]{1,0:T(8,128)S(1)} collective-permute-done((f32[8,128]{1,0:T(8,128)S(1)}, f32[8,128]{1,0:T(8,128)S(1)}, u32[]{:S(2)}, u32[]{:S(2)}) %collective-permute-start.13) | collective-permute-done | bytes 4128 | tf_op jit(solution)/shard_map/ppermute | solution.py:674
  61.6 2.5 %collective-permute-start.18 = (f32[8,128]{1,0:T(8,128)S(1)}, f32[8,128]{1,0:T(8,128)S(1)}, u32[]{:S(2)}, u32[]{:S(2)}) collective-permute-start(f32[8,128]{1,0:T(8,128)S(1)} %add_add_fusion.rest_0_), channel_id=1, source_target_pairs={{0,24},{4,28},{8,16},{12,20},{16,8},{20,12},{24,0},{28,4},{1,25},{... | collective-permute-start | bytes 12296 | tf_op jit(solution)/shard_map/ppermute | solution.py:674
  64.2 0.9 %collective-permute-start.17 = (f32[8,128]{1,0:T(8,128)S(1)}, f32[8,128]{1,0:T(8,128)S(1)}, u32[]{:S(2)}, u32[]{:S(2)}) collective-permute-start(f32[8,128]{1,0:T(8,128)S(1)} %add_add_fusion.rest_0_), channel_id=1, source_target_pairs={{0,16},{4,20},{8,24},{12,28},{16,0},{20,4},{24,8},{28,12},{1,17},{... | collective-permute-start | bytes 12296 | tf_op jit(solution)/shard_map/ppermute | solution.py:674
  65.1 1.4 %collective-permute-start.16 = (f32[8,128]{1,0:T(8,128)S(1)}, f32[8,128]{1,0:T(8,128)S(1)}, u32[]{:S(2)}, u32[]{:S(2)}) collective-permute-start(f32[8,128]{1,0:T(8,128)S(1)} %add_add_fusion.rest_0_), channel_id=1, source_target_pairs={{0,8},{4,12},{8,0},{12,4},{16,24},{20,28},{24,16},{28,20},{1,9},{5... | collective-permute-start | bytes 12296 | tf_op jit(solution)/shard_map/ppermute | solution.py:674
  66.5 0.0 collective-permute-done.18.rest_3_
  66.5 1.3 %collective-permute-done.17.rest_2_ = f32[8,128]{1,0:T(8,128)S(1)} collective-permute-done((f32[8,128]{1,0:T(8,128)S(1)}, f32[8,128]{1,0:T(8,128)S(1)}, u32[]{:S(2)}, u32[]{:S(2)}) %collective-permute-start.17) | collective-permute-done | bytes 4128 | tf_op jit(solution)/shard_map/ppermute | solution.py:674
  67.8 0.9 %collective-permute-done.16.rest_1_ = f32[8,128]{1,0:T(8,128)S(1)} collective-permute-done((f32[8,128]{1,0:T(8,128)S(1)}, f32[8,128]{1,0:T(8,128)S(1)}, u32[]{:S(2)}, u32[]{:S(2)}) %collective-permute-start.16) | collective-permute-done | bytes 4128 | tf_op jit(solution)/shard_map/ppermute | solution.py:674
  68.7 0.9 %finish.1 = (f32[32,128]{1,0:T(8,128)}, f32[32,128]{1,0:T(8,128)}) custom-call(f32[32,128]{1,0:T(8,128)S(1)} %get-tuple-element.33.source, f32[32,128]{1,0:T(8,128)S(1)} %get-tuple-element.50.field.precond, f32[32,128]{1,0:T(8,128)S(1)} %get-tuple-element.58.spill, f32[32,128]{1,0:T(8,128)S(1)} %get-tuple-element.59.field.scaled, ...), custom_call_target="tpu_custom_call" | custom-call | tf_op jit(solution)/shard_map/finish/pallas_call | solution.py:661
  (2 shorter events, 0.0 us)
Async XLA Ops:
  0.6 5.0 %collective-permute-start.2 = (s32[7,128]{1,0:T(8,128)}, s32[7,128]{1,0:T(8,128)S(1)}, u32[]{:S(2)}, u32[]{:S(2)}) collective-permute-start(s32[7,128]{1,0:T(8,128)} %bitcast.1), channel_id=1, source_target_pairs={{0,1},{1,0},{2,3},{3,2},{4,5},{5,4},{6,7},{7,6},{8,9},{9,8},{10,11... | collective-permute-start | bytes 10760 | tf_op jit(solution)/shard_map/ppermute | solution.py:674
  5.4 15.7 %collective-permute-start = (f32[4,32,128]{2,1,0:T(8,128)S(1)}, f32[4,32,128]{2,1,0:T(8,128)S(1)}, u32[]{:S(2)}, u32[]{:S(2)}) collective-permute-start(f32[4,32,128]{2,1,0:T(8,128)S(1)} %get-tuple-element.40), channel_id=1, source_target_pairs={{0,4},{4,0},{8,12},{12,8},{16,20},{20,16},{24,28},{28,24},{1,5},{5... | collective-permute-start | bytes 196616 | tf_op jit(solution)/shard_map/ppermute | solution.py:696
  5.5 15.6 %collective-permute-start.1 = (f32[4,32,128]{2,1,0:T(8,128)S(1)}, f32[4,32,128]{2,1,0:T(8,128)S(1)}, u32[]{:S(2)}, u32[]{:S(2)}) collective-permute-start(f32[4,32,128]{2,1,0:T(8,128)S(1)} %get-tuple-element.41), channel_id=1, source_target_pairs={{0,1},{1,0},{2,3},{3,2},{4,8},{5,9},{6,10},{7,11},{8,4},{9,5},{10,... | collective-permute-start | bytes 196616 | tf_op jit(solution)/shard_map/ppermute | solution.py:701
  6.3 14.8 %collective-permute-start.3 = (s32[14,128]{1,0:T(8,128)S(1)}, s32[14,128]{1,0:T(8,128)S(1)}, u32[]{:S(2)}, u32[]{:S(2)}) collective-permute-start(s32[14,128]{1,0:T(8,128)S(1)} %pad_add_fusion.rest_0_), channel_id=1, source_target_pairs={{0,3},{1,2},{2,1},{3,0},{4,7},{5,6},{6,5},{7,4},{8,11},{9,10},{10,... | collective-permute-start | bytes 21512 | tf_op jit(solution)/shard_map/ppermute | solution.py:674
  25.7 11.1 %collective-permute-start.7 = (f32[32,128]{1,0:T(8,128)S(1)}, f32[32,128]{1,0:T(8,128)S(1)}, u32[]{:S(2)}, u32[]{:S(2)}) collective-permute-start(f32[32,128]{1,0:T(8,128)S(1)} %get-tuple-element.50.field.precond), channel_id=1, source_target_pairs={{0,1},{1,3},{2,4},{3,0},{4,2},{5,7},{6,8},{7,5},{8,6},{9,11},{10,1... | collective-permute-start | bytes 49160 | tf_op jit(solution)/shard_map/ppermute | solution.py:748
  28.5 8.4 %collective-permute-start.6 = (f32[32,128]{1,0:T(8,128)S(1)}, f32[32,128]{1,0:T(8,128)S(1)}, u32[]{:S(2)}, u32[]{:S(2)}) collective-permute-start(f32[32,128]{1,0:T(8,128)S(1)} %get-tuple-element.50.field.precond), channel_id=1, source_target_pairs={{0,2},{1,4},{2,3},{3,0},{4,1},{5,8},{6,7},{7,6},{8,5},{9,12},{10,1... | collective-permute-start | bytes 49160 | tf_op jit(solution)/shard_map/ppermute | solution.py:748
  31.7 6.8 %collective-permute-start.5 = (f32[32,128]{1,0:T(8,128)S(1)}, f32[32,128]{1,0:T(8,128)S(1)}, u32[]{:S(2)}, u32[]{:S(2)}) collective-permute-start(f32[32,128]{1,0:T(8,128)S(1)} %get-tuple-element.50.field.precond), channel_id=1, source_target_pairs={{0,31},{1,2},{2,1},{3,4},{4,3},{5,6},{6,5},{7,8},{8,7},{9,10},{10,... | collective-permute-start | bytes 49160 | tf_op jit(solution)/shard_map/ppermute | solution.py:748
  32.5 6.0 %collective-permute-start.4 = (f32[32,128]{1,0:T(8,128)S(1)}, f32[32,128]{1,0:T(8,128)S(1)}, u32[]{:S(2)}, u32[]{:S(2)}) collective-permute-start(f32[32,128]{1,0:T(8,128)S(1)} %get-tuple-element.50.field.precond), channel_id=1, source_target_pairs={{0,1},{1,0},{2,3},{3,2},{4,5},{5,4},{6,7},{7,6},{8,9},{9,8},{10,11... | collective-permute-start | bytes 49160 | tf_op jit(solution)/shard_map/ppermute | solution.py:748
  40.6 9.8 %collective-permute-start.11 = (f32[32,128]{1,0:T(8,128)S(1)}, f32[32,128]{1,0:T(8,128)S(1)}, u32[]{:S(2)}, u32[]{:S(2)}) collective-permute-start(f32[32,128]{1,0:T(8,128)S(1)} %get-tuple-element.59.field.scaled), channel_id=1, source_target_pairs={{0,1},{1,3},{2,4},{3,0},{4,2},{5,7},{6,8},{7,5},{8,6},{9,11},{10,1... | collective-permute-start | bytes 49160 | tf_op jit(solution)/shard_map/ppermute | solution.py:748
  41.8 8.6 %collective-permute-start.10 = (f32[32,128]{1,0:T(8,128)S(1)}, f32[32,128]{1,0:T(8,128)S(1)}, u32[]{:S(2)}, u32[]{:S(2)}) collective-permute-start(f32[32,128]{1,0:T(8,128)S(1)} %get-tuple-element.59.field.scaled), channel_id=1, source_target_pairs={{0,2},{1,4},{2,3},{3,0},{4,1},{5,8},{6,7},{7,6},{8,5},{9,12},{10,1... | collective-permute-start | bytes 49160 | tf_op jit(solution)/shard_map/ppermute | solution.py:748
  43.2 7.2 %collective-permute-start.9 = (f32[32,128]{1,0:T(8,128)S(1)}, f32[32,128]{1,0:T(8,128)S(1)}, u32[]{:S(2)}, u32[]{:S(2)}) collective-permute-start(f32[32,128]{1,0:T(8,128)S(1)} %get-tuple-element.59.field.scaled), channel_id=1, source_target_pairs={{0,31},{1,2},{2,1},{3,4},{4,3},{5,6},{6,5},{7,8},{8,7},{9,10},{10,... | collective-permute-start | bytes 49160 | tf_op jit(solution)/shard_map/ppermute | solution.py:748
  46.1 4.3 %collective-permute-start.8 = (f32[32,128]{1,0:T(8,128)S(1)}, f32[32,128]{1,0:T(8,128)S(1)}, u32[]{:S(2)}, u32[]{:S(2)}) collective-permute-start(f32[32,128]{1,0:T(8,128)S(1)} %get-tuple-element.59.field.scaled), channel_id=1, source_target_pairs={{0,1},{1,0},{2,3},{3,2},{4,5},{5,4},{6,7},{7,6},{8,9},{9,8},{10,11... | collective-permute-start | bytes 49160 | tf_op jit(solution)/shard_map/ppermute | solution.py:748
  52.7 1.2 %collective-permute-start.12 = (f32[8,128]{1,0:T(8,128)S(1)}, f32[8,128]{1,0:T(8,128)S(1)}, u32[]{:S(2)}, u32[]{:S(2)}) collective-permute-start(f32[8,128]{1,0:T(8,128)S(1)} %get-tuple-element.63), channel_id=1, source_target_pairs={{0,4},{4,0},{8,12},{12,8},{16,20},{20,16},{24,28},{28,24},{1,5},{5... | collective-permute-start | bytes 12296 | tf_op jit(solution)/shard_map/ppermute | solution.py:674
  53.9 5.4 %collective-permute-start.15 = (f32[8,128]{1,0:T(8,128)S(1)}, f32[8,128]{1,0:T(8,128)S(1)}, u32[]{:S(2)}, u32[]{:S(2)}) collective-permute-start(f32[8,128]{1,0:T(8,128)S(1)} %add.12), channel_id=1, source_target_pairs={{0,3},{1,2},{2,1},{3,0},{4,7},{5,6},{6,5},{7,4},{8,11},{9,10},{10,... | collective-permute-start | bytes 12296 | tf_op jit(solution)/shard_map/ppermute | solution.py:674
  56.4 4.5 %collective-permute-start.14 = (f32[8,128]{1,0:T(8,128)S(1)}, f32[8,128]{1,0:T(8,128)S(1)}, u32[]{:S(2)}, u32[]{:S(2)}) collective-permute-start(f32[8,128]{1,0:T(8,128)S(1)} %add.12), channel_id=1, source_target_pairs={{0,2},{1,3},{2,0},{3,1},{4,6},{5,7},{6,4},{7,5},{8,10},{9,11},{10,... | collective-permute-start | bytes 12296 | tf_op jit(solution)/shard_map/ppermute | solution.py:674
  58.0 3.6 %collective-permute-start.13 = (f32[8,128]{1,0:T(8,128)S(1)}, f32[8,128]{1,0:T(8,128)S(1)}, u32[]{:S(2)}, u32[]{:S(2)}) collective-permute-start(f32[8,128]{1,0:T(8,128)S(1)} %add.12), channel_id=1, source_target_pairs={{0,1},{1,0},{2,3},{3,2},{4,5},{5,4},{6,7},{7,6},{8,9},{9,8},{10,11... | collective-permute-start | bytes 12296 | tf_op jit(solution)/shard_map/ppermute | solution.py:674
  61.6 4.9 %collective-permute-start.18 = (f32[8,128]{1,0:T(8,128)S(1)}, f32[8,128]{1,0:T(8,128)S(1)}, u32[]{:S(2)}, u32[]{:S(2)}) collective-permute-start(f32[8,128]{1,0:T(8,128)S(1)} %add_add_fusion.rest_0_), channel_id=1, source_target_pairs={{0,24},{4,28},{8,16},{12,20},{16,8},{20,12},{24,0},{28,4},{1,25},{... | collective-permute-start | bytes 12296 | tf_op jit(solution)/shard_map/ppermute | solution.py:674
  64.2 3.6 %collective-permute-start.17 = (f32[8,128]{1,0:T(8,128)S(1)}, f32[8,128]{1,0:T(8,128)S(1)}, u32[]{:S(2)}, u32[]{:S(2)}) collective-permute-start(f32[8,128]{1,0:T(8,128)S(1)} %add_add_fusion.rest_0_), channel_id=1, source_target_pairs={{0,16},{4,20},{8,24},{12,28},{16,0},{20,4},{24,8},{28,12},{1,17},{... | collective-permute-start | bytes 12296 | tf_op jit(solution)/shard_map/ppermute | solution.py:674
  65.1 3.6 %collective-permute-start.16 = (f32[8,128]{1,0:T(8,128)S(1)}, f32[8,128]{1,0:T(8,128)S(1)}, u32[]{:S(2)}, u32[]{:S(2)}) collective-permute-start(f32[8,128]{1,0:T(8,128)S(1)} %add_add_fusion.rest_0_), channel_id=1, source_target_pairs={{0,8},{4,12},{8,0},{12,4},{16,24},{20,28},{24,16},{28,20},{1,9},{5... | collective-permute-start | bytes 12296 | tf_op jit(solution)/shard_map/ppermute | solution.py:674

commit v13 on v12

--- a/solution.py
+++ b/solution.py
@@ -202,9 +202,15 @@
 GROUP = 4
 
 
-def flat_tiles(count, runs, most, table, sides, middles, weights, other_at, buffers, tiles, rows_ref, cols_ref):
-    share, width = rows_ref.shape[0] - 1, rows_ref.shape[2]
+def flat_tiles(count, runs, most, table, sides, middles, weights, other_at, buffers, tiles, sums_ref, both_ways):
+    share, width = weights.shape[:2]
     chunks = pieces_of(width)
+    lane = lax.broadcasted_iota(jnp.int32, (SUB, width), 1)
+    diagonal = lane - lax.broadcasted_iota(jnp.int32, (SUB, width), 0)
+
+    def add_to(block, term):
+        here = pl.ds(pl.multiple_of(block * SUB, SUB), SUB)
+        sums_ref[here, :] = sums_ref[here, :] + term
 
     def steps(state):
         found = []
@@ -230,23 +236,25 @@
 
     def weigh(at, found, ahead):
         for k, (a, n) in enumerate(found):
-            alone = a == n
-            row = jnp.where(alone, share, a)
             own = jnp.minimum(a, share - 1)
             other = wide(other_at(3, n))
             down = [None] * 2
+            along = jnp.zeros((SUB, width), jnp.float32)
             for c, here in enumerate(chunks):
                 left = ahead[k, here, :]
                 rest = jnp.maximum(left, 0.0)
                 inverse = pltpu.reciprocal((1.01 - left) * (weights[own, here, :] + other), approx=True)
                 tile = rest * rest * inverse
                 tiles[at + k, here, :] = tile
-                rows_ref[row, here, :] = rows_ref[row, here, :] + tile
-                if cols_ref is not None:
+                along = jnp.where(diagonal == c * SUB, jnp.sum(tile, axis=1, keepdims=True), along)
+                if both_ways:
                     gather(down, c, tile)
-            if cols_ref is not None:
-                there = pl.ds(pl.multiple_of(jnp.where(alone, share, n) * SUB, SUB), SUB)
-                cols_ref[there, :] = cols_ref[there, :] + tree(down)
+            if both_ways:
+                alone = a == n
+                add_to(jnp.where(alone, share, a), along)
+                add_to(jnp.where(alone, share, n), tree(down))
+            else:
+                add_to(a, along)
 
     def turn(i, carry):
         state, found = carry
@@ -340,10 +348,10 @@
 
 
 def build_inner(
-    meta, table, near, plan, outer_runs, tiles, sides, middles, weights, rows_out, cols_out, self_ref,
-    inner_runs, rows_ref, cols_ref, *buffers,
+    meta, table, near, plan, outer_runs, tiles, sides, middles, weights, sums_out, self_ref,
+    inner_runs, sums_ref, *buffers,
 ):
-    share, width = rows_out.shape[0], rows_out.shape[2]
+    share, width = weights.shape[:2]
     chunks = pieces_of(width)
     write_runs(meta, table, plan, inner_runs, outer_runs, share)
     for k in range(3):
@@ -355,12 +363,11 @@
         for which in range(2):
             sides[which, a] = own_side(centred, which).T.astype(jnp.bfloat16)
     spread_columns(weights, lambda a: a, near[3, 0:share, :])
-    cols_ref[...] = jnp.zeros_like(cols_ref)
-    rows_ref[...] = jnp.zeros_like(rows_ref)
+    sums_ref[...] = jnp.zeros_like(sums_ref)
     count = plan[share * FIELDS]
     flat_tiles(
         count, inner_runs, plan[share * FIELDS + 2], table, sides, middles, weights,
-        lambda k, n: near[k, pl.ds(n, 1), :], buffers, tiles, rows_ref, cols_ref,
+        lambda k, n: near[k, pl.ds(n, 1), :], buffers, tiles, sums_ref, True,
     )
     finish_tiles(tiles, count)
     lane = lax.broadcasted_iota(jnp.int32, (SUB, width), 1)
@@ -377,8 +384,7 @@
         return at + 1
 
     lax.fori_loop(0, meta[0], block, 0)
-    rows_out[...] = rows_ref[0:share]
-    cols_out[...] = cols_ref[0 : share * SUB, :]
+    sums_out[...] = sums_ref[0 : share * SUB, :]
 
 
 def count_listed(meta, lists, width):
@@ -415,15 +421,15 @@
         run(True)
 
 
-TAIL = 13
+TAIL = 14
 
 
 def build_outer(
     meta, table, plan, runs, around, first, second, density, source, tiles_in, sides, middles, weights,
-    rows_ref, cols_ref, self_ref, *rest
+    inner_sums, self_ref, *rest
 ):
     lists, rest = rest[:-TAIL], rest[-TAIL:]
-    again_ref, tiles, diagonal_ref, precond_ref, times, alone_ref, hood, work, sums_ref, extra, all_times, *buffers = rest
+    again_ref, tiles, diagonal_ref, precond_ref, times, alone_ref, hood, work, outer_sums, sums_ref, extra, all_times, *buffers = rest
     share, width = diagonal_ref.shape
     base, filled = meta[3], meta[4]
     even = lax.rem(lax.axis_index("piece"), 2) == 0
@@ -440,14 +446,14 @@
     again_ref[0] = again.astype(jnp.int32)
 
 
-    work[...] = jnp.zeros_like(work)
+    outer_sums[...] = jnp.zeros_like(outer_sums)
     count = plan[share * FIELDS + 1]
     flat_tiles(
         count, runs, plan[share * FIELDS + 3], table, sides, middles, weights,
-        lambda k, n: hood[k, pl.ds(base + share + n, 1), :], buffers, tiles, work, None,
+        lambda k, n: hood[k, pl.ds(base + share + n, 1), :], buffers, tiles, outer_sums, False,
     )
     finish_tiles(tiles, count)
-    sums_ref[...] = lane_sums([rows_ref[a] + work[a] for a in range(share)], share, width) + sub_sums(cols_ref)
+    sums_ref[...] = sub_sums(inner_sums) + sub_sums(outer_sums)[0:share]
 
     @pl.when(again)
     def _():
@@ -652,7 +658,7 @@
     inner_tiles = pltpu.VMEM((most_inner + 2 * GROUP, width, width), f32)
     outer_tiles = pltpu.VMEM((most_outer + 2 * GROUP, width, width), f32)
     ahead = pltpu.VMEM((GROUP, width, width), f32)
-    square_more = pltpu.VMEM((share + 1, width, width), f32)
+    narrow_more = pltpu.VMEM(((share + 1) * SUB, width), f32)
     square = pltpu.VMEM((share, width, width), f32)
     narrow = pltpu.VMEM((share * SUB, width), f32)
     table = jnp.asarray(FLAT)
@@ -700,21 +706,21 @@
     partner = [(q, d) if 0 <= q < pieces else (p, c ^ 1) for (q, d), (p, c) in zip(partner, device)]
     second = lax.ppermute(second, axes, [(i, q * columns + d) for i, (q, d) in enumerate(partner)])
 
-    plan, runs, tiles_in, sides, middles, weights, rows, cols, selfs = call(
+    plan, runs, tiles_in, sides, middles, weights, inner_sums, selfs = call(
         build_inner,
         (meta, table, near),
         [pltpu.SMEM((share * FIELDS + 4,), jnp.int32), pltpu.SMEM((6 * share + 3,), jnp.int32), inner_tiles,
-         pltpu.VMEM((2, share, width, width), jnp.bfloat16), pltpu.VMEM((3, share, width), f32), square, square, narrow, narrow],
-        [pltpu.SMEM((3 * share + 3,), jnp.int32), square_more, pltpu.VMEM(((share + 1) * SUB, width), f32), ahead, ahead],
+         pltpu.VMEM((2, share, width, width), jnp.bfloat16), pltpu.VMEM((3, share, width), f32), square, narrow, narrow],
+        [pltpu.SMEM((3 * share + 3,), jnp.int32), narrow_more, ahead, ahead],
         16 * most_inner,
     )
     plan, runs = (pltpu.with_memory_space_constraint(array, pltpu.SMEM) for array in (plan, runs))
     again, tiles_out, diagonal, precond, times, alone = call(
         build_outer,
         (meta, table, plan, runs, around, first, second, density, source,
-         held(tiles_in), held(sides), held(middles), held(weights), held(rows), held(cols), held(selfs), *lists),
+         held(tiles_in), held(sides), held(middles), held(weights), held(inner_sums), held(selfs), *lists),
         [pltpu.SMEM((1,), jnp.int32), outer_tiles, vector, vector, vector, vector],
-        [pltpu.VMEM((4, capacity + 2 * share, width), f32), square_more]
+        [pltpu.VMEM((4, capacity + 2 * share, width), f32), square, narrow_more]
         + [pltpu.VMEM((share, width), f32)] * 2 + [pltpu.VMEM((capacity, width), f32), ahead, ahead],
         16 * most_outer,
         scalars=4,

time: 70.1 us -> 72.4 us (1.033)
  Pallas kernels: 31 us -> 32.5 us
    pallas_call x8, Pallas kernels: 31 us -> 32.5 us  [call(): pl.pallas_call(kernel, out_shape=outs, in_specs=[SMEM] * scalars + [HBM]...]
  transfers between devices with their start and end apart: 19 -> 19, of which waited for: 7 -> 8; matrix products, arithmetic and copies ran while one was open for 1% -> 1% of each run, Pallas kernels for 30% -> 31%
where the time goes in v13:
time: 72.4 us; the launch traced here: 72.1 us
  Pallas kernels  32.5 us (45%)
  starting transfers between devices  29.9 us (41%)
  waiting for transfers between devices  8.16 us (11%)
  between operations  0.75 us (1%)
    pallas_call x8, Pallas kernels, call(): pl.pallas_call(kernel, out_shape=outs, in_specs=[SMEM] * scalars + [HBM]...  32.5 us
    ppermute x9, starting transfers between devices, swap(): lax.ppermute(values, axis, [(i, i ^ step) for i in range(lax.axis_size(ax...  17.2 us
    ppermute x8, starting transfers between devices, exchange(): return [lax.ppermute(field, axes, list(enumerate(to))) for to in swaps]  12.6 us
    ppermute x9, waiting for transfers between devices, swap(): lax.ppermute(values, axis, [(i, i ^ step) for i in range(lax.axis_size(ax...  6.15 us
    ppermute x8, waiting for transfers between devices, exchange(): return [lax.ppermute(field, axes, list(enumerate(to))) for to in swaps]  2 us
  transfers between devices with their start and end apart: 19, of which 8 were waited for; matrix products, arithmetic and copies ran while one was open for 1% of the time, Pallas kernels for 31%

profile of v13, /device:TPU:0, one launch (start us, length us, event | category | flops | bytes accessed | tf_op | source)
XLA Modules:
  0.0 72.1 jit_solution(12263259281036880701)
XLA Ops:
  0.6 3.1 %collective-permute-start.2 = (s32[7,128]{1,0:T(8,128)}, s32[7,128]{1,0:T(8,128)S(1)}, u32[]{:S(2)}, u32[]{:S(2)}) collective-permute-start(s32[7,128]{1,0:T(8,128)} %bitcast.1), channel_id=1, source_target_pairs={{0,1},{1,0},{2,3},{3,2},{4,5},{5,4},{6,7},{7,6},{8,9},{9,8},{10,11... | collective-permute-start | bytes 10760 | tf_op jit(solution)/shard_map/ppermute | solution.py:680
  3.7 1.7 %prepare.1 = (s32[8]{0:T(128)S(4)}, s32[1480]{0:T(1024)S(4)}, f32[4,192,128]{2,1,0:T(8,128)S(1)}, f32[4,64,128]{2,1,0:T(8,128)S(1)}, f32[32,128]{1,0:T(8,128)S(1...) custom-call(s32[8]{0:T(128)} %counts.1, f32[3]{0:T(128)} %densities.1, ...), custom_call_target="tpu_custom_call" | custom-call | tf_op jit(solution)/shard_map/prepare/pallas_call | solution.py:667
  5.4 0.1 collective-permute-start
  5.5 0.1 collective-permute-start.1
  5.6 0.0 collective-permute-done.2
  5.6 0.7 pad_add_fusion.rest_0_
  6.3 4.0 %collective-permute-start.3 = (s32[14,128]{1,0:T(8,128)S(1)}, s32[14,128]{1,0:T(8,128)S(1)}, u32[]{:S(2)}, u32[]{:S(2)}) collective-permute-start(s32[14,128]{1,0:T(8,128)S(1)} %pad_add_fusion.rest_0_), channel_id=1, source_target_pairs={{0,3},{1,2},{2,1},{3,0},{4,7},{5,6},{6,5},{7,4},{8,11},{9,10},{10,... | collective-permute-start | bytes 21512 | tf_op jit(solution)/shard_map/ppermute | solution.py:680
  10.3 12.0 %build_inner.1 = (s32[196]{0:T(256)S(4)}, s32[195]{0:T(256)S(4)}, f32[224,128,128]{2,1,0:T(8,128)S(1)}, bf16[2,32,128,128]{3,2,1,0:T(8,128)(2,1)S(1)}, f32[3,32,...) custom-call(s32[8]{0:T(128)S(4)} %get-tuple-element.33.meta, ...), custom_call_target="tpu_custom_call" | custom-call | flops 56623104 | tf_op jit(solution)/shard_map/build_inner/pallas_call | solution.py:667
  22.3 0.0 collective-permute-done.3.rest_1_
  22.3 0.0 collective-permute-done.first
  22.4 0.0 collective-permute-done.1.second
  22.4 4.9 %build_outer.1 = (s32[1]{0:T(128)S(4)}, f32[230,128,128]{2,1,0:T(8,128)S(1)}, f32[32,128]{1,0:T(8,128)S(1)}, f32[32,128]{1,0:T(8,128)S(1)}, f32[32,128]{1,0:T(8,128)S(1)}, /*index=5*/f32[32,128]{1,0:T(8,128)S(1)}) custom-call(s32[8]{0:T(128)S(4)} %get-tuple-element.33.meta, s32[1480]{0:T(1024)S(4)} %get-tuple-element.34.table, ...), custom_call_target="tpu_custom_call" | custom-call | flops 58195968 | tf_op jit(solution)/shard_map/build_outer/pallas_call | solution.py:667
  27.2 3.6 %collective-permute-start.7 = (f32[32,128]{1,0:T(8,128)S(1)}, f32[32,128]{1,0:T(8,128)S(1)}, u32[]{:S(2)}, u32[]{:S(2)}) collective-permute-start(f32[32,128]{1,0:T(8,128)S(1)} %get-tuple-element.48.field.precond), channel_id=1, source_target_pairs={{0,1},{1,3},{2,4},{3,0},{4,2},{5,7},{6,8},{7,5},{8,6},{9,11},{10,1... | collective-permute-start | bytes 49160 | tf_op jit(solution)/shard_map/ppermute | solution.py:754
  30.9 3.4 %collective-permute-start.6 = (f32[32,128]{1,0:T(8,128)S(1)}, f32[32,128]{1,0:T(8,128)S(1)}, u32[]{:S(2)}, u32[]{:S(2)}) collective-permute-start(f32[32,128]{1,0:T(8,128)S(1)} %get-tuple-element.48.field.precond), channel_id=1, source_target_pairs={{0,2},{1,4},{2,3},{3,0},{4,1},{5,8},{6,7},{7,6},{8,5},{9,12},{10,1... | collective-permute-start | bytes 49160 | tf_op jit(solution)/shard_map/ppermute | solution.py:754
  34.3 0.0 collective-permute-start.5
  34.3 0.6 collective-permute-start.4
  34.8 4.3 %apply_inner.2 = (f32[32,128,128]{2,1,0:T(8,128)S(1)}, f32[256,128]{1,0:T(8,128)S(1)}) custom-call(s32[8]{0:T(128)S(4)} %get-tuple-element.33.meta, s32[1480]{0:T(1024)S(4)} %get-tuple-element.34.table, s32[196]{0:T(256)S(4)} %get-tuple-element.36.plan, s32[1]{0:T(128)S(4)} %get-tuple-element.49.again, f32[32,128]{1,0:T(8,128)S(1)} %get-tuple-element.48.field.precond, ...), custom_call_target="tpu_custom_call" | custom-call | flops 14155776 | tf_op jit(solution)/shard_map/apply_inner/pallas_call | solution.py:667
  39.1 0.0 collective-permute-done.7.rest_3_
  39.1 0.0 collective-permute-done.6.rest_2_
  39.2 1.9 %collective-permute-done.5.rest_1_ = f32[32,128]{1,0:T(8,128)S(1)} collective-permute-done((f32[32,128]{1,0:T(8,128)S(1)}, f32[32,128]{1,0:T(8,128)S(1)}, u32[]{:S(2)}, u32[]{:S(2)}) %collective-permute-start.5) | collective-permute-done | bytes 16416 | tf_op jit(solution)/shard_map/ppermute | solution.py:754
  41.0 0.0 collective-permute-done.4.rest_0_
  41.0 2.2 %apply_first.1 = (f32[32,128]{1,0:T(8,128)S(1)}, f32[32,128]{1,0:T(8,128)S(1)}) custom-call(s32[8]{0:T(128)S(4)} %get-tuple-element.33.meta, s32[1480]{0:T(1024)S(4)} %get-tuple-element.34.table, s32[196]{0:T(256)S(4)} %get-tuple-element.36.plan, s32[1]{0:T(128)S(4)} %get-tuple-element.49.again, f32[32,128]{1,0:T(8,128)S(1)} %get-tuple-element.50.diagonal, ...), custom_call_target="tpu_custom_call" | custom-call | flops 7274496 | tf_op jit(solution)/shard_map/apply_first/pallas_call | solution.py:667
  43.2 0.3 collective-permute-start.11
  43.5 2.2 %collective-permute-start.10 = (f32[32,128]{1,0:T(8,128)S(1)}, f32[32,128]{1,0:T(8,128)S(1)}, u32[]{:S(2)}, u32[]{:S(2)}) collective-permute-start(f32[32,128]{1,0:T(8,128)S(1)} %get-tuple-element.57.field.scaled), channel_id=1, source_target_pairs={{0,2},{1,4},{2,3},{3,0},{4,1},{5,8},{6,7},{7,6},{8,5},{9,12},{10,1... | collective-permute-start | bytes 49160 | tf_op jit(solution)/shard_map/ppermute | solution.py:754
  45.8 2.4 %collective-permute-start.9 = (f32[32,128]{1,0:T(8,128)S(1)}, f32[32,128]{1,0:T(8,128)S(1)}, u32[]{:S(2)}, u32[]{:S(2)}) collective-permute-start(f32[32,128]{1,0:T(8,128)S(1)} %get-tuple-element.57.field.scaled), channel_id=1, source_target_pairs={{0,31},{1,2},{2,1},{3,4},{4,3},{5,6},{6,5},{7,8},{8,7},{9,10},{10,... | collective-permute-start | bytes 49160 | tf_op jit(solution)/shard_map/ppermute | solution.py:754
  48.1 0.0 collective-permute-start.8
  48.2 4.3 %apply_inner.3 = (f32[32,128,128]{2,1,0:T(8,128)S(1)}, f32[256,128]{1,0:T(8,128)S(1)}) custom-call(s32[8]{0:T(128)S(4)} %get-tuple-element.33.meta, s32[1480]{0:T(1024)S(4)} %get-tuple-element.34.table, s32[196]{0:T(256)S(4)} %get-tuple-element.36.plan, s32[1]{0:T(128)S(4)} %get-tuple-element.49.again, f32[32,128]{1,0:T(8,128)S(1)} %get-tuple-element.57.field.scaled, ...), custom_call_target="tpu_custom_call" | custom-call | flops 14155776 | tf_op jit(solution)/shard_map/apply_inner/pallas_call | solution.py:667
  52.5 0.0 collective-permute-done.11.rest_3_
  52.5 0.0 collective-permute-done.10.rest_2_
  52.5 0.1 collective-permute-done.9.rest_1_
  52.6 0.0 collective-permute-done.8.rest_0_
  52.6 2.2 %apply_second.1 = (f32[32,128]{1,0:T(8,128)S(1)}, f32[8,128]{1,0:T(8,128)S(1)}) custom-call(s32[8]{0:T(128)S(4)} %get-tuple-element.33.meta, s32[1480]{0:T(1024)S(4)} %get-tuple-element.34.table, s32[196]{0:T(256)S(4)} %get-tuple-element.36.plan, s32[1]{0:T(128)S(4)} %get-tuple-element.49.again, f32[32,128]{1,0:T(8,128)S(1)} %get-tuple-element.32.source, ...), custom_call_target="tpu_custom_call" | custom-call | flops 7274496 | tf_op jit(solution)/shard_map/apply_second/pallas_call | solution.py:667
  54.9 0.5 collective-permute-start.12
  55.4 0.8 %collective-permute-done.12 = f32[8,128]{1,0:T(8,128)S(1)} collective-permute-done((f32[8,128]{1,0:T(8,128)S(1)}, f32[8,128]{1,0:T(8,128)S(1)}, u32[]{:S(2)}, u32[]{:S(2)}) %collective-permute-start.12) | collective-permute-done | bytes 4128 | tf_op jit(solution)/shard_map/ppermute | solution.py:680
  56.2 2.8 %collective-permute-start.15 = (f32[8,128]{1,0:T(8,128)S(1)}, f32[8,128]{1,0:T(8,128)S(1)}, u32[]{:S(2)}, u32[]{:S(2)}) collective-permute-start(f32[8,128]{1,0:T(8,128)S(1)} %add.12), channel_id=1, source_target_pairs={{0,3},{1,2},{2,1},{3,0},{4,7},{5,6},{6,5},{7,4},{8,11},{9,10},{10,... | collective-permute-start | bytes 12296 | tf_op jit(solution)/shard_map/ppermute | solution.py:680
  58.9 1.1 %collective-permute-start.14 = (f32[8,128]{1,0:T(8,128)S(1)}, f32[8,128]{1,0:T(8,128)S(1)}, u32[]{:S(2)}, u32[]{:S(2)}) collective-permute-start(f32[8,128]{1,0:T(8,128)S(1)} %add.12), channel_id=1, source_target_pairs={{0,2},{1,3},{2,0},{3,1},{4,6},{5,7},{6,4},{7,5},{8,10},{9,11},{10,... | collective-permute-start | bytes 12296 | tf_op jit(solution)/shard_map/ppermute | solution.py:680
  60.1 0.5 collective-permute-start.13
  60.6 1.0 %collective-permute-done.15 = f32[8,128]{1,0:T(8,128)S(1)} collective-permute-done((f32[8,128]{1,0:T(8,128)S(1)}, f32[8,128]{1,0:T(8,128)S(1)}, u32[]{:S(2)}, u32[]{:S(2)}) %collective-permute-start.15) | collective-permute-done | bytes 4128 | tf_op jit(solution)/shard_map/ppermute | solution.py:680
  61.6 1.9 %collective-permute-done.14 = f32[8,128]{1,0:T(8,128)S(1)} collective-permute-done((f32[8,128]{1,0:T(8,128)S(1)}, f32[8,128]{1,0:T(8,128)S(1)}, u32[]{:S(2)}, u32[]{:S(2)}) %collective-permute-start.14) | collective-permute-done | bytes 4128 | tf_op jit(solution)/shard_map/ppermute | solution.py:680
  63.4 0.2 collective-permute-done.13
  63.7 3.0 %collective-permute-start.18 = (f32[8,128]{1,0:T(8,128)S(1)}, f32[8,128]{1,0:T(8,128)S(1)}, u32[]{:S(2)}, u32[]{:S(2)}) collective-permute-start(f32[8,128]{1,0:T(8,128)S(1)} %add_add_fusion.rest_0_), channel_id=1, source_target_pairs={{0,24},{4,28},{8,16},{12,20},{16,8},{20,12},{24,0},{28,4},{1,25},{... | collective-permute-start | bytes 12296 | tf_op jit(solution)/shard_map/ppermute | solution.py:680
  66.7 0.8 %collective-permute-start.17 = (f32[8,128]{1,0:T(8,128)S(1)}, f32[8,128]{1,0:T(8,128)S(1)}, u32[]{:S(2)}, u32[]{:S(2)}) collective-permute-start(f32[8,128]{1,0:T(8,128)S(1)} %add_add_fusion.rest_0_), channel_id=1, source_target_pairs={{0,16},{4,20},{8,24},{12,28},{16,0},{20,4},{24,8},{28,12},{1,17},{... | collective-permute-start | bytes 12296 | tf_op jit(solution)/shard_map/ppermute | solution.py:680
  67.5 1.4 %collective-permute-start.16 = (f32[8,128]{1,0:T(8,128)S(1)}, f32[8,128]{1,0:T(8,128)S(1)}, u32[]{:S(2)}, u32[]{:S(2)}) collective-permute-start(f32[8,128]{1,0:T(8,128)S(1)} %add_add_fusion.rest_0_), channel_id=1, source_target_pairs={{0,8},{4,12},{8,0},{12,4},{16,24},{20,28},{24,16},{28,20},{1,9},{5... | collective-permute-start | bytes 12296 | tf_op jit(solution)/shard_map/ppermute | solution.py:680
  68.9 0.0 collective-permute-done.18.rest_3_
  68.9 1.4 %collective-permute-done.17.rest_2_ = f32[8,128]{1,0:T(8,128)S(1)} collective-permute-done((f32[8,128]{1,0:T(8,128)S(1)}, f32[8,128]{1,0:T(8,128)S(1)}, u32[]{:S(2)}, u32[]{:S(2)}) %collective-permute-start.17) | collective-permute-done | bytes 4128 | tf_op jit(solution)/shard_map/ppermute | solution.py:680
  70.3 0.8 %collective-permute-done.16.rest_1_ = f32[8,128]{1,0:T(8,128)S(1)} collective-permute-done((f32[8,128]{1,0:T(8,128)S(1)}, f32[8,128]{1,0:T(8,128)S(1)}, u32[]{:S(2)}, u32[]{:S(2)}) %collective-permute-start.16) | collective-permute-done | bytes 4128 | tf_op jit(solution)/shard_map/ppermute | solution.py:680
  71.1 0.9 %finish.1 = (f32[32,128]{1,0:T(8,128)}, f32[32,128]{1,0:T(8,128)}) custom-call(f32[32,128]{1,0:T(8,128)S(1)} %get-tuple-element.32.source, f32[32,128]{1,0:T(8,128)S(1)} %get-tuple-element.48.field.precond, f32[32,128]{1,0:T(8,128)S(1)} %get-tuple-element.56.spill, f32[32,128]{1,0:T(8,128)S(1)} %get-tuple-element.57.field.scaled, ...), custom_call_target="tpu_custom_call" | custom-call | tf_op jit(solution)/shard_map/finish/pallas_call | solution.py:667
  (2 shorter events, 0.0 us)
Async XLA Ops:
  0.6 5.0 %collective-permute-start.2 = (s32[7,128]{1,0:T(8,128)}, s32[7,128]{1,0:T(8,128)S(1)}, u32[]{:S(2)}, u32[]{:S(2)}) collective-permute-start(s32[7,128]{1,0:T(8,128)} %bitcast.1), channel_id=1, source_target_pairs={{0,1},{1,0},{2,3},{3,2},{4,5},{5,4},{6,7},{7,6},{8,9},{9,8},{10,11... | collective-permute-start | bytes 10760 | tf_op jit(solution)/shard_map/ppermute | solution.py:680
  5.4 16.9 %collective-permute-start = (f32[4,32,128]{2,1,0:T(8,128)S(1)}, f32[4,32,128]{2,1,0:T(8,128)S(1)}, u32[]{:S(2)}, u32[]{:S(2)}) collective-permute-start(f32[4,32,128]{2,1,0:T(8,128)S(1)} %get-tuple-element.39), channel_id=1, source_target_pairs={{0,4},{4,0},{8,12},{12,8},{16,20},{20,16},{24,28},{28,24},{1,5},{5... | collective-permute-start | bytes 196616 | tf_op jit(solution)/shard_map/ppermute | solution.py:702
  5.5 16.8 %collective-permute-start.1 = (f32[4,32,128]{2,1,0:T(8,128)S(1)}, f32[4,32,128]{2,1,0:T(8,128)S(1)}, u32[]{:S(2)}, u32[]{:S(2)}) collective-permute-start(f32[4,32,128]{2,1,0:T(8,128)S(1)} %get-tuple-element.40), channel_id=1, source_target_pairs={{0,1},{1,0},{2,3},{3,2},{4,8},{5,9},{6,10},{7,11},{8,4},{9,5},{10,... | collective-permute-start | bytes 196616 | tf_op jit(solution)/shard_map/ppermute | solution.py:707
  6.3 16.0 %collective-permute-start.3 = (s32[14,128]{1,0:T(8,128)S(1)}, s32[14,128]{1,0:T(8,128)S(1)}, u32[]{:S(2)}, u32[]{:S(2)}) collective-permute-start(s32[14,128]{1,0:T(8,128)S(1)} %pad_add_fusion.rest_0_), channel_id=1, source_target_pairs={{0,3},{1,2},{2,1},{3,0},{4,7},{5,6},{6,5},{7,4},{8,11},{9,10},{10,... | collective-permute-start | bytes 21512 | tf_op jit(solution)/shard_map/ppermute | solution.py:680
  27.2 11.9 %collective-permute-start.7 = (f32[32,128]{1,0:T(8,128)S(1)}, f32[32,128]{1,0:T(8,128)S(1)}, u32[]{:S(2)}, u32[]{:S(2)}) collective-permute-start(f32[32,128]{1,0:T(8,128)S(1)} %get-tuple-element.48.field.precond), channel_id=1, source_target_pairs={{0,1},{1,3},{2,4},{3,0},{4,2},{5,7},{6,8},{7,5},{8,6},{9,11},{10,1... | collective-permute-start | bytes 49160 | tf_op jit(solution)/shard_map/ppermute | solution.py:754
  30.9 8.3 %collective-permute-start.6 = (f32[32,128]{1,0:T(8,128)S(1)}, f32[32,128]{1,0:T(8,128)S(1)}, u32[]{:S(2)}, u32[]{:S(2)}) collective-permute-start(f32[32,128]{1,0:T(8,128)S(1)} %get-tuple-element.48.field.precond), channel_id=1, source_target_pairs={{0,2},{1,4},{2,3},{3,0},{4,1},{5,8},{6,7},{7,6},{8,5},{9,12},{10,1... | collective-permute-start | bytes 49160 | tf_op jit(solution)/shard_map/ppermute | solution.py:754
  34.3 6.8 %collective-permute-start.5 = (f32[32,128]{1,0:T(8,128)S(1)}, f32[32,128]{1,0:T(8,128)S(1)}, u32[]{:S(2)}, u32[]{:S(2)}) collective-permute-start(f32[32,128]{1,0:T(8,128)S(1)} %get-tuple-element.48.field.precond), channel_id=1, source_target_pairs={{0,31},{1,2},{2,1},{3,4},{4,3},{5,6},{6,5},{7,8},{8,7},{9,10},{10,... | collective-permute-start | bytes 49160 | tf_op jit(solution)/shard_map/ppermute | solution.py:754
  34.3 6.8 %collective-permute-start.4 = (f32[32,128]{1,0:T(8,128)S(1)}, f32[32,128]{1,0:T(8,128)S(1)}, u32[]{:S(2)}, u32[]{:S(2)}) collective-permute-start(f32[32,128]{1,0:T(8,128)S(1)} %get-tuple-element.48.field.precond), channel_id=1, source_target_pairs={{0,1},{1,0},{2,3},{3,2},{4,5},{5,4},{6,7},{7,6},{8,9},{9,8},{10,11... | collective-permute-start | bytes 49160 | tf_op jit(solution)/shard_map/ppermute | solution.py:754
  43.2 9.3 %collective-permute-start.11 = (f32[32,128]{1,0:T(8,128)S(1)}, f32[32,128]{1,0:T(8,128)S(1)}, u32[]{:S(2)}, u32[]{:S(2)}) collective-permute-start(f32[32,128]{1,0:T(8,128)S(1)} %get-tuple-element.57.field.scaled), channel_id=1, source_target_pairs={{0,1},{1,3},{2,4},{3,0},{4,2},{5,7},{6,8},{7,5},{8,6},{9,11},{10,1... | collective-permute-start | bytes 49160 | tf_op jit(solution)/shard_map/ppermute | solution.py:754
  43.5 9.0 %collective-permute-start.10 = (f32[32,128]{1,0:T(8,128)S(1)}, f32[32,128]{1,0:T(8,128)S(1)}, u32[]{:S(2)}, u32[]{:S(2)}) collective-permute-start(f32[32,128]{1,0:T(8,128)S(1)} %get-tuple-element.57.field.scaled), channel_id=1, source_target_pairs={{0,2},{1,4},{2,3},{3,0},{4,1},{5,8},{6,7},{7,6},{8,5},{9,12},{10,1... | collective-permute-start | bytes 49160 | tf_op jit(solution)/shard_map/ppermute | solution.py:754
  45.8 6.9 %collective-permute-start.9 = (f32[32,128]{1,0:T(8,128)S(1)}, f32[32,128]{1,0:T(8,128)S(1)}, u32[]{:S(2)}, u32[]{:S(2)}) collective-permute-start(f32[32,128]{1,0:T(8,128)S(1)} %get-tuple-element.57.field.scaled), channel_id=1, source_target_pairs={{0,31},{1,2},{2,1},{3,4},{4,3},{5,6},{6,5},{7,8},{8,7},{9,10},{10,... | collective-permute-start | bytes 49160 | tf_op jit(solution)/shard_map/ppermute | solution.py:754
  48.1 4.5 %collective-permute-start.8 = (f32[32,128]{1,0:T(8,128)S(1)}, f32[32,128]{1,0:T(8,128)S(1)}, u32[]{:S(2)}, u32[]{:S(2)}) collective-permute-start(f32[32,128]{1,0:T(8,128)S(1)} %get-tuple-element.57.field.scaled), channel_id=1, source_target_pairs={{0,1},{1,0},{2,3},{3,2},{4,5},{5,4},{6,7},{7,6},{8,9},{9,8},{10,11... | collective-permute-start | bytes 49160 | tf_op jit(solution)/shard_map/ppermute | solution.py:754
  54.9 1.3 %collective-permute-start.12 = (f32[8,128]{1,0:T(8,128)S(1)}, f32[8,128]{1,0:T(8,128)S(1)}, u32[]{:S(2)}, u32[]{:S(2)}) collective-permute-start(f32[8,128]{1,0:T(8,128)S(1)} %get-tuple-element.61), channel_id=1, source_target_pairs={{0,4},{4,0},{8,12},{12,8},{16,20},{20,16},{24,28},{28,24},{1,5},{5... | collective-permute-start | bytes 12296 | tf_op jit(solution)/shard_map/ppermute | solution.py:680
  56.2 5.4 %collective-permute-start.15 = (f32[8,128]{1,0:T(8,128)S(1)}, f32[8,128]{1,0:T(8,128)S(1)}, u32[]{:S(2)}, u32[]{:S(2)}) collective-permute-start(f32[8,128]{1,0:T(8,128)S(1)} %add.12), channel_id=1, source_target_pairs={{0,3},{1,2},{2,1},{3,0},{4,7},{5,6},{6,5},{7,4},{8,11},{9,10},{10,... | collective-permute-start | bytes 12296 | tf_op jit(solution)/shard_map/ppermute | solution.py:680
  58.9 4.5 %collective-permute-start.14 = (f32[8,128]{1,0:T(8,128)S(1)}, f32[8,128]{1,0:T(8,128)S(1)}, u32[]{:S(2)}, u32[]{:S(2)}) collective-permute-start(f32[8,128]{1,0:T(8,128)S(1)} %add.12), channel_id=1, source_target_pairs={{0,2},{1,3},{2,0},{3,1},{4,6},{5,7},{6,4},{7,5},{8,10},{9,11},{10,... | collective-permute-start | bytes 12296 | tf_op jit(solution)/shard_map/ppermute | solution.py:680
  60.1 3.6 %collective-permute-start.13 = (f32[8,128]{1,0:T(8,128)S(1)}, f32[8,128]{1,0:T(8,128)S(1)}, u32[]{:S(2)}, u32[]{:S(2)}) collective-permute-start(f32[8,128]{1,0:T(8,128)S(1)} %add.12), channel_id=1, source_target_pairs={{0,1},{1,0},{2,3},{3,2},{4,5},{5,4},{6,7},{7,6},{8,9},{9,8},{10,11... | collective-permute-start | bytes 12296 | tf_op jit(solution)/shard_map/ppermute | solution.py:680
  63.7 5.2 %collective-permute-start.18 = (f32[8,128]{1,0:T(8,128)S(1)}, f32[8,128]{1,0:T(8,128)S(1)}, u32[]{:S(2)}, u32[]{:S(2)}) collective-permute-start(f32[8,128]{1,0:T(8,128)S(1)} %add_add_fusion.rest_0_), channel_id=1, source_target_pairs={{0,24},{4,28},{8,16},{12,20},{16,8},{20,12},{24,0},{28,4},{1,25},{... | collective-permute-start | bytes 12296 | tf_op jit(solution)/shard_map/ppermute | solution.py:680
  66.7 3.6 %collective-permute-start.17 = (f32[8,128]{1,0:T(8,128)S(1)}, f32[8,128]{1,0:T(8,128)S(1)}, u32[]{:S(2)}, u32[]{:S(2)}) collective-permute-start(f32[8,128]{1,0:T(8,128)S(1)} %add_add_fusion.rest_0_), channel_id=1, source_target_pairs={{0,16},{4,20},{8,24},{12,28},{16,0},{20,4},{24,8},{28,12},{1,17},{... | collective-permute-start | bytes 12296 | tf_op jit(solution)/shard_map/ppermute | solution.py:680
  67.5 3.6 %collective-permute-start.16 = (f32[8,128]{1,0:T(8,128)S(1)}, f32[8,128]{1,0:T(8,128)S(1)}, u32[]{:S(2)}, u32[]{:S(2)}) collective-permute-start(f32[8,128]{1,0:T(8,128)S(1)} %add_add_fusion.rest_0_), channel_id=1, source_target_pairs={{0,8},{4,12},{8,0},{12,4},{16,24},{20,28},{24,16},{28,20},{1,9},{5... | collective-permute-start | bytes 12296 | tf_op jit(solution)/shard_map/ppermute | solution.py:680

commit v14 on v13

--- a/solution.py
+++ b/solution.py
@@ -51,8 +51,11 @@
 WIDEST = OFFSETS.shape[1]
 TABLE = np.concatenate([OFFSETS, BELOW], 1)
 STRIDE = TABLE.shape[1]
-FLAT = np.concatenate([TABLE.reshape(-1), np.zeros(8, np.int32)])
 LIMIT = pltpu.CompilerParams(vmem_limit_bytes=8 * 1024 * 1024)
+
+
+def evened(count):
+    return (count + 1) // 2 * 2 if isinstance(count, int) else lax.bitwise_and(count + 1, -2)
 
 
 def tile_bounds(share):
@@ -63,8 +66,8 @@
             for a in range(live):
                 code = (first + a) % LAYER
                 row = [int(o) for o in OFFSETS[code][: BELOW[code, -1]]]
-                near += sum(0 <= a + o and o <= 0 for o in row)
-                far += sum(a + o < 0 or a + o >= live for o in row)
+                near += evened(sum(0 <= a + o and o <= 0 for o in row))
+                far += evened(sum(a + o < 0 or a + o >= live for o in row))
             inner, outer = max(inner, near), max(outer, far)
     return inner, outer
 
@@ -91,8 +94,12 @@
     plan[a * FIELDS + 5] = row + resume - ahead
 
 
-def write_run(runs, at, a, start, count):
-    runs[3 * at], runs[3 * at + 1], runs[3 * at + 2] = a, start, count
+RUN = 5
+
+
+def write_run(runs, at, a, count, ahead, start, start_after):
+    for k, value in enumerate((a, count, ahead, start, start_after)):
+        runs[RUN * at + k] = value
     return at + (count > 0).astype(jnp.int32)
 
 
@@ -102,13 +109,14 @@
         write_plan(meta, table, plan, a)
         alive = a < meta[0]
         count, start, count_far, ahead, start_far, start_after = (plan[a * FIELDS + k] for k in range(FIELDS))
-        inner = write_run(inner_runs, inner, a, start, jnp.where(alive, count + 1, 0))
-        outer = write_run(outer_runs, outer, a, start_far, jnp.where(alive, ahead, 0))
-        outer = write_run(outer_runs, outer, a, start_after + ahead, jnp.where(alive, count_far - ahead, 0))
-        total = total + jnp.where(alive, count + 1, 0)
-        far = far + jnp.where(alive, count_far, 0)
+        count, count_far = jnp.where(alive, count + 1, 0), jnp.where(alive, count_far, 0)
+        inner = write_run(inner_runs, inner, a, count, count, start, start)
+        outer = write_run(outer_runs, outer, a, count_far, ahead, start_far, start_after)
+        total, far = total + evened(count), far + evened(count_far)
     for runs, at in ((inner_runs, inner), (outer_runs, outer)):
-        write_run(runs, at, share, len(FLAT) - 8, jnp.int32(1))
+        runs[RUN * at], runs[RUN * at + 1] = share, 0
+        for k in range(2, RUN):
+            runs[RUN * at + k] = 0
     plan[share * FIELDS] = total
     plan[share * FIELDS + 1] = far
     plan[share * FIELDS + 2] = inner
@@ -202,7 +210,10 @@
 GROUP = 4
 
 
-def flat_tiles(count, runs, most, table, sides, middles, weights, other_at, buffers, tiles, sums_ref, both_ways):
+FAR = 1024.0
+
+
+def flat_tiles(count, runs, most, empty, table, sides, middles, weights, other_at, buffers, tiles, sums_ref, both_ways):
     share, width = weights.shape[:2]
     chunks = pieces_of(width)
     lane = lax.broadcasted_iota(jnp.int32, (SUB, width), 1)
@@ -214,47 +225,54 @@
 
     def steps(state):
         found = []
-        for _ in range(GROUP):
+        for _ in range(GROUP // 2):
             run, t = state
-            a, start, size = (runs[3 * run + k] for k in range(3))
-            found.append((a, a + table[start + t]))
-            over = t + 1 >= size
-            state = jnp.minimum(run + over.astype(jnp.int32), most), jnp.where(over, 0, t + 1)
+            a, size, ahead, start, start_after = (runs[RUN * run + k] for k in range(RUN))
+            places = []
+            for u in (t, t + 1):
+                offset = table[u + jnp.where(u < ahead, start, start_after)]
+                places.append(jnp.where(u < size, a + offset, empty))
+            found.append((a, places))
+            over = t + 2 >= size
+            state = jnp.minimum(run + over.astype(jnp.int32), most), jnp.where(over, 0, t + 2)
         return state, found
 
-    def other_of(a, n):
-        here = pl.ds(a, 1)
-        return [wide(other_at(c, n)) - wide(middles[c, here, :]) for c in range(3)]
-
     def products(found, ahead):
-        for k in range(0, GROUP, 2):
-            (a, n), (b, m) = ((jnp.minimum(a, share - 1), n) for a, n in found[k : k + 2])
-            own = jnp.concatenate([sides[0, a], sides[1, b]], 0)
-            both = jnp.dot(own, other_sides(other_of(a, n), other_of(b, m)), preferred_element_type=jnp.float32)
-            ahead[k] = both[:width]
-            ahead[k + 1] = both[width:]
+        for k, (a, places) in enumerate(found):
+            own = jnp.minimum(a, share - 1)
+            here = pl.ds(own, 1)
+            middle = [wide(middles[c, here, :]) for c in range(3)]
+            others = [[wide(other_at(c, n)) - middle[c] for c in range(3)] for n in places]
+            both = jnp.dot(
+                jnp.concatenate([sides[0, own], sides[1, own]], 0), other_sides(*others),
+                preferred_element_type=jnp.float32,
+            )
+            ahead[2 * k] = both[:width]
+            ahead[2 * k + 1] = both[width:]
 
     def weigh(at, found, ahead):
-        for k, (a, n) in enumerate(found):
+        for k, (a, places) in enumerate(found):
             own = jnp.minimum(a, share - 1)
-            other = wide(other_at(3, n))
-            down = [None] * 2
+            others = [wide(other_at(3, n)) for n in places]
+            down = [[None] * 2 for _ in places]
             along = jnp.zeros((SUB, width), jnp.float32)
             for c, here in enumerate(chunks):
-                left = ahead[k, here, :]
-                rest = jnp.maximum(left, 0.0)
-                inverse = pltpu.reciprocal((1.01 - left) * (weights[own, here, :] + other), approx=True)
-                tile = rest * rest * inverse
-                tiles[at + k, here, :] = tile
-                along = jnp.where(diagonal == c * SUB, jnp.sum(tile, axis=1, keepdims=True), along)
-                if both_ways:
-                    gather(down, c, tile)
+                weight = weights[own, here, :]
+                pair = []
+                for u in range(2):
+                    left = ahead[2 * k + u, here, :]
+                    rest = jnp.maximum(left, 0.0)
+                    inverse = pltpu.reciprocal((1.01 - left) * (weight + others[u]), approx=True)
+                    tile = rest * rest * inverse
+                    tiles[at + 2 * k + u, here, :] = tile
+                    pair.append(tile)
+                    if both_ways:
+                        gather(down[u], c, tile)
+                along = jnp.where(diagonal == c * SUB, jnp.sum(pair[0] + pair[1], axis=1, keepdims=True), along)
+            add_to(a, along)
             if both_ways:
-                alone = a == n
-                add_to(jnp.where(alone, share, a), along)
-                add_to(jnp.where(alone, share, n), tree(down))
-            else:
-                add_to(a, along)
+                for n, partial in zip(places, down):
+                    add_to(jnp.where(n == a, share, n), tree(partial))
 
     def turn(i, carry):
         state, found = carry
@@ -349,7 +367,7 @@
 
 def build_inner(
     meta, table, near, plan, outer_runs, tiles, sides, middles, weights, sums_out, self_ref,
-    inner_runs, sums_ref, *buffers,
+    inner_runs, sums_ref, far_near, *buffers,
 ):
     share, width = weights.shape[:2]
     chunks = pieces_of(width)
@@ -364,24 +382,34 @@
             sides[which, a] = own_side(centred, which).T.astype(jnp.bfloat16)
     spread_columns(weights, lambda a: a, near[3, 0:share, :])
     sums_ref[...] = jnp.zeros_like(sums_ref)
+    for k in range(4):
+        far_near[k, 0 : 2 * share, :] = near[k]
+        far_near[k, share : share + SUB, :] = jnp.full((SUB, width), FAR, jnp.float32)
     count = plan[share * FIELDS]
     flat_tiles(
-        count, inner_runs, plan[share * FIELDS + 2], table, sides, middles, weights,
-        lambda k, n: near[k, pl.ds(n, 1), :], buffers, tiles, sums_ref, True,
+        count, inner_runs, plan[share * FIELDS + 2], share, table, sides, middles, weights,
+        lambda k, n: far_near[k, pl.ds(n, 1), :], buffers, tiles, sums_ref, True,
     )
     finish_tiles(tiles, count)
     lane = lax.broadcasted_iota(jnp.int32, (SUB, width), 1)
     sublane = lax.broadcasted_iota(jnp.int32, (SUB, width), 0)
 
     def block(a, at):
-        at = at + plan[a * FIELDS]
+        count = plan[a * FIELDS]
+        at = at + count
         down = [None] * 4
+        apart = [None] * 4
         for c, here in enumerate(chunks):
-            tile = jnp.where(lane == sublane + c * SUB, 0.0, tiles[at, here, :])
+            same = lane == sublane + c * SUB
+            whole = tiles[at, here, :]
+            tile = jnp.where(same, 0.0, whole)
             tiles[at, here, :] = tile
             gather(down, c, tile)
-        self_ref[pl.ds(pl.multiple_of(a * SUB, SUB), SUB), :] = tree(down)
-        return at + 1
+            gather(apart, c, jnp.where(same, whole, 0.0))
+        there = pl.ds(pl.multiple_of(a * SUB, SUB), SUB)
+        self_ref[there, :] = tree(down)
+        sums_ref[there, :] = sums_ref[there, :] - tree(apart)
+        return at - count + evened(count + 1)
 
     lax.fori_loop(0, meta[0], block, 0)
     sums_out[...] = sums_ref[0 : share * SUB, :]
@@ -435,8 +463,9 @@
     even = lax.rem(lax.axis_index("piece"), 2) == 0
     for k in range(4):
         hood[k, 0:share, :] = jnp.where(even, second[k], first[k])
-        hood[k, share:, :] = around[k, share:, :]
+        hood[k, share : around.shape[1], :] = around[k, share:, :]
         hood[k, pl.ds(share + filled, share), :] = jnp.where(even, first[k], second[k])
+    hood[:, around.shape[1] :, :] = jnp.full((4, SUB, width), FAR, jnp.float32)
     alive = alive_rows(meta, share, width)
     all_times[...] = count_listed(meta, lists, width)
     often = jnp.where(alive, all_times[pl.ds(pl.multiple_of(base, SUB), share), :], 0.0)
@@ -449,7 +478,7 @@
     outer_sums[...] = jnp.zeros_like(outer_sums)
     count = plan[share * FIELDS + 1]
     flat_tiles(
-        count, runs, plan[share * FIELDS + 3], table, sides, middles, weights,
+        count, runs, plan[share * FIELDS + 3], hood.shape[1] - SUB - base - share, table, sides, middles, weights,
         lambda k, n: hood[k, pl.ds(base + share + n, 1), :], buffers, tiles, outer_sums, False,
     )
     finish_tiles(tiles, count)
@@ -472,21 +501,24 @@
                 extra[there, :] = extra[there, :] + down * factor(times, n, a)
                 return at + 1
 
-            at = lax.fori_loop(0, count, inner, state[0]) + 1
+            at = lax.fori_loop(0, count, inner, state[0])
+            work[a] = work[a] + tiles_in[at]
+            at = at - count + evened(count + 1)
             count, place_far = outer_range(plan, table, a)
 
             def outer(t, at):
                 work[a] = work[a] + tiles[at] * factor(times, a, place_far(t))
                 return at + 1
 
-            return at, lax.fori_loop(0, count, outer, state[1])
+            lax.fori_loop(0, count, outer, state[1])
+            return at, state[1] + evened(count)
 
         lax.fori_loop(0, meta[0], block, (0, 0))
         sums_ref[...] = lane_sums(work, share, width) + extra[...]
 
     alone = jnp.sum(jnp.where(lane == REACH, often, 0.0), axis=1, keepdims=True)
     alone_ref[...] = jnp.broadcast_to(alone, (share, width))
-    pairs = jnp.where(alive, sums_ref[...] + sub_sums(self_ref) * alone, 0.0)
+    pairs = jnp.where(alive, sums_ref[...] + sub_sums(self_ref) * (alone - 1.0), 0.0)
     diagonal = 1.0 / density[...] + pairs
     diagonal_ref[...] = diagonal
     precond_ref[...] = source[...] / diagonal
@@ -533,11 +565,10 @@
 
             zero = jnp.zeros((SUB, width), jnp.float32)
             _, sums = padded_sweep(count, fetch, pairs, (at, [zero] * len(chunks)))
-            at = at + count
             value = wide(lone[pl.ds(a, 1), :])
             for here, old in zip(chunks, sums):
-                rows_ref[a, here, :] = old + tiles[at, here, :] * value
-            return at + 1
+                rows_ref[a, here, :] = old + tiles[at + count, here, :] * value
+            return at + evened(count + 1)
 
         lax.fori_loop(0, meta[0], block, 0)
 
@@ -589,7 +620,7 @@
             _, sums = padded_sweep(count, fetch, pairs, (at, [rows_ref[a, here, :] for here in chunks]))
             for here, values in zip(chunks, sums):
                 work[a, here, :] = values
-            return at + count
+            return at + evened(count)
 
         lax.fori_loop(0, meta[0], block, 0)
 
@@ -661,7 +692,7 @@
     narrow_more = pltpu.VMEM(((share + 1) * SUB, width), f32)
     square = pltpu.VMEM((share, width, width), f32)
     narrow = pltpu.VMEM((share * SUB, width), f32)
-    table = jnp.asarray(FLAT)
+    table = jnp.asarray(TABLE.reshape(-1))
 
     def call(kernel, args, outs, scratch=(), work=0, scalars=2, far=0, **more):
         return pl.pallas_call(
@@ -709,9 +740,9 @@
     plan, runs, tiles_in, sides, middles, weights, inner_sums, selfs = call(
         build_inner,
         (meta, table, near),
-        [pltpu.SMEM((share * FIELDS + 4,), jnp.int32), pltpu.SMEM((6 * share + 3,), jnp.int32), inner_tiles,
+        [pltpu.SMEM((share * FIELDS + 4,), jnp.int32), pltpu.SMEM((RUN * (share + 1),), jnp.int32), inner_tiles,
          pltpu.VMEM((2, share, width, width), jnp.bfloat16), pltpu.VMEM((3, share, width), f32), square, narrow, narrow],
-        [pltpu.SMEM((3 * share + 3,), jnp.int32), narrow_more, ahead, ahead],
+        [pltpu.SMEM((RUN * (share + 1),), jnp.int32), narrow_more, pltpu.VMEM((4, 2 * share, width), f32), ahead, ahead],
         16 * most_inner,
     )
     plan, runs = (pltpu.with_memory_space_constraint(array, pltpu.SMEM) for array in (plan, runs))
@@ -720,7 +751,7 @@
         (meta, table, plan, runs, around, first, second, density, source,
          held(tiles_in), held(sides), held(middles), held(weights), held(inner_sums), held(selfs), *lists),
         [pltpu.SMEM((1,), jnp.int32), outer_tiles, vector, vector, vector, vector],
-        [pltpu.VMEM((4, capacity + 2 * share, width), f32), square, narrow_more]
+        [pltpu.VMEM((4, capacity + 2 * share + SUB, width), f32), square, narrow_more]
         + [pltpu.VMEM((share, width), f32)] * 2 + [pltpu.VMEM((capacity, width), f32), ahead, ahead],
         16 * most_outer,
         scalars=4,

time: 72.4 us -> 72.8 us (level)
  transfers between devices with their start and end apart: 19 -> 19, of which waited for: 8 -> 7; matrix products, arithmetic and copies ran while one was open for 1% -> 1% of each run, Pallas kernels for 31% -> 32%
where the time goes in v14:
time: 72.8 us; the launch traced here: 72.4 us
  Pallas kernels  32.8 us (45%)
  starting transfers between devices  29.4 us (40%)
  waiting for transfers between devices  8.69 us (12%)
  between operations  0.78 us (1%)
    pallas_call x8, Pallas kernels, call(): pl.pallas_call(kernel, out_shape=outs, in_specs=[SMEM] * scalars + [HBM]...  32.8 us
    ppermute x9, starting transfers between devices, swap(): lax.ppermute(values, axis, [(i, i ^ step) for i in range(lax.axis_size(ax...  16.8 us
    ppermute x8, starting transfers between devices, exchange(): return [lax.ppermute(field, axes, list(enumerate(to))) for to in swaps]  12.5 us
    ppermute x9, waiting for transfers between devices, swap(): lax.ppermute(values, axis, [(i, i ^ step) for i in range(lax.axis_size(ax...  6.73 us
    ppermute x8, waiting for transfers between devices, exchange(): return [lax.ppermute(field, axes, list(enumerate(to))) for to in swaps]  1.95 us
  transfers between devices with their start and end apart: 19, of which 7 were waited for; matrix products, arithmetic and copies ran while one was open for 1% of the time, Pallas kernels for 32%

profile of v14, /device:TPU:0, one launch (start us, length us, event | category | flops | bytes accessed | tf_op | source)
XLA Modules:
  0.0 72.4 jit_solution(14507191019400936899)
XLA Ops:
  0.6 3.1 %collective-permute-start.2 = (s32[7,128]{1,0:T(8,128)}, s32[7,128]{1,0:T(8,128)S(1)}, u32[]{:S(2)}, u32[]{:S(2)}) collective-permute-start(s32[7,128]{1,0:T(8,128)} %bitcast.1), channel_id=1, source_target_pairs={{0,1},{1,0},{2,3},{3,2},{4,5},{5,4},{6,7},{7,6},{8,9},{9,8},{10,11... | collective-permute-start | bytes 10760 | tf_op jit(solution)/shard_map/ppermute | solution.py:711
  3.7 1.7 %prepare.1 = (s32[8]{0:T(128)S(4)}, s32[1472]{0:T(1024)S(4)}, f32[4,192,128]{2,1,0:T(8,128)S(1)}, f32[4,64,128]{2,1,0:T(8,128)S(1)}, f32[32,128]{1,0:T(8,128)S(1...) custom-call(s32[8]{0:T(128)} %counts.1, f32[3]{0:T(128)} %densities.1, ...), custom_call_target="tpu_custom_call" | custom-call | tf_op jit(solution)/shard_map/prepare/pallas_call | solution.py:698
  5.4 0.1 collective-permute-start
  5.5 0.1 collective-permute-start.1
  5.6 0.0 collective-permute-done.2
  5.6 0.7 pad_add_fusion.rest_0_
  6.3 4.0 %collective-permute-start.3 = (s32[14,128]{1,0:T(8,128)S(1)}, s32[14,128]{1,0:T(8,128)S(1)}, u32[]{:S(2)}, u32[]{:S(2)}) collective-permute-start(s32[14,128]{1,0:T(8,128)S(1)} %pad_add_fusion.rest_0_), channel_id=1, source_target_pairs={{0,3},{1,2},{2,1},{3,0},{4,7},{5,6},{6,5},{7,4},{8,11},{9,10},{10,... | collective-permute-start | bytes 21512 | tf_op jit(solution)/shard_map/ppermute | solution.py:711
  10.3 12.6 %build_inner.1 = (s32[196]{0:T(256)S(4)}, s32[165]{0:T(256)S(4)}, f32[240,128,128]{2,1,0:T(8,128)S(1)}, bf16[2,32,128,128]{3,2,1,0:T(8,128)(2,1)S(1)}, f32[3,32,...) custom-call(s32[8]{0:T(128)S(4)} %get-tuple-element.33.meta, ...), custom_call_target="tpu_custom_call" | custom-call | flops 60817408 | tf_op jit(solution)/shard_map/build_inner/pallas_call | solution.py:698
  23.0 0.0 collective-permute-done.3.rest_1_
  23.0 0.0 collective-permute-done.first
  23.0 0.0 collective-permute-done.1.second
  23.0 4.5 %build_outer.1 = (s32[1]{0:T(128)S(4)}, f32[246,128,128]{2,1,0:T(8,128)S(1)}, f32[32,128]{1,0:T(8,128)S(1)}, f32[32,128]{1,0:T(8,128)S(1)}, f32[32,128]{1,0:T(8,128)S(1)}, /*index=5*/f32[32,128]{1,0:T(8,128)S(1)}) custom-call(s32[8]{0:T(128)S(4)} %get-tuple-element.33.meta, s32[1472]{0:T(1024)S(4)} %get-tuple-element.34.table, ...), custom_call_target="tpu_custom_call" | custom-call | flops 62390272 | tf_op jit(solution)/shard_map/build_outer/pallas_call | solution.py:698
  27.5 3.6 %collective-permute-start.7 = (f32[32,128]{1,0:T(8,128)S(1)}, f32[32,128]{1,0:T(8,128)S(1)}, u32[]{:S(2)}, u32[]{:S(2)}) collective-permute-start(f32[32,128]{1,0:T(8,128)S(1)} %get-tuple-element.48.field.precond), channel_id=1, source_target_pairs={{0,1},{1,3},{2,4},{3,0},{4,2},{5,7},{6,8},{7,5},{8,6},{9,11},{10,1... | collective-permute-start | bytes 49160 | tf_op jit(solution)/shard_map/ppermute | solution.py:785
  31.1 2.7 %collective-permute-start.6 = (f32[32,128]{1,0:T(8,128)S(1)}, f32[32,128]{1,0:T(8,128)S(1)}, u32[]{:S(2)}, u32[]{:S(2)}) collective-permute-start(f32[32,128]{1,0:T(8,128)S(1)} %get-tuple-element.48.field.precond), channel_id=1, source_target_pairs={{0,2},{1,4},{2,3},{3,0},{4,1},{5,8},{6,7},{7,6},{8,5},{9,12},{10,1... | collective-permute-start | bytes 49160 | tf_op jit(solution)/shard_map/ppermute | solution.py:785
  33.8 0.5 collective-permute-start.5
  34.3 0.1 collective-permute-start.4
  34.4 4.3 %apply_inner.2 = (f32[32,128,128]{2,1,0:T(8,128)S(1)}, f32[256,128]{1,0:T(8,128)S(1)}) custom-call(s32[8]{0:T(128)S(4)} %get-tuple-element.33.meta, s32[1472]{0:T(1024)S(4)} %get-tuple-element.34.table, s32[196]{0:T(256)S(4)} %get-tuple-element.36.plan, s32[1]{0:T(128)S(4)} %get-tuple-element.49.again, f32[32,128]{1,0:T(8,128)S(1)} %get-tuple-element.48.field.precond, ...), custom_call_target="tpu_custom_call" | custom-call | flops 15204352 | tf_op jit(solution)/shard_map/apply_inner/pallas_call | solution.py:698
  38.7 0.0 collective-permute-done.7.rest_3_
  38.7 0.0 collective-permute-done.6.rest_2_
  38.7 1.9 %collective-permute-done.5.rest_1_ = f32[32,128]{1,0:T(8,128)S(1)} collective-permute-done((f32[32,128]{1,0:T(8,128)S(1)}, f32[32,128]{1,0:T(8,128)S(1)}, u32[]{:S(2)}, u32[]{:S(2)}) %collective-permute-start.5) | collective-permute-done | bytes 16416 | tf_op jit(solution)/shard_map/ppermute | solution.py:785
  40.7 0.0 collective-permute-done.4.rest_0_
  40.7 2.2 %apply_first.1 = (f32[32,128]{1,0:T(8,128)S(1)}, f32[32,128]{1,0:T(8,128)S(1)}) custom-call(s32[8]{0:T(128)S(4)} %get-tuple-element.33.meta, s32[1472]{0:T(1024)S(4)} %get-tuple-element.34.table, s32[196]{0:T(256)S(4)} %get-tuple-element.36.plan, s32[1]{0:T(128)S(4)} %get-tuple-element.49.again, f32[32,128]{1,0:T(8,128)S(1)} %get-tuple-element.50.diagonal, ...), custom_call_target="tpu_custom_call" | custom-call | flops 7798784 | tf_op jit(solution)/shard_map/apply_first/pallas_call | solution.py:698
  42.8 0.7 collective-permute-start.11
  43.6 1.7 %collective-permute-start.10 = (f32[32,128]{1,0:T(8,128)S(1)}, f32[32,128]{1,0:T(8,128)S(1)}, u32[]{:S(2)}, u32[]{:S(2)}) collective-permute-start(f32[32,128]{1,0:T(8,128)S(1)} %get-tuple-element.57.field.scaled), channel_id=1, source_target_pairs={{0,2},{1,4},{2,3},{3,0},{4,1},{5,8},{6,7},{7,6},{8,5},{9,12},{10,1... | collective-permute-start | bytes 49160 | tf_op jit(solution)/shard_map/ppermute | solution.py:785
  45.2 3.2 %collective-permute-start.9 = (f32[32,128]{1,0:T(8,128)S(1)}, f32[32,128]{1,0:T(8,128)S(1)}, u32[]{:S(2)}, u32[]{:S(2)}) collective-permute-start(f32[32,128]{1,0:T(8,128)S(1)} %get-tuple-element.57.field.scaled), channel_id=1, source_target_pairs={{0,31},{1,2},{2,1},{3,4},{4,3},{5,6},{6,5},{7,8},{8,7},{9,10},{10,... | collective-permute-start | bytes 49160 | tf_op jit(solution)/shard_map/ppermute | solution.py:785
  48.4 0.0 collective-permute-start.8
  48.4 4.3 %apply_inner.3 = (f32[32,128,128]{2,1,0:T(8,128)S(1)}, f32[256,128]{1,0:T(8,128)S(1)}) custom-call(s32[8]{0:T(128)S(4)} %get-tuple-element.33.meta, s32[1472]{0:T(1024)S(4)} %get-tuple-element.34.table, s32[196]{0:T(256)S(4)} %get-tuple-element.36.plan, s32[1]{0:T(128)S(4)} %get-tuple-element.49.again, f32[32,128]{1,0:T(8,128)S(1)} %get-tuple-element.57.field.scaled, ...), custom_call_target="tpu_custom_call" | custom-call | flops 15204352 | tf_op jit(solution)/shard_map/apply_inner/pallas_call | solution.py:698
  52.7 0.0 collective-permute-done.11.rest_3_
  52.7 0.0 collective-permute-done.10.rest_2_
  52.8 0.0 collective-permute-done.9.rest_1_
  52.8 0.0 collective-permute-done.8.rest_0_
  52.8 2.3 %apply_second.1 = (f32[32,128]{1,0:T(8,128)S(1)}, f32[8,128]{1,0:T(8,128)S(1)}) custom-call(s32[8]{0:T(128)S(4)} %get-tuple-element.33.meta, s32[1472]{0:T(1024)S(4)} %get-tuple-element.34.table, s32[196]{0:T(256)S(4)} %get-tuple-element.36.plan, s32[1]{0:T(128)S(4)} %get-tuple-element.49.again, f32[32,128]{1,0:T(8,128)S(1)} %get-tuple-element.32.source, ...), custom_call_target="tpu_custom_call" | custom-call | flops 7798784 | tf_op jit(solution)/shard_map/apply_second/pallas_call | solution.py:698
  55.1 0.0 collective-permute-start.12
  55.1 1.2 %collective-permute-done.12 = f32[8,128]{1,0:T(8,128)S(1)} collective-permute-done((f32[8,128]{1,0:T(8,128)S(1)}, f32[8,128]{1,0:T(8,128)S(1)}, u32[]{:S(2)}, u32[]{:S(2)}) %collective-permute-start.12) | collective-permute-done | bytes 4128 | tf_op jit(solution)/shard_map/ppermute | solution.py:711
  56.2 2.0 %collective-permute-start.15 = (f32[8,128]{1,0:T(8,128)S(1)}, f32[8,128]{1,0:T(8,128)S(1)}, u32[]{:S(2)}, u32[]{:S(2)}) collective-permute-start(f32[8,128]{1,0:T(8,128)S(1)} %add.12), channel_id=1, source_target_pairs={{0,3},{1,2},{2,1},{3,0},{4,7},{5,6},{6,5},{7,4},{8,11},{9,10},{10,... | collective-permute-start | bytes 12296 | tf_op jit(solution)/shard_map/ppermute | solution.py:711
  58.3 2.1 %collective-permute-start.14 = (f32[8,128]{1,0:T(8,128)S(1)}, f32[8,128]{1,0:T(8,128)S(1)}, u32[]{:S(2)}, u32[]{:S(2)}) collective-permute-start(f32[8,128]{1,0:T(8,128)S(1)} %add.12), channel_id=1, source_target_pairs={{0,2},{1,3},{2,0},{3,1},{4,6},{5,7},{6,4},{7,5},{8,10},{9,11},{10,... | collective-permute-start | bytes 12296 | tf_op jit(solution)/shard_map/ppermute | solution.py:711
  60.4 0.2 collective-permute-start.13
  60.6 1.0 %collective-permute-done.15 = f32[8,128]{1,0:T(8,128)S(1)} collective-permute-done((f32[8,128]{1,0:T(8,128)S(1)}, f32[8,128]{1,0:T(8,128)S(1)}, u32[]{:S(2)}, u32[]{:S(2)}) %collective-permute-start.15) | collective-permute-done | bytes 4128 | tf_op jit(solution)/shard_map/ppermute | solution.py:711
  61.6 1.1 %collective-permute-done.14 = f32[8,128]{1,0:T(8,128)S(1)} collective-permute-done((f32[8,128]{1,0:T(8,128)S(1)}, f32[8,128]{1,0:T(8,128)S(1)}, u32[]{:S(2)}, u32[]{:S(2)}) %collective-permute-start.14) | collective-permute-done | bytes 4128 | tf_op jit(solution)/shard_map/ppermute | solution.py:711
  62.8 1.2 %collective-permute-done.13 = f32[8,128]{1,0:T(8,128)S(1)} collective-permute-done((f32[8,128]{1,0:T(8,128)S(1)}, f32[8,128]{1,0:T(8,128)S(1)}, u32[]{:S(2)}, u32[]{:S(2)}) %collective-permute-start.13) | collective-permute-done | bytes 4128 | tf_op jit(solution)/shard_map/ppermute | solution.py:711
  64.0 3.0 %collective-permute-start.18 = (f32[8,128]{1,0:T(8,128)S(1)}, f32[8,128]{1,0:T(8,128)S(1)}, u32[]{:S(2)}, u32[]{:S(2)}) collective-permute-start(f32[8,128]{1,0:T(8,128)S(1)} %add_add_fusion.rest_0_), channel_id=1, source_target_pairs={{0,24},{4,28},{8,16},{12,20},{16,8},{20,12},{24,0},{28,4},{1,25},{... | collective-permute-start | bytes 12296 | tf_op jit(solution)/shard_map/ppermute | solution.py:711
  67.0 0.8 %collective-permute-start.17 = (f32[8,128]{1,0:T(8,128)S(1)}, f32[8,128]{1,0:T(8,128)S(1)}, u32[]{:S(2)}, u32[]{:S(2)}) collective-permute-start(f32[8,128]{1,0:T(8,128)S(1)} %add_add_fusion.rest_0_), channel_id=1, source_target_pairs={{0,16},{4,20},{8,24},{12,28},{16,0},{20,4},{24,8},{28,12},{1,17},{... | collective-permute-start | bytes 12296 | tf_op jit(solution)/shard_map/ppermute | solution.py:711
  67.9 1.4 %collective-permute-start.16 = (f32[8,128]{1,0:T(8,128)S(1)}, f32[8,128]{1,0:T(8,128)S(1)}, u32[]{:S(2)}, u32[]{:S(2)}) collective-permute-start(f32[8,128]{1,0:T(8,128)S(1)} %add_add_fusion.rest_0_), channel_id=1, source_target_pairs={{0,8},{4,12},{8,0},{12,4},{16,24},{20,28},{24,16},{28,20},{1,9},{5... | collective-permute-start | bytes 12296 | tf_op jit(solution)/shard_map/ppermute | solution.py:711
  69.3 0.0 collective-permute-done.18.rest_3_
  69.3 1.4 %collective-permute-done.17.rest_2_ = f32[8,128]{1,0:T(8,128)S(1)} collective-permute-done((f32[8,128]{1,0:T(8,128)S(1)}, f32[8,128]{1,0:T(8,128)S(1)}, u32[]{:S(2)}, u32[]{:S(2)}) %collective-permute-start.17) | collective-permute-done | bytes 4128 | tf_op jit(solution)/shard_map/ppermute | solution.py:711
  70.6 0.8 %collective-permute-done.16.rest_1_ = f32[8,128]{1,0:T(8,128)S(1)} collective-permute-done((f32[8,128]{1,0:T(8,128)S(1)}, f32[8,128]{1,0:T(8,128)S(1)}, u32[]{:S(2)}, u32[]{:S(2)}) %collective-permute-start.16) | collective-permute-done | bytes 4128 | tf_op jit(solution)/shard_map/ppermute | solution.py:711
  71.5 0.9 %finish.1 = (f32[32,128]{1,0:T(8,128)}, f32[32,128]{1,0:T(8,128)}) custom-call(f32[32,128]{1,0:T(8,128)S(1)} %get-tuple-element.32.source, f32[32,128]{1,0:T(8,128)S(1)} %get-tuple-element.48.field.precond, f32[32,128]{1,0:T(8,128)S(1)} %get-tuple-element.56.spill, f32[32,128]{1,0:T(8,128)S(1)} %get-tuple-element.57.field.scaled, ...), custom_call_target="tpu_custom_call" | custom-call | tf_op jit(solution)/shard_map/finish/pallas_call | solution.py:698
  (2 shorter events, 0.0 us)
Async XLA Ops:
  0.6 5.0 %collective-permute-start.2 = (s32[7,128]{1,0:T(8,128)}, s32[7,128]{1,0:T(8,128)S(1)}, u32[]{:S(2)}, u32[]{:S(2)}) collective-permute-start(s32[7,128]{1,0:T(8,128)} %bitcast.1), channel_id=1, source_target_pairs={{0,1},{1,0},{2,3},{3,2},{4,5},{5,4},{6,7},{7,6},{8,9},{9,8},{10,11... | collective-permute-start | bytes 10760 | tf_op jit(solution)/shard_map/ppermute | solution.py:711
  5.4 17.5 %collective-permute-start = (f32[4,32,128]{2,1,0:T(8,128)S(1)}, f32[4,32,128]{2,1,0:T(8,128)S(1)}, u32[]{:S(2)}, u32[]{:S(2)}) collective-permute-start(f32[4,32,128]{2,1,0:T(8,128)S(1)} %get-tuple-element.39), channel_id=1, source_target_pairs={{0,4},{4,0},{8,12},{12,8},{16,20},{20,16},{24,28},{28,24},{1,5},{5... | collective-permute-start | bytes 196616 | tf_op jit(solution)/shard_map/ppermute | solution.py:733
  5.5 17.5 %collective-permute-start.1 = (f32[4,32,128]{2,1,0:T(8,128)S(1)}, f32[4,32,128]{2,1,0:T(8,128)S(1)}, u32[]{:S(2)}, u32[]{:S(2)}) collective-permute-start(f32[4,32,128]{2,1,0:T(8,128)S(1)} %get-tuple-element.40), channel_id=1, source_target_pairs={{0,1},{1,0},{2,3},{3,2},{4,8},{5,9},{6,10},{7,11},{8,4},{9,5},{10,... | collective-permute-start | bytes 196616 | tf_op jit(solution)/shard_map/ppermute | solution.py:738
  6.3 16.7 %collective-permute-start.3 = (s32[14,128]{1,0:T(8,128)S(1)}, s32[14,128]{1,0:T(8,128)S(1)}, u32[]{:S(2)}, u32[]{:S(2)}) collective-permute-start(s32[14,128]{1,0:T(8,128)S(1)} %pad_add_fusion.rest_0_), channel_id=1, source_target_pairs={{0,3},{1,2},{2,1},{3,0},{4,7},{5,6},{6,5},{7,4},{8,11},{9,10},{10,... | collective-permute-start | bytes 21512 | tf_op jit(solution)/shard_map/ppermute | solution.py:711
  27.5 11.2 %collective-permute-start.7 = (f32[32,128]{1,0:T(8,128)S(1)}, f32[32,128]{1,0:T(8,128)S(1)}, u32[]{:S(2)}, u32[]{:S(2)}) collective-permute-start(f32[32,128]{1,0:T(8,128)S(1)} %get-tuple-element.48.field.precond), channel_id=1, source_target_pairs={{0,1},{1,3},{2,4},{3,0},{4,2},{5,7},{6,8},{7,5},{8,6},{9,11},{10,1... | collective-permute-start | bytes 49160 | tf_op jit(solution)/shard_map/ppermute | solution.py:785
  31.1 7.6 %collective-permute-start.6 = (f32[32,128]{1,0:T(8,128)S(1)}, f32[32,128]{1,0:T(8,128)S(1)}, u32[]{:S(2)}, u32[]{:S(2)}) collective-permute-start(f32[32,128]{1,0:T(8,128)S(1)} %get-tuple-element.48.field.precond), channel_id=1, source_target_pairs={{0,2},{1,4},{2,3},{3,0},{4,1},{5,8},{6,7},{7,6},{8,5},{9,12},{10,1... | collective-permute-start | bytes 49160 | tf_op jit(solution)/shard_map/ppermute | solution.py:785
  33.8 6.8 %collective-permute-start.5 = (f32[32,128]{1,0:T(8,128)S(1)}, f32[32,128]{1,0:T(8,128)S(1)}, u32[]{:S(2)}, u32[]{:S(2)}) collective-permute-start(f32[32,128]{1,0:T(8,128)S(1)} %get-tuple-element.48.field.precond), channel_id=1, source_target_pairs={{0,31},{1,2},{2,1},{3,4},{4,3},{5,6},{6,5},{7,8},{8,7},{9,10},{10,... | collective-permute-start | bytes 49160 | tf_op jit(solution)/shard_map/ppermute | solution.py:785
  34.3 6.4 %collective-permute-start.4 = (f32[32,128]{1,0:T(8,128)S(1)}, f32[32,128]{1,0:T(8,128)S(1)}, u32[]{:S(2)}, u32[]{:S(2)}) collective-permute-start(f32[32,128]{1,0:T(8,128)S(1)} %get-tuple-element.48.field.precond), channel_id=1, source_target_pairs={{0,1},{1,0},{2,3},{3,2},{4,5},{5,4},{6,7},{7,6},{8,9},{9,8},{10,11... | collective-permute-start | bytes 49160 | tf_op jit(solution)/shard_map/ppermute | solution.py:785
  42.8 9.9 %collective-permute-start.11 = (f32[32,128]{1,0:T(8,128)S(1)}, f32[32,128]{1,0:T(8,128)S(1)}, u32[]{:S(2)}, u32[]{:S(2)}) collective-permute-start(f32[32,128]{1,0:T(8,128)S(1)} %get-tuple-element.57.field.scaled), channel_id=1, source_target_pairs={{0,1},{1,3},{2,4},{3,0},{4,2},{5,7},{6,8},{7,5},{8,6},{9,11},{10,1... | collective-permute-start | bytes 49160 | tf_op jit(solution)/shard_map/ppermute | solution.py:785
  43.6 9.2 %collective-permute-start.10 = (f32[32,128]{1,0:T(8,128)S(1)}, f32[32,128]{1,0:T(8,128)S(1)}, u32[]{:S(2)}, u32[]{:S(2)}) collective-permute-start(f32[32,128]{1,0:T(8,128)S(1)} %get-tuple-element.57.field.scaled), channel_id=1, source_target_pairs={{0,2},{1,4},{2,3},{3,0},{4,1},{5,8},{6,7},{7,6},{8,5},{9,12},{10,1... | collective-permute-start | bytes 49160 | tf_op jit(solution)/shard_map/ppermute | solution.py:785
  45.2 7.5 %collective-permute-start.9 = (f32[32,128]{1,0:T(8,128)S(1)}, f32[32,128]{1,0:T(8,128)S(1)}, u32[]{:S(2)}, u32[]{:S(2)}) collective-permute-start(f32[32,128]{1,0:T(8,128)S(1)} %get-tuple-element.57.field.scaled), channel_id=1, source_target_pairs={{0,31},{1,2},{2,1},{3,4},{4,3},{5,6},{6,5},{7,8},{8,7},{9,10},{10,... | collective-permute-start | bytes 49160 | tf_op jit(solution)/shard_map/ppermute | solution.py:785
  48.4 4.3 %collective-permute-start.8 = (f32[32,128]{1,0:T(8,128)S(1)}, f32[32,128]{1,0:T(8,128)S(1)}, u32[]{:S(2)}, u32[]{:S(2)}) collective-permute-start(f32[32,128]{1,0:T(8,128)S(1)} %get-tuple-element.57.field.scaled), channel_id=1, source_target_pairs={{0,1},{1,0},{2,3},{3,2},{4,5},{5,4},{6,7},{7,6},{8,9},{9,8},{10,11... | collective-permute-start | bytes 49160 | tf_op jit(solution)/shard_map/ppermute | solution.py:785
  55.1 1.2 %collective-permute-start.12 = (f32[8,128]{1,0:T(8,128)S(1)}, f32[8,128]{1,0:T(8,128)S(1)}, u32[]{:S(2)}, u32[]{:S(2)}) collective-permute-start(f32[8,128]{1,0:T(8,128)S(1)} %get-tuple-element.61), channel_id=1, source_target_pairs={{0,4},{4,0},{8,12},{12,8},{16,20},{20,16},{24,28},{28,24},{1,5},{5... | collective-permute-start | bytes 12296 | tf_op jit(solution)/shard_map/ppermute | solution.py:711
  56.2 5.4 %collective-permute-start.15 = (f32[8,128]{1,0:T(8,128)S(1)}, f32[8,128]{1,0:T(8,128)S(1)}, u32[]{:S(2)}, u32[]{:S(2)}) collective-permute-start(f32[8,128]{1,0:T(8,128)S(1)} %add.12), channel_id=1, source_target_pairs={{0,3},{1,2},{2,1},{3,0},{4,7},{5,6},{6,5},{7,4},{8,11},{9,10},{10,... | collective-permute-start | bytes 12296 | tf_op jit(solution)/shard_map/ppermute | solution.py:711
  58.3 4.5 %collective-permute-start.14 = (f32[8,128]{1,0:T(8,128)S(1)}, f32[8,128]{1,0:T(8,128)S(1)}, u32[]{:S(2)}, u32[]{:S(2)}) collective-permute-start(f32[8,128]{1,0:T(8,128)S(1)} %add.12), channel_id=1, source_target_pairs={{0,2},{1,3},{2,0},{3,1},{4,6},{5,7},{6,4},{7,5},{8,10},{9,11},{10,... | collective-permute-start | bytes 12296 | tf_op jit(solution)/shard_map/ppermute | solution.py:711
  60.4 3.6 %collective-permute-start.13 = (f32[8,128]{1,0:T(8,128)S(1)}, f32[8,128]{1,0:T(8,128)S(1)}, u32[]{:S(2)}, u32[]{:S(2)}) collective-permute-start(f32[8,128]{1,0:T(8,128)S(1)} %add.12), channel_id=1, source_target_pairs={{0,1},{1,0},{2,3},{3,2},{4,5},{5,4},{6,7},{7,6},{8,9},{9,8},{10,11... | collective-permute-start | bytes 12296 | tf_op jit(solution)/shard_map/ppermute | solution.py:711
  64.0 5.3 %collective-permute-start.18 = (f32[8,128]{1,0:T(8,128)S(1)}, f32[8,128]{1,0:T(8,128)S(1)}, u32[]{:S(2)}, u32[]{:S(2)}) collective-permute-start(f32[8,128]{1,0:T(8,128)S(1)} %add_add_fusion.rest_0_), channel_id=1, source_target_pairs={{0,24},{4,28},{8,16},{12,20},{16,8},{20,12},{24,0},{28,4},{1,25},{... | collective-permute-start | bytes 12296 | tf_op jit(solution)/shard_map/ppermute | solution.py:711
  67.0 3.6 %collective-permute-start.17 = (f32[8,128]{1,0:T(8,128)S(1)}, f32[8,128]{1,0:T(8,128)S(1)}, u32[]{:S(2)}, u32[]{:S(2)}) collective-permute-start(f32[8,128]{1,0:T(8,128)S(1)} %add_add_fusion.rest_0_), channel_id=1, source_target_pairs={{0,16},{4,20},{8,24},{12,28},{16,0},{20,4},{24,8},{28,12},{1,17},{... | collective-permute-start | bytes 12296 | tf_op jit(solution)/shard_map/ppermute | solution.py:711
  67.9 3.6 %collective-permute-start.16 = (f32[8,128]{1,0:T(8,128)S(1)}, f32[8,128]{1,0:T(8,128)S(1)}, u32[]{:S(2)}, u32[]{:S(2)}) collective-permute-start(f32[8,128]{1,0:T(8,128)S(1)} %add_add_fusion.rest_0_), channel_id=1, source_target_pairs={{0,8},{4,12},{8,0},{12,4},{16,24},{20,28},{24,16},{28,20},{1,9},{5... | collective-permute-start | bytes 12296 | tf_op jit(solution)/shard_map/ppermute | solution.py:711

commit v15 on v12

--- a/solution.py
+++ b/solution.py
@@ -745,7 +745,8 @@
                 rest = [i for i in range(p * columns, (p + 1) * columns) if i not in to]
                 to.update(zip(rest, rest[1:] + rest[:1]))
             swaps.append([to[i] for i in range(count)])
-        return [lax.ppermute(field, axes, list(enumerate(to))) for to in swaps]
+        received = [lax.ppermute(field, axes, list(enumerate(to))) for to in swaps[::-1]]
+        return received[::-1]
 
     scratch = [pltpu.VMEM((share, width, width), f32), pltpu.VMEM((8 * share, width), f32)]
 
@@ -772,7 +773,7 @@
     )
 
     def together(values, axis, low, size):
-        return tree([values] + [swap(values, axis, low * k) for k in range(1, size)])
+        return tree([values] + [swap(values, axis, low * k) for k in range(size - 1, 0, -1)][::-1])
 
     sums = together(sums, "piece", 1, 2)
     sums = together(sums, "col", 1, columns)
@@ -780,7 +781,7 @@
     while pieces // step > 4:
         sums = together(sums, "piece", step, 4)
         step *= 4
-    others = [swap(sums, "piece", step * k) for k in range(1, pieces // step)]
+    others = [swap(sums, "piece", step * k) for k in range(pieces // step - 1, 0, -1)][::-1]
 
     return tuple(call(
         finish,

time: 70.1 us -> 70.1 us (level)
  waiting for transfers between devices: 7.99 us -> 8.86 us
where the time goes in v15:
time: 70.1 us; the launch traced here: 70 us
  Pallas kernels  31 us (44%)
  starting transfers between devices  28.7 us (41%)
  waiting for transfers between devices  8.86 us (13%)
  between operations  0.77 us (1%)
  other arithmetic  0.71 us (1%)
    pallas_call x8, Pallas kernels, call(): pl.pallas_call(kernel, out_shape=outs, in_specs=[SMEM] * scalars + [HBM]...  31 us
    ppermute x9, starting transfers between devices, swap(): lax.ppermute(values, axis, [(i, i ^ step) for i in range(lax.axis_size(ax...  16.5 us
    ppermute x8, starting transfers between devices, exchange(): lax.ppermute(field, axes, list(enumerate(to)))  12 us
    ppermute x9, waiting for transfers between devices, swap(): lax.ppermute(values, axis, [(i, i ^ step) for i in range(lax.axis_size(ax...  6.98 us
    ppermute x8, waiting for transfers between devices, exchange(): lax.ppermute(field, axes, list(enumerate(to)))  1.88 us
  transfers between devices with their start and end apart: 19, of which 7 were waited for; matrix products, arithmetic and copies ran while one was open for 1% of the time, Pallas kernels for 30%

profile of v15, /device:TPU:0, one launch (start us, length us, event | category | flops | bytes accessed | tf_op | source)
XLA Modules:
  0.0 70.0 jit_solution(11777660422901618732)
XLA Ops:
  0.6 3.1 %collective-permute-start.2 = (s32[7,128]{1,0:T(8,128)}, s32[7,128]{1,0:T(8,128)S(1)}, u32[]{:S(2)}, u32[]{:S(2)}) collective-permute-start(s32[7,128]{1,0:T(8,128)} %bitcast.1), channel_id=1, source_target_pairs={{0,1},{1,0},{2,3},{3,2},{4,5},{5,4},{6,7},{7,6},{8,9},{9,8},{10,11... | collective-permute-start | bytes 10760 | tf_op jit(solution)/shard_map/ppermute | solution.py:674
  3.7 1.7 %prepare.1 = (s32[8]{0:T(128)S(4)}, s32[1480]{0:T(1024)S(4)}, f32[4,192,128]{2,1,0:T(8,128)S(1)}, f32[4,64,128]{2,1,0:T(8,128)S(1)}, f32[32,128]{1,0:T(8,128)S(1...) custom-call(s32[8]{0:T(128)} %counts.1, f32[3]{0:T(128)} %densities.1, ...), custom_call_target="tpu_custom_call" | custom-call | tf_op jit(solution)/shard_map/prepare/pallas_call | solution.py:661
  5.4 0.1 collective-permute-start
  5.5 0.1 collective-permute-start.1
  5.6 0.0 collective-permute-done.2
  5.6 0.7 pad_add_fusion.rest_0_
  6.3 4.0 %collective-permute-start.3 = (s32[14,128]{1,0:T(8,128)S(1)}, s32[14,128]{1,0:T(8,128)S(1)}, u32[]{:S(2)}, u32[]{:S(2)}) collective-permute-start(s32[14,128]{1,0:T(8,128)S(1)} %pad_add_fusion.rest_0_), channel_id=1, source_target_pairs={{0,3},{1,2},{2,1},{3,0},{4,7},{5,6},{6,5},{7,4},{8,11},{9,10},{10,... | collective-permute-start | bytes 21512 | tf_op jit(solution)/shard_map/ppermute | solution.py:674
  10.3 10.8 %build_inner.1 = (s32[196]{0:T(256)S(4)}, s32[195]{0:T(256)S(4)}, f32[224,128,128]{2,1,0:T(8,128)S(1)}, bf16[2,32,128,128]{3,2,1,0:T(8,128)(2,1)S(1)}, f32[3,32,...) custom-call(s32[8]{0:T(128)S(4)} %get-tuple-element.34.meta, ...), custom_call_target="tpu_custom_call" | custom-call | flops 56623104 | tf_op jit(solution)/shard_map/build_inner/pallas_call | solution.py:661
  21.1 0.0 collective-permute-done.3.rest_1_
  21.1 0.0 collective-permute-done.first
  21.1 0.0 collective-permute-done.1.second
  21.1 4.6 %build_outer.1 = (s32[1]{0:T(128)S(4)}, f32[230,128,128]{2,1,0:T(8,128)S(1)}, f32[32,128]{1,0:T(8,128)S(1)}, f32[32,128]{1,0:T(8,128)S(1)}, f32[32,128]{1,0:T(8,128)S(1)}, /*index=5*/f32[32,128]{1,0:T(8,128)S(1)}) custom-call(s32[8]{0:T(128)S(4)} %get-tuple-element.34.meta, s32[1480]{0:T(1024)S(4)} %get-tuple-element.35.table, ...), custom_call_target="tpu_custom_call" | custom-call | flops 58195968 | tf_op jit(solution)/shard_map/build_outer/pallas_call | solution.py:661
  25.7 2.7 %collective-permute-start.7 = (f32[32,128]{1,0:T(8,128)S(1)}, f32[32,128]{1,0:T(8,128)S(1)}, u32[]{:S(2)}, u32[]{:S(2)}) collective-permute-start(f32[32,128]{1,0:T(8,128)S(1)} %get-tuple-element.50.field.precond), channel_id=1, source_target_pairs={{0,1},{1,3},{2,4},{3,0},{4,2},{5,7},{6,8},{7,5},{8,6},{9,11},{10,1... | collective-permute-start | bytes 49160 | tf_op jit(solution)/shard_map/ppermute | solution.py:748
  28.5 3.2 %collective-permute-start.6 = (f32[32,128]{1,0:T(8,128)S(1)}, f32[32,128]{1,0:T(8,128)S(1)}, u32[]{:S(2)}, u32[]{:S(2)}) collective-permute-start(f32[32,128]{1,0:T(8,128)S(1)} %get-tuple-element.50.field.precond), channel_id=1, source_target_pairs={{0,2},{1,4},{2,3},{3,0},{4,1},{5,8},{6,7},{7,6},{8,5},{9,12},{10,1... | collective-permute-start | bytes 49160 | tf_op jit(solution)/shard_map/ppermute | solution.py:748
  31.7 0.5 collective-permute-start.5
  32.2 0.0 collective-permute-start.4
  32.3 4.3 %apply_inner.2 = (f32[32,128,128]{2,1,0:T(8,128)S(1)}, f32[256,128]{1,0:T(8,128)S(1)}) custom-call(s32[8]{0:T(128)S(4)} %get-tuple-element.34.meta, s32[1480]{0:T(1024)S(4)} %get-tuple-element.35.table, s32[196]{0:T(256)S(4)} %get-tuple-element.37.plan, s32[1]{0:T(128)S(4)} %get-tuple-element.51.again, f32[32,128]{1,0:T(8,128)S(1)} %get-tuple-element.50.field.precond, ...), custom_call_target="tpu_custom_call" | custom-call | flops 14155776 | tf_op jit(solution)/shard_map/apply_inner/pallas_call | solution.py:661
  36.6 0.0 collective-permute-done.7.rest_3_
  36.6 0.0 collective-permute-done.6.rest_2_
  36.6 1.9 %collective-permute-done.5.rest_1_ = f32[32,128]{1,0:T(8,128)S(1)} collective-permute-done((f32[32,128]{1,0:T(8,128)S(1)}, f32[32,128]{1,0:T(8,128)S(1)}, u32[]{:S(2)}, u32[]{:S(2)}) %collective-permute-start.5) | collective-permute-done | bytes 16416 | tf_op jit(solution)/shard_map/ppermute | solution.py:748
  38.5 0.0 collective-permute-done.4.rest_0_
  38.5 2.2 %apply_first.1 = (f32[32,128]{1,0:T(8,128)S(1)}, f32[32,128]{1,0:T(8,128)S(1)}) custom-call(s32[8]{0:T(128)S(4)} %get-tuple-element.34.meta, s32[1480]{0:T(1024)S(4)} %get-tuple-element.35.table, s32[196]{0:T(256)S(4)} %get-tuple-element.37.plan, s32[1]{0:T(128)S(4)} %get-tuple-element.51.again, f32[32,128]{1,0:T(8,128)S(1)} %get-tuple-element.52.diagonal, ...), custom_call_target="tpu_custom_call" | custom-call | flops 7274496 | tf_op jit(solution)/shard_map/apply_first/pallas_call | solution.py:661
  40.6 0.9 %collective-permute-start.11 = (f32[32,128]{1,0:T(8,128)S(1)}, f32[32,128]{1,0:T(8,128)S(1)}, u32[]{:S(2)}, u32[]{:S(2)}) collective-permute-start(f32[32,128]{1,0:T(8,128)S(1)} %get-tuple-element.59.field.scaled), channel_id=1, source_target_pairs={{0,1},{1,3},{2,4},{3,0},{4,2},{5,7},{6,8},{7,5},{8,6},{9,11},{10,1... | collective-permute-start | bytes 49160 | tf_op jit(solution)/shard_map/ppermute | solution.py:748
  41.5 1.4 %collective-permute-start.10 = (f32[32,128]{1,0:T(8,128)S(1)}, f32[32,128]{1,0:T(8,128)S(1)}, u32[]{:S(2)}, u32[]{:S(2)}) collective-permute-start(f32[32,128]{1,0:T(8,128)S(1)} %get-tuple-element.59.field.scaled), channel_id=1, source_target_pairs={{0,2},{1,4},{2,3},{3,0},{4,1},{5,8},{6,7},{7,6},{8,5},{9,12},{10,1... | collective-permute-start | bytes 49160 | tf_op jit(solution)/shard_map/ppermute | solution.py:748
  42.9 3.2 %collective-permute-start.9 = (f32[32,128]{1,0:T(8,128)S(1)}, f32[32,128]{1,0:T(8,128)S(1)}, u32[]{:S(2)}, u32[]{:S(2)}) collective-permute-start(f32[32,128]{1,0:T(8,128)S(1)} %get-tuple-element.59.field.scaled), channel_id=1, source_target_pairs={{0,31},{1,2},{2,1},{3,4},{4,3},{5,6},{6,5},{7,8},{8,7},{9,10},{10,... | collective-permute-start | bytes 49160 | tf_op jit(solution)/shard_map/ppermute | solution.py:748
  46.1 0.0 collective-permute-start.8
  46.1 4.3 %apply_inner.3 = (f32[32,128,128]{2,1,0:T(8,128)S(1)}, f32[256,128]{1,0:T(8,128)S(1)}) custom-call(s32[8]{0:T(128)S(4)} %get-tuple-element.34.meta, s32[1480]{0:T(1024)S(4)} %get-tuple-element.35.table, s32[196]{0:T(256)S(4)} %get-tuple-element.37.plan, s32[1]{0:T(128)S(4)} %get-tuple-element.51.again, f32[32,128]{1,0:T(8,128)S(1)} %get-tuple-element.59.field.scaled, ...), custom_call_target="tpu_custom_call" | custom-call | flops 14155776 | tf_op jit(solution)/shard_map/apply_inner/pallas_call | solution.py:661
  50.4 0.0 collective-permute-done.11.rest_3_
  50.4 0.0 collective-permute-done.10.rest_2_
  50.4 0.0 collective-permute-done.9.rest_1_
  50.5 0.0 collective-permute-done.8.rest_0_
  50.5 2.3 %apply_second.1 = (f32[32,128]{1,0:T(8,128)S(1)}, f32[8,128]{1,0:T(8,128)S(1)}) custom-call(s32[8]{0:T(128)S(4)} %get-tuple-element.34.meta, s32[1480]{0:T(1024)S(4)} %get-tuple-element.35.table, s32[196]{0:T(256)S(4)} %get-tuple-element.37.plan, s32[1]{0:T(128)S(4)} %get-tuple-element.51.again, f32[32,128]{1,0:T(8,128)S(1)} %get-tuple-element.33.source, ...), custom_call_target="tpu_custom_call" | custom-call | flops 7274496 | tf_op jit(solution)/shard_map/apply_second/pallas_call | solution.py:661
  52.7 0.0 collective-permute-start.12
  52.8 1.1 %collective-permute-done.12 = f32[8,128]{1,0:T(8,128)S(1)} collective-permute-done((f32[8,128]{1,0:T(8,128)S(1)}, f32[8,128]{1,0:T(8,128)S(1)}, u32[]{:S(2)}, u32[]{:S(2)}) %collective-permute-start.12) | collective-permute-done | bytes 4128 | tf_op jit(solution)/shard_map/ppermute | solution.py:674
  53.9 2.0 %collective-permute-start.15 = (f32[8,128]{1,0:T(8,128)S(1)}, f32[8,128]{1,0:T(8,128)S(1)}, u32[]{:S(2)}, u32[]{:S(2)}) collective-permute-start(f32[8,128]{1,0:T(8,128)S(1)} %add.12), channel_id=1, source_target_pairs={{0,3},{1,2},{2,1},{3,0},{4,7},{5,6},{6,5},{7,4},{8,11},{9,10},{10,... | collective-permute-start | bytes 12296 | tf_op jit(solution)/shard_map/ppermute | solution.py:674
  55.9 2.2 %collective-permute-start.14 = (f32[8,128]{1,0:T(8,128)S(1)}, f32[8,128]{1,0:T(8,128)S(1)}, u32[]{:S(2)}, u32[]{:S(2)}) collective-permute-start(f32[8,128]{1,0:T(8,128)S(1)} %add.12), channel_id=1, source_target_pairs={{0,2},{1,3},{2,0},{3,1},{4,6},{5,7},{6,4},{7,5},{8,10},{9,11},{10,... | collective-permute-start | bytes 12296 | tf_op jit(solution)/shard_map/ppermute | solution.py:674
  58.0 0.2 collective-permute-start.13
  58.3 1.0 %collective-permute-done.15 = f32[8,128]{1,0:T(8,128)S(1)} collective-permute-done((f32[8,128]{1,0:T(8,128)S(1)}, f32[8,128]{1,0:T(8,128)S(1)}, u32[]{:S(2)}, u32[]{:S(2)}) %collective-permute-start.15) | collective-permute-done | bytes 4128 | tf_op jit(solution)/shard_map/ppermute | solution.py:674
  59.3 1.1 %collective-permute-done.14 = f32[8,128]{1,0:T(8,128)S(1)} collective-permute-done((f32[8,128]{1,0:T(8,128)S(1)}, f32[8,128]{1,0:T(8,128)S(1)}, u32[]{:S(2)}, u32[]{:S(2)}) %collective-permute-start.14) | collective-permute-done | bytes 4128 | tf_op jit(solution)/shard_map/ppermute | solution.py:674
  60.4 1.3 %collective-permute-done.13 = f32[8,128]{1,0:T(8,128)S(1)} collective-permute-done((f32[8,128]{1,0:T(8,128)S(1)}, f32[8,128]{1,0:T(8,128)S(1)}, u32[]{:S(2)}, u32[]{:S(2)}) %collective-permute-start.13) | collective-permute-done | bytes 4128 | tf_op jit(solution)/shard_map/ppermute | solution.py:674
  61.7 2.6 %collective-permute-start.18 = (f32[8,128]{1,0:T(8,128)S(1)}, f32[8,128]{1,0:T(8,128)S(1)}, u32[]{:S(2)}, u32[]{:S(2)}) collective-permute-start(f32[8,128]{1,0:T(8,128)S(1)} %add_add_fusion.rest_0_), channel_id=1, source_target_pairs={{0,24},{4,28},{8,16},{12,20},{16,8},{20,12},{24,0},{28,4},{1,25},{... | collective-permute-start | bytes 12296 | tf_op jit(solution)/shard_map/ppermute | solution.py:674
  64.3 1.2 %collective-permute-start.17 = (f32[8,128]{1,0:T(8,128)S(1)}, f32[8,128]{1,0:T(8,128)S(1)}, u32[]{:S(2)}, u32[]{:S(2)}) collective-permute-start(f32[8,128]{1,0:T(8,128)S(1)} %add_add_fusion.rest_0_), channel_id=1, source_target_pairs={{0,16},{4,20},{8,24},{12,28},{16,0},{20,4},{24,8},{28,12},{1,17},{... | collective-permute-start | bytes 12296 | tf_op jit(solution)/shard_map/ppermute | solution.py:674
  65.5 1.1 %collective-permute-start.16 = (f32[8,128]{1,0:T(8,128)S(1)}, f32[8,128]{1,0:T(8,128)S(1)}, u32[]{:S(2)}, u32[]{:S(2)}) collective-permute-start(f32[8,128]{1,0:T(8,128)S(1)} %add_add_fusion.rest_0_), channel_id=1, source_target_pairs={{0,8},{4,12},{8,0},{12,4},{16,24},{20,28},{24,16},{28,20},{1,9},{5... | collective-permute-start | bytes 12296 | tf_op jit(solution)/shard_map/ppermute | solution.py:674
  66.6 0.0 collective-permute-done.18.rest_3_
  66.6 1.3 %collective-permute-done.17.rest_2_ = f32[8,128]{1,0:T(8,128)S(1)} collective-permute-done((f32[8,128]{1,0:T(8,128)S(1)}, f32[8,128]{1,0:T(8,128)S(1)}, u32[]{:S(2)}, u32[]{:S(2)}) %collective-permute-start.17) | collective-permute-done | bytes 4128 | tf_op jit(solution)/shard_map/ppermute | solution.py:674
  67.9 1.2 %collective-permute-done.16.rest_1_ = f32[8,128]{1,0:T(8,128)S(1)} collective-permute-done((f32[8,128]{1,0:T(8,128)S(1)}, f32[8,128]{1,0:T(8,128)S(1)}, u32[]{:S(2)}, u32[]{:S(2)}) %collective-permute-start.16) | collective-permute-done | bytes 4128 | tf_op jit(solution)/shard_map/ppermute | solution.py:674
  69.1 0.9 %finish.1 = (f32[32,128]{1,0:T(8,128)}, f32[32,128]{1,0:T(8,128)}) custom-call(f32[32,128]{1,0:T(8,128)S(1)} %get-tuple-element.33.source, f32[32,128]{1,0:T(8,128)S(1)} %get-tuple-element.50.field.precond, f32[32,128]{1,0:T(8,128)S(1)} %get-tuple-element.58.spill, f32[32,128]{1,0:T(8,128)S(1)} %get-tuple-element.59.field.scaled, ...), custom_call_target="tpu_custom_call" | custom-call | tf_op jit(solution)/shard_map/finish/pallas_call | solution.py:661
  (2 shorter events, 0.0 us)
Async XLA Ops:
  0.6 5.0 %collective-permute-start.2 = (s32[7,128]{1,0:T(8,128)}, s32[7,128]{1,0:T(8,128)S(1)}, u32[]{:S(2)}, u32[]{:S(2)}) collective-permute-start(s32[7,128]{1,0:T(8,128)} %bitcast.1), channel_id=1, source_target_pairs={{0,1},{1,0},{2,3},{3,2},{4,5},{5,4},{6,7},{7,6},{8,9},{9,8},{10,11... | collective-permute-start | bytes 10760 | tf_op jit(solution)/shard_map/ppermute | solution.py:674
  5.4 15.7 %collective-permute-start = (f32[4,32,128]{2,1,0:T(8,128)S(1)}, f32[4,32,128]{2,1,0:T(8,128)S(1)}, u32[]{:S(2)}, u32[]{:S(2)}) collective-permute-start(f32[4,32,128]{2,1,0:T(8,128)S(1)} %get-tuple-element.40), channel_id=1, source_target_pairs={{0,4},{4,0},{8,12},{12,8},{16,20},{20,16},{24,28},{28,24},{1,5},{5... | collective-permute-start | bytes 196616 | tf_op jit(solution)/shard_map/ppermute | solution.py:696
  5.5 15.6 %collective-permute-start.1 = (f32[4,32,128]{2,1,0:T(8,128)S(1)}, f32[4,32,128]{2,1,0:T(8,128)S(1)}, u32[]{:S(2)}, u32[]{:S(2)}) collective-permute-start(f32[4,32,128]{2,1,0:T(8,128)S(1)} %get-tuple-element.41), channel_id=1, source_target_pairs={{0,1},{1,0},{2,3},{3,2},{4,8},{5,9},{6,10},{7,11},{8,4},{9,5},{10,... | collective-permute-start | bytes 196616 | tf_op jit(solution)/shard_map/ppermute | solution.py:701
  6.3 14.8 %collective-permute-start.3 = (s32[14,128]{1,0:T(8,128)S(1)}, s32[14,128]{1,0:T(8,128)S(1)}, u32[]{:S(2)}, u32[]{:S(2)}) collective-permute-start(s32[14,128]{1,0:T(8,128)S(1)} %pad_add_fusion.rest_0_), channel_id=1, source_target_pairs={{0,3},{1,2},{2,1},{3,0},{4,7},{5,6},{6,5},{7,4},{8,11},{9,10},{10,... | collective-permute-start | bytes 21512 | tf_op jit(solution)/shard_map/ppermute | solution.py:674
  25.7 10.9 %collective-permute-start.7 = (f32[32,128]{1,0:T(8,128)S(1)}, f32[32,128]{1,0:T(8,128)S(1)}, u32[]{:S(2)}, u32[]{:S(2)}) collective-permute-start(f32[32,128]{1,0:T(8,128)S(1)} %get-tuple-element.50.field.precond), channel_id=1, source_target_pairs={{0,1},{1,3},{2,4},{3,0},{4,2},{5,7},{6,8},{7,5},{8,6},{9,11},{10,1... | collective-permute-start | bytes 49160 | tf_op jit(solution)/shard_map/ppermute | solution.py:748
  28.5 8.1 %collective-permute-start.6 = (f32[32,128]{1,0:T(8,128)S(1)}, f32[32,128]{1,0:T(8,128)S(1)}, u32[]{:S(2)}, u32[]{:S(2)}) collective-permute-start(f32[32,128]{1,0:T(8,128)S(1)} %get-tuple-element.50.field.precond), channel_id=1, source_target_pairs={{0,2},{1,4},{2,3},{3,0},{4,1},{5,8},{6,7},{7,6},{8,5},{9,12},{10,1... | collective-permute-start | bytes 49160 | tf_op jit(solution)/shard_map/ppermute | solution.py:748
  31.7 6.8 %collective-permute-start.5 = (f32[32,128]{1,0:T(8,128)S(1)}, f32[32,128]{1,0:T(8,128)S(1)}, u32[]{:S(2)}, u32[]{:S(2)}) collective-permute-start(f32[32,128]{1,0:T(8,128)S(1)} %get-tuple-element.50.field.precond), channel_id=1, source_target_pairs={{0,31},{1,2},{2,1},{3,4},{4,3},{5,6},{6,5},{7,8},{8,7},{9,10},{10,... | collective-permute-start | bytes 49160 | tf_op jit(solution)/shard_map/ppermute | solution.py:748
  32.2 6.2 %collective-permute-start.4 = (f32[32,128]{1,0:T(8,128)S(1)}, f32[32,128]{1,0:T(8,128)S(1)}, u32[]{:S(2)}, u32[]{:S(2)}) collective-permute-start(f32[32,128]{1,0:T(8,128)S(1)} %get-tuple-element.50.field.precond), channel_id=1, source_target_pairs={{0,1},{1,0},{2,3},{3,2},{4,5},{5,4},{6,7},{7,6},{8,9},{9,8},{10,11... | collective-permute-start | bytes 49160 | tf_op jit(solution)/shard_map/ppermute | solution.py:748
  40.6 9.8 %collective-permute-start.11 = (f32[32,128]{1,0:T(8,128)S(1)}, f32[32,128]{1,0:T(8,128)S(1)}, u32[]{:S(2)}, u32[]{:S(2)}) collective-permute-start(f32[32,128]{1,0:T(8,128)S(1)} %get-tuple-element.59.field.scaled), channel_id=1, source_target_pairs={{0,1},{1,3},{2,4},{3,0},{4,2},{5,7},{6,8},{7,5},{8,6},{9,11},{10,1... | collective-permute-start | bytes 49160 | tf_op jit(solution)/shard_map/ppermute | solution.py:748
  41.5 9.0 %collective-permute-start.10 = (f32[32,128]{1,0:T(8,128)S(1)}, f32[32,128]{1,0:T(8,128)S(1)}, u32[]{:S(2)}, u32[]{:S(2)}) collective-permute-start(f32[32,128]{1,0:T(8,128)S(1)} %get-tuple-element.59.field.scaled), channel_id=1, source_target_pairs={{0,2},{1,4},{2,3},{3,0},{4,1},{5,8},{6,7},{7,6},{8,5},{9,12},{10,1... | collective-permute-start | bytes 49160 | tf_op jit(solution)/shard_map/ppermute | solution.py:748
  42.9 7.5 %collective-permute-start.9 = (f32[32,128]{1,0:T(8,128)S(1)}, f32[32,128]{1,0:T(8,128)S(1)}, u32[]{:S(2)}, u32[]{:S(2)}) collective-permute-start(f32[32,128]{1,0:T(8,128)S(1)} %get-tuple-element.59.field.scaled), channel_id=1, source_target_pairs={{0,31},{1,2},{2,1},{3,4},{4,3},{5,6},{6,5},{7,8},{8,7},{9,10},{10,... | collective-permute-start | bytes 49160 | tf_op jit(solution)/shard_map/ppermute | solution.py:748
  46.1 4.3 %collective-permute-start.8 = (f32[32,128]{1,0:T(8,128)S(1)}, f32[32,128]{1,0:T(8,128)S(1)}, u32[]{:S(2)}, u32[]{:S(2)}) collective-permute-start(f32[32,128]{1,0:T(8,128)S(1)} %get-tuple-element.59.field.scaled), channel_id=1, source_target_pairs={{0,1},{1,0},{2,3},{3,2},{4,5},{5,4},{6,7},{7,6},{8,9},{9,8},{10,11... | collective-permute-start | bytes 49160 | tf_op jit(solution)/shard_map/ppermute | solution.py:748
  52.7 1.2 %collective-permute-start.12 = (f32[8,128]{1,0:T(8,128)S(1)}, f32[8,128]{1,0:T(8,128)S(1)}, u32[]{:S(2)}, u32[]{:S(2)}) collective-permute-start(f32[8,128]{1,0:T(8,128)S(1)} %get-tuple-element.63), channel_id=1, source_target_pairs={{0,4},{4,0},{8,12},{12,8},{16,20},{20,16},{24,28},{28,24},{1,5},{5... | collective-permute-start | bytes 12296 | tf_op jit(solution)/shard_map/ppermute | solution.py:674
  53.9 5.4 %collective-permute-start.15 = (f32[8,128]{1,0:T(8,128)S(1)}, f32[8,128]{1,0:T(8,128)S(1)}, u32[]{:S(2)}, u32[]{:S(2)}) collective-permute-start(f32[8,128]{1,0:T(8,128)S(1)} %add.12), channel_id=1, source_target_pairs={{0,3},{1,2},{2,1},{3,0},{4,7},{5,6},{6,5},{7,4},{8,11},{9,10},{10,... | collective-permute-start | bytes 12296 | tf_op jit(solution)/shard_map/ppermute | solution.py:674
  55.9 4.5 %collective-permute-start.14 = (f32[8,128]{1,0:T(8,128)S(1)}, f32[8,128]{1,0:T(8,128)S(1)}, u32[]{:S(2)}, u32[]{:S(2)}) collective-permute-start(f32[8,128]{1,0:T(8,128)S(1)} %add.12), channel_id=1, source_target_pairs={{0,2},{1,3},{2,0},{3,1},{4,6},{5,7},{6,4},{7,5},{8,10},{9,11},{10,... | collective-permute-start | bytes 12296 | tf_op jit(solution)/shard_map/ppermute | solution.py:674
  58.0 3.6 %collective-permute-start.13 = (f32[8,128]{1,0:T(8,128)S(1)}, f32[8,128]{1,0:T(8,128)S(1)}, u32[]{:S(2)}, u32[]{:S(2)}) collective-permute-start(f32[8,128]{1,0:T(8,128)S(1)} %add.12), channel_id=1, source_target_pairs={{0,1},{1,0},{2,3},{3,2},{4,5},{5,4},{6,7},{7,6},{8,9},{9,8},{10,11... | collective-permute-start | bytes 12296 | tf_op jit(solution)/shard_map/ppermute | solution.py:674
  61.7 5.0 %collective-permute-start.18 = (f32[8,128]{1,0:T(8,128)S(1)}, f32[8,128]{1,0:T(8,128)S(1)}, u32[]{:S(2)}, u32[]{:S(2)}) collective-permute-start(f32[8,128]{1,0:T(8,128)S(1)} %add_add_fusion.rest_0_), channel_id=1, source_target_pairs={{0,24},{4,28},{8,16},{12,20},{16,8},{20,12},{24,0},{28,4},{1,25},{... | collective-permute-start | bytes 12296 | tf_op jit(solution)/shard_map/ppermute | solution.py:674
  64.3 3.6 %collective-permute-start.17 = (f32[8,128]{1,0:T(8,128)S(1)}, f32[8,128]{1,0:T(8,128)S(1)}, u32[]{:S(2)}, u32[]{:S(2)}) collective-permute-start(f32[8,128]{1,0:T(8,128)S(1)} %add_add_fusion.rest_0_), channel_id=1, source_target_pairs={{0,16},{4,20},{8,24},{12,28},{16,0},{20,4},{24,8},{28,12},{1,17},{... | collective-permute-start | bytes 12296 | tf_op jit(solution)/shard_map/ppermute | solution.py:674
  65.5 3.6 %collective-permute-start.16 = (f32[8,128]{1,0:T(8,128)S(1)}, f32[8,128]{1,0:T(8,128)S(1)}, u32[]{:S(2)}, u32[]{:S(2)}) collective-permute-start(f32[8,128]{1,0:T(8,128)S(1)} %add_add_fusion.rest_0_), channel_id=1, source_target_pairs={{0,8},{4,12},{8,0},{12,4},{16,24},{20,28},{24,16},{28,20},{1,9},{5... | collective-permute-start | bytes 12296 | tf_op jit(solution)/shard_map/ppermute | solution.py:674

commit v16 on v15

--- a/solution.py
+++ b/solution.py
@@ -235,15 +235,20 @@
             own = jnp.minimum(a, share - 1)
             other = wide(other_at(3, n))
             down = [None] * 2
-            for c, here in enumerate(chunks):
-                left = ahead[k, here, :]
-                rest = jnp.maximum(left, 0.0)
-                inverse = pltpu.reciprocal((1.01 - left) * (weights[own, here, :] + other), approx=True)
-                tile = rest * rest * inverse
-                tiles[at + k, here, :] = tile
-                rows_ref[row, here, :] = rows_ref[row, here, :] + tile
-                if cols_ref is not None:
-                    gather(down, c, tile)
+            for c in range(0, len(chunks), 2):
+                above, below = [], []
+                for here in chunks[c : c + 2]:
+                    left = ahead[k, here, :]
+                    rest = jnp.maximum(left, 0.0)
+                    above.append(rest * rest)
+                    below.append((1.01 - left) * (weights[own, here, :] + other))
+                inverse = pltpu.reciprocal(below[0] * below[1], approx=True)
+                pair = above[0] * (inverse * below[1]), above[1] * (inverse * below[0])
+                for b, (here, tile) in enumerate(zip(chunks[c : c + 2], pair)):
+                    tiles[at + k, here, :] = tile
+                    rows_ref[row, here, :] = rows_ref[row, here, :] + tile
+                    if cols_ref is not None:
+                        gather(down, c + b, tile)
             if cols_ref is not None:
                 there = pl.ds(pl.multiple_of(jnp.where(alone, share, n) * SUB, SUB), SUB)
                 cols_ref[there, :] = cols_ref[there, :] + tree(down)
@@ -540,7 +545,8 @@
 
 
 def apply_outer(meta, table, plan, again, received, times, tiles, rows_ref, cols_ref, work, hood):
-    first, second, *ends = received
+    *ends, second, first = received
+    ends = ends[::-1]
     columns = len(received)
     share, width = first.shape
     chunks = pieces_of(width)
@@ -745,8 +751,7 @@
                 rest = [i for i in range(p * columns, (p + 1) * columns) if i not in to]
                 to.update(zip(rest, rest[1:] + rest[:1]))
             swaps.append([to[i] for i in range(count)])
-        received = [lax.ppermute(field, axes, list(enumerate(to))) for to in swaps[::-1]]
-        return received[::-1]
+        return [lax.ppermute(field, axes, list(enumerate(to))) for to in swaps[::-1]]
 
     scratch = [pltpu.VMEM((share, width, width), f32), pltpu.VMEM((8 * share, width), f32)]
 

time: 70.1 us -> 70.1 us (level)
    ppermute x9, waiting for transfers between devices: 6.98 us -> 6.04 us  [swap(): lax.ppermute(values, axis, [(i, i ^ step) for i in range(lax.axis_size(ax...]
    ppermute x8, starting transfers between devices: 12 us -> 11.3 us  [exchange(): lax.ppermute(field, axes, list(enumerate(to)))]
  transfers between devices with their start and end apart: 19 -> 19, of which waited for: 7 -> 9; matrix products, arithmetic and copies ran while one was open for 1% -> 1% of each run, Pallas kernels for 30% -> 31%
where the time goes in v16:
time: 70.1 us; the launch traced here: 69.9 us
  Pallas kernels  31.5 us (45%)
  starting transfers between devices  28.4 us (41%)
  waiting for transfers between devices  8.55 us (12%)
  between operations  0.74 us (1%)
  other arithmetic  0.71 us (1%)
    pallas_call x8, Pallas kernels, call(): pl.pallas_call(kernel, out_shape=outs, in_specs=[SMEM] * scalars + [HBM]...  31.5 us
    ppermute x9, starting transfers between devices, swap(): lax.ppermute(values, axis, [(i, i ^ step) for i in range(lax.axis_size(ax...  17 us
    ppermute x8, starting transfers between devices, exchange(): lax.ppermute(field, axes, list(enumerate(to)))  11.3 us
    ppermute x9, waiting for transfers between devices, swap(): lax.ppermute(values, axis, [(i, i ^ step) for i in range(lax.axis_size(ax...  6.04 us
    ppermute x8, waiting for transfers between devices, exchange(): lax.ppermute(field, axes, list(enumerate(to)))  2.51 us
  transfers between devices with their start and end apart: 19, of which 9 were waited for; matrix products, arithmetic and copies ran while one was open for 1% of the time, Pallas kernels for 31%

profile of v16, /device:TPU:0, one launch (start us, length us, event | category | flops | bytes accessed | tf_op | source)
XLA Modules:
  0.0 69.9 jit_solution(4563857306444734336)
XLA Ops:
  0.6 3.1 %collective-permute-start.2 = (s32[7,128]{1,0:T(8,128)}, s32[7,128]{1,0:T(8,128)S(1)}, u32[]{:S(2)}, u32[]{:S(2)}) collective-permute-start(s32[7,128]{1,0:T(8,128)} %bitcast.1), channel_id=1, source_target_pairs={{0,1},{1,0},{2,3},{3,2},{4,5},{5,4},{6,7},{7,6},{8,9},{9,8},{10,11... | collective-permute-start | bytes 10760 | tf_op jit(solution)/shard_map/ppermute | solution.py:680
  3.7 1.7 %prepare.1 = (s32[8]{0:T(128)S(4)}, s32[1480]{0:T(1024)S(4)}, f32[4,192,128]{2,1,0:T(8,128)S(1)}, f32[4,64,128]{2,1,0:T(8,128)S(1)}, f32[32,128]{1,0:T(8,128)S(1...) custom-call(s32[8]{0:T(128)} %counts.1, f32[3]{0:T(128)} %densities.1, ...), custom_call_target="tpu_custom_call" | custom-call | tf_op jit(solution)/shard_map/prepare/pallas_call | solution.py:667
  5.4 0.1 collective-permute-start
  5.5 0.1 collective-permute-start.1
  5.6 0.0 collective-permute-done.2
  5.6 0.7 pad_add_fusion.rest_0_
  6.3 4.0 %collective-permute-start.3 = (s32[14,128]{1,0:T(8,128)S(1)}, s32[14,128]{1,0:T(8,128)S(1)}, u32[]{:S(2)}, u32[]{:S(2)}) collective-permute-start(s32[14,128]{1,0:T(8,128)S(1)} %pad_add_fusion.rest_0_), channel_id=1, source_target_pairs={{0,3},{1,2},{2,1},{3,0},{4,7},{5,6},{6,5},{7,4},{8,11},{9,10},{10,... | collective-permute-start | bytes 21512 | tf_op jit(solution)/shard_map/ppermute | solution.py:680
  10.3 11.1 %build_inner.1 = (s32[196]{0:T(256)S(4)}, s32[195]{0:T(256)S(4)}, f32[224,128,128]{2,1,0:T(8,128)S(1)}, bf16[2,32,128,128]{3,2,1,0:T(8,128)(2,1)S(1)}, f32[3,32,...) custom-call(s32[8]{0:T(128)S(4)} %get-tuple-element.34.meta, ...), custom_call_target="tpu_custom_call" | custom-call | flops 56623104 | tf_op jit(solution)/shard_map/build_inner/pallas_call | solution.py:667
  21.5 0.0 collective-permute-done.3.rest_1_
  21.5 0.0 collective-permute-done.first
  21.5 0.0 collective-permute-done.1.second
  21.5 4.7 %build_outer.1 = (s32[1]{0:T(128)S(4)}, f32[230,128,128]{2,1,0:T(8,128)S(1)}, f32[32,128]{1,0:T(8,128)S(1)}, f32[32,128]{1,0:T(8,128)S(1)}, f32[32,128]{1,0:T(8,128)S(1)}, /*index=5*/f32[32,128]{1,0:T(8,128)S(1)}) custom-call(s32[8]{0:T(128)S(4)} %get-tuple-element.34.meta, s32[1480]{0:T(1024)S(4)} %get-tuple-element.35.table, ...), custom_call_target="tpu_custom_call" | custom-call | flops 58195968 | tf_op jit(solution)/shard_map/build_outer/pallas_call | solution.py:667
  26.2 2.9 %collective-permute-start.7 = (f32[32,128]{1,0:T(8,128)S(1)}, f32[32,128]{1,0:T(8,128)S(1)}, u32[]{:S(2)}, u32[]{:S(2)}) collective-permute-start(f32[32,128]{1,0:T(8,128)S(1)} %get-tuple-element.50.field.precond), channel_id=1, source_target_pairs={{0,1},{1,0},{2,3},{3,2},{4,5},{5,4},{6,7},{7,6},{8,9},{9,8},{10,11... | collective-permute-start | bytes 49160 | tf_op jit(solution)/shard_map/ppermute | solution.py:754
  29.1 3.0 %collective-permute-start.6 = (f32[32,128]{1,0:T(8,128)S(1)}, f32[32,128]{1,0:T(8,128)S(1)}, u32[]{:S(2)}, u32[]{:S(2)}) collective-permute-start(f32[32,128]{1,0:T(8,128)S(1)} %get-tuple-element.50.field.precond), channel_id=1, source_target_pairs={{0,31},{1,2},{2,1},{3,4},{4,3},{5,6},{6,5},{7,8},{8,7},{9,10},{10,... | collective-permute-start | bytes 49160 | tf_op jit(solution)/shard_map/ppermute | solution.py:754
  32.1 0.0 collective-permute-start.5
  32.1 0.1 collective-permute-start.4
  32.2 4.3 %apply_inner.2 = (f32[32,128,128]{2,1,0:T(8,128)S(1)}, f32[256,128]{1,0:T(8,128)S(1)}) custom-call(s32[8]{0:T(128)S(4)} %get-tuple-element.34.meta, s32[1480]{0:T(1024)S(4)} %get-tuple-element.35.table, s32[196]{0:T(256)S(4)} %get-tuple-element.37.plan, s32[1]{0:T(128)S(4)} %get-tuple-element.51.again, f32[32,128]{1,0:T(8,128)S(1)} %get-tuple-element.50.field.precond, ...), custom_call_target="tpu_custom_call" | custom-call | flops 14155776 | tf_op jit(solution)/shard_map/apply_inner/pallas_call | solution.py:667
  36.5 0.0 collective-permute-done.7.rest_3_
  36.5 0.0 collective-permute-done.6.rest_2_
  36.5 1.1 %collective-permute-done.5.rest_1_ = f32[32,128]{1,0:T(8,128)S(1)} collective-permute-done((f32[32,128]{1,0:T(8,128)S(1)}, f32[32,128]{1,0:T(8,128)S(1)}, u32[]{:S(2)}, u32[]{:S(2)}) %collective-permute-start.5) | collective-permute-done | bytes 16416 | tf_op jit(solution)/shard_map/ppermute | solution.py:754
  37.6 0.2 collective-permute-done.4.rest_0_
  37.8 2.2 %apply_first.1 = (f32[32,128]{1,0:T(8,128)S(1)}, f32[32,128]{1,0:T(8,128)S(1)}) custom-call(s32[8]{0:T(128)S(4)} %get-tuple-element.34.meta, s32[1480]{0:T(1024)S(4)} %get-tuple-element.35.table, s32[196]{0:T(256)S(4)} %get-tuple-element.37.plan, s32[1]{0:T(128)S(4)} %get-tuple-element.51.again, f32[32,128]{1,0:T(8,128)S(1)} %get-tuple-element.52.diagonal, ...), custom_call_target="tpu_custom_call" | custom-call | flops 7274496 | tf_op jit(solution)/shard_map/apply_first/pallas_call | solution.py:667
  39.9 3.8 %collective-permute-start.11 = (f32[32,128]{1,0:T(8,128)S(1)}, f32[32,128]{1,0:T(8,128)S(1)}, u32[]{:S(2)}, u32[]{:S(2)}) collective-permute-start(f32[32,128]{1,0:T(8,128)S(1)} %get-tuple-element.59.field.scaled), channel_id=1, source_target_pairs={{0,1},{1,0},{2,3},{3,2},{4,5},{5,4},{6,7},{7,6},{8,9},{9,8},{10,11... | collective-permute-start | bytes 49160 | tf_op jit(solution)/shard_map/ppermute | solution.py:754
  43.7 0.3 collective-permute-start.10
  44.0 1.2 %collective-permute-start.9 = (f32[32,128]{1,0:T(8,128)S(1)}, f32[32,128]{1,0:T(8,128)S(1)}, u32[]{:S(2)}, u32[]{:S(2)}) collective-permute-start(f32[32,128]{1,0:T(8,128)S(1)} %get-tuple-element.59.field.scaled), channel_id=1, source_target_pairs={{0,2},{1,4},{2,3},{3,0},{4,1},{5,8},{6,7},{7,6},{8,5},{9,12},{10,1... | collective-permute-start | bytes 49160 | tf_op jit(solution)/shard_map/ppermute | solution.py:754
  45.3 0.0 collective-permute-start.8
  45.3 4.3 %apply_inner.3 = (f32[32,128,128]{2,1,0:T(8,128)S(1)}, f32[256,128]{1,0:T(8,128)S(1)}) custom-call(s32[8]{0:T(128)S(4)} %get-tuple-element.34.meta, s32[1480]{0:T(1024)S(4)} %get-tuple-element.35.table, s32[196]{0:T(256)S(4)} %get-tuple-element.37.plan, s32[1]{0:T(128)S(4)} %get-tuple-element.51.again, f32[32,128]{1,0:T(8,128)S(1)} %get-tuple-element.59.field.scaled, ...), custom_call_target="tpu_custom_call" | custom-call | flops 14155776 | tf_op jit(solution)/shard_map/apply_inner/pallas_call | solution.py:667
  49.6 0.0 collective-permute-done.11.rest_3_
  49.6 1.0 %collective-permute-done.10.rest_2_ = f32[32,128]{1,0:T(8,128)S(1)} collective-permute-done((f32[32,128]{1,0:T(8,128)S(1)}, f32[32,128]{1,0:T(8,128)S(1)}, u32[]{:S(2)}, u32[]{:S(2)}) %collective-permute-start.10) | collective-permute-done | bytes 16416 | tf_op jit(solution)/shard_map/ppermute | solution.py:754
  50.6 0.0 collective-permute-done.9.rest_1_
  50.6 0.2 collective-permute-done.8.rest_0_
  50.8 2.2 %apply_second.1 = (f32[32,128]{1,0:T(8,128)S(1)}, f32[8,128]{1,0:T(8,128)S(1)}) custom-call(s32[8]{0:T(128)S(4)} %get-tuple-element.34.meta, s32[1480]{0:T(1024)S(4)} %get-tuple-element.35.table, s32[196]{0:T(256)S(4)} %get-tuple-element.37.plan, s32[1]{0:T(128)S(4)} %get-tuple-element.51.again, f32[32,128]{1,0:T(8,128)S(1)} %get-tuple-element.33.source, ...), custom_call_target="tpu_custom_call" | custom-call | flops 7274496 | tf_op jit(solution)/shard_map/apply_second/pallas_call | solution.py:667
  53.0 0.7 %collective-permute-start.12 = (f32[8,128]{1,0:T(8,128)S(1)}, f32[8,128]{1,0:T(8,128)S(1)}, u32[]{:S(2)}, u32[]{:S(2)}) collective-permute-start(f32[8,128]{1,0:T(8,128)S(1)} %get-tuple-element.63), channel_id=1, source_target_pairs={{0,4},{4,0},{8,12},{12,8},{16,20},{20,16},{24,28},{28,24},{1,5},{5... | collective-permute-start | bytes 12296 | tf_op jit(solution)/shard_map/ppermute | solution.py:680
  53.7 0.8 %collective-permute-done.12 = f32[8,128]{1,0:T(8,128)S(1)} collective-permute-done((f32[8,128]{1,0:T(8,128)S(1)}, f32[8,128]{1,0:T(8,128)S(1)}, u32[]{:S(2)}, u32[]{:S(2)}) %collective-permute-start.12) | collective-permute-done | bytes 4128 | tf_op jit(solution)/shard_map/ppermute | solution.py:680
  54.6 0.8 %collective-permute-start.15 = (f32[8,128]{1,0:T(8,128)S(1)}, f32[8,128]{1,0:T(8,128)S(1)}, u32[]{:S(2)}, u32[]{:S(2)}) collective-permute-start(f32[8,128]{1,0:T(8,128)S(1)} %add.12), channel_id=1, source_target_pairs={{0,3},{1,2},{2,1},{3,0},{4,7},{5,6},{6,5},{7,4},{8,11},{9,10},{10,... | collective-permute-start | bytes 12296 | tf_op jit(solution)/shard_map/ppermute | solution.py:680
  55.4 3.0 %collective-permute-start.14 = (f32[8,128]{1,0:T(8,128)S(1)}, f32[8,128]{1,0:T(8,128)S(1)}, u32[]{:S(2)}, u32[]{:S(2)}) collective-permute-start(f32[8,128]{1,0:T(8,128)S(1)} %add.12), channel_id=1, source_target_pairs={{0,2},{1,3},{2,0},{3,1},{4,6},{5,7},{6,4},{7,5},{8,10},{9,11},{10,... | collective-permute-start | bytes 12296 | tf_op jit(solution)/shard_map/ppermute | solution.py:680
  58.3 0.6 collective-permute-start.13
  58.9 1.1 %collective-permute-done.15 = f32[8,128]{1,0:T(8,128)S(1)} collective-permute-done((f32[8,128]{1,0:T(8,128)S(1)}, f32[8,128]{1,0:T(8,128)S(1)}, u32[]{:S(2)}, u32[]{:S(2)}) %collective-permute-start.15) | collective-permute-done | bytes 4128 | tf_op jit(solution)/shard_map/ppermute | solution.py:680
  60.0 0.0 collective-permute-done.14
  60.0 1.9 %collective-permute-done.13 = f32[8,128]{1,0:T(8,128)S(1)} collective-permute-done((f32[8,128]{1,0:T(8,128)S(1)}, f32[8,128]{1,0:T(8,128)S(1)}, u32[]{:S(2)}, u32[]{:S(2)}) %collective-permute-start.13) | collective-permute-done | bytes 4128 | tf_op jit(solution)/shard_map/ppermute | solution.py:680
  62.0 2.6 %collective-permute-start.18 = (f32[8,128]{1,0:T(8,128)S(1)}, f32[8,128]{1,0:T(8,128)S(1)}, u32[]{:S(2)}, u32[]{:S(2)}) collective-permute-start(f32[8,128]{1,0:T(8,128)S(1)} %add_add_fusion.rest_0_), channel_id=1, source_target_pairs={{0,24},{4,28},{8,16},{12,20},{16,8},{20,12},{24,0},{28,4},{1,25},{... | collective-permute-start | bytes 12296 | tf_op jit(solution)/shard_map/ppermute | solution.py:680
  64.5 0.8 %collective-permute-start.17 = (f32[8,128]{1,0:T(8,128)S(1)}, f32[8,128]{1,0:T(8,128)S(1)}, u32[]{:S(2)}, u32[]{:S(2)}) collective-permute-start(f32[8,128]{1,0:T(8,128)S(1)} %add_add_fusion.rest_0_), channel_id=1, source_target_pairs={{0,16},{4,20},{8,24},{12,28},{16,0},{20,4},{24,8},{28,12},{1,17},{... | collective-permute-start | bytes 12296 | tf_op jit(solution)/shard_map/ppermute | solution.py:680
  65.3 1.4 %collective-permute-start.16 = (f32[8,128]{1,0:T(8,128)S(1)}, f32[8,128]{1,0:T(8,128)S(1)}, u32[]{:S(2)}, u32[]{:S(2)}) collective-permute-start(f32[8,128]{1,0:T(8,128)S(1)} %add_add_fusion.rest_0_), channel_id=1, source_target_pairs={{0,8},{4,12},{8,0},{12,4},{16,24},{20,28},{24,16},{28,20},{1,9},{5... | collective-permute-start | bytes 12296 | tf_op jit(solution)/shard_map/ppermute | solution.py:680
  66.7 0.0 collective-permute-done.18.rest_3_
  66.7 1.4 %collective-permute-done.17.rest_2_ = f32[8,128]{1,0:T(8,128)S(1)} collective-permute-done((f32[8,128]{1,0:T(8,128)S(1)}, f32[8,128]{1,0:T(8,128)S(1)}, u32[]{:S(2)}, u32[]{:S(2)}) %collective-permute-start.17) | collective-permute-done | bytes 4128 | tf_op jit(solution)/shard_map/ppermute | solution.py:680
  68.1 0.8 %collective-permute-done.16.rest_1_ = f32[8,128]{1,0:T(8,128)S(1)} collective-permute-done((f32[8,128]{1,0:T(8,128)S(1)}, f32[8,128]{1,0:T(8,128)S(1)}, u32[]{:S(2)}, u32[]{:S(2)}) %collective-permute-start.16) | collective-permute-done | bytes 4128 | tf_op jit(solution)/shard_map/ppermute | solution.py:680
  69.0 0.9 %finish.1 = (f32[32,128]{1,0:T(8,128)}, f32[32,128]{1,0:T(8,128)}) custom-call(f32[32,128]{1,0:T(8,128)S(1)} %get-tuple-element.33.source, f32[32,128]{1,0:T(8,128)S(1)} %get-tuple-element.50.field.precond, f32[32,128]{1,0:T(8,128)S(1)} %get-tuple-element.58.spill, f32[32,128]{1,0:T(8,128)S(1)} %get-tuple-element.59.field.scaled, ...), custom_call_target="tpu_custom_call" | custom-call | tf_op jit(solution)/shard_map/finish/pallas_call | solution.py:667
  (2 shorter events, 0.0 us)
Async XLA Ops:
  0.6 5.0 %collective-permute-start.2 = (s32[7,128]{1,0:T(8,128)}, s32[7,128]{1,0:T(8,128)S(1)}, u32[]{:S(2)}, u32[]{:S(2)}) collective-permute-start(s32[7,128]{1,0:T(8,128)} %bitcast.1), channel_id=1, source_target_pairs={{0,1},{1,0},{2,3},{3,2},{4,5},{5,4},{6,7},{7,6},{8,9},{9,8},{10,11... | collective-permute-start | bytes 10760 | tf_op jit(solution)/shard_map/ppermute | solution.py:680
  5.4 16.0 %collective-permute-start = (f32[4,32,128]{2,1,0:T(8,128)S(1)}, f32[4,32,128]{2,1,0:T(8,128)S(1)}, u32[]{:S(2)}, u32[]{:S(2)}) collective-permute-start(f32[4,32,128]{2,1,0:T(8,128)S(1)} %get-tuple-element.40), channel_id=1, source_target_pairs={{0,4},{4,0},{8,12},{12,8},{16,20},{20,16},{24,28},{28,24},{1,5},{5... | collective-permute-start | bytes 196616 | tf_op jit(solution)/shard_map/ppermute | solution.py:702
  5.5 16.0 %collective-permute-start.1 = (f32[4,32,128]{2,1,0:T(8,128)S(1)}, f32[4,32,128]{2,1,0:T(8,128)S(1)}, u32[]{:S(2)}, u32[]{:S(2)}) collective-permute-start(f32[4,32,128]{2,1,0:T(8,128)S(1)} %get-tuple-element.41), channel_id=1, source_target_pairs={{0,1},{1,0},{2,3},{3,2},{4,8},{5,9},{6,10},{7,11},{8,4},{9,5},{10,... | collective-permute-start | bytes 196616 | tf_op jit(solution)/shard_map/ppermute | solution.py:707
  6.3 15.2 %collective-permute-start.3 = (s32[14,128]{1,0:T(8,128)S(1)}, s32[14,128]{1,0:T(8,128)S(1)}, u32[]{:S(2)}, u32[]{:S(2)}) collective-permute-start(s32[14,128]{1,0:T(8,128)S(1)} %pad_add_fusion.rest_0_), channel_id=1, source_target_pairs={{0,3},{1,2},{2,1},{3,0},{4,7},{5,6},{6,5},{7,4},{8,11},{9,10},{10,... | collective-permute-start | bytes 21512 | tf_op jit(solution)/shard_map/ppermute | solution.py:680
  26.2 10.3 %collective-permute-start.7 = (f32[32,128]{1,0:T(8,128)S(1)}, f32[32,128]{1,0:T(8,128)S(1)}, u32[]{:S(2)}, u32[]{:S(2)}) collective-permute-start(f32[32,128]{1,0:T(8,128)S(1)} %get-tuple-element.50.field.precond), channel_id=1, source_target_pairs={{0,1},{1,0},{2,3},{3,2},{4,5},{5,4},{6,7},{7,6},{8,9},{9,8},{10,11... | collective-permute-start | bytes 49160 | tf_op jit(solution)/shard_map/ppermute | solution.py:754
  29.1 7.4 %collective-permute-start.6 = (f32[32,128]{1,0:T(8,128)S(1)}, f32[32,128]{1,0:T(8,128)S(1)}, u32[]{:S(2)}, u32[]{:S(2)}) collective-permute-start(f32[32,128]{1,0:T(8,128)S(1)} %get-tuple-element.50.field.precond), channel_id=1, source_target_pairs={{0,31},{1,2},{2,1},{3,4},{4,3},{5,6},{6,5},{7,8},{8,7},{9,10},{10,... | collective-permute-start | bytes 49160 | tf_op jit(solution)/shard_map/ppermute | solution.py:754
  32.1 5.5 %collective-permute-start.5 = (f32[32,128]{1,0:T(8,128)S(1)}, f32[32,128]{1,0:T(8,128)S(1)}, u32[]{:S(2)}, u32[]{:S(2)}) collective-permute-start(f32[32,128]{1,0:T(8,128)S(1)} %get-tuple-element.50.field.precond), channel_id=1, source_target_pairs={{0,2},{1,4},{2,3},{3,0},{4,1},{5,8},{6,7},{7,6},{8,5},{9,12},{10,1... | collective-permute-start | bytes 49160 | tf_op jit(solution)/shard_map/ppermute | solution.py:754
  32.1 5.7 %collective-permute-start.4 = (f32[32,128]{1,0:T(8,128)S(1)}, f32[32,128]{1,0:T(8,128)S(1)}, u32[]{:S(2)}, u32[]{:S(2)}) collective-permute-start(f32[32,128]{1,0:T(8,128)S(1)} %get-tuple-element.50.field.precond), channel_id=1, source_target_pairs={{0,1},{1,3},{2,4},{3,0},{4,2},{5,7},{6,8},{7,5},{8,6},{9,11},{10,1... | collective-permute-start | bytes 49160 | tf_op jit(solution)/shard_map/ppermute | solution.py:754
  39.9 9.6 %collective-permute-start.11 = (f32[32,128]{1,0:T(8,128)S(1)}, f32[32,128]{1,0:T(8,128)S(1)}, u32[]{:S(2)}, u32[]{:S(2)}) collective-permute-start(f32[32,128]{1,0:T(8,128)S(1)} %get-tuple-element.59.field.scaled), channel_id=1, source_target_pairs={{0,1},{1,0},{2,3},{3,2},{4,5},{5,4},{6,7},{7,6},{8,9},{9,8},{10,11... | collective-permute-start | bytes 49160 | tf_op jit(solution)/shard_map/ppermute | solution.py:754
  43.7 6.9 %collective-permute-start.10 = (f32[32,128]{1,0:T(8,128)S(1)}, f32[32,128]{1,0:T(8,128)S(1)}, u32[]{:S(2)}, u32[]{:S(2)}) collective-permute-start(f32[32,128]{1,0:T(8,128)S(1)} %get-tuple-element.59.field.scaled), channel_id=1, source_target_pairs={{0,31},{1,2},{2,1},{3,4},{4,3},{5,6},{6,5},{7,8},{8,7},{9,10},{10,... | collective-permute-start | bytes 49160 | tf_op jit(solution)/shard_map/ppermute | solution.py:754
  44.0 6.5 %collective-permute-start.9 = (f32[32,128]{1,0:T(8,128)S(1)}, f32[32,128]{1,0:T(8,128)S(1)}, u32[]{:S(2)}, u32[]{:S(2)}) collective-permute-start(f32[32,128]{1,0:T(8,128)S(1)} %get-tuple-element.59.field.scaled), channel_id=1, source_target_pairs={{0,2},{1,4},{2,3},{3,0},{4,1},{5,8},{6,7},{7,6},{8,5},{9,12},{10,1... | collective-permute-start | bytes 49160 | tf_op jit(solution)/shard_map/ppermute | solution.py:754
  45.3 5.5 %collective-permute-start.8 = (f32[32,128]{1,0:T(8,128)S(1)}, f32[32,128]{1,0:T(8,128)S(1)}, u32[]{:S(2)}, u32[]{:S(2)}) collective-permute-start(f32[32,128]{1,0:T(8,128)S(1)} %get-tuple-element.59.field.scaled), channel_id=1, source_target_pairs={{0,1},{1,3},{2,4},{3,0},{4,2},{5,7},{6,8},{7,5},{8,6},{9,11},{10,1... | collective-permute-start | bytes 49160 | tf_op jit(solution)/shard_map/ppermute | solution.py:754
  53.0 1.5 %collective-permute-start.12 = (f32[8,128]{1,0:T(8,128)S(1)}, f32[8,128]{1,0:T(8,128)S(1)}, u32[]{:S(2)}, u32[]{:S(2)}) collective-permute-start(f32[8,128]{1,0:T(8,128)S(1)} %get-tuple-element.63), channel_id=1, source_target_pairs={{0,4},{4,0},{8,12},{12,8},{16,20},{20,16},{24,28},{28,24},{1,5},{5... | collective-permute-start | bytes 12296 | tf_op jit(solution)/shard_map/ppermute | solution.py:680
  54.6 5.4 %collective-permute-start.15 = (f32[8,128]{1,0:T(8,128)S(1)}, f32[8,128]{1,0:T(8,128)S(1)}, u32[]{:S(2)}, u32[]{:S(2)}) collective-permute-start(f32[8,128]{1,0:T(8,128)S(1)} %add.12), channel_id=1, source_target_pairs={{0,3},{1,2},{2,1},{3,0},{4,7},{5,6},{6,5},{7,4},{8,11},{9,10},{10,... | collective-permute-start | bytes 12296 | tf_op jit(solution)/shard_map/ppermute | solution.py:680
  55.4 4.7 %collective-permute-start.14 = (f32[8,128]{1,0:T(8,128)S(1)}, f32[8,128]{1,0:T(8,128)S(1)}, u32[]{:S(2)}, u32[]{:S(2)}) collective-permute-start(f32[8,128]{1,0:T(8,128)S(1)} %add.12), channel_id=1, source_target_pairs={{0,2},{1,3},{2,0},{3,1},{4,6},{5,7},{6,4},{7,5},{8,10},{9,11},{10,... | collective-permute-start | bytes 12296 | tf_op jit(solution)/shard_map/ppermute | solution.py:680
  58.3 3.6 %collective-permute-start.13 = (f32[8,128]{1,0:T(8,128)S(1)}, f32[8,128]{1,0:T(8,128)S(1)}, u32[]{:S(2)}, u32[]{:S(2)}) collective-permute-start(f32[8,128]{1,0:T(8,128)S(1)} %add.12), channel_id=1, source_target_pairs={{0,1},{1,0},{2,3},{3,2},{4,5},{5,4},{6,7},{7,6},{8,9},{9,8},{10,11... | collective-permute-start | bytes 12296 | tf_op jit(solution)/shard_map/ppermute | solution.py:680
  62.0 4.8 %collective-permute-start.18 = (f32[8,128]{1,0:T(8,128)S(1)}, f32[8,128]{1,0:T(8,128)S(1)}, u32[]{:S(2)}, u32[]{:S(2)}) collective-permute-start(f32[8,128]{1,0:T(8,128)S(1)} %add_add_fusion.rest_0_), channel_id=1, source_target_pairs={{0,24},{4,28},{8,16},{12,20},{16,8},{20,12},{24,0},{28,4},{1,25},{... | collective-permute-start | bytes 12296 | tf_op jit(solution)/shard_map/ppermute | solution.py:680
  64.5 3.6 %collective-permute-start.17 = (f32[8,128]{1,0:T(8,128)S(1)}, f32[8,128]{1,0:T(8,128)S(1)}, u32[]{:S(2)}, u32[]{:S(2)}) collective-permute-start(f32[8,128]{1,0:T(8,128)S(1)} %add_add_fusion.rest_0_), channel_id=1, source_target_pairs={{0,16},{4,20},{8,24},{12,28},{16,0},{20,4},{24,8},{28,12},{1,17},{... | collective-permute-start | bytes 12296 | tf_op jit(solution)/shard_map/ppermute | solution.py:680
  65.3 3.6 %collective-permute-start.16 = (f32[8,128]{1,0:T(8,128)S(1)}, f32[8,128]{1,0:T(8,128)S(1)}, u32[]{:S(2)}, u32[]{:S(2)}) collective-permute-start(f32[8,128]{1,0:T(8,128)S(1)} %add_add_fusion.rest_0_), channel_id=1, source_target_pairs={{0,8},{4,12},{8,0},{12,4},{16,24},{20,28},{24,16},{28,20},{1,9},{5... | collective-permute-start | bytes 12296 | tf_op jit(solution)/shard_map/ppermute | solution.py:680

commit v17 on v12

--- a/solution.py
+++ b/solution.py
@@ -288,8 +288,8 @@
 
 
 def prepare(
-    counts, densities, position_in, phase_in, right_side_in, table_in,
-    meta, table, hood, near, density, source, first_swap, second_swap, phase, right_side, sems
+    counts, densities, position_in, phase_in, right_side_in, table_in, lists_in,
+    meta, table, hood, near, density, source, first_swap, second_swap, lists, phase, right_side, sems
 ):
     share, width = source.shape
     capacity = phase.shape[0]
@@ -299,6 +299,7 @@
         pltpu.make_async_copy(position_in, hood.at[pl.ds(0, 3), body_rows, :], sems.at[1]),
         pltpu.make_async_copy(right_side_in, right_side, sems.at[2]),
         pltpu.make_async_copy(table_in, table, sems.at[3]),
+        pltpu.make_async_copy(lists_in, lists, sems.at[4]),
     ]
     for copy in copies:
         copy.start()
@@ -673,23 +674,18 @@
     def swap(values, axis, step):
         return lax.ppermute(values, axis, [(i, i ^ step) for i in range(lax.axis_size(axis))])
 
-    col_steps = [(1 << k) | 1 for k in range(columns.bit_length() - 1)]
-    lists = [neighbours.T]
-    for step in col_steps:
-        known = lists[0] if len(lists) == 1 else jnp.concatenate(lists, 0)
-        lists = [known, swap(known, "col", step)]
-
     def away(array):
         return pltpu.with_memory_space_constraint(array, pltpu.HBM)
 
     around = jax.ShapeDtypeStruct((4, capacity + 2 * share, width), f32)
     near = jax.ShapeDtypeStruct((4, 2 * share, width), f32)
-    far = [away(array) for array in (positions, phase, right_side, table)]
-    meta, table, around, near, density, source, first, second = call(
+    far = [away(array) for array in (positions, phase, right_side, table, neighbours.T)]
+    meta, table, around, near, density, source, first, second, own_lists = call(
         prepare,
         (away(counts), away(phase_density), *far),
-        [pltpu.SMEM((8,), jnp.int32), pltpu.SMEM(table.shape, jnp.int32), around, near, vector, vector, message, message],
-        [pltpu.VMEM(phase.shape, jnp.int32), pltpu.VMEM((share, width), f32), pltpu.SemaphoreType.DMA((4,))],
+        [pltpu.SMEM((8,), jnp.int32), pltpu.SMEM(table.shape, jnp.int32), around, near, vector, vector, message, message,
+         jax.ShapeDtypeStruct(far[-1].shape, jnp.int32)],
+        [pltpu.VMEM(phase.shape, jnp.int32), pltpu.VMEM((share, width), f32), pltpu.SemaphoreType.DMA((5,))],
         far=len(far),
     )
     meta, table = (pltpu.with_memory_space_constraint(array, pltpu.SMEM) for array in (meta, table))
@@ -699,6 +695,12 @@
     partner = [(p + (1 if p % 2 else -1), c) for p, c in device]
     partner = [(q, d) if 0 <= q < pieces else (p, c ^ 1) for (q, d), (p, c) in zip(partner, device)]
     second = lax.ppermute(second, axes, [(i, q * columns + d) for i, (q, d) in enumerate(partner)])
+
+    col_steps = [(1 << k) | 1 for k in range(columns.bit_length() - 1)]
+    lists = [own_lists]
+    for step in col_steps:
+        known = lists[0] if len(lists) == 1 else jnp.concatenate(lists, 0)
+        lists = [known, swap(known, "col", step)]
 
     plan, runs, tiles_in, sides, middles, weights, rows, cols, selfs = call(
         build_inner,
@@ -741,9 +743,13 @@
             for p in range(pieces - 1):
                 low, high = p * columns + c, (p + 1) * columns
                 to[low], to[high] = high, low
-            for p in range(pieces):
-                rest = [i for i in range(p * columns, (p + 1) * columns) if i not in to]
-                to.update(zip(rest, rest[1:] + rest[:1]))
+            spare = {c % (columns - 1) + 1: [0], (c + 1) % (columns - 1) + 1: [(pieces - 1) * columns + c]}
+            for p in range(0, pieces, 2):
+                for d in range(1, columns):
+                    if d != c:
+                        ring = [p * columns + d, (p + 1) * columns + d]
+                        ring += spare.get(d, []) if p == (0 if spare.get(d) == [0] else pieces - 2) else []
+                        to.update(zip(ring, ring[1:] + ring[:1]))
             swaps.append([to[i] for i in range(count)])
         return [lax.ppermute(field, axes, list(enumerate(to))) for to in swaps]
 

time: 70.1 us -> 68.7 us (0.980)
    ppermute x8, waiting for transfers between devices: 1.64 us -> 0.02 us  [exchange(): return [lax.ppermute(field, axes, list(enumerate(to))) for to in swaps]]
    ppermute x9, starting transfers between devices: 16.8 us -> 15.4 us  [swap(): lax.ppermute(values, axis, [(i, i ^ step) for i in range(lax.axis_size(ax...]
    ppermute x8, starting transfers between devices: 12.2 us -> 13.5 us  [exchange(): return [lax.ppermute(field, axes, list(enumerate(to))) for to in swaps]]
    ppermute x9, waiting for transfers between devices: 6.34 us -> 7.62 us  [swap(): lax.ppermute(values, axis, [(i, i ^ step) for i in range(lax.axis_size(ax...]
  transfers between devices with their start and end apart: 19 -> 19, of which waited for: 7 -> 7; matrix products, arithmetic and copies ran while one was open for 1% -> 0% of each run, Pallas kernels for 30% -> 28%
where the time goes in v17:
time: 68.7 us; the launch traced here: 68.6 us
  Pallas kernels  31.1 us (45%)
  starting transfers between devices  29.1 us (42%)
  waiting for transfers between devices  7.65 us (11%)
  between operations  0.79 us (1%)
    pallas_call x8, Pallas kernels, call(): pl.pallas_call(kernel, out_shape=outs, in_specs=[SMEM] * scalars + [HBM]...  31.1 us
    ppermute x9, starting transfers between devices, swap(): lax.ppermute(values, axis, [(i, i ^ step) for i in range(lax.axis_size(ax...  15.4 us
    ppermute x8, starting transfers between devices, exchange(): return [lax.ppermute(field, axes, list(enumerate(to))) for to in swaps]  13.5 us
    ppermute x9, waiting for transfers between devices, swap(): lax.ppermute(values, axis, [(i, i ^ step) for i in range(lax.axis_size(ax...  7.62 us
  transfers between devices with their start and end apart: 19, of which 7 were waited for; matrix products, arithmetic and copies ran while one was open for 0% of the time, Pallas kernels for 28%

profile of v17, /device:TPU:0, one launch (start us, length us, event | category | flops | bytes accessed | tf_op | source)
XLA Modules:
  0.0 68.6 jit_solution(8191658519217236960)
XLA Ops:
  0.6 1.7 %prepare.1 = (s32[8]{0:T(128)S(4)}, s32[1480]{0:T(1024)S(4)}, f32[4,192,128]{2,1,0:T(8,128)S(1)}, f32[4,64,128]{2,1,0:T(8,128)S(1)}, f32[32,128]{1,0:T(8,128)S(1...) custom-call(s32[8]{0:T(128)} %counts.1, f32[3]{0:T(128)} %densities.1, ...), custom_call_target="tpu_custom_call" | custom-call | tf_op jit(solution)/shard_map/prepare/pallas_call | solution.py:662
  2.4 3.1 %collective-permute-start.2 = (s32[7,128]{1,0:T(8,128)S(1)}, s32[7,128]{1,0:T(8,128)S(1)}, u32[]{:S(2)}, u32[]{:S(2)}) collective-permute-start(s32[7,128]{1,0:T(8,128)S(1)} %get-tuple-element.51), channel_id=1, source_target_pairs={{0,1},{1,0},{2,3},{3,2},{4,5},{5,4},{6,7},{7,6},{8,9},{9,8},{10,11... | collective-permute-start | bytes 10760 | tf_op jit(solution)/shard_map/ppermute | solution.py:675
  5.5 0.0 collective-permute-start
  5.5 0.2 collective-permute-start.1
  5.6 1.4 %collective-permute-done.2 = s32[7,128]{1,0:T(8,128)S(1)} collective-permute-done((s32[7,128]{1,0:T(8,128)S(1)}, s32[7,128]{1,0:T(8,128)S(1)}, u32[]{:S(2)}, u32[]{:S(2)}) %collective-permute-start.2) | collective-permute-done | bytes 3616 | tf_op jit(solution)/shard_map/ppermute | solution.py:675
  7.0 4.0 %collective-permute-start.3 = (s32[14,128]{1,0:T(8,128)S(1)}, s32[14,128]{1,0:T(8,128)S(1)}, u32[]{:S(2)}, u32[]{:S(2)}) collective-permute-start(s32[14,128]{1,0:T(8,128)S(1)} %pad_add_fusion.rest_0_), channel_id=1, source_target_pairs={{0,3},{1,2},{2,1},{3,0},{4,7},{5,6},{6,5},{7,4},{8,11},{9,10},{10,... | collective-permute-start | bytes 21512 | tf_op jit(solution)/shard_map/ppermute | solution.py:675
  11.1 10.8 %build_inner.1 = (s32[196]{0:T(256)S(4)}, s32[195]{0:T(256)S(4)}, f32[224,128,128]{2,1,0:T(8,128)S(1)}, bf16[2,32,128,128]{3,2,1,0:T(8,128)(2,1)S(1)}, f32[3,32,...) custom-call(s32[8]{0:T(128)S(4)} %get-tuple-element.35.meta, ...), custom_call_target="tpu_custom_call" | custom-call | flops 56623104 | tf_op jit(solution)/shard_map/build_inner/pallas_call | solution.py:662
  21.9 0.0 collective-permute-done.3.rest_1_
  21.9 0.0 collective-permute-done.first
  21.9 0.0 collective-permute-done.1.second
  21.9 4.6 %build_outer.1 = (s32[1]{0:T(128)S(4)}, f32[230,128,128]{2,1,0:T(8,128)S(1)}, f32[32,128]{1,0:T(8,128)S(1)}, f32[32,128]{1,0:T(8,128)S(1)}, f32[32,128]{1,0:T(8,128)S(1)}, /*index=5*/f32[32,128]{1,0:T(8,128)S(1)}) custom-call(s32[8]{0:T(128)S(4)} %get-tuple-element.35.meta, s32[1480]{0:T(1024)S(4)} %get-tuple-element.36.table, ...), custom_call_target="tpu_custom_call" | custom-call | flops 58195968 | tf_op jit(solution)/shard_map/build_outer/pallas_call | solution.py:662
  26.5 0.1 collective-permute-start.7
  26.6 4.6 %collective-permute-start.6 = (f32[32,128]{1,0:T(8,128)S(1)}, f32[32,128]{1,0:T(8,128)S(1)}, u32[]{:S(2)}, u32[]{:S(2)}) collective-permute-start(f32[32,128]{1,0:T(8,128)S(1)} %get-tuple-element.52.field.precond), channel_id=1, source_target_pairs={{0,2},{1,4},{2,6},{3,7},{4,1},{5,8},{6,0},{7,3},{8,5},{9,12},{10,1... | collective-permute-start | bytes 49160 | tf_op jit(solution)/shard_map/ppermute | solution.py:754
  31.1 0.5 collective-permute-start.5
  31.6 3.1 %collective-permute-start.4 = (f32[32,128]{1,0:T(8,128)S(1)}, f32[32,128]{1,0:T(8,128)S(1)}, u32[]{:S(2)}, u32[]{:S(2)}) collective-permute-start(f32[32,128]{1,0:T(8,128)S(1)} %get-tuple-element.52.field.precond), channel_id=1, source_target_pairs={{0,1},{1,0},{2,3},{3,2},{4,5},{5,4},{6,7},{7,6},{8,9},{9,8},{10,11... | collective-permute-start | bytes 49160 | tf_op jit(solution)/shard_map/ppermute | solution.py:754
  34.7 4.3 %apply_inner.2 = (f32[32,128,128]{2,1,0:T(8,128)S(1)}, f32[256,128]{1,0:T(8,128)S(1)}) custom-call(s32[8]{0:T(128)S(4)} %get-tuple-element.35.meta, s32[1480]{0:T(1024)S(4)} %get-tuple-element.36.table, s32[196]{0:T(256)S(4)} %get-tuple-element.38.plan, s32[1]{0:T(128)S(4)} %get-tuple-element.53.again, f32[32,128]{1,0:T(8,128)S(1)} %get-tuple-element.52.field.precond, ...), custom_call_target="tpu_custom_call" | custom-call | flops 14155776 | tf_op jit(solution)/shard_map/apply_inner/pallas_call | solution.py:662
  39.0 0.0 collective-permute-done.7.rest_3_
  39.0 0.0 collective-permute-done.6.rest_2_
  39.1 0.0 collective-permute-done.5.rest_1_
  39.1 0.0 collective-permute-done.4.rest_0_
  39.1 2.2 %apply_first.1 = (f32[32,128]{1,0:T(8,128)S(1)}, f32[32,128]{1,0:T(8,128)S(1)}) custom-call(s32[8]{0:T(128)S(4)} %get-tuple-element.35.meta, s32[1480]{0:T(1024)S(4)} %get-tuple-element.36.table, s32[196]{0:T(256)S(4)} %get-tuple-element.38.plan, s32[1]{0:T(128)S(4)} %get-tuple-element.53.again, f32[32,128]{1,0:T(8,128)S(1)} %get-tuple-element.54.diagonal, ...), custom_call_target="tpu_custom_call" | custom-call | flops 7274496 | tf_op jit(solution)/shard_map/apply_first/pallas_call | solution.py:662
  41.2 0.1 collective-permute-start.11
  41.3 2.7 %collective-permute-start.10 = (f32[32,128]{1,0:T(8,128)S(1)}, f32[32,128]{1,0:T(8,128)S(1)}, u32[]{:S(2)}, u32[]{:S(2)}) collective-permute-start(f32[32,128]{1,0:T(8,128)S(1)} %get-tuple-element.61.field.scaled), channel_id=1, source_target_pairs={{0,2},{1,4},{2,6},{3,7},{4,1},{5,8},{6,0},{7,3},{8,5},{9,12},{10,1... | collective-permute-start | bytes 49160 | tf_op jit(solution)/shard_map/ppermute | solution.py:754
  44.0 0.6 collective-permute-start.9
  44.6 2.0 %collective-permute-start.8 = (f32[32,128]{1,0:T(8,128)S(1)}, f32[32,128]{1,0:T(8,128)S(1)}, u32[]{:S(2)}, u32[]{:S(2)}) collective-permute-start(f32[32,128]{1,0:T(8,128)S(1)} %get-tuple-element.61.field.scaled), channel_id=1, source_target_pairs={{0,1},{1,0},{2,3},{3,2},{4,5},{5,4},{6,7},{7,6},{8,9},{9,8},{10,11... | collective-permute-start | bytes 49160 | tf_op jit(solution)/shard_map/ppermute | solution.py:754
  46.6 4.3 %apply_inner.3 = (f32[32,128,128]{2,1,0:T(8,128)S(1)}, f32[256,128]{1,0:T(8,128)S(1)}) custom-call(s32[8]{0:T(128)S(4)} %get-tuple-element.35.meta, s32[1480]{0:T(1024)S(4)} %get-tuple-element.36.table, s32[196]{0:T(256)S(4)} %get-tuple-element.38.plan, s32[1]{0:T(128)S(4)} %get-tuple-element.53.again, f32[32,128]{1,0:T(8,128)S(1)} %get-tuple-element.61.field.scaled, ...), custom_call_target="tpu_custom_call" | custom-call | flops 14155776 | tf_op jit(solution)/shard_map/apply_inner/pallas_call | solution.py:662
  50.9 0.0 collective-permute-done.11.rest_3_
  50.9 0.0 collective-permute-done.10.rest_2_
  50.9 0.0 collective-permute-done.9.rest_1_
  50.9 0.0 collective-permute-done.8.rest_0_
  50.9 2.3 %apply_second.1 = (f32[32,128]{1,0:T(8,128)S(1)}, f32[8,128]{1,0:T(8,128)S(1)}) custom-call(s32[8]{0:T(128)S(4)} %get-tuple-element.35.meta, s32[1480]{0:T(1024)S(4)} %get-tuple-element.36.table, s32[196]{0:T(256)S(4)} %get-tuple-element.38.plan, s32[1]{0:T(128)S(4)} %get-tuple-element.53.again, f32[32,128]{1,0:T(8,128)S(1)} %get-tuple-element.34.source, ...), custom_call_target="tpu_custom_call" | custom-call | flops 7274496 | tf_op jit(solution)/shard_map/apply_second/pallas_call | solution.py:662
  53.2 0.2 collective-permute-start.12
  53.4 1.0 %collective-permute-done.12 = f32[8,128]{1,0:T(8,128)S(1)} collective-permute-done((f32[8,128]{1,0:T(8,128)S(1)}, f32[8,128]{1,0:T(8,128)S(1)}, u32[]{:S(2)}, u32[]{:S(2)}) %collective-permute-start.12) | collective-permute-done | bytes 4128 | tf_op jit(solution)/shard_map/ppermute | solution.py:675
  54.4 0.0 collective-permute-start.15
  54.4 2.4 %collective-permute-start.14 = (f32[8,128]{1,0:T(8,128)S(1)}, f32[8,128]{1,0:T(8,128)S(1)}, u32[]{:S(2)}, u32[]{:S(2)}) collective-permute-start(f32[8,128]{1,0:T(8,128)S(1)} %add.12), channel_id=1, source_target_pairs={{0,2},{1,3},{2,0},{3,1},{4,6},{5,7},{6,4},{7,5},{8,10},{9,11},{10,... | collective-permute-start | bytes 12296 | tf_op jit(solution)/shard_map/ppermute | solution.py:675
  56.7 2.0 %collective-permute-start.13 = (f32[8,128]{1,0:T(8,128)S(1)}, f32[8,128]{1,0:T(8,128)S(1)}, u32[]{:S(2)}, u32[]{:S(2)}) collective-permute-start(f32[8,128]{1,0:T(8,128)S(1)} %add.12), channel_id=1, source_target_pairs={{0,1},{1,0},{2,3},{3,2},{4,5},{5,4},{6,7},{7,6},{8,9},{9,8},{10,11... | collective-permute-start | bytes 12296 | tf_op jit(solution)/shard_map/ppermute | solution.py:675
  58.8 1.0 %collective-permute-done.15 = f32[8,128]{1,0:T(8,128)S(1)} collective-permute-done((f32[8,128]{1,0:T(8,128)S(1)}, f32[8,128]{1,0:T(8,128)S(1)}, u32[]{:S(2)}, u32[]{:S(2)}) %collective-permute-start.15) | collective-permute-done | bytes 4128 | tf_op jit(solution)/shard_map/ppermute | solution.py:675
  59.8 0.0 collective-permute-done.14
  59.8 0.6 collective-permute-done.13
  60.3 0.6 collective-permute-start.18
  60.9 3.1 %collective-permute-start.17 = (f32[8,128]{1,0:T(8,128)S(1)}, f32[8,128]{1,0:T(8,128)S(1)}, u32[]{:S(2)}, u32[]{:S(2)}) collective-permute-start(f32[8,128]{1,0:T(8,128)S(1)} %add_add_fusion.rest_0_), channel_id=1, source_target_pairs={{0,16},{4,20},{8,24},{12,28},{16,0},{20,4},{24,8},{28,12},{1,17},{... | collective-permute-start | bytes 12296 | tf_op jit(solution)/shard_map/ppermute | solution.py:675
  64.0 0.0 collective-permute-start.16
  64.0 0.8 %collective-permute-done.18.rest_3_ = f32[8,128]{1,0:T(8,128)S(1)} collective-permute-done((f32[8,128]{1,0:T(8,128)S(1)}, f32[8,128]{1,0:T(8,128)S(1)}, u32[]{:S(2)}, u32[]{:S(2)}) %collective-permute-start.18) | collective-permute-done | bytes 4128 | tf_op jit(solution)/shard_map/ppermute | solution.py:675
  64.9 0.7 %collective-permute-done.17.rest_2_ = f32[8,128]{1,0:T(8,128)S(1)} collective-permute-done((f32[8,128]{1,0:T(8,128)S(1)}, f32[8,128]{1,0:T(8,128)S(1)}, u32[]{:S(2)}, u32[]{:S(2)}) %collective-permute-start.17) | collective-permute-done | bytes 4128 | tf_op jit(solution)/shard_map/ppermute | solution.py:675
  65.6 2.0 %collective-permute-done.16.rest_1_ = f32[8,128]{1,0:T(8,128)S(1)} collective-permute-done((f32[8,128]{1,0:T(8,128)S(1)}, f32[8,128]{1,0:T(8,128)S(1)}, u32[]{:S(2)}, u32[]{:S(2)}) %collective-permute-start.16) | collective-permute-done | bytes 4128 | tf_op jit(solution)/shard_map/ppermute | solution.py:675
  67.6 0.9 %finish.1 = (f32[32,128]{1,0:T(8,128)}, f32[32,128]{1,0:T(8,128)}) custom-call(f32[32,128]{1,0:T(8,128)S(1)} %get-tuple-element.34.source, f32[32,128]{1,0:T(8,128)S(1)} %get-tuple-element.52.field.precond, f32[32,128]{1,0:T(8,128)S(1)} %get-tuple-element.60.spill, f32[32,128]{1,0:T(8,128)S(1)} %get-tuple-element.61.field.scaled, ...), custom_call_target="tpu_custom_call" | custom-call | tf_op jit(solution)/shard_map/finish/pallas_call | solution.py:662
  (3 shorter events, 0.0 us)
Async XLA Ops:
  2.4 4.7 %collective-permute-start.2 = (s32[7,128]{1,0:T(8,128)S(1)}, s32[7,128]{1,0:T(8,128)S(1)}, u32[]{:S(2)}, u32[]{:S(2)}) collective-permute-start(s32[7,128]{1,0:T(8,128)S(1)} %get-tuple-element.51), channel_id=1, source_target_pairs={{0,1},{1,0},{2,3},{3,2},{4,5},{5,4},{6,7},{7,6},{8,9},{9,8},{10,11... | collective-permute-start | bytes 10760 | tf_op jit(solution)/shard_map/ppermute | solution.py:675
  5.5 16.4 %collective-permute-start = (f32[4,32,128]{2,1,0:T(8,128)S(1)}, f32[4,32,128]{2,1,0:T(8,128)S(1)}, u32[]{:S(2)}, u32[]{:S(2)}) collective-permute-start(f32[4,32,128]{2,1,0:T(8,128)S(1)} %get-tuple-element.41), channel_id=1, source_target_pairs={{0,4},{4,0},{8,12},{12,8},{16,20},{20,16},{24,28},{28,24},{1,5},{5... | collective-permute-start | bytes 196616 | tf_op jit(solution)/shard_map/ppermute | solution.py:692
  5.5 16.4 %collective-permute-start.1 = (f32[4,32,128]{2,1,0:T(8,128)S(1)}, f32[4,32,128]{2,1,0:T(8,128)S(1)}, u32[]{:S(2)}, u32[]{:S(2)}) collective-permute-start(f32[4,32,128]{2,1,0:T(8,128)S(1)} %get-tuple-element.42), channel_id=1, source_target_pairs={{0,1},{1,0},{2,3},{3,2},{4,8},{5,9},{6,10},{7,11},{8,4},{9,5},{10,... | collective-permute-start | bytes 196616 | tf_op jit(solution)/shard_map/ppermute | solution.py:697
  7.0 14.8 %collective-permute-start.3 = (s32[14,128]{1,0:T(8,128)S(1)}, s32[14,128]{1,0:T(8,128)S(1)}, u32[]{:S(2)}, u32[]{:S(2)}) collective-permute-start(s32[14,128]{1,0:T(8,128)S(1)} %pad_add_fusion.rest_0_), channel_id=1, source_target_pairs={{0,3},{1,2},{2,1},{3,0},{4,7},{5,6},{6,5},{7,4},{8,11},{9,10},{10,... | collective-permute-start | bytes 21512 | tf_op jit(solution)/shard_map/ppermute | solution.py:675
  26.5 12.5 %collective-permute-start.7 = (f32[32,128]{1,0:T(8,128)S(1)}, f32[32,128]{1,0:T(8,128)S(1)}, u32[]{:S(2)}, u32[]{:S(2)}) collective-permute-start(f32[32,128]{1,0:T(8,128)S(1)} %get-tuple-element.52.field.precond), channel_id=1, source_target_pairs={{0,3},{1,5},{2,4},{3,7},{4,2},{5,1},{6,8},{7,0},{8,6},{9,13},{10,1... | collective-permute-start | bytes 49160 | tf_op jit(solution)/shard_map/ppermute | solution.py:754
  26.6 12.5 %collective-permute-start.6 = (f32[32,128]{1,0:T(8,128)S(1)}, f32[32,128]{1,0:T(8,128)S(1)}, u32[]{:S(2)}, u32[]{:S(2)}) collective-permute-start(f32[32,128]{1,0:T(8,128)S(1)} %get-tuple-element.52.field.precond), channel_id=1, source_target_pairs={{0,2},{1,4},{2,6},{3,7},{4,1},{5,8},{6,0},{7,3},{8,5},{9,12},{10,1... | collective-permute-start | bytes 49160 | tf_op jit(solution)/shard_map/ppermute | solution.py:754
  31.1 7.9 %collective-permute-start.5 = (f32[32,128]{1,0:T(8,128)S(1)}, f32[32,128]{1,0:T(8,128)S(1)}, u32[]{:S(2)}, u32[]{:S(2)}) collective-permute-start(f32[32,128]{1,0:T(8,128)S(1)} %get-tuple-element.52.field.precond), channel_id=1, source_target_pairs={{0,31},{1,2},{2,1},{3,4},{4,3},{5,6},{6,5},{7,8},{8,7},{9,10},{10,... | collective-permute-start | bytes 49160 | tf_op jit(solution)/shard_map/ppermute | solution.py:754
  31.6 7.5 %collective-permute-start.4 = (f32[32,128]{1,0:T(8,128)S(1)}, f32[32,128]{1,0:T(8,128)S(1)}, u32[]{:S(2)}, u32[]{:S(2)}) collective-permute-start(f32[32,128]{1,0:T(8,128)S(1)} %get-tuple-element.52.field.precond), channel_id=1, source_target_pairs={{0,1},{1,0},{2,3},{3,2},{4,5},{5,4},{6,7},{7,6},{8,9},{9,8},{10,11... | collective-permute-start | bytes 49160 | tf_op jit(solution)/shard_map/ppermute | solution.py:754
  41.2 9.6 %collective-permute-start.11 = (f32[32,128]{1,0:T(8,128)S(1)}, f32[32,128]{1,0:T(8,128)S(1)}, u32[]{:S(2)}, u32[]{:S(2)}) collective-permute-start(f32[32,128]{1,0:T(8,128)S(1)} %get-tuple-element.61.field.scaled), channel_id=1, source_target_pairs={{0,3},{1,5},{2,4},{3,7},{4,2},{5,1},{6,8},{7,0},{8,6},{9,13},{10,1... | collective-permute-start | bytes 49160 | tf_op jit(solution)/shard_map/ppermute | solution.py:754
  41.3 9.6 %collective-permute-start.10 = (f32[32,128]{1,0:T(8,128)S(1)}, f32[32,128]{1,0:T(8,128)S(1)}, u32[]{:S(2)}, u32[]{:S(2)}) collective-permute-start(f32[32,128]{1,0:T(8,128)S(1)} %get-tuple-element.61.field.scaled), channel_id=1, source_target_pairs={{0,2},{1,4},{2,6},{3,7},{4,1},{5,8},{6,0},{7,3},{8,5},{9,12},{10,1... | collective-permute-start | bytes 49160 | tf_op jit(solution)/shard_map/ppermute | solution.py:754
  44.0 6.9 %collective-permute-start.9 = (f32[32,128]{1,0:T(8,128)S(1)}, f32[32,128]{1,0:T(8,128)S(1)}, u32[]{:S(2)}, u32[]{:S(2)}) collective-permute-start(f32[32,128]{1,0:T(8,128)S(1)} %get-tuple-element.61.field.scaled), channel_id=1, source_target_pairs={{0,31},{1,2},{2,1},{3,4},{4,3},{5,6},{6,5},{7,8},{8,7},{9,10},{10,... | collective-permute-start | bytes 49160 | tf_op jit(solution)/shard_map/ppermute | solution.py:754
  44.6 6.4 %collective-permute-start.8 = (f32[32,128]{1,0:T(8,128)S(1)}, f32[32,128]{1,0:T(8,128)S(1)}, u32[]{:S(2)}, u32[]{:S(2)}) collective-permute-start(f32[32,128]{1,0:T(8,128)S(1)} %get-tuple-element.61.field.scaled), channel_id=1, source_target_pairs={{0,1},{1,0},{2,3},{3,2},{4,5},{5,4},{6,7},{7,6},{8,9},{9,8},{10,11... | collective-permute-start | bytes 49160 | tf_op jit(solution)/shard_map/ppermute | solution.py:754
  53.2 1.2 %collective-permute-start.12 = (f32[8,128]{1,0:T(8,128)S(1)}, f32[8,128]{1,0:T(8,128)S(1)}, u32[]{:S(2)}, u32[]{:S(2)}) collective-permute-start(f32[8,128]{1,0:T(8,128)S(1)} %get-tuple-element.65), channel_id=1, source_target_pairs={{0,4},{4,0},{8,12},{12,8},{16,20},{20,16},{24,28},{28,24},{1,5},{5... | collective-permute-start | bytes 12296 | tf_op jit(solution)/shard_map/ppermute | solution.py:675
  54.4 5.4 %collective-permute-start.15 = (f32[8,128]{1,0:T(8,128)S(1)}, f32[8,128]{1,0:T(8,128)S(1)}, u32[]{:S(2)}, u32[]{:S(2)}) collective-permute-start(f32[8,128]{1,0:T(8,128)S(1)} %add.12), channel_id=1, source_target_pairs={{0,3},{1,2},{2,1},{3,0},{4,7},{5,6},{6,5},{7,4},{8,11},{9,10},{10,... | collective-permute-start | bytes 12296 | tf_op jit(solution)/shard_map/ppermute | solution.py:675
  54.4 5.4 %collective-permute-start.14 = (f32[8,128]{1,0:T(8,128)S(1)}, f32[8,128]{1,0:T(8,128)S(1)}, u32[]{:S(2)}, u32[]{:S(2)}) collective-permute-start(f32[8,128]{1,0:T(8,128)S(1)} %add.12), channel_id=1, source_target_pairs={{0,2},{1,3},{2,0},{3,1},{4,6},{5,7},{6,4},{7,5},{8,10},{9,11},{10,... | collective-permute-start | bytes 12296 | tf_op jit(solution)/shard_map/ppermute | solution.py:675
  56.7 3.6 %collective-permute-start.13 = (f32[8,128]{1,0:T(8,128)S(1)}, f32[8,128]{1,0:T(8,128)S(1)}, u32[]{:S(2)}, u32[]{:S(2)}) collective-permute-start(f32[8,128]{1,0:T(8,128)S(1)} %add.12), channel_id=1, source_target_pairs={{0,1},{1,0},{2,3},{3,2},{4,5},{5,4},{6,7},{7,6},{8,9},{9,8},{10,11... | collective-permute-start | bytes 12296 | tf_op jit(solution)/shard_map/ppermute | solution.py:675
  60.3 4.5 %collective-permute-start.18 = (f32[8,128]{1,0:T(8,128)S(1)}, f32[8,128]{1,0:T(8,128)S(1)}, u32[]{:S(2)}, u32[]{:S(2)}) collective-permute-start(f32[8,128]{1,0:T(8,128)S(1)} %add_add_fusion.rest_0_), channel_id=1, source_target_pairs={{0,24},{4,28},{8,16},{12,20},{16,8},{20,12},{24,0},{28,4},{1,25},{... | collective-permute-start | bytes 12296 | tf_op jit(solution)/shard_map/ppermute | solution.py:675
  60.9 4.7 %collective-permute-start.17 = (f32[8,128]{1,0:T(8,128)S(1)}, f32[8,128]{1,0:T(8,128)S(1)}, u32[]{:S(2)}, u32[]{:S(2)}) collective-permute-start(f32[8,128]{1,0:T(8,128)S(1)} %add_add_fusion.rest_0_), channel_id=1, source_target_pairs={{0,16},{4,20},{8,24},{12,28},{16,0},{20,4},{24,8},{28,12},{1,17},{... | collective-permute-start | bytes 12296 | tf_op jit(solution)/shard_map/ppermute | solution.py:675
  64.0 3.6 %collective-permute-start.16 = (f32[8,128]{1,0:T(8,128)S(1)}, f32[8,128]{1,0:T(8,128)S(1)}, u32[]{:S(2)}, u32[]{:S(2)}) collective-permute-start(f32[8,128]{1,0:T(8,128)S(1)} %add_add_fusion.rest_0_), channel_id=1, source_target_pairs={{0,8},{4,12},{8,0},{12,4},{16,24},{20,28},{24,16},{28,20},{1,9},{5... | collective-permute-start | bytes 12296 | tf_op jit(solution)/shard_map/ppermute | solution.py:675

commit v18 on v17

--- a/solution.py
+++ b/solution.py
@@ -341,10 +341,10 @@
 
 
 def build_inner(
-    meta, table, near, plan, outer_runs, tiles, sides, middles, weights, rows_out, cols_out, self_ref,
-    inner_runs, rows_ref, cols_ref, *buffers,
+    meta, table, near, plan, outer_runs, tiles, sides, middles, weights, rows_ref, cols_ref, self_ref,
+    inner_runs, *buffers,
 ):
-    share, width = rows_out.shape[0], rows_out.shape[2]
+    share, width = weights.shape[:2]
     chunks = pieces_of(width)
     write_runs(meta, table, plan, inner_runs, outer_runs, share)
     for k in range(3):
@@ -378,8 +378,6 @@
         return at + 1
 
     lax.fori_loop(0, meta[0], block, 0)
-    rows_out[...] = rows_ref[0:share]
-    cols_out[...] = cols_ref[0 : share * SUB, :]
 
 
 def count_listed(meta, lists, width):
@@ -448,7 +446,7 @@
         lambda k, n: hood[k, pl.ds(base + share + n, 1), :], buffers, tiles, work, None,
     )
     finish_tiles(tiles, count)
-    sums_ref[...] = lane_sums([rows_ref[a] + work[a] for a in range(share)], share, width) + sub_sums(cols_ref)
+    sums_ref[...] = lane_sums([rows_ref[a] + work[a] for a in range(share)], share, width) + sub_sums(cols_ref)[0:share]
 
     @pl.when(again)
     def _():
@@ -610,7 +608,7 @@
     for k, (first, second) in enumerate(pairs):
         along = jnp.sum(first * second, axis=0, keepdims=True)
         sums = jnp.where(lane == k, jnp.sum(along, axis=1, keepdims=True), sums)
-    sums_ref[...] = wide(sums)
+    sums_ref[...] = sums
 
 
 def finish(source, precond, spill, scaled, twice, *rest):
@@ -647,13 +645,14 @@
     share = capacity // columns
     f32 = jnp.float32
     vector = jax.ShapeDtypeStruct((share, width), f32)
-    few = jax.ShapeDtypeStruct((SUB, width), f32)
+    few = jax.ShapeDtypeStruct((1, width), f32)
     message = jax.ShapeDtypeStruct((4, share, width), f32)
     most_inner, most_outer = tile_bounds(share)
     inner_tiles = pltpu.VMEM((most_inner + 2 * GROUP, width, width), f32)
     outer_tiles = pltpu.VMEM((most_outer + 2 * GROUP, width, width), f32)
     ahead = pltpu.VMEM((GROUP, width, width), f32)
     square_more = pltpu.VMEM((share + 1, width, width), f32)
+    narrow_more = pltpu.VMEM(((share + 1) * SUB, width), f32)
     square = pltpu.VMEM((share, width, width), f32)
     narrow = pltpu.VMEM((share * SUB, width), f32)
     table = jnp.asarray(FLAT)
@@ -706,8 +705,9 @@
         build_inner,
         (meta, table, near),
         [pltpu.SMEM((share * FIELDS + 4,), jnp.int32), pltpu.SMEM((6 * share + 3,), jnp.int32), inner_tiles,
-         pltpu.VMEM((2, share, width, width), jnp.bfloat16), pltpu.VMEM((3, share, width), f32), square, square, narrow, narrow],
-        [pltpu.SMEM((3 * share + 3,), jnp.int32), square_more, pltpu.VMEM(((share + 1) * SUB, width), f32), ahead, ahead],
+         pltpu.VMEM((2, share, width, width), jnp.bfloat16), pltpu.VMEM((3, share, width), f32), square,
+         square_more, narrow_more, narrow],
+        [pltpu.SMEM((3 * share + 3,), jnp.int32), ahead, ahead],
         16 * most_inner,
     )
     plan, runs = (pltpu.with_memory_space_constraint(array, pltpu.SMEM) for array in (plan, runs))
@@ -751,12 +751,14 @@
                         ring += spare.get(d, []) if p == (0 if spare.get(d) == [0] else pieces - 2) else []
                         to.update(zip(ring, ring[1:] + ring[:1]))
             swaps.append([to[i] for i in range(count)])
-        return [lax.ppermute(field, axes, list(enumerate(to))) for to in swaps]
+        received = [lax.ppermute(field, axes, list(enumerate(to))) for to in swaps[1:]]
+        rows, cols = inner(field)
+        late, cols = lax.optimization_barrier((field, cols))
+        return [lax.ppermute(late, axes, list(enumerate(swaps[0]))), *received], rows, cols
 
     scratch = [pltpu.VMEM((share, width, width), f32), pltpu.VMEM((8 * share, width), f32)]
 
-    received = exchange(precond)
-    rows, cols = inner(precond)
+    received, rows, cols = exchange(precond)
     spill, scaled = call(
         apply_first,
         (meta, table, plan, again, diagonal, times, *received, held(tiles_out), held(rows), held(cols)),
@@ -766,8 +768,7 @@
         scalars=4,
     )
 
-    received = exchange(scaled)
-    rows, cols = inner(scaled)
+    received, rows, cols = exchange(scaled)
     twice, sums = call(
         apply_second,
         (meta, table, plan, again, source, precond, spill, scaled, times, *received, held(tiles_out), held(rows), held(cols)),

time: 68.7 us -> 74.1 us (1.079)
  waiting for transfers between devices: 7.65 us -> 14.1 us
  starting transfers between devices: 29.1 us -> 28.1 us
    ppermute x8, waiting for transfers between devices: 0.02 us -> 7.82 us  [the longest x6 5.95 us: exchange(): lax.ppermute(field, axes, list(enumerate(to)))]
    ppermute x9, waiting for transfers between devices: 7.62 us -> 6.32 us  [swap(): lax.ppermute(values, axis, [(i, i ^ step) for i in range(lax.axis_size(ax...]
    ppermute x8, starting transfers between devices: 13.5 us -> 12.6 us  [the longest x6 7.49 us: exchange(): lax.ppermute(field, axes, list(enumerate(to)))]
  transfers between devices with their start and end apart: 19 -> 19, of which waited for: 7 -> 12; matrix products, arithmetic and copies ran while one was open for 0% -> 0% of each run, Pallas kernels for 28% -> 20%
where the time goes in v18:
time: 74.1 us; the launch traced here: 73.9 us
  Pallas kernels  31 us (42%)
  starting transfers between devices  28.1 us (38%)
  waiting for transfers between devices  14.1 us (19%)
    pallas_call x8, Pallas kernels, call(): pl.pallas_call(kernel, out_shape=outs, in_specs=[SMEM] * scalars + [HBM]...  31 us
    ppermute x9, starting transfers between devices, swap(): lax.ppermute(values, axis, [(i, i ^ step) for i in range(lax.axis_size(ax...  15.3 us
    ppermute x6, starting transfers between devices, exchange(): lax.ppermute(field, axes, list(enumerate(to)))  7.49 us
    ppermute x9, waiting for transfers between devices, swap(): lax.ppermute(values, axis, [(i, i ^ step) for i in range(lax.axis_size(ax...  6.32 us
    ppermute x6, waiting for transfers between devices, exchange(): lax.ppermute(field, axes, list(enumerate(to)))  5.95 us
    ppermute x2, starting transfers between devices, exchange(): lax.ppermute(late, axes, list(enumerate(swaps[0])))  5.12 us
    ppermute x2, waiting for transfers between devices, exchange(): lax.ppermute(late, axes, list(enumerate(swaps[0])))  1.87 us
  transfers between devices with their start and end apart: 19, of which 12 were waited for; matrix products, arithmetic and copies ran while one was open for 0% of the time, Pallas kernels for 20%

profile of v18, /device:TPU:0, one launch (start us, length us, event | category | flops | bytes accessed | tf_op | source)
XLA Modules:
  0.0 73.9 jit_solution(15882594720761371578)
XLA Ops:
  0.6 1.7 %prepare.1 = (s32[8]{0:T(128)S(4)}, s32[1480]{0:T(1024)S(4)}, f32[4,192,128]{2,1,0:T(8,128)S(1)}, f32[4,64,128]{2,1,0:T(8,128)S(1)}, f32[32,128]{1,0:T(8,128)S(1...) custom-call(s32[8]{0:T(128)} %counts.1, f32[3]{0:T(128)} %densities.1, ...), custom_call_target="tpu_custom_call" | custom-call | tf_op jit(solution)/shard_map/prepare/pallas_call | solution.py:661
  2.4 3.1 %collective-permute-start.2 = (s32[7,128]{1,0:T(8,128)S(1)}, s32[7,128]{1,0:T(8,128)S(1)}, u32[]{:S(2)}, u32[]{:S(2)}) collective-permute-start(s32[7,128]{1,0:T(8,128)S(1)} %get-tuple-element.55), channel_id=1, source_target_pairs={{0,1},{1,0},{2,3},{3,2},{4,5},{5,4},{6,7},{7,6},{8,9},{9,8},{10,11... | collective-permute-start | bytes 10760 | tf_op jit(solution)/shard_map/ppermute | solution.py:674
  5.5 0.0 collective-permute-start
  5.5 0.2 collective-permute-start.1
  5.6 1.4 %collective-permute-done.2 = s32[7,128]{1,0:T(8,128)S(1)} collective-permute-done((s32[7,128]{1,0:T(8,128)S(1)}, s32[7,128]{1,0:T(8,128)S(1)}, u32[]{:S(2)}, u32[]{:S(2)}) %collective-permute-start.2) | collective-permute-done | bytes 3616 | tf_op jit(solution)/shard_map/ppermute | solution.py:674
  7.0 4.0 %collective-permute-start.3 = (s32[14,128]{1,0:T(8,128)S(1)}, s32[14,128]{1,0:T(8,128)S(1)}, u32[]{:S(2)}, u32[]{:S(2)}) collective-permute-start(s32[14,128]{1,0:T(8,128)S(1)} %pad_add_fusion.rest_0_), channel_id=1, source_target_pairs={{0,3},{1,2},{2,1},{3,0},{4,7},{5,6},{6,5},{7,4},{8,11},{9,10},{10,... | collective-permute-start | bytes 21512 | tf_op jit(solution)/shard_map/ppermute | solution.py:674
  11.1 10.7 %build_inner.1 = (s32[196]{0:T(256)S(4)}, s32[195]{0:T(256)S(4)}, f32[224,128,128]{2,1,0:T(8,128)S(1)}, bf16[2,32,128,128]{3,2,1,0:T(8,128)(2,1)S(1)}, f32[3,32,...) custom-call(s32[8]{0:T(128)S(4)} %get-tuple-element.39.meta, ...), custom_call_target="tpu_custom_call" | custom-call | flops 56623104 | tf_op jit(solution)/shard_map/build_inner/pallas_call | solution.py:661
  21.8 0.0 collective-permute-done.3.rest_1_
  21.8 0.0 collective-permute-done.first
  21.8 0.0 collective-permute-done.1.second
  21.8 4.6 %build_outer.1 = (s32[1]{0:T(128)S(4)}, f32[230,128,128]{2,1,0:T(8,128)S(1)}, f32[32,128]{1,0:T(8,128)S(1)}, f32[32,128]{1,0:T(8,128)S(1)}, f32[32,128]{1,0:T(8,128)S(1)}, /*index=5*/f32[32,128]{1,0:T(8,128)S(1)}) custom-call(s32[8]{0:T(128)S(4)} %get-tuple-element.39.meta, s32[1480]{0:T(1024)S(4)} %get-tuple-element.40.table, ...), custom_call_target="tpu_custom_call" | custom-call | flops 58195968 | tf_op jit(solution)/shard_map/build_outer/pallas_call | solution.py:661
  26.5 0.1 collective-permute-start.7
  26.5 4.6 %collective-permute-start.6 = (f32[32,128]{1,0:T(8,128)S(1)}, f32[32,128]{1,0:T(8,128)S(1)}, u32[]{:S(2)}, u32[]{:S(2)}) collective-permute-start(f32[32,128]{1,0:T(8,128)S(1)} %get-tuple-element.62.field.precond), channel_id=1, source_target_pairs={{0,2},{1,4},{2,6},{3,7},{4,1},{5,8},{6,0},{7,3},{8,5},{9,12},{10,1... | collective-permute-start | bytes 49160 | tf_op jit(solution)/shard_map/ppermute | solution.py:754
  31.1 1.2 %collective-permute-start.5 = (f32[32,128]{1,0:T(8,128)S(1)}, f32[32,128]{1,0:T(8,128)S(1)}, u32[]{:S(2)}, u32[]{:S(2)}) collective-permute-start(f32[32,128]{1,0:T(8,128)S(1)} %get-tuple-element.62.field.precond), channel_id=1, source_target_pairs={{0,31},{1,2},{2,1},{3,4},{4,3},{5,6},{6,5},{7,8},{8,7},{9,10},{10,... | collective-permute-start | bytes 49160 | tf_op jit(solution)/shard_map/ppermute | solution.py:754
  32.4 4.3 %apply_inner.2 = (f32[32,128,128]{2,1,0:T(8,128)S(1)}, f32[256,128]{1,0:T(8,128)S(1)}) custom-call(s32[8]{0:T(128)S(4)} %get-tuple-element.39.meta, s32[1480]{0:T(1024)S(4)} %get-tuple-element.40.table, s32[196]{0:T(256)S(4)} %get-tuple-element.42.plan, s32[1]{0:T(128)S(4)} %get-tuple-element.57.again, f32[32,128]{1,0:T(8,128)S(1)} %get-tuple-element.62.field.precond, ...), custom_call_target="tpu_custom_call" | custom-call | flops 14155776 | tf_op jit(solution)/shard_map/apply_inner/pallas_call | solution.py:661
  36.7 2.4 %collective-permute-start.4 = (f32[32,128]{1,0:T(8,128)S(1)}, f32[32,128]{1,0:T(8,128)S(1)}, u32[]{:S(2)}, u32[]{:S(2)}) collective-permute-start(f32[32,128]{1,0:T(8,128)S(1)} %get-tuple-element.62.field.precond), channel_id=1, source_target_pairs={{0,1},{1,0},{2,3},{3,2},{4,5},{5,4},{6,7},{7,6},{8,9},{9,8},{10,11... | collective-permute-start | bytes 49160 | tf_op jit(solution)/shard_map/ppermute | solution.py:757
  39.1 0.0 collective-permute-done.7.rest_3_
  39.1 0.0 collective-permute-done.6.rest_2_
  39.1 0.0 collective-permute-done.5.rest_1_
  39.1 1.7 %collective-permute-done.4.rest_0_ = f32[32,128]{1,0:T(8,128)S(1)} collective-permute-done((f32[32,128]{1,0:T(8,128)S(1)}, f32[32,128]{1,0:T(8,128)S(1)}, u32[]{:S(2)}, u32[]{:S(2)}) %collective-permute-start.4) | collective-permute-done | bytes 16416 | tf_op jit(solution)/shard_map/ppermute | solution.py:757
  40.8 2.2 %apply_first.1 = (f32[32,128]{1,0:T(8,128)S(1)}, f32[32,128]{1,0:T(8,128)S(1)}) custom-call(s32[8]{0:T(128)S(4)} %get-tuple-element.39.meta, s32[1480]{0:T(1024)S(4)} %get-tuple-element.40.table, s32[196]{0:T(256)S(4)} %get-tuple-element.42.plan, s32[1]{0:T(128)S(4)} %get-tuple-element.57.again, f32[32,128]{1,0:T(8,128)S(1)} %get-tuple-element.58.diagonal, ...), custom_call_target="tpu_custom_call" | custom-call | flops 7274496 | tf_op jit(solution)/shard_map/apply_first/pallas_call | solution.py:661
  42.9 4.3 %apply_inner.3 = (f32[32,128,128]{2,1,0:T(8,128)S(1)}, f32[256,128]{1,0:T(8,128)S(1)}) custom-call(s32[8]{0:T(128)S(4)} %get-tuple-element.39.meta, s32[1480]{0:T(1024)S(4)} %get-tuple-element.40.table, s32[196]{0:T(256)S(4)} %get-tuple-element.42.plan, s32[1]{0:T(128)S(4)} %get-tuple-element.57.again, f32[32,128]{1,0:T(8,128)S(1)} %get-tuple-element.69.field.scaled, ...), custom_call_target="tpu_custom_call" | custom-call | flops 14155776 | tf_op jit(solution)/shard_map/apply_inner/pallas_call | solution.py:661
  47.3 2.7 %collective-permute-start.8 = (f32[32,128]{1,0:T(8,128)S(1)}, f32[32,128]{1,0:T(8,128)S(1)}, u32[]{:S(2)}, u32[]{:S(2)}) collective-permute-start(f32[32,128]{1,0:T(8,128)S(1)} %get-tuple-element.69.field.scaled), channel_id=1, source_target_pairs={{0,1},{1,0},{2,3},{3,2},{4,5},{5,4},{6,7},{7,6},{8,9},{9,8},{10,11... | collective-permute-start | bytes 49160 | tf_op jit(solution)/shard_map/ppermute | solution.py:757
  50.0 0.9 %collective-permute-start.11 = (f32[32,128]{1,0:T(8,128)S(1)}, f32[32,128]{1,0:T(8,128)S(1)}, u32[]{:S(2)}, u32[]{:S(2)}) collective-permute-start(f32[32,128]{1,0:T(8,128)S(1)} %get-tuple-element.69.field.scaled), channel_id=1, source_target_pairs={{0,3},{1,5},{2,4},{3,7},{4,2},{5,1},{6,8},{7,0},{8,6},{9,13},{10,1... | collective-permute-start | bytes 49160 | tf_op jit(solution)/shard_map/ppermute | solution.py:754
  50.9 0.0 collective-permute-start.10
  50.9 0.7 collective-permute-start.9
  51.6 0.2 collective-permute-done.8.rest_0_
  51.7 3.3 %collective-permute-done.11.rest_3_ = f32[32,128]{1,0:T(8,128)S(1)} collective-permute-done((f32[32,128]{1,0:T(8,128)S(1)}, f32[32,128]{1,0:T(8,128)S(1)}, u32[]{:S(2)}, u32[]{:S(2)}) %collective-permute-start.11) | collective-permute-done | bytes 16416 | tf_op jit(solution)/shard_map/ppermute | solution.py:754
  55.1 0.2 collective-permute-done.10.rest_2_
  55.3 2.4 %collective-permute-done.9.rest_1_ = f32[32,128]{1,0:T(8,128)S(1)} collective-permute-done((f32[32,128]{1,0:T(8,128)S(1)}, f32[32,128]{1,0:T(8,128)S(1)}, u32[]{:S(2)}, u32[]{:S(2)}) %collective-permute-start.9) | collective-permute-done | bytes 16416 | tf_op jit(solution)/shard_map/ppermute | solution.py:754
  57.7 2.2 %apply_second.1 = (f32[32,128]{1,0:T(8,128)S(1)}, f32[1,128]{1,0:T(1,128)S(1)}) custom-call(s32[8]{0:T(128)S(4)} %get-tuple-element.39.meta, s32[1480]{0:T(1024)S(4)} %get-tuple-element.40.table, s32[196]{0:T(256)S(4)} %get-tuple-element.42.plan, s32[1]{0:T(128)S(4)} %get-tuple-element.57.again, f32[32,128]{1,0:T(8,128)S(1)} %get-tuple-element.38.source, ...), custom_call_target="tpu_custom_call" | custom-call | flops 7274496 | tf_op jit(solution)/shard_map/apply_second/pallas_call | solution.py:661
  59.9 0.0 collective-permute-start.12
  59.9 1.1 %collective-permute-done.12 = f32[1,128]{1,0:T(1,128)S(1)} collective-permute-done((f32[1,128]{1,0:T(1,128)S(1)}, f32[1,128]{1,0:T(1,128)S(1)}, u32[]{:S(2)}, u32[]{:S(2)}) %collective-permute-start.12) | collective-permute-done | bytes 544 | tf_op jit(solution)/shard_map/ppermute | solution.py:674
  61.0 1.6 %collective-permute-start.15 = (f32[1,128]{1,0:T(1,128)S(1)}, f32[1,128]{1,0:T(1,128)S(1)}, u32[]{:S(2)}, u32[]{:S(2)}) collective-permute-start(f32[1,128]{1,0:T(1,128)S(1)} %add.12), channel_id=1, source_target_pairs={{0,3},{1,2},{2,1},{3,0},{4,7},{5,6},{6,5},{7,4},{8,11},{9,10},{10,... | collective-permute-start | bytes 1544 | tf_op jit(solution)/shard_map/ppermute | solution.py:674
  62.6 0.0 collective-permute-start.14
  62.6 2.8 %collective-permute-start.13 = (f32[1,128]{1,0:T(1,128)S(1)}, f32[1,128]{1,0:T(1,128)S(1)}, u32[]{:S(2)}, u32[]{:S(2)}) collective-permute-start(f32[1,128]{1,0:T(1,128)S(1)} %add.12), channel_id=1, source_target_pairs={{0,1},{1,0},{2,3},{3,2},{4,5},{5,4},{6,7},{7,6},{8,9},{9,8},{10,11... | collective-permute-start | bytes 1544 | tf_op jit(solution)/shard_map/ppermute | solution.py:674
  65.4 0.9 %collective-permute-done.15 = f32[1,128]{1,0:T(1,128)S(1)} collective-permute-done((f32[1,128]{1,0:T(1,128)S(1)}, f32[1,128]{1,0:T(1,128)S(1)}, u32[]{:S(2)}, u32[]{:S(2)}) %collective-permute-start.15) | collective-permute-done | bytes 544 | tf_op jit(solution)/shard_map/ppermute | solution.py:674
  66.4 0.7 collective-permute-done.14
  67.1 0.0 collective-permute-done.13
  67.1 1.7 %collective-permute-start.18 = (f32[1,128]{1,0:T(1,128)S(1)}, f32[1,128]{1,0:T(1,128)S(1)}, u32[]{:S(2)}, u32[]{:S(2)}) collective-permute-start(f32[1,128]{1,0:T(1,128)S(1)} %add_add_fusion.rest_0_), channel_id=1, source_target_pairs={{0,24},{4,28},{8,16},{12,20},{16,8},{20,12},{24,0},{28,4},{1,25},{... | collective-permute-start | bytes 1544 | tf_op jit(solution)/shard_map/ppermute | solution.py:674
  68.7 0.7 %collective-permute-start.17 = (f32[1,128]{1,0:T(1,128)S(1)}, f32[1,128]{1,0:T(1,128)S(1)}, u32[]{:S(2)}, u32[]{:S(2)}) collective-permute-start(f32[1,128]{1,0:T(1,128)S(1)} %add_add_fusion.rest_0_), channel_id=1, source_target_pairs={{0,16},{4,20},{8,24},{12,28},{16,0},{20,4},{24,8},{28,12},{1,17},{... | collective-permute-start | bytes 1544 | tf_op jit(solution)/shard_map/ppermute | solution.py:674
  69.5 1.4 %collective-permute-start.16 = (f32[1,128]{1,0:T(1,128)S(1)}, f32[1,128]{1,0:T(1,128)S(1)}, u32[]{:S(2)}, u32[]{:S(2)}) collective-permute-start(f32[1,128]{1,0:T(1,128)S(1)} %add_add_fusion.rest_0_), channel_id=1, source_target_pairs={{0,8},{4,12},{8,0},{12,4},{16,24},{20,28},{24,16},{28,20},{1,9},{5... | collective-permute-start | bytes 1544 | tf_op jit(solution)/shard_map/ppermute | solution.py:674
  70.9 0.7 collective-permute-done.18.rest_3_
  71.6 0.7 collective-permute-done.17.rest_2_
  72.3 0.7 %collective-permute-done.16.rest_1_ = f32[1,128]{1,0:T(1,128)S(1)} collective-permute-done((f32[1,128]{1,0:T(1,128)S(1)}, f32[1,128]{1,0:T(1,128)S(1)}, u32[]{:S(2)}, u32[]{:S(2)}) %collective-permute-start.16) | collective-permute-done | bytes 544 | tf_op jit(solution)/shard_map/ppermute | solution.py:674
  73.0 0.9 %finish.1 = (f32[32,128]{1,0:T(8,128)}, f32[32,128]{1,0:T(8,128)}) custom-call(f32[32,128]{1,0:T(8,128)S(1)} %get-tuple-element.38.source, f32[32,128]{1,0:T(8,128)S(1)} %get-tuple-element.62.field.precond, f32[32,128]{1,0:T(8,128)S(1)} %get-tuple-element.66.spill, f32[32,128]{1,0:T(8,128)S(1)} %get-tuple-element.69.field.scaled, ...), custom_call_target="tpu_custom_call" | custom-call | tf_op jit(solution)/shard_map/finish/pallas_call | solution.py:661
  (3 shorter events, 0.0 us)
Async XLA Ops:
  2.4 4.7 %collective-permute-start.2 = (s32[7,128]{1,0:T(8,128)S(1)}, s32[7,128]{1,0:T(8,128)S(1)}, u32[]{:S(2)}, u32[]{:S(2)}) collective-permute-start(s32[7,128]{1,0:T(8,128)S(1)} %get-tuple-element.55), channel_id=1, source_target_pairs={{0,1},{1,0},{2,3},{3,2},{4,5},{5,4},{6,7},{7,6},{8,9},{9,8},{10,11... | collective-permute-start | bytes 10760 | tf_op jit(solution)/shard_map/ppermute | solution.py:674
  5.5 16.4 %collective-permute-start = (f32[4,32,128]{2,1,0:T(8,128)S(1)}, f32[4,32,128]{2,1,0:T(8,128)S(1)}, u32[]{:S(2)}, u32[]{:S(2)}) collective-permute-start(f32[4,32,128]{2,1,0:T(8,128)S(1)} %get-tuple-element.45), channel_id=1, source_target_pairs={{0,4},{4,0},{8,12},{12,8},{16,20},{20,16},{24,28},{28,24},{1,5},{5... | collective-permute-start | bytes 196616 | tf_op jit(solution)/shard_map/ppermute | solution.py:691
  5.5 16.4 %collective-permute-start.1 = (f32[4,32,128]{2,1,0:T(8,128)S(1)}, f32[4,32,128]{2,1,0:T(8,128)S(1)}, u32[]{:S(2)}, u32[]{:S(2)}) collective-permute-start(f32[4,32,128]{2,1,0:T(8,128)S(1)} %get-tuple-element.46), channel_id=1, source_target_pairs={{0,1},{1,0},{2,3},{3,2},{4,8},{5,9},{6,10},{7,11},{8,4},{9,5},{10,... | collective-permute-start | bytes 196616 | tf_op jit(solution)/shard_map/ppermute | solution.py:696
  7.0 14.8 %collective-permute-start.3 = (s32[14,128]{1,0:T(8,128)S(1)}, s32[14,128]{1,0:T(8,128)S(1)}, u32[]{:S(2)}, u32[]{:S(2)}) collective-permute-start(s32[14,128]{1,0:T(8,128)S(1)} %pad_add_fusion.rest_0_), channel_id=1, source_target_pairs={{0,3},{1,2},{2,1},{3,0},{4,7},{5,6},{6,5},{7,4},{8,11},{9,10},{10,... | collective-permute-start | bytes 21512 | tf_op jit(solution)/shard_map/ppermute | solution.py:674
  26.5 12.6 %collective-permute-start.7 = (f32[32,128]{1,0:T(8,128)S(1)}, f32[32,128]{1,0:T(8,128)S(1)}, u32[]{:S(2)}, u32[]{:S(2)}) collective-permute-start(f32[32,128]{1,0:T(8,128)S(1)} %get-tuple-element.62.field.precond), channel_id=1, source_target_pairs={{0,3},{1,5},{2,4},{3,7},{4,2},{5,1},{6,8},{7,0},{8,6},{9,13},{10,1... | collective-permute-start | bytes 49160 | tf_op jit(solution)/shard_map/ppermute | solution.py:754
  26.5 12.6 %collective-permute-start.6 = (f32[32,128]{1,0:T(8,128)S(1)}, f32[32,128]{1,0:T(8,128)S(1)}, u32[]{:S(2)}, u32[]{:S(2)}) collective-permute-start(f32[32,128]{1,0:T(8,128)S(1)} %get-tuple-element.62.field.precond), channel_id=1, source_target_pairs={{0,2},{1,4},{2,6},{3,7},{4,1},{5,8},{6,0},{7,3},{8,5},{9,12},{10,1... | collective-permute-start | bytes 49160 | tf_op jit(solution)/shard_map/ppermute | solution.py:754
  31.1 7.9 %collective-permute-start.5 = (f32[32,128]{1,0:T(8,128)S(1)}, f32[32,128]{1,0:T(8,128)S(1)}, u32[]{:S(2)}, u32[]{:S(2)}) collective-permute-start(f32[32,128]{1,0:T(8,128)S(1)} %get-tuple-element.62.field.precond), channel_id=1, source_target_pairs={{0,31},{1,2},{2,1},{3,4},{4,3},{5,6},{6,5},{7,8},{8,7},{9,10},{10,... | collective-permute-start | bytes 49160 | tf_op jit(solution)/shard_map/ppermute | solution.py:754
  36.7 4.1 %collective-permute-start.4 = (f32[32,128]{1,0:T(8,128)S(1)}, f32[32,128]{1,0:T(8,128)S(1)}, u32[]{:S(2)}, u32[]{:S(2)}) collective-permute-start(f32[32,128]{1,0:T(8,128)S(1)} %get-tuple-element.62.field.precond), channel_id=1, source_target_pairs={{0,1},{1,0},{2,3},{3,2},{4,5},{5,4},{6,7},{7,6},{8,9},{9,8},{10,11... | collective-permute-start | bytes 49160 | tf_op jit(solution)/shard_map/ppermute | solution.py:757
  47.3 4.5 %collective-permute-start.8 = (f32[32,128]{1,0:T(8,128)S(1)}, f32[32,128]{1,0:T(8,128)S(1)}, u32[]{:S(2)}, u32[]{:S(2)}) collective-permute-start(f32[32,128]{1,0:T(8,128)S(1)} %get-tuple-element.69.field.scaled), channel_id=1, source_target_pairs={{0,1},{1,0},{2,3},{3,2},{4,5},{5,4},{6,7},{7,6},{8,9},{9,8},{10,11... | collective-permute-start | bytes 49160 | tf_op jit(solution)/shard_map/ppermute | solution.py:757
  50.0 5.1 %collective-permute-start.11 = (f32[32,128]{1,0:T(8,128)S(1)}, f32[32,128]{1,0:T(8,128)S(1)}, u32[]{:S(2)}, u32[]{:S(2)}) collective-permute-start(f32[32,128]{1,0:T(8,128)S(1)} %get-tuple-element.69.field.scaled), channel_id=1, source_target_pairs={{0,3},{1,5},{2,4},{3,7},{4,2},{5,1},{6,8},{7,0},{8,6},{9,13},{10,1... | collective-permute-start | bytes 49160 | tf_op jit(solution)/shard_map/ppermute | solution.py:754
  50.9 4.4 %collective-permute-start.10 = (f32[32,128]{1,0:T(8,128)S(1)}, f32[32,128]{1,0:T(8,128)S(1)}, u32[]{:S(2)}, u32[]{:S(2)}) collective-permute-start(f32[32,128]{1,0:T(8,128)S(1)} %get-tuple-element.69.field.scaled), channel_id=1, source_target_pairs={{0,2},{1,4},{2,6},{3,7},{4,1},{5,8},{6,0},{7,3},{8,5},{9,12},{10,1... | collective-permute-start | bytes 49160 | tf_op jit(solution)/shard_map/ppermute | solution.py:754
  50.9 6.8 %collective-permute-start.9 = (f32[32,128]{1,0:T(8,128)S(1)}, f32[32,128]{1,0:T(8,128)S(1)}, u32[]{:S(2)}, u32[]{:S(2)}) collective-permute-start(f32[32,128]{1,0:T(8,128)S(1)} %get-tuple-element.69.field.scaled), channel_id=1, source_target_pairs={{0,31},{1,2},{2,1},{3,4},{4,3},{5,6},{6,5},{7,8},{8,7},{9,10},{10,... | collective-permute-start | bytes 49160 | tf_op jit(solution)/shard_map/ppermute | solution.py:754
  59.9 1.1 %collective-permute-start.12 = (f32[1,128]{1,0:T(1,128)S(1)}, f32[1,128]{1,0:T(1,128)S(1)}, u32[]{:S(2)}, u32[]{:S(2)}) collective-permute-start(f32[1,128]{1,0:T(1,128)S(1)} %get-tuple-element.73), channel_id=1, source_target_pairs={{0,4},{4,0},{8,12},{12,8},{16,20},{20,16},{24,28},{28,24},{1,5},{5... | collective-permute-start | bytes 1544 | tf_op jit(solution)/shard_map/ppermute | solution.py:674
  61.0 5.3 %collective-permute-start.15 = (f32[1,128]{1,0:T(1,128)S(1)}, f32[1,128]{1,0:T(1,128)S(1)}, u32[]{:S(2)}, u32[]{:S(2)}) collective-permute-start(f32[1,128]{1,0:T(1,128)S(1)} %add.12), channel_id=1, source_target_pairs={{0,3},{1,2},{2,1},{3,0},{4,7},{5,6},{6,5},{7,4},{8,11},{9,10},{10,... | collective-permute-start | bytes 1544 | tf_op jit(solution)/shard_map/ppermute | solution.py:674
  62.6 4.4 %collective-permute-start.14 = (f32[1,128]{1,0:T(1,128)S(1)}, f32[1,128]{1,0:T(1,128)S(1)}, u32[]{:S(2)}, u32[]{:S(2)}) collective-permute-start(f32[1,128]{1,0:T(1,128)S(1)} %add.12), channel_id=1, source_target_pairs={{0,2},{1,3},{2,0},{3,1},{4,6},{5,7},{6,4},{7,5},{8,10},{9,11},{10,... | collective-permute-start | bytes 1544 | tf_op jit(solution)/shard_map/ppermute | solution.py:674
  62.6 4.4 %collective-permute-start.13 = (f32[1,128]{1,0:T(1,128)S(1)}, f32[1,128]{1,0:T(1,128)S(1)}, u32[]{:S(2)}, u32[]{:S(2)}) collective-permute-start(f32[1,128]{1,0:T(1,128)S(1)} %add.12), channel_id=1, source_target_pairs={{0,1},{1,0},{2,3},{3,2},{4,5},{5,4},{6,7},{7,6},{8,9},{9,8},{10,11... | collective-permute-start | bytes 1544 | tf_op jit(solution)/shard_map/ppermute | solution.py:674
  67.1 4.5 %collective-permute-start.18 = (f32[1,128]{1,0:T(1,128)S(1)}, f32[1,128]{1,0:T(1,128)S(1)}, u32[]{:S(2)}, u32[]{:S(2)}) collective-permute-start(f32[1,128]{1,0:T(1,128)S(1)} %add_add_fusion.rest_0_), channel_id=1, source_target_pairs={{0,24},{4,28},{8,16},{12,20},{16,8},{20,12},{24,0},{28,4},{1,25},{... | collective-permute-start | bytes 1544 | tf_op jit(solution)/shard_map/ppermute | solution.py:674
  68.7 3.5 %collective-permute-start.17 = (f32[1,128]{1,0:T(1,128)S(1)}, f32[1,128]{1,0:T(1,128)S(1)}, u32[]{:S(2)}, u32[]{:S(2)}) collective-permute-start(f32[1,128]{1,0:T(1,128)S(1)} %add_add_fusion.rest_0_), channel_id=1, source_target_pairs={{0,16},{4,20},{8,24},{12,28},{16,0},{20,4},{24,8},{28,12},{1,17},{... | collective-permute-start | bytes 1544 | tf_op jit(solution)/shard_map/ppermute | solution.py:674
  69.5 3.5 %collective-permute-start.16 = (f32[1,128]{1,0:T(1,128)S(1)}, f32[1,128]{1,0:T(1,128)S(1)}, u32[]{:S(2)}, u32[]{:S(2)}) collective-permute-start(f32[1,128]{1,0:T(1,128)S(1)} %add_add_fusion.rest_0_), channel_id=1, source_target_pairs={{0,8},{4,12},{8,0},{12,4},{16,24},{20,28},{24,16},{28,20},{1,9},{5... | collective-permute-start | bytes 1544 | tf_op jit(solution)/shard_map/ppermute | solution.py:674

commit v19 on v18

--- a/solution.py
+++ b/solution.py
@@ -178,10 +178,8 @@
     return 0.5 - (x[0] * x[0] + x[1] * x[1] + x[2] * x[2])
 
 
-def own_side(x, which):
-    nothing = [jnp.zeros_like(x[0])] * 4
-    rows = [2.0 * x[0], 2.0 * x[1], 2.0 * x[2], jnp.ones_like(x[0])]
-    high, middle, low = three_parts(stacked(nothing + rows if which else rows))
+def own_side(x):
+    high, middle, low = three_parts(stacked([2.0 * x[0], 2.0 * x[1], 2.0 * x[2], jnp.ones_like(x[0])]))
     sizes = stacked(list(three_parts(half_size(x))))
     width = sizes.shape[1]
     rest = jnp.zeros((width - 7 * SUB, width), jnp.float32)
@@ -199,7 +197,7 @@
     return jnp.concatenate([front, front, back, ones, rest], 0)
 
 
-GROUP = 4
+GROUP = 6
 
 
 def flat_tiles(count, runs, most, table, sides, middles, weights, other_at, buffers, tiles, rows_ref, cols_ref):
@@ -350,11 +348,13 @@
     for k in range(3):
         first = near[k, 0:share, 0:1]
         middles[k] = jnp.broadcast_to(jnp.floor(first) + 0.5, (share, width))
+    parts = lax.broadcasted_iota(jnp.int32, (width, width), 1) < 6 * SUB
     for a in range(share):
         here = slice(a, a + 1)
         centred = [wide(near[k, here, :] - middles[k, here, :]) for k in range(3)]
-        for which in range(2):
-            sides[which, a] = own_side(centred, which).T.astype(jnp.bfloat16)
+        turned = own_side(centred).T
+        sides[0, a] = turned.astype(jnp.bfloat16)
+        sides[1, a] = jnp.where(parts, pltpu.roll(turned, SUB // 2, 1), turned).astype(jnp.bfloat16)
     spread_columns(weights, lambda a: a, near[3, 0:share, :])
     cols_ref[...] = jnp.zeros_like(cols_ref)
     rows_ref[...] = jnp.zeros_like(rows_ref)
@@ -608,7 +608,7 @@
     for k, (first, second) in enumerate(pairs):
         along = jnp.sum(first * second, axis=0, keepdims=True)
         sums = jnp.where(lane == k, jnp.sum(along, axis=1, keepdims=True), sums)
-    sums_ref[...] = sums
+    sums_ref[...] = wide(sums)
 
 
 def finish(source, precond, spill, scaled, twice, *rest):
@@ -645,7 +645,7 @@
     share = capacity // columns
     f32 = jnp.float32
     vector = jax.ShapeDtypeStruct((share, width), f32)
-    few = jax.ShapeDtypeStruct((1, width), f32)
+    few = jax.ShapeDtypeStruct((SUB, width), f32)
     message = jax.ShapeDtypeStruct((4, share, width), f32)
     most_inner, most_outer = tile_bounds(share)
     inner_tiles = pltpu.VMEM((most_inner + 2 * GROUP, width, width), f32)
@@ -751,14 +751,12 @@
                         ring += spare.get(d, []) if p == (0 if spare.get(d) == [0] else pieces - 2) else []
                         to.update(zip(ring, ring[1:] + ring[:1]))
             swaps.append([to[i] for i in range(count)])
-        received = [lax.ppermute(field, axes, list(enumerate(to))) for to in swaps[1:]]
-        rows, cols = inner(field)
-        late, cols = lax.optimization_barrier((field, cols))
-        return [lax.ppermute(late, axes, list(enumerate(swaps[0]))), *received], rows, cols
+        return [lax.ppermute(field, axes, list(enumerate(to))) for to in swaps]
 
     scratch = [pltpu.VMEM((share, width, width), f32), pltpu.VMEM((8 * share, width), f32)]
 
-    received, rows, cols = exchange(precond)
+    received = exchange(precond)
+    rows, cols = inner(precond)
     spill, scaled = call(
         apply_first,
         (meta, table, plan, again, diagonal, times, *received, held(tiles_out), held(rows), held(cols)),
@@ -768,7 +766,8 @@
         scalars=4,
     )
 
-    received, rows, cols = exchange(scaled)
+    received = exchange(scaled)
+    rows, cols = inner(scaled)
     twice, sums = call(
         apply_second,
         (meta, table, plan, again, source, precond, spill, scaled, times, *received, held(tiles_out), held(rows), held(cols)),

time: 74.1 us -> 68.6 us (0.926)
  waiting for transfers between devices: 14.1 us -> 8.21 us
    ppermute x8, waiting for transfers between devices: 7.82 us -> 0.02 us  [exchange(): return [lax.ppermute(field, axes, list(enumerate(to))) for to in swaps]]
    ppermute x9, waiting for transfers between devices: 6.32 us -> 8.19 us  [swap(): lax.ppermute(values, axis, [(i, i ^ step) for i in range(lax.axis_size(ax...]
    ppermute x8, starting transfers between devices: 12.6 us -> 13.4 us  [exchange(): return [lax.ppermute(field, axes, list(enumerate(to))) for to in swaps]]
  transfers between devices with their start and end apart: 19 -> 19, of which waited for: 12 -> 8; matrix products, arithmetic and copies ran while one was open for 0% -> 0% of each run, Pallas kernels for 20% -> 28%
where the time goes in v19:
time: 68.6 us; the launch traced here: 68.2 us
  Pallas kernels  30.5 us (44%)
  starting transfers between devices  28.7 us (42%)
  waiting for transfers between devices  8.21 us (12%)
  between operations  0.79 us (1%)
    pallas_call x8, Pallas kernels, call(): pl.pallas_call(kernel, out_shape=outs, in_specs=[SMEM] * scalars + [HBM]...  30.5 us
    ppermute x9, starting transfers between devices, swap(): lax.ppermute(values, axis, [(i, i ^ step) for i in range(lax.axis_size(ax...  15.1 us
    ppermute x8, starting transfers between devices, exchange(): return [lax.ppermute(field, axes, list(enumerate(to))) for to in swaps]  13.4 us
    ppermute x9, waiting for transfers between devices, swap(): lax.ppermute(values, axis, [(i, i ^ step) for i in range(lax.axis_size(ax...  8.19 us
  transfers between devices with their start and end apart: 19, of which 8 were waited for; matrix products, arithmetic and copies ran while one was open for 0% of the time, Pallas kernels for 28%

profile of v19, /device:TPU:0, one launch (start us, length us, event | category | flops | bytes accessed | tf_op | source)
XLA Modules:
  0.0 68.2 jit_solution(15659758051810408121)
XLA Ops:
  0.6 1.7 %prepare.1 = (s32[8]{0:T(128)S(4)}, s32[1480]{0:T(1024)S(4)}, f32[4,192,128]{2,1,0:T(8,128)S(1)}, f32[4,64,128]{2,1,0:T(8,128)S(1)}, f32[32,128]{1,0:T(8,128)S(1...) custom-call(s32[8]{0:T(128)} %counts.1, f32[3]{0:T(128)} %densities.1, ...), custom_call_target="tpu_custom_call" | custom-call | tf_op jit(solution)/shard_map/prepare/pallas_call | solution.py:661
  2.4 3.1 %collective-permute-start.2 = (s32[7,128]{1,0:T(8,128)S(1)}, s32[7,128]{1,0:T(8,128)S(1)}, u32[]{:S(2)}, u32[]{:S(2)}) collective-permute-start(s32[7,128]{1,0:T(8,128)S(1)} %get-tuple-element.51), channel_id=1, source_target_pairs={{0,1},{1,0},{2,3},{3,2},{4,5},{5,4},{6,7},{7,6},{8,9},{9,8},{10,11... | collective-permute-start | bytes 10760 | tf_op jit(solution)/shard_map/ppermute | solution.py:674
  5.4 0.0 collective-permute-start
  5.4 0.2 collective-permute-start.1
  5.6 1.4 %collective-permute-done.2 = s32[7,128]{1,0:T(8,128)S(1)} collective-permute-done((s32[7,128]{1,0:T(8,128)S(1)}, s32[7,128]{1,0:T(8,128)S(1)}, u32[]{:S(2)}, u32[]{:S(2)}) %collective-permute-start.2) | collective-permute-done | bytes 3616 | tf_op jit(solution)/shard_map/ppermute | solution.py:674
  7.0 4.0 %collective-permute-start.3 = (s32[14,128]{1,0:T(8,128)S(1)}, s32[14,128]{1,0:T(8,128)S(1)}, u32[]{:S(2)}, u32[]{:S(2)}) collective-permute-start(s32[14,128]{1,0:T(8,128)S(1)} %pad_add_fusion.rest_0_), channel_id=1, source_target_pairs={{0,3},{1,2},{2,1},{3,0},{4,7},{5,6},{6,5},{7,4},{8,11},{9,10},{10,... | collective-permute-start | bytes 21512 | tf_op jit(solution)/shard_map/ppermute | solution.py:674
  11.1 10.5 %build_inner.1 = (s32[196]{0:T(256)S(4)}, s32[195]{0:T(256)S(4)}, f32[228,128,128]{2,1,0:T(8,128)S(1)}, bf16[2,32,128,128]{3,2,1,0:T(8,128)(2,1)S(1)}, f32[3,32,...) custom-call(s32[8]{0:T(128)S(4)} %get-tuple-element.35.meta, ...), custom_call_target="tpu_custom_call" | custom-call | flops 56623104 | tf_op jit(solution)/shard_map/build_inner/pallas_call | solution.py:661
  21.6 0.0 collective-permute-done.3.rest_1_
  21.6 0.0 collective-permute-done.first
  21.6 0.0 collective-permute-done.1.second
  21.6 4.4 %build_outer.1 = (s32[1]{0:T(128)S(4)}, f32[234,128,128]{2,1,0:T(8,128)S(1)}, f32[32,128]{1,0:T(8,128)S(1)}, f32[32,128]{1,0:T(8,128)S(1)}, f32[32,128]{1,0:T(8,128)S(1)}, /*index=5*/f32[32,128]{1,0:T(8,128)S(1)}) custom-call(s32[8]{0:T(128)S(4)} %get-tuple-element.35.meta, s32[1480]{0:T(1024)S(4)} %get-tuple-element.36.table, ...), custom_call_target="tpu_custom_call" | custom-call | flops 58195968 | tf_op jit(solution)/shard_map/build_outer/pallas_call | solution.py:661
  26.0 0.1 collective-permute-start.7
  26.0 4.1 %collective-permute-start.6 = (f32[32,128]{1,0:T(8,128)S(1)}, f32[32,128]{1,0:T(8,128)S(1)}, u32[]{:S(2)}, u32[]{:S(2)}) collective-permute-start(f32[32,128]{1,0:T(8,128)S(1)} %get-tuple-element.52.field.precond), channel_id=1, source_target_pairs={{0,2},{1,4},{2,6},{3,7},{4,1},{5,8},{6,0},{7,3},{8,5},{9,12},{10,1... | collective-permute-start | bytes 49160 | tf_op jit(solution)/shard_map/ppermute | solution.py:754
  30.2 0.7 %collective-permute-start.5 = (f32[32,128]{1,0:T(8,128)S(1)}, f32[32,128]{1,0:T(8,128)S(1)}, u32[]{:S(2)}, u32[]{:S(2)}) collective-permute-start(f32[32,128]{1,0:T(8,128)S(1)} %get-tuple-element.52.field.precond), channel_id=1, source_target_pairs={{0,31},{1,2},{2,1},{3,4},{4,3},{5,6},{6,5},{7,8},{8,7},{9,10},{10,... | collective-permute-start | bytes 49160 | tf_op jit(solution)/shard_map/ppermute | solution.py:754
  30.9 2.9 %collective-permute-start.4 = (f32[32,128]{1,0:T(8,128)S(1)}, f32[32,128]{1,0:T(8,128)S(1)}, u32[]{:S(2)}, u32[]{:S(2)}) collective-permute-start(f32[32,128]{1,0:T(8,128)S(1)} %get-tuple-element.52.field.precond), channel_id=1, source_target_pairs={{0,1},{1,0},{2,3},{3,2},{4,5},{5,4},{6,7},{7,6},{8,9},{9,8},{10,11... | collective-permute-start | bytes 49160 | tf_op jit(solution)/shard_map/ppermute | solution.py:754
  33.7 4.3 %apply_inner.2 = (f32[32,128,128]{2,1,0:T(8,128)S(1)}, f32[256,128]{1,0:T(8,128)S(1)}) custom-call(s32[8]{0:T(128)S(4)} %get-tuple-element.35.meta, s32[1480]{0:T(1024)S(4)} %get-tuple-element.36.table, s32[196]{0:T(256)S(4)} %get-tuple-element.38.plan, s32[1]{0:T(128)S(4)} %get-tuple-element.53.again, f32[32,128]{1,0:T(8,128)S(1)} %get-tuple-element.52.field.precond, ...), custom_call_target="tpu_custom_call" | custom-call | flops 14155776 | tf_op jit(solution)/shard_map/apply_inner/pallas_call | solution.py:661
  38.1 0.0 collective-permute-done.7.rest_3_
  38.1 0.0 collective-permute-done.6.rest_2_
  38.1 0.0 collective-permute-done.5.rest_1_
  38.1 0.0 collective-permute-done.4.rest_0_
  38.1 2.2 %apply_first.1 = (f32[32,128]{1,0:T(8,128)S(1)}, f32[32,128]{1,0:T(8,128)S(1)}) custom-call(s32[8]{0:T(128)S(4)} %get-tuple-element.35.meta, s32[1480]{0:T(1024)S(4)} %get-tuple-element.36.table, s32[196]{0:T(256)S(4)} %get-tuple-element.38.plan, s32[1]{0:T(128)S(4)} %get-tuple-element.53.again, f32[32,128]{1,0:T(8,128)S(1)} %get-tuple-element.54.diagonal, ...), custom_call_target="tpu_custom_call" | custom-call | flops 7274496 | tf_op jit(solution)/shard_map/apply_first/pallas_call | solution.py:661
  40.3 0.1 collective-permute-start.11
  40.3 2.6 %collective-permute-start.10 = (f32[32,128]{1,0:T(8,128)S(1)}, f32[32,128]{1,0:T(8,128)S(1)}, u32[]{:S(2)}, u32[]{:S(2)}) collective-permute-start(f32[32,128]{1,0:T(8,128)S(1)} %get-tuple-element.61.field.scaled), channel_id=1, source_target_pairs={{0,2},{1,4},{2,6},{3,7},{4,1},{5,8},{6,0},{7,3},{8,5},{9,12},{10,1... | collective-permute-start | bytes 49160 | tf_op jit(solution)/shard_map/ppermute | solution.py:754
  43.0 2.2 %collective-permute-start.9 = (f32[32,128]{1,0:T(8,128)S(1)}, f32[32,128]{1,0:T(8,128)S(1)}, u32[]{:S(2)}, u32[]{:S(2)}) collective-permute-start(f32[32,128]{1,0:T(8,128)S(1)} %get-tuple-element.61.field.scaled), channel_id=1, source_target_pairs={{0,31},{1,2},{2,1},{3,4},{4,3},{5,6},{6,5},{7,8},{8,7},{9,10},{10,... | collective-permute-start | bytes 49160 | tf_op jit(solution)/shard_map/ppermute | solution.py:754
  45.1 0.8 %collective-permute-start.8 = (f32[32,128]{1,0:T(8,128)S(1)}, f32[32,128]{1,0:T(8,128)S(1)}, u32[]{:S(2)}, u32[]{:S(2)}) collective-permute-start(f32[32,128]{1,0:T(8,128)S(1)} %get-tuple-element.61.field.scaled), channel_id=1, source_target_pairs={{0,1},{1,0},{2,3},{3,2},{4,5},{5,4},{6,7},{7,6},{8,9},{9,8},{10,11... | collective-permute-start | bytes 49160 | tf_op jit(solution)/shard_map/ppermute | solution.py:754
  45.9 4.3 %apply_inner.3 = (f32[32,128,128]{2,1,0:T(8,128)S(1)}, f32[256,128]{1,0:T(8,128)S(1)}) custom-call(s32[8]{0:T(128)S(4)} %get-tuple-element.35.meta, s32[1480]{0:T(1024)S(4)} %get-tuple-element.36.table, s32[196]{0:T(256)S(4)} %get-tuple-element.38.plan, s32[1]{0:T(128)S(4)} %get-tuple-element.53.again, f32[32,128]{1,0:T(8,128)S(1)} %get-tuple-element.61.field.scaled, ...), custom_call_target="tpu_custom_call" | custom-call | flops 14155776 | tf_op jit(solution)/shard_map/apply_inner/pallas_call | solution.py:661
  50.2 0.0 collective-permute-done.11.rest_3_
  50.2 0.0 collective-permute-done.10.rest_2_
  50.2 0.0 collective-permute-done.9.rest_1_
  50.2 0.0 collective-permute-done.8.rest_0_
  50.3 2.3 %apply_second.1 = (f32[32,128]{1,0:T(8,128)S(1)}, f32[8,128]{1,0:T(8,128)S(1)}) custom-call(s32[8]{0:T(128)S(4)} %get-tuple-element.35.meta, s32[1480]{0:T(1024)S(4)} %get-tuple-element.36.table, s32[196]{0:T(256)S(4)} %get-tuple-element.38.plan, s32[1]{0:T(128)S(4)} %get-tuple-element.53.again, f32[32,128]{1,0:T(8,128)S(1)} %get-tuple-element.34.source, ...), custom_call_target="tpu_custom_call" | custom-call | flops 7274496 | tf_op jit(solution)/shard_map/apply_second/pallas_call | solution.py:661
  52.5 0.1 collective-permute-start.12
  52.6 1.0 %collective-permute-done.12 = f32[8,128]{1,0:T(8,128)S(1)} collective-permute-done((f32[8,128]{1,0:T(8,128)S(1)}, f32[8,128]{1,0:T(8,128)S(1)}, u32[]{:S(2)}, u32[]{:S(2)}) %collective-permute-start.12) | collective-permute-done | bytes 4128 | tf_op jit(solution)/shard_map/ppermute | solution.py:674
  53.7 1.2 %collective-permute-start.15 = (f32[8,128]{1,0:T(8,128)S(1)}, f32[8,128]{1,0:T(8,128)S(1)}, u32[]{:S(2)}, u32[]{:S(2)}) collective-permute-start(f32[8,128]{1,0:T(8,128)S(1)} %add.12), channel_id=1, source_target_pairs={{0,3},{1,2},{2,1},{3,0},{4,7},{5,6},{6,5},{7,4},{8,11},{9,10},{10,... | collective-permute-start | bytes 12296 | tf_op jit(solution)/shard_map/ppermute | solution.py:674
  54.9 2.2 %collective-permute-start.14 = (f32[8,128]{1,0:T(8,128)S(1)}, f32[8,128]{1,0:T(8,128)S(1)}, u32[]{:S(2)}, u32[]{:S(2)}) collective-permute-start(f32[8,128]{1,0:T(8,128)S(1)} %add.12), channel_id=1, source_target_pairs={{0,2},{1,3},{2,0},{3,1},{4,6},{5,7},{6,4},{7,5},{8,10},{9,11},{10,... | collective-permute-start | bytes 12296 | tf_op jit(solution)/shard_map/ppermute | solution.py:674
  57.1 1.0 %collective-permute-start.13 = (f32[8,128]{1,0:T(8,128)S(1)}, f32[8,128]{1,0:T(8,128)S(1)}, u32[]{:S(2)}, u32[]{:S(2)}) collective-permute-start(f32[8,128]{1,0:T(8,128)S(1)} %add.12), channel_id=1, source_target_pairs={{0,1},{1,0},{2,3},{3,2},{4,5},{5,4},{6,7},{7,6},{8,9},{9,8},{10,11... | collective-permute-start | bytes 12296 | tf_op jit(solution)/shard_map/ppermute | solution.py:674
  58.1 1.0 %collective-permute-done.15 = f32[8,128]{1,0:T(8,128)S(1)} collective-permute-done((f32[8,128]{1,0:T(8,128)S(1)}, f32[8,128]{1,0:T(8,128)S(1)}, u32[]{:S(2)}, u32[]{:S(2)}) %collective-permute-start.15) | collective-permute-done | bytes 4128 | tf_op jit(solution)/shard_map/ppermute | solution.py:674
  59.1 0.3 collective-permute-done.14
  59.4 1.3 %collective-permute-done.13 = f32[8,128]{1,0:T(8,128)S(1)} collective-permute-done((f32[8,128]{1,0:T(8,128)S(1)}, f32[8,128]{1,0:T(8,128)S(1)}, u32[]{:S(2)}, u32[]{:S(2)}) %collective-permute-start.13) | collective-permute-done | bytes 4128 | tf_op jit(solution)/shard_map/ppermute | solution.py:674
  60.7 0.3 collective-permute-start.18
  61.0 2.7 %collective-permute-start.17 = (f32[8,128]{1,0:T(8,128)S(1)}, f32[8,128]{1,0:T(8,128)S(1)}, u32[]{:S(2)}, u32[]{:S(2)}) collective-permute-start(f32[8,128]{1,0:T(8,128)S(1)} %add_add_fusion.rest_0_), channel_id=1, source_target_pairs={{0,16},{4,20},{8,24},{12,28},{16,0},{20,4},{24,8},{28,12},{1,17},{... | collective-permute-start | bytes 12296 | tf_op jit(solution)/shard_map/ppermute | solution.py:674
  63.7 0.5 collective-permute-start.16
  64.2 1.0 %collective-permute-done.18.rest_3_ = f32[8,128]{1,0:T(8,128)S(1)} collective-permute-done((f32[8,128]{1,0:T(8,128)S(1)}, f32[8,128]{1,0:T(8,128)S(1)}, u32[]{:S(2)}, u32[]{:S(2)}) %collective-permute-start.18) | collective-permute-done | bytes 4128 | tf_op jit(solution)/shard_map/ppermute | solution.py:674
  65.2 0.1 collective-permute-done.17.rest_2_
  65.3 2.0 %collective-permute-done.16.rest_1_ = f32[8,128]{1,0:T(8,128)S(1)} collective-permute-done((f32[8,128]{1,0:T(8,128)S(1)}, f32[8,128]{1,0:T(8,128)S(1)}, u32[]{:S(2)}, u32[]{:S(2)}) %collective-permute-start.16) | collective-permute-done | bytes 4128 | tf_op jit(solution)/shard_map/ppermute | solution.py:674
  67.3 0.9 %finish.1 = (f32[32,128]{1,0:T(8,128)}, f32[32,128]{1,0:T(8,128)}) custom-call(f32[32,128]{1,0:T(8,128)S(1)} %get-tuple-element.34.source, f32[32,128]{1,0:T(8,128)S(1)} %get-tuple-element.52.field.precond, f32[32,128]{1,0:T(8,128)S(1)} %get-tuple-element.60.spill, f32[32,128]{1,0:T(8,128)S(1)} %get-tuple-element.61.field.scaled, ...), custom_call_target="tpu_custom_call" | custom-call | tf_op jit(solution)/shard_map/finish/pallas_call | solution.py:661
  (3 shorter events, 0.0 us)
Async XLA Ops:
  2.4 4.7 %collective-permute-start.2 = (s32[7,128]{1,0:T(8,128)S(1)}, s32[7,128]{1,0:T(8,128)S(1)}, u32[]{:S(2)}, u32[]{:S(2)}) collective-permute-start(s32[7,128]{1,0:T(8,128)S(1)} %get-tuple-element.51), channel_id=1, source_target_pairs={{0,1},{1,0},{2,3},{3,2},{4,5},{5,4},{6,7},{7,6},{8,9},{9,8},{10,11... | collective-permute-start | bytes 10760 | tf_op jit(solution)/shard_map/ppermute | solution.py:674
  5.4 16.1 %collective-permute-start = (f32[4,32,128]{2,1,0:T(8,128)S(1)}, f32[4,32,128]{2,1,0:T(8,128)S(1)}, u32[]{:S(2)}, u32[]{:S(2)}) collective-permute-start(f32[4,32,128]{2,1,0:T(8,128)S(1)} %get-tuple-element.41), channel_id=1, source_target_pairs={{0,4},{4,0},{8,12},{12,8},{16,20},{20,16},{24,28},{28,24},{1,5},{5... | collective-permute-start | bytes 196616 | tf_op jit(solution)/shard_map/ppermute | solution.py:691
  5.4 16.1 %collective-permute-start.1 = (f32[4,32,128]{2,1,0:T(8,128)S(1)}, f32[4,32,128]{2,1,0:T(8,128)S(1)}, u32[]{:S(2)}, u32[]{:S(2)}) collective-permute-start(f32[4,32,128]{2,1,0:T(8,128)S(1)} %get-tuple-element.42), channel_id=1, source_target_pairs={{0,1},{1,0},{2,3},{3,2},{4,8},{5,9},{6,10},{7,11},{8,4},{9,5},{10,... | collective-permute-start | bytes 196616 | tf_op jit(solution)/shard_map/ppermute | solution.py:696
  7.0 14.5 %collective-permute-start.3 = (s32[14,128]{1,0:T(8,128)S(1)}, s32[14,128]{1,0:T(8,128)S(1)}, u32[]{:S(2)}, u32[]{:S(2)}) collective-permute-start(s32[14,128]{1,0:T(8,128)S(1)} %pad_add_fusion.rest_0_), channel_id=1, source_target_pairs={{0,3},{1,2},{2,1},{3,0},{4,7},{5,6},{6,5},{7,4},{8,11},{9,10},{10,... | collective-permute-start | bytes 21512 | tf_op jit(solution)/shard_map/ppermute | solution.py:674
  26.0 12.1 %collective-permute-start.7 = (f32[32,128]{1,0:T(8,128)S(1)}, f32[32,128]{1,0:T(8,128)S(1)}, u32[]{:S(2)}, u32[]{:S(2)}) collective-permute-start(f32[32,128]{1,0:T(8,128)S(1)} %get-tuple-element.52.field.precond), channel_id=1, source_target_pairs={{0,3},{1,5},{2,4},{3,7},{4,2},{5,1},{6,8},{7,0},{8,6},{9,13},{10,1... | collective-permute-start | bytes 49160 | tf_op jit(solution)/shard_map/ppermute | solution.py:754
  26.0 12.0 %collective-permute-start.6 = (f32[32,128]{1,0:T(8,128)S(1)}, f32[32,128]{1,0:T(8,128)S(1)}, u32[]{:S(2)}, u32[]{:S(2)}) collective-permute-start(f32[32,128]{1,0:T(8,128)S(1)} %get-tuple-element.52.field.precond), channel_id=1, source_target_pairs={{0,2},{1,4},{2,6},{3,7},{4,1},{5,8},{6,0},{7,3},{8,5},{9,12},{10,1... | collective-permute-start | bytes 49160 | tf_op jit(solution)/shard_map/ppermute | solution.py:754
  30.2 7.9 %collective-permute-start.5 = (f32[32,128]{1,0:T(8,128)S(1)}, f32[32,128]{1,0:T(8,128)S(1)}, u32[]{:S(2)}, u32[]{:S(2)}) collective-permute-start(f32[32,128]{1,0:T(8,128)S(1)} %get-tuple-element.52.field.precond), channel_id=1, source_target_pairs={{0,31},{1,2},{2,1},{3,4},{4,3},{5,6},{6,5},{7,8},{8,7},{9,10},{10,... | collective-permute-start | bytes 49160 | tf_op jit(solution)/shard_map/ppermute | solution.py:754
  30.9 7.2 %collective-permute-start.4 = (f32[32,128]{1,0:T(8,128)S(1)}, f32[32,128]{1,0:T(8,128)S(1)}, u32[]{:S(2)}, u32[]{:S(2)}) collective-permute-start(f32[32,128]{1,0:T(8,128)S(1)} %get-tuple-element.52.field.precond), channel_id=1, source_target_pairs={{0,1},{1,0},{2,3},{3,2},{4,5},{5,4},{6,7},{7,6},{8,9},{9,8},{10,11... | collective-permute-start | bytes 49160 | tf_op jit(solution)/shard_map/ppermute | solution.py:754
  40.3 9.9 %collective-permute-start.11 = (f32[32,128]{1,0:T(8,128)S(1)}, f32[32,128]{1,0:T(8,128)S(1)}, u32[]{:S(2)}, u32[]{:S(2)}) collective-permute-start(f32[32,128]{1,0:T(8,128)S(1)} %get-tuple-element.61.field.scaled), channel_id=1, source_target_pairs={{0,3},{1,5},{2,4},{3,7},{4,2},{5,1},{6,8},{7,0},{8,6},{9,13},{10,1... | collective-permute-start | bytes 49160 | tf_op jit(solution)/shard_map/ppermute | solution.py:754
  40.3 9.9 %collective-permute-start.10 = (f32[32,128]{1,0:T(8,128)S(1)}, f32[32,128]{1,0:T(8,128)S(1)}, u32[]{:S(2)}, u32[]{:S(2)}) collective-permute-start(f32[32,128]{1,0:T(8,128)S(1)} %get-tuple-element.61.field.scaled), channel_id=1, source_target_pairs={{0,2},{1,4},{2,6},{3,7},{4,1},{5,8},{6,0},{7,3},{8,5},{9,12},{10,1... | collective-permute-start | bytes 49160 | tf_op jit(solution)/shard_map/ppermute | solution.py:754
  43.0 7.3 %collective-permute-start.9 = (f32[32,128]{1,0:T(8,128)S(1)}, f32[32,128]{1,0:T(8,128)S(1)}, u32[]{:S(2)}, u32[]{:S(2)}) collective-permute-start(f32[32,128]{1,0:T(8,128)S(1)} %get-tuple-element.61.field.scaled), channel_id=1, source_target_pairs={{0,31},{1,2},{2,1},{3,4},{4,3},{5,6},{6,5},{7,8},{8,7},{9,10},{10,... | collective-permute-start | bytes 49160 | tf_op jit(solution)/shard_map/ppermute | solution.py:754
  45.1 5.1 %collective-permute-start.8 = (f32[32,128]{1,0:T(8,128)S(1)}, f32[32,128]{1,0:T(8,128)S(1)}, u32[]{:S(2)}, u32[]{:S(2)}) collective-permute-start(f32[32,128]{1,0:T(8,128)S(1)} %get-tuple-element.61.field.scaled), channel_id=1, source_target_pairs={{0,1},{1,0},{2,3},{3,2},{4,5},{5,4},{6,7},{7,6},{8,9},{9,8},{10,11... | collective-permute-start | bytes 49160 | tf_op jit(solution)/shard_map/ppermute | solution.py:754
  52.5 1.2 %collective-permute-start.12 = (f32[8,128]{1,0:T(8,128)S(1)}, f32[8,128]{1,0:T(8,128)S(1)}, u32[]{:S(2)}, u32[]{:S(2)}) collective-permute-start(f32[8,128]{1,0:T(8,128)S(1)} %get-tuple-element.65), channel_id=1, source_target_pairs={{0,4},{4,0},{8,12},{12,8},{16,20},{20,16},{24,28},{28,24},{1,5},{5... | collective-permute-start | bytes 12296 | tf_op jit(solution)/shard_map/ppermute | solution.py:674
  53.7 5.4 %collective-permute-start.15 = (f32[8,128]{1,0:T(8,128)S(1)}, f32[8,128]{1,0:T(8,128)S(1)}, u32[]{:S(2)}, u32[]{:S(2)}) collective-permute-start(f32[8,128]{1,0:T(8,128)S(1)} %add.12), channel_id=1, source_target_pairs={{0,3},{1,2},{2,1},{3,0},{4,7},{5,6},{6,5},{7,4},{8,11},{9,10},{10,... | collective-permute-start | bytes 12296 | tf_op jit(solution)/shard_map/ppermute | solution.py:674
  54.9 4.5 %collective-permute-start.14 = (f32[8,128]{1,0:T(8,128)S(1)}, f32[8,128]{1,0:T(8,128)S(1)}, u32[]{:S(2)}, u32[]{:S(2)}) collective-permute-start(f32[8,128]{1,0:T(8,128)S(1)} %add.12), channel_id=1, source_target_pairs={{0,2},{1,3},{2,0},{3,1},{4,6},{5,7},{6,4},{7,5},{8,10},{9,11},{10,... | collective-permute-start | bytes 12296 | tf_op jit(solution)/shard_map/ppermute | solution.py:674
  57.1 3.6 %collective-permute-start.13 = (f32[8,128]{1,0:T(8,128)S(1)}, f32[8,128]{1,0:T(8,128)S(1)}, u32[]{:S(2)}, u32[]{:S(2)}) collective-permute-start(f32[8,128]{1,0:T(8,128)S(1)} %add.12), channel_id=1, source_target_pairs={{0,1},{1,0},{2,3},{3,2},{4,5},{5,4},{6,7},{7,6},{8,9},{9,8},{10,11... | collective-permute-start | bytes 12296 | tf_op jit(solution)/shard_map/ppermute | solution.py:674
  60.7 4.5 %collective-permute-start.18 = (f32[8,128]{1,0:T(8,128)S(1)}, f32[8,128]{1,0:T(8,128)S(1)}, u32[]{:S(2)}, u32[]{:S(2)}) collective-permute-start(f32[8,128]{1,0:T(8,128)S(1)} %add_add_fusion.rest_0_), channel_id=1, source_target_pairs={{0,24},{4,28},{8,16},{12,20},{16,8},{20,12},{24,0},{28,4},{1,25},{... | collective-permute-start | bytes 12296 | tf_op jit(solution)/shard_map/ppermute | solution.py:674
  61.0 4.2 %collective-permute-start.17 = (f32[8,128]{1,0:T(8,128)S(1)}, f32[8,128]{1,0:T(8,128)S(1)}, u32[]{:S(2)}, u32[]{:S(2)}) collective-permute-start(f32[8,128]{1,0:T(8,128)S(1)} %add_add_fusion.rest_0_), channel_id=1, source_target_pairs={{0,16},{4,20},{8,24},{12,28},{16,0},{20,4},{24,8},{28,12},{1,17},{... | collective-permute-start | bytes 12296 | tf_op jit(solution)/shard_map/ppermute | solution.py:674
  63.7 3.6 %collective-permute-start.16 = (f32[8,128]{1,0:T(8,128)S(1)}, f32[8,128]{1,0:T(8,128)S(1)}, u32[]{:S(2)}, u32[]{:S(2)}) collective-permute-start(f32[8,128]{1,0:T(8,128)S(1)} %add_add_fusion.rest_0_), channel_id=1, source_target_pairs={{0,8},{4,12},{8,0},{12,4},{16,24},{20,28},{24,16},{28,20},{1,9},{5... | collective-permute-start | bytes 12296 | tf_op jit(solution)/shard_map/ppermute | solution.py:674

commit v20 on v19

--- a/solution.py
+++ b/solution.py
@@ -197,7 +197,7 @@
     return jnp.concatenate([front, front, back, ones, rest], 0)
 
 
-GROUP = 6
+GROUP = 8
 
 
 def flat_tiles(count, runs, most, table, sides, middles, weights, other_at, buffers, tiles, rows_ref, cols_ref):
@@ -232,7 +232,7 @@
             row = jnp.where(alone, share, a)
             own = jnp.minimum(a, share - 1)
             other = wide(other_at(3, n))
-            down = [None] * 2
+            down = [None] * 4
             for c, here in enumerate(chunks):
                 left = ahead[k, here, :]
                 rest = jnp.maximum(left, 0.0)

time: 68.6 us -> 67.1 us (0.978)
  starting transfers between devices: 28.7 us -> 27.7 us
    ppermute x8, starting transfers between devices: 13.4 us -> 12.5 us  [exchange(): return [lax.ppermute(field, axes, list(enumerate(to))) for to in swaps]]
  transfers between devices with their start and end apart: 19 -> 19, of which waited for: 8 -> 7; matrix products, arithmetic and copies ran while one was open for 0% -> 0% of each run, Pallas kernels for 28% -> 28%
where the time goes in v20:
time: 67.1 us; the launch traced here: 67 us
  Pallas kernels  30.4 us (45%)
  starting transfers between devices  27.7 us (41%)
  waiting for transfers between devices  8.15 us (12%)
  between operations  0.78 us (1%)
    pallas_call x8, Pallas kernels, call(): pl.pallas_call(kernel, out_shape=outs, in_specs=[SMEM] * scalars + [HBM]...  30.4 us
    ppermute x9, starting transfers between devices, swap(): lax.ppermute(values, axis, [(i, i ^ step) for i in range(lax.axis_size(ax...  15 us
    ppermute x8, starting transfers between devices, exchange(): return [lax.ppermute(field, axes, list(enumerate(to))) for to in swaps]  12.5 us
    ppermute x9, waiting for transfers between devices, swap(): lax.ppermute(values, axis, [(i, i ^ step) for i in range(lax.axis_size(ax...  7.73 us
  transfers between devices with their start and end apart: 19, of which 7 were waited for; matrix products, arithmetic and copies ran while one was open for 0% of the time, Pallas kernels for 28%

profile of v20, /device:TPU:0, one launch (start us, length us, event | category | flops | bytes accessed | tf_op | source)
XLA Modules:
  0.0 67.0 jit_solution(16610610647019666340)
XLA Ops:
  0.6 1.7 %prepare.1 = (s32[8]{0:T(128)S(4)}, s32[1480]{0:T(1024)S(4)}, f32[4,192,128]{2,1,0:T(8,128)S(1)}, f32[4,64,128]{2,1,0:T(8,128)S(1)}, f32[32,128]{1,0:T(8,128)S(1...) custom-call(s32[8]{0:T(128)} %counts.1, f32[3]{0:T(128)} %densities.1, ...), custom_call_target="tpu_custom_call" | custom-call | tf_op jit(solution)/shard_map/prepare/pallas_call | solution.py:661
  2.4 3.1 %collective-permute-start.2 = (s32[7,128]{1,0:T(8,128)S(1)}, s32[7,128]{1,0:T(8,128)S(1)}, u32[]{:S(2)}, u32[]{:S(2)}) collective-permute-start(s32[7,128]{1,0:T(8,128)S(1)} %get-tuple-element.51), channel_id=1, source_target_pairs={{0,1},{1,0},{2,3},{3,2},{4,5},{5,4},{6,7},{7,6},{8,9},{9,8},{10,11... | collective-permute-start | bytes 10760 | tf_op jit(solution)/shard_map/ppermute | solution.py:674
  5.4 0.0 collective-permute-start
  5.4 0.2 collective-permute-start.1
  5.6 1.4 %collective-permute-done.2 = s32[7,128]{1,0:T(8,128)S(1)} collective-permute-done((s32[7,128]{1,0:T(8,128)S(1)}, s32[7,128]{1,0:T(8,128)S(1)}, u32[]{:S(2)}, u32[]{:S(2)}) %collective-permute-start.2) | collective-permute-done | bytes 3616 | tf_op jit(solution)/shard_map/ppermute | solution.py:674
  7.0 4.0 %collective-permute-start.3 = (s32[14,128]{1,0:T(8,128)S(1)}, s32[14,128]{1,0:T(8,128)S(1)}, u32[]{:S(2)}, u32[]{:S(2)}) collective-permute-start(s32[14,128]{1,0:T(8,128)S(1)} %pad_add_fusion.rest_0_), channel_id=1, source_target_pairs={{0,3},{1,2},{2,1},{3,0},{4,7},{5,6},{6,5},{7,4},{8,11},{9,10},{10,... | collective-permute-start | bytes 21512 | tf_op jit(solution)/shard_map/ppermute | solution.py:674
  11.1 10.3 %build_inner.1 = (s32[196]{0:T(256)S(4)}, s32[195]{0:T(256)S(4)}, f32[232,128,128]{2,1,0:T(8,128)S(1)}, bf16[2,32,128,128]{3,2,1,0:T(8,128)(2,1)S(1)}, f32[3,32,...) custom-call(s32[8]{0:T(128)S(4)} %get-tuple-element.35.meta, ...), custom_call_target="tpu_custom_call" | custom-call | flops 56623104 | tf_op jit(solution)/shard_map/build_inner/pallas_call | solution.py:661
  21.4 0.0 collective-permute-done.3.rest_1_
  21.4 0.0 collective-permute-done.first
  21.4 0.0 collective-permute-done.1.second
  21.4 4.4 %build_outer.1 = (s32[1]{0:T(128)S(4)}, f32[238,128,128]{2,1,0:T(8,128)S(1)}, f32[32,128]{1,0:T(8,128)S(1)}, f32[32,128]{1,0:T(8,128)S(1)}, f32[32,128]{1,0:T(8,128)S(1)}, /*index=5*/f32[32,128]{1,0:T(8,128)S(1)}) custom-call(s32[8]{0:T(128)S(4)} %get-tuple-element.35.meta, s32[1480]{0:T(1024)S(4)} %get-tuple-element.36.table, ...), custom_call_target="tpu_custom_call" | custom-call | flops 58195968 | tf_op jit(solution)/shard_map/build_outer/pallas_call | solution.py:661
  25.8 0.1 collective-permute-start.7
  25.9 3.6 %collective-permute-start.6 = (f32[32,128]{1,0:T(8,128)S(1)}, f32[32,128]{1,0:T(8,128)S(1)}, u32[]{:S(2)}, u32[]{:S(2)}) collective-permute-start(f32[32,128]{1,0:T(8,128)S(1)} %get-tuple-element.52.field.precond), channel_id=1, source_target_pairs={{0,2},{1,4},{2,6},{3,7},{4,1},{5,8},{6,0},{7,3},{8,5},{9,12},{10,1... | collective-permute-start | bytes 49160 | tf_op jit(solution)/shard_map/ppermute | solution.py:754
  29.5 0.8 %collective-permute-start.5 = (f32[32,128]{1,0:T(8,128)S(1)}, f32[32,128]{1,0:T(8,128)S(1)}, u32[]{:S(2)}, u32[]{:S(2)}) collective-permute-start(f32[32,128]{1,0:T(8,128)S(1)} %get-tuple-element.52.field.precond), channel_id=1, source_target_pairs={{0,31},{1,2},{2,1},{3,4},{4,3},{5,6},{6,5},{7,8},{8,7},{9,10},{10,... | collective-permute-start | bytes 49160 | tf_op jit(solution)/shard_map/ppermute | solution.py:754
  30.3 3.4 %collective-permute-start.4 = (f32[32,128]{1,0:T(8,128)S(1)}, f32[32,128]{1,0:T(8,128)S(1)}, u32[]{:S(2)}, u32[]{:S(2)}) collective-permute-start(f32[32,128]{1,0:T(8,128)S(1)} %get-tuple-element.52.field.precond), channel_id=1, source_target_pairs={{0,1},{1,0},{2,3},{3,2},{4,5},{5,4},{6,7},{7,6},{8,9},{9,8},{10,11... | collective-permute-start | bytes 49160 | tf_op jit(solution)/shard_map/ppermute | solution.py:754
  33.6 4.3 %apply_inner.2 = (f32[32,128,128]{2,1,0:T(8,128)S(1)}, f32[256,128]{1,0:T(8,128)S(1)}) custom-call(s32[8]{0:T(128)S(4)} %get-tuple-element.35.meta, s32[1480]{0:T(1024)S(4)} %get-tuple-element.36.table, s32[196]{0:T(256)S(4)} %get-tuple-element.38.plan, s32[1]{0:T(128)S(4)} %get-tuple-element.53.again, f32[32,128]{1,0:T(8,128)S(1)} %get-tuple-element.52.field.precond, ...), custom_call_target="tpu_custom_call" | custom-call | flops 14155776 | tf_op jit(solution)/shard_map/apply_inner/pallas_call | solution.py:661
  38.0 0.0 collective-permute-done.7.rest_3_
  38.0 0.0 collective-permute-done.6.rest_2_
  38.0 0.0 collective-permute-done.5.rest_1_
  38.0 0.0 collective-permute-done.4.rest_0_
  38.0 2.2 %apply_first.1 = (f32[32,128]{1,0:T(8,128)S(1)}, f32[32,128]{1,0:T(8,128)S(1)}) custom-call(s32[8]{0:T(128)S(4)} %get-tuple-element.35.meta, s32[1480]{0:T(1024)S(4)} %get-tuple-element.36.table, s32[196]{0:T(256)S(4)} %get-tuple-element.38.plan, s32[1]{0:T(128)S(4)} %get-tuple-element.53.again, f32[32,128]{1,0:T(8,128)S(1)} %get-tuple-element.54.diagonal, ...), custom_call_target="tpu_custom_call" | custom-call | flops 7274496 | tf_op jit(solution)/shard_map/apply_first/pallas_call | solution.py:661
  40.2 0.1 collective-permute-start.11
  40.2 2.6 %collective-permute-start.10 = (f32[32,128]{1,0:T(8,128)S(1)}, f32[32,128]{1,0:T(8,128)S(1)}, u32[]{:S(2)}, u32[]{:S(2)}) collective-permute-start(f32[32,128]{1,0:T(8,128)S(1)} %get-tuple-element.61.field.scaled), channel_id=1, source_target_pairs={{0,2},{1,4},{2,6},{3,7},{4,1},{5,8},{6,0},{7,3},{8,5},{9,12},{10,1... | collective-permute-start | bytes 49160 | tf_op jit(solution)/shard_map/ppermute | solution.py:754
  42.8 1.9 %collective-permute-start.9 = (f32[32,128]{1,0:T(8,128)S(1)}, f32[32,128]{1,0:T(8,128)S(1)}, u32[]{:S(2)}, u32[]{:S(2)}) collective-permute-start(f32[32,128]{1,0:T(8,128)S(1)} %get-tuple-element.61.field.scaled), channel_id=1, source_target_pairs={{0,31},{1,2},{2,1},{3,4},{4,3},{5,6},{6,5},{7,8},{8,7},{9,10},{10,... | collective-permute-start | bytes 49160 | tf_op jit(solution)/shard_map/ppermute | solution.py:754
  44.8 0.1 collective-permute-start.8
  44.9 4.3 %apply_inner.3 = (f32[32,128,128]{2,1,0:T(8,128)S(1)}, f32[256,128]{1,0:T(8,128)S(1)}) custom-call(s32[8]{0:T(128)S(4)} %get-tuple-element.35.meta, s32[1480]{0:T(1024)S(4)} %get-tuple-element.36.table, s32[196]{0:T(256)S(4)} %get-tuple-element.38.plan, s32[1]{0:T(128)S(4)} %get-tuple-element.53.again, f32[32,128]{1,0:T(8,128)S(1)} %get-tuple-element.61.field.scaled, ...), custom_call_target="tpu_custom_call" | custom-call | flops 14155776 | tf_op jit(solution)/shard_map/apply_inner/pallas_call | solution.py:661
  49.2 0.0 collective-permute-done.11.rest_3_
  49.2 0.0 collective-permute-done.10.rest_2_
  49.2 0.4 collective-permute-done.9.rest_1_
  49.6 0.0 collective-permute-done.8.rest_0_
  49.6 2.2 %apply_second.1 = (f32[32,128]{1,0:T(8,128)S(1)}, f32[8,128]{1,0:T(8,128)S(1)}) custom-call(s32[8]{0:T(128)S(4)} %get-tuple-element.35.meta, s32[1480]{0:T(1024)S(4)} %get-tuple-element.36.table, s32[196]{0:T(256)S(4)} %get-tuple-element.38.plan, s32[1]{0:T(128)S(4)} %get-tuple-element.53.again, f32[32,128]{1,0:T(8,128)S(1)} %get-tuple-element.34.source, ...), custom_call_target="tpu_custom_call" | custom-call | flops 7274496 | tf_op jit(solution)/shard_map/apply_second/pallas_call | solution.py:661
  51.9 0.0 collective-permute-start.12
  51.9 1.2 %collective-permute-done.12 = f32[8,128]{1,0:T(8,128)S(1)} collective-permute-done((f32[8,128]{1,0:T(8,128)S(1)}, f32[8,128]{1,0:T(8,128)S(1)}, u32[]{:S(2)}, u32[]{:S(2)}) %collective-permute-start.12) | collective-permute-done | bytes 4128 | tf_op jit(solution)/shard_map/ppermute | solution.py:674
  53.0 0.0 collective-permute-start.15
  53.0 3.7 %collective-permute-start.14 = (f32[8,128]{1,0:T(8,128)S(1)}, f32[8,128]{1,0:T(8,128)S(1)}, u32[]{:S(2)}, u32[]{:S(2)}) collective-permute-start(f32[8,128]{1,0:T(8,128)S(1)} %add.12), channel_id=1, source_target_pairs={{0,2},{1,3},{2,0},{3,1},{4,6},{5,7},{6,4},{7,5},{8,10},{9,11},{10,... | collective-permute-start | bytes 12296 | tf_op jit(solution)/shard_map/ppermute | solution.py:674
  56.7 0.7 %collective-permute-start.13 = (f32[8,128]{1,0:T(8,128)S(1)}, f32[8,128]{1,0:T(8,128)S(1)}, u32[]{:S(2)}, u32[]{:S(2)}) collective-permute-start(f32[8,128]{1,0:T(8,128)S(1)} %add.12), channel_id=1, source_target_pairs={{0,1},{1,0},{2,3},{3,2},{4,5},{5,4},{6,7},{7,6},{8,9},{9,8},{10,11... | collective-permute-start | bytes 12296 | tf_op jit(solution)/shard_map/ppermute | solution.py:674
  57.4 1.0 %collective-permute-done.15 = f32[8,128]{1,0:T(8,128)S(1)} collective-permute-done((f32[8,128]{1,0:T(8,128)S(1)}, f32[8,128]{1,0:T(8,128)S(1)}, u32[]{:S(2)}, u32[]{:S(2)}) %collective-permute-start.15) | collective-permute-done | bytes 4128 | tf_op jit(solution)/shard_map/ppermute | solution.py:674
  58.4 0.0 collective-permute-done.14
  58.4 1.9 %collective-permute-done.13 = f32[8,128]{1,0:T(8,128)S(1)} collective-permute-done((f32[8,128]{1,0:T(8,128)S(1)}, f32[8,128]{1,0:T(8,128)S(1)}, u32[]{:S(2)}, u32[]{:S(2)}) %collective-permute-start.13) | collective-permute-done | bytes 4128 | tf_op jit(solution)/shard_map/ppermute | solution.py:674
  60.3 0.9 %collective-permute-start.18 = (f32[8,128]{1,0:T(8,128)S(1)}, f32[8,128]{1,0:T(8,128)S(1)}, u32[]{:S(2)}, u32[]{:S(2)}) collective-permute-start(f32[8,128]{1,0:T(8,128)S(1)} %add_add_fusion.rest_0_), channel_id=1, source_target_pairs={{0,24},{4,28},{8,16},{12,20},{16,8},{20,12},{24,0},{28,4},{1,25},{... | collective-permute-start | bytes 12296 | tf_op jit(solution)/shard_map/ppermute | solution.py:674
  61.2 1.2 %collective-permute-start.17 = (f32[8,128]{1,0:T(8,128)S(1)}, f32[8,128]{1,0:T(8,128)S(1)}, u32[]{:S(2)}, u32[]{:S(2)}) collective-permute-start(f32[8,128]{1,0:T(8,128)S(1)} %add_add_fusion.rest_0_), channel_id=1, source_target_pairs={{0,16},{4,20},{8,24},{12,28},{16,0},{20,4},{24,8},{28,12},{1,17},{... | collective-permute-start | bytes 12296 | tf_op jit(solution)/shard_map/ppermute | solution.py:674
  62.4 1.4 %collective-permute-start.16 = (f32[8,128]{1,0:T(8,128)S(1)}, f32[8,128]{1,0:T(8,128)S(1)}, u32[]{:S(2)}, u32[]{:S(2)}) collective-permute-start(f32[8,128]{1,0:T(8,128)S(1)} %add_add_fusion.rest_0_), channel_id=1, source_target_pairs={{0,8},{4,12},{8,0},{12,4},{16,24},{20,28},{24,16},{28,20},{1,9},{5... | collective-permute-start | bytes 12296 | tf_op jit(solution)/shard_map/ppermute | solution.py:674
  63.8 1.0 %collective-permute-done.18.rest_3_ = f32[8,128]{1,0:T(8,128)S(1)} collective-permute-done((f32[8,128]{1,0:T(8,128)S(1)}, f32[8,128]{1,0:T(8,128)S(1)}, u32[]{:S(2)}, u32[]{:S(2)}) %collective-permute-start.18) | collective-permute-done | bytes 4128 | tf_op jit(solution)/shard_map/ppermute | solution.py:674
  64.8 0.0 collective-permute-done.17.rest_2_
  64.9 1.2 %collective-permute-done.16.rest_1_ = f32[8,128]{1,0:T(8,128)S(1)} collective-permute-done((f32[8,128]{1,0:T(8,128)S(1)}, f32[8,128]{1,0:T(8,128)S(1)}, u32[]{:S(2)}, u32[]{:S(2)}) %collective-permute-start.16) | collective-permute-done | bytes 4128 | tf_op jit(solution)/shard_map/ppermute | solution.py:674
  66.1 0.9 %finish.1 = (f32[32,128]{1,0:T(8,128)}, f32[32,128]{1,0:T(8,128)}) custom-call(f32[32,128]{1,0:T(8,128)S(1)} %get-tuple-element.34.source, f32[32,128]{1,0:T(8,128)S(1)} %get-tuple-element.52.field.precond, f32[32,128]{1,0:T(8,128)S(1)} %get-tuple-element.60.spill, f32[32,128]{1,0:T(8,128)S(1)} %get-tuple-element.61.field.scaled, ...), custom_call_target="tpu_custom_call" | custom-call | tf_op jit(solution)/shard_map/finish/pallas_call | solution.py:661
  (3 shorter events, 0.0 us)
Async XLA Ops:
  2.4 4.7 %collective-permute-start.2 = (s32[7,128]{1,0:T(8,128)S(1)}, s32[7,128]{1,0:T(8,128)S(1)}, u32[]{:S(2)}, u32[]{:S(2)}) collective-permute-start(s32[7,128]{1,0:T(8,128)S(1)} %get-tuple-element.51), channel_id=1, source_target_pairs={{0,1},{1,0},{2,3},{3,2},{4,5},{5,4},{6,7},{7,6},{8,9},{9,8},{10,11... | collective-permute-start | bytes 10760 | tf_op jit(solution)/shard_map/ppermute | solution.py:674
  5.4 15.9 %collective-permute-start = (f32[4,32,128]{2,1,0:T(8,128)S(1)}, f32[4,32,128]{2,1,0:T(8,128)S(1)}, u32[]{:S(2)}, u32[]{:S(2)}) collective-permute-start(f32[4,32,128]{2,1,0:T(8,128)S(1)} %get-tuple-element.41), channel_id=1, source_target_pairs={{0,4},{4,0},{8,12},{12,8},{16,20},{20,16},{24,28},{28,24},{1,5},{5... | collective-permute-start | bytes 196616 | tf_op jit(solution)/shard_map/ppermute | solution.py:691
  5.4 15.9 %collective-permute-start.1 = (f32[4,32,128]{2,1,0:T(8,128)S(1)}, f32[4,32,128]{2,1,0:T(8,128)S(1)}, u32[]{:S(2)}, u32[]{:S(2)}) collective-permute-start(f32[4,32,128]{2,1,0:T(8,128)S(1)} %get-tuple-element.42), channel_id=1, source_target_pairs={{0,1},{1,0},{2,3},{3,2},{4,8},{5,9},{6,10},{7,11},{8,4},{9,5},{10,... | collective-permute-start | bytes 196616 | tf_op jit(solution)/shard_map/ppermute | solution.py:696
  7.0 14.3 %collective-permute-start.3 = (s32[14,128]{1,0:T(8,128)S(1)}, s32[14,128]{1,0:T(8,128)S(1)}, u32[]{:S(2)}, u32[]{:S(2)}) collective-permute-start(s32[14,128]{1,0:T(8,128)S(1)} %pad_add_fusion.rest_0_), channel_id=1, source_target_pairs={{0,3},{1,2},{2,1},{3,0},{4,7},{5,6},{6,5},{7,4},{8,11},{9,10},{10,... | collective-permute-start | bytes 21512 | tf_op jit(solution)/shard_map/ppermute | solution.py:674
  25.8 12.2 %collective-permute-start.7 = (f32[32,128]{1,0:T(8,128)S(1)}, f32[32,128]{1,0:T(8,128)S(1)}, u32[]{:S(2)}, u32[]{:S(2)}) collective-permute-start(f32[32,128]{1,0:T(8,128)S(1)} %get-tuple-element.52.field.precond), channel_id=1, source_target_pairs={{0,3},{1,5},{2,4},{3,7},{4,2},{5,1},{6,8},{7,0},{8,6},{9,13},{10,1... | collective-permute-start | bytes 49160 | tf_op jit(solution)/shard_map/ppermute | solution.py:754
  25.9 12.1 %collective-permute-start.6 = (f32[32,128]{1,0:T(8,128)S(1)}, f32[32,128]{1,0:T(8,128)S(1)}, u32[]{:S(2)}, u32[]{:S(2)}) collective-permute-start(f32[32,128]{1,0:T(8,128)S(1)} %get-tuple-element.52.field.precond), channel_id=1, source_target_pairs={{0,2},{1,4},{2,6},{3,7},{4,1},{5,8},{6,0},{7,3},{8,5},{9,12},{10,1... | collective-permute-start | bytes 49160 | tf_op jit(solution)/shard_map/ppermute | solution.py:754
  29.5 8.5 %collective-permute-start.5 = (f32[32,128]{1,0:T(8,128)S(1)}, f32[32,128]{1,0:T(8,128)S(1)}, u32[]{:S(2)}, u32[]{:S(2)}) collective-permute-start(f32[32,128]{1,0:T(8,128)S(1)} %get-tuple-element.52.field.precond), channel_id=1, source_target_pairs={{0,31},{1,2},{2,1},{3,4},{4,3},{5,6},{6,5},{7,8},{8,7},{9,10},{10,... | collective-permute-start | bytes 49160 | tf_op jit(solution)/shard_map/ppermute | solution.py:754
  30.3 7.7 %collective-permute-start.4 = (f32[32,128]{1,0:T(8,128)S(1)}, f32[32,128]{1,0:T(8,128)S(1)}, u32[]{:S(2)}, u32[]{:S(2)}) collective-permute-start(f32[32,128]{1,0:T(8,128)S(1)} %get-tuple-element.52.field.precond), channel_id=1, source_target_pairs={{0,1},{1,0},{2,3},{3,2},{4,5},{5,4},{6,7},{7,6},{8,9},{9,8},{10,11... | collective-permute-start | bytes 49160 | tf_op jit(solution)/shard_map/ppermute | solution.py:754
  40.2 9.0 %collective-permute-start.11 = (f32[32,128]{1,0:T(8,128)S(1)}, f32[32,128]{1,0:T(8,128)S(1)}, u32[]{:S(2)}, u32[]{:S(2)}) collective-permute-start(f32[32,128]{1,0:T(8,128)S(1)} %get-tuple-element.61.field.scaled), channel_id=1, source_target_pairs={{0,3},{1,5},{2,4},{3,7},{4,2},{5,1},{6,8},{7,0},{8,6},{9,13},{10,1... | collective-permute-start | bytes 49160 | tf_op jit(solution)/shard_map/ppermute | solution.py:754
  40.2 9.0 %collective-permute-start.10 = (f32[32,128]{1,0:T(8,128)S(1)}, f32[32,128]{1,0:T(8,128)S(1)}, u32[]{:S(2)}, u32[]{:S(2)}) collective-permute-start(f32[32,128]{1,0:T(8,128)S(1)} %get-tuple-element.61.field.scaled), channel_id=1, source_target_pairs={{0,2},{1,4},{2,6},{3,7},{4,1},{5,8},{6,0},{7,3},{8,5},{9,12},{10,1... | collective-permute-start | bytes 49160 | tf_op jit(solution)/shard_map/ppermute | solution.py:754
  42.8 6.8 %collective-permute-start.9 = (f32[32,128]{1,0:T(8,128)S(1)}, f32[32,128]{1,0:T(8,128)S(1)}, u32[]{:S(2)}, u32[]{:S(2)}) collective-permute-start(f32[32,128]{1,0:T(8,128)S(1)} %get-tuple-element.61.field.scaled), channel_id=1, source_target_pairs={{0,31},{1,2},{2,1},{3,4},{4,3},{5,6},{6,5},{7,8},{8,7},{9,10},{10,... | collective-permute-start | bytes 49160 | tf_op jit(solution)/shard_map/ppermute | solution.py:754
  44.8 4.8 %collective-permute-start.8 = (f32[32,128]{1,0:T(8,128)S(1)}, f32[32,128]{1,0:T(8,128)S(1)}, u32[]{:S(2)}, u32[]{:S(2)}) collective-permute-start(f32[32,128]{1,0:T(8,128)S(1)} %get-tuple-element.61.field.scaled), channel_id=1, source_target_pairs={{0,1},{1,0},{2,3},{3,2},{4,5},{5,4},{6,7},{7,6},{8,9},{9,8},{10,11... | collective-permute-start | bytes 49160 | tf_op jit(solution)/shard_map/ppermute | solution.py:754
  51.9 1.2 %collective-permute-start.12 = (f32[8,128]{1,0:T(8,128)S(1)}, f32[8,128]{1,0:T(8,128)S(1)}, u32[]{:S(2)}, u32[]{:S(2)}) collective-permute-start(f32[8,128]{1,0:T(8,128)S(1)} %get-tuple-element.65), channel_id=1, source_target_pairs={{0,4},{4,0},{8,12},{12,8},{16,20},{20,16},{24,28},{28,24},{1,5},{5... | collective-permute-start | bytes 12296 | tf_op jit(solution)/shard_map/ppermute | solution.py:674
  53.0 5.4 %collective-permute-start.15 = (f32[8,128]{1,0:T(8,128)S(1)}, f32[8,128]{1,0:T(8,128)S(1)}, u32[]{:S(2)}, u32[]{:S(2)}) collective-permute-start(f32[8,128]{1,0:T(8,128)S(1)} %add.12), channel_id=1, source_target_pairs={{0,3},{1,2},{2,1},{3,0},{4,7},{5,6},{6,5},{7,4},{8,11},{9,10},{10,... | collective-permute-start | bytes 12296 | tf_op jit(solution)/shard_map/ppermute | solution.py:674
  53.0 5.4 %collective-permute-start.14 = (f32[8,128]{1,0:T(8,128)S(1)}, f32[8,128]{1,0:T(8,128)S(1)}, u32[]{:S(2)}, u32[]{:S(2)}) collective-permute-start(f32[8,128]{1,0:T(8,128)S(1)} %add.12), channel_id=1, source_target_pairs={{0,2},{1,3},{2,0},{3,1},{4,6},{5,7},{6,4},{7,5},{8,10},{9,11},{10,... | collective-permute-start | bytes 12296 | tf_op jit(solution)/shard_map/ppermute | solution.py:674
  56.7 3.6 %collective-permute-start.13 = (f32[8,128]{1,0:T(8,128)S(1)}, f32[8,128]{1,0:T(8,128)S(1)}, u32[]{:S(2)}, u32[]{:S(2)}) collective-permute-start(f32[8,128]{1,0:T(8,128)S(1)} %add.12), channel_id=1, source_target_pairs={{0,1},{1,0},{2,3},{3,2},{4,5},{5,4},{6,7},{7,6},{8,9},{9,8},{10,11... | collective-permute-start | bytes 12296 | tf_op jit(solution)/shard_map/ppermute | solution.py:674
  60.3 4.5 %collective-permute-start.18 = (f32[8,128]{1,0:T(8,128)S(1)}, f32[8,128]{1,0:T(8,128)S(1)}, u32[]{:S(2)}, u32[]{:S(2)}) collective-permute-start(f32[8,128]{1,0:T(8,128)S(1)} %add_add_fusion.rest_0_), channel_id=1, source_target_pairs={{0,24},{4,28},{8,16},{12,20},{16,8},{20,12},{24,0},{28,4},{1,25},{... | collective-permute-start | bytes 12296 | tf_op jit(solution)/shard_map/ppermute | solution.py:674
  61.2 3.6 %collective-permute-start.17 = (f32[8,128]{1,0:T(8,128)S(1)}, f32[8,128]{1,0:T(8,128)S(1)}, u32[]{:S(2)}, u32[]{:S(2)}) collective-permute-start(f32[8,128]{1,0:T(8,128)S(1)} %add_add_fusion.rest_0_), channel_id=1, source_target_pairs={{0,16},{4,20},{8,24},{12,28},{16,0},{20,4},{24,8},{28,12},{1,17},{... | collective-permute-start | bytes 12296 | tf_op jit(solution)/shard_map/ppermute | solution.py:674
  62.4 3.6 %collective-permute-start.16 = (f32[8,128]{1,0:T(8,128)S(1)}, f32[8,128]{1,0:T(8,128)S(1)}, u32[]{:S(2)}, u32[]{:S(2)}) collective-permute-start(f32[8,128]{1,0:T(8,128)S(1)} %add_add_fusion.rest_0_), channel_id=1, source_target_pairs={{0,8},{4,12},{8,0},{12,4},{16,24},{20,28},{24,16},{28,20},{1,9},{5... | collective-permute-start | bytes 12296 | tf_op jit(solution)/shard_map/ppermute | solution.py:674

commit v21 on v20

--- a/solution.py
+++ b/solution.py
@@ -691,8 +691,7 @@
     first = lax.ppermute(first, "piece", [(i, i ^ 1) for i in range(pieces)])
     axes = ("piece", "col")
     device = [(p, c) for p in range(pieces) for c in range(columns)]
-    partner = [(p + (1 if p % 2 else -1), c) for p, c in device]
-    partner = [(q, d) if 0 <= q < pieces else (p, c ^ 1) for (q, d), (p, c) in zip(partner, device)]
+    partner = [((p + (1 if p % 2 else -1)) % pieces, c) for p, c in device]
     second = lax.ppermute(second, axes, [(i, q * columns + d) for i, (q, d) in enumerate(partner)])
 
     col_steps = [(1 << k) | 1 for k in range(columns.bit_length() - 1)]

time: 67.1 us -> 67.4 us (level)
  starting transfers between devices: 27.7 us -> 29.3 us
  waiting for transfers between devices: 8.15 us -> 7.07 us
    ppermute x1, starting transfers between devices: 0.15 us -> 2.56 us  [body(): lax.ppermute(second, axes, [(i, q * columns + d) for i, (q, d) in enumera...]
    ppermute x9, starting transfers between devices: 15 us -> 14.1 us  [swap(): lax.ppermute(values, axis, [(i, i ^ step) for i in range(lax.axis_size(ax...]
    ppermute x9, waiting for transfers between devices: 7.73 us -> 7.05 us  [swap(): lax.ppermute(values, axis, [(i, i ^ step) for i in range(lax.axis_size(ax...]
  transfers between devices with their start and end apart: 19 -> 19, of which waited for: 7 -> 6; matrix products, arithmetic and copies ran while one was open for 0% -> 0% of each run, Pallas kernels for 28% -> 28%
where the time goes in v21:
time: 67.4 us; the launch traced here: 67.5 us
  Pallas kernels  30.4 us (45%)
  starting transfers between devices  29.3 us (43%)
  waiting for transfers between devices  7.07 us (10%)
  between operations  0.79 us (1%)
    pallas_call x8, Pallas kernels, call(): pl.pallas_call(kernel, out_shape=outs, in_specs=[SMEM] * scalars + [HBM]...  30.4 us
    ppermute x9, starting transfers between devices, swap(): lax.ppermute(values, axis, [(i, i ^ step) for i in range(lax.axis_size(ax...  14.1 us
    ppermute x8, starting transfers between devices, exchange(): return [lax.ppermute(field, axes, list(enumerate(to))) for to in swaps]  12.6 us
    ppermute x9, waiting for transfers between devices, swap(): lax.ppermute(values, axis, [(i, i ^ step) for i in range(lax.axis_size(ax...  7.05 us
    ppermute x1, starting transfers between devices, body(): lax.ppermute(second, axes, [(i, q * columns + d) for i, (q, d) in enumera...  2.56 us
  transfers between devices with their start and end apart: 19, of which 6 were waited for; matrix products, arithmetic and copies ran while one was open for 0% of the time, Pallas kernels for 28%

profile of v21, /device:TPU:0, one launch (start us, length us, event | category | flops | bytes accessed | tf_op | source)
XLA Modules:
  0.0 67.5 jit_solution(16970346623786550600)
XLA Ops:
  0.6 1.7 %prepare.1 = (s32[8]{0:T(128)S(4)}, s32[1480]{0:T(1024)S(4)}, f32[4,192,128]{2,1,0:T(8,128)S(1)}, f32[4,64,128]{2,1,0:T(8,128)S(1)}, f32[32,128]{1,0:T(8,128)S(1...) custom-call(s32[8]{0:T(128)} %counts.1, f32[3]{0:T(128)} %densities.1, ...), custom_call_target="tpu_custom_call" | custom-call | tf_op jit(solution)/shard_map/prepare/pallas_call | solution.py:661
  2.4 3.1 %collective-permute-start.2 = (s32[7,128]{1,0:T(8,128)S(1)}, s32[7,128]{1,0:T(8,128)S(1)}, u32[]{:S(2)}, u32[]{:S(2)}) collective-permute-start(s32[7,128]{1,0:T(8,128)S(1)} %get-tuple-element.51), channel_id=1, source_target_pairs={{0,1},{1,0},{2,3},{3,2},{4,5},{5,4},{6,7},{7,6},{8,9},{9,8},{10,11... | collective-permute-start | bytes 10760 | tf_op jit(solution)/shard_map/ppermute | solution.py:674
  5.4 0.0 collective-permute-start
  5.4 2.6 %collective-permute-start.1 = (f32[4,32,128]{2,1,0:T(8,128)S(1)}, f32[4,32,128]{2,1,0:T(8,128)S(1)}, u32[]{:S(2)}, u32[]{:S(2)}) collective-permute-start(f32[4,32,128]{2,1,0:T(8,128)S(1)} %get-tuple-element.42), channel_id=1, source_target_pairs={{0,28},{1,29},{2,30},{3,31},{4,8},{5,9},{6,10},{7,11},{8,4},{9,5},... | collective-permute-start | bytes 196616 | tf_op jit(solution)/shard_map/ppermute | solution.py:695
  8.0 0.0 collective-permute-done.2
  8.0 3.1 %collective-permute-start.3 = (s32[14,128]{1,0:T(8,128)S(1)}, s32[14,128]{1,0:T(8,128)S(1)}, u32[]{:S(2)}, u32[]{:S(2)}) collective-permute-start(s32[14,128]{1,0:T(8,128)S(1)} %pad_add_fusion.rest_0_), channel_id=1, source_target_pairs={{0,3},{1,2},{2,1},{3,0},{4,7},{5,6},{6,5},{7,4},{8,11},{9,10},{10,... | collective-permute-start | bytes 21512 | tf_op jit(solution)/shard_map/ppermute | solution.py:674
  11.1 10.3 %build_inner.1 = (s32[196]{0:T(256)S(4)}, s32[195]{0:T(256)S(4)}, f32[232,128,128]{2,1,0:T(8,128)S(1)}, bf16[2,32,128,128]{3,2,1,0:T(8,128)(2,1)S(1)}, f32[3,32,...) custom-call(s32[8]{0:T(128)S(4)} %get-tuple-element.35.meta, ...), custom_call_target="tpu_custom_call" | custom-call | flops 56623104 | tf_op jit(solution)/shard_map/build_inner/pallas_call | solution.py:661
  21.4 0.0 collective-permute-done.3.rest_1_
  21.4 0.0 collective-permute-done.first
  21.4 0.0 collective-permute-done.1.second
  21.4 4.4 %build_outer.1 = (s32[1]{0:T(128)S(4)}, f32[238,128,128]{2,1,0:T(8,128)S(1)}, f32[32,128]{1,0:T(8,128)S(1)}, f32[32,128]{1,0:T(8,128)S(1)}, f32[32,128]{1,0:T(8,128)S(1)}, /*index=5*/f32[32,128]{1,0:T(8,128)S(1)}) custom-call(s32[8]{0:T(128)S(4)} %get-tuple-element.35.meta, s32[1480]{0:T(1024)S(4)} %get-tuple-element.36.table, ...), custom_call_target="tpu_custom_call" | custom-call | flops 58195968 | tf_op jit(solution)/shard_map/build_outer/pallas_call | solution.py:661
  25.8 0.1 collective-permute-start.7
  25.9 3.7 %collective-permute-start.6 = (f32[32,128]{1,0:T(8,128)S(1)}, f32[32,128]{1,0:T(8,128)S(1)}, u32[]{:S(2)}, u32[]{:S(2)}) collective-permute-start(f32[32,128]{1,0:T(8,128)S(1)} %get-tuple-element.52.field.precond), channel_id=1, source_target_pairs={{0,2},{1,4},{2,6},{3,7},{4,1},{5,8},{6,0},{7,3},{8,5},{9,12},{10,1... | collective-permute-start | bytes 49160 | tf_op jit(solution)/shard_map/ppermute | solution.py:753
  29.6 0.7 collective-permute-start.5
  30.2 2.8 %collective-permute-start.4 = (f32[32,128]{1,0:T(8,128)S(1)}, f32[32,128]{1,0:T(8,128)S(1)}, u32[]{:S(2)}, u32[]{:S(2)}) collective-permute-start(f32[32,128]{1,0:T(8,128)S(1)} %get-tuple-element.52.field.precond), channel_id=1, source_target_pairs={{0,1},{1,0},{2,3},{3,2},{4,5},{5,4},{6,7},{7,6},{8,9},{9,8},{10,11... | collective-permute-start | bytes 49160 | tf_op jit(solution)/shard_map/ppermute | solution.py:753
  33.1 4.3 %apply_inner.2 = (f32[32,128,128]{2,1,0:T(8,128)S(1)}, f32[256,128]{1,0:T(8,128)S(1)}) custom-call(s32[8]{0:T(128)S(4)} %get-tuple-element.35.meta, s32[1480]{0:T(1024)S(4)} %get-tuple-element.36.table, s32[196]{0:T(256)S(4)} %get-tuple-element.38.plan, s32[1]{0:T(128)S(4)} %get-tuple-element.53.again, f32[32,128]{1,0:T(8,128)S(1)} %get-tuple-element.52.field.precond, ...), custom_call_target="tpu_custom_call" | custom-call | flops 14155776 | tf_op jit(solution)/shard_map/apply_inner/pallas_call | solution.py:661
  37.4 0.0 collective-permute-done.7.rest_3_
  37.4 0.0 collective-permute-done.6.rest_2_
  37.4 0.0 collective-permute-done.5.rest_1_
  37.4 0.0 collective-permute-done.4.rest_0_
  37.4 2.2 %apply_first.1 = (f32[32,128]{1,0:T(8,128)S(1)}, f32[32,128]{1,0:T(8,128)S(1)}) custom-call(s32[8]{0:T(128)S(4)} %get-tuple-element.35.meta, s32[1480]{0:T(1024)S(4)} %get-tuple-element.36.table, s32[196]{0:T(256)S(4)} %get-tuple-element.38.plan, s32[1]{0:T(128)S(4)} %get-tuple-element.53.again, f32[32,128]{1,0:T(8,128)S(1)} %get-tuple-element.54.diagonal, ...), custom_call_target="tpu_custom_call" | custom-call | flops 7274496 | tf_op jit(solution)/shard_map/apply_first/pallas_call | solution.py:661
  39.6 0.1 collective-permute-start.11
  39.7 2.6 %collective-permute-start.10 = (f32[32,128]{1,0:T(8,128)S(1)}, f32[32,128]{1,0:T(8,128)S(1)}, u32[]{:S(2)}, u32[]{:S(2)}) collective-permute-start(f32[32,128]{1,0:T(8,128)S(1)} %get-tuple-element.61.field.scaled), channel_id=1, source_target_pairs={{0,2},{1,4},{2,6},{3,7},{4,1},{5,8},{6,0},{7,3},{8,5},{9,12},{10,1... | collective-permute-start | bytes 49160 | tf_op jit(solution)/shard_map/ppermute | solution.py:753
  42.3 2.6 %collective-permute-start.9 = (f32[32,128]{1,0:T(8,128)S(1)}, f32[32,128]{1,0:T(8,128)S(1)}, u32[]{:S(2)}, u32[]{:S(2)}) collective-permute-start(f32[32,128]{1,0:T(8,128)S(1)} %get-tuple-element.61.field.scaled), channel_id=1, source_target_pairs={{0,31},{1,2},{2,1},{3,4},{4,3},{5,6},{6,5},{7,8},{8,7},{9,10},{10,... | collective-permute-start | bytes 49160 | tf_op jit(solution)/shard_map/ppermute | solution.py:753
  44.8 0.1 collective-permute-start.8
  44.9 4.3 %apply_inner.3 = (f32[32,128,128]{2,1,0:T(8,128)S(1)}, f32[256,128]{1,0:T(8,128)S(1)}) custom-call(s32[8]{0:T(128)S(4)} %get-tuple-element.35.meta, s32[1480]{0:T(1024)S(4)} %get-tuple-element.36.table, s32[196]{0:T(256)S(4)} %get-tuple-element.38.plan, s32[1]{0:T(128)S(4)} %get-tuple-element.53.again, f32[32,128]{1,0:T(8,128)S(1)} %get-tuple-element.61.field.scaled, ...), custom_call_target="tpu_custom_call" | custom-call | flops 14155776 | tf_op jit(solution)/shard_map/apply_inner/pallas_call | solution.py:661
  49.2 0.0 collective-permute-done.11.rest_3_
  49.2 0.0 collective-permute-done.10.rest_2_
  49.3 0.0 collective-permute-done.9.rest_1_
  49.3 0.0 collective-permute-done.8.rest_0_
  49.3 2.3 %apply_second.1 = (f32[32,128]{1,0:T(8,128)S(1)}, f32[8,128]{1,0:T(8,128)S(1)}) custom-call(s32[8]{0:T(128)S(4)} %get-tuple-element.35.meta, s32[1480]{0:T(1024)S(4)} %get-tuple-element.36.table, s32[196]{0:T(256)S(4)} %get-tuple-element.38.plan, s32[1]{0:T(128)S(4)} %get-tuple-element.53.again, f32[32,128]{1,0:T(8,128)S(1)} %get-tuple-element.34.source, ...), custom_call_target="tpu_custom_call" | custom-call | flops 7274496 | tf_op jit(solution)/shard_map/apply_second/pallas_call | solution.py:661
  51.5 0.1 collective-permute-start.12
  51.6 1.1 %collective-permute-done.12 = f32[8,128]{1,0:T(8,128)S(1)} collective-permute-done((f32[8,128]{1,0:T(8,128)S(1)}, f32[8,128]{1,0:T(8,128)S(1)}, u32[]{:S(2)}, u32[]{:S(2)}) %collective-permute-start.12) | collective-permute-done | bytes 4128 | tf_op jit(solution)/shard_map/ppermute | solution.py:674
  52.7 0.4 collective-permute-start.15
  53.1 3.6 %collective-permute-start.14 = (f32[8,128]{1,0:T(8,128)S(1)}, f32[8,128]{1,0:T(8,128)S(1)}, u32[]{:S(2)}, u32[]{:S(2)}) collective-permute-start(f32[8,128]{1,0:T(8,128)S(1)} %add.12), channel_id=1, source_target_pairs={{0,2},{1,3},{2,0},{3,1},{4,6},{5,7},{6,4},{7,5},{8,10},{9,11},{10,... | collective-permute-start | bytes 12296 | tf_op jit(solution)/shard_map/ppermute | solution.py:674
  56.8 0.3 collective-permute-start.13
  57.1 1.0 %collective-permute-done.15 = f32[8,128]{1,0:T(8,128)S(1)} collective-permute-done((f32[8,128]{1,0:T(8,128)S(1)}, f32[8,128]{1,0:T(8,128)S(1)}, u32[]{:S(2)}, u32[]{:S(2)}) %collective-permute-start.15) | collective-permute-done | bytes 4128 | tf_op jit(solution)/shard_map/ppermute | solution.py:674
  58.1 0.3 collective-permute-done.14
  58.4 2.0 %collective-permute-done.13 = f32[8,128]{1,0:T(8,128)S(1)} collective-permute-done((f32[8,128]{1,0:T(8,128)S(1)}, f32[8,128]{1,0:T(8,128)S(1)}, u32[]{:S(2)}, u32[]{:S(2)}) %collective-permute-start.13) | collective-permute-done | bytes 4128 | tf_op jit(solution)/shard_map/ppermute | solution.py:674
  60.4 0.2 collective-permute-start.18
  60.6 2.3 %collective-permute-start.17 = (f32[8,128]{1,0:T(8,128)S(1)}, f32[8,128]{1,0:T(8,128)S(1)}, u32[]{:S(2)}, u32[]{:S(2)}) collective-permute-start(f32[8,128]{1,0:T(8,128)S(1)} %add_add_fusion.rest_0_), channel_id=1, source_target_pairs={{0,16},{4,20},{8,24},{12,28},{16,0},{20,4},{24,8},{28,12},{1,17},{... | collective-permute-start | bytes 12296 | tf_op jit(solution)/shard_map/ppermute | solution.py:674
  63.0 0.9 %collective-permute-start.16 = (f32[8,128]{1,0:T(8,128)S(1)}, f32[8,128]{1,0:T(8,128)S(1)}, u32[]{:S(2)}, u32[]{:S(2)}) collective-permute-start(f32[8,128]{1,0:T(8,128)S(1)} %add_add_fusion.rest_0_), channel_id=1, source_target_pairs={{0,8},{4,12},{8,0},{12,4},{16,24},{20,28},{24,16},{28,20},{1,9},{5... | collective-permute-start | bytes 12296 | tf_op jit(solution)/shard_map/ppermute | solution.py:674
  63.9 1.0 %collective-permute-done.18.rest_3_ = f32[8,128]{1,0:T(8,128)S(1)} collective-permute-done((f32[8,128]{1,0:T(8,128)S(1)}, f32[8,128]{1,0:T(8,128)S(1)}, u32[]{:S(2)}, u32[]{:S(2)}) %collective-permute-start.18) | collective-permute-done | bytes 4128 | tf_op jit(solution)/shard_map/ppermute | solution.py:674
  64.9 0.0 collective-permute-done.17.rest_2_
  64.9 1.7 %collective-permute-done.16.rest_1_ = f32[8,128]{1,0:T(8,128)S(1)} collective-permute-done((f32[8,128]{1,0:T(8,128)S(1)}, f32[8,128]{1,0:T(8,128)S(1)}, u32[]{:S(2)}, u32[]{:S(2)}) %collective-permute-start.16) | collective-permute-done | bytes 4128 | tf_op jit(solution)/shard_map/ppermute | solution.py:674
  66.6 0.9 %finish.1 = (f32[32,128]{1,0:T(8,128)}, f32[32,128]{1,0:T(8,128)}) custom-call(f32[32,128]{1,0:T(8,128)S(1)} %get-tuple-element.34.source, f32[32,128]{1,0:T(8,128)S(1)} %get-tuple-element.52.field.precond, f32[32,128]{1,0:T(8,128)S(1)} %get-tuple-element.60.spill, f32[32,128]{1,0:T(8,128)S(1)} %get-tuple-element.61.field.scaled, ...), custom_call_target="tpu_custom_call" | custom-call | tf_op jit(solution)/shard_map/finish/pallas_call | solution.py:661
  (3 shorter events, 0.0 us)
Async XLA Ops:
  2.4 5.7 %collective-permute-start.2 = (s32[7,128]{1,0:T(8,128)S(1)}, s32[7,128]{1,0:T(8,128)S(1)}, u32[]{:S(2)}, u32[]{:S(2)}) collective-permute-start(s32[7,128]{1,0:T(8,128)S(1)} %get-tuple-element.51), channel_id=1, source_target_pairs={{0,1},{1,0},{2,3},{3,2},{4,5},{5,4},{6,7},{7,6},{8,9},{9,8},{10,11... | collective-permute-start | bytes 10760 | tf_op jit(solution)/shard_map/ppermute | solution.py:674
  5.4 15.9 %collective-permute-start = (f32[4,32,128]{2,1,0:T(8,128)S(1)}, f32[4,32,128]{2,1,0:T(8,128)S(1)}, u32[]{:S(2)}, u32[]{:S(2)}) collective-permute-start(f32[4,32,128]{2,1,0:T(8,128)S(1)} %get-tuple-element.41), channel_id=1, source_target_pairs={{0,4},{4,0},{8,12},{12,8},{16,20},{20,16},{24,28},{28,24},{1,5},{5... | collective-permute-start | bytes 196616 | tf_op jit(solution)/shard_map/ppermute | solution.py:691
  5.4 15.9 %collective-permute-start.1 = (f32[4,32,128]{2,1,0:T(8,128)S(1)}, f32[4,32,128]{2,1,0:T(8,128)S(1)}, u32[]{:S(2)}, u32[]{:S(2)}) collective-permute-start(f32[4,32,128]{2,1,0:T(8,128)S(1)} %get-tuple-element.42), channel_id=1, source_target_pairs={{0,28},{1,29},{2,30},{3,31},{4,8},{5,9},{6,10},{7,11},{8,4},{9,5},... | collective-permute-start | bytes 196616 | tf_op jit(solution)/shard_map/ppermute | solution.py:695
  8.0 13.3 %collective-permute-start.3 = (s32[14,128]{1,0:T(8,128)S(1)}, s32[14,128]{1,0:T(8,128)S(1)}, u32[]{:S(2)}, u32[]{:S(2)}) collective-permute-start(s32[14,128]{1,0:T(8,128)S(1)} %pad_add_fusion.rest_0_), channel_id=1, source_target_pairs={{0,3},{1,2},{2,1},{3,0},{4,7},{5,6},{6,5},{7,4},{8,11},{9,10},{10,... | collective-permute-start | bytes 21512 | tf_op jit(solution)/shard_map/ppermute | solution.py:674
  25.8 11.6 %collective-permute-start.7 = (f32[32,128]{1,0:T(8,128)S(1)}, f32[32,128]{1,0:T(8,128)S(1)}, u32[]{:S(2)}, u32[]{:S(2)}) collective-permute-start(f32[32,128]{1,0:T(8,128)S(1)} %get-tuple-element.52.field.precond), channel_id=1, source_target_pairs={{0,3},{1,5},{2,4},{3,7},{4,2},{5,1},{6,8},{7,0},{8,6},{9,13},{10,1... | collective-permute-start | bytes 49160 | tf_op jit(solution)/shard_map/ppermute | solution.py:753
  25.9 11.5 %collective-permute-start.6 = (f32[32,128]{1,0:T(8,128)S(1)}, f32[32,128]{1,0:T(8,128)S(1)}, u32[]{:S(2)}, u32[]{:S(2)}) collective-permute-start(f32[32,128]{1,0:T(8,128)S(1)} %get-tuple-element.52.field.precond), channel_id=1, source_target_pairs={{0,2},{1,4},{2,6},{3,7},{4,1},{5,8},{6,0},{7,3},{8,5},{9,12},{10,1... | collective-permute-start | bytes 49160 | tf_op jit(solution)/shard_map/ppermute | solution.py:753
  29.6 7.8 %collective-permute-start.5 = (f32[32,128]{1,0:T(8,128)S(1)}, f32[32,128]{1,0:T(8,128)S(1)}, u32[]{:S(2)}, u32[]{:S(2)}) collective-permute-start(f32[32,128]{1,0:T(8,128)S(1)} %get-tuple-element.52.field.precond), channel_id=1, source_target_pairs={{0,31},{1,2},{2,1},{3,4},{4,3},{5,6},{6,5},{7,8},{8,7},{9,10},{10,... | collective-permute-start | bytes 49160 | tf_op jit(solution)/shard_map/ppermute | solution.py:753
  30.2 7.2 %collective-permute-start.4 = (f32[32,128]{1,0:T(8,128)S(1)}, f32[32,128]{1,0:T(8,128)S(1)}, u32[]{:S(2)}, u32[]{:S(2)}) collective-permute-start(f32[32,128]{1,0:T(8,128)S(1)} %get-tuple-element.52.field.precond), channel_id=1, source_target_pairs={{0,1},{1,0},{2,3},{3,2},{4,5},{5,4},{6,7},{7,6},{8,9},{9,8},{10,11... | collective-permute-start | bytes 49160 | tf_op jit(solution)/shard_map/ppermute | solution.py:753
  39.6 9.6 %collective-permute-start.11 = (f32[32,128]{1,0:T(8,128)S(1)}, f32[32,128]{1,0:T(8,128)S(1)}, u32[]{:S(2)}, u32[]{:S(2)}) collective-permute-start(f32[32,128]{1,0:T(8,128)S(1)} %get-tuple-element.61.field.scaled), channel_id=1, source_target_pairs={{0,3},{1,5},{2,4},{3,7},{4,2},{5,1},{6,8},{7,0},{8,6},{9,13},{10,1... | collective-permute-start | bytes 49160 | tf_op jit(solution)/shard_map/ppermute | solution.py:753
  39.7 9.6 %collective-permute-start.10 = (f32[32,128]{1,0:T(8,128)S(1)}, f32[32,128]{1,0:T(8,128)S(1)}, u32[]{:S(2)}, u32[]{:S(2)}) collective-permute-start(f32[32,128]{1,0:T(8,128)S(1)} %get-tuple-element.61.field.scaled), channel_id=1, source_target_pairs={{0,2},{1,4},{2,6},{3,7},{4,1},{5,8},{6,0},{7,3},{8,5},{9,12},{10,1... | collective-permute-start | bytes 49160 | tf_op jit(solution)/shard_map/ppermute | solution.py:753
  42.3 7.0 %collective-permute-start.9 = (f32[32,128]{1,0:T(8,128)S(1)}, f32[32,128]{1,0:T(8,128)S(1)}, u32[]{:S(2)}, u32[]{:S(2)}) collective-permute-start(f32[32,128]{1,0:T(8,128)S(1)} %get-tuple-element.61.field.scaled), channel_id=1, source_target_pairs={{0,31},{1,2},{2,1},{3,4},{4,3},{5,6},{6,5},{7,8},{8,7},{9,10},{10,... | collective-permute-start | bytes 49160 | tf_op jit(solution)/shard_map/ppermute | solution.py:753
  44.8 4.4 %collective-permute-start.8 = (f32[32,128]{1,0:T(8,128)S(1)}, f32[32,128]{1,0:T(8,128)S(1)}, u32[]{:S(2)}, u32[]{:S(2)}) collective-permute-start(f32[32,128]{1,0:T(8,128)S(1)} %get-tuple-element.61.field.scaled), channel_id=1, source_target_pairs={{0,1},{1,0},{2,3},{3,2},{4,5},{5,4},{6,7},{7,6},{8,9},{9,8},{10,11... | collective-permute-start | bytes 49160 | tf_op jit(solution)/shard_map/ppermute | solution.py:753
  51.5 1.2 %collective-permute-start.12 = (f32[8,128]{1,0:T(8,128)S(1)}, f32[8,128]{1,0:T(8,128)S(1)}, u32[]{:S(2)}, u32[]{:S(2)}) collective-permute-start(f32[8,128]{1,0:T(8,128)S(1)} %get-tuple-element.65), channel_id=1, source_target_pairs={{0,4},{4,0},{8,12},{12,8},{16,20},{20,16},{24,28},{28,24},{1,5},{5... | collective-permute-start | bytes 12296 | tf_op jit(solution)/shard_map/ppermute | solution.py:674
  52.7 5.4 %collective-permute-start.15 = (f32[8,128]{1,0:T(8,128)S(1)}, f32[8,128]{1,0:T(8,128)S(1)}, u32[]{:S(2)}, u32[]{:S(2)}) collective-permute-start(f32[8,128]{1,0:T(8,128)S(1)} %add.12), channel_id=1, source_target_pairs={{0,3},{1,2},{2,1},{3,0},{4,7},{5,6},{6,5},{7,4},{8,11},{9,10},{10,... | collective-permute-start | bytes 12296 | tf_op jit(solution)/shard_map/ppermute | solution.py:674
  53.1 5.3 %collective-permute-start.14 = (f32[8,128]{1,0:T(8,128)S(1)}, f32[8,128]{1,0:T(8,128)S(1)}, u32[]{:S(2)}, u32[]{:S(2)}) collective-permute-start(f32[8,128]{1,0:T(8,128)S(1)} %add.12), channel_id=1, source_target_pairs={{0,2},{1,3},{2,0},{3,1},{4,6},{5,7},{6,4},{7,5},{8,10},{9,11},{10,... | collective-permute-start | bytes 12296 | tf_op jit(solution)/shard_map/ppermute | solution.py:674
  56.8 3.6 %collective-permute-start.13 = (f32[8,128]{1,0:T(8,128)S(1)}, f32[8,128]{1,0:T(8,128)S(1)}, u32[]{:S(2)}, u32[]{:S(2)}) collective-permute-start(f32[8,128]{1,0:T(8,128)S(1)} %add.12), channel_id=1, source_target_pairs={{0,1},{1,0},{2,3},{3,2},{4,5},{5,4},{6,7},{7,6},{8,9},{9,8},{10,11... | collective-permute-start | bytes 12296 | tf_op jit(solution)/shard_map/ppermute | solution.py:674
  60.4 4.5 %collective-permute-start.18 = (f32[8,128]{1,0:T(8,128)S(1)}, f32[8,128]{1,0:T(8,128)S(1)}, u32[]{:S(2)}, u32[]{:S(2)}) collective-permute-start(f32[8,128]{1,0:T(8,128)S(1)} %add_add_fusion.rest_0_), channel_id=1, source_target_pairs={{0,24},{4,28},{8,16},{12,20},{16,8},{20,12},{24,0},{28,4},{1,25},{... | collective-permute-start | bytes 12296 | tf_op jit(solution)/shard_map/ppermute | solution.py:674
  60.6 4.3 %collective-permute-start.17 = (f32[8,128]{1,0:T(8,128)S(1)}, f32[8,128]{1,0:T(8,128)S(1)}, u32[]{:S(2)}, u32[]{:S(2)}) collective-permute-start(f32[8,128]{1,0:T(8,128)S(1)} %add_add_fusion.rest_0_), channel_id=1, source_target_pairs={{0,16},{4,20},{8,24},{12,28},{16,0},{20,4},{24,8},{28,12},{1,17},{... | collective-permute-start | bytes 12296 | tf_op jit(solution)/shard_map/ppermute | solution.py:674
  63.0 3.6 %collective-permute-start.16 = (f32[8,128]{1,0:T(8,128)S(1)}, f32[8,128]{1,0:T(8,128)S(1)}, u32[]{:S(2)}, u32[]{:S(2)}) collective-permute-start(f32[8,128]{1,0:T(8,128)S(1)} %add_add_fusion.rest_0_), channel_id=1, source_target_pairs={{0,8},{4,12},{8,0},{12,4},{16,24},{20,28},{24,16},{28,20},{1,9},{5... | collective-permute-start | bytes 12296 | tf_op jit(solution)/shard_map/ppermute | solution.py:674

commit v22 on v21

--- a/solution.py
+++ b/solution.py
@@ -197,7 +197,7 @@
     return jnp.concatenate([front, front, back, ones, rest], 0)
 
 
-GROUP = 8
+GROUP = 10
 
 
 def flat_tiles(count, runs, most, table, sides, middles, weights, other_at, buffers, tiles, rows_ref, cols_ref):

time: 67.4 us -> 68.3 us (1.013)
  starting transfers between devices: 29.3 us -> 30.5 us
  waiting for transfers between devices: 7.07 us -> 6.36 us
    ppermute x8, starting transfers between devices: 12.6 us -> 13.8 us  [exchange(): return [lax.ppermute(field, axes, list(enumerate(to))) for to in swaps]]
    ppermute x9, waiting for transfers between devices: 7.05 us -> 6.34 us  [swap(): lax.ppermute(values, axis, [(i, i ^ step) for i in range(lax.axis_size(ax...]
  transfers between devices with their start and end apart: 19 -> 19, of which waited for: 6 -> 7; matrix products, arithmetic and copies ran while one was open for 0% -> 0% of each run, Pallas kernels for 28% -> 28%
where the time goes in v22:
time: 68.3 us; the launch traced here: 68.1 us
  Pallas kernels  30.5 us (45%)
  starting transfers between devices  30.5 us (45%)
  waiting for transfers between devices  6.36 us (9%)
  between operations  0.77 us (1%)
    pallas_call x8, Pallas kernels, call(): pl.pallas_call(kernel, out_shape=outs, in_specs=[SMEM] * scalars + [HBM]...  30.5 us
    ppermute x9, starting transfers between devices, swap(): lax.ppermute(values, axis, [(i, i ^ step) for i in range(lax.axis_size(ax...  14.1 us
    ppermute x8, starting transfers between devices, exchange(): return [lax.ppermute(field, axes, list(enumerate(to))) for to in swaps]  13.8 us
    ppermute x9, waiting for transfers between devices, swap(): lax.ppermute(values, axis, [(i, i ^ step) for i in range(lax.axis_size(ax...  6.34 us
    ppermute x1, starting transfers between devices, body(): lax.ppermute(second, axes, [(i, q * columns + d) for i, (q, d) in enumera...  2.56 us
  transfers between devices with their start and end apart: 19, of which 7 were waited for; matrix products, arithmetic and copies ran while one was open for 0% of the time, Pallas kernels for 28%

profile of v22, /device:TPU:0, one launch (start us, length us, event | category | flops | bytes accessed | tf_op | source)
XLA Modules:
  0.0 68.1 jit_solution(17954986895116096749)
XLA Ops:
  0.6 1.7 %prepare.1 = (s32[8]{0:T(128)S(4)}, s32[1480]{0:T(1024)S(4)}, f32[4,192,128]{2,1,0:T(8,128)S(1)}, f32[4,64,128]{2,1,0:T(8,128)S(1)}, f32[32,128]{1,0:T(8,128)S(1...) custom-call(s32[8]{0:T(128)} %counts.1, f32[3]{0:T(128)} %densities.1, ...), custom_call_target="tpu_custom_call" | custom-call | tf_op jit(solution)/shard_map/prepare/pallas_call | solution.py:661
  2.4 3.1 %collective-permute-start.2 = (s32[7,128]{1,0:T(8,128)S(1)}, s32[7,128]{1,0:T(8,128)S(1)}, u32[]{:S(2)}, u32[]{:S(2)}) collective-permute-start(s32[7,128]{1,0:T(8,128)S(1)} %get-tuple-element.51), channel_id=1, source_target_pairs={{0,1},{1,0},{2,3},{3,2},{4,5},{5,4},{6,7},{7,6},{8,9},{9,8},{10,11... | collective-permute-start | bytes 10760 | tf_op jit(solution)/shard_map/ppermute | solution.py:674
  5.4 0.0 collective-permute-start
  5.4 2.6 %collective-permute-start.1 = (f32[4,32,128]{2,1,0:T(8,128)S(1)}, f32[4,32,128]{2,1,0:T(8,128)S(1)}, u32[]{:S(2)}, u32[]{:S(2)}) collective-permute-start(f32[4,32,128]{2,1,0:T(8,128)S(1)} %get-tuple-element.42), channel_id=1, source_target_pairs={{0,28},{1,29},{2,30},{3,31},{4,8},{5,9},{6,10},{7,11},{8,4},{9,5},... | collective-permute-start | bytes 196616 | tf_op jit(solution)/shard_map/ppermute | solution.py:695
  8.0 0.0 collective-permute-done.2
  8.0 3.1 %collective-permute-start.3 = (s32[14,128]{1,0:T(8,128)S(1)}, s32[14,128]{1,0:T(8,128)S(1)}, u32[]{:S(2)}, u32[]{:S(2)}) collective-permute-start(s32[14,128]{1,0:T(8,128)S(1)} %pad_add_fusion.rest_0_), channel_id=1, source_target_pairs={{0,3},{1,2},{2,1},{3,0},{4,7},{5,6},{6,5},{7,4},{8,11},{9,10},{10,... | collective-permute-start | bytes 21512 | tf_op jit(solution)/shard_map/ppermute | solution.py:674
  11.1 10.3 %build_inner.1 = (s32[196]{0:T(256)S(4)}, s32[195]{0:T(256)S(4)}, f32[236,128,128]{2,1,0:T(8,128)S(1)}, bf16[2,32,128,128]{3,2,1,0:T(8,128)(2,1)S(1)}, f32[3,32,...) custom-call(s32[8]{0:T(128)S(4)} %get-tuple-element.35.meta, ...), custom_call_target="tpu_custom_call" | custom-call | flops 56623104 | tf_op jit(solution)/shard_map/build_inner/pallas_call | solution.py:661
  21.4 0.0 collective-permute-done.3.rest_1_
  21.4 0.0 collective-permute-done.first
  21.4 0.0 collective-permute-done.1.second
  21.5 4.4 %build_outer.1 = (s32[1]{0:T(128)S(4)}, f32[242,128,128]{2,1,0:T(8,128)S(1)}, f32[32,128]{1,0:T(8,128)S(1)}, f32[32,128]{1,0:T(8,128)S(1)}, f32[32,128]{1,0:T(8,128)S(1)}, /*index=5*/f32[32,128]{1,0:T(8,128)S(1)}) custom-call(s32[8]{0:T(128)S(4)} %get-tuple-element.35.meta, s32[1480]{0:T(1024)S(4)} %get-tuple-element.36.table, ...), custom_call_target="tpu_custom_call" | custom-call | flops 58195968 | tf_op jit(solution)/shard_map/build_outer/pallas_call | solution.py:661
  25.9 4.1 %collective-permute-start.7 = (f32[32,128]{1,0:T(8,128)S(1)}, f32[32,128]{1,0:T(8,128)S(1)}, u32[]{:S(2)}, u32[]{:S(2)}) collective-permute-start(f32[32,128]{1,0:T(8,128)S(1)} %get-tuple-element.52.field.precond), channel_id=1, source_target_pairs={{0,3},{1,5},{2,4},{3,7},{4,2},{5,1},{6,8},{7,0},{8,6},{9,13},{10,1... | collective-permute-start | bytes 49160 | tf_op jit(solution)/shard_map/ppermute | solution.py:753
  30.0 0.1 collective-permute-start.6
  30.1 0.8 %collective-permute-start.5 = (f32[32,128]{1,0:T(8,128)S(1)}, f32[32,128]{1,0:T(8,128)S(1)}, u32[]{:S(2)}, u32[]{:S(2)}) collective-permute-start(f32[32,128]{1,0:T(8,128)S(1)} %get-tuple-element.52.field.precond), channel_id=1, source_target_pairs={{0,31},{1,2},{2,1},{3,4},{4,3},{5,6},{6,5},{7,8},{8,7},{9,10},{10,... | collective-permute-start | bytes 49160 | tf_op jit(solution)/shard_map/ppermute | solution.py:753
  30.9 3.5 %collective-permute-start.4 = (f32[32,128]{1,0:T(8,128)S(1)}, f32[32,128]{1,0:T(8,128)S(1)}, u32[]{:S(2)}, u32[]{:S(2)}) collective-permute-start(f32[32,128]{1,0:T(8,128)S(1)} %get-tuple-element.52.field.precond), channel_id=1, source_target_pairs={{0,1},{1,0},{2,3},{3,2},{4,5},{5,4},{6,7},{7,6},{8,9},{9,8},{10,11... | collective-permute-start | bytes 49160 | tf_op jit(solution)/shard_map/ppermute | solution.py:753
  34.4 4.3 %apply_inner.2 = (f32[32,128,128]{2,1,0:T(8,128)S(1)}, f32[256,128]{1,0:T(8,128)S(1)}) custom-call(s32[8]{0:T(128)S(4)} %get-tuple-element.35.meta, s32[1480]{0:T(1024)S(4)} %get-tuple-element.36.table, s32[196]{0:T(256)S(4)} %get-tuple-element.38.plan, s32[1]{0:T(128)S(4)} %get-tuple-element.53.again, f32[32,128]{1,0:T(8,128)S(1)} %get-tuple-element.52.field.precond, ...), custom_call_target="tpu_custom_call" | custom-call | flops 14155776 | tf_op jit(solution)/shard_map/apply_inner/pallas_call | solution.py:661
  38.7 0.0 collective-permute-done.7.rest_3_
  38.7 0.0 collective-permute-done.6.rest_2_
  38.7 0.0 collective-permute-done.5.rest_1_
  38.7 0.0 collective-permute-done.4.rest_0_
  38.7 2.2 %apply_first.1 = (f32[32,128]{1,0:T(8,128)S(1)}, f32[32,128]{1,0:T(8,128)S(1)}) custom-call(s32[8]{0:T(128)S(4)} %get-tuple-element.35.meta, s32[1480]{0:T(1024)S(4)} %get-tuple-element.36.table, s32[196]{0:T(256)S(4)} %get-tuple-element.38.plan, s32[1]{0:T(128)S(4)} %get-tuple-element.53.again, f32[32,128]{1,0:T(8,128)S(1)} %get-tuple-element.54.diagonal, ...), custom_call_target="tpu_custom_call" | custom-call | flops 7274496 | tf_op jit(solution)/shard_map/apply_first/pallas_call | solution.py:661
  40.9 1.6 %collective-permute-start.11 = (f32[32,128]{1,0:T(8,128)S(1)}, f32[32,128]{1,0:T(8,128)S(1)}, u32[]{:S(2)}, u32[]{:S(2)}) collective-permute-start(f32[32,128]{1,0:T(8,128)S(1)} %get-tuple-element.61.field.scaled), channel_id=1, source_target_pairs={{0,3},{1,5},{2,4},{3,7},{4,2},{5,1},{6,8},{7,0},{8,6},{9,13},{10,1... | collective-permute-start | bytes 49160 | tf_op jit(solution)/shard_map/ppermute | solution.py:753
  42.5 1.1 %collective-permute-start.10 = (f32[32,128]{1,0:T(8,128)S(1)}, f32[32,128]{1,0:T(8,128)S(1)}, u32[]{:S(2)}, u32[]{:S(2)}) collective-permute-start(f32[32,128]{1,0:T(8,128)S(1)} %get-tuple-element.61.field.scaled), channel_id=1, source_target_pairs={{0,2},{1,4},{2,6},{3,7},{4,1},{5,8},{6,0},{7,3},{8,5},{9,12},{10,1... | collective-permute-start | bytes 49160 | tf_op jit(solution)/shard_map/ppermute | solution.py:753
  43.6 1.7 %collective-permute-start.9 = (f32[32,128]{1,0:T(8,128)S(1)}, f32[32,128]{1,0:T(8,128)S(1)}, u32[]{:S(2)}, u32[]{:S(2)}) collective-permute-start(f32[32,128]{1,0:T(8,128)S(1)} %get-tuple-element.61.field.scaled), channel_id=1, source_target_pairs={{0,31},{1,2},{2,1},{3,4},{4,3},{5,6},{6,5},{7,8},{8,7},{9,10},{10,... | collective-permute-start | bytes 49160 | tf_op jit(solution)/shard_map/ppermute | solution.py:753
  45.3 0.9 %collective-permute-start.8 = (f32[32,128]{1,0:T(8,128)S(1)}, f32[32,128]{1,0:T(8,128)S(1)}, u32[]{:S(2)}, u32[]{:S(2)}) collective-permute-start(f32[32,128]{1,0:T(8,128)S(1)} %get-tuple-element.61.field.scaled), channel_id=1, source_target_pairs={{0,1},{1,0},{2,3},{3,2},{4,5},{5,4},{6,7},{7,6},{8,9},{9,8},{10,11... | collective-permute-start | bytes 49160 | tf_op jit(solution)/shard_map/ppermute | solution.py:753
  46.2 4.3 %apply_inner.3 = (f32[32,128,128]{2,1,0:T(8,128)S(1)}, f32[256,128]{1,0:T(8,128)S(1)}) custom-call(s32[8]{0:T(128)S(4)} %get-tuple-element.35.meta, s32[1480]{0:T(1024)S(4)} %get-tuple-element.36.table, s32[196]{0:T(256)S(4)} %get-tuple-element.38.plan, s32[1]{0:T(128)S(4)} %get-tuple-element.53.again, f32[32,128]{1,0:T(8,128)S(1)} %get-tuple-element.61.field.scaled, ...), custom_call_target="tpu_custom_call" | custom-call | flops 14155776 | tf_op jit(solution)/shard_map/apply_inner/pallas_call | solution.py:661
  50.5 0.0 collective-permute-done.11.rest_3_
  50.5 0.0 collective-permute-done.10.rest_2_
  50.5 0.0 collective-permute-done.9.rest_1_
  50.5 0.0 collective-permute-done.8.rest_0_
  50.5 2.3 %apply_second.1 = (f32[32,128]{1,0:T(8,128)S(1)}, f32[8,128]{1,0:T(8,128)S(1)}) custom-call(s32[8]{0:T(128)S(4)} %get-tuple-element.35.meta, s32[1480]{0:T(1024)S(4)} %get-tuple-element.36.table, s32[196]{0:T(256)S(4)} %get-tuple-element.38.plan, s32[1]{0:T(128)S(4)} %get-tuple-element.53.again, f32[32,128]{1,0:T(8,128)S(1)} %get-tuple-element.34.source, ...), custom_call_target="tpu_custom_call" | custom-call | flops 7274496 | tf_op jit(solution)/shard_map/apply_second/pallas_call | solution.py:661
  52.8 0.1 collective-permute-start.12
  52.9 1.1 %collective-permute-done.12 = f32[8,128]{1,0:T(8,128)S(1)} collective-permute-done((f32[8,128]{1,0:T(8,128)S(1)}, f32[8,128]{1,0:T(8,128)S(1)}, u32[]{:S(2)}, u32[]{:S(2)}) %collective-permute-start.12) | collective-permute-done | bytes 4128 | tf_op jit(solution)/shard_map/ppermute | solution.py:674
  54.0 1.6 %collective-permute-start.15 = (f32[8,128]{1,0:T(8,128)S(1)}, f32[8,128]{1,0:T(8,128)S(1)}, u32[]{:S(2)}, u32[]{:S(2)}) collective-permute-start(f32[8,128]{1,0:T(8,128)S(1)} %add.12), channel_id=1, source_target_pairs={{0,3},{1,2},{2,1},{3,0},{4,7},{5,6},{6,5},{7,4},{8,11},{9,10},{10,... | collective-permute-start | bytes 12296 | tf_op jit(solution)/shard_map/ppermute | solution.py:674
  55.5 1.7 %collective-permute-start.14 = (f32[8,128]{1,0:T(8,128)S(1)}, f32[8,128]{1,0:T(8,128)S(1)}, u32[]{:S(2)}, u32[]{:S(2)}) collective-permute-start(f32[8,128]{1,0:T(8,128)S(1)} %add.12), channel_id=1, source_target_pairs={{0,2},{1,3},{2,0},{3,1},{4,6},{5,7},{6,4},{7,5},{8,10},{9,11},{10,... | collective-permute-start | bytes 12296 | tf_op jit(solution)/shard_map/ppermute | solution.py:674
  57.2 1.1 %collective-permute-start.13 = (f32[8,128]{1,0:T(8,128)S(1)}, f32[8,128]{1,0:T(8,128)S(1)}, u32[]{:S(2)}, u32[]{:S(2)}) collective-permute-start(f32[8,128]{1,0:T(8,128)S(1)} %add.12), channel_id=1, source_target_pairs={{0,1},{1,0},{2,3},{3,2},{4,5},{5,4},{6,7},{7,6},{8,9},{9,8},{10,11... | collective-permute-start | bytes 12296 | tf_op jit(solution)/shard_map/ppermute | solution.py:674
  58.4 1.0 %collective-permute-done.15 = f32[8,128]{1,0:T(8,128)S(1)} collective-permute-done((f32[8,128]{1,0:T(8,128)S(1)}, f32[8,128]{1,0:T(8,128)S(1)}, u32[]{:S(2)}, u32[]{:S(2)}) %collective-permute-start.15) | collective-permute-done | bytes 4128 | tf_op jit(solution)/shard_map/ppermute | solution.py:674
  59.4 0.7 collective-permute-done.14
  60.0 0.8 %collective-permute-done.13 = f32[8,128]{1,0:T(8,128)S(1)} collective-permute-done((f32[8,128]{1,0:T(8,128)S(1)}, f32[8,128]{1,0:T(8,128)S(1)}, u32[]{:S(2)}, u32[]{:S(2)}) %collective-permute-start.13) | collective-permute-done | bytes 4128 | tf_op jit(solution)/shard_map/ppermute | solution.py:674
  60.9 1.0 %collective-permute-start.18 = (f32[8,128]{1,0:T(8,128)S(1)}, f32[8,128]{1,0:T(8,128)S(1)}, u32[]{:S(2)}, u32[]{:S(2)}) collective-permute-start(f32[8,128]{1,0:T(8,128)S(1)} %add_add_fusion.rest_0_), channel_id=1, source_target_pairs={{0,24},{4,28},{8,16},{12,20},{16,8},{20,12},{24,0},{28,4},{1,25},{... | collective-permute-start | bytes 12296 | tf_op jit(solution)/shard_map/ppermute | solution.py:674
  61.9 1.7 %collective-permute-start.17 = (f32[8,128]{1,0:T(8,128)S(1)}, f32[8,128]{1,0:T(8,128)S(1)}, u32[]{:S(2)}, u32[]{:S(2)}) collective-permute-start(f32[8,128]{1,0:T(8,128)S(1)} %add_add_fusion.rest_0_), channel_id=1, source_target_pairs={{0,16},{4,20},{8,24},{12,28},{16,0},{20,4},{24,8},{28,12},{1,17},{... | collective-permute-start | bytes 12296 | tf_op jit(solution)/shard_map/ppermute | solution.py:674
  63.5 0.8 %collective-permute-start.16 = (f32[8,128]{1,0:T(8,128)S(1)}, f32[8,128]{1,0:T(8,128)S(1)}, u32[]{:S(2)}, u32[]{:S(2)}) collective-permute-start(f32[8,128]{1,0:T(8,128)S(1)} %add_add_fusion.rest_0_), channel_id=1, source_target_pairs={{0,8},{4,12},{8,0},{12,4},{16,24},{20,28},{24,16},{28,20},{1,9},{5... | collective-permute-start | bytes 12296 | tf_op jit(solution)/shard_map/ppermute | solution.py:674
  64.3 1.0 %collective-permute-done.18.rest_3_ = f32[8,128]{1,0:T(8,128)S(1)} collective-permute-done((f32[8,128]{1,0:T(8,128)S(1)}, f32[8,128]{1,0:T(8,128)S(1)}, u32[]{:S(2)}, u32[]{:S(2)}) %collective-permute-start.18) | collective-permute-done | bytes 4128 | tf_op jit(solution)/shard_map/ppermute | solution.py:674
  65.4 0.1 collective-permute-done.17.rest_2_
  65.5 1.7 %collective-permute-done.16.rest_1_ = f32[8,128]{1,0:T(8,128)S(1)} collective-permute-done((f32[8,128]{1,0:T(8,128)S(1)}, f32[8,128]{1,0:T(8,128)S(1)}, u32[]{:S(2)}, u32[]{:S(2)}) %collective-permute-start.16) | collective-permute-done | bytes 4128 | tf_op jit(solution)/shard_map/ppermute | solution.py:674
  67.1 0.9 %finish.1 = (f32[32,128]{1,0:T(8,128)}, f32[32,128]{1,0:T(8,128)}) custom-call(f32[32,128]{1,0:T(8,128)S(1)} %get-tuple-element.34.source, f32[32,128]{1,0:T(8,128)S(1)} %get-tuple-element.52.field.precond, f32[32,128]{1,0:T(8,128)S(1)} %get-tuple-element.60.spill, f32[32,128]{1,0:T(8,128)S(1)} %get-tuple-element.61.field.scaled, ...), custom_call_target="tpu_custom_call" | custom-call | tf_op jit(solution)/shard_map/finish/pallas_call | solution.py:661
  (3 shorter events, 0.0 us)
Async XLA Ops:
  2.4 5.7 %collective-permute-start.2 = (s32[7,128]{1,0:T(8,128)S(1)}, s32[7,128]{1,0:T(8,128)S(1)}, u32[]{:S(2)}, u32[]{:S(2)}) collective-permute-start(s32[7,128]{1,0:T(8,128)S(1)} %get-tuple-element.51), channel_id=1, source_target_pairs={{0,1},{1,0},{2,3},{3,2},{4,5},{5,4},{6,7},{7,6},{8,9},{9,8},{10,11... | collective-permute-start | bytes 10760 | tf_op jit(solution)/shard_map/ppermute | solution.py:674
  5.4 16.0 %collective-permute-start = (f32[4,32,128]{2,1,0:T(8,128)S(1)}, f32[4,32,128]{2,1,0:T(8,128)S(1)}, u32[]{:S(2)}, u32[]{:S(2)}) collective-permute-start(f32[4,32,128]{2,1,0:T(8,128)S(1)} %get-tuple-element.41), channel_id=1, source_target_pairs={{0,4},{4,0},{8,12},{12,8},{16,20},{20,16},{24,28},{28,24},{1,5},{5... | collective-permute-start | bytes 196616 | tf_op jit(solution)/shard_map/ppermute | solution.py:691
  5.4 16.0 %collective-permute-start.1 = (f32[4,32,128]{2,1,0:T(8,128)S(1)}, f32[4,32,128]{2,1,0:T(8,128)S(1)}, u32[]{:S(2)}, u32[]{:S(2)}) collective-permute-start(f32[4,32,128]{2,1,0:T(8,128)S(1)} %get-tuple-element.42), channel_id=1, source_target_pairs={{0,28},{1,29},{2,30},{3,31},{4,8},{5,9},{6,10},{7,11},{8,4},{9,5},... | collective-permute-start | bytes 196616 | tf_op jit(solution)/shard_map/ppermute | solution.py:695
  8.0 13.4 %collective-permute-start.3 = (s32[14,128]{1,0:T(8,128)S(1)}, s32[14,128]{1,0:T(8,128)S(1)}, u32[]{:S(2)}, u32[]{:S(2)}) collective-permute-start(s32[14,128]{1,0:T(8,128)S(1)} %pad_add_fusion.rest_0_), channel_id=1, source_target_pairs={{0,3},{1,2},{2,1},{3,0},{4,7},{5,6},{6,5},{7,4},{8,11},{9,10},{10,... | collective-permute-start | bytes 21512 | tf_op jit(solution)/shard_map/ppermute | solution.py:674
  25.9 12.8 %collective-permute-start.7 = (f32[32,128]{1,0:T(8,128)S(1)}, f32[32,128]{1,0:T(8,128)S(1)}, u32[]{:S(2)}, u32[]{:S(2)}) collective-permute-start(f32[32,128]{1,0:T(8,128)S(1)} %get-tuple-element.52.field.precond), channel_id=1, source_target_pairs={{0,3},{1,5},{2,4},{3,7},{4,2},{5,1},{6,8},{7,0},{8,6},{9,13},{10,1... | collective-permute-start | bytes 49160 | tf_op jit(solution)/shard_map/ppermute | solution.py:753
  30.0 8.7 %collective-permute-start.6 = (f32[32,128]{1,0:T(8,128)S(1)}, f32[32,128]{1,0:T(8,128)S(1)}, u32[]{:S(2)}, u32[]{:S(2)}) collective-permute-start(f32[32,128]{1,0:T(8,128)S(1)} %get-tuple-element.52.field.precond), channel_id=1, source_target_pairs={{0,2},{1,4},{2,6},{3,7},{4,1},{5,8},{6,0},{7,3},{8,5},{9,12},{10,1... | collective-permute-start | bytes 49160 | tf_op jit(solution)/shard_map/ppermute | solution.py:753
  30.1 8.6 %collective-permute-start.5 = (f32[32,128]{1,0:T(8,128)S(1)}, f32[32,128]{1,0:T(8,128)S(1)}, u32[]{:S(2)}, u32[]{:S(2)}) collective-permute-start(f32[32,128]{1,0:T(8,128)S(1)} %get-tuple-element.52.field.precond), channel_id=1, source_target_pairs={{0,31},{1,2},{2,1},{3,4},{4,3},{5,6},{6,5},{7,8},{8,7},{9,10},{10,... | collective-permute-start | bytes 49160 | tf_op jit(solution)/shard_map/ppermute | solution.py:753
  30.9 7.9 %collective-permute-start.4 = (f32[32,128]{1,0:T(8,128)S(1)}, f32[32,128]{1,0:T(8,128)S(1)}, u32[]{:S(2)}, u32[]{:S(2)}) collective-permute-start(f32[32,128]{1,0:T(8,128)S(1)} %get-tuple-element.52.field.precond), channel_id=1, source_target_pairs={{0,1},{1,0},{2,3},{3,2},{4,5},{5,4},{6,7},{7,6},{8,9},{9,8},{10,11... | collective-permute-start | bytes 49160 | tf_op jit(solution)/shard_map/ppermute | solution.py:753
  40.9 9.6 %collective-permute-start.11 = (f32[32,128]{1,0:T(8,128)S(1)}, f32[32,128]{1,0:T(8,128)S(1)}, u32[]{:S(2)}, u32[]{:S(2)}) collective-permute-start(f32[32,128]{1,0:T(8,128)S(1)} %get-tuple-element.61.field.scaled), channel_id=1, source_target_pairs={{0,3},{1,5},{2,4},{3,7},{4,2},{5,1},{6,8},{7,0},{8,6},{9,13},{10,1... | collective-permute-start | bytes 49160 | tf_op jit(solution)/shard_map/ppermute | solution.py:753
  42.5 8.0 %collective-permute-start.10 = (f32[32,128]{1,0:T(8,128)S(1)}, f32[32,128]{1,0:T(8,128)S(1)}, u32[]{:S(2)}, u32[]{:S(2)}) collective-permute-start(f32[32,128]{1,0:T(8,128)S(1)} %get-tuple-element.61.field.scaled), channel_id=1, source_target_pairs={{0,2},{1,4},{2,6},{3,7},{4,1},{5,8},{6,0},{7,3},{8,5},{9,12},{10,1... | collective-permute-start | bytes 49160 | tf_op jit(solution)/shard_map/ppermute | solution.py:753
  43.6 7.0 %collective-permute-start.9 = (f32[32,128]{1,0:T(8,128)S(1)}, f32[32,128]{1,0:T(8,128)S(1)}, u32[]{:S(2)}, u32[]{:S(2)}) collective-permute-start(f32[32,128]{1,0:T(8,128)S(1)} %get-tuple-element.61.field.scaled), channel_id=1, source_target_pairs={{0,31},{1,2},{2,1},{3,4},{4,3},{5,6},{6,5},{7,8},{8,7},{9,10},{10,... | collective-permute-start | bytes 49160 | tf_op jit(solution)/shard_map/ppermute | solution.py:753
  45.3 5.2 %collective-permute-start.8 = (f32[32,128]{1,0:T(8,128)S(1)}, f32[32,128]{1,0:T(8,128)S(1)}, u32[]{:S(2)}, u32[]{:S(2)}) collective-permute-start(f32[32,128]{1,0:T(8,128)S(1)} %get-tuple-element.61.field.scaled), channel_id=1, source_target_pairs={{0,1},{1,0},{2,3},{3,2},{4,5},{5,4},{6,7},{7,6},{8,9},{9,8},{10,11... | collective-permute-start | bytes 49160 | tf_op jit(solution)/shard_map/ppermute | solution.py:753
  52.8 1.2 %collective-permute-start.12 = (f32[8,128]{1,0:T(8,128)S(1)}, f32[8,128]{1,0:T(8,128)S(1)}, u32[]{:S(2)}, u32[]{:S(2)}) collective-permute-start(f32[8,128]{1,0:T(8,128)S(1)} %get-tuple-element.65), channel_id=1, source_target_pairs={{0,4},{4,0},{8,12},{12,8},{16,20},{20,16},{24,28},{28,24},{1,5},{5... | collective-permute-start | bytes 12296 | tf_op jit(solution)/shard_map/ppermute | solution.py:674
  54.0 5.4 %collective-permute-start.15 = (f32[8,128]{1,0:T(8,128)S(1)}, f32[8,128]{1,0:T(8,128)S(1)}, u32[]{:S(2)}, u32[]{:S(2)}) collective-permute-start(f32[8,128]{1,0:T(8,128)S(1)} %add.12), channel_id=1, source_target_pairs={{0,3},{1,2},{2,1},{3,0},{4,7},{5,6},{6,5},{7,4},{8,11},{9,10},{10,... | collective-permute-start | bytes 12296 | tf_op jit(solution)/shard_map/ppermute | solution.py:674
  55.5 4.5 %collective-permute-start.14 = (f32[8,128]{1,0:T(8,128)S(1)}, f32[8,128]{1,0:T(8,128)S(1)}, u32[]{:S(2)}, u32[]{:S(2)}) collective-permute-start(f32[8,128]{1,0:T(8,128)S(1)} %add.12), channel_id=1, source_target_pairs={{0,2},{1,3},{2,0},{3,1},{4,6},{5,7},{6,4},{7,5},{8,10},{9,11},{10,... | collective-permute-start | bytes 12296 | tf_op jit(solution)/shard_map/ppermute | solution.py:674
  57.2 3.6 %collective-permute-start.13 = (f32[8,128]{1,0:T(8,128)S(1)}, f32[8,128]{1,0:T(8,128)S(1)}, u32[]{:S(2)}, u32[]{:S(2)}) collective-permute-start(f32[8,128]{1,0:T(8,128)S(1)} %add.12), channel_id=1, source_target_pairs={{0,1},{1,0},{2,3},{3,2},{4,5},{5,4},{6,7},{7,6},{8,9},{9,8},{10,11... | collective-permute-start | bytes 12296 | tf_op jit(solution)/shard_map/ppermute | solution.py:674
  60.9 4.5 %collective-permute-start.18 = (f32[8,128]{1,0:T(8,128)S(1)}, f32[8,128]{1,0:T(8,128)S(1)}, u32[]{:S(2)}, u32[]{:S(2)}) collective-permute-start(f32[8,128]{1,0:T(8,128)S(1)} %add_add_fusion.rest_0_), channel_id=1, source_target_pairs={{0,24},{4,28},{8,16},{12,20},{16,8},{20,12},{24,0},{28,4},{1,25},{... | collective-permute-start | bytes 12296 | tf_op jit(solution)/shard_map/ppermute | solution.py:674
  61.9 3.6 %collective-permute-start.17 = (f32[8,128]{1,0:T(8,128)S(1)}, f32[8,128]{1,0:T(8,128)S(1)}, u32[]{:S(2)}, u32[]{:S(2)}) collective-permute-start(f32[8,128]{1,0:T(8,128)S(1)} %add_add_fusion.rest_0_), channel_id=1, source_target_pairs={{0,16},{4,20},{8,24},{12,28},{16,0},{20,4},{24,8},{28,12},{1,17},{... | collective-permute-start | bytes 12296 | tf_op jit(solution)/shard_map/ppermute | solution.py:674
  63.5 3.6 %collective-permute-start.16 = (f32[8,128]{1,0:T(8,128)S(1)}, f32[8,128]{1,0:T(8,128)S(1)}, u32[]{:S(2)}, u32[]{:S(2)}) collective-permute-start(f32[8,128]{1,0:T(8,128)S(1)} %add_add_fusion.rest_0_), channel_id=1, source_target_pairs={{0,8},{4,12},{8,0},{12,4},{16,24},{20,28},{24,16},{28,20},{1,9},{5... | collective-permute-start | bytes 12296 | tf_op jit(solution)/shard_map/ppermute | solution.py:674
